TPU v7x, 32 devices: a whole 2x2x4 slice. The times are simulated.
32 devices in a mesh: pair: 2 (over core), batch: 4 (over y, x), vocab: 4 (over z).
Axes of the slice: x: 2, y: 2, z: 4, core: 2. Of those that a mesh axis runs over, the one named last changes fastest.
Arguments:
- hidden: bfloat16 [2, 512, 8192], P('pair', 'batch', 'vocab'), may hold values from -120 to 120
- norm_gain: bfloat16 [8192], P('vocab'), may hold values from 0.099609375 to 1.8984375
- head_weight: bfloat16 [8192, 16384], P(('pair', 'batch'), 'vocab'), may hold values from -1 to 1
Outputs:
- guided_logprobs: float32 [512, 16384], P(('pair', 'batch'), 'vocab')
- cond_logprobs: float32 [512, 16384], P(('pair', 'batch'), 'vocab')
All inputs are finite; a program needn't handle non-finite values.
Results may differ from a plain program's by a relative error of at most 0.007.
Values may be sent and summed in bfloat16 or wider, within the bound.
No kernel may reach another device: no remote copies, remote signals or barrier semaphores. Data moves between devices by JAX's collectives and lax.ppermute only.
A program may use at most 128 MiB of HBM per device.

v0:
```python
import jax
import jax.numpy as jnp
from jax import lax
from jax.sharding import PartitionSpec as P

D = 8192


EPS = 1e-05
GUIDE = 1.5


def on_device(hidden, norm_gain, head_weight):
    rows = hidden[0]
    wide = rows.astype(jnp.float32)
    partial_sq = jnp.sum(wide * wide, axis=1)
    total_sq = lax.psum(partial_sq, "vocab")
    scaled = wide * lax.rsqrt(total_sq / D + EPS)[:, None] * norm_gain.astype(jnp.float32)[None, :]
    features = lax.all_gather(scaled.astype(jnp.bfloat16), "vocab", axis=1, tiled=True)
    blocks = lax.all_to_all(features, ("pair", "batch"), split_axis=1, concat_axis=0, tiled=True)
    groups = lax.axis_size("pair") * lax.axis_size("batch")
    width = blocks.shape[1]
    out_rows = blocks.shape[0] // (2 * groups)
    ordered = blocks.reshape(2, groups, out_rows, width).transpose(1, 0, 2, 3).reshape(-1, width)
    logits = lax.psum_scatter(
        jnp.dot(ordered, head_weight, preferred_element_type=jnp.float32),
        ("pair", "batch"),
        scatter_dimension=0,
        tiled=True,
    )
    cond = logits[:out_rows]
    uncond = logits[out_rows:]
    guided = GUIDE * cond + (1.0 - GUIDE) * uncond
    peak_c, peak_g = lax.pmax((jnp.max(cond, axis=1), jnp.max(guided, axis=1)), "vocab")
    local_c = jnp.sum(jnp.exp(cond - peak_c[:, None]), axis=1)
    local_g = jnp.sum(jnp.exp(guided - peak_g[:, None]), axis=1)
    total_c, total_g = lax.psum((local_c, local_g), "vocab")
    cond_out = cond - (peak_c + jnp.log(total_c))[:, None]
    guided_out = guided - (peak_g + jnp.log(total_g))[:, None]
    return (guided_out, cond_out)


def solution(mesh):
    in_specs = (P("pair", "batch", "vocab"), P("vocab"), P(("pair", "batch"), "vocab"))
    out_specs = (P(("pair", "batch"), "vocab"), P(("pair", "batch"), "vocab"))
    return jax.shard_map(
        on_device, mesh=mesh, in_specs=in_specs, out_specs=out_specs, check_vma=False
    )
```

profile of v0, /device:TPU:0, one launch (start us, length us, event | category | flops | bytes accessed | tf_op | source)
XLA Modules:
  0.0 261.6 jit_solution(3090659099556776236)
XLA Ops:
  7.2 0.0 all-gather.2.cloned.1.call-start
  7.2 0.7 convert_element_type.14
  7.9 1.3 copy.6
  9.2 0.3 fusion
  9.5 13.5 %psum.21 = f32[128]{0:T(128)S(1)} all-reduce(f32[128]{0:T(128)S(1)} %fusion), channel_id=1, replica_groups=mesh['pair'=2,'batch'=4,'vocab'=4] {'vocab'}, use_global_device_ids=true, to_apply=%region_1.0 | all-reduce | flops 128 | bytes 1024 | tf_op jit(solution)/shard_map/psum | solution.py:17
  23.0 1.1 fusion.2
  24.1 0.0 all-gather.2.cloned.1.call-update
  24.1 0.0 reduce-scatter.2.cloned.1.call-start
  24.2 44.3 %all-gather.2.cloned.1.call-done = bf16[128,8192]{0,1:T(8,128)(2,1)} async-done(((bf16[128,2048]{0,1:T(8,128)(2,1)}), bf16[128,8192]{0,1:T(8,128)(2,1)}) %all-gather.2.cloned.1.call-update) | async-done | bytes 2097168 | tf_op jit(solution)/shard_map/all_gather | solution.py:19
  68.4 29.9 %all_to_all.16 = bf16[128,8,1024]{0,2,1:T(8,128)(2,1)S(1)} all-to-all(bf16[128,8,1024]{0,2,1:T(8,128)(2,1)} %bitcast.14), channel_id=1, replica_groups=mesh['pair'=2,'batch'=4,'vocab'=4] {'pair','batch'}, dimensions={1} | all-to-all | bytes 4194304 | tf_op jit(solution)/shard_map/all_to_all | solution.py:20
  98.3 2.6 copy.7
  100.9 1.8 copy.8
  102.7 14.4 %fusion.5 = f32[1024,4096]{1,0:T(8,128)} fusion(bf16[1024,1024]{1,0:T(8,128)(2,1)S(1)} %bitcast.15, bf16[1024,4096]{1,0:T(8,128)(2,1)} %param.5), kind=kOutput, calls=%fused_computation.16 | convolution fusion | flops 8589934592 | bytes 27262976 | tf_op jit(solution)/shard_map/dot_general | solution.py:26
  117.1 0.0 reduce-scatter.2.cloned.1.call-update
  117.2 113.4 %reduce-scatter.2.cloned.1.call-done = f32[128,4096]{1,0:T(8,128)} async-done(((f32[1024,4096]{1,0:T(8,128)}), f32[128,4096]{1,0:T(8,128)}) %reduce-scatter.2.cloned.1.call-update) | async-done | bytes 2097168 | tf_op jit(solution)/shard_map/reduce_scatter | solution.py:25
  230.6 0.0 copy-start
  230.6 2.0 slice_reduce_fusion
  232.5 11.7 %all-reduce.1 = (f32[64]{0:T(128)S(1)}, f32[64]{0:T(128)S(1)}) all-reduce(f32[64]{0:T(128)S(1)} %get-tuple-element.5, f32[64]{0:T(128)S(1)} %get-tuple-element.4), channel_id=1, replica_groups=mesh['pair'=2,'batch'=4,'vocab'=4] {'vocab'}, use_global_device_ids=true, to_apply=%region_4.0 | all-reduce | flops 128 | bytes 1024 | tf_op jit(solution)/shard_map/pmax | solution.py:34
  244.2 0.0 copy-done
  244.2 0.5 exponential_reduce_fusion
  244.7 8.4 %all-reduce = (f32[64]{0:T(128)S(1)}, f32[64]{0:T(128)S(1)}) all-reduce(f32[64]{0:T(128)S(1)} %get-tuple-element.3, f32[64]{0:T(128)S(1)} %get-tuple-element.2), channel_id=1, replica_groups=mesh['pair'=2,'batch'=4,'vocab'=4] {'vocab'}, use_global_device_ids=true, to_apply=%region_6.0 | all-reduce | flops 128 | bytes 1024 | tf_op jit(solution)/shard_map/psum | solution.py:37
  253.1 1.6 slice_subtract_fusion
  (2 shorter events, 0.0 us)
Async XLA Ops:
  7.2 61.3 %all-gather.2.cloned.1.call-start = ((), (), s32[]{:S(2)}) async-start(), calls=%async_computation.2 | async-start | bytes 2621440 | tf_op jit(solution)/shard_map/all_gather | solution.py:19
  24.1 206.4 %reduce-scatter.2.cloned.1.call-start = ((), (), s32[]{:S(2)}) async-start(), calls=%async_computation.3 | async-start | bytes 18874368 | tf_op jit(solution)/shard_map/reduce_scatter | solution.py:25
  230.6 13.6 %copy-start = (f32[128,4096]{1,0:T(8,128)S(1)}, f32[128,4096]{1,0:T(8,128)}, u32[]{:S(2)}) copy-start(f32[128,4096]{1,0:T(8,128)} %reduce-scatter.2.cloned.1.call-done) | copy-start | bytes 6291460
Sparse Core Ops, SparseCore 0:
  24.2 44.1 all-gather.1
  117.3 113.2 reduce-scatter.1
where the time goes:
time: 262 us
  waiting for transfers between devices  158 us (60%)
  blocking collectives  63.4 us (24%)
  matrix products  14.4 us (5%)
  between operations  14.1 us (5%)
  other arithmetic  6.23 us (2%)
  local copies, waits for them, and re-layouts  5.73 us (2%)
    reduce_scatter x1, waiting for transfers between devices, on_device(): lax.psum_scatter(jnp.dot(ordered, head_weight, preferred_element_type=jnp...  113 us
    all_gather x1, waiting for transfers between devices, on_device(): lax.all_gather(scaled.astype(jnp.bfloat16), 'vocab', axis=1, tiled=True)  44.3 us
    all_to_all x1, blocking collectives, on_device(): lax.all_to_all(features, ('pair', 'batch'), split_axis=1, concat_axis=0,...  29.9 us
    dot_general x1, matrix products, on_device(): jnp.dot(ordered, head_weight, preferred_element_type=jnp.float32)  14.4 us
    psum x1, blocking collectives, on_device(): total_sq = lax.psum(partial_sq, 'vocab')  13.5 us
    pmax x1, blocking collectives, on_device(): lax.pmax((jnp.max(cond, axis=1), jnp.max(guided, axis=1)), 'vocab')  11.7 us
    psum x1, blocking collectives, on_device(): total_c, total_g = lax.psum((local_c, local_g), 'vocab')  8.37 us
  transfers between devices with their start and end apart: 2, of which 2 were waited for; matrix products, arithmetic and copies ran while one was open for 0% of the time, Pallas kernels for 0%

commit v1 on v0

v1 whole, which is shorter than its diff:
```python
import jax
import jax.numpy as jnp
from jax import lax
from jax.sharding import PartitionSpec as P

EPS = 1e-05
GUIDE = 1.5
CHUNKS = 4
SUM_TYPE = jnp.float16

X_SWAP = [(0, 1), (1, 0), (2, 3), (3, 2)]
Y_SWAP = [(0, 2), (2, 0), (1, 3), (3, 1)]
CORE_SWAP = [(0, 1), (1, 0)]


def pick(array, index, axis):
    return lax.dynamic_index_in_dim(array, index, axis, keepdims=False)


def in_order(mine, other, index, axis):
    first = jnp.where(index == 0, mine, other)
    second = jnp.where(index == 0, other, mine)
    return jnp.stack([first, second], axis=axis)


def on_device(hidden, norm_gain, head_weight):
    core = lax.axis_index("pair")
    place = lax.axis_index("batch")
    y, x = place // 2, place % 2
    vocab = lax.axis_size("vocab")
    rows = hidden[0]
    seg = rows.shape[0] // 2
    depth = rows.shape[1]
    block, columns = head_weight.shape
    width = columns // 2
    model = depth * vocab
    step = seg // CHUNKS

    halves = head_weight.reshape(block, 2, width)
    weight = in_order(
        pick(halves, core, 1),
        lax.ppermute(pick(halves, 1 - core, 1), "pair", CORE_SWAP),
        core,
        0,
    ).reshape(2 * block, width)

    wide = rows.astype(jnp.float32)
    gained = (wide * norm_gain.astype(jnp.float32)[None, :]).astype(jnp.bfloat16)
    squares = lax.all_gather(jnp.sum(wide * wide, axis=1), ("pair", "batch", "vocab"))
    total_sq = squares.reshape(2, 4, vocab, 2, seg).sum(axis=2)
    scale = lax.rsqrt(total_sq / model + EPS).reshape(2, 2, 2, 2, seg)

    if depth == 2 * block:
        parts = gained.reshape(2, seg, 2, block)
        mine = pick(parts, x, 2)
        other = lax.ppermute(pick(parts, 1 - x, 2), "batch", X_SWAP)
        shard = in_order(mine, other, x, 0)

    def features(c):
        if depth == 2 * block:
            piece = shard[:, :, c * step : (c + 1) * step]
            whole = lax.all_gather(piece, "vocab").reshape(2, 2, 2, 2, step, block)
            mine = pick(whole, y, 1)
            other = lax.ppermute(pick(whole, 1 - y, 1), "batch", Y_SWAP)
            branch = in_order(mine, other, y, 1)
        else:
            piece = gained.reshape(2, seg, depth)[:, c * step : (c + 1) * step]
            whole = lax.all_gather(piece, "vocab", axis=2, tiled=True)
            whole = whole.reshape(2, step, 2, 4, block).transpose(3, 2, 0, 1, 4)
            branch = lax.all_to_all(whole, "batch", split_axis=0, concat_axis=0)
            branch = branch.reshape(2, 2, 2, 2, step, block).transpose(2, 0, 1, 3, 4, 5)
        return in_order(branch, lax.ppermute(branch, "pair", CORE_SWAP), core, 0)

    def partial(feats, gain, j):
        left = pick(feats, j, 4).transpose(0, 2, 3, 4, 1, 5).reshape(-1, 2 * block)
        out = jnp.dot(left, weight, preferred_element_type=jnp.float32)
        return out.reshape(2, 2, 2, step, width) * pick(gain, j, 3)[..., None]

    def chunk(c):
        feats = features(c)
        gain = scale[..., c * step : (c + 1) * step]
        away = lax.ppermute(partial(feats, gain, 1 - x).astype(SUM_TYPE), "batch", X_SWAP)
        half = partial(feats, gain, x) + away.astype(jnp.float32)
        away = lax.ppermute(pick(half, 1 - y, 2).astype(SUM_TYPE), "batch", Y_SWAP)
        whole = pick(half, y, 2) + away.astype(jnp.float32)
        mine = pick(whole, core, 1).astype(SUM_TYPE)
        other = lax.ppermute(pick(whole, 1 - core, 1).astype(SUM_TYPE), "pair", CORE_SWAP)
        return in_order(mine, other, core, 2).reshape(2, step, columns)

    logits = jnp.concatenate([chunk(c) for c in range(CHUNKS)], axis=1).astype(jnp.float32)
    cond, uncond = logits[0], logits[1]
    guided = GUIDE * cond + (1.0 - GUIDE) * uncond

    def stats(values):
        peak = jnp.max(values, axis=1)
        return peak, jnp.sum(jnp.exp(values - peak[:, None]), axis=1)

    peak_c, sum_c = stats(cond)
    peak_g, sum_g = stats(guided)
    every = lax.all_gather(jnp.stack([peak_c, peak_g, sum_c, sum_g]), "vocab")
    top = jnp.max(every[:, :2], axis=0)
    total = jnp.sum(every[:, 2:] * jnp.exp(every[:, :2] - top[None]), axis=0)
    norm = top + jnp.log(total)
    return (guided - norm[1][:, None], cond - norm[0][:, None])


def solution(mesh):
    in_specs = (P("pair", "batch", "vocab"), P("vocab"), P(("pair", "batch"), "vocab"))
    out_specs = (P(("pair", "batch"), "vocab"), P(("pair", "batch"), "vocab"))
    return jax.shard_map(
        on_device, mesh=mesh, in_specs=in_specs, out_specs=out_specs, check_vma=False
    )
```

time: 262 us -> 278 us (1.061)
  waiting for transfers between devices: 158 us -> 47.2 us
  blocking collectives: 63.4 us -> 142 us
  local copies, waits for them, and re-layouts: 5.73 us -> 45.7 us
  starting transfers between devices: 0.08 us -> 18.2 us
  between operations: 14.1 us -> 1.38 us
  other arithmetic: 6.23 us -> 10.6 us
    all_gather x0 -> x6, blocking collectives: none -> 142 us  [the longest x1 67.6 us: on_device(): lax.all_gather(jnp.sum(wide * wide, axis=1), ('pair', 'batch', 'vocab'))]
    reduce_scatter x1 -> x0, waiting for transfers between devices: 113 us -> none  [on_device(): lax.psum_scatter(jnp.dot(ordered, head_weight, preferred_element_type=jnp...]
    ppermute x0 -> x22, waiting for transfers between devices: none -> 47.2 us  [the longest x4 33.2 us: chunk(): lax.ppermute(partial(feats, gain, 1 - x).astype(SUM_TYPE), 'batch', X_SWAP)]
    all_gather x1 -> x0, waiting for transfers between devices: 44.3 us -> none  [on_device(): lax.all_gather(scaled.astype(jnp.bfloat16), 'vocab', axis=1, tiled=True)]
    all_to_all x1 -> x0, blocking collectives: 29.9 us -> none  [on_device(): lax.all_to_all(features, ('pair', 'batch'), split_axis=1, concat_axis=0,...]
    psum x2 -> x0, blocking collectives: 21.8 us -> none  [the longest x1 13.5 us: on_device(): total_sq = lax.psum(partial_sq, 'vocab')]
    dynamic_slice x0 -> x4, local copies, waits for them, and re-layouts: none -> 21.4 us  [pick(): return lax.dynamic_index_in_dim(array, index, axis, keepdims=False)]
    ppermute x0 -> x22, starting transfers between devices: none -> 18.2 us  [the longest x4 8.3 us: features(): other = lax.ppermute(pick(whole, 1 - y, 1), 'batch', Y_SWAP)]
  transfers between devices with their start and end apart: 2 -> 22, of which waited for: 2 -> 8; matrix products, arithmetic and copies ran while one was open for 0% -> 20% of each run, Pallas kernels for 0% -> 0%
where the time goes in v1:
time: 278 us
  blocking collectives  142 us (51%)
  waiting for transfers between devices  47.2 us (17%)
  local copies, waits for them, and re-layouts  45.7 us (16%)
  starting transfers between devices  18.2 us (7%)
  matrix products  12.8 us (5%)
  other arithmetic  10.6 us (4%)
    all_gather x1, blocking collectives, on_device(): lax.all_gather(jnp.sum(wide * wide, axis=1), ('pair', 'batch', 'vocab'))  67.6 us
    all_gather x4, blocking collectives, features(): whole = lax.all_gather(piece, 'vocab').reshape(2, 2, 2, 2, step, block)  62.5 us
    ppermute x4, waiting for transfers between devices, chunk(): lax.ppermute(partial(feats, gain, 1 - x).astype(SUM_TYPE), 'batch', X_SWAP)  33.2 us
    dynamic_slice x4, local copies, waits for them, and re-layouts, pick(): return lax.dynamic_index_in_dim(array, index, axis, keepdims=False)  21.4 us
    reshape x1, local copies, waits for them, and re-layouts, on_device(): halves = head_weight.reshape(block, 2, width)  14.5 us
    dot_general x8, matrix products, partial(): out = jnp.dot(left, weight, preferred_element_type=jnp.float32)  12.8 us
    all_gather x1, blocking collectives, on_device(): every = lax.all_gather(jnp.stack([peak_c, peak_g, sum_c, sum_g]), 'vocab')  11.9 us
    ppermute x4, starting transfers between devices, features(): other = lax.ppermute(pick(whole, 1 - y, 1), 'batch', Y_SWAP)  8.3 us
  transfers between devices with their start and end apart: 22, of which 8 were waited for; matrix products, arithmetic and copies ran while one was open for 20% of the time, Pallas kernels for 0%

profile of v1, /device:TPU:0, one launch (start us, length us, event | category | flops | bytes accessed | tf_op | source)
XLA Modules:
  0.0 277.8 jit_solution(4951491450570670861)
XLA Ops:
  0.6 2.1 reshape.132
  5.0 3.0 %collective-permute-start = (bf16[2,64,1024]{2,1,0:T(8,128)(2,1)S(1)}, bf16[2,64,1024]{2,1,0:T(8,128)(2,1)S(1)}, u32[]{:S(2)}, u32[]{:S(2)}) collective-permute-start(bf16[2,64,1024]{2,1,0:T(8,128)(2,1)S(1)} %bitcast.410), channel_id=1, source_target_pairs={{0,4},{4,0},{8,12},{12,8},{1,5},{5,1},{9,13},{13,9},{2,6},{6,2},{1... | collective-permute-start | bytes 786440 | tf_op jit(solution)/shard_map/ppermute | solution.py:56
  8.0 14.5 %reshape.123 = bf16[1024,2,2048]{2,1,0:T(2,128)(2,1)} reshape(bf16[1024,4096]{1,0:T(8,128)(2,1)} %param.5) | data formatting | bytes 16777216 | tf_op jit(solution)/shard_map/reshape | solution.py:39
  22.5 20.2 %constant_dynamic-slice_fusion.9 = (bf16[1024,1,2048]{2,1,0:T(2,128)(2,1)}, bf16[1024,1,2048]{2,1,0:T(2,128)(2,1)S(1)}) fusion(bf16[1024,2,2048]{2,1,0:T(2,128)(2,1)} %reshape.123, s32[]{:T(128)S(6)} %select_n.223, s32[]{:T(128)S(6)} %select_n.224), kind=kLoop, calls=%fused_computation.195 | loop fusion | bytes 16777224 | tf_op jit(solution)/shard_map/jit(dynamic_index_in_dim)/dynamic_slice | solution.py:17
  42.8 4.6 %copy.190 = bf16[1024,1,2048]{2,0,1:T(8,128)(2,1)} copy(bf16[1024,1,2048]{2,1,0:T(2,128)(2,1)S(1)} %get-tuple-element.7) | data formatting | bytes 8388608
  47.6 67.6 %all-gather.6 = f32[32,1,128]{2,1,0:T(1,128)S(1)} all-gather(f32[1,1,128]{2,1,0:T(1,128)S(1)} %bitcast.422), channel_id=3, replica_groups=mesh['pair'=2,'batch'=4,'vocab'=4] {'pair','batch','vocab'}, dimensions={0}, use_global_device_ids=true | all-gather | bytes 16896 | tf_op jit(solution)/shard_map/all_gather | solution.py:49
  116.9 16.3 %all-gather = bf16[8,2,16,1024]{3,2,1,0:T(8,128)(2,1)S(1)} all-gather(bf16[2,2,16,1024]{3,2,1,0:T(8,128)(2,1)S(1)} %get-tuple-element.44), channel_id=2, replica_groups=mesh['pair'=2,'batch'=4,'vocab'=4] {'vocab'}, dimensions={0}, use_global_device_ids=true | all-gather | bytes 655360 | tf_op jit(solution)/shard_map/all_gather | solution.py:62
  133.2 6.0 %collective-permute-start.1 = (bf16[2,2,2,16,1024]{4,3,2,1,0:T(8,128)(2,1)S(1)}, bf16[2,2,2,16,1024]{4,3,2,1,0:T(8,128)(2,1)S(1)}, u32[]{:S(2)}, u32[]{:S(2)}) collective-permute-start(bf16[2,2,2,16,1024]{4,3,2,1,0:T(8,128)(2,1)S(1)} %dynamic-slice_bitcast_fusion.3), channel_id=1, source_target_pairs={{0,8},{8,0},{4,12},{12,4},{1,9},{9,1},{5,13},{13,5},{2,10},{10,2},... | collective-permute-start | bytes 786440 | tf_op jit(solution)/shard_map/ppermute | solution.py:64
  139.2 15.5 %all-gather.2 = bf16[8,2,16,1024]{3,2,1,0:T(8,128)(2,1)S(1)} all-gather(bf16[2,2,16,1024]{3,2,1,0:T(8,128)(2,1)S(1)} %get-tuple-element.45), channel_id=4, replica_groups=mesh['pair'=2,'batch'=4,'vocab'=4] {'vocab'}, dimensions={0}, use_global_device_ids=true | all-gather | bytes 655360 | tf_op jit(solution)/shard_map/all_gather | solution.py:62
  154.9 15.9 %all-gather.3 = bf16[8,2,16,1024]{3,2,1,0:T(8,128)(2,1)S(1)} all-gather(bf16[2,2,16,1024]{3,2,1,0:T(8,128)(2,1)S(1)} %get-tuple-element.47), channel_id=5, replica_groups=mesh['pair'=2,'batch'=4,'vocab'=4] {'vocab'}, dimensions={0}, use_global_device_ids=true | all-gather | bytes 655360 | tf_op jit(solution)/shard_map/all_gather | solution.py:62
  170.8 1.9 collective-permute-start.12
  172.7 14.8 %all-gather.4 = bf16[8,2,16,1024]{3,2,1,0:T(8,128)(2,1)S(1)} all-gather(bf16[2,2,16,1024]{3,2,1,0:T(8,128)(2,1)S(1)} %get-tuple-element.46), channel_id=6, replica_groups=mesh['pair'=2,'batch'=4,'vocab'=4] {'vocab'}, dimensions={0}, use_global_device_ids=true | all-gather | bytes 655360 | tf_op jit(solution)/shard_map/all_gather | solution.py:62
  188.9 5.1 %collective-permute-done.17 = bf16[2,2,2,16,1024]{4,3,2,1,0:T(8,128)(2,1)S(1)} collective-permute-done((bf16[2,2,2,16,1024]{4,3,2,1,0:T(8,128)(2,1)S(1)}, bf16[2,2,2,16,1024]{4,3,2,1,0:T(8,128)(2,1)S(1)}, u32[]{:S(2)}, u32[]{:S(2)}) %collective-permute-start.17) | collective-permute-done | bytes 262176 | tf_op jit(solution)/shard_map/ppermute | solution.py:64
  194.7 1.4 collective-permute-done.18
  197.8 4.2 %select_bitcast_fusion.1 = (bf16[1,1024,2048]{2,1,0:T(8,128)(2,1)S(1)}, bf16[1,1024,2048]{2,1,0:T(8,128)(2,1)S(1)}) fusion(bf16[1024,2048]{1,0:T(8,128)(2,1)} %collective-permute-done.3, pred[]{:T(512)S(6)} %eq.8, bf16[1024,1,2048]{2,1,0:T(2,128)(2,1)S(1)} %bitcast.397), kind=kLoop, calls=%fused_computation.20 | loop fusion | flops 4194304 | bytes 16777216 | tf_op jit(solution)/shard_map/stack | solution.py:23
  202.0 1.6 fusion.85
  203.7 1.6 fusion.79
  205.3 2.1 collective-permute-start.9
  207.4 1.6 fusion.82
  209.1 1.8 fusion.76
  210.9 2.0 collective-permute-start.19
  213.0 5.4 %collective-permute-done.4 = f16[2,2,2,16,2048]{4,3,2,1,0:T(8,128)(2,1)S(1)} collective-permute-done((f16[2,2,2,16,2048]{4,3,2,1,0:T(8,128)(2,1)S(1)}, f16[2,2,2,16,2048]{4,3,2,1,0:T(8,128)(2,1)S(1)}, u32[]{:S(2)}, u32[]{:S(2)}) %collective-permute-start.4) | collective-permute-done | bytes 524320 | tf_op jit(solution)/shard_map/ppermute | solution.py:82
  218.4 1.5 fusion.46
  220.3 9.4 %collective-permute-done.9 = f16[2,2,2,16,2048]{4,3,0,1,2:T(8,128)(2,1)S(1)} collective-permute-done((f16[2,2,2,16,2048]{4,3,0,1,2:T(8,128)(2,1)S(1)}, f16[2,2,2,16,2048]{4,3,0,1,2:T(8,128)(2,1)S(1)}, u32[]{:S(2)}, u32[]{:S(2)}) %collective-permute-start.9) | collective-permute-done | bytes 524320 | tf_op jit(solution)/shard_map/ppermute | solution.py:82
  229.6 1.5 fusion.70
  231.5 9.4 %collective-permute-done.14 = f16[2,2,2,16,2048]{4,3,0,1,2:T(8,128)(2,1)S(1)} collective-permute-done((f16[2,2,2,16,2048]{4,3,0,1,2:T(8,128)(2,1)S(1)}, f16[2,2,2,16,2048]{4,3,0,1,2:T(8,128)(2,1)S(1)}, u32[]{:S(2)}, u32[]{:S(2)}) %collective-permute-start.14) | collective-permute-done | bytes 524320 | tf_op jit(solution)/shard_map/ppermute | solution.py:82
  240.9 1.5 fusion.61
  242.7 9.0 %collective-permute-done.19 = f16[2,2,2,16,2048]{4,3,0,1,2:T(8,128)(2,1)S(1)} collective-permute-done((f16[2,2,2,16,2048]{4,3,0,1,2:T(8,128)(2,1)S(1)}, f16[2,2,2,16,2048]{4,3,0,1,2:T(8,128)(2,1)S(1)}, u32[]{:S(2)}, u32[]{:S(2)}) %collective-permute-start.19) | collective-permute-done | bytes 524320 | tf_op jit(solution)/shard_map/ppermute | solution.py:82
  251.7 1.5 fusion.52
  254.6 6.7 %collective-permute-done.20 = f16[2,2,16,2048]{3,2,0,1:T(8,128)(2,1)S(1)} collective-permute-done((f16[2,2,16,2048]{3,2,0,1:T(8,128)(2,1)S(1)}, f16[2,2,16,2048]{3,2,0,1:T(8,128)(2,1)S(1)}, u32[]{:S(2)}, u32[]{:S(2)}) %collective-permute-start.20) | collective-permute-done | bytes 262176 | tf_op jit(solution)/shard_map/ppermute | solution.py:84
  264.2 11.9 %all-gather.7 = f32[4,4,64]{2,1,0:T(4,128)S(1)} all-gather(f32[1,4,64]{2,1,0:T(4,128)S(1)} %maximum_bitcast_fusion.4), channel_id=7, replica_groups=mesh['pair'=2,'batch'=4,'vocab'=4] {'vocab'}, dimensions={0}, use_global_device_ids=true | all-gather | bytes 5120 | tf_op jit(solution)/shard_map/all_gather | solution.py:100
  276.2 1.6 bitcast_subtract_fusion
  (112 shorter events, 12.9 us)
Async XLA Ops:
  5.0 111.7 %collective-permute-start = (bf16[2,64,1024]{2,1,0:T(8,128)(2,1)S(1)}, bf16[2,64,1024]{2,1,0:T(8,128)(2,1)S(1)}, u32[]{:S(2)}, u32[]{:S(2)}) collective-permute-start(bf16[2,64,1024]{2,1,0:T(8,128)(2,1)S(1)} %bitcast.410), channel_id=1, source_target_pairs={{0,4},{4,0},{8,12},{12,8},{1,5},{5,1},{9,13},{13,9},{2,6},{6,2},{1... | collective-permute-start | bytes 786440 | tf_op jit(solution)/shard_map/ppermute | solution.py:56
  42.8 4.6 %copy-start = (bf16[1,128,2048]{2,1,0:T(8,128)(2,1)S(1)}, bf16[1,128,2048]{2,1,0:T(8,128)(2,1)}, u32[]{:S(2)}) copy-start(bf16[1,128,2048]{2,1,0:T(8,128)(2,1)} %param.3) | copy-start | bytes 1572868
  47.4 149.0 %collective-permute-start.3 = (bf16[1024,2048]{1,0:T(8,128)(2,1)}, bf16[1024,2048]{1,0:T(8,128)(2,1)}, u32[]{:S(2)}, u32[]{:S(2)}) collective-permute-start(bf16[1024,2048]{1,0:T(8,128)(2,1)} %bitcast.394), channel_id=1, source_target_pairs={{0,16},{16,0},{1,17},{17,1},{2,18},{18,2},{3,19},{19,3},{4,20},{20... | collective-permute-start | bytes 12582920 | tf_op jit(solution)/shard_map/ppermute | solution.py:42
  133.2 54.7 %collective-permute-start.1 = (bf16[2,2,2,16,1024]{4,3,2,1,0:T(8,128)(2,1)S(1)}, bf16[2,2,2,16,1024]{4,3,2,1,0:T(8,128)(2,1)S(1)}, u32[]{:S(2)}, u32[]{:S(2)}) collective-permute-start(bf16[2,2,2,16,1024]{4,3,2,1,0:T(8,128)(2,1)S(1)} %dynamic-slice_bitcast_fusion.3), channel_id=1, source_target_pairs={{0,8},{8,0},{4,12},{12,4},{1,9},{9,1},{5,13},{13,5},{2,10},{10,2},... | collective-permute-start | bytes 786440 | tf_op jit(solution)/shard_map/ppermute | solution.py:64
  154.8 33.2 %collective-permute-start.7 = (bf16[2,2,2,16,1024]{4,3,2,1,0:T(8,128)(2,1)S(1)}, bf16[2,2,2,16,1024]{4,3,2,1,0:T(8,128)(2,1)S(1)}, u32[]{:S(2)}, u32[]{:S(2)}) collective-permute-start(bf16[2,2,2,16,1024]{4,3,2,1,0:T(8,128)(2,1)S(1)} %dynamic-slice_bitcast_fusion.2), channel_id=1, source_target_pairs={{0,8},{8,0},{4,12},{12,4},{1,9},{9,1},{5,13},{13,5},{2,10},{10,2},... | collective-permute-start | bytes 786440 | tf_op jit(solution)/shard_map/ppermute | solution.py:64
  170.8 17.9 %collective-permute-start.12 = (bf16[2,2,2,16,1024]{4,3,2,1,0:T(8,128)(2,1)S(1)}, bf16[2,2,2,16,1024]{4,3,2,1,0:T(8,128)(2,1)S(1)}, u32[]{:S(2)}, u32[]{:S(2)}) collective-permute-start(bf16[2,2,2,16,1024]{4,3,2,1,0:T(8,128)(2,1)S(1)} %dynamic-slice_bitcast_fusion.1), channel_id=1, source_target_pairs={{0,8},{8,0},{4,12},{12,4},{1,9},{9,1},{5,13},{13,5},{2,10},{10,2},... | collective-permute-start | bytes 786440 | tf_op jit(solution)/shard_map/ppermute | solution.py:64
  187.6 6.4 %collective-permute-start.17 = (bf16[2,2,2,16,1024]{4,3,2,1,0:T(8,128)(2,1)S(1)}, bf16[2,2,2,16,1024]{4,3,2,1,0:T(8,128)(2,1)S(1)}, u32[]{:S(2)}, u32[]{:S(2)}) collective-permute-start(bf16[2,2,2,16,1024]{4,3,2,1,0:T(8,128)(2,1)S(1)} %dynamic-slice_bitcast_fusion), channel_id=1, source_target_pairs={{0,8},{8,0},{4,12},{12,4},{1,9},{9,1},{5,13},{13,5},{2,10},{10,2},... | collective-permute-start | bytes 786440 | tf_op jit(solution)/shard_map/ppermute | solution.py:64
  187.9 6.3 %collective-permute-start.2 = (bf16[2,2,2,2,16,1024]{5,4,3,2,0,1:T(8,128)(2,1)S(1)}, bf16[2,2,2,2,16,1024]{5,4,3,2,0,1:T(8,128)(2,1)S(1)}, u32[]{:S(2)}, u32[]{:S(2)}) collective-permute-start(bf16[2,2,2,2,16,1024]{5,4,3,2,0,1:T(8,128)(2,1)S(1)} %pad_maximum_fusion.1), channel_id=1, source_target_pairs={{0,16},{16,0},{1,17},{17,1},{2,18},{18,2},{3,19},{19,3},{4,20},{20... | collective-permute-start | bytes 1572872 | tf_op jit(solution)/shard_map/ppermute | solution.py:72
  188.2 6.2 %collective-permute-start.8 = (bf16[2,2,2,2,16,1024]{5,4,3,2,0,1:T(8,128)(2,1)S(1)}, bf16[2,2,2,2,16,1024]{5,4,3,2,0,1:T(8,128)(2,1)S(1)}, u32[]{:S(2)}, u32[]{:S(2)}) collective-permute-start(bf16[2,2,2,2,16,1024]{5,4,3,2,0,1:T(8,128)(2,1)S(1)} %pad_maximum_fusion.2), channel_id=1, source_target_pairs={{0,16},{16,0},{1,17},{17,1},{2,18},{18,2},{3,19},{19,3},{4,20},{20... | collective-permute-start | bytes 1572872 | tf_op jit(solution)/shard_map/ppermute | solution.py:72
  188.8 5.8 %collective-permute-start.13 = (bf16[2,2,2,2,16,1024]{5,4,3,2,0,1:T(8,128)(2,1)S(1)}, bf16[2,2,2,2,16,1024]{5,4,3,2,0,1:T(8,128)(2,1)S(1)}, u32[]{:S(2)}, u32[]{:S(2)}) collective-permute-start(bf16[2,2,2,2,16,1024]{5,4,3,2,0,1:T(8,128)(2,1)S(1)} %pad_maximum_fusion.3), channel_id=1, source_target_pairs={{0,16},{16,0},{1,17},{17,1},{2,18},{18,2},{3,19},{19,3},{4,20},{20... | collective-permute-start | bytes 1572872 | tf_op jit(solution)/shard_map/ppermute | solution.py:72
  194.1 2.0 collective-permute-start.18
  194.2 2.2 slice-start
  194.6 3.2 %slice-start.1 = ((s8[8388608]{0:T(1024)(128)(4,1)}), s8[4194304]{0:T(1024)(128)(4,1)S(1)}, s32[]{:S(2)}) async-start(s8[8388608]{0:T(1024)(128)(4,1)} %bitcast.396), calls=%async_computation.1 | async-start | bytes 8388608
  203.6 14.8 %collective-permute-start.4 = (f16[2,2,2,16,2048]{4,3,2,1,0:T(8,128)(2,1)S(1)}, f16[2,2,2,16,2048]{4,3,2,1,0:T(8,128)(2,1)S(1)}, u32[]{:S(2)}, u32[]{:S(2)}) collective-permute-start(f16[2,2,2,16,2048]{4,3,2,1,0:T(8,128)(2,1)S(1)} %fusion.85), channel_id=1, source_target_pairs={{0,4},{4,0},{8,12},{12,8},{1,5},{5,1},{9,13},{13,9},{2,6},{6,2},{1... | collective-permute-start | bytes 1572872 | tf_op jit(solution)/shard_map/ppermute | solution.py:82
  205.3 24.3 %collective-permute-start.9 = (f16[2,2,2,16,2048]{4,3,0,1,2:T(8,128)(2,1)S(1)}, f16[2,2,2,16,2048]{4,3,0,1,2:T(8,128)(2,1)S(1)}, u32[]{:S(2)}, u32[]{:S(2)}) collective-permute-start(f16[2,2,2,16,2048]{4,3,0,1,2:T(8,128)(2,1)S(1)} %fusion.79), channel_id=1, source_target_pairs={{0,4},{4,0},{8,12},{12,8},{1,5},{5,1},{9,13},{13,9},{2,6},{6,2},{1... | collective-permute-start | bytes 1572872 | tf_op jit(solution)/shard_map/ppermute | solution.py:82
  209.0 31.9 %collective-permute-start.14 = (f16[2,2,2,16,2048]{4,3,0,1,2:T(8,128)(2,1)S(1)}, f16[2,2,2,16,2048]{4,3,0,1,2:T(8,128)(2,1)S(1)}, u32[]{:S(2)}, u32[]{:S(2)}) collective-permute-start(f16[2,2,2,16,2048]{4,3,0,1,2:T(8,128)(2,1)S(1)} %fusion.82), channel_id=1, source_target_pairs={{0,4},{4,0},{8,12},{12,8},{1,5},{5,1},{9,13},{13,9},{2,6},{6,2},{1... | collective-permute-start | bytes 1572872 | tf_op jit(solution)/shard_map/ppermute | solution.py:82
  210.9 40.8 %collective-permute-start.19 = (f16[2,2,2,16,2048]{4,3,0,1,2:T(8,128)(2,1)S(1)}, f16[2,2,2,16,2048]{4,3,0,1,2:T(8,128)(2,1)S(1)}, u32[]{:S(2)}, u32[]{:S(2)}) collective-permute-start(f16[2,2,2,16,2048]{4,3,0,1,2:T(8,128)(2,1)S(1)} %fusion.76), channel_id=1, source_target_pairs={{0,4},{4,0},{8,12},{12,8},{1,5},{5,1},{9,13},{13,9},{2,6},{6,2},{1... | collective-permute-start | bytes 1572872 | tf_op jit(solution)/shard_map/ppermute | solution.py:82
  220.0 33.6 %collective-permute-start.5 = (f16[2,2,16,2048]{3,2,1,0:T(8,128)(2,1)S(1)}, f16[2,2,16,2048]{3,2,1,0:T(8,128)(2,1)S(1)}, u32[]{:S(2)}, u32[]{:S(2)}) collective-permute-start(f16[2,2,16,2048]{3,2,1,0:T(8,128)(2,1)S(1)} %fusion.116), channel_id=1, source_target_pairs={{0,8},{8,0},{4,12},{12,4},{1,9},{9,1},{5,13},{13,5},{2,10},{10,2},... | collective-permute-start | bytes 786440 | tf_op jit(solution)/shard_map/ppermute | solution.py:84
  231.2 22.5 %collective-permute-start.10 = (f16[2,2,16,2048]{3,2,0,1:T(8,128)(2,1)S(1)}, f16[2,2,16,2048]{3,2,0,1:T(8,128)(2,1)S(1)}, u32[]{:S(2)}, u32[]{:S(2)}) collective-permute-start(f16[2,2,16,2048]{3,2,0,1:T(8,128)(2,1)S(1)} %fusion.117), channel_id=1, source_target_pairs={{0,8},{8,0},{4,12},{12,4},{1,9},{9,1},{5,13},{13,5},{2,10},{10,2},... | collective-permute-start | bytes 786440 | tf_op jit(solution)/shard_map/ppermute | solution.py:84
  242.5 11.9 %collective-permute-start.15 = (f16[2,2,16,2048]{3,2,0,1:T(8,128)(2,1)S(1)}, f16[2,2,16,2048]{3,2,0,1:T(8,128)(2,1)S(1)}, u32[]{:S(2)}, u32[]{:S(2)}) collective-permute-start(f16[2,2,16,2048]{3,2,0,1:T(8,128)(2,1)S(1)} %fusion.118), channel_id=1, source_target_pairs={{0,8},{8,0},{4,12},{12,4},{1,9},{9,1},{5,13},{13,5},{2,10},{10,2},... | collective-permute-start | bytes 786440 | tf_op jit(solution)/shard_map/ppermute | solution.py:84
  253.3 8.0 %collective-permute-start.20 = (f16[2,2,16,2048]{3,2,0,1:T(8,128)(2,1)S(1)}, f16[2,2,16,2048]{3,2,0,1:T(8,128)(2,1)S(1)}, u32[]{:S(2)}, u32[]{:S(2)}) collective-permute-start(f16[2,2,16,2048]{3,2,0,1:T(8,128)(2,1)S(1)} %fusion.119), channel_id=1, source_target_pairs={{0,8},{8,0},{4,12},{12,4},{1,9},{9,1},{5,13},{13,5},{2,10},{10,2},... | collective-permute-start | bytes 786440 | tf_op jit(solution)/shard_map/ppermute | solution.py:84
  253.7 7.8 %collective-permute-start.6 = (f16[2,16,2048]{2,1,0:T(8,128)(2,1)S(1)}, f16[2,16,2048]{2,1,0:T(8,128)(2,1)S(1)}, u32[]{:S(2)}, u32[]{:S(2)}) collective-permute-start(f16[2,16,2048]{2,1,0:T(8,128)(2,1)S(1)} %fusion.130), channel_id=1, source_target_pairs={{0,16},{16,0},{1,17},{17,1},{2,18},{18,2},{3,19},{19,3},{4,20},{20... | collective-permute-start | bytes 393224 | tf_op jit(solution)/shard_map/ppermute | solution.py:87
  253.9 7.8 %collective-permute-start.11 = (f16[2,16,2048]{2,1,0:T(8,128)(2,1)S(1)}, f16[2,16,2048]{2,1,0:T(8,128)(2,1)S(1)}, u32[]{:S(2)}, u32[]{:S(2)}) collective-permute-start(f16[2,16,2048]{2,1,0:T(8,128)(2,1)S(1)} %fusion.132), channel_id=1, source_target_pairs={{0,16},{16,0},{1,17},{17,1},{2,18},{18,2},{3,19},{19,3},{4,20},{20... | collective-permute-start | bytes 393224 | tf_op jit(solution)/shard_map/ppermute | solution.py:87
  254.5 7.4 %collective-permute-start.16 = (f16[2,16,2048]{2,1,0:T(8,128)(2,1)S(1)}, f16[2,16,2048]{2,1,0:T(8,128)(2,1)S(1)}, u32[]{:S(2)}, u32[]{:S(2)}) collective-permute-start(f16[2,16,2048]{2,1,0:T(8,128)(2,1)S(1)} %fusion.134), channel_id=1, source_target_pairs={{0,16},{16,0},{1,17},{17,1},{2,18},{18,2},{3,19},{19,3},{4,20},{20... | collective-permute-start | bytes 393224 | tf_op jit(solution)/shard_map/ppermute | solution.py:87
  261.4 1.4 collective-permute-start.21

commit v2 on v1

v2 whole, which is shorter than its diff:
```python
import jax
import jax.numpy as jnp
from jax import lax
from jax.sharding import PartitionSpec as P

EPS = 1e-05
GUIDE = 1.5
CHUNKS = 4
SHRINK = 1.0 / 32.0
SUM_TYPE = jnp.float16

X_SWAP = [(0, 1), (1, 0), (2, 3), (3, 2)]
Y_SWAP = [(0, 2), (2, 0), (1, 3), (3, 1)]
CORE_SWAP = [(0, 1), (1, 0)]


def pick(array, index, axis):
    return lax.dynamic_index_in_dim(array, index, axis, keepdims=False)


def relative(array, index, axis):
    return jnp.where(index == 0, array, jnp.flip(array, axis))


def line_pairs(vocab, moves, hop=False):
    pairs = []
    for b in range(4):
        y = b // 2
        for start, end in moves:
            z = start if y == 0 else vocab - 1 - start
            if hop:
                pairs.append((b * vocab + z, (b ^ 2) * vocab + z))
            else:
                w = end if y == 0 else vocab - 1 - end
                pairs.append((b * vocab + z, b * vocab + w))
    return pairs


def on_device(hidden, norm_gain, head_weight):
    core = lax.axis_index("pair")
    place = lax.axis_index("batch")
    level = lax.axis_index("vocab")
    vocab = lax.axis_size("vocab")
    y, x = place // 2, place % 2
    rows = hidden[0]
    seg = rows.shape[0] // 2
    depth = rows.shape[1]
    block, columns = head_weight.shape
    width = columns // 2
    model = depth * vocab
    step = seg // CHUNKS

    wide = rows.astype(jnp.float32)
    gained = (wide * norm_gain.astype(jnp.float32)[None, :]).astype(jnp.bfloat16)

    keep = lax.dynamic_slice_in_dim(head_weight, core * width, width, 1)
    give = lax.dynamic_slice_in_dim(head_weight, (1 - core) * width, width, 1)
    take = lax.ppermute(give, "pair", CORE_SWAP)
    weight = jnp.concatenate([jnp.where(core == y, keep, take), jnp.where(core == y, take, keep)])

    squares = jnp.sum(wide * wide, axis=1)
    reach = 1
    while reach < vocab:
        squares += lax.ppermute(squares, "vocab", [(i, i ^ reach) for i in range(vocab)])
        reach *= 2
    squares = squares.reshape(2, seg)
    sent = [
        lax.ppermute(
            pick(squares, core ^ k, 0),
            ("pair", "batch"),
            [(4 * s + b, 2 * b + (s ^ k)) for s in range(2) for b in range(4)],
        )
        for k in range(2)
    ]
    total_sq = jnp.stack([jnp.where(x == 0, sent[0], sent[1]), jnp.where(x == 0, sent[1], sent[0])])
    scale = lax.rsqrt(total_sq / model + EPS) / SHRINK

    u = jnp.where(y == 0, level, vocab - 1 - level)

    def line(value, moves, hop=False):
        return lax.ppermute(value, ("batch", "vocab"), line_pairs(vocab, moves, hop))

    def line_features(c):
        piece = gained[:, :].reshape(2, seg, depth)[:, c * step : (c + 1) * step]
        mine = lax.dynamic_slice_in_dim(piece, x * block, block, 2)
        other = lax.ppermute(
            lax.dynamic_slice_in_dim(piece, (1 - x) * block, block, 2), "batch", X_SWAP
        )
        own = jnp.stack([mine, other])
        ahead = line(own, [(0, 1), (2, 3)])
        back = line(own, [(2, 1), (1, 0)])
        beside = line(own, [(1, 1), (3, 3)], hop=True)
        ahead_b = line(beside, [(0, 1)])
        back_b = line(beside, [(2, 1)])
        detour = line(back, [(0, 0)], hop=True)
        second = line(jnp.stack([ahead, ahead_b]), [(1, 2)])
        first = line(jnp.stack([back, back_b]), [(1, 0)])
        last = line(second, [(2, 3)])
        home = jnp.stack([own, beside])
        from_0 = jnp.where(
            u == 0, home, jnp.where(u == 1, jnp.stack([ahead, ahead_b]), jnp.where(u == 2, second, last))
        )
        from_2 = jnp.where(
            u == 2,
            home,
            jnp.where(u == 1, jnp.stack([back, back_b]), jnp.where(u == 0, first, jnp.stack([ahead, detour]))),
        )
        return jnp.stack([from_0, from_2], axis=4)

    def gathered_features(c):
        piece = gained.reshape(2, seg, depth)[:, c * step : (c + 1) * step]
        whole = lax.all_gather(piece, "vocab", axis=2, tiled=True)
        whole = whole.reshape(2, step, 2, 4, block).transpose(3, 0, 1, 2, 4)
        whole = lax.all_to_all(whole, "batch", split_axis=0, concat_axis=0)
        whole = whole.reshape(2, 2, 2, step, 2, block)
        return relative(relative(relative(whole, y, 0), x, 1), y, 4)

    features = line_features if depth == 2 * block and vocab == 4 else gathered_features

    def partial(left, low, high):
        lead = left.shape[:-2]
        out = jnp.dot(
            left.reshape(-1, 2 * block), weight[:, low:high], preferred_element_type=jnp.float32
        )
        return (out * SHRINK).reshape(*lead, high - low)

    def chunk(c):
        branch = features(c)
        branch = relative(relative(branch, x ^ y, 1), x, 2).transpose(1, 2, 0, 3, 4, 5)
        left = jnp.stack([branch, lax.ppermute(branch, "pair", CORE_SWAP)], axis=2)
        middle = width // 2
        away_x = lax.ppermute(partial(left[:, 1], 0, middle).astype(SUM_TYPE), "batch", X_SWAP)
        away_y = lax.ppermute(partial(left[1], middle, width).astype(SUM_TYPE), "batch", Y_SWAP)
        sum_x = partial(left[:, 0], 0, middle) + away_x.astype(jnp.float32)
        sum_y = partial(left[0], middle, width) + jnp.flip(away_y, 2).astype(jnp.float32)
        next_y = lax.ppermute(sum_x[1].astype(SUM_TYPE), "batch", Y_SWAP)
        next_x = lax.ppermute(sum_y[1].astype(SUM_TYPE), "batch", X_SWAP)
        whole = jnp.concatenate(
            [
                sum_x[0] + jnp.flip(next_y, 1).astype(jnp.float32),
                sum_y[0] + next_x.astype(jnp.float32),
            ],
            axis=-1,
        ).astype(SUM_TYPE)
        mine = pick(whole, core ^ y, 1)
        other = jnp.flip(lax.ppermute(pick(whole, 1 - (core ^ y), 1), "pair", CORE_SWAP), 0)
        return mine, other

    pieces = [chunk(c) for c in range(CHUNKS)]
    mine = jnp.concatenate([piece[0] for piece in pieces], axis=1)
    other = jnp.concatenate([piece[1] for piece in pieces], axis=1)
    logits = jnp.concatenate(
        [jnp.where(core == 0, mine, other), jnp.where(core == 0, other, mine)], axis=2
    )
    logits = relative(logits, core, 0).astype(jnp.float32) * scale[..., None]
    cond, uncond = logits[0], logits[1]
    guided = GUIDE * cond + (1.0 - GUIDE) * uncond

    def stats(values):
        peak = jnp.max(values, axis=1)
        return peak, jnp.sum(jnp.exp(values - peak[:, None]), axis=1)

    peak_c, sum_c = stats(cond)
    peak_g, sum_g = stats(guided)
    own = jnp.stack([peak_c, peak_g, sum_c, sum_g])
    every = jnp.stack(
        [own]
        + [
            lax.ppermute(own, "vocab", [(i, (i + k) % vocab) for i in range(vocab)])
            for k in range(1, vocab)
        ]
    )
    top = jnp.max(every[:, :2], axis=0)
    total = jnp.sum(every[:, 2:] * jnp.exp(every[:, :2] - top[None]), axis=0)
    norm = top + jnp.log(total)
    return (guided - norm[1][:, None], cond - norm[0][:, None])


def solution(mesh):
    in_specs = (P("pair", "batch", "vocab"), P("vocab"), P(("pair", "batch"), "vocab"))
    out_specs = (P(("pair", "batch"), "vocab"), P(("pair", "batch"), "vocab"))
    return jax.shard_map(
        on_device, mesh=mesh, in_specs=in_specs, out_specs=out_specs, check_vma=False
    )
```

time: 278 us -> 188 us (0.68)
  blocking collectives: 142 us -> 0 us
  starting transfers between devices: 18.2 us -> 103 us
  local copies, waits for them, and re-layouts: 45.7 us -> 15.8 us
  waiting for transfers between devices: 47.2 us -> 39.1 us
  other arithmetic: 10.6 us -> 14.7 us
    all_gather x6 -> x0, blocking collectives: 142 us -> none  [the longest x1 67.6 us: on_device(): lax.all_gather(jnp.sum(wide * wide, axis=1), ('pair', 'batch', 'vocab'))]
    ppermute x22 -> x72, starting transfers between devices: 18.2 us -> 103 us  [the longest x36 65.2 us: line(): lax.ppermute(value, ('batch', 'vocab'), line_pairs(vocab, moves, hop))]
    dynamic_slice x4 -> x1, local copies, waits for them, and re-layouts: 21.4 us -> 4.79 us  [on_device(): give = lax.dynamic_slice_in_dim(head_weight, (1 - core) * width, width, 1)]
    reshape x6 -> x1, local copies, waits for them, and re-layouts: 14.8 us -> 0.08 us  [on_device(): squares = squares.reshape(2, seg)]
    slice x1 -> x17, local copies, waits for them, and re-layouts: 0.08 us -> 8.92 us  [the longest x4 2.39 us: chunk(): sum_x = partial(left[:, 0], 0, middle) + away_x.astype(jnp.float32)]
    ppermute x22 -> x72, waiting for transfers between devices: 47.2 us -> 39.1 us  [the longest x36 16.5 us: line(): lax.ppermute(value, ('batch', 'vocab'), line_pairs(vocab, moves, hop))]
    unnamed x8 -> x22, local copies, waits for them, and re-layouts: 6.07 us -> 1.88 us
    another operation x20 -> x39, other arithmetic: 5.36 us -> 2 us  [the longest x8 0.74 us: chunk(): left = jnp.stack([branch, lax.ppermute(branch, 'pair', CORE_SWAP)], axis=2)]
  transfers between devices with their start and end apart: 22 -> 72, of which waited for: 8 -> 22; matrix products, arithmetic and copies ran while one was open for 20% -> 20% of each run, Pallas kernels for 0% -> 0%
where the time goes in v2:
time: 188 us; the launch traced here: 187 us
  starting transfers between devices  103 us (55%)
  waiting for transfers between devices  39.1 us (21%)
  local copies, waits for them, and re-layouts  15.8 us (8%)
  other arithmetic  14.7 us (8%)
  matrix products  11.6 us (6%)
  between operations  2.26 us (1%)
    ppermute x36, starting transfers between devices, line(): lax.ppermute(value, ('batch', 'vocab'), line_pairs(vocab, moves, hop))  65.2 us
    ppermute x36, waiting for transfers between devices, line(): lax.ppermute(value, ('batch', 'vocab'), line_pairs(vocab, moves, hop))  16.5 us
    dot_general x16, matrix products, partial(): jnp.dot(left.reshape(-1, 2 * block), weight[:, low:high], preferred_eleme...  11.6 us
    ppermute x4, waiting for transfers between devices, chunk(): lax.ppermute(partial(left[:, 1], 0, middle).astype(SUM_TYPE), 'batch', X_...  10 us
    ppermute x4, starting transfers between devices, chunk(): next_y = lax.ppermute(sum_x[1].astype(SUM_TYPE), 'batch', Y_SWAP)  6.69 us
    ppermute x4, starting transfers between devices, line_features(): lax.ppermute(lax.dynamic_slice_in_dim(piece, (1 - x) * block, block, 2),...  5.25 us
    ppermute x4, starting transfers between devices, chunk(): lax.ppermute(partial(left[1], middle, width).astype(SUM_TYPE), 'batch', Y...  5.19 us
    ppermute x4, starting transfers between devices, chunk(): lax.ppermute(partial(left[:, 1], 0, middle).astype(SUM_TYPE), 'batch', X_...  4.85 us
  transfers between devices with their start and end apart: 72, of which 22 were waited for; matrix products, arithmetic and copies ran while one was open for 20% of the time, Pallas kernels for 0%

profile of v2, /device:TPU:0, one launch (start us, length us, event | category | flops | bytes accessed | tf_op | source)
XLA Modules:
  0.0 187.0 jit_solution(5781323602032711620)
XLA Ops:
  2.6 3.0 %collective-permute-start = (bf16[2,16,1024]{2,1,0:T(8,128)(2,1)S(1)}, bf16[2,16,1024]{2,1,0:T(8,128)(2,1)S(1)}, u32[]{:S(2)}, u32[]{:S(2)}) collective-permute-start(bf16[2,16,1024]{2,1,0:T(8,128)(2,1)S(1)} %get-tuple-element.59), channel_id=1, source_target_pairs={{0,4},{4,0},{8,12},{12,8},{1,5},{5,1},{9,13},{13,9},{2,6},{6,2},{1... | collective-permute-start | bytes 196616 | tf_op jit(solution)/shard_map/ppermute | solution.py:86
  5.7 2.1 %collective-permute-start.31 = (bf16[2,16,1024]{2,1,0:T(8,128)(2,1)S(1)}, bf16[2,16,1024]{2,1,0:T(8,128)(2,1)S(1)}, u32[]{:S(2)}, u32[]{:S(2)}) collective-permute-start(bf16[2,16,1024]{2,1,0:T(8,128)(2,1)S(1)} %get-tuple-element.67), channel_id=1, source_target_pairs={{0,4},{4,0},{8,12},{12,8},{1,5},{5,1},{9,13},{13,9},{2,6},{6,2},{1... | collective-permute-start | bytes 196616 | tf_op jit(solution)/shard_map/ppermute | solution.py:86
  9.1 2.1 %collective-permute-start.65 = (f32[128]{0:T(128)S(1)}, f32[128]{0:T(128)S(1)}, u32[]{:S(2)}, u32[]{:S(2)}) collective-permute-start(f32[128]{0:T(128)S(1)} %multiply_reduce_fusion), channel_id=1, source_target_pairs={{0,1},{1,0},{2,3},{3,2},{4,5},{5,4},{6,7},{7,6},{8,9},{9,8},{10,11... | collective-permute-start | bytes 1544 | tf_op jit(solution)/shard_map/ppermute | solution.py:64
  11.2 4.8 %constant_dynamic-slice_fusion.5 = bf16[1024,2048]{1,0:T(8,128)(2,1)} fusion(bf16[1024,4096]{1,0:T(8,128)(2,1)} %param.5, s32[]{:T(128)S(6)} %select_n.260), kind=kLoop, calls=%fused_computation.240 | loop fusion | bytes 8388612 | tf_op jit(solution)/shard_map/dynamic_slice | solution.py:57
  16.0 2.6 %collective-permute-start.66 = (f32[128]{0:T(128)S(1)}, f32[128]{0:T(128)S(1)}, u32[]{:S(2)}, u32[]{:S(2)}) collective-permute-start(f32[128]{0:T(128)S(1)} %add.137), channel_id=1, source_target_pairs={{0,2},{1,3},{2,0},{3,1},{4,6},{5,7},{6,4},{7,5},{8,10},{9,11},{10,... | collective-permute-start | bytes 1544 | tf_op jit(solution)/shard_map/ppermute | solution.py:64
  18.6 1.9 collective-permute-done.66
  22.2 4.5 %collective-permute-start.2 = (bf16[2,2,16,1024]{3,2,1,0:T(8,128)(2,1)S(1)}, bf16[2,2,16,1024]{3,2,1,0:T(8,128)(2,1)S(1)}, u32[]{:S(2)}, u32[]{:S(2)}) collective-permute-start(bf16[2,2,16,1024]{3,2,1,0:T(8,128)(2,1)S(1)} %get-tuple-element.57), channel_id=1, source_target_pairs={{0,1},{2,3},{4,5},{6,7},{11,10},{9,8},{15,14},{13,12},{16,17},{18,... | collective-permute-start | bytes 393224 | tf_op jit(solution)/shard_map/ppermute | solution.py:81
  29.3 5.7 %collective-permute-start.18 = (bf16[2,2,16,1024]{3,2,1,0:T(8,128)(2,1)S(1)}, bf16[2,2,16,1024]{3,2,1,0:T(8,128)(2,1)S(1)}, u32[]{:S(2)}, u32[]{:S(2)}) collective-permute-start(bf16[2,2,16,1024]{3,2,1,0:T(8,128)(2,1)S(1)} %get-tuple-element.61), channel_id=1, source_target_pairs={{0,1},{2,3},{4,5},{6,7},{11,10},{9,8},{15,14},{13,12},{16,17},{18,... | collective-permute-start | bytes 393224 | tf_op jit(solution)/shard_map/ppermute | solution.py:81
  41.1 5.8 %collective-permute-start.19 = (bf16[2,2,16,1024]{3,2,1,0:T(8,128)(2,1)S(1)}, bf16[2,2,16,1024]{3,2,1,0:T(8,128)(2,1)S(1)}, u32[]{:S(2)}, u32[]{:S(2)}) collective-permute-start(bf16[2,2,16,1024]{3,2,1,0:T(8,128)(2,1)S(1)} %collective-permute-done.17), channel_id=1, source_target_pairs={{0,1},{4,5},{11,10},{15,14},{16,17},{20,21},{27,26},{31,30}} | collective-permute-start | bytes 393224 | tf_op jit(solution)/shard_map/ppermute | solution.py:81
  53.0 2.1 %collective-permute-done.47 = bf16[2,2,16,1024]{3,2,1,0:T(8,128)(2,1)S(1)} collective-permute-done((bf16[2,2,16,1024]{3,2,1,0:T(8,128)(2,1)S(1)}, bf16[2,2,16,1024]{3,2,1,0:T(8,128)(2,1)S(1)}, u32[]{:S(2)}, u32[]{:S(2)}) %collective-permute-start.47) | collective-permute-done | bytes 131104 | tf_op jit(solution)/shard_map/ppermute | solution.py:81
  55.1 7.0 %collective-permute-start.48 = (bf16[2,2,16,1024]{3,2,1,0:T(8,128)(2,1)S(1)}, bf16[2,2,16,1024]{3,2,1,0:T(8,128)(2,1)S(1)}, u32[]{:S(2)}, u32[]{:S(2)}) collective-permute-start(bf16[2,2,16,1024]{3,2,1,0:T(8,128)(2,1)S(1)} %get-tuple-element.69), channel_id=1, source_target_pairs={{0,1},{2,3},{4,5},{6,7},{11,10},{9,8},{15,14},{13,12},{16,17},{18,... | collective-permute-start | bytes 393224 | tf_op jit(solution)/shard_map/ppermute | solution.py:81
  64.2 2.8 %collective-permute-start.49 = (bf16[2,2,16,1024]{3,2,1,0:T(8,128)(2,1)S(1)}, bf16[2,2,16,1024]{3,2,1,0:T(8,128)(2,1)S(1)}, u32[]{:S(2)}, u32[]{:S(2)}) collective-permute-start(bf16[2,2,16,1024]{3,2,1,0:T(8,128)(2,1)S(1)} %collective-permute-done.47), channel_id=1, source_target_pairs={{0,1},{4,5},{11,10},{15,14},{16,17},{20,21},{27,26},{31,30}} | collective-permute-start | bytes 393224 | tf_op jit(solution)/shard_map/ppermute | solution.py:81
  71.5 2.3 %collective-permute-done.9 = bf16[2,2,16,1024]{3,2,1,0:T(8,128)(2,1)S(1)} collective-permute-done((bf16[2,2,16,1024]{3,2,1,0:T(8,128)(2,1)S(1)}, bf16[2,2,16,1024]{3,2,1,0:T(8,128)(2,1)S(1)}, u32[]{:S(2)}, u32[]{:S(2)}) %collective-permute-start.9) | collective-permute-done | bytes 131104 | tf_op jit(solution)/shard_map/ppermute | solution.py:81
  73.8 4.4 %collective-permute-start.25 = (bf16[2,2,16,1024]{3,2,1,0:T(8,128)(2,1)S(1)}, bf16[2,2,16,1024]{3,2,1,0:T(8,128)(2,1)S(1)}, u32[]{:S(2)}, u32[]{:S(2)}) collective-permute-start(bf16[2,2,16,1024]{3,2,1,0:T(8,128)(2,1)S(1)} %collective-permute-done.22), channel_id=1, source_target_pairs={{0,8},{4,12},{11,3},{15,7},{16,24},{20,28},{27,19},{31,23}} | collective-permute-start | bytes 393224 | tf_op jit(solution)/shard_map/ppermute | solution.py:81
  82.0 4.4 %collective-permute-start.40 = (bf16[2,2,16,1024]{3,2,1,0:T(8,128)(2,1)S(1)}, bf16[2,2,16,1024]{3,2,1,0:T(8,128)(2,1)S(1)}, u32[]{:S(2)}, u32[]{:S(2)}) collective-permute-start(bf16[2,2,16,1024]{3,2,1,0:T(8,128)(2,1)S(1)} %collective-permute-done.37), channel_id=1, source_target_pairs={{0,8},{4,12},{11,3},{15,7},{16,24},{20,28},{27,19},{31,23}} | collective-permute-start | bytes 393224 | tf_op jit(solution)/shard_map/ppermute | solution.py:81
  86.3 1.8 collective-permute-done.24
  92.1 4.3 %collective-permute-done.39 = bf16[2,2,2,16,1024]{4,3,2,1,0:T(8,128)(2,1)S(1)} collective-permute-done((bf16[2,2,2,16,1024]{4,3,2,1,0:T(8,128)(2,1)S(1)}, bf16[2,2,2,16,1024]{4,3,2,1,0:T(8,128)(2,1)S(1)}, u32[]{:S(2)}, u32[]{:S(2)}) %collective-permute-start.39) | collective-permute-done | bytes 262176 | tf_op jit(solution)/shard_map/ppermute | solution.py:81
  100.2 1.6 collective-permute-start.68
  101.8 4.9 %collective-permute-done.54 = bf16[2,2,2,16,1024]{4,3,2,1,0:T(8,128)(2,1)S(1)} collective-permute-done((bf16[2,2,2,16,1024]{4,3,2,1,0:T(8,128)(2,1)S(1)}, bf16[2,2,2,16,1024]{4,3,2,1,0:T(8,128)(2,1)S(1)}, u32[]{:S(2)}, u32[]{:S(2)}) %collective-permute-start.54) | collective-permute-done | bytes 262176 | tf_op jit(solution)/shard_map/ppermute | solution.py:81
  121.0 2.4 %broadcast_select_fusion = (bf16[1024,2048]{1,0:T(8,128)(2,1)S(1)}, bf16[1024,2048]{1,0:T(8,128)(2,1)S(1)}) fusion(bf16[1024,2048]{1,0:T(8,128)(2,1)S(1)} %collective-permute-done.11, pred[]{:T(512)S(6)} %eq.25, bf16[1024,4096]{1,0:T(8,128)(2,1)S(1)} %bitcast.318, s32[]{:T(128)S(6)} %select_n.259), kind=kLoop, calls=%fused_computation.4 | loop fusion | flops 4194304 | bytes 16777220 | tf_op jit(solution)/shard_map/jit(_where)/select_n | solution.py:59
  142.5 1.6 collective-permute-start.42
  144.1 4.7 %collective-permute-done.27 = f16[2,2,2,16,1024]{4,3,2,1,0:T(8,128)(2,1)S(1)} collective-permute-done((f16[2,2,2,16,1024]{4,3,2,1,0:T(8,128)(2,1)S(1)}, f16[2,2,2,16,1024]{4,3,2,1,0:T(8,128)(2,1)S(1)}, u32[]{:S(2)}, u32[]{:S(2)}) %collective-permute-start.27) | collective-permute-done | bytes 262176 | tf_op jit(solution)/shard_map/ppermute | solution.py:132
  148.8 2.1 %collective-permute-start.59 = (f16[2,2,2,16,1024]{4,3,2,1,0:T(8,128)(2,1)S(1)}, f16[2,2,2,16,1024]{4,3,2,1,0:T(8,128)(2,1)S(1)}, u32[]{:S(2)}, u32[]{:S(2)}) collective-permute-start(f16[2,2,2,16,1024]{4,3,2,1,0:T(8,128)(2,1)S(1)} %bitcast.401), channel_id=1, source_target_pairs={{0,8},{8,0},{4,12},{12,4},{1,9},{9,1},{5,13},{13,5},{2,10},{10,2},... | collective-permute-start | bytes 786440 | tf_op jit(solution)/shard_map/ppermute | solution.py:133
  151.7 2.7 %collective-permute-done.42 = f16[2,2,2,16,1024]{4,3,2,1,0:T(8,128)(2,1)S(1)} collective-permute-done((f16[2,2,2,16,1024]{4,3,2,1,0:T(8,128)(2,1)S(1)}, f16[2,2,2,16,1024]{4,3,2,1,0:T(8,128)(2,1)S(1)}, u32[]{:S(2)}, u32[]{:S(2)}) %collective-permute-start.42) | collective-permute-done | bytes 262176 | tf_op jit(solution)/shard_map/ppermute | solution.py:132
  155.7 1.9 collective-permute-start.13
  157.7 2.6 %collective-permute-done.57 = f16[2,2,2,16,1024]{4,3,2,1,0:T(8,128)(2,1)S(1)} collective-permute-done((f16[2,2,2,16,1024]{4,3,2,1,0:T(8,128)(2,1)S(1)}, f16[2,2,2,16,1024]{4,3,2,1,0:T(8,128)(2,1)S(1)}, u32[]{:S(2)}, u32[]{:S(2)}) %collective-permute-start.57) | collective-permute-done | bytes 262176 | tf_op jit(solution)/shard_map/ppermute | solution.py:132
  161.2 1.9 %collective-permute-done.15 = f16[2,2,16,1024]{3,2,1,0:T(8,128)(2,1)S(1)} collective-permute-done((f16[2,2,16,1024]{3,2,1,0:T(8,128)(2,1)S(1)}, f16[2,2,16,1024]{3,2,1,0:T(8,128)(2,1)S(1)}, u32[]{:S(2)}, u32[]{:S(2)}) %collective-permute-start.15) | collective-permute-done | bytes 131104 | tf_op jit(solution)/shard_map/ppermute | solution.py:137
  163.1 1.8 collective-permute-start.28
  166.1 1.6 collective-permute-start.43
  179.3 2.2 %collective-permute-start.70 = (f32[4,64]{1,0:T(4,128)S(1)}, f32[4,64]{1,0:T(4,128)S(1)}, u32[]{:S(2)}, u32[]{:S(2)}) collective-permute-start(f32[4,64]{1,0:T(4,128)S(1)} %get-tuple-element.73), channel_id=1, source_target_pairs={{0,2},{1,3},{2,0},{3,1},{4,6},{5,7},{6,4},{7,5},{8,10},{9,11},{10,... | collective-permute-start | bytes 3080 | tf_op jit(solution)/shard_map/ppermute | solution.py:169
  181.5 1.6 collective-permute-start.71
  185.3 1.6 bitcast_subtract_fusion
  (263 shorter events, 87.9 us)
Async XLA Ops:
  2.6 18.0 %collective-permute-start = (bf16[2,16,1024]{2,1,0:T(8,128)(2,1)S(1)}, bf16[2,16,1024]{2,1,0:T(8,128)(2,1)S(1)}, u32[]{:S(2)}, u32[]{:S(2)}) collective-permute-start(bf16[2,16,1024]{2,1,0:T(8,128)(2,1)S(1)} %get-tuple-element.59), channel_id=1, source_target_pairs={{0,4},{4,0},{8,12},{12,8},{1,5},{5,1},{9,13},{13,9},{2,6},{6,2},{1... | collective-permute-start | bytes 196616 | tf_op jit(solution)/shard_map/ppermute | solution.py:86
  5.6 21.1 %collective-permute-start.16 = (bf16[2,16,1024]{2,1,0:T(8,128)(2,1)S(1)}, bf16[2,16,1024]{2,1,0:T(8,128)(2,1)S(1)}, u32[]{:S(2)}, u32[]{:S(2)}) collective-permute-start(bf16[2,16,1024]{2,1,0:T(8,128)(2,1)S(1)} %get-tuple-element.63), channel_id=1, source_target_pairs={{0,4},{4,0},{8,12},{12,8},{1,5},{5,1},{9,13},{13,9},{2,6},{6,2},{1... | collective-permute-start | bytes 196616 | tf_op jit(solution)/shard_map/ppermute | solution.py:86
  5.7 22.3 %collective-permute-start.31 = (bf16[2,16,1024]{2,1,0:T(8,128)(2,1)S(1)}, bf16[2,16,1024]{2,1,0:T(8,128)(2,1)S(1)}, u32[]{:S(2)}, u32[]{:S(2)}) collective-permute-start(bf16[2,16,1024]{2,1,0:T(8,128)(2,1)S(1)} %get-tuple-element.67), channel_id=1, source_target_pairs={{0,4},{4,0},{8,12},{12,8},{1,5},{5,1},{9,13},{13,9},{2,6},{6,2},{1... | collective-permute-start | bytes 196616 | tf_op jit(solution)/shard_map/ppermute | solution.py:86
  7.8 21.6 %collective-permute-start.46 = (bf16[2,16,1024]{2,1,0:T(8,128)(2,1)S(1)}, bf16[2,16,1024]{2,1,0:T(8,128)(2,1)S(1)}, u32[]{:S(2)}, u32[]{:S(2)}) collective-permute-start(bf16[2,16,1024]{2,1,0:T(8,128)(2,1)S(1)} %get-tuple-element.71), channel_id=1, source_target_pairs={{0,4},{4,0},{8,12},{12,8},{1,5},{5,1},{9,13},{13,9},{2,6},{6,2},{1... | collective-permute-start | bytes 196616 | tf_op jit(solution)/shard_map/ppermute | solution.py:86
  20.6 14.5 %collective-permute-start.1 = (bf16[2,2,16,1024]{3,2,1,0:T(8,128)(2,1)S(1)}, bf16[2,2,16,1024]{3,2,1,0:T(8,128)(2,1)S(1)}, u32[]{:S(2)}, u32[]{:S(2)}) collective-permute-start(bf16[2,2,16,1024]{3,2,1,0:T(8,128)(2,1)S(1)} %get-tuple-element.57), channel_id=1, source_target_pairs={{1,9},{3,11},{5,13},{7,15},{10,2},{8,0},{14,6},{12,4},{17,25},{19,... | collective-permute-start | bytes 393224 | tf_op jit(solution)/shard_map/ppermute | solution.py:81
  22.2 14.3 %collective-permute-start.2 = (bf16[2,2,16,1024]{3,2,1,0:T(8,128)(2,1)S(1)}, bf16[2,2,16,1024]{3,2,1,0:T(8,128)(2,1)S(1)}, u32[]{:S(2)}, u32[]{:S(2)}) collective-permute-start(bf16[2,2,16,1024]{3,2,1,0:T(8,128)(2,1)S(1)} %get-tuple-element.57), channel_id=1, source_target_pairs={{0,1},{2,3},{4,5},{6,7},{11,10},{9,8},{15,14},{13,12},{16,17},{18,... | collective-permute-start | bytes 393224 | tf_op jit(solution)/shard_map/ppermute | solution.py:81
  26.7 11.1 %collective-permute-start.6 = (bf16[2,2,16,1024]{3,2,1,0:T(8,128)(2,1)S(1)}, bf16[2,2,16,1024]{3,2,1,0:T(8,128)(2,1)S(1)}, u32[]{:S(2)}, u32[]{:S(2)}) collective-permute-start(bf16[2,2,16,1024]{3,2,1,0:T(8,128)(2,1)S(1)} %get-tuple-element.57), channel_id=1, source_target_pairs={{2,1},{1,0},{6,5},{5,4},{9,10},{10,11},{13,14},{14,15},{18,17},{17... | collective-permute-start | bytes 393224 | tf_op jit(solution)/shard_map/ppermute | solution.py:81
  28.0 11.0 %collective-permute-start.17 = (bf16[2,2,16,1024]{3,2,1,0:T(8,128)(2,1)S(1)}, bf16[2,2,16,1024]{3,2,1,0:T(8,128)(2,1)S(1)}, u32[]{:S(2)}, u32[]{:S(2)}) collective-permute-start(bf16[2,2,16,1024]{3,2,1,0:T(8,128)(2,1)S(1)} %get-tuple-element.61), channel_id=1, source_target_pairs={{1,9},{3,11},{5,13},{7,15},{10,2},{8,0},{14,6},{12,4},{17,25},{19,... | collective-permute-start | bytes 393224 | tf_op jit(solution)/shard_map/ppermute | solution.py:81
  29.3 10.4 %collective-permute-start.18 = (bf16[2,2,16,1024]{3,2,1,0:T(8,128)(2,1)S(1)}, bf16[2,2,16,1024]{3,2,1,0:T(8,128)(2,1)S(1)}, u32[]{:S(2)}, u32[]{:S(2)}) collective-permute-start(bf16[2,2,16,1024]{3,2,1,0:T(8,128)(2,1)S(1)} %get-tuple-element.61), channel_id=1, source_target_pairs={{0,1},{2,3},{4,5},{6,7},{11,10},{9,8},{15,14},{13,12},{16,17},{18,... | collective-permute-start | bytes 393224 | tf_op jit(solution)/shard_map/ppermute | solution.py:81
  36.4 10.5 %collective-permute-start.22 = (bf16[2,2,16,1024]{3,2,1,0:T(8,128)(2,1)S(1)}, bf16[2,2,16,1024]{3,2,1,0:T(8,128)(2,1)S(1)}, u32[]{:S(2)}, u32[]{:S(2)}) collective-permute-start(bf16[2,2,16,1024]{3,2,1,0:T(8,128)(2,1)S(1)} %get-tuple-element.61), channel_id=1, source_target_pairs={{2,1},{1,0},{6,5},{5,4},{9,10},{10,11},{13,14},{14,15},{18,17},{17... | collective-permute-start | bytes 393224 | tf_op jit(solution)/shard_map/ppermute | solution.py:81
  37.8 10.5 %collective-permute-start.32 = (bf16[2,2,16,1024]{3,2,1,0:T(8,128)(2,1)S(1)}, bf16[2,2,16,1024]{3,2,1,0:T(8,128)(2,1)S(1)}, u32[]{:S(2)}, u32[]{:S(2)}) collective-permute-start(bf16[2,2,16,1024]{3,2,1,0:T(8,128)(2,1)S(1)} %get-tuple-element.65), channel_id=1, source_target_pairs={{1,9},{3,11},{5,13},{7,15},{10,2},{8,0},{14,6},{12,4},{17,25},{19,... | collective-permute-start | bytes 393224 | tf_op jit(solution)/shard_map/ppermute | solution.py:81
  39.1 10.5 %collective-permute-start.7 = (bf16[2,2,16,1024]{3,2,1,0:T(8,128)(2,1)S(1)}, bf16[2,2,16,1024]{3,2,1,0:T(8,128)(2,1)S(1)}, u32[]{:S(2)}, u32[]{:S(2)}) collective-permute-start(bf16[2,2,16,1024]{3,2,1,0:T(8,128)(2,1)S(1)} %collective-permute-done.1), channel_id=1, source_target_pairs={{2,1},{6,5},{9,10},{13,14},{18,17},{22,21},{25,26},{29,30}} | collective-permute-start | bytes 393224 | tf_op jit(solution)/shard_map/ppermute | solution.py:81
  39.8 10.5 %collective-permute-start.37 = (bf16[2,2,16,1024]{3,2,1,0:T(8,128)(2,1)S(1)}, bf16[2,2,16,1024]{3,2,1,0:T(8,128)(2,1)S(1)}, u32[]{:S(2)}, u32[]{:S(2)}) collective-permute-start(bf16[2,2,16,1024]{3,2,1,0:T(8,128)(2,1)S(1)} %get-tuple-element.65), channel_id=1, source_target_pairs={{2,1},{1,0},{6,5},{5,4},{9,10},{10,11},{13,14},{14,15},{18,17},{17... | collective-permute-start | bytes 393224 | tf_op jit(solution)/shard_map/ppermute | solution.py:81
  41.1 9.9 %collective-permute-start.19 = (bf16[2,2,16,1024]{3,2,1,0:T(8,128)(2,1)S(1)}, bf16[2,2,16,1024]{3,2,1,0:T(8,128)(2,1)S(1)}, u32[]{:S(2)}, u32[]{:S(2)}) collective-permute-start(bf16[2,2,16,1024]{3,2,1,0:T(8,128)(2,1)S(1)} %collective-permute-done.17), channel_id=1, source_target_pairs={{0,1},{4,5},{11,10},{15,14},{16,17},{20,21},{27,26},{31,30}} | collective-permute-start | bytes 393224 | tf_op jit(solution)/shard_map/ppermute | solution.py:81
  49.6 12.5 %collective-permute-start.23 = (bf16[2,2,16,1024]{3,2,1,0:T(8,128)(2,1)S(1)}, bf16[2,2,16,1024]{3,2,1,0:T(8,128)(2,1)S(1)}, u32[]{:S(2)}, u32[]{:S(2)}) collective-permute-start(bf16[2,2,16,1024]{3,2,1,0:T(8,128)(2,1)S(1)} %collective-permute-done.17), channel_id=1, source_target_pairs={{2,1},{6,5},{9,10},{13,14},{18,17},{22,21},{25,26},{29,30}} | collective-permute-start | bytes 393224 | tf_op jit(solution)/shard_map/ppermute | solution.py:81
  50.3 13.2 %collective-permute-start.38 = (bf16[2,2,16,1024]{3,2,1,0:T(8,128)(2,1)S(1)}, bf16[2,2,16,1024]{3,2,1,0:T(8,128)(2,1)S(1)}, u32[]{:S(2)}, u32[]{:S(2)}) collective-permute-start(bf16[2,2,16,1024]{3,2,1,0:T(8,128)(2,1)S(1)} %collective-permute-done.32), channel_id=1, source_target_pairs={{2,1},{6,5},{9,10},{13,14},{18,17},{22,21},{25,26},{29,30}} | collective-permute-start | bytes 393224 | tf_op jit(solution)/shard_map/ppermute | solution.py:81
  51.0 18.1 %collective-permute-start.4 = (bf16[2,2,2,16,1024]{4,3,2,1,0:T(8,128)(2,1)S(1)}, bf16[2,2,2,16,1024]{4,3,2,1,0:T(8,128)(2,1)S(1)}, u32[]{:S(2)}, u32[]{:S(2)}) collective-permute-start(bf16[2,2,2,16,1024]{4,3,2,1,0:T(8,128)(2,1)S(1)} %pad_maximum_fusion.13), channel_id=1, source_target_pairs={{1,2},{5,6},{10,9},{14,13},{17,18},{21,22},{26,25},{30,29}} | collective-permute-start | bytes 786440 | tf_op jit(solution)/shard_map/ppermute | solution.py:81
  51.7 12.5 %collective-permute-start.52 = (bf16[2,2,16,1024]{3,2,1,0:T(8,128)(2,1)S(1)}, bf16[2,2,16,1024]{3,2,1,0:T(8,128)(2,1)S(1)}, u32[]{:S(2)}, u32[]{:S(2)}) collective-permute-start(bf16[2,2,16,1024]{3,2,1,0:T(8,128)(2,1)S(1)} %get-tuple-element.69), channel_id=1, source_target_pairs={{2,1},{1,0},{6,5},{5,4},{9,10},{10,11},{13,14},{14,15},{18,17},{17... | collective-permute-start | bytes 393224 | tf_op jit(solution)/shard_map/ppermute | solution.py:81
  55.1 11.9 %collective-permute-start.48 = (bf16[2,2,16,1024]{3,2,1,0:T(8,128)(2,1)S(1)}, bf16[2,2,16,1024]{3,2,1,0:T(8,128)(2,1)S(1)}, u32[]{:S(2)}, u32[]{:S(2)}) collective-permute-start(bf16[2,2,16,1024]{3,2,1,0:T(8,128)(2,1)S(1)} %get-tuple-element.69), channel_id=1, source_target_pairs={{0,1},{2,3},{4,5},{6,7},{11,10},{9,8},{15,14},{13,12},{16,17},{18,... | collective-permute-start | bytes 393224 | tf_op jit(solution)/shard_map/ppermute | solution.py:81
  67.0 11.2 %collective-permute-start.8 = (bf16[2,2,2,16,1024]{4,3,2,1,0:T(8,128)(2,1)S(1)}, bf16[2,2,2,16,1024]{4,3,2,1,0:T(8,128)(2,1)S(1)}, u32[]{:S(2)}, u32[]{:S(2)}) collective-permute-start(bf16[2,2,2,16,1024]{4,3,2,1,0:T(8,128)(2,1)S(1)} %pad_maximum_fusion.21), channel_id=1, source_target_pairs={{1,0},{5,4},{10,11},{14,15},{17,16},{21,20},{26,27},{30,31}} | collective-permute-start | bytes 786440 | tf_op jit(solution)/shard_map/ppermute | solution.py:81
  68.4 11.2 %collective-permute-start.20 = (bf16[2,2,2,16,1024]{4,3,2,1,0:T(8,128)(2,1)S(1)}, bf16[2,2,2,16,1024]{4,3,2,1,0:T(8,128)(2,1)S(1)}, u32[]{:S(2)}, u32[]{:S(2)}) collective-permute-start(bf16[2,2,2,16,1024]{4,3,2,1,0:T(8,128)(2,1)S(1)} %pad_maximum_fusion.15), channel_id=1, source_target_pairs={{1,2},{5,6},{10,9},{14,13},{17,18},{21,22},{26,25},{30,29}} | collective-permute-start | bytes 786440 | tf_op jit(solution)/shard_map/ppermute | solution.py:81
  69.0 11.2 %collective-permute-start.5 = (bf16[2,2,2,16,1024]{4,3,2,1,0:T(8,128)(2,1)S(1)}, bf16[2,2,2,16,1024]{4,3,2,1,0:T(8,128)(2,1)S(1)}, u32[]{:S(2)}, u32[]{:S(2)}) collective-permute-start(bf16[2,2,2,16,1024]{4,3,2,1,0:T(8,128)(2,1)S(1)} %collective-permute-done.4), channel_id=1, source_target_pairs={{2,3},{6,7},{9,8},{13,12},{18,19},{22,23},{25,24},{29,28}} | collective-permute-start | bytes 786440 | tf_op jit(solution)/shard_map/ppermute | solution.py:81
  71.4 49.6 %collective-permute-start.11 = (bf16[1024,2048]{1,0:T(8,128)(2,1)S(1)}, bf16[1024,2048]{1,0:T(8,128)(2,1)S(1)}, u32[]{:S(2)}, u32[]{:S(2)}) collective-permute-start(bf16[1024,2048]{1,0:T(8,128)(2,1)S(1)} %copy-done), channel_id=1, source_target_pairs={{0,16},{16,0},{1,17},{17,1},{2,18},{18,2},{3,19},{19,3},{4,20},{20... | collective-permute-start | bytes 12582920 | tf_op jit(solution)/shard_map/ppermute | solution.py:58
  78.3 9.9 %collective-permute-start.24 = (bf16[2,2,2,16,1024]{4,3,2,1,0:T(8,128)(2,1)S(1)}, bf16[2,2,2,16,1024]{4,3,2,1,0:T(8,128)(2,1)S(1)}, u32[]{:S(2)}, u32[]{:S(2)}) collective-permute-start(bf16[2,2,2,16,1024]{4,3,2,1,0:T(8,128)(2,1)S(1)} %pad_maximum_fusion.23), channel_id=1, source_target_pairs={{1,0},{5,4},{10,11},{14,15},{17,16},{21,20},{26,27},{30,31}} | collective-permute-start | bytes 786440 | tf_op jit(solution)/shard_map/ppermute | solution.py:81
  91.4 84.3 %collective-permute-start.67 = (f32[64]{0:T(128)S(1)}, f32[64]{0:T(128)S(1)}, u32[]{:S(2)}, u32[]{:S(2)}) collective-permute-start(f32[64]{0:T(128)S(1)} %get-tuple-element.78), channel_id=1, source_target_pairs={{0,0},{4,8},{8,16},{12,24},{16,4},{20,12},{24,20},{28,28},{1,1},{5... | collective-permute-start | bytes 776 | tf_op jit(solution)/shard_map/ppermute | solution.py:68
  100.2 76.1 %collective-permute-start.68 = (f32[64]{0:T(128)S(1)}, f32[64]{0:T(128)S(1)}, u32[]{:S(2)}, u32[]{:S(2)}) collective-permute-start(f32[64]{0:T(128)S(1)} %get-tuple-element.79), channel_id=1, source_target_pairs={{0,4},{4,12},{8,20},{12,28},{16,0},{20,8},{24,16},{28,24},{1,5},{5... | collective-permute-start | bytes 776 | tf_op jit(solution)/shard_map/ppermute | solution.py:68
  125.4 14.1 %collective-permute-start.14 = (f16[2,2,2,16,1024]{4,3,2,1,0:T(8,128)(2,1)S(1)}, f16[2,2,2,16,1024]{4,3,2,1,0:T(8,128)(2,1)S(1)}, u32[]{:S(2)}, u32[]{:S(2)}) collective-permute-start(f16[2,2,2,16,1024]{4,3,2,1,0:T(8,128)(2,1)S(1)} %bitcast.407), channel_id=1, source_target_pairs={{0,8},{8,0},{4,12},{12,4},{1,9},{9,1},{5,13},{13,5},{2,10},{10,2},... | collective-permute-start | bytes 786440 | tf_op jit(solution)/shard_map/ppermute | solution.py:133
  128.4 12.4 %collective-permute-start.12 = (f16[2,2,2,16,1024]{4,3,2,1,0:T(8,128)(2,1)S(1)}, f16[2,2,2,16,1024]{4,3,2,1,0:T(8,128)(2,1)S(1)}, u32[]{:S(2)}, u32[]{:S(2)}) collective-permute-start(f16[2,2,2,16,1024]{4,3,2,1,0:T(8,128)(2,1)S(1)} %bitcast.406), channel_id=1, source_target_pairs={{0,4},{4,0},{8,12},{12,8},{1,5},{5,1},{9,13},{13,9},{2,6},{6,2},{1... | collective-permute-start | bytes 786440 | tf_op jit(solution)/shard_map/ppermute | solution.py:132
  131.4 11.0 %collective-permute-start.29 = (f16[2,2,2,16,1024]{4,3,2,1,0:T(8,128)(2,1)S(1)}, f16[2,2,2,16,1024]{4,3,2,1,0:T(8,128)(2,1)S(1)}, u32[]{:S(2)}, u32[]{:S(2)}) collective-permute-start(f16[2,2,2,16,1024]{4,3,2,1,0:T(8,128)(2,1)S(1)} %bitcast.405), channel_id=1, source_target_pairs={{0,8},{8,0},{4,12},{12,4},{1,9},{9,1},{5,13},{13,5},{2,10},{10,2},... | collective-permute-start | bytes 786440 | tf_op jit(solution)/shard_map/ppermute | solution.py:133
  140.8 10.1 %collective-permute-start.44 = (f16[2,2,2,16,1024]{4,3,2,1,0:T(8,128)(2,1)S(1)}, f16[2,2,2,16,1024]{4,3,2,1,0:T(8,128)(2,1)S(1)}, u32[]{:S(2)}, u32[]{:S(2)}) collective-permute-start(f16[2,2,2,16,1024]{4,3,2,1,0:T(8,128)(2,1)S(1)} %bitcast.403), channel_id=1, source_target_pairs={{0,8},{8,0},{4,12},{12,4},{1,9},{9,1},{5,13},{13,5},{2,10},{10,2},... | collective-permute-start | bytes 786440 | tf_op jit(solution)/shard_map/ppermute | solution.py:133
  142.5 12.0 %collective-permute-start.42 = (f16[2,2,2,16,1024]{4,3,2,1,0:T(8,128)(2,1)S(1)}, f16[2,2,2,16,1024]{4,3,2,1,0:T(8,128)(2,1)S(1)}, u32[]{:S(2)}, u32[]{:S(2)}) collective-permute-start(f16[2,2,2,16,1024]{4,3,2,1,0:T(8,128)(2,1)S(1)} %bitcast.402), channel_id=1, source_target_pairs={{0,4},{4,0},{8,12},{12,8},{1,5},{5,1},{9,13},{13,9},{2,6},{6,2},{1... | collective-permute-start | bytes 786440 | tf_op jit(solution)/shard_map/ppermute | solution.py:132
  155.7 10.4 %collective-permute-start.13 = (f16[2,2,16,1024]{3,2,1,0:T(8,128)(2,1)S(1)}, f16[2,2,16,1024]{3,2,1,0:T(8,128)(2,1)S(1)}, u32[]{:S(2)}, u32[]{:S(2)}) collective-permute-start(f16[2,2,16,1024]{3,2,1,0:T(8,128)(2,1)S(1)} %fusion.65), channel_id=1, source_target_pairs={{0,8},{8,0},{4,12},{12,4},{1,9},{9,1},{5,13},{13,5},{2,10},{10,2},... | collective-permute-start | bytes 393224 | tf_op jit(solution)/shard_map/ppermute | solution.py:136
  (43 other events, 302.8 us)

commit v3 on v2

v3 whole, which is shorter than its diff:
```python
import jax
import jax.numpy as jnp
from jax import lax
from jax.sharding import PartitionSpec as P

EPS = 1e-05
GUIDE = 1.5
CHUNKS = 2
SHRINK = 1.0 / 32.0
SUM_TYPE = jnp.float16

X_SWAP = [(0, 1), (1, 0), (2, 3), (3, 2)]
Y_SWAP = [(0, 2), (2, 0), (1, 3), (3, 1)]
CORE_SWAP = [(0, 1), (1, 0)]


def pick(array, index, axis):
    return lax.dynamic_index_in_dim(array, index, axis, keepdims=False)


def after(value, *others):
    return lax.optimization_barrier((value, *others))[0]


def on_device(hidden, norm_gain, head_weight):
    core = lax.axis_index("pair")
    place = lax.axis_index("batch")
    level = lax.axis_index("vocab")
    vocab = lax.axis_size("vocab")
    y, x = place // 2, place % 2
    rows = hidden[0]
    seg = rows.shape[0] // 2
    depth = rows.shape[1]
    block, columns = head_weight.shape
    width = columns // 2
    model = depth * vocab
    step = seg // CHUNKS

    wide = rows.astype(jnp.float32)
    gained = (wide * norm_gain.astype(jnp.float32)[None, :]).astype(jnp.bfloat16)
    gained = gained.reshape(2, seg, depth)

    diagonal = [
        pair
        for b in range(2)
        for z in range(1, vocab, 2)
        for pair in (
            (b * vocab + z, (b + 2) * vocab + z - 1),
            ((b + 2) * vocab + z - 1, b * vocab + z),
        )
    ]

    def line_features(c):
        piece = gained[:, c * step : (c + 1) * step]
        mine = lax.dynamic_slice_in_dim(piece, x * block, block, 2)
        other = lax.ppermute(
            lax.dynamic_slice_in_dim(piece, (1 - x) * block, block, 2), "batch", X_SWAP
        )
        own = jnp.stack([jnp.where(x == 0, mine, other), jnp.where(x == 0, other, mine)])
        moved = lax.ppermute(own, ("batch", "vocab"), diagonal)
        held = jnp.where((level + y) % 2 == 1, moved, own)
        whole = lax.all_gather(held.reshape(-1, block), "vocab", axis=0, tiled=True)
        return whole.reshape(2, 2, 2, 2, step, block), other, held

    def gathered_features(c):
        piece = gained[:, c * step : (c + 1) * step]
        whole = lax.all_gather(piece, "vocab", axis=2, tiled=True)
        whole = whole.reshape(2, step, 2, 4, block).transpose(3, 2, 0, 1, 4)
        whole = lax.all_to_all(whole, "batch", split_axis=0, concat_axis=0)
        whole = whole.reshape(2, 2, 2, 2, step, block).transpose(2, 0, 1, 3, 4, 5)
        return whole, piece, piece

    features = line_features if depth == 2 * block and vocab == 4 else gathered_features
    found = [features(c) for c in range(CHUNKS)]

    side = after(core, found[0][1])
    give = lax.dynamic_slice_in_dim(head_weight, (1 - side) * width, width, 1)
    take = lax.ppermute(give, "pair", CORE_SWAP)
    keep = lax.dynamic_slice_in_dim(head_weight, side * width, width, 1)

    squares = jnp.sum(wide * wide, axis=1)
    reach = 1
    while reach < vocab:
        squares += lax.ppermute(squares, "vocab", [(i, i ^ reach) for i in range(vocab)])
        reach *= 2
    squares = squares.reshape(2, seg)
    sent = [
        lax.ppermute(
            pick(squares, core ^ k, 0),
            ("pair", "batch"),
            [(4 * s + b, 2 * b + (s ^ k)) for s in range(2) for b in range(4)],
        )
        for k in range(2)
    ]
    total_sq = jnp.stack([jnp.where(x == 0, sent[0], sent[1]), jnp.where(x == 0, sent[1], sent[0])])
    scale = lax.rsqrt(total_sq / model + EPS) / SHRINK

    def partial(left, low, high):
        lead = left.shape[1:-1]
        out = jnp.dot(
            pick(left, core, 0).reshape(-1, block),
            keep[:, low:high],
            preferred_element_type=jnp.float32,
        ) + jnp.dot(
            pick(left, 1 - core, 0).reshape(-1, block),
            take[:, low:high],
            preferred_element_type=jnp.float32,
        )
        return (out * SHRINK).reshape(*lead, high - low)

    def reduced(left):
        middle = width // 2
        away_x = lax.ppermute(
            partial(pick(left, 1 - x, 3), 0, middle).astype(SUM_TYPE), "batch", X_SWAP
        )
        away_y = lax.ppermute(
            partial(pick(left, 1 - y, 2), middle, width).astype(SUM_TYPE), "batch", Y_SWAP
        )
        sum_x = partial(pick(left, x, 3), 0, middle) + away_x.astype(jnp.float32)
        sum_y = partial(pick(left, y, 2), middle, width) + away_y.astype(jnp.float32)
        next_y = lax.ppermute(pick(sum_x, 1 - y, 1).astype(SUM_TYPE), "batch", Y_SWAP)
        next_x = lax.ppermute(pick(sum_y, 1 - x, 1).astype(SUM_TYPE), "batch", X_SWAP)
        return jnp.concatenate(
            [
                pick(sum_x, y, 1) + next_y.astype(jnp.float32),
                pick(sum_y, x, 1) + next_x.astype(jnp.float32),
            ],
            axis=-1,
        ).astype(SUM_TYPE)

    def chunk(c, *earlier):
        ready = [found[c + 1][2]] if c + 1 < CHUNKS else []
        own = after(found[c][0], *earlier, *ready)
        other = lax.ppermute(own, "pair", CORE_SWAP)
        sums = jnp.stack([reduced(own), reduced(other)])
        return pick(sums, core, 1), lax.ppermute(pick(sums, 1 - core, 1), "pair", CORE_SWAP)

    pieces = [chunk(0)]
    for c in range(1, CHUNKS):
        pieces.append(chunk(c, *pieces[-1]))
    mine = jnp.concatenate([piece[0] for piece in pieces], axis=1)
    theirs = jnp.concatenate([piece[1] for piece in pieces], axis=1)

    def scores(own, other, got_own, got_other, gain):
        low = jnp.where(core == 0, own, got_own)
        high = jnp.where(core == 0, got_other, other)
        return jnp.concatenate([low, high], axis=1).astype(jnp.float32) * gain[:, None]

    cond = scores(mine[0], mine[1], theirs[0], theirs[1], scale[0])
    uncond = scores(mine[1], mine[0], theirs[1], theirs[0], scale[1])
    guided = GUIDE * cond + (1.0 - GUIDE) * uncond

    def stats(values):
        peak = jnp.max(values, axis=1)
        return peak, jnp.sum(jnp.exp(values - peak[:, None]), axis=1)

    peak_c, sum_c = stats(cond)
    peak_g, sum_g = stats(guided)
    own = jnp.stack([peak_c, peak_g, sum_c, sum_g])
    every = jnp.stack(
        [own]
        + [
            lax.ppermute(own, "vocab", [(i, (i + k) % vocab) for i in range(vocab)])
            for k in range(1, vocab)
        ]
    )
    top = jnp.max(every[:, :2], axis=0)
    total = jnp.sum(every[:, 2:] * jnp.exp(every[:, :2] - top[None]), axis=0)
    norm = top + jnp.log(total)
    return (guided - norm[1][:, None], cond - norm[0][:, None])


def solution(mesh):
    in_specs = (P("pair", "batch", "vocab"), P("vocab"), P(("pair", "batch"), "vocab"))
    out_specs = (P(("pair", "batch"), "vocab"), P(("pair", "batch"), "vocab"))
    return jax.shard_map(
        on_device, mesh=mesh, in_specs=in_specs, out_specs=out_specs, check_vma=False
    )
```

time: 188 us -> 187 us (level)
  starting transfers between devices: 103 us -> 50.3 us
  matrix products: 11.6 us -> 51.9 us
  between operations: 2.26 us -> 15 us
  waiting for transfers between devices: 39.1 us -> 48.6 us
  other arithmetic: 14.7 us -> 8.94 us
  local copies, waits for them, and re-layouts: 15.8 us -> 11.1 us
    ppermute x60 -> x22, starting transfers between devices: 87.2 us -> 19.7 us  [the longest x4 5.67 us: reduced(): lax.ppermute(pick(sum_x, 1 - y, 1).astype(SUM_TYPE), 'batch', Y_SWAP)]
    dot_general x16 -> x32, matrix products: 11.6 us -> 51.9 us  [the longest x16 33 us: partial(): jnp.dot(pick(left, 1 - core, 0).reshape(-1, block), take[:, low:high], pr...]
    ppermute x2, starting transfers between devices: 4.73 us -> 17.1 us  [on_device(): lax.ppermute(squares, 'vocab', [(i, i ^ reach) for i in range(vocab)])]
    ppermute x60 -> x22, waiting for transfers between devices: 35.1 us -> 23.5 us  [the longest x4 7.74 us: reduced(): lax.ppermute(pick(sum_y, 1 - x, 1).astype(SUM_TYPE), 'batch', X_SWAP)]
    all_gather x0 -> x2, waiting for transfers between devices: none -> 9.49 us  [line_features(): whole = lax.all_gather(held.reshape(-1, block), 'vocab', axis=0, tiled=True)]
    slice x17 -> x1, local copies, waits for them, and re-layouts: 8.92 us -> 0.04 us  [line_features(): piece = gained[:, c * step:(c + 1) * step]]
    ppermute x4 -> x2, waiting for transfers between devices: 0.01 us -> 7.66 us  [line_features(): lax.ppermute(lax.dynamic_slice_in_dim(piece, (1 - x) * block, block, 2),...]
    dynamic_slice x1 -> x11, local copies, waits for them, and re-layouts: 4.79 us -> 10.4 us  [the longest x8 5.54 us: pick(): return lax.dynamic_index_in_dim(array, index, axis, keepdims=False)]
  transfers between devices with their start and end apart: 72 -> 34, of which waited for: 22 -> 20; matrix products, arithmetic and copies ran while one was open for 20% -> 30% of each run, Pallas kernels for 0% -> 0%
where the time goes in v3:
time: 187 us; the launch traced here: 186 us
  matrix products  51.9 us (28%)
  starting transfers between devices  50.3 us (27%)
  waiting for transfers between devices  48.6 us (26%)
  between operations  15 us (8%)
  local copies, waits for them, and re-layouts  11.1 us (6%)
  other arithmetic  8.94 us (5%)
    dot_general x16, matrix products, partial(): jnp.dot(pick(left, 1 - core, 0).reshape(-1, block), take[:, low:high], pr...  33 us
    dot_general x16, matrix products, partial(): jnp.dot(pick(left, core, 0).reshape(-1, block), keep[:, low:high], prefer...  19 us
    ppermute x2, starting transfers between devices, on_device(): lax.ppermute(squares, 'vocab', [(i, i ^ reach) for i in range(vocab)])  17.1 us
    all_gather x2, waiting for transfers between devices, line_features(): whole = lax.all_gather(held.reshape(-1, block), 'vocab', axis=0, tiled=True)  9.49 us
    ppermute x4, waiting for transfers between devices, reduced(): lax.ppermute(pick(sum_y, 1 - x, 1).astype(SUM_TYPE), 'batch', X_SWAP)  7.74 us
    ppermute x2, waiting for transfers between devices, line_features(): lax.ppermute(lax.dynamic_slice_in_dim(piece, (1 - x) * block, block, 2),...  7.66 us
    ppermute x4, waiting for transfers between devices, reduced(): lax.ppermute(partial(pick(left, 1 - y, 2), middle, width).astype(SUM_TYPE...  7.36 us
    ppermute x2, waiting for transfers between devices, on_device(): lax.ppermute(squares, 'vocab', [(i, i ^ reach) for i in range(vocab)])  6.58 us
  transfers between devices with their start and end apart: 34, of which 20 were waited for; matrix products, arithmetic and copies ran while one was open for 30% of the time, Pallas kernels for 0%

profile of v3, /device:TPU:0, one launch (start us, length us, event | category | flops | bytes accessed | tf_op | source)
XLA Modules:
  0.0 185.9 jit_solution(11173153507013628904)
XLA Ops:
  9.1 3.0 %collective-permute-start = (bf16[2,32,1024]{2,1,0:T(8,128)(2,1)S(1)}, bf16[2,32,1024]{2,1,0:T(8,128)(2,1)S(1)}, u32[]{:S(2)}, u32[]{:S(2)}) collective-permute-start(bf16[2,32,1024]{2,1,0:T(8,128)(2,1)S(1)} %constant_dynamic-slice_fusion.36), channel_id=1, source_target_pairs={{0,4},{4,0},{8,12},{12,8},{1,5},{5,1},{9,13},{13,9},{2,6},{6,2},{1... | collective-permute-start | bytes 393224 | tf_op jit(solution)/shard_map/ppermute | solution.py:56
  12.1 3.5 %collective-permute-done = bf16[2,32,1024]{2,1,0:T(8,128)(2,1)S(1)} collective-permute-done((bf16[2,32,1024]{2,1,0:T(8,128)(2,1)S(1)}, bf16[2,32,1024]{2,1,0:T(8,128)(2,1)S(1)}, u32[]{:S(2)}, u32[]{:S(2)}) %collective-permute-start) | collective-permute-done | bytes 131104 | tf_op jit(solution)/shard_map/ppermute | solution.py:56
  15.6 4.8 %constant_dynamic-slice_fusion.32 = bf16[1024,2048]{1,0:T(8,128)(2,1)} fusion(bf16[1024,4096]{1,0:T(8,128)(2,1)} %param.5, s32[]{:T(128)S(6)} %select_n.230), kind=kLoop, calls=%fused_computation.215 | loop fusion | bytes 8388612 | tf_op jit(solution)/shard_map/dynamic_slice | solution.py:77
  22.3 4.2 %collective-permute-done.2 = bf16[2,32,1024]{2,1,0:T(8,128)(2,1)S(1)} collective-permute-done((bf16[2,32,1024]{2,1,0:T(8,128)(2,1)S(1)}, bf16[2,32,1024]{2,1,0:T(8,128)(2,1)S(1)}, u32[]{:S(2)}, u32[]{:S(2)}) %collective-permute-start.2) | collective-permute-done | bytes 131104 | tf_op jit(solution)/shard_map/ppermute | solution.py:56
  29.1 14.5 %collective-permute-start.25 = (f32[128]{0:T(128)S(1)}, f32[128]{0:T(128)S(1)}, u32[]{:S(2)}, u32[]{:S(2)}) collective-permute-start(f32[128]{0:T(128)S(1)} %multiply_reduce_fusion), channel_id=1, source_target_pairs={{0,1},{1,0},{2,3},{3,2},{4,5},{5,4},{6,7},{7,6},{8,9},{9,8},{10,11... | collective-permute-start | bytes 1544 | tf_op jit(solution)/shard_map/ppermute | solution.py:84
  43.6 4.7 %collective-permute-done.25 = f32[128]{0:T(128)S(1)} collective-permute-done((f32[128]{0:T(128)S(1)}, f32[128]{0:T(128)S(1)}, u32[]{:S(2)}, u32[]{:S(2)}) %collective-permute-start.25) | collective-permute-done | bytes 544 | tf_op jit(solution)/shard_map/ppermute | solution.py:84
  48.3 2.6 %collective-permute-start.26 = (f32[128]{0:T(128)S(1)}, f32[128]{0:T(128)S(1)}, u32[]{:S(2)}, u32[]{:S(2)}) collective-permute-start(f32[128]{0:T(128)S(1)} %add.471), channel_id=1, source_target_pairs={{0,2},{1,3},{2,0},{3,1},{4,6},{5,7},{6,4},{7,5},{8,10},{9,11},{10,... | collective-permute-start | bytes 1544 | tf_op jit(solution)/shard_map/ppermute | solution.py:84
  53.6 3.0 %collective-permute-start.28 = (f32[64]{0:T(128)S(1)}, f32[64]{0:T(128)S(1)}, u32[]{:S(2)}, u32[]{:S(2)}) collective-permute-start(f32[64]{0:T(128)S(1)} %get-tuple-element.66), channel_id=1, source_target_pairs={{0,4},{4,12},{8,20},{12,28},{16,0},{20,8},{24,16},{28,24},{1,5},{5... | collective-permute-start | bytes 776 | tf_op jit(solution)/shard_map/ppermute | solution.py:88
  57.3 9.5 %all-gather.3.cloned.1.call-done = bf16[512,1024]{1,0:T(8,128)(2,1)} async-done(((bf16[128,1024]{1,0:T(8,128)(2,1)}), bf16[512,1024]{1,0:T(8,128)(2,1)}) %all-gather.3.cloned.1.call-update) | async-done | bytes 1048592 | tf_op jit(solution)/shard_map/all_gather | solution.py:62
  69.4 2.0 %fusion.70 = f32[128,1024]{1,0:T(8,128)S(1)} fusion(bf16[128,1024]{1,0:T(8,128)(2,1)S(1)} %bitcast.243, bf16[1024,4096]{1,0:T(8,128)(2,1)} %param.5, s32[]{:T(128)S(6)} %select_n.227), kind=kOutput, calls=%fused_computation.106 | convolution fusion | flops 268435456 | bytes 2883588 | tf_op jit(solution)/shard_map/dot_general | solution.py:100
  73.5 2.1 %fusion.58 = f32[128,1024]{1,0:T(8,128)S(1)} fusion(bf16[128,1024]{1,0:T(8,128)(2,1)S(1)} %bitcast.245, bf16[1024,4096]{1,0:T(8,128)(2,1)} %param.5, s32[]{:T(128)S(6)} %add.478), kind=kOutput, calls=%fused_computation.94 | convolution fusion | flops 268435456 | bytes 2883588 | tf_op jit(solution)/shard_map/dot_general | solution.py:100
  75.6 2.3 %fusion.60 = f32[128,1024]{1,0:T(8,128)S(1)} fusion(bf16[128,1024]{1,0:T(8,128)(2,1)S(1)} %bitcast.244, bf16[1024,4096]{1,0:T(8,128)(2,1)} %param.5, s32[]{:T(128)S(6)} %add.478), kind=kOutput, calls=%fused_computation.96 | convolution fusion | flops 268435456 | bytes 2883588 | tf_op jit(solution)/shard_map/dot_general | solution.py:100
  78.1 2.2 %fusion.16 = f16[128,1024]{1,0:T(8,128)(2,1)S(1)} fusion(f32[128,1024]{1,0:T(8,128)S(1)} %fusion.70, bf16[128,1024]{1,0:T(8,128)(2,1)S(1)} %bitcast.263, bf16[1024,2048]{1,0:T(8,128)(2,1)} %collective-permute-done.4), kind=kOutput, calls=%fused_computation.32 | convolution fusion | flops 268828672 | bytes 3145728 | tf_op jit(solution)/shard_map/dot_general | solution.py:104
  81.8 2.1 %fusion.17 = f16[128,1024]{1,0:T(8,128)(2,1)S(1)} fusion(f32[128,1024]{1,0:T(8,128)S(1)} %fusion.58, bf16[128,1024]{1,0:T(8,128)(2,1)S(1)} %bitcast.262, bf16[1024,2048]{1,0:T(8,128)(2,1)} %collective-permute-done.4), kind=kOutput, calls=%fused_computation.33 | convolution fusion | flops 268828672 | bytes 3145728 | tf_op jit(solution)/shard_map/dot_general | solution.py:104
  85.4 2.0 %fusion.44 = f32[128,1024]{1,0:T(8,128)S(1)} fusion(bf16[128,1024]{1,0:T(8,128)(2,1)S(1)} %bitcast.265, bf16[1024,2048]{1,0:T(8,128)(2,1)} %collective-permute-done.4), kind=kOutput, calls=%fused_computation.80 | convolution fusion | flops 268435456 | bytes 2883584 | tf_op jit(solution)/shard_map/dot_general | solution.py:104
  88.6 2.1 %fusion.46 = f32[128,1024]{1,0:T(8,128)S(1)} fusion(bf16[128,1024]{1,0:T(8,128)(2,1)S(1)} %bitcast.261, bf16[1024,2048]{1,0:T(8,128)(2,1)} %collective-permute-done.4), kind=kOutput, calls=%fused_computation.82 | convolution fusion | flops 268435456 | bytes 2883584 | tf_op jit(solution)/shard_map/dot_general | solution.py:104
  91.2 2.0 %fusion.32 = f32[128,1024]{1,0:T(8,128)S(1)} fusion(bf16[128,1024]{1,0:T(8,128)(2,1)S(1)} %bitcast.260, bf16[1024,2048]{1,0:T(8,128)(2,1)} %collective-permute-done.4), kind=kOutput, calls=%fused_computation.68 | convolution fusion | flops 268435456 | bytes 2883584 | tf_op jit(solution)/shard_map/dot_general | solution.py:104
  95.3 2.0 %fusion.15 = f32[128,1024]{1,0:T(8,128)S(1)} fusion(f32[128,1024]{1,0:T(8,128)S(1)} %fusion.72, bf16[128,1024]{1,0:T(8,128)(2,1)S(1)} %bitcast.248, bf16[1024,2048]{1,0:T(8,128)(2,1)} %collective-permute-done.4), kind=kOutput, calls=%fused_computation.31 | convolution fusion | flops 268697600 | bytes 3407872 | tf_op jit(solution)/shard_map/dot_general | solution.py:104
  97.3 2.0 %fusion.13 = f32[128,1024]{1,0:T(8,128)S(1)} fusion(f32[128,1024]{1,0:T(8,128)S(1)} %fusion.60, bf16[128,1024]{1,0:T(8,128)(2,1)S(1)} %bitcast.249, bf16[1024,2048]{1,0:T(8,128)(2,1)} %collective-permute-done.4), kind=kOutput, calls=%fused_computation.27 | convolution fusion | flops 268697600 | bytes 3407872 | tf_op jit(solution)/shard_map/dot_general | solution.py:104
  104.4 5.2 %collective-permute-done.12 = f16[2,2,32,1024]{3,2,0,1:T(8,128)(2,1)S(1)} collective-permute-done((f16[2,2,32,1024]{3,2,0,1:T(8,128)(2,1)S(1)}, f16[2,2,32,1024]{3,2,0,1:T(8,128)(2,1)S(1)}, u32[]{:S(2)}, u32[]{:S(2)}) %collective-permute-start.12) | collective-permute-done | bytes 262176 | tf_op jit(solution)/shard_map/ppermute | solution.py:116
  110.3 2.1 %collective-permute-done.6 = f16[2,32,1024]{2,1,0:T(8,128)(2,1)S(1)} collective-permute-done((f16[2,32,1024]{2,1,0:T(8,128)(2,1)S(1)}, f16[2,32,1024]{2,1,0:T(8,128)(2,1)S(1)}, u32[]{:S(2)}, u32[]{:S(2)}) %collective-permute-start.6) | collective-permute-done | bytes 131104 | tf_op jit(solution)/shard_map/ppermute | solution.py:121
  114.7 2.8 %collective-permute-done.13 = f16[2,32,1024]{2,1,0:T(8,128)(2,1)S(1)} collective-permute-done((f16[2,32,1024]{2,1,0:T(8,128)(2,1)S(1)}, f16[2,32,1024]{2,1,0:T(8,128)(2,1)S(1)}, u32[]{:S(2)}, u32[]{:S(2)}) %collective-permute-start.13) | collective-permute-done | bytes 131104 | tf_op jit(solution)/shard_map/ppermute | solution.py:122
  122.1 2.2 %fusion.64 = f32[128,1024]{1,0:T(8,128)S(1)} fusion(bf16[128,1024]{1,0:T(8,128)(2,1)S(1)} %bitcast.241, bf16[1024,4096]{1,0:T(8,128)(2,1)} %param.5, s32[]{:T(128)S(6)} %select_n.227), kind=kOutput, calls=%fused_computation.100 | convolution fusion | flops 268435456 | bytes 2883588 | tf_op jit(solution)/shard_map/dot_general | solution.py:100
  124.3 2.0 %fusion.20 = f16[128,1024]{1,0:T(8,128)(2,1)S(1)} fusion(f32[128,1024]{1,0:T(8,128)S(1)} %fusion.64, bf16[128,1024]{1,0:T(8,128)(2,1)S(1)} %bitcast.268, bf16[1024,2048]{1,0:T(8,128)(2,1)} %collective-permute-done.4), kind=kOutput, calls=%fused_computation.36 | convolution fusion | flops 268828672 | bytes 3145728 | tf_op jit(solution)/shard_map/dot_general | solution.py:104
  128.0 2.2 %fusion.66 = f32[128,1024]{1,0:T(8,128)S(1)} fusion(bf16[128,1024]{1,0:T(8,128)(2,1)S(1)} %bitcast.239, bf16[1024,4096]{1,0:T(8,128)(2,1)} %param.5, s32[]{:T(128)S(6)} %select_n.227), kind=kOutput, calls=%fused_computation.102 | convolution fusion | flops 268435456 | bytes 2883588 | tf_op jit(solution)/shard_map/dot_general | solution.py:100
  132.2 2.0 %fusion.21 = f16[128,1024]{1,0:T(8,128)(2,1)S(1)} fusion(f32[128,1024]{1,0:T(8,128)S(1)} %fusion.52, bf16[128,1024]{1,0:T(8,128)(2,1)S(1)} %bitcast.266, bf16[1024,2048]{1,0:T(8,128)(2,1)} %collective-permute-done.4), kind=kOutput, calls=%fused_computation.37 | convolution fusion | flops 268828672 | bytes 3145728 | tf_op jit(solution)/shard_map/dot_general | solution.py:104
  135.4 2.0 %fusion.7 = f32[128,1024]{1,0:T(8,128)S(1)} fusion(f32[128,1024]{1,0:T(8,128)S(1)} %fusion.66, bf16[128,1024]{1,0:T(8,128)(2,1)S(1)} %bitcast.251, bf16[1024,2048]{1,0:T(8,128)(2,1)} %collective-permute-done.4), kind=kOutput, calls=%fused_computation.15 | convolution fusion | flops 268697600 | bytes 3407872 | tf_op jit(solution)/shard_map/dot_general | solution.py:104
  141.2 2.1 %collective-permute-done.17 = f16[2,2,32,1024]{3,2,0,1:T(8,128)(2,1)S(1)} collective-permute-done((f16[2,2,32,1024]{3,2,0,1:T(8,128)(2,1)S(1)}, f16[2,2,32,1024]{3,2,0,1:T(8,128)(2,1)S(1)}, u32[]{:S(2)}, u32[]{:S(2)}) %collective-permute-start.17) | collective-permute-done | bytes 262176 | tf_op jit(solution)/shard_map/ppermute | solution.py:116
  145.5 2.8 %collective-permute-done.18 = f16[2,32,1024]{2,1,0:T(8,128)(2,1)S(1)} collective-permute-done((f16[2,32,1024]{2,1,0:T(8,128)(2,1)S(1)}, f16[2,32,1024]{2,1,0:T(8,128)(2,1)S(1)}, u32[]{:S(2)}, u32[]{:S(2)}) %collective-permute-start.18) | collective-permute-done | bytes 131104 | tf_op jit(solution)/shard_map/ppermute | solution.py:122
  148.5 2.2 %fusion.38 = f32[128,1024]{1,0:T(8,128)S(1)} fusion(bf16[128,1024]{1,0:T(8,128)(2,1)S(1)} %bitcast.270, bf16[1024,2048]{1,0:T(8,128)(2,1)} %collective-permute-done.4), kind=kOutput, calls=%fused_computation.74 | convolution fusion | flops 268435456 | bytes 2883584 | tf_op jit(solution)/shard_map/dot_general | solution.py:104
  164.8 2.1 %collective-permute-done.23 = f16[2,32,1024]{2,1,0:T(8,128)(2,1)S(1)} collective-permute-done((f16[2,32,1024]{2,1,0:T(8,128)(2,1)S(1)}, f16[2,32,1024]{2,1,0:T(8,128)(2,1)S(1)}, u32[]{:S(2)}, u32[]{:S(2)}) %collective-permute-start.23) | collective-permute-done | bytes 131104 | tf_op jit(solution)/shard_map/ppermute | solution.py:122
  173.0 2.4 %collective-permute-start.31 = (f32[4,64]{1,0:T(4,128)S(1)}, f32[4,64]{1,0:T(4,128)S(1)}, u32[]{:S(2)}, u32[]{:S(2)}) collective-permute-start(f32[4,64]{1,0:T(4,128)S(1)} %get-tuple-element.58), channel_id=1, source_target_pairs={{0,3},{1,0},{2,1},{3,2},{4,7},{5,4},{6,5},{7,6},{8,11},{9,8},{10,9... | collective-permute-start | bytes 3080 | tf_op jit(solution)/shard_map/ppermute | solution.py:163
  (159 shorter events, 67.9 us)
Async XLA Ops:
  7.2 59.6 %all-gather.3.cloned.1.call-start = ((), (), s32[]{:S(2)}) async-start(), calls=%async_computation | async-start | bytes 1310720 | tf_op jit(solution)/shard_map/all_gather | solution.py:62
  9.1 6.5 %collective-permute-start = (bf16[2,32,1024]{2,1,0:T(8,128)(2,1)S(1)}, bf16[2,32,1024]{2,1,0:T(8,128)(2,1)S(1)}, u32[]{:S(2)}, u32[]{:S(2)}) collective-permute-start(bf16[2,32,1024]{2,1,0:T(8,128)(2,1)S(1)} %constant_dynamic-slice_fusion.36), channel_id=1, source_target_pairs={{0,4},{4,0},{8,12},{12,8},{1,5},{5,1},{9,13},{13,9},{2,6},{6,2},{1... | collective-permute-start | bytes 393224 | tf_op jit(solution)/shard_map/ppermute | solution.py:56
  20.5 57.6 %collective-permute-start.4 = (bf16[1024,2048]{1,0:T(8,128)(2,1)}, bf16[1024,2048]{1,0:T(8,128)(2,1)}, u32[]{:S(2)}, u32[]{:S(2)}) collective-permute-start(bf16[1024,2048]{1,0:T(8,128)(2,1)} %constant_dynamic-slice_fusion.32), channel_id=1, source_target_pairs={{0,16},{16,0},{1,17},{17,1},{2,18},{18,2},{3,19},{19,3},{4,20},{20... | collective-permute-start | bytes 12582920 | tf_op jit(solution)/shard_map/ppermute | solution.py:78
  20.5 6.0 %collective-permute-start.2 = (bf16[2,32,1024]{2,1,0:T(8,128)(2,1)S(1)}, bf16[2,32,1024]{2,1,0:T(8,128)(2,1)S(1)}, u32[]{:S(2)}, u32[]{:S(2)}) collective-permute-start(bf16[2,32,1024]{2,1,0:T(8,128)(2,1)S(1)} %constant_dynamic-slice_fusion.35), channel_id=1, source_target_pairs={{0,4},{4,0},{8,12},{12,8},{1,5},{5,1},{9,13},{13,9},{2,6},{6,2},{1... | collective-permute-start | bytes 393224 | tf_op jit(solution)/shard_map/ppermute | solution.py:56
  28.1 89.7 %all-gather.5.cloned.1.call-start = ((), (), s32[]{:S(2)}) async-start(), calls=%async_computation.1 | async-start | bytes 1310720 | tf_op jit(solution)/shard_map/all_gather | solution.py:62
  28.2 28.3 %collective-permute-start.3 = (bf16[2,2,32,1024]{3,2,1,0:T(8,128)(2,1)S(1)}, bf16[2,2,32,1024]{3,2,1,0:T(8,128)(2,1)S(1)}, u32[]{:S(2)}, u32[]{:S(2)}) collective-permute-start(bf16[2,2,32,1024]{3,2,1,0:T(8,128)(2,1)S(1)} %pad_maximum_fusion.3), channel_id=1, source_target_pairs={{1,8},{8,1},{3,10},{10,3},{5,12},{12,5},{7,14},{14,7},{17,24},{24,... | collective-permute-start | bytes 786440 | tf_op jit(solution)/shard_map/ppermute | solution.py:60
  29.1 19.2 %collective-permute-start.25 = (f32[128]{0:T(128)S(1)}, f32[128]{0:T(128)S(1)}, u32[]{:S(2)}, u32[]{:S(2)}) collective-permute-start(f32[128]{0:T(128)S(1)} %multiply_reduce_fusion), channel_id=1, source_target_pairs={{0,1},{1,0},{2,3},{3,2},{4,5},{5,4},{6,7},{7,6},{8,9},{9,8},{10,11... | collective-permute-start | bytes 1544 | tf_op jit(solution)/shard_map/ppermute | solution.py:84
  48.3 4.4 %collective-permute-start.26 = (f32[128]{0:T(128)S(1)}, f32[128]{0:T(128)S(1)}, u32[]{:S(2)}, u32[]{:S(2)}) collective-permute-start(f32[128]{0:T(128)S(1)} %add.471), channel_id=1, source_target_pairs={{0,2},{1,3},{2,0},{3,1},{4,6},{5,7},{6,4},{7,5},{8,10},{9,11},{10,... | collective-permute-start | bytes 1544 | tf_op jit(solution)/shard_map/ppermute | solution.py:84
  52.9 64.9 %collective-permute-start.27 = (f32[64]{0:T(128)S(1)}, f32[64]{0:T(128)S(1)}, u32[]{:S(2)}, u32[]{:S(2)}) collective-permute-start(f32[64]{0:T(128)S(1)} %get-tuple-element.65), channel_id=1, source_target_pairs={{0,0},{4,8},{8,16},{12,24},{16,4},{20,12},{24,20},{28,28},{1,1},{5... | collective-permute-start | bytes 776 | tf_op jit(solution)/shard_map/ppermute | solution.py:88
  53.6 64.3 %collective-permute-start.28 = (f32[64]{0:T(128)S(1)}, f32[64]{0:T(128)S(1)}, u32[]{:S(2)}, u32[]{:S(2)}) collective-permute-start(f32[64]{0:T(128)S(1)} %get-tuple-element.66), channel_id=1, source_target_pairs={{0,4},{4,12},{8,20},{12,28},{16,0},{20,8},{24,16},{28,24},{1,5},{5... | collective-permute-start | bytes 776 | tf_op jit(solution)/shard_map/ppermute | solution.py:88
  66.8 11.1 %collective-permute-start.9 = (bf16[2,2,2,2,32,1024]{5,4,3,2,1,0:T(8,128)(2,1)}, bf16[2,2,2,2,32,1024]{5,4,3,2,1,0:T(8,128)(2,1)S(1)}, u32[]{:S(2)}, u32[]{:S(2)}) collective-permute-start(bf16[2,2,2,2,32,1024]{5,4,3,2,1,0:T(8,128)(2,1)} %bitcast.222), channel_id=1, source_target_pairs={{0,16},{16,0},{1,17},{17,1},{2,18},{18,2},{3,19},{19,3},{4,20},{20... | collective-permute-start | bytes 3145736 | tf_op jit(solution)/shard_map/ppermute | solution.py:134
  80.3 20.0 %collective-permute-start.5 = (f16[2,2,32,1024]{3,2,1,0:T(8,128)(2,1)S(1)}, f16[2,2,32,1024]{3,2,1,0:T(8,128)(2,1)S(1)}, u32[]{:S(2)}, u32[]{:S(2)}) collective-permute-start(f16[2,2,32,1024]{3,2,1,0:T(8,128)(2,1)S(1)} %bitcast.282), channel_id=1, source_target_pairs={{0,4},{4,0},{8,12},{12,8},{1,5},{5,1},{9,13},{13,9},{2,6},{6,2},{1... | collective-permute-start | bytes 786440 | tf_op jit(solution)/shard_map/ppermute | solution.py:113
  83.9 17.2 %collective-permute-start.7 = (f16[2,2,32,1024]{3,2,0,1:T(8,128)(2,1)S(1)}, f16[2,2,32,1024]{3,2,0,1:T(8,128)(2,1)S(1)}, u32[]{:S(2)}, u32[]{:S(2)}) collective-permute-start(f16[2,2,32,1024]{3,2,0,1:T(8,128)(2,1)S(1)} %copy.5), channel_id=1, source_target_pairs={{0,8},{8,0},{4,12},{12,4},{1,9},{9,1},{5,13},{13,5},{2,10},{10,2},... | collective-permute-start | bytes 786440 | tf_op jit(solution)/shard_map/ppermute | solution.py:116
  88.0 14.7 %collective-permute-start.10 = (f16[2,2,32,1024]{3,2,0,1:T(8,128)(2,1)S(1)}, f16[2,2,32,1024]{3,2,0,1:T(8,128)(2,1)S(1)}, u32[]{:S(2)}, u32[]{:S(2)}) collective-permute-start(f16[2,2,32,1024]{3,2,0,1:T(8,128)(2,1)S(1)} %copy.7), channel_id=1, source_target_pairs={{0,4},{4,0},{8,12},{12,8},{1,5},{5,1},{9,13},{13,9},{2,6},{6,2},{1... | collective-permute-start | bytes 786440 | tf_op jit(solution)/shard_map/ppermute | solution.py:113
  100.4 9.3 %collective-permute-start.12 = (f16[2,2,32,1024]{3,2,0,1:T(8,128)(2,1)S(1)}, f16[2,2,32,1024]{3,2,0,1:T(8,128)(2,1)S(1)}, u32[]{:S(2)}, u32[]{:S(2)}) collective-permute-start(f16[2,2,32,1024]{3,2,0,1:T(8,128)(2,1)S(1)} %copy.9), channel_id=1, source_target_pairs={{0,8},{8,0},{4,12},{12,4},{1,9},{9,1},{5,13},{13,5},{2,10},{10,2},... | collective-permute-start | bytes 786440 | tf_op jit(solution)/shard_map/ppermute | solution.py:116
  101.1 11.3 %collective-permute-start.6 = (f16[2,32,1024]{2,1,0:T(8,128)(2,1)S(1)}, f16[2,32,1024]{2,1,0:T(8,128)(2,1)S(1)}, u32[]{:S(2)}, u32[]{:S(2)}) collective-permute-start(f16[2,32,1024]{2,1,0:T(8,128)(2,1)S(1)} %fusion.83), channel_id=1, source_target_pairs={{0,8},{8,0},{4,12},{12,4},{1,9},{9,1},{5,13},{13,5},{2,10},{10,2},... | collective-permute-start | bytes 393224 | tf_op jit(solution)/shard_map/ppermute | solution.py:121
  102.8 11.2 %collective-permute-start.8 = (f16[2,32,1024]{2,1,0:T(8,128)(2,1)S(1)}, f16[2,32,1024]{2,1,0:T(8,128)(2,1)S(1)}, u32[]{:S(2)}, u32[]{:S(2)}) collective-permute-start(f16[2,32,1024]{2,1,0:T(8,128)(2,1)S(1)} %fusion.84), channel_id=1, source_target_pairs={{0,4},{4,0},{8,12},{12,8},{1,5},{5,1},{9,13},{13,9},{2,6},{6,2},{1... | collective-permute-start | bytes 393224 | tf_op jit(solution)/shard_map/ppermute | solution.py:122
  109.6 5.0 %collective-permute-start.11 = (f16[2,32,1024]{2,1,0:T(8,128)(2,1)S(1)}, f16[2,32,1024]{2,1,0:T(8,128)(2,1)S(1)}, u32[]{:S(2)}, u32[]{:S(2)}) collective-permute-start(f16[2,32,1024]{2,1,0:T(8,128)(2,1)S(1)} %fusion.85), channel_id=1, source_target_pairs={{0,8},{8,0},{4,12},{12,4},{1,9},{9,1},{5,13},{13,5},{2,10},{10,2},... | collective-permute-start | bytes 393224 | tf_op jit(solution)/shard_map/ppermute | solution.py:121
  112.4 5.0 %collective-permute-start.13 = (f16[2,32,1024]{2,1,0:T(8,128)(2,1)S(1)}, f16[2,32,1024]{2,1,0:T(8,128)(2,1)S(1)}, u32[]{:S(2)}, u32[]{:S(2)}) collective-permute-start(f16[2,32,1024]{2,1,0:T(8,128)(2,1)S(1)} %fusion.86), channel_id=1, source_target_pairs={{0,4},{4,0},{8,12},{12,8},{1,5},{5,1},{9,13},{13,9},{2,6},{6,2},{1... | collective-permute-start | bytes 393224 | tf_op jit(solution)/shard_map/ppermute | solution.py:122
  117.7 1.6 collective-permute-start.14
  121.9 26.5 %collective-permute-start.19 = (bf16[2,2,2,2,32,1024]{5,4,3,2,1,0:T(8,128)(2,1)S(1)}, bf16[2,2,2,2,32,1024]{5,4,3,2,1,0:T(8,128)(2,1)S(1)}, u32[]{:S(2)}, u32[]{:S(2)}) collective-permute-start(bf16[2,2,2,2,32,1024]{5,4,3,2,1,0:T(8,128)(2,1)S(1)} %bitcast.221), channel_id=1, source_target_pairs={{0,16},{16,0},{1,17},{17,1},{2,18},{18,2},{3,19},{19,3},{4,20},{20... | collective-permute-start | bytes 3145736 | tf_op jit(solution)/shard_map/ppermute | solution.py:134
  126.4 13.1 %collective-permute-start.15 = (f16[2,2,32,1024]{3,2,0,1:T(8,128)(2,1)S(1)}, f16[2,2,32,1024]{3,2,0,1:T(8,128)(2,1)S(1)}, u32[]{:S(2)}, u32[]{:S(2)}) collective-permute-start(f16[2,2,32,1024]{3,2,0,1:T(8,128)(2,1)S(1)} %copy.11), channel_id=1, source_target_pairs={{0,4},{4,0},{8,12},{12,8},{1,5},{5,1},{9,13},{13,9},{2,6},{6,2},{1... | collective-permute-start | bytes 786440 | tf_op jit(solution)/shard_map/ppermute | solution.py:113
  134.3 8.9 %collective-permute-start.17 = (f16[2,2,32,1024]{3,2,0,1:T(8,128)(2,1)S(1)}, f16[2,2,32,1024]{3,2,0,1:T(8,128)(2,1)S(1)}, u32[]{:S(2)}, u32[]{:S(2)}) collective-permute-start(f16[2,2,32,1024]{3,2,0,1:T(8,128)(2,1)S(1)} %copy.13), channel_id=1, source_target_pairs={{0,8},{8,0},{4,12},{12,4},{1,9},{9,1},{5,13},{13,5},{2,10},{10,2},... | collective-permute-start | bytes 786440 | tf_op jit(solution)/shard_map/ppermute | solution.py:116
  139.6 5.9 %collective-permute-start.16 = (f16[2,32,1024]{2,1,0:T(8,128)(2,1)S(1)}, f16[2,32,1024]{2,1,0:T(8,128)(2,1)S(1)}, u32[]{:S(2)}, u32[]{:S(2)}) collective-permute-start(f16[2,32,1024]{2,1,0:T(8,128)(2,1)S(1)} %fusion.87), channel_id=1, source_target_pairs={{0,8},{8,0},{4,12},{12,4},{1,9},{9,1},{5,13},{13,5},{2,10},{10,2},... | collective-permute-start | bytes 393224 | tf_op jit(solution)/shard_map/ppermute | solution.py:121
  143.3 5.0 %collective-permute-start.18 = (f16[2,32,1024]{2,1,0:T(8,128)(2,1)S(1)}, f16[2,32,1024]{2,1,0:T(8,128)(2,1)S(1)}, u32[]{:S(2)}, u32[]{:S(2)}) collective-permute-start(f16[2,32,1024]{2,1,0:T(8,128)(2,1)S(1)} %fusion.88), channel_id=1, source_target_pairs={{0,4},{4,0},{8,12},{12,8},{1,5},{5,1},{9,13},{13,9},{2,6},{6,2},{1... | collective-permute-start | bytes 393224 | tf_op jit(solution)/shard_map/ppermute | solution.py:122
  151.3 8.3 %collective-permute-start.20 = (f16[2,2,32,1024]{3,2,0,1:T(8,128)(2,1)S(1)}, f16[2,2,32,1024]{3,2,0,1:T(8,128)(2,1)S(1)}, u32[]{:S(2)}, u32[]{:S(2)}) collective-permute-start(f16[2,2,32,1024]{3,2,0,1:T(8,128)(2,1)S(1)} %copy.15), channel_id=1, source_target_pairs={{0,4},{4,0},{8,12},{12,8},{1,5},{5,1},{9,13},{13,9},{2,6},{6,2},{1... | collective-permute-start | bytes 786440 | tf_op jit(solution)/shard_map/ppermute | solution.py:113
  154.5 7.4 %collective-permute-start.22 = (f16[2,2,32,1024]{3,2,1,0:T(8,128)(2,1)S(1)}, f16[2,2,32,1024]{3,2,1,0:T(8,128)(2,1)S(1)}, u32[]{:S(2)}, u32[]{:S(2)}) collective-permute-start(f16[2,2,32,1024]{3,2,1,0:T(8,128)(2,1)S(1)} %bitcast.274), channel_id=1, source_target_pairs={{0,8},{8,0},{4,12},{12,4},{1,9},{9,1},{5,13},{13,5},{2,10},{10,2},... | collective-permute-start | bytes 786440 | tf_op jit(solution)/shard_map/ppermute | solution.py:116
  159.8 5.0 %collective-permute-start.21 = (f16[2,32,1024]{2,1,0:T(8,128)(2,1)S(1)}, f16[2,32,1024]{2,1,0:T(8,128)(2,1)S(1)}, u32[]{:S(2)}, u32[]{:S(2)}) collective-permute-start(f16[2,32,1024]{2,1,0:T(8,128)(2,1)S(1)} %fusion.89), channel_id=1, source_target_pairs={{0,8},{8,0},{4,12},{12,4},{1,9},{9,1},{5,13},{13,5},{2,10},{10,2},... | collective-permute-start | bytes 393224 | tf_op jit(solution)/shard_map/ppermute | solution.py:121
  162.0 5.0 %collective-permute-start.23 = (f16[2,32,1024]{2,1,0:T(8,128)(2,1)S(1)}, f16[2,32,1024]{2,1,0:T(8,128)(2,1)S(1)}, u32[]{:S(2)}, u32[]{:S(2)}) collective-permute-start(f16[2,32,1024]{2,1,0:T(8,128)(2,1)S(1)} %fusion.90), channel_id=1, source_target_pairs={{0,4},{4,0},{8,12},{12,8},{1,5},{5,1},{9,13},{13,9},{2,6},{6,2},{1... | collective-permute-start | bytes 393224 | tf_op jit(solution)/shard_map/ppermute | solution.py:122
  170.5 5.4 %collective-permute-start.29 = (f32[4,64]{1,0:T(4,128)S(1)}, f32[4,64]{1,0:T(4,128)S(1)}, u32[]{:S(2)}, u32[]{:S(2)}) collective-permute-start(f32[4,64]{1,0:T(4,128)S(1)} %get-tuple-element.58), channel_id=1, source_target_pairs={{0,1},{1,2},{2,3},{3,0},{4,5},{5,6},{6,7},{7,4},{8,9},{9,10},{10,1... | collective-permute-start | bytes 3080 | tf_op jit(solution)/shard_map/ppermute | solution.py:163
  171.9 4.5 %collective-permute-start.30 = (f32[4,64]{1,0:T(4,128)S(1)}, f32[4,64]{1,0:T(4,128)S(1)}, u32[]{:S(2)}, u32[]{:S(2)}) collective-permute-start(f32[4,64]{1,0:T(4,128)S(1)} %get-tuple-element.58), channel_id=1, source_target_pairs={{0,2},{1,3},{2,0},{3,1},{4,6},{5,7},{6,4},{7,5},{8,10},{9,11},{10,... | collective-permute-start | bytes 3080 | tf_op jit(solution)/shard_map/ppermute | solution.py:163
  173.0 3.7 %collective-permute-start.31 = (f32[4,64]{1,0:T(4,128)S(1)}, f32[4,64]{1,0:T(4,128)S(1)}, u32[]{:S(2)}, u32[]{:S(2)}) collective-permute-start(f32[4,64]{1,0:T(4,128)S(1)} %get-tuple-element.58), channel_id=1, source_target_pairs={{0,3},{1,0},{2,1},{3,2},{4,7},{5,4},{6,5},{7,6},{8,11},{9,8},{10,9... | collective-permute-start | bytes 3080 | tf_op jit(solution)/shard_map/ppermute | solution.py:163
  (8 other events, 60.7 us)
Sparse Core Ops, SparseCore 0:
  28.3 38.4 all-gather.2
  68.9 27.4 all-gather.4

commit v4 on v3

--- a/solution.py
+++ b/solution.py
@@ -50,35 +50,59 @@
         )
     ]
 
-    def line_features(c):
-        piece = gained[:, c * step : (c + 1) * step]
-        mine = lax.dynamic_slice_in_dim(piece, x * block, block, 2)
-        other = lax.ppermute(
-            lax.dynamic_slice_in_dim(piece, (1 - x) * block, block, 2), "batch", X_SWAP
-        )
-        own = jnp.stack([jnp.where(x == 0, mine, other), jnp.where(x == 0, other, mine)])
-        moved = lax.ppermute(own, ("batch", "vocab"), diagonal)
-        held = jnp.where((level + y) % 2 == 1, moved, own)
-        whole = lax.all_gather(held.reshape(-1, block), "vocab", axis=0, tiled=True)
-        return whole.reshape(2, 2, 2, 2, step, block), other, held
-
-    def gathered_features(c):
-        piece = gained[:, c * step : (c + 1) * step]
-        whole = lax.all_gather(piece, "vocab", axis=2, tiled=True)
-        whole = whole.reshape(2, step, 2, 4, block).transpose(3, 2, 0, 1, 4)
-        whole = lax.all_to_all(whole, "batch", split_axis=0, concat_axis=0)
-        whole = whole.reshape(2, 2, 2, 2, step, block).transpose(2, 0, 1, 3, 4, 5)
-        return whole, piece, piece
-
-    features = line_features if depth == 2 * block and vocab == 4 else gathered_features
-    found = [features(c) for c in range(CHUNKS)]
-
-    side = after(core, found[0][1])
-    give = lax.dynamic_slice_in_dim(head_weight, (1 - side) * width, width, 1)
+    def line_features():
+        pieces = [gained[:, c * step : (c + 1) * step] for c in range(CHUNKS)]
+        sides = [lax.dynamic_slice_in_dim(piece, (1 - x) * block, block, 2) for piece in pieces]
+        sides = [lax.ppermute(side, "batch", X_SWAP) for side in sides]
+        held = []
+        for piece, other in zip(pieces, sides):
+            mine = lax.dynamic_slice_in_dim(piece, x * block, block, 2)
+            own = jnp.stack([jnp.where(x == 0, mine, other), jnp.where(x == 0, other, mine)])
+            moved = lax.ppermute(own, ("batch", "vocab"), diagonal)
+            held.append(jnp.where((level + y) % 2 == 1, moved, own))
+
+        wholes = []
+        for own in held:
+            below, above = [own], [own]
+            for k in range(1, vocab):
+                below.append(
+                    lax.ppermute(below[-1], "vocab", [(z, z + 1) for z in range(k - 1, vocab - 1)])
+                )
+                above.append(
+                    lax.ppermute(above[-1], "vocab", [(z + 1, z) for z in range(vocab - k)])
+                )
+            ordered = []
+            for z in range(vocab):
+                part = own
+                for k in range(1, vocab):
+                    if z + k < vocab:
+                        part = jnp.where(level == z + k, below[k], part)
+                    if z - k >= 0:
+                        part = jnp.where(level == z - k, above[k], part)
+                ordered.append(part)
+            wholes.append(jnp.stack(ordered).reshape(2, 2, 2, 2, step, block))
+        return wholes, held, sides[0]
+
+    def gathered_features():
+        wholes = []
+        for c in range(CHUNKS):
+            piece = gained[:, c * step : (c + 1) * step]
+            whole = lax.all_gather(piece, "vocab", axis=2, tiled=True)
+            whole = whole.reshape(2, step, 2, 4, block).transpose(3, 2, 0, 1, 4)
+            whole = lax.all_to_all(whole, "batch", split_axis=0, concat_axis=0)
+            wholes.append(whole.reshape(2, 2, 2, 2, step, block).transpose(2, 0, 1, 3, 4, 5))
+        return wholes, wholes, gained
+
+    lined = depth == 2 * block and vocab == 4
+    found, held, begun = line_features() if lined else gathered_features()
+
+    give = lax.dynamic_slice_in_dim(head_weight, (1 - core) * width, width, 1)
     take = lax.ppermute(give, "pair", CORE_SWAP)
-    keep = lax.dynamic_slice_in_dim(head_weight, side * width, width, 1)
+    side = after(core, begun)
+    keep = lax.optimization_barrier(lax.dynamic_slice_in_dim(head_weight, side * width, width, 1))
 
     squares = jnp.sum(wide * wide, axis=1)
+    squares = after(squares, begun)
     reach = 1
     while reach < vocab:
         squares += lax.ppermute(squares, "vocab", [(i, i ^ reach) for i in range(vocab)])
@@ -129,8 +153,7 @@
         ).astype(SUM_TYPE)
 
     def chunk(c, *earlier):
-        ready = [found[c + 1][2]] if c + 1 < CHUNKS else []
-        own = after(found[c][0], *earlier, *ready)
+        own = after(found[c], *earlier)
         other = lax.ppermute(own, "pair", CORE_SWAP)
         sums = jnp.stack([reduced(own), reduced(other)])
         return pick(sums, core, 1), lax.ppermute(pick(sums, 1 - core, 1), "pair", CORE_SWAP)

time: 187 us -> 173 us (0.925)
  between operations: 15 us -> 1.8 us
  matrix products: 51.9 us -> 40 us
  starting transfers between devices: 50.3 us -> 60.7 us
  waiting for transfers between devices: 48.6 us -> 51.5 us
    ppermute x2 -> x14, starting transfers between devices: 4.81 us -> 28.8 us  [the longest x6 17.8 us: line_features(): lax.ppermute(below[-1], 'vocab', [(z, z + 1) for z in range(k - 1, vocab...]
    ppermute x2 -> x14, waiting for transfers between devices: 7.66 us -> 23.4 us  [the longest x6 16.3 us: line_features(): lax.ppermute(above[-1], 'vocab', [(z + 1, z) for z in range(vocab - k)])]
    ppermute x2, starting transfers between devices: 17.1 us -> 5.23 us  [on_device(): lax.ppermute(squares, 'vocab', [(i, i ^ reach) for i in range(vocab)])]
    dot_general x16, matrix products: 19 us -> 7.21 us  [partial(): jnp.dot(pick(left, core, 0).reshape(-1, block), keep[:, low:high], prefer...]
    all_gather x2 -> x0, waiting for transfers between devices: 9.49 us -> none  [line_features(): whole = lax.all_gather(held.reshape(-1, block), 'vocab', axis=0, tiled=True)]
    ppermute x4, waiting for transfers between devices: 7.36 us -> 0.01 us  [reduced(): lax.ppermute(partial(pick(left, 1 - y, 2), middle, width).astype(SUM_TYPE...]
    ppermute x4, waiting for transfers between devices: 0.01 us -> 7.16 us  [reduced(): lax.ppermute(partial(pick(left, 1 - x, 3), 0, middle).astype(SUM_TYPE), '...]
    ppermute x2, waiting for transfers between devices: 6.58 us -> 1.47 us  [on_device(): lax.ppermute(squares, 'vocab', [(i, i ^ reach) for i in range(vocab)])]
  transfers between devices with their start and end apart: 34 -> 44, of which waited for: 20 -> 23; matrix products, arithmetic and copies ran while one was open for 30% -> 29% of each run, Pallas kernels for 0% -> 0%
where the time goes in v4:
time: 173 us; the launch traced here: 172 us
  starting transfers between devices  60.7 us (35%)
  waiting for transfers between devices  51.5 us (30%)
  matrix products  40 us (23%)
  local copies, waits for them, and re-layouts  10.2 us (6%)
  other arithmetic  7.42 us (4%)
  between operations  1.8 us (1%)
    dot_general x16, matrix products, partial(): jnp.dot(pick(left, 1 - core, 0).reshape(-1, block), take[:, low:high], pr...  32.8 us
    ppermute x6, starting transfers between devices, line_features(): lax.ppermute(below[-1], 'vocab', [(z, z + 1) for z in range(k - 1, vocab...  17.8 us
    ppermute x6, waiting for transfers between devices, line_features(): lax.ppermute(above[-1], 'vocab', [(z + 1, z) for z in range(vocab - k)])  16.3 us
    dynamic_slice x1, local copies, waits for them, and re-layouts, on_device(): lax.dynamic_slice_in_dim(head_weight, side * width, width, 1)  8.46 us
    ppermute x6, starting transfers between devices, line_features(): lax.ppermute(above[-1], 'vocab', [(z + 1, z) for z in range(vocab - k)])  7.9 us
    dot_general x16, matrix products, partial(): jnp.dot(pick(left, core, 0).reshape(-1, block), keep[:, low:high], prefer...  7.21 us
    ppermute x4, waiting for transfers between devices, reduced(): lax.ppermute(partial(pick(left, 1 - x, 3), 0, middle).astype(SUM_TYPE), '...  7.16 us
    ppermute x4, waiting for transfers between devices, reduced(): lax.ppermute(pick(sum_y, 1 - x, 1).astype(SUM_TYPE), 'batch', X_SWAP)  6.68 us
  transfers between devices with their start and end apart: 44, of which 23 were waited for; matrix products, arithmetic and copies ran while one was open for 29% of the time, Pallas kernels for 0%

profile of v4, /device:TPU:0, one launch (start us, length us, event | category | flops | bytes accessed | tf_op | source)
XLA Modules:
  0.0 171.6 jit_solution(18270050799412205286)
XLA Ops:
  2.6 3.0 %collective-permute-start = (bf16[2,32,1024]{2,1,0:T(8,128)(2,1)S(1)}, bf16[2,32,1024]{2,1,0:T(8,128)(2,1)S(1)}, u32[]{:S(2)}, u32[]{:S(2)}) collective-permute-start(bf16[2,32,1024]{2,1,0:T(8,128)(2,1)S(1)} %constant_dynamic-slice_fusion.37), channel_id=1, source_target_pairs={{0,4},{4,0},{8,12},{12,8},{1,5},{5,1},{9,13},{13,9},{2,6},{6,2},{1... | collective-permute-start | bytes 393224 | tf_op jit(solution)/shard_map/ppermute | solution.py:56
  5.7 4.2 %collective-permute-done = bf16[2,32,1024]{2,1,0:T(8,128)(2,1)S(1)} collective-permute-done((bf16[2,32,1024]{2,1,0:T(8,128)(2,1)S(1)}, bf16[2,32,1024]{2,1,0:T(8,128)(2,1)S(1)}, u32[]{:S(2)}, u32[]{:S(2)}) %collective-permute-start) | collective-permute-done | bytes 131104 | tf_op jit(solution)/shard_map/ppermute | solution.py:56
  9.9 8.5 %constant_dynamic-slice_fusion.35 = (bf16[1024,2048]{1,0:T(8,128)(2,1)}, bf16[1024,2048]{1,0:T(8,128)(2,1)}) fusion(bf16[1024,4096]{1,0:T(8,128)(2,1)} %param.5, s32[]{:T(128)S(6)} %select_n.344, s32[]{:T(128)S(6)} %select_n.347), kind=kLoop, calls=%fused_computation.213 | loop fusion | bytes 16777224 | tf_op jit(solution)/shard_map/dynamic_slice | solution.py:102
  18.5 2.2 %collective-permute-start.37 = (f32[128]{0:T(128)S(1)}, f32[128]{0:T(128)S(1)}, u32[]{:S(2)}, u32[]{:S(2)}) collective-permute-start(f32[128]{0:T(128)S(1)} %multiply_reduce_fusion), channel_id=1, source_target_pairs={{0,1},{1,0},{2,3},{3,2},{4,5},{5,4},{6,7},{7,6},{8,9},{9,8},{10,11... | collective-permute-start | bytes 1544 | tf_op jit(solution)/shard_map/ppermute | solution.py:108
  22.3 3.0 %collective-permute-start.38 = (f32[128]{0:T(128)S(1)}, f32[128]{0:T(128)S(1)}, u32[]{:S(2)}, u32[]{:S(2)}) collective-permute-start(f32[128]{0:T(128)S(1)} %add.471), channel_id=1, source_target_pairs={{0,2},{1,3},{2,0},{3,1},{4,6},{5,7},{6,4},{7,5},{8,10},{9,11},{10,... | collective-permute-start | bytes 1544 | tf_op jit(solution)/shard_map/ppermute | solution.py:108
  27.0 10.5 %collective-permute-start.2 = (bf16[2,2,32,1024]{3,2,1,0:T(8,128)(2,1)S(1)}, bf16[2,2,32,1024]{3,2,1,0:T(8,128)(2,1)S(1)}, u32[]{:S(2)}, u32[]{:S(2)}) collective-permute-start(bf16[2,2,32,1024]{3,2,1,0:T(8,128)(2,1)S(1)} %broadcast_select_fusion.1), channel_id=1, source_target_pairs={{0,1},{1,2},{2,3},{4,5},{5,6},{6,7},{8,9},{9,10},{10,11},{12,13},{... | collective-permute-start | bytes 786440 | tf_op jit(solution)/shard_map/ppermute | solution.py:69
  39.5 2.8 %collective-permute-start.40 = (f32[64]{0:T(128)S(1)}, f32[64]{0:T(128)S(1)}, u32[]{:S(2)}, u32[]{:S(2)}) collective-permute-start(f32[64]{0:T(128)S(1)} %get-tuple-element.76), channel_id=1, source_target_pairs={{0,4},{4,12},{8,20},{12,28},{16,0},{20,8},{24,16},{28,24},{1,5},{5... | collective-permute-start | bytes 776 | tf_op jit(solution)/shard_map/ppermute | solution.py:112
  42.3 4.6 %collective-permute-start.20 = (bf16[2,2,32,1024]{3,2,1,0:T(8,128)(2,1)S(1)}, bf16[2,2,32,1024]{3,2,1,0:T(8,128)(2,1)S(1)}, u32[]{:S(2)}, u32[]{:S(2)}) collective-permute-start(bf16[2,2,32,1024]{3,2,1,0:T(8,128)(2,1)S(1)} %broadcast_select_fusion), channel_id=1, source_target_pairs={{0,1},{1,2},{2,3},{4,5},{5,6},{6,7},{8,9},{9,10},{10,11},{12,13},{... | collective-permute-start | bytes 786440 | tf_op jit(solution)/shard_map/ppermute | solution.py:69
  50.3 3.0 %collective-permute-done.20 = bf16[2,2,32,1024]{3,2,1,0:T(8,128)(2,1)S(1)} collective-permute-done((bf16[2,2,32,1024]{3,2,1,0:T(8,128)(2,1)S(1)}, bf16[2,2,32,1024]{3,2,1,0:T(8,128)(2,1)S(1)}, u32[]{:S(2)}, u32[]{:S(2)}) %collective-permute-start.20) | collective-permute-done | bytes 262176 | tf_op jit(solution)/shard_map/ppermute | solution.py:69
  53.9 4.0 %collective-permute-done.23 = bf16[2,2,32,1024]{3,2,1,0:T(8,128)(2,1)S(1)} collective-permute-done((bf16[2,2,32,1024]{3,2,1,0:T(8,128)(2,1)S(1)}, bf16[2,2,32,1024]{3,2,1,0:T(8,128)(2,1)S(1)}, u32[]{:S(2)}, u32[]{:S(2)}) %collective-permute-start.23) | collective-permute-done | bytes 262176 | tf_op jit(solution)/shard_map/ppermute | solution.py:72
  59.9 3.7 %collective-permute-done.6 = bf16[2,2,32,1024]{3,2,1,0:T(8,128)(2,1)S(1)} collective-permute-done((bf16[2,2,32,1024]{3,2,1,0:T(8,128)(2,1)S(1)}, bf16[2,2,32,1024]{3,2,1,0:T(8,128)(2,1)S(1)}, u32[]{:S(2)}, u32[]{:S(2)}) %collective-permute-start.6) | collective-permute-done | bytes 262176 | tf_op jit(solution)/shard_map/ppermute | solution.py:72
  65.7 4.4 %collective-permute-done.24 = bf16[2,2,32,1024]{3,2,1,0:T(8,128)(2,1)S(1)} collective-permute-done((bf16[2,2,32,1024]{3,2,1,0:T(8,128)(2,1)S(1)}, bf16[2,2,32,1024]{3,2,1,0:T(8,128)(2,1)S(1)}, u32[]{:S(2)}, u32[]{:S(2)}) %collective-permute-start.24) | collective-permute-done | bytes 262176 | tf_op jit(solution)/shard_map/ppermute | solution.py:72
  71.5 4.1 %collective-permute-done.7 = bf16[2,2,32,1024]{3,2,1,0:T(8,128)(2,1)S(1)} collective-permute-done((bf16[2,2,32,1024]{3,2,1,0:T(8,128)(2,1)S(1)}, bf16[2,2,32,1024]{3,2,1,0:T(8,128)(2,1)S(1)}, u32[]{:S(2)}, u32[]{:S(2)}) %collective-permute-start.7) | collective-permute-done | bytes 262176 | tf_op jit(solution)/shard_map/ppermute | solution.py:72
  78.9 2.1 %fusion.32 = f32[128,1024]{1,0:T(8,128)S(1)} fusion(bf16[128,1024]{1,0:T(8,128)(2,1)S(1)} %bitcast.264, bf16[1024,2048]{1,0:T(8,128)(2,1)} %collective-permute-done.8), kind=kOutput, calls=%fused_computation.70 | convolution fusion | flops 268435456 | bytes 2883584 | tf_op jit(solution)/shard_map/dot_general | solution.py:128
  81.5 2.6 %collective-permute-start.16 = (f16[2,2,32,1024]{3,2,0,1:T(8,128)(2,1)S(1)}, f16[2,2,32,1024]{3,2,0,1:T(8,128)(2,1)S(1)}, u32[]{:S(2)}, u32[]{:S(2)}) collective-permute-start(f16[2,2,32,1024]{3,2,0,1:T(8,128)(2,1)S(1)} %copy.9), channel_id=1, source_target_pairs={{0,8},{8,0},{4,12},{12,4},{1,9},{9,1},{5,13},{13,5},{2,10},{10,2},... | collective-permute-start | bytes 786440 | tf_op jit(solution)/shard_map/ppermute | solution.py:140
  84.1 2.1 %fusion.56 = f32[128,1024]{1,0:T(8,128)S(1)} fusion(bf16[128,1024]{1,0:T(8,128)(2,1)S(1)} %bitcast.259, bf16[1024,2048]{1,0:T(8,128)(2,1)} %collective-permute-done.8), kind=kOutput, calls=%fused_computation.94 | convolution fusion | flops 268435456 | bytes 2883584 | tf_op jit(solution)/shard_map/dot_general | solution.py:128
  94.5 2.0 %fusion.13 = f32[128,1024]{1,0:T(8,128)S(1)} fusion(f32[128,1024]{1,0:T(8,128)S(1)} %fusion.48, bf16[128,1024]{1,0:T(8,128)(2,1)S(1)} %bitcast.244, bf16[1024,2048]{1,0:T(8,128)(2,1)} %collective-permute-done.8), kind=kOutput, calls=%fused_computation.27 | convolution fusion | flops 268697600 | bytes 3407872 | tf_op jit(solution)/shard_map/dot_general | solution.py:128
  96.6 2.1 %fusion.15 = f32[128,1024]{1,0:T(8,128)S(1)} fusion(f32[128,1024]{1,0:T(8,128)S(1)} %fusion.72, bf16[128,1024]{1,0:T(8,128)(2,1)S(1)} %bitcast.245, bf16[1024,2048]{1,0:T(8,128)(2,1)} %collective-permute-done.8), kind=kOutput, calls=%fused_computation.31 | convolution fusion | flops 268697600 | bytes 3407872 | tf_op jit(solution)/shard_map/dot_general | solution.py:128
  98.7 2.0 %fusion.16 = f16[128,1024]{1,0:T(8,128)(2,1)S(1)} fusion(f32[128,1024]{1,0:T(8,128)S(1)} %fusion.70, bf16[128,1024]{1,0:T(8,128)(2,1)S(1)} %bitcast.252, bf16[1024,2048]{1,0:T(8,128)(2,1)} %collective-permute-done.8), kind=kOutput, calls=%fused_computation.32 | convolution fusion | flops 268828672 | bytes 3145728 | tf_op jit(solution)/shard_map/dot_general | solution.py:128
  104.8 5.0 %collective-permute-done.9 = f16[2,2,32,1024]{3,2,1,0:T(8,128)(2,1)S(1)} collective-permute-done((f16[2,2,32,1024]{3,2,1,0:T(8,128)(2,1)S(1)}, f16[2,2,32,1024]{3,2,1,0:T(8,128)(2,1)S(1)}, u32[]{:S(2)}, u32[]{:S(2)}) %collective-permute-start.9) | collective-permute-done | bytes 262176 | tf_op jit(solution)/shard_map/ppermute | solution.py:137
  114.8 2.7 %collective-permute-done.10 = f16[2,32,1024]{2,1,0:T(8,128)(2,1)S(1)} collective-permute-done((f16[2,32,1024]{2,1,0:T(8,128)(2,1)S(1)}, f16[2,32,1024]{2,1,0:T(8,128)(2,1)S(1)}, u32[]{:S(2)}, u32[]{:S(2)}) %collective-permute-start.10) | collective-permute-done | bytes 131104 | tf_op jit(solution)/shard_map/ppermute | solution.py:145
  120.7 2.1 %fusion.21 = f16[128,1024]{1,0:T(8,128)(2,1)S(1)} fusion(f32[128,1024]{1,0:T(8,128)S(1)} %fusion.40, bf16[128,1024]{1,0:T(8,128)(2,1)S(1)} %bitcast.265, bf16[1024,2048]{1,0:T(8,128)(2,1)} %collective-permute-done.8), kind=kOutput, calls=%fused_computation.37 | convolution fusion | flops 268828672 | bytes 3145728 | tf_op jit(solution)/shard_map/dot_general | solution.py:128
  125.5 2.1 %fusion.20 = f16[128,1024]{1,0:T(8,128)(2,1)S(1)} fusion(f32[128,1024]{1,0:T(8,128)S(1)} %fusion.64, bf16[128,1024]{1,0:T(8,128)(2,1)S(1)} %bitcast.260, bf16[1024,2048]{1,0:T(8,128)(2,1)} %collective-permute-done.8), kind=kOutput, calls=%fused_computation.36 | convolution fusion | flops 268828672 | bytes 3145728 | tf_op jit(solution)/shard_map/dot_general | solution.py:128
  129.4 2.1 %fusion.5 = f32[128,1024]{1,0:T(8,128)S(1)} fusion(f32[128,1024]{1,0:T(8,128)S(1)} %fusion.42, bf16[128,1024]{1,0:T(8,128)(2,1)S(1)} %bitcast.249, bf16[1024,2048]{1,0:T(8,128)(2,1)} %collective-permute-done.8), kind=kOutput, calls=%fused_computation.11 | convolution fusion | flops 268697600 | bytes 3407872 | tf_op jit(solution)/shard_map/dot_general | solution.py:128
  131.5 2.1 %fusion.7 = f32[128,1024]{1,0:T(8,128)S(1)} fusion(f32[128,1024]{1,0:T(8,128)S(1)} %fusion.66, bf16[128,1024]{1,0:T(8,128)(2,1)S(1)} %bitcast.250, bf16[1024,2048]{1,0:T(8,128)(2,1)} %collective-permute-done.8), kind=kOutput, calls=%fused_computation.15 | convolution fusion | flops 268697600 | bytes 3407872 | tf_op jit(solution)/shard_map/dot_general | solution.py:128
  134.0 2.1 %collective-permute-done.27 = f16[2,2,32,1024]{3,2,0,1:T(8,128)(2,1)S(1)} collective-permute-done((f16[2,2,32,1024]{3,2,0,1:T(8,128)(2,1)S(1)}, f16[2,2,32,1024]{3,2,0,1:T(8,128)(2,1)S(1)}, u32[]{:S(2)}, u32[]{:S(2)}) %collective-permute-start.27) | collective-permute-done | bytes 262176 | tf_op jit(solution)/shard_map/ppermute | solution.py:137
  136.5 2.5 %collective-permute-done.30 = f16[2,32,1024]{2,1,0:T(8,128)(2,1)S(1)} collective-permute-done((f16[2,32,1024]{2,1,0:T(8,128)(2,1)S(1)}, f16[2,32,1024]{2,1,0:T(8,128)(2,1)S(1)}, u32[]{:S(2)}, u32[]{:S(2)}) %collective-permute-start.30) | collective-permute-done | bytes 131104 | tf_op jit(solution)/shard_map/ppermute | solution.py:146
  139.0 2.2 %collective-permute-done.28 = f16[2,32,1024]{2,1,0:T(8,128)(2,1)S(1)} collective-permute-done((f16[2,32,1024]{2,1,0:T(8,128)(2,1)S(1)}, f16[2,32,1024]{2,1,0:T(8,128)(2,1)S(1)}, u32[]{:S(2)}, u32[]{:S(2)}) %collective-permute-start.28) | collective-permute-done | bytes 131104 | tf_op jit(solution)/shard_map/ppermute | solution.py:145
  141.6 2.1 %fusion.26 = f32[128,1024]{1,0:T(8,128)S(1)} fusion(bf16[128,1024]{1,0:T(8,128)(2,1)S(1)} %bitcast.274, bf16[1024,2048]{1,0:T(8,128)(2,1)} %collective-permute-done.8), kind=kOutput, calls=%fused_computation.64 | convolution fusion | flops 268435456 | bytes 2883584 | tf_op jit(solution)/shard_map/dot_general | solution.py:128
  147.0 2.5 %collective-permute-start.32 = (f16[2,2,32,1024]{3,2,0,1:T(8,128)(2,1)S(1)}, f16[2,2,32,1024]{3,2,0,1:T(8,128)(2,1)S(1)}, u32[]{:S(2)}, u32[]{:S(2)}) collective-permute-start(f16[2,2,32,1024]{3,2,0,1:T(8,128)(2,1)S(1)} %copy.15), channel_id=1, source_target_pairs={{0,4},{4,0},{8,12},{12,8},{1,5},{5,1},{9,13},{13,9},{2,6},{6,2},{1... | collective-permute-start | bytes 786440 | tf_op jit(solution)/shard_map/ppermute | solution.py:137
  149.6 2.0 %fusion.28 = f32[128,1024]{1,0:T(8,128)S(1)} fusion(bf16[128,1024]{1,0:T(8,128)(2,1)S(1)} %bitcast.256, bf16[1024,2048]{1,0:T(8,128)(2,1)} %collective-permute-done.8), kind=kOutput, calls=%fused_computation.66 | convolution fusion | flops 268435456 | bytes 2883584 | tf_op jit(solution)/shard_map/dot_general | solution.py:128
  156.9 2.8 %collective-permute-done.35 = f16[2,32,1024]{2,1,0:T(8,128)(2,1)S(1)} collective-permute-done((f16[2,32,1024]{2,1,0:T(8,128)(2,1)S(1)}, f16[2,32,1024]{2,1,0:T(8,128)(2,1)S(1)}, u32[]{:S(2)}, u32[]{:S(2)}) %collective-permute-start.35) | collective-permute-done | bytes 131104 | tf_op jit(solution)/shard_map/ppermute | solution.py:146
  (171 shorter events, 66.7 us)
Async XLA Ops:
  2.6 7.3 %collective-permute-start = (bf16[2,32,1024]{2,1,0:T(8,128)(2,1)S(1)}, bf16[2,32,1024]{2,1,0:T(8,128)(2,1)S(1)}, u32[]{:S(2)}, u32[]{:S(2)}) collective-permute-start(bf16[2,32,1024]{2,1,0:T(8,128)(2,1)S(1)} %constant_dynamic-slice_fusion.37), channel_id=1, source_target_pairs={{0,4},{4,0},{8,12},{12,8},{1,5},{5,1},{9,13},{13,9},{2,6},{6,2},{1... | collective-permute-start | bytes 393224 | tf_op jit(solution)/shard_map/ppermute | solution.py:56
  5.6 16.0 %collective-permute-start.18 = (bf16[2,32,1024]{2,1,0:T(8,128)(2,1)S(1)}, bf16[2,32,1024]{2,1,0:T(8,128)(2,1)S(1)}, u32[]{:S(2)}, u32[]{:S(2)}) collective-permute-start(bf16[2,32,1024]{2,1,0:T(8,128)(2,1)S(1)} %constant_dynamic-slice_fusion.18), channel_id=1, source_target_pairs={{0,4},{4,0},{8,12},{12,8},{1,5},{5,1},{9,13},{13,9},{2,6},{6,2},{1... | collective-permute-start | bytes 393224 | tf_op jit(solution)/shard_map/ppermute | solution.py:56
  18.4 60.5 %collective-permute-start.8 = (bf16[1024,2048]{1,0:T(8,128)(2,1)}, bf16[1024,2048]{1,0:T(8,128)(2,1)}, u32[]{:S(2)}, u32[]{:S(2)}) collective-permute-start(bf16[1024,2048]{1,0:T(8,128)(2,1)} %get-tuple-element.11), channel_id=1, source_target_pairs={{0,16},{16,0},{1,17},{17,1},{2,18},{18,2},{3,19},{19,3},{4,20},{20... | collective-permute-start | bytes 12582920 | tf_op jit(solution)/shard_map/ppermute | solution.py:100
  20.8 6.1 %collective-permute-start.1 = (bf16[2,2,32,1024]{3,2,1,0:T(8,128)(2,1)S(1)}, bf16[2,2,32,1024]{3,2,1,0:T(8,128)(2,1)S(1)}, u32[]{:S(2)}, u32[]{:S(2)}) collective-permute-start(bf16[2,2,32,1024]{3,2,1,0:T(8,128)(2,1)S(1)} %pad_maximum_fusion.4), channel_id=1, source_target_pairs={{1,8},{8,1},{3,10},{10,3},{5,12},{12,5},{7,14},{14,7},{17,24},{24,... | collective-permute-start | bytes 786440 | tf_op jit(solution)/shard_map/ppermute | solution.py:61
  25.3 14.1 %collective-permute-start.19 = (bf16[2,2,32,1024]{3,2,1,0:T(8,128)(2,1)S(1)}, bf16[2,2,32,1024]{3,2,1,0:T(8,128)(2,1)S(1)}, u32[]{:S(2)}, u32[]{:S(2)}) collective-permute-start(bf16[2,2,32,1024]{3,2,1,0:T(8,128)(2,1)S(1)} %pad_maximum_fusion.5), channel_id=1, source_target_pairs={{1,8},{8,1},{3,10},{10,3},{5,12},{12,5},{7,14},{14,7},{17,24},{24,... | collective-permute-start | bytes 786440 | tf_op jit(solution)/shard_map/ppermute | solution.py:61
  27.0 21.2 %collective-permute-start.2 = (bf16[2,2,32,1024]{3,2,1,0:T(8,128)(2,1)S(1)}, bf16[2,2,32,1024]{3,2,1,0:T(8,128)(2,1)S(1)}, u32[]{:S(2)}, u32[]{:S(2)}) collective-permute-start(bf16[2,2,32,1024]{3,2,1,0:T(8,128)(2,1)S(1)} %broadcast_select_fusion.1), channel_id=1, source_target_pairs={{0,1},{1,2},{2,3},{4,5},{5,6},{6,7},{8,9},{9,10},{10,11},{12,13},{... | collective-permute-start | bytes 786440 | tf_op jit(solution)/shard_map/ppermute | solution.py:69
  37.5 11.4 %collective-permute-start.5 = (bf16[2,2,32,1024]{3,2,1,0:T(8,128)(2,1)S(1)}, bf16[2,2,32,1024]{3,2,1,0:T(8,128)(2,1)S(1)}, u32[]{:S(2)}, u32[]{:S(2)}) collective-permute-start(bf16[2,2,32,1024]{3,2,1,0:T(8,128)(2,1)S(1)} %broadcast_select_fusion.1), channel_id=1, source_target_pairs={{1,0},{2,1},{3,2},{5,4},{6,5},{7,6},{9,8},{10,9},{11,10},{13,12},{... | collective-permute-start | bytes 786440 | tf_op jit(solution)/shard_map/ppermute | solution.py:72
  39.5 7.4 %collective-permute-start.40 = (f32[64]{0:T(128)S(1)}, f32[64]{0:T(128)S(1)}, u32[]{:S(2)}, u32[]{:S(2)}) collective-permute-start(f32[64]{0:T(128)S(1)} %get-tuple-element.76), channel_id=1, source_target_pairs={{0,4},{4,12},{8,20},{12,28},{16,0},{20,8},{24,16},{28,24},{1,5},{5... | collective-permute-start | bytes 776 | tf_op jit(solution)/shard_map/ppermute | solution.py:112
  42.3 10.9 %collective-permute-start.20 = (bf16[2,2,32,1024]{3,2,1,0:T(8,128)(2,1)S(1)}, bf16[2,2,32,1024]{3,2,1,0:T(8,128)(2,1)S(1)}, u32[]{:S(2)}, u32[]{:S(2)}) collective-permute-start(bf16[2,2,32,1024]{3,2,1,0:T(8,128)(2,1)S(1)} %broadcast_select_fusion), channel_id=1, source_target_pairs={{0,1},{1,2},{2,3},{4,5},{5,6},{6,7},{8,9},{9,10},{10,11},{12,13},{... | collective-permute-start | bytes 786440 | tf_op jit(solution)/shard_map/ppermute | solution.py:69
  46.9 11.0 %collective-permute-start.23 = (bf16[2,2,32,1024]{3,2,1,0:T(8,128)(2,1)S(1)}, bf16[2,2,32,1024]{3,2,1,0:T(8,128)(2,1)S(1)}, u32[]{:S(2)}, u32[]{:S(2)}) collective-permute-start(bf16[2,2,32,1024]{3,2,1,0:T(8,128)(2,1)S(1)} %broadcast_select_fusion), channel_id=1, source_target_pairs={{1,0},{2,1},{3,2},{5,4},{6,5},{7,6},{9,8},{10,9},{11,10},{13,12},{... | collective-permute-start | bytes 786440 | tf_op jit(solution)/shard_map/ppermute | solution.py:72
  48.2 11.0 %collective-permute-start.3 = (bf16[2,2,32,1024]{3,2,1,0:T(8,128)(2,1)S(1)}, bf16[2,2,32,1024]{3,2,1,0:T(8,128)(2,1)S(1)}, u32[]{:S(2)}, u32[]{:S(2)}) collective-permute-start(bf16[2,2,32,1024]{3,2,1,0:T(8,128)(2,1)S(1)} %collective-permute-done.2), channel_id=1, source_target_pairs={{1,2},{2,3},{5,6},{6,7},{9,10},{10,11},{13,14},{14,15},{17,18},{18... | collective-permute-start | bytes 786440 | tf_op jit(solution)/shard_map/ppermute | solution.py:69
  48.9 14.8 %collective-permute-start.6 = (bf16[2,2,32,1024]{3,2,1,0:T(8,128)(2,1)S(1)}, bf16[2,2,32,1024]{3,2,1,0:T(8,128)(2,1)S(1)}, u32[]{:S(2)}, u32[]{:S(2)}) collective-permute-start(bf16[2,2,32,1024]{3,2,1,0:T(8,128)(2,1)S(1)} %collective-permute-done.5), channel_id=1, source_target_pairs={{1,0},{2,1},{5,4},{6,5},{9,8},{10,9},{13,12},{14,13},{17,16},{18,1... | collective-permute-start | bytes 786440 | tf_op jit(solution)/shard_map/ppermute | solution.py:72
  53.3 11.7 %collective-permute-start.21 = (bf16[2,2,32,1024]{3,2,1,0:T(8,128)(2,1)S(1)}, bf16[2,2,32,1024]{3,2,1,0:T(8,128)(2,1)S(1)}, u32[]{:S(2)}, u32[]{:S(2)}) collective-permute-start(bf16[2,2,32,1024]{3,2,1,0:T(8,128)(2,1)S(1)} %collective-permute-done.20), channel_id=1, source_target_pairs={{1,2},{2,3},{5,6},{6,7},{9,10},{10,11},{13,14},{14,15},{17,18},{18... | collective-permute-start | bytes 786440 | tf_op jit(solution)/shard_map/ppermute | solution.py:69
  58.0 12.1 %collective-permute-start.24 = (bf16[2,2,32,1024]{3,2,1,0:T(8,128)(2,1)S(1)}, bf16[2,2,32,1024]{3,2,1,0:T(8,128)(2,1)S(1)}, u32[]{:S(2)}, u32[]{:S(2)}) collective-permute-start(bf16[2,2,32,1024]{3,2,1,0:T(8,128)(2,1)S(1)} %collective-permute-done.23), channel_id=1, source_target_pairs={{1,0},{2,1},{5,4},{6,5},{9,8},{10,9},{13,12},{14,13},{17,16},{18,1... | collective-permute-start | bytes 786440 | tf_op jit(solution)/shard_map/ppermute | solution.py:72
  59.3 12.3 %collective-permute-start.4 = (bf16[2,2,32,1024]{3,2,1,0:T(8,128)(2,1)S(1)}, bf16[2,2,32,1024]{3,2,1,0:T(8,128)(2,1)S(1)}, u32[]{:S(2)}, u32[]{:S(2)}) collective-permute-start(bf16[2,2,32,1024]{3,2,1,0:T(8,128)(2,1)S(1)} %collective-permute-done.3), channel_id=1, source_target_pairs={{2,3},{6,7},{10,11},{14,15},{18,19},{22,23},{26,27},{30,31}} | collective-permute-start | bytes 786440 | tf_op jit(solution)/shard_map/ppermute | solution.py:69
  63.7 12.0 %collective-permute-start.7 = (bf16[2,2,32,1024]{3,2,1,0:T(8,128)(2,1)S(1)}, bf16[2,2,32,1024]{3,2,1,0:T(8,128)(2,1)S(1)}, u32[]{:S(2)}, u32[]{:S(2)}) collective-permute-start(bf16[2,2,32,1024]{3,2,1,0:T(8,128)(2,1)S(1)} %collective-permute-done.6), channel_id=1, source_target_pairs={{1,0},{5,4},{9,8},{13,12},{17,16},{21,20},{25,24},{29,28}} | collective-permute-start | bytes 786440 | tf_op jit(solution)/shard_map/ppermute | solution.py:72
  65.0 52.9 %collective-permute-start.22 = (bf16[2,2,32,1024]{3,2,1,0:T(8,128)(2,1)S(1)}, bf16[2,2,32,1024]{3,2,1,0:T(8,128)(2,1)S(1)}, u32[]{:S(2)}, u32[]{:S(2)}) collective-permute-start(bf16[2,2,32,1024]{3,2,1,0:T(8,128)(2,1)S(1)} %collective-permute-done.21), channel_id=1, source_target_pairs={{2,3},{6,7},{10,11},{14,15},{18,19},{22,23},{26,27},{30,31}} | collective-permute-start | bytes 786440 | tf_op jit(solution)/shard_map/ppermute | solution.py:69
  70.1 47.8 %collective-permute-start.25 = (bf16[2,2,32,1024]{3,2,1,0:T(8,128)(2,1)S(1)}, bf16[2,2,32,1024]{3,2,1,0:T(8,128)(2,1)S(1)}, u32[]{:S(2)}, u32[]{:S(2)}) collective-permute-start(bf16[2,2,32,1024]{3,2,1,0:T(8,128)(2,1)S(1)} %collective-permute-done.24), channel_id=1, source_target_pairs={{1,0},{5,4},{9,8},{13,12},{17,16},{21,20},{25,24},{29,28}} | collective-permute-start | bytes 786440 | tf_op jit(solution)/shard_map/ppermute | solution.py:72
  81.5 19.3 %collective-permute-start.16 = (f16[2,2,32,1024]{3,2,0,1:T(8,128)(2,1)S(1)}, f16[2,2,32,1024]{3,2,0,1:T(8,128)(2,1)S(1)}, u32[]{:S(2)}, u32[]{:S(2)}) collective-permute-start(f16[2,2,32,1024]{3,2,0,1:T(8,128)(2,1)S(1)} %copy.9), channel_id=1, source_target_pairs={{0,8},{8,0},{4,12},{12,4},{1,9},{9,1},{5,13},{13,5},{2,10},{10,2},... | collective-permute-start | bytes 786440 | tf_op jit(solution)/shard_map/ppermute | solution.py:140
  86.7 15.7 %collective-permute-start.14 = (f16[2,2,32,1024]{3,2,0,1:T(8,128)(2,1)S(1)}, f16[2,2,32,1024]{3,2,0,1:T(8,128)(2,1)S(1)}, u32[]{:S(2)}, u32[]{:S(2)}) collective-permute-start(f16[2,2,32,1024]{3,2,0,1:T(8,128)(2,1)S(1)} %copy.7), channel_id=1, source_target_pairs={{0,4},{4,0},{8,12},{12,8},{1,5},{5,1},{9,13},{13,9},{2,6},{6,2},{1... | collective-permute-start | bytes 786440 | tf_op jit(solution)/shard_map/ppermute | solution.py:137
  88.9 14.2 %collective-permute-start.11 = (f16[2,2,32,1024]{3,2,0,1:T(8,128)(2,1)S(1)}, f16[2,2,32,1024]{3,2,0,1:T(8,128)(2,1)S(1)}, u32[]{:S(2)}, u32[]{:S(2)}) collective-permute-start(f16[2,2,32,1024]{3,2,0,1:T(8,128)(2,1)S(1)} %copy.5), channel_id=1, source_target_pairs={{0,8},{8,0},{4,12},{12,4},{1,9},{9,1},{5,13},{13,5},{2,10},{10,2},... | collective-permute-start | bytes 786440 | tf_op jit(solution)/shard_map/ppermute | solution.py:140
  100.7 9.1 %collective-permute-start.9 = (f16[2,2,32,1024]{3,2,1,0:T(8,128)(2,1)S(1)}, f16[2,2,32,1024]{3,2,1,0:T(8,128)(2,1)S(1)}, u32[]{:S(2)}, u32[]{:S(2)}) collective-permute-start(f16[2,2,32,1024]{3,2,1,0:T(8,128)(2,1)S(1)} %bitcast.290), channel_id=1, source_target_pairs={{0,4},{4,0},{8,12},{12,8},{1,5},{5,1},{9,13},{13,9},{2,6},{6,2},{1... | collective-permute-start | bytes 786440 | tf_op jit(solution)/shard_map/ppermute | solution.py:137
  102.4 10.2 %collective-permute-start.17 = (f16[2,32,1024]{2,1,0:T(8,128)(2,1)S(1)}, f16[2,32,1024]{2,1,0:T(8,128)(2,1)S(1)}, u32[]{:S(2)}, u32[]{:S(2)}) collective-permute-start(f16[2,32,1024]{2,1,0:T(8,128)(2,1)S(1)} %fusion.86), channel_id=1, source_target_pairs={{0,4},{4,0},{8,12},{12,8},{1,5},{5,1},{9,13},{13,9},{2,6},{6,2},{1... | collective-permute-start | bytes 393224 | tf_op jit(solution)/shard_map/ppermute | solution.py:146
  103.1 11.2 %collective-permute-start.15 = (f16[2,32,1024]{2,1,0:T(8,128)(2,1)S(1)}, f16[2,32,1024]{2,1,0:T(8,128)(2,1)S(1)}, u32[]{:S(2)}, u32[]{:S(2)}) collective-permute-start(f16[2,32,1024]{2,1,0:T(8,128)(2,1)S(1)} %fusion.85), channel_id=1, source_target_pairs={{0,8},{8,0},{4,12},{12,4},{1,9},{9,1},{5,13},{13,5},{2,10},{10,2},... | collective-permute-start | bytes 393224 | tf_op jit(solution)/shard_map/ppermute | solution.py:145
  119.4 21.9 %collective-permute-start.31 = (bf16[2,2,2,2,32,1024]{5,4,3,2,1,0:T(8,128)(2,1)S(1)}, bf16[2,2,2,2,32,1024]{5,4,3,2,1,0:T(8,128)(2,1)S(1)}, u32[]{:S(2)}, u32[]{:S(2)}) collective-permute-start(bf16[2,2,2,2,32,1024]{5,4,3,2,1,0:T(8,128)(2,1)S(1)} %bitcast.229), channel_id=1, source_target_pairs={{0,16},{16,0},{1,17},{17,1},{2,18},{18,2},{3,19},{19,3},{4,20},{20... | collective-permute-start | bytes 3145736 | tf_op jit(solution)/shard_map/ppermute | solution.py:157
  122.8 10.7 %collective-permute-start.29 = (f16[2,2,32,1024]{3,2,0,1:T(8,128)(2,1)S(1)}, f16[2,2,32,1024]{3,2,0,1:T(8,128)(2,1)S(1)}, u32[]{:S(2)}, u32[]{:S(2)}) collective-permute-start(f16[2,2,32,1024]{3,2,0,1:T(8,128)(2,1)S(1)} %copy.13), channel_id=1, source_target_pairs={{0,8},{8,0},{4,12},{12,4},{1,9},{9,1},{5,13},{13,5},{2,10},{10,2},... | collective-permute-start | bytes 786440 | tf_op jit(solution)/shard_map/ppermute | solution.py:140
  127.6 8.5 %collective-permute-start.27 = (f16[2,2,32,1024]{3,2,0,1:T(8,128)(2,1)S(1)}, f16[2,2,32,1024]{3,2,0,1:T(8,128)(2,1)S(1)}, u32[]{:S(2)}, u32[]{:S(2)}) collective-permute-start(f16[2,2,32,1024]{3,2,0,1:T(8,128)(2,1)S(1)} %copy.11), channel_id=1, source_target_pairs={{0,4},{4,0},{8,12},{12,8},{1,5},{5,1},{9,13},{13,9},{2,6},{6,2},{1... | collective-permute-start | bytes 786440 | tf_op jit(solution)/shard_map/ppermute | solution.py:137
  133.7 5.3 %collective-permute-start.30 = (f16[2,32,1024]{2,1,0:T(8,128)(2,1)S(1)}, f16[2,32,1024]{2,1,0:T(8,128)(2,1)S(1)}, u32[]{:S(2)}, u32[]{:S(2)}) collective-permute-start(f16[2,32,1024]{2,1,0:T(8,128)(2,1)S(1)} %fusion.88), channel_id=1, source_target_pairs={{0,4},{4,0},{8,12},{12,8},{1,5},{5,1},{9,13},{13,9},{2,6},{6,2},{1... | collective-permute-start | bytes 393224 | tf_op jit(solution)/shard_map/ppermute | solution.py:146
  136.2 5.0 %collective-permute-start.28 = (f16[2,32,1024]{2,1,0:T(8,128)(2,1)S(1)}, f16[2,32,1024]{2,1,0:T(8,128)(2,1)S(1)}, u32[]{:S(2)}, u32[]{:S(2)}) collective-permute-start(f16[2,32,1024]{2,1,0:T(8,128)(2,1)S(1)} %fusion.87), channel_id=1, source_target_pairs={{0,8},{8,0},{4,12},{12,4},{1,9},{9,1},{5,13},{13,5},{2,10},{10,2},... | collective-permute-start | bytes 393224 | tf_op jit(solution)/shard_map/ppermute | solution.py:145
  144.1 10.5 %collective-permute-start.34 = (f16[2,2,32,1024]{3,2,1,0:T(8,128)(2,1)S(1)}, f16[2,2,32,1024]{3,2,1,0:T(8,128)(2,1)S(1)}, u32[]{:S(2)}, u32[]{:S(2)}) collective-permute-start(f16[2,2,32,1024]{3,2,1,0:T(8,128)(2,1)S(1)} %bitcast.289), channel_id=1, source_target_pairs={{0,8},{8,0},{4,12},{12,4},{1,9},{9,1},{5,13},{13,5},{2,10},{10,2},... | collective-permute-start | bytes 786440 | tf_op jit(solution)/shard_map/ppermute | solution.py:140
  147.0 7.8 %collective-permute-start.32 = (f16[2,2,32,1024]{3,2,0,1:T(8,128)(2,1)S(1)}, f16[2,2,32,1024]{3,2,0,1:T(8,128)(2,1)S(1)}, u32[]{:S(2)}, u32[]{:S(2)}) collective-permute-start(f16[2,2,32,1024]{3,2,0,1:T(8,128)(2,1)S(1)} %copy.15), channel_id=1, source_target_pairs={{0,4},{4,0},{8,12},{12,8},{1,5},{5,1},{9,13},{13,9},{2,6},{6,2},{1... | collective-permute-start | bytes 786440 | tf_op jit(solution)/shard_map/ppermute | solution.py:137
  164.5 5.4 %collective-permute-start.41 = (f32[4,64]{1,0:T(4,128)S(1)}, f32[4,64]{1,0:T(4,128)S(1)}, u32[]{:S(2)}, u32[]{:S(2)}) collective-permute-start(f32[4,64]{1,0:T(4,128)S(1)} %get-tuple-element.68), channel_id=1, source_target_pairs={{0,1},{1,2},{2,3},{3,0},{4,5},{5,6},{6,7},{7,4},{8,9},{9,10},{10,1... | collective-permute-start | bytes 3080 | tf_op jit(solution)/shard_map/ppermute | solution.py:186
  (14 other events, 80.3 us)

commit v5 on v4

--- a/solution.py
+++ b/solution.py
@@ -1,6 +1,8 @@
 import jax
 import jax.numpy as jnp
 from jax import lax
+from jax.experimental import pallas as pl
+from jax.experimental.pallas import tpu as pltpu
 from jax.sharding import PartitionSpec as P
 
 EPS = 1e-05
@@ -8,6 +10,7 @@
 CHUNKS = 2
 SHRINK = 1.0 / 32.0
 SUM_TYPE = jnp.float16
+TILE = 512
 
 X_SWAP = [(0, 1), (1, 0), (2, 3), (3, 2)]
 Y_SWAP = [(0, 2), (2, 0), (1, 3), (3, 1)]
@@ -20,6 +23,40 @@
 
 def after(value, *others):
     return lax.optimization_barrier((value, *others))[0]
+
+
+def logits_kernel(core_ref, left_ref, keep_ref, take_ref, out_ref):
+    core = core_ref[0]
+    out = jnp.dot(left_ref[core], keep_ref[...], preferred_element_type=jnp.float32)
+    out += jnp.dot(left_ref[1 - core], take_ref[...], preferred_element_type=jnp.float32)
+    out_ref[...] = out * SHRINK
+
+
+def partial_logits(core, left, head_weight, take):
+    _, rows, block = left.shape
+    width = take.shape[1]
+    tile = min(TILE, width)
+    tiles = width // tile
+    return pl.pallas_call(
+        logits_kernel,
+        grid_spec=pltpu.PrefetchScalarGridSpec(
+            num_scalar_prefetch=1,
+            grid=(tiles,),
+            in_specs=[
+                pl.BlockSpec((2, rows, block), lambda t, core: (0, 0, 0)),
+                pl.BlockSpec((block, tile), lambda t, core: (0, core[0] * tiles + t)),
+                pl.BlockSpec((block, tile), lambda t, core: (0, t)),
+            ],
+            out_specs=pl.BlockSpec((rows, tile), lambda t, core: (0, t)),
+        ),
+        out_shape=jax.ShapeDtypeStruct((rows, width), jnp.float32),
+        compiler_params=pltpu.CompilerParams(vmem_limit_bytes=24 * 1024 * 1024),
+        cost_estimate=pl.CostEstimate(
+            flops=4 * rows * block * width,
+            bytes_accessed=4 * block * width + 4 * rows * block + 4 * rows * width,
+            transcendentals=0,
+        ),
+    )(core.reshape(1).astype(jnp.int32), left, head_weight, take)
 
 
 def on_device(hidden, norm_gain, head_weight):
@@ -58,6 +95,10 @@
         for piece, other in zip(pieces, sides):
             mine = lax.dynamic_slice_in_dim(piece, x * block, block, 2)
             own = jnp.stack([jnp.where(x == 0, mine, other), jnp.where(x == 0, other, mine)])
+            if held:
+                own = after(own, held[-1])
+            else:
+                begun = own
             moved = lax.ppermute(own, ("batch", "vocab"), diagonal)
             held.append(jnp.where((level + y) % 2 == 1, moved, own))
 
@@ -81,7 +122,7 @@
                         part = jnp.where(level == z - k, above[k], part)
                 ordered.append(part)
             wholes.append(jnp.stack(ordered).reshape(2, 2, 2, 2, step, block))
-        return wholes, held, sides[0]
+        return wholes, held, begun
 
     def gathered_features():
         wholes = []
@@ -96,13 +137,12 @@
     lined = depth == 2 * block and vocab == 4
     found, held, begun = line_features() if lined else gathered_features()
 
-    give = lax.dynamic_slice_in_dim(head_weight, (1 - core) * width, width, 1)
+    side = after(core, begun)
+    give = lax.dynamic_slice_in_dim(head_weight, (1 - side) * width, width, 1)
     take = lax.ppermute(give, "pair", CORE_SWAP)
-    side = after(core, begun)
-    keep = lax.optimization_barrier(lax.dynamic_slice_in_dim(head_weight, side * width, width, 1))
 
     squares = jnp.sum(wide * wide, axis=1)
-    squares = after(squares, begun)
+    squares = after(squares, held[-1])
     reach = 1
     while reach < vocab:
         squares += lax.ppermute(squares, "vocab", [(i, i ^ reach) for i in range(vocab)])
@@ -119,29 +159,15 @@
     total_sq = jnp.stack([jnp.where(x == 0, sent[0], sent[1]), jnp.where(x == 0, sent[1], sent[0])])
     scale = lax.rsqrt(total_sq / model + EPS) / SHRINK
 
-    def partial(left, low, high):
-        lead = left.shape[1:-1]
-        out = jnp.dot(
-            pick(left, core, 0).reshape(-1, block),
-            keep[:, low:high],
-            preferred_element_type=jnp.float32,
-        ) + jnp.dot(
-            pick(left, 1 - core, 0).reshape(-1, block),
-            take[:, low:high],
-            preferred_element_type=jnp.float32,
-        )
-        return (out * SHRINK).reshape(*lead, high - low)
-
     def reduced(left):
         middle = width // 2
-        away_x = lax.ppermute(
-            partial(pick(left, 1 - x, 3), 0, middle).astype(SUM_TYPE), "batch", X_SWAP
-        )
-        away_y = lax.ppermute(
-            partial(pick(left, 1 - y, 2), middle, width).astype(SUM_TYPE), "batch", Y_SWAP
-        )
-        sum_x = partial(pick(left, x, 3), 0, middle) + away_x.astype(jnp.float32)
-        sum_y = partial(pick(left, y, 2), middle, width) + away_y.astype(jnp.float32)
+        parts = partial_logits(core, left.reshape(2, -1, block), head_weight, take)
+        parts = parts.reshape(2, 2, 2, step, width)
+        low, high = parts[..., :middle], parts[..., middle:]
+        away_x = lax.ppermute(pick(low, 1 - x, 2).astype(SUM_TYPE), "batch", X_SWAP)
+        away_y = lax.ppermute(pick(high, 1 - y, 1).astype(SUM_TYPE), "batch", Y_SWAP)
+        sum_x = pick(low, x, 2) + away_x.astype(jnp.float32)
+        sum_y = pick(high, y, 1) + away_y.astype(jnp.float32)
         next_y = lax.ppermute(pick(sum_x, 1 - y, 1).astype(SUM_TYPE), "batch", Y_SWAP)
         next_x = lax.ppermute(pick(sum_y, 1 - x, 1).astype(SUM_TYPE), "batch", X_SWAP)
         return jnp.concatenate(

time: 173 us -> 171 us (0.988)
  matrix products: 40 us -> 0 us
  Pallas kernels: 0 us -> 20.3 us
  waiting for transfers between devices: 51.5 us -> 67 us
  starting transfers between devices: 60.7 us -> 64 us
    dot_general x32 -> x0, matrix products: 40 us -> none  [the longest x16 32.8 us: partial(): jnp.dot(pick(left, 1 - core, 0).reshape(-1, block), take[:, low:high], pr...]
    pallas_call x0 -> x4, Pallas kernels: none -> 20.3 us  [partial_logits(): pl.pallas_call(logits_kernel, grid_spec=pltpu.PrefetchScalarGridSpec(num_...]
    ppermute x2, waiting for transfers between devices: 1.47 us -> 8.57 us  [on_device(): lax.ppermute(squares, 'vocab', [(i, i ^ reach) for i in range(vocab)])]
    ppermute x8, waiting for transfers between devices: 7.17 us -> 14.1 us  [the longest x4 11.7 us: reduced(): away_x = lax.ppermute(pick(low, 1 - x, 2).astype(SUM_TYPE), 'batch', X_SWAP)]
    dynamic_slice x1, local copies, waits for them, and re-layouts: 8.46 us -> 4.73 us  [on_device(): give = lax.dynamic_slice_in_dim(head_weight, (1 - side) * width, width, 1)]
    unnamed x5, local copies, waits for them, and re-layouts: 0.05 us -> 3.43 us
    ppermute x4, starting transfers between devices: 2.76 us -> 5.89 us  [reduced(): lax.ppermute(pick(sum_y, 1 - x, 1).astype(SUM_TYPE), 'batch', X_SWAP)]
    ppermute x2, waiting for transfers between devices: 4.18 us -> 6.99 us  [line_features(): sides = [lax.ppermute(side, 'batch', X_SWAP) for side in sides]]
  transfers between devices with their start and end apart: 44 -> 44, of which waited for: 23 -> 25; matrix products, arithmetic and copies ran while one was open for 29% -> 2% of each run, Pallas kernels for 0% -> 12%
where the time goes in v5:
time: 171 us
  waiting for transfers between devices  67 us (39%)
  starting transfers between devices  64 us (37%)
  Pallas kernels  20.3 us (12%)
  local copies, waits for them, and re-layouts  10 us (6%)
  other arithmetic  7.71 us (5%)
    pallas_call x4, Pallas kernels, partial_logits(): pl.pallas_call(logits_kernel, grid_spec=pltpu.PrefetchScalarGridSpec(num_...  20.3 us
    ppermute x6, waiting for transfers between devices, line_features(): lax.ppermute(above[-1], 'vocab', [(z + 1, z) for z in range(vocab - k)])  17.7 us
    ppermute x6, starting transfers between devices, line_features(): lax.ppermute(below[-1], 'vocab', [(z, z + 1) for z in range(k - 1, vocab...  15 us
    ppermute x4, waiting for transfers between devices, reduced(): away_x = lax.ppermute(pick(low, 1 - x, 2).astype(SUM_TYPE), 'batch', X_SWAP)  11.7 us
    ppermute x2, waiting for transfers between devices, on_device(): lax.ppermute(squares, 'vocab', [(i, i ^ reach) for i in range(vocab)])  8.57 us
    ppermute x6, starting transfers between devices, line_features(): lax.ppermute(above[-1], 'vocab', [(z + 1, z) for z in range(vocab - k)])  7.72 us
    ppermute x2, waiting for transfers between devices, line_features(): sides = [lax.ppermute(side, 'batch', X_SWAP) for side in sides]  6.99 us
    ppermute x4, starting transfers between devices, reduced(): away_x = lax.ppermute(pick(low, 1 - x, 2).astype(SUM_TYPE), 'batch', X_SWAP)  6.64 us
  transfers between devices with their start and end apart: 44, of which 25 were waited for; matrix products, arithmetic and copies ran while one was open for 2% of the time, Pallas kernels for 12%

profile of v5, /device:TPU:0, one launch (start us, length us, event | category | flops | bytes accessed | tf_op | source)
XLA Modules:
  0.0 170.6 jit_solution(3517018133771287470)
XLA Ops:
  2.6 3.0 %collective-permute-start = (bf16[2,32,1024]{2,1,0:T(8,128)(2,1)S(1)}, bf16[2,32,1024]{2,1,0:T(8,128)(2,1)S(1)}, u32[]{:S(2)}, u32[]{:S(2)}) collective-permute-start(bf16[2,32,1024]{2,1,0:T(8,128)(2,1)S(1)} %constant_dynamic-slice_fusion.16), channel_id=1, source_target_pairs={{0,4},{4,0},{8,12},{12,8},{1,5},{5,1},{9,13},{13,9},{2,6},{6,2},{1... | collective-permute-start | bytes 393224 | tf_op jit(solution)/shard_map/ppermute | solution.py:93
  5.6 3.5 %collective-permute-done = bf16[2,32,1024]{2,1,0:T(8,128)(2,1)S(1)} collective-permute-done((bf16[2,32,1024]{2,1,0:T(8,128)(2,1)S(1)}, bf16[2,32,1024]{2,1,0:T(8,128)(2,1)S(1)}, u32[]{:S(2)}, u32[]{:S(2)}) %collective-permute-start) | collective-permute-done | bytes 131104 | tf_op jit(solution)/shard_map/ppermute | solution.py:93
  9.2 4.7 %constant_dynamic-slice_fusion.15 = bf16[1024,2048]{1,0:T(8,128)(2,1)} fusion(bf16[1024,4096]{1,0:T(8,128)(2,1)} %keep_ref.7, s32[]{:T(128)S(6)} %select_n.292), kind=kLoop, calls=%fused_computation.127 | loop fusion | bytes 8388612 | tf_op jit(solution)/shard_map/dynamic_slice | solution.py:141
  13.9 1.8 %collective-permute-start.18 = (bf16[2,32,1024]{2,1,0:T(8,128)(2,1)S(1)}, bf16[2,32,1024]{2,1,0:T(8,128)(2,1)S(1)}, u32[]{:S(2)}, u32[]{:S(2)}) collective-permute-start(bf16[2,32,1024]{2,1,0:T(8,128)(2,1)S(1)} %constant_dynamic-slice_fusion.8), channel_id=1, source_target_pairs={{0,4},{4,0},{8,12},{12,8},{1,5},{5,1},{9,13},{13,9},{2,6},{6,2},{1... | collective-permute-start | bytes 393224 | tf_op jit(solution)/shard_map/ppermute | solution.py:93
  16.4 3.5 %collective-permute-done.18 = bf16[2,32,1024]{2,1,0:T(8,128)(2,1)S(1)} collective-permute-done((bf16[2,32,1024]{2,1,0:T(8,128)(2,1)S(1)}, bf16[2,32,1024]{2,1,0:T(8,128)(2,1)S(1)}, u32[]{:S(2)}, u32[]{:S(2)}) %collective-permute-start.18) | collective-permute-done | bytes 131104 | tf_op jit(solution)/shard_map/ppermute | solution.py:93
  20.0 10.4 %collective-permute-start.2 = (bf16[2,2,32,1024]{3,2,1,0:T(8,128)(2,1)S(1)}, bf16[2,2,32,1024]{3,2,1,0:T(8,128)(2,1)S(1)}, u32[]{:S(2)}, u32[]{:S(2)}) collective-permute-start(bf16[2,2,32,1024]{3,2,1,0:T(8,128)(2,1)S(1)} %broadcast_select_fusion.1), channel_id=1, source_target_pairs={{0,1},{1,2},{2,3},{4,5},{5,6},{6,7},{8,9},{9,10},{10,11},{12,13},{... | collective-permute-start | bytes 786440 | tf_op jit(solution)/shard_map/ppermute | solution.py:110
  32.7 2.9 %collective-permute-done.2 = bf16[2,2,32,1024]{3,2,1,0:T(8,128)(2,1)S(1)} collective-permute-done((bf16[2,2,32,1024]{3,2,1,0:T(8,128)(2,1)S(1)}, bf16[2,2,32,1024]{3,2,1,0:T(8,128)(2,1)S(1)}, u32[]{:S(2)}, u32[]{:S(2)}) %collective-permute-start.2) | collective-permute-done | bytes 262176 | tf_op jit(solution)/shard_map/ppermute | solution.py:110
  36.3 5.4 %collective-permute-done.5 = bf16[2,2,32,1024]{3,2,1,0:T(8,128)(2,1)S(1)} collective-permute-done((bf16[2,2,32,1024]{3,2,1,0:T(8,128)(2,1)S(1)}, bf16[2,2,32,1024]{3,2,1,0:T(8,128)(2,1)S(1)}, u32[]{:S(2)}, u32[]{:S(2)}) %collective-permute-start.5) | collective-permute-done | bytes 262176 | tf_op jit(solution)/shard_map/ppermute | solution.py:113
  43.0 3.9 %collective-permute-start.37 = (f32[128]{0:T(128)S(1)}, f32[128]{0:T(128)S(1)}, u32[]{:S(2)}, u32[]{:S(2)}) collective-permute-start(f32[128]{0:T(128)S(1)} %multiply_reduce_fusion), channel_id=1, source_target_pairs={{0,1},{1,0},{2,3},{3,2},{4,5},{5,4},{6,7},{7,6},{8,9},{9,8},{10,11... | collective-permute-start | bytes 1544 | tf_op jit(solution)/shard_map/ppermute | solution.py:148
  46.9 4.1 %collective-permute-done.37 = f32[128]{0:T(128)S(1)} collective-permute-done((f32[128]{0:T(128)S(1)}, f32[128]{0:T(128)S(1)}, u32[]{:S(2)}, u32[]{:S(2)}) %collective-permute-start.37) | collective-permute-done | bytes 544 | tf_op jit(solution)/shard_map/ppermute | solution.py:148
  51.0 4.4 %collective-permute-done.38 = f32[128]{0:T(128)S(1)} collective-permute-done((f32[128]{0:T(128)S(1)}, f32[128]{0:T(128)S(1)}, u32[]{:S(2)}, u32[]{:S(2)}) %collective-permute-start.38) | collective-permute-done | bytes 544 | tf_op jit(solution)/shard_map/ppermute | solution.py:148
  56.2 4.1 %collective-permute-start.40 = (f32[64]{0:T(128)S(1)}, f32[64]{0:T(128)S(1)}, u32[]{:S(2)}, u32[]{:S(2)}) collective-permute-start(f32[64]{0:T(128)S(1)} %get-tuple-element.64), channel_id=1, source_target_pairs={{0,4},{4,12},{8,20},{12,28},{16,0},{20,8},{24,16},{28,24},{1,5},{5... | collective-permute-start | bytes 776 | tf_op jit(solution)/shard_map/ppermute | solution.py:152
  60.3 1.9 %collective-permute-start.20 = (bf16[2,2,32,1024]{3,2,1,0:T(8,128)(2,1)S(1)}, bf16[2,2,32,1024]{3,2,1,0:T(8,128)(2,1)S(1)}, u32[]{:S(2)}, u32[]{:S(2)}) collective-permute-start(bf16[2,2,32,1024]{3,2,1,0:T(8,128)(2,1)S(1)} %broadcast_select_fusion), channel_id=1, source_target_pairs={{0,1},{1,2},{2,3},{4,5},{5,6},{6,7},{8,9},{9,10},{10,11},{12,13},{... | collective-permute-start | bytes 786440 | tf_op jit(solution)/shard_map/ppermute | solution.py:110
  65.6 2.1 %collective-permute-done.20 = bf16[2,2,32,1024]{3,2,1,0:T(8,128)(2,1)S(1)} collective-permute-done((bf16[2,2,32,1024]{3,2,1,0:T(8,128)(2,1)S(1)}, bf16[2,2,32,1024]{3,2,1,0:T(8,128)(2,1)S(1)}, u32[]{:S(2)}, u32[]{:S(2)}) %collective-permute-start.20) | collective-permute-done | bytes 262176 | tf_op jit(solution)/shard_map/ppermute | solution.py:110
  68.4 5.0 %collective-permute-done.23 = bf16[2,2,32,1024]{3,2,1,0:T(8,128)(2,1)S(1)} collective-permute-done((bf16[2,2,32,1024]{3,2,1,0:T(8,128)(2,1)S(1)}, bf16[2,2,32,1024]{3,2,1,0:T(8,128)(2,1)S(1)}, u32[]{:S(2)}, u32[]{:S(2)}) %collective-permute-start.23) | collective-permute-done | bytes 262176 | tf_op jit(solution)/shard_map/ppermute | solution.py:113
  74.7 4.3 %collective-permute-done.7 = bf16[2,2,32,1024]{3,2,1,0:T(8,128)(2,1)S(1)} collective-permute-done((bf16[2,2,32,1024]{3,2,1,0:T(8,128)(2,1)S(1)}, bf16[2,2,32,1024]{3,2,1,0:T(8,128)(2,1)S(1)}, u32[]{:S(2)}, u32[]{:S(2)}) %collective-permute-start.7) | collective-permute-done | bytes 262176 | tf_op jit(solution)/shard_map/ppermute | solution.py:113
  80.1 3.0 %collective-permute-done.24 = bf16[2,2,32,1024]{3,2,1,0:T(8,128)(2,1)S(1)} collective-permute-done((bf16[2,2,32,1024]{3,2,1,0:T(8,128)(2,1)S(1)}, bf16[2,2,32,1024]{3,2,1,0:T(8,128)(2,1)S(1)}, u32[]{:S(2)}, u32[]{:S(2)}) %collective-permute-start.24) | collective-permute-done | bytes 262176 | tf_op jit(solution)/shard_map/ppermute | solution.py:113
  84.4 3.4 %copy-done = bf16[1024,4096]{1,0:T(8,128)(2,1)S(1)} copy-done((bf16[1024,4096]{1,0:T(8,128)(2,1)S(1)}, bf16[1024,4096]{1,0:T(8,128)(2,1)}, u32[]{:S(2)}) %copy-start) | copy-done | bytes 8388632
  87.8 5.1 %shard_map.50 = f32[256,2048]{1,0:T(8,128)S(1)} custom-call(s32[1]{0:T(128)} %bitcast.core_ref, bf16[2,256,1024]{2,1,0:T(8,128)(2,1)S(1)} %bitcast.209, bf16[1024,4096]{1,0:T(8,128)(2,1)S(1)} %copy-done, bf16[1024,2048]{1,0:T(8,128)(2,1)} %collective-permute-done.8.take_ref), custom_call_target="tpu_custom_call" | custom-call | flops 2147483648 | bytes 11534336 | tf_op jit(solution)/shard_map/pallas_call | solution.py:40
  95.2 5.1 %shard_map.51 = f32[256,2048]{1,0:T(8,128)S(1)} custom-call(s32[1]{0:T(128)} %bitcast.core_ref, bf16[2,256,1024]{2,1,0:T(8,128)(2,1)S(1)} %bitcast.211, bf16[1024,4096]{1,0:T(8,128)(2,1)S(1)} %copy-done, bf16[1024,2048]{1,0:T(8,128)(2,1)} %collective-permute-done.8.take_ref), custom_call_target="tpu_custom_call" | custom-call | flops 2147483648 | bytes 11534336 | tf_op jit(solution)/shard_map/pallas_call | solution.py:40
  104.8 2.5 %collective-permute-done.14 = f16[2,2,32,1024]{3,2,0,1:T(8,128)(2,1)S(1)} collective-permute-done((f16[2,2,32,1024]{3,2,0,1:T(8,128)(2,1)S(1)}, f16[2,2,32,1024]{3,2,0,1:T(8,128)(2,1)S(1)}, u32[]{:S(2)}, u32[]{:S(2)}) %collective-permute-start.14) | collective-permute-done | bytes 262176 | tf_op jit(solution)/shard_map/ppermute | solution.py:167
  107.3 2.4 %collective-permute-start.12 = (f16[2,32,1024]{2,1,0:T(8,128)(2,1)S(1)}, f16[2,32,1024]{2,1,0:T(8,128)(2,1)S(1)}, u32[]{:S(2)}, u32[]{:S(2)}) collective-permute-start(f16[2,32,1024]{2,1,0:T(8,128)(2,1)S(1)} %fusion.26), channel_id=1, source_target_pairs={{0,4},{4,0},{8,12},{12,8},{1,5},{5,1},{9,13},{13,9},{2,6},{6,2},{1... | collective-permute-start | bytes 393224 | tf_op jit(solution)/shard_map/ppermute | solution.py:172
  113.9 1.8 %collective-permute-done.15 = f16[2,32,1024]{2,1,0:T(8,128)(2,1)S(1)} collective-permute-done((f16[2,32,1024]{2,1,0:T(8,128)(2,1)S(1)}, f16[2,32,1024]{2,1,0:T(8,128)(2,1)S(1)}, u32[]{:S(2)}, u32[]{:S(2)}) %collective-permute-start.15) | collective-permute-done | bytes 131104 | tf_op jit(solution)/shard_map/ppermute | solution.py:171
  119.3 5.1 %shard_map.52 = f32[256,2048]{1,0:T(8,128)S(1)} custom-call(s32[1]{0:T(128)} %bitcast.core_ref, bf16[2,256,1024]{2,1,0:T(8,128)(2,1)S(1)} %bitcast.207, bf16[1024,4096]{1,0:T(8,128)(2,1)S(1)} %copy-done, bf16[1024,2048]{1,0:T(8,128)(2,1)} %collective-permute-done.8.take_ref), custom_call_target="tpu_custom_call" | custom-call | flops 2147483648 | bytes 11534336 | tf_op jit(solution)/shard_map/pallas_call | solution.py:40
  127.9 5.5 %collective-permute-done.27 = f16[2,2,32,1024]{3,2,0,1:T(8,128)(2,1)S(1)} collective-permute-done((f16[2,2,32,1024]{3,2,0,1:T(8,128)(2,1)S(1)}, f16[2,2,32,1024]{3,2,0,1:T(8,128)(2,1)S(1)}, u32[]{:S(2)}, u32[]{:S(2)}) %collective-permute-start.27) | collective-permute-done | bytes 262176 | tf_op jit(solution)/shard_map/ppermute | solution.py:167
  136.6 2.0 %collective-permute-done.28 = f16[2,32,1024]{2,1,0:T(8,128)(2,1)S(1)} collective-permute-done((f16[2,32,1024]{2,1,0:T(8,128)(2,1)S(1)}, f16[2,32,1024]{2,1,0:T(8,128)(2,1)S(1)}, u32[]{:S(2)}, u32[]{:S(2)}) %collective-permute-start.28) | collective-permute-done | bytes 131104 | tf_op jit(solution)/shard_map/ppermute | solution.py:171
  138.6 5.1 %shard_map.53 = f32[256,2048]{1,0:T(8,128)S(1)} custom-call(s32[1]{0:T(128)} %bitcast.core_ref, bf16[2,256,1024]{2,1,0:T(8,128)(2,1)S(1)} %bitcast.210, bf16[1024,4096]{1,0:T(8,128)(2,1)S(1)} %copy-done, bf16[1024,2048]{1,0:T(8,128)(2,1)} %collective-permute-done.8.take_ref), custom_call_target="tpu_custom_call" | custom-call | flops 2147483648 | bytes 11534336 | tf_op jit(solution)/shard_map/pallas_call | solution.py:40
  147.0 3.6 %collective-permute-done.32 = f16[2,2,32,1024]{3,2,0,1:T(8,128)(2,1)S(1)} collective-permute-done((f16[2,2,32,1024]{3,2,0,1:T(8,128)(2,1)S(1)}, f16[2,2,32,1024]{3,2,0,1:T(8,128)(2,1)S(1)}, u32[]{:S(2)}, u32[]{:S(2)}) %collective-permute-start.32) | collective-permute-done | bytes 262176 | tf_op jit(solution)/shard_map/ppermute | solution.py:167
  153.8 2.0 %collective-permute-done.33 = f16[2,32,1024]{2,1,0:T(8,128)(2,1)S(1)} collective-permute-done((f16[2,32,1024]{2,1,0:T(8,128)(2,1)S(1)}, f16[2,32,1024]{2,1,0:T(8,128)(2,1)S(1)}, u32[]{:S(2)}, u32[]{:S(2)}) %collective-permute-start.33) | collective-permute-done | bytes 131104 | tf_op jit(solution)/shard_map/ppermute | solution.py:171
  155.8 2.7 %collective-permute-done.35 = f16[2,32,1024]{2,1,0:T(8,128)(2,1)S(1)} collective-permute-done((f16[2,32,1024]{2,1,0:T(8,128)(2,1)S(1)}, f16[2,32,1024]{2,1,0:T(8,128)(2,1)S(1)}, u32[]{:S(2)}, u32[]{:S(2)}) %collective-permute-start.35) | collective-permute-done | bytes 131104 | tf_op jit(solution)/shard_map/ppermute | solution.py:172
  162.0 2.4 %collective-permute-start.41 = (f32[4,64]{1,0:T(4,128)S(1)}, f32[4,64]{1,0:T(4,128)S(1)}, u32[]{:S(2)}, u32[]{:S(2)}) collective-permute-start(f32[4,64]{1,0:T(4,128)S(1)} %get-tuple-element.56), channel_id=1, source_target_pairs={{0,1},{1,2},{2,3},{3,0},{4,5},{5,6},{6,7},{7,4},{8,9},{9,10},{10,1... | collective-permute-start | bytes 3080 | tf_op jit(solution)/shard_map/ppermute | solution.py:212
  164.4 2.4 %collective-permute-start.43 = (f32[4,64]{1,0:T(4,128)S(1)}, f32[4,64]{1,0:T(4,128)S(1)}, u32[]{:S(2)}, u32[]{:S(2)}) collective-permute-start(f32[4,64]{1,0:T(4,128)S(1)} %get-tuple-element.56), channel_id=1, source_target_pairs={{0,3},{1,0},{2,1},{3,2},{4,7},{5,4},{6,5},{7,6},{8,11},{9,8},{10,9... | collective-permute-start | bytes 3080 | tf_op jit(solution)/shard_map/ppermute | solution.py:212
  (147 shorter events, 49.9 us)
Async XLA Ops:
  2.6 6.5 %collective-permute-start = (bf16[2,32,1024]{2,1,0:T(8,128)(2,1)S(1)}, bf16[2,32,1024]{2,1,0:T(8,128)(2,1)S(1)}, u32[]{:S(2)}, u32[]{:S(2)}) collective-permute-start(bf16[2,32,1024]{2,1,0:T(8,128)(2,1)S(1)} %constant_dynamic-slice_fusion.16), channel_id=1, source_target_pairs={{0,4},{4,0},{8,12},{12,8},{1,5},{5,1},{9,13},{13,9},{2,6},{6,2},{1... | collective-permute-start | bytes 393224 | tf_op jit(solution)/shard_map/ppermute | solution.py:93
  13.9 70.5 %collective-permute-start.8 = (bf16[1024,2048]{1,0:T(8,128)(2,1)}, bf16[1024,2048]{1,0:T(8,128)(2,1)}, u32[]{:S(2)}, u32[]{:S(2)}) collective-permute-start(bf16[1024,2048]{1,0:T(8,128)(2,1)} %constant_dynamic-slice_fusion.15), channel_id=1, source_target_pairs={{0,16},{16,0},{1,17},{17,1},{2,18},{18,2},{3,19},{19,3},{4,20},{20... | collective-permute-start | bytes 12582920 | tf_op jit(solution)/shard_map/ppermute | solution.py:142
  13.9 6.0 %collective-permute-start.18 = (bf16[2,32,1024]{2,1,0:T(8,128)(2,1)S(1)}, bf16[2,32,1024]{2,1,0:T(8,128)(2,1)S(1)}, u32[]{:S(2)}, u32[]{:S(2)}) collective-permute-start(bf16[2,32,1024]{2,1,0:T(8,128)(2,1)S(1)} %constant_dynamic-slice_fusion.8), channel_id=1, source_target_pairs={{0,4},{4,0},{8,12},{12,8},{1,5},{5,1},{9,13},{13,9},{2,6},{6,2},{1... | collective-permute-start | bytes 393224 | tf_op jit(solution)/shard_map/ppermute | solution.py:93
  20.0 15.5 %collective-permute-start.2 = (bf16[2,2,32,1024]{3,2,1,0:T(8,128)(2,1)S(1)}, bf16[2,2,32,1024]{3,2,1,0:T(8,128)(2,1)S(1)}, u32[]{:S(2)}, u32[]{:S(2)}) collective-permute-start(bf16[2,2,32,1024]{3,2,1,0:T(8,128)(2,1)S(1)} %broadcast_select_fusion.1), channel_id=1, source_target_pairs={{0,1},{1,2},{2,3},{4,5},{5,6},{6,7},{8,9},{9,10},{10,11},{12,13},{... | collective-permute-start | bytes 786440 | tf_op jit(solution)/shard_map/ppermute | solution.py:110
  30.5 11.1 %collective-permute-start.5 = (bf16[2,2,32,1024]{3,2,1,0:T(8,128)(2,1)S(1)}, bf16[2,2,32,1024]{3,2,1,0:T(8,128)(2,1)S(1)}, u32[]{:S(2)}, u32[]{:S(2)}) collective-permute-start(bf16[2,2,32,1024]{3,2,1,0:T(8,128)(2,1)S(1)} %broadcast_select_fusion.1), channel_id=1, source_target_pairs={{1,0},{2,1},{3,2},{5,4},{6,5},{7,6},{9,8},{10,9},{11,10},{13,12},{... | collective-permute-start | bytes 786440 | tf_op jit(solution)/shard_map/ppermute | solution.py:113
  31.8 11.1 %collective-permute-start.19 = (bf16[2,2,32,1024]{3,2,1,0:T(8,128)(2,1)S(1)}, bf16[2,2,32,1024]{3,2,1,0:T(8,128)(2,1)S(1)}, u32[]{:S(2)}, u32[]{:S(2)}) collective-permute-start(bf16[2,2,32,1024]{3,2,1,0:T(8,128)(2,1)S(1)} %pad_maximum_fusion.5), channel_id=1, source_target_pairs={{1,8},{8,1},{3,10},{10,3},{5,12},{12,5},{7,14},{14,7},{17,24},{24,... | collective-permute-start | bytes 786440 | tf_op jit(solution)/shard_map/ppermute | solution.py:102
  35.6 28.0 %collective-permute-start.3 = (bf16[2,2,32,1024]{3,2,1,0:T(8,128)(2,1)S(1)}, bf16[2,2,32,1024]{3,2,1,0:T(8,128)(2,1)S(1)}, u32[]{:S(2)}, u32[]{:S(2)}) collective-permute-start(bf16[2,2,32,1024]{3,2,1,0:T(8,128)(2,1)S(1)} %collective-permute-done.2), channel_id=1, source_target_pairs={{1,2},{2,3},{5,6},{6,7},{9,10},{10,11},{13,14},{14,15},{17,18},{18... | collective-permute-start | bytes 786440 | tf_op jit(solution)/shard_map/ppermute | solution.py:110
  41.6 22.6 %collective-permute-start.6 = (bf16[2,2,32,1024]{3,2,1,0:T(8,128)(2,1)S(1)}, bf16[2,2,32,1024]{3,2,1,0:T(8,128)(2,1)S(1)}, u32[]{:S(2)}, u32[]{:S(2)}) collective-permute-start(bf16[2,2,32,1024]{3,2,1,0:T(8,128)(2,1)S(1)} %collective-permute-done.5), channel_id=1, source_target_pairs={{1,0},{2,1},{5,4},{6,5},{9,8},{10,9},{13,12},{14,13},{17,16},{18,1... | collective-permute-start | bytes 786440 | tf_op jit(solution)/shard_map/ppermute | solution.py:113
  43.0 8.1 %collective-permute-start.37 = (f32[128]{0:T(128)S(1)}, f32[128]{0:T(128)S(1)}, u32[]{:S(2)}, u32[]{:S(2)}) collective-permute-start(f32[128]{0:T(128)S(1)} %multiply_reduce_fusion), channel_id=1, source_target_pairs={{0,1},{1,0},{2,3},{3,2},{4,5},{5,4},{6,7},{7,6},{8,9},{9,8},{10,11... | collective-permute-start | bytes 1544 | tf_op jit(solution)/shard_map/ppermute | solution.py:148
  56.2 6.0 %collective-permute-start.40 = (f32[64]{0:T(128)S(1)}, f32[64]{0:T(128)S(1)}, u32[]{:S(2)}, u32[]{:S(2)}) collective-permute-start(f32[64]{0:T(128)S(1)} %get-tuple-element.64), channel_id=1, source_target_pairs={{0,4},{4,12},{8,20},{12,28},{16,0},{20,8},{24,16},{28,24},{1,5},{5... | collective-permute-start | bytes 776 | tf_op jit(solution)/shard_map/ppermute | solution.py:152
  60.3 7.4 %collective-permute-start.20 = (bf16[2,2,32,1024]{3,2,1,0:T(8,128)(2,1)S(1)}, bf16[2,2,32,1024]{3,2,1,0:T(8,128)(2,1)S(1)}, u32[]{:S(2)}, u32[]{:S(2)}) collective-permute-start(bf16[2,2,32,1024]{3,2,1,0:T(8,128)(2,1)S(1)} %broadcast_select_fusion), channel_id=1, source_target_pairs={{0,1},{1,2},{2,3},{4,5},{5,6},{6,7},{8,9},{9,10},{10,11},{12,13},{... | collective-permute-start | bytes 786440 | tf_op jit(solution)/shard_map/ppermute | solution.py:110
  62.2 11.1 %collective-permute-start.23 = (bf16[2,2,32,1024]{3,2,1,0:T(8,128)(2,1)S(1)}, bf16[2,2,32,1024]{3,2,1,0:T(8,128)(2,1)S(1)}, u32[]{:S(2)}, u32[]{:S(2)}) collective-permute-start(bf16[2,2,32,1024]{3,2,1,0:T(8,128)(2,1)S(1)} %broadcast_select_fusion), channel_id=1, source_target_pairs={{1,0},{2,1},{3,2},{5,4},{6,5},{7,6},{9,8},{10,9},{11,10},{13,12},{... | collective-permute-start | bytes 786440 | tf_op jit(solution)/shard_map/ppermute | solution.py:113
  63.6 11.1 %collective-permute-start.4 = (bf16[2,2,32,1024]{3,2,1,0:T(8,128)(2,1)S(1)}, bf16[2,2,32,1024]{3,2,1,0:T(8,128)(2,1)S(1)}, u32[]{:S(2)}, u32[]{:S(2)}) collective-permute-start(bf16[2,2,32,1024]{3,2,1,0:T(8,128)(2,1)S(1)} %collective-permute-done.3), channel_id=1, source_target_pairs={{2,3},{6,7},{10,11},{14,15},{18,19},{22,23},{26,27},{30,31}} | collective-permute-start | bytes 786440 | tf_op jit(solution)/shard_map/ppermute | solution.py:110
  64.2 14.7 %collective-permute-start.7 = (bf16[2,2,32,1024]{3,2,1,0:T(8,128)(2,1)S(1)}, bf16[2,2,32,1024]{3,2,1,0:T(8,128)(2,1)S(1)}, u32[]{:S(2)}, u32[]{:S(2)}) collective-permute-start(bf16[2,2,32,1024]{3,2,1,0:T(8,128)(2,1)S(1)} %collective-permute-done.6), channel_id=1, source_target_pairs={{1,0},{5,4},{9,8},{13,12},{17,16},{21,20},{25,24},{29,28}} | collective-permute-start | bytes 786440 | tf_op jit(solution)/shard_map/ppermute | solution.py:113
  67.7 11.7 %collective-permute-start.21 = (bf16[2,2,32,1024]{3,2,1,0:T(8,128)(2,1)S(1)}, bf16[2,2,32,1024]{3,2,1,0:T(8,128)(2,1)S(1)}, u32[]{:S(2)}, u32[]{:S(2)}) collective-permute-start(bf16[2,2,32,1024]{3,2,1,0:T(8,128)(2,1)S(1)} %collective-permute-done.20), channel_id=1, source_target_pairs={{1,2},{2,3},{5,6},{6,7},{9,10},{10,11},{13,14},{14,15},{17,18},{18... | collective-permute-start | bytes 786440 | tf_op jit(solution)/shard_map/ppermute | solution.py:110
  73.4 9.7 %collective-permute-start.24 = (bf16[2,2,32,1024]{3,2,1,0:T(8,128)(2,1)S(1)}, bf16[2,2,32,1024]{3,2,1,0:T(8,128)(2,1)S(1)}, u32[]{:S(2)}, u32[]{:S(2)}) collective-permute-start(bf16[2,2,32,1024]{3,2,1,0:T(8,128)(2,1)S(1)} %collective-permute-done.23), channel_id=1, source_target_pairs={{1,0},{2,1},{5,4},{6,5},{9,8},{10,9},{13,12},{14,13},{17,16},{18,1... | collective-permute-start | bytes 786440 | tf_op jit(solution)/shard_map/ppermute | solution.py:113
  79.3 15.8 %collective-permute-start.13 = (bf16[2,2,2,2,32,1024]{5,4,3,2,1,0:T(8,128)(2,1)S(1)}, bf16[2,2,2,2,32,1024]{5,4,3,2,1,0:T(8,128)(2,1)S(1)}, u32[]{:S(2)}, u32[]{:S(2)}) collective-permute-start(bf16[2,2,2,2,32,1024]{5,4,3,2,1,0:T(8,128)(2,1)S(1)} %bitcast.208), channel_id=1, source_target_pairs={{0,16},{16,0},{1,17},{17,1},{2,18},{18,2},{3,19},{19,3},{4,20},{20... | collective-permute-start | bytes 3145736 | tf_op jit(solution)/shard_map/ppermute | solution.py:183
  79.4 38.2 %collective-permute-start.22 = (bf16[2,2,32,1024]{3,2,1,0:T(8,128)(2,1)S(1)}, bf16[2,2,32,1024]{3,2,1,0:T(8,128)(2,1)S(1)}, u32[]{:S(2)}, u32[]{:S(2)}) collective-permute-start(bf16[2,2,32,1024]{3,2,1,0:T(8,128)(2,1)S(1)} %collective-permute-done.21), channel_id=1, source_target_pairs={{2,3},{6,7},{10,11},{14,15},{18,19},{22,23},{26,27},{30,31}} | collective-permute-start | bytes 786440 | tf_op jit(solution)/shard_map/ppermute | solution.py:110
  83.1 34.5 %collective-permute-start.25 = (bf16[2,2,32,1024]{3,2,1,0:T(8,128)(2,1)S(1)}, bf16[2,2,32,1024]{3,2,1,0:T(8,128)(2,1)S(1)}, u32[]{:S(2)}, u32[]{:S(2)}) collective-permute-start(bf16[2,2,32,1024]{3,2,1,0:T(8,128)(2,1)S(1)} %collective-permute-done.24), channel_id=1, source_target_pairs={{1,0},{5,4},{9,8},{13,12},{17,16},{21,20},{25,24},{29,28}} | collective-permute-start | bytes 786440 | tf_op jit(solution)/shard_map/ppermute | solution.py:113
  93.3 9.1 %collective-permute-start.9 = (f16[2,2,32,1024]{3,2,0,1:T(8,128)(2,1)S(1)}, f16[2,2,32,1024]{3,2,0,1:T(8,128)(2,1)S(1)}, u32[]{:S(2)}, u32[]{:S(2)}) collective-permute-start(f16[2,2,32,1024]{3,2,0,1:T(8,128)(2,1)S(1)} %fusion.10), channel_id=1, source_target_pairs={{0,4},{4,0},{8,12},{12,8},{1,5},{5,1},{9,13},{13,9},{2,6},{6,2},{1... | collective-permute-start | bytes 786440 | tf_op jit(solution)/shard_map/ppermute | solution.py:167
  95.1 8.3 %collective-permute-start.11 = (f16[2,2,32,1024]{3,2,0,1:T(8,128)(2,1)S(1)}, f16[2,2,32,1024]{3,2,0,1:T(8,128)(2,1)S(1)}, u32[]{:S(2)}, u32[]{:S(2)}) collective-permute-start(f16[2,2,32,1024]{3,2,0,1:T(8,128)(2,1)S(1)} %fusion.11), channel_id=1, source_target_pairs={{0,8},{8,0},{4,12},{12,4},{1,9},{9,1},{5,13},{13,5},{2,10},{10,2},... | collective-permute-start | bytes 786440 | tf_op jit(solution)/shard_map/ppermute | solution.py:168
  100.7 6.6 %collective-permute-start.14 = (f16[2,2,32,1024]{3,2,0,1:T(8,128)(2,1)S(1)}, f16[2,2,32,1024]{3,2,0,1:T(8,128)(2,1)S(1)}, u32[]{:S(2)}, u32[]{:S(2)}) collective-permute-start(f16[2,2,32,1024]{3,2,0,1:T(8,128)(2,1)S(1)} %fusion.12), channel_id=1, source_target_pairs={{0,4},{4,0},{8,12},{12,8},{1,5},{5,1},{9,13},{13,9},{2,6},{6,2},{1... | collective-permute-start | bytes 786440 | tf_op jit(solution)/shard_map/ppermute | solution.py:167
  102.4 8.4 %collective-permute-start.16 = (f16[2,2,32,1024]{3,2,1,0:T(8,128)(2,1)S(1)}, f16[2,2,32,1024]{3,2,1,0:T(8,128)(2,1)S(1)}, u32[]{:S(2)}, u32[]{:S(2)}) collective-permute-start(f16[2,2,32,1024]{3,2,1,0:T(8,128)(2,1)S(1)} %fusion.8), channel_id=1, source_target_pairs={{0,8},{8,0},{4,12},{12,4},{1,9},{9,1},{5,13},{13,5},{2,10},{10,2},... | collective-permute-start | bytes 786440 | tf_op jit(solution)/shard_map/ppermute | solution.py:168
  103.4 8.8 %collective-permute-start.10 = (f16[2,32,1024]{2,1,0:T(8,128)(2,1)S(1)}, f16[2,32,1024]{2,1,0:T(8,128)(2,1)S(1)}, u32[]{:S(2)}, u32[]{:S(2)}) collective-permute-start(f16[2,32,1024]{2,1,0:T(8,128)(2,1)S(1)} %fusion.25), channel_id=1, source_target_pairs={{0,8},{8,0},{4,12},{12,4},{1,9},{9,1},{5,13},{13,5},{2,10},{10,2},... | collective-permute-start | bytes 393224 | tf_op jit(solution)/shard_map/ppermute | solution.py:171
  107.3 6.6 %collective-permute-start.12 = (f16[2,32,1024]{2,1,0:T(8,128)(2,1)S(1)}, f16[2,32,1024]{2,1,0:T(8,128)(2,1)S(1)}, u32[]{:S(2)}, u32[]{:S(2)}) collective-permute-start(f16[2,32,1024]{2,1,0:T(8,128)(2,1)S(1)} %fusion.26), channel_id=1, source_target_pairs={{0,4},{4,0},{8,12},{12,8},{1,5},{5,1},{9,13},{13,9},{2,6},{6,2},{1... | collective-permute-start | bytes 393224 | tf_op jit(solution)/shard_map/ppermute | solution.py:172
  119.1 19.5 %collective-permute-start.31 = (bf16[2,2,2,2,32,1024]{5,4,3,2,1,0:T(8,128)(2,1)S(1)}, bf16[2,2,2,2,32,1024]{5,4,3,2,1,0:T(8,128)(2,1)S(1)}, u32[]{:S(2)}, u32[]{:S(2)}) collective-permute-start(bf16[2,2,2,2,32,1024]{5,4,3,2,1,0:T(8,128)(2,1)S(1)} %bitcast.206), channel_id=1, source_target_pairs={{0,16},{16,0},{1,17},{17,1},{2,18},{18,2},{3,19},{19,3},{4,20},{20... | collective-permute-start | bytes 3145736 | tf_op jit(solution)/shard_map/ppermute | solution.py:183
  124.8 8.7 %collective-permute-start.27 = (f16[2,2,32,1024]{3,2,0,1:T(8,128)(2,1)S(1)}, f16[2,2,32,1024]{3,2,0,1:T(8,128)(2,1)S(1)}, u32[]{:S(2)}, u32[]{:S(2)}) collective-permute-start(f16[2,2,32,1024]{3,2,0,1:T(8,128)(2,1)S(1)} %fusion.13), channel_id=1, source_target_pairs={{0,4},{4,0},{8,12},{12,8},{1,5},{5,1},{9,13},{13,9},{2,6},{6,2},{1... | collective-permute-start | bytes 786440 | tf_op jit(solution)/shard_map/ppermute | solution.py:167
  126.6 8.4 %collective-permute-start.29 = (f16[2,2,32,1024]{3,2,0,1:T(8,128)(2,1)S(1)}, f16[2,2,32,1024]{3,2,0,1:T(8,128)(2,1)S(1)}, u32[]{:S(2)}, u32[]{:S(2)}) collective-permute-start(f16[2,2,32,1024]{3,2,0,1:T(8,128)(2,1)S(1)} %fusion.14), channel_id=1, source_target_pairs={{0,8},{8,0},{4,12},{12,4},{1,9},{9,1},{5,13},{13,5},{2,10},{10,2},... | collective-permute-start | bytes 786440 | tf_op jit(solution)/shard_map/ppermute | solution.py:168
  135.0 10.6 %collective-permute-start.30 = (f16[2,32,1024]{2,1,0:T(8,128)(2,1)S(1)}, f16[2,32,1024]{2,1,0:T(8,128)(2,1)S(1)}, u32[]{:S(2)}, u32[]{:S(2)}) collective-permute-start(f16[2,32,1024]{2,1,0:T(8,128)(2,1)S(1)} %fusion.30), channel_id=1, source_target_pairs={{0,4},{4,0},{8,12},{12,8},{1,5},{5,1},{9,13},{13,9},{2,6},{6,2},{1... | collective-permute-start | bytes 393224 | tf_op jit(solution)/shard_map/ppermute | solution.py:172
  144.0 6.7 %collective-permute-start.32 = (f16[2,2,32,1024]{3,2,0,1:T(8,128)(2,1)S(1)}, f16[2,2,32,1024]{3,2,0,1:T(8,128)(2,1)S(1)}, u32[]{:S(2)}, u32[]{:S(2)}) collective-permute-start(f16[2,2,32,1024]{3,2,0,1:T(8,128)(2,1)S(1)} %fusion.15), channel_id=1, source_target_pairs={{0,4},{4,0},{8,12},{12,8},{1,5},{5,1},{9,13},{13,9},{2,6},{6,2},{1... | collective-permute-start | bytes 786440 | tf_op jit(solution)/shard_map/ppermute | solution.py:167
  145.7 7.6 %collective-permute-start.34 = (f16[2,2,32,1024]{3,2,1,0:T(8,128)(2,1)S(1)}, f16[2,2,32,1024]{3,2,1,0:T(8,128)(2,1)S(1)}, u32[]{:S(2)}, u32[]{:S(2)}) collective-permute-start(f16[2,2,32,1024]{3,2,1,0:T(8,128)(2,1)S(1)} %fusion.9), channel_id=1, source_target_pairs={{0,8},{8,0},{4,12},{12,4},{1,9},{9,1},{5,13},{13,5},{2,10},{10,2},... | collective-permute-start | bytes 786440 | tf_op jit(solution)/shard_map/ppermute | solution.py:168
  162.0 5.4 %collective-permute-start.41 = (f32[4,64]{1,0:T(4,128)S(1)}, f32[4,64]{1,0:T(4,128)S(1)}, u32[]{:S(2)}, u32[]{:S(2)}) collective-permute-start(f32[4,64]{1,0:T(4,128)S(1)} %get-tuple-element.56), channel_id=1, source_target_pairs={{0,1},{1,2},{2,3},{3,0},{4,5},{5,6},{6,7},{7,4},{8,9},{9,10},{10,1... | collective-permute-start | bytes 3080 | tf_op jit(solution)/shard_map/ppermute | solution.py:212
  (14 other events, 72.7 us)

commit v6 on v3

v6 whole, which is shorter than its diff:
```python
import jax
import jax.numpy as jnp
from jax import lax
from jax.experimental import pallas as pl
from jax.experimental.pallas import tpu as pltpu
from jax.sharding import PartitionSpec as P

EPS = 1e-05
GUIDE = 1.5
CHUNKS = 2
SHRINK = 1.0 / 32.0
SUM_TYPE = jnp.float16
TILE = 512

X_SWAP = [(0, 1), (1, 0), (2, 3), (3, 2)]
Y_SWAP = [(0, 2), (2, 0), (1, 3), (3, 1)]
CORE_SWAP = [(0, 1), (1, 0)]


def pick(array, index, axis):
    return lax.dynamic_index_in_dim(array, index, axis, keepdims=False)


def after(value, *others):
    return lax.optimization_barrier((value, *others))[0]


def logits_kernel(place_ref, left_ref, weight_ref, take_ref, out_ref):
    side, own = place_ref[0], place_ref[1]
    width = out_ref.shape[1]
    tile = min(TILE, width)

    @pl.loop(0, width // tile)
    def _(t):
        here = pl.ds(pl.multiple_of(t * tile, tile), tile)
        there = pl.ds(pl.multiple_of(side * width + t * tile, tile), tile)
        out = jnp.dot(left_ref[own], weight_ref[:, there], preferred_element_type=jnp.float32)
        out += jnp.dot(left_ref[1 - own], take_ref[:, there], preferred_element_type=jnp.float32)
        out_ref[:, here] = out * SHRINK


def partial_logits(core, own, left, head_weight, take):
    _, rows, block = left.shape
    width = take.shape[1] // 2
    whole = pl.BlockSpec(memory_space=pltpu.VMEM)
    return pl.pallas_call(
        logits_kernel,
        in_specs=[pl.BlockSpec(memory_space=pltpu.SMEM), whole, whole, whole],
        out_specs=whole,
        out_shape=jax.ShapeDtypeStruct((rows, width), jnp.float32),
        compiler_params=pltpu.CompilerParams(vmem_limit_bytes=32 * 1024 * 1024),
        cost_estimate=pl.CostEstimate(
            flops=4 * rows * block * width,
            bytes_accessed=4 * block * width + 4 * rows * block + 4 * rows * width,
            transcendentals=0,
        ),
    )(jnp.stack([core, own]).astype(jnp.int32), left, head_weight, take)


def on_device(hidden, norm_gain, head_weight):
    core = lax.axis_index("pair")
    place = lax.axis_index("batch")
    level = lax.axis_index("vocab")
    vocab = lax.axis_size("vocab")
    y, x = place // 2, place % 2
    rows = hidden[0]
    seg = rows.shape[0] // 2
    depth = rows.shape[1]
    block, columns = head_weight.shape
    width = columns // 2
    model = depth * vocab
    step = seg // CHUNKS

    wide = rows.astype(jnp.float32)
    gained = (wide * norm_gain.astype(jnp.float32)[None, :]).astype(jnp.bfloat16)
    gained = gained.reshape(2, seg, depth)

    squares = jnp.sum(wide * wide, axis=1)
    reach = 1
    while reach < vocab:
        squares += lax.ppermute(squares, "vocab", [(i, i ^ reach) for i in range(vocab)])
        reach *= 2

    first = level // 2 if vocab == 4 else 0
    pieces = [gained[:, c * step : (c + 1) * step] for c in range(CHUNKS)]
    lined = depth == 2 * block and vocab == 4
    if lined:
        sides = [lax.dynamic_slice_in_dim(piece, (1 - x) * block, block, 2) for piece in pieces]
        sides = [lax.ppermute(side, "batch", X_SWAP) for side in sides]

    def line_features(c, held, *earlier):
        mine = lax.dynamic_slice_in_dim(pieces[c], x * block, block, 2)
        other = sides[c]
        own = jnp.stack([jnp.where(x == 0, mine, other), jnp.where(x == 0, other, mine)])
        own = after(own, squares, *held)
        below, above = [own], [own]
        for k in range(1, vocab):
            below.append(
                lax.ppermute(below[-1], "vocab", [(z, z + 1) for z in range(k - 1, vocab - 1)])
            )
            above.append(
                lax.ppermute(above[-1], "vocab", [(z + 1, z) for z in range(vocab - k)])
            )

        def quarter(place, reach):
            part = own
            for k in range(1, reach + 1):
                part = jnp.where(level - place == k, below[k], part)
                part = jnp.where(place - level == k, above[k], part)
            return part

        far = 1 - y + 2 * (1 - first)
        got_near = lax.ppermute(quarter(1 - y + 2 * first, 1), "batch", Y_SWAP)
        ends = [(0, 0), (1, vocab - 1)]
        pairs = [(b * vocab + z, (b ^ 2) * vocab + z) for b in range(4) for z in range(vocab)]
        late = [pair for pair in pairs if (pair[0] // vocab // 2, pair[0] % vocab) in ends]
        early = [pair for pair in pairs if pair not in late]
        got_early = after(lax.ppermute(quarter(far, 2), ("batch", "vocab"), early), *earlier)
        below[-1], above[-1] = after(below[-1], *earlier), after(above[-1], *earlier)
        last = jnp.where(level == 0, above[-1], below[-1])
        got_late = lax.ppermute(last, ("batch", "vocab"), late)
        is_late = (level == 0) & (y == 1) | (level == vocab - 1) & (y == 0)
        got_far = jnp.where(is_late, got_late, got_early)
        halves = []
        for mine, other in (
            (quarter(y + 2 * first, 1), got_near),
            (quarter(y + 2 * (1 - first), vocab - 1), got_far),
        ):
            halves.append(
                jnp.stack([jnp.where(y == 0, mine, other), jnp.where(y == 0, other, mine)])
            )
        return jnp.stack(halves), (below[-1], above[-1], got_near, got_early)

    def gathered_features(c, held, *earlier):
        whole = lax.all_gather(pieces[c], "vocab", axis=2, tiled=True)
        whole = whole.reshape(2, step, 2, 4, block).transpose(3, 2, 0, 1, 4)
        whole = lax.all_to_all(whole, "batch", split_axis=0, concat_axis=0)
        whole = whole.reshape(2, 2, 2, 2, step, block).transpose(2, 0, 1, 3, 4, 5)
        return after(whole, *earlier), (gained,)

    features = line_features if lined else gathered_features
    own_half = core ^ first if lined else core
    found, begun = features(0, ())

    take = lax.ppermute(head_weight, "pair", CORE_SWAP)

    squares = squares.reshape(2, seg)
    sent = [
        lax.ppermute(
            pick(squares, core ^ k, 0),
            ("pair", "batch"),
            [(4 * s + b, 2 * b + (s ^ k)) for s in range(2) for b in range(4)],
        )
        for k in range(2)
    ]
    total_sq = jnp.stack([jnp.where(x == 0, sent[0], sent[1]), jnp.where(x == 0, sent[1], sent[0])])
    scale = lax.rsqrt(total_sq / model + EPS) / SHRINK

    def reduced(left):
        middle = width // 2
        parts = partial_logits(core, own_half, left.reshape(2, -1, block), head_weight, take)
        parts = parts.reshape(2, 2, 2, step, width)
        low, high = parts[..., :middle], parts[..., middle:]
        away_x = lax.ppermute(pick(low, 1 - x, 2).astype(SUM_TYPE), "batch", X_SWAP)
        away_y = lax.ppermute(pick(high, 1 - y, 1).astype(SUM_TYPE), "batch", Y_SWAP)
        sum_x = pick(low, x, 2) + away_x.astype(jnp.float32)
        sum_y = pick(high, y, 1) + away_y.astype(jnp.float32)
        next_y = lax.ppermute(pick(sum_x, 1 - y, 1).astype(SUM_TYPE), "batch", Y_SWAP)
        next_x = lax.ppermute(pick(sum_y, 1 - x, 1).astype(SUM_TYPE), "batch", X_SWAP)
        sums = jnp.concatenate(
            [
                pick(sum_x, y, 1) + next_y.astype(jnp.float32),
                pick(sum_y, x, 1) + next_x.astype(jnp.float32),
            ],
            axis=-1,
        ).astype(SUM_TYPE)
        return sums, parts, sum_y

    done = []
    for c in range(CHUNKS):
        other = lax.ppermute(found, "pair", CORE_SWAP)
        own_sums, parts, _ = reduced(found)
        other_sums, _, halfway = reduced(other)
        if c + 1 < CHUNKS:
            found = after(features(c + 1, begun, parts)[0], halfway)
        sums = jnp.stack([own_sums, other_sums])
        theirs = lax.ppermute(pick(sums, 1 - core, 1), "pair", CORE_SWAP)
        done.append((pick(sums, core, 1), theirs))

    mine = jnp.concatenate([part[0] for part in done], axis=1)
    theirs = jnp.concatenate([part[1] for part in done], axis=1)

    def scores(own, other, got_own, got_other, gain):
        low = jnp.where(core == 0, own, got_own)
        high = jnp.where(core == 0, got_other, other)
        return jnp.concatenate([low, high], axis=1).astype(jnp.float32) * gain[:, None]

    cond = scores(mine[0], mine[1], theirs[0], theirs[1], scale[0])
    uncond = scores(mine[1], mine[0], theirs[1], theirs[0], scale[1])
    guided = GUIDE * cond + (1.0 - GUIDE) * uncond

    def stats(values):
        peak = jnp.max(values, axis=1)
        return peak, jnp.sum(jnp.exp(values - peak[:, None]), axis=1)

    peak_c, sum_c = stats(cond)
    peak_g, sum_g = stats(guided)
    own = jnp.stack([peak_c, peak_g, sum_c, sum_g])
    every = jnp.stack(
        [own]
        + [
            lax.ppermute(own, "vocab", [(i, (i + k) % vocab) for i in range(vocab)])
            for k in range(1, vocab)
        ]
    )
    top = jnp.max(every[:, :2], axis=0)
    total = jnp.sum(every[:, 2:] * jnp.exp(every[:, :2] - top[None]), axis=0)
    norm = top + jnp.log(total)
    return (guided - norm[1][:, None], cond - norm[0][:, None])


def solution(mesh):
    in_specs = (P("pair", "batch", "vocab"), P("vocab"), P(("pair", "batch"), "vocab"))
    out_specs = (P(("pair", "batch"), "vocab"), P(("pair", "batch"), "vocab"))
    return jax.shard_map(
        on_device, mesh=mesh, in_specs=in_specs, out_specs=out_specs, check_vma=False
    )
```

time: 187 us -> 166 us (0.89)
  matrix products: 51.9 us -> 0 us
  Pallas kernels: 0 us -> 25.1 us
  starting transfers between devices: 50.3 us -> 66.3 us
  waiting for transfers between devices: 48.6 us -> 62.4 us
  between operations: 15 us -> 1.6 us
  local copies, waits for them, and re-layouts: 11.1 us -> 1.76 us
    dot_general x32 -> x0, matrix products: 51.9 us -> none  [the longest x16 33 us: partial(): jnp.dot(pick(left, 1 - core, 0).reshape(-1, block), take[:, low:high], pr...]
    ppermute x17 -> x33, starting transfers between devices: 13.6 us -> 48.2 us  [the longest x6 11.6 us: line_features(): lax.ppermute(below[-1], 'vocab', [(z, z + 1) for z in range(k - 1, vocab...]
    ppermute x17 -> x33, waiting for transfers between devices: 17.9 us -> 46.6 us  [the longest x6 24.3 us: line_features(): lax.ppermute(above[-1], 'vocab', [(z + 1, z) for z in range(vocab - k)])]
    pallas_call x0 -> x4, Pallas kernels: none -> 25.1 us  [partial_logits(): pl.pallas_call(logits_kernel, in_specs=[pl.BlockSpec(memory_space=pltpu.S...]
    ppermute x2, starting transfers between devices: 17.1 us -> 4.22 us  [on_device(): lax.ppermute(squares, 'vocab', [(i, i ^ reach) for i in range(vocab)])]
    all_gather x2 -> x0, waiting for transfers between devices: 9.49 us -> none  [line_features(): whole = lax.all_gather(held.reshape(-1, block), 'vocab', axis=0, tiled=True)]
    dynamic_slice x8 -> x6, local copies, waits for them, and re-layouts: 5.54 us -> 0.54 us  [pick(): return lax.dynamic_index_in_dim(array, index, axis, keepdims=False)]
    dynamic_slice x3 -> x2, local copies, waits for them, and re-layouts: 4.87 us -> 0.04 us  [on_device(): lax.dynamic_slice_in_dim(piece, (1 - x) * block, block, 2)]
  transfers between devices with their start and end apart: 34 -> 48, of which waited for: 20 -> 25; matrix products, arithmetic and copies ran while one was open for 30% -> 4% of each run, Pallas kernels for 0% -> 15%
where the time goes in v6:
time: 166 us
  starting transfers between devices  66.3 us (40%)
  waiting for transfers between devices  62.4 us (38%)
  Pallas kernels  25.1 us (15%)
  other arithmetic  8.41 us (5%)
  local copies, waits for them, and re-layouts  1.76 us (1%)
    pallas_call x4, Pallas kernels, partial_logits(): pl.pallas_call(logits_kernel, in_specs=[pl.BlockSpec(memory_space=pltpu.S...  25.1 us
    ppermute x6, waiting for transfers between devices, line_features(): lax.ppermute(above[-1], 'vocab', [(z + 1, z) for z in range(vocab - k)])  24.3 us
    ppermute x6, starting transfers between devices, line_features(): lax.ppermute(below[-1], 'vocab', [(z, z + 1) for z in range(k - 1, vocab...  11.6 us
    ppermute x4, waiting for transfers between devices, reduced(): lax.ppermute(pick(high, 1 - y, 1).astype(SUM_TYPE), 'batch', Y_SWAP)  11.3 us
    ppermute x2, starting transfers between devices, line_features(): got_late = lax.ppermute(last, ('batch', 'vocab'), late)  8.6 us
    ppermute x6, starting transfers between devices, line_features(): lax.ppermute(above[-1], 'vocab', [(z + 1, z) for z in range(vocab - k)])  7.72 us
    ppermute x4, starting transfers between devices, reduced(): away_x = lax.ppermute(pick(low, 1 - x, 2).astype(SUM_TYPE), 'batch', X_SWAP)  6.24 us
    ppermute x4, starting transfers between devices, reduced(): lax.ppermute(pick(high, 1 - y, 1).astype(SUM_TYPE), 'batch', Y_SWAP)  6.12 us
  transfers between devices with their start and end apart: 48, of which 25 were waited for; matrix products, arithmetic and copies ran while one was open for 4% of the time, Pallas kernels for 15%

profile of v6, /device:TPU:0, one launch (start us, length us, event | category | flops | bytes accessed | tf_op | source)
XLA Modules:
  0.0 165.5 jit_solution(5914448248468295326)
XLA Ops:
  3.1 2.6 %collective-permute-start = (bf16[2,32,1024]{2,1,0:T(8,128)(2,1)S(1)}, bf16[2,32,1024]{2,1,0:T(8,128)(2,1)S(1)}, u32[]{:S(2)}, u32[]{:S(2)}) collective-permute-start(bf16[2,32,1024]{2,1,0:T(8,128)(2,1)S(1)} %constant_dynamic-slice_fusion.15), channel_id=1, source_target_pairs={{0,4},{4,0},{8,12},{12,8},{1,5},{5,1},{9,13},{13,9},{2,6},{6,2},{1... | collective-permute-start | bytes 393224 | tf_op jit(solution)/shard_map/ppermute | solution.py:89
  5.9 1.6 collective-permute-start.1
  7.5 2.0 %collective-permute-done.1 = f32[128]{0:T(128)S(1)} collective-permute-done((f32[128]{0:T(128)S(1)}, f32[128]{0:T(128)S(1)}, u32[]{:S(2)}, u32[]{:S(2)}) %collective-permute-start.1) | collective-permute-done | bytes 544 | tf_op jit(solution)/shard_map/ppermute | solution.py:81
  9.5 2.6 %collective-permute-start.2 = (f32[128]{0:T(128)S(1)}, f32[128]{0:T(128)S(1)}, u32[]{:S(2)}, u32[]{:S(2)}) collective-permute-start(f32[128]{0:T(128)S(1)} %add.160), channel_id=1, source_target_pairs={{0,2},{1,3},{2,0},{3,1},{4,6},{5,7},{6,4},{7,5},{8,10},{9,11},{10,... | collective-permute-start | bytes 1544 | tf_op jit(solution)/shard_map/ppermute | solution.py:81
  12.1 1.9 %collective-permute-done.2 = f32[128]{0:T(128)S(1)} collective-permute-done((f32[128]{0:T(128)S(1)}, f32[128]{0:T(128)S(1)}, u32[]{:S(2)}, u32[]{:S(2)}) %collective-permute-start.2) | collective-permute-done | bytes 544 | tf_op jit(solution)/shard_map/ppermute | solution.py:81
  15.3 4.6 %collective-permute-start.4 = (bf16[2,2,32,1024]{3,2,1,0:T(8,128)(2,1)S(1)}, bf16[2,2,32,1024]{3,2,1,0:T(8,128)(2,1)S(1)}, u32[]{:S(2)}, u32[]{:S(2)}) collective-permute-start(bf16[2,2,32,1024]{3,2,1,0:T(8,128)(2,1)S(1)} %pad_maximum_fusion.7), channel_id=1, source_target_pairs={{0,1},{1,2},{2,3},{4,5},{5,6},{6,7},{8,9},{9,10},{10,11},{12,13},{... | collective-permute-start | bytes 786440 | tf_op jit(solution)/shard_map/ppermute | solution.py:99
  27.5 7.0 %collective-permute-done.6 = bf16[2,2,32,1024]{3,2,1,0:T(8,128)(2,1)S(1)} collective-permute-done((bf16[2,2,32,1024]{3,2,1,0:T(8,128)(2,1)S(1)}, bf16[2,2,32,1024]{3,2,1,0:T(8,128)(2,1)S(1)}, u32[]{:S(2)}, u32[]{:S(2)}) %collective-permute-start.6) | collective-permute-done | bytes 262176 | tf_op jit(solution)/shard_map/ppermute | solution.py:102
  38.1 7.0 %collective-permute-done.7 = bf16[2,2,32,1024]{3,2,1,0:T(8,128)(2,1)S(1)} collective-permute-done((bf16[2,2,32,1024]{3,2,1,0:T(8,128)(2,1)S(1)}, bf16[2,2,32,1024]{3,2,1,0:T(8,128)(2,1)S(1)}, u32[]{:S(2)}, u32[]{:S(2)}) %collective-permute-start.7) | collective-permute-done | bytes 262176 | tf_op jit(solution)/shard_map/ppermute | solution.py:102
  46.4 4.6 %collective-permute-start.10 = (bf16[2,2,32,1024]{3,2,1,0:T(8,128)(2,1)S(1)}, bf16[2,2,32,1024]{3,2,1,0:T(8,128)(2,1)S(1)}, u32[]{:S(2)}, u32[]{:S(2)}) collective-permute-start(bf16[2,2,32,1024]{3,2,1,0:T(8,128)(2,1)S(1)} %broadcast_select_fusion.1), channel_id=1, source_target_pairs={{0,8},{4,12},{11,3},{15,7},{16,24},{20,28},{27,19},{31,23}} | collective-permute-start | bytes 786440 | tf_op jit(solution)/shard_map/ppermute | solution.py:121
  51.1 2.2 %collective-permute-done.11 = bf16[2,2,32,1024]{3,2,1,0:T(8,128)(2,1)S(1)} collective-permute-done((bf16[2,2,32,1024]{3,2,1,0:T(8,128)(2,1)S(1)}, bf16[2,2,32,1024]{3,2,1,0:T(8,128)(2,1)S(1)}, u32[]{:S(2)}, u32[]{:S(2)}) %collective-permute-start.11) | collective-permute-done | bytes 262176 | tf_op jit(solution)/shard_map/ppermute | solution.py:118
  54.8 4.3 %collective-permute-start.24 = (bf16[2,2,32,1024]{3,2,1,0:T(8,128)(2,1)S(1)}, bf16[2,2,32,1024]{3,2,1,0:T(8,128)(2,1)S(1)}, u32[]{:S(2)}, u32[]{:S(2)}) collective-permute-start(bf16[2,2,32,1024]{3,2,1,0:T(8,128)(2,1)S(1)} %pad_maximum_fusion.8), channel_id=1, source_target_pairs={{0,1},{1,2},{2,3},{4,5},{5,6},{6,7},{8,9},{9,10},{10,11},{12,13},{... | collective-permute-start | bytes 786440 | tf_op jit(solution)/shard_map/ppermute | solution.py:99
  59.6 2.0 %collective-permute-done.23 = bf16[2,2,32,1024]{3,2,1,0:T(8,128)(2,1)S(1)} collective-permute-done((bf16[2,2,32,1024]{3,2,1,0:T(8,128)(2,1)S(1)}, bf16[2,2,32,1024]{3,2,1,0:T(8,128)(2,1)S(1)}, u32[]{:S(2)}, u32[]{:S(2)}) %collective-permute-start.23) | collective-permute-done | bytes 262176 | tf_op jit(solution)/shard_map/ppermute | solution.py:102
  65.3 7.0 %collective-permute-done.26 = bf16[2,2,32,1024]{3,2,1,0:T(8,128)(2,1)S(1)} collective-permute-done((bf16[2,2,32,1024]{3,2,1,0:T(8,128)(2,1)S(1)}, bf16[2,2,32,1024]{3,2,1,0:T(8,128)(2,1)S(1)}, u32[]{:S(2)}, u32[]{:S(2)}) %collective-permute-start.26) | collective-permute-done | bytes 262176 | tf_op jit(solution)/shard_map/ppermute | solution.py:102
  75.9 6.3 %shard_map.51 = f32[256,2048]{1,0:T(8,128)S(1)} custom-call(s32[2]{0:T(128)S(1)} %pad_add_fusion.place_ref, bf16[2,256,1024]{2,1,0:T(8,128)(2,1)S(1)} %bitcast.218, bf16[1024,4096]{1,0:T(8,128)(2,1)S(1)} %bitcast.211, bf16[1024,4096]{1,0:T(8,128)(2,1)} %collective-permute-done.12.take_ref), custom_call_target="tpu_custom_call" | custom-call | flops 2147483648 | bytes 11534336 | tf_op jit(solution)/shard_map/pallas_call | solution.py:46
  82.5 2.7 %collective-permute-start.20 = (f16[2,2,32,1024]{3,2,1,0:T(8,128)(2,1)S(1)}, f16[2,2,32,1024]{3,2,1,0:T(8,128)(2,1)S(1)}, u32[]{:S(2)}, u32[]{:S(2)}) collective-permute-start(f16[2,2,32,1024]{3,2,1,0:T(8,128)(2,1)S(1)} %fusion.8), channel_id=1, source_target_pairs={{0,8},{8,0},{4,12},{12,4},{1,9},{9,1},{5,13},{13,5},{2,10},{10,2},... | collective-permute-start | bytes 786440 | tf_op jit(solution)/shard_map/ppermute | solution.py:165
  85.4 4.0 %collective-permute-start.18 = (f16[2,2,32,1024]{3,2,0,1:T(8,128)(2,1)S(1)}, f16[2,2,32,1024]{3,2,0,1:T(8,128)(2,1)S(1)}, u32[]{:S(2)}, u32[]{:S(2)}) collective-permute-start(f16[2,2,32,1024]{3,2,0,1:T(8,128)(2,1)S(1)} %fusion.12), channel_id=1, source_target_pairs={{0,4},{4,0},{8,12},{12,8},{1,5},{5,1},{9,13},{13,9},{2,6},{6,2},{1... | collective-permute-start | bytes 786440 | tf_op jit(solution)/shard_map/ppermute | solution.py:164
  89.4 6.3 %shard_map.50 = f32[256,2048]{1,0:T(8,128)S(1)} custom-call(s32[2]{0:T(128)S(1)} %pad_add_fusion.place_ref, bf16[2,256,1024]{2,1,0:T(8,128)(2,1)S(1)} %pad_maximum_fusion.left_ref, bf16[1024,4096]{1,0:T(8,128)(2,1)S(1)} %bitcast.211, bf16[1024,4096]{1,0:T(8,128)(2,1)} %collective-permute-done.12.take_ref), custom_call_target="tpu_custom_call" | custom-call | flops 2147483648 | bytes 11534336 | tf_op jit(solution)/shard_map/pallas_call | solution.py:46
  96.4 4.0 %collective-permute-start.30 = (bf16[2,2,32,1024]{3,2,1,0:T(8,128)(2,1)S(1)}, bf16[2,2,32,1024]{3,2,1,0:T(8,128)(2,1)S(1)}, u32[]{:S(2)}, u32[]{:S(2)}) collective-permute-start(bf16[2,2,32,1024]{3,2,1,0:T(8,128)(2,1)S(1)} %broadcast_select_fusion), channel_id=1, source_target_pairs={{0,8},{4,12},{11,3},{15,7},{16,24},{20,28},{27,19},{31,23}} | collective-permute-start | bytes 786440 | tf_op jit(solution)/shard_map/ppermute | solution.py:121
  100.5 2.1 %collective-permute-start.21 = (f16[2,32,1024]{2,1,0:T(8,128)(2,1)S(1)}, f16[2,32,1024]{2,1,0:T(8,128)(2,1)S(1)}, u32[]{:S(2)}, u32[]{:S(2)}) collective-permute-start(f16[2,32,1024]{2,1,0:T(8,128)(2,1)S(1)} %fusion.28), channel_id=1, source_target_pairs={{0,4},{4,0},{8,12},{12,8},{1,5},{5,1},{9,13},{13,9},{2,6},{6,2},{1... | collective-permute-start | bytes 393224 | tf_op jit(solution)/shard_map/ppermute | solution.py:169
  106.2 2.0 %collective-permute-done.30 = bf16[2,2,32,1024]{3,2,1,0:T(8,128)(2,1)S(1)} collective-permute-done((bf16[2,2,32,1024]{3,2,1,0:T(8,128)(2,1)S(1)}, bf16[2,2,32,1024]{3,2,1,0:T(8,128)(2,1)S(1)}, u32[]{:S(2)}, u32[]{:S(2)}) %collective-permute-start.30) | collective-permute-done | bytes 262176 | tf_op jit(solution)/shard_map/ppermute | solution.py:121
  108.6 6.3 %shard_map.52 = f32[256,2048]{1,0:T(8,128)S(1)} custom-call(s32[2]{0:T(128)S(1)} %pad_add_fusion.place_ref, bf16[2,256,1024]{2,1,0:T(8,128)(2,1)S(1)} %bitcast.216, bf16[1024,4096]{1,0:T(8,128)(2,1)S(1)} %bitcast.211, bf16[1024,4096]{1,0:T(8,128)(2,1)} %collective-permute-done.12.take_ref), custom_call_target="tpu_custom_call" | custom-call | flops 2147483648 | bytes 11534336 | tf_op jit(solution)/shard_map/pallas_call | solution.py:46
  115.4 2.6 %collective-permute-start.34 = (f16[2,2,32,1024]{3,2,0,1:T(8,128)(2,1)S(1)}, f16[2,2,32,1024]{3,2,0,1:T(8,128)(2,1)S(1)}, u32[]{:S(2)}, u32[]{:S(2)}) collective-permute-start(f16[2,2,32,1024]{3,2,0,1:T(8,128)(2,1)S(1)} %fusion.14), channel_id=1, source_target_pairs={{0,8},{8,0},{4,12},{12,4},{1,9},{9,1},{5,13},{13,5},{2,10},{10,2},... | collective-permute-start | bytes 786440 | tf_op jit(solution)/shard_map/ppermute | solution.py:165
  118.9 6.0 %collective-permute-done.34 = f16[2,2,32,1024]{3,2,0,1:T(8,128)(2,1)S(1)} collective-permute-done((f16[2,2,32,1024]{3,2,0,1:T(8,128)(2,1)S(1)}, f16[2,2,32,1024]{3,2,0,1:T(8,128)(2,1)S(1)}, u32[]{:S(2)}, u32[]{:S(2)}) %collective-permute-start.34) | collective-permute-done | bytes 262176 | tf_op jit(solution)/shard_map/ppermute | solution.py:165
  127.4 3.0 %collective-permute-done.35 = f16[2,32,1024]{2,1,0:T(8,128)(2,1)S(1)} collective-permute-done((f16[2,32,1024]{2,1,0:T(8,128)(2,1)S(1)}, f16[2,32,1024]{2,1,0:T(8,128)(2,1)S(1)}, u32[]{:S(2)}, u32[]{:S(2)}) %collective-permute-start.35) | collective-permute-done | bytes 131104 | tf_op jit(solution)/shard_map/ppermute | solution.py:169
  131.7 6.3 %shard_map.53 = f32[256,2048]{1,0:T(8,128)S(1)} custom-call(s32[2]{0:T(128)S(1)} %pad_add_fusion.place_ref, bf16[2,256,1024]{2,1,0:T(8,128)(2,1)S(1)} %bitcast.217, bf16[1024,4096]{1,0:T(8,128)(2,1)S(1)} %bitcast.211, bf16[1024,4096]{1,0:T(8,128)(2,1)} %collective-permute-done.12.take_ref), custom_call_target="tpu_custom_call" | custom-call | flops 2147483648 | bytes 11534336 | tf_op jit(solution)/shard_map/pallas_call | solution.py:46
  139.0 1.7 %collective-permute-start.37 = (f16[2,2,32,1024]{3,2,0,1:T(8,128)(2,1)S(1)}, f16[2,2,32,1024]{3,2,0,1:T(8,128)(2,1)S(1)}, u32[]{:S(2)}, u32[]{:S(2)}) collective-permute-start(f16[2,2,32,1024]{3,2,0,1:T(8,128)(2,1)S(1)} %fusion.15), channel_id=1, source_target_pairs={{0,4},{4,0},{8,12},{12,8},{1,5},{5,1},{9,13},{13,9},{2,6},{6,2},{1... | collective-permute-start | bytes 786440 | tf_op jit(solution)/shard_map/ppermute | solution.py:164
  140.7 4.2 %collective-permute-done.39 = f16[2,2,32,1024]{3,2,1,0:T(8,128)(2,1)S(1)} collective-permute-done((f16[2,2,32,1024]{3,2,1,0:T(8,128)(2,1)S(1)}, f16[2,2,32,1024]{3,2,1,0:T(8,128)(2,1)S(1)}, u32[]{:S(2)}, u32[]{:S(2)}) %collective-permute-start.39) | collective-permute-done | bytes 262176 | tf_op jit(solution)/shard_map/ppermute | solution.py:165
  146.1 1.7 collective-permute-start.38
  147.8 2.3 %collective-permute-done.40 = f16[2,32,1024]{2,1,0:T(8,128)(2,1)S(1)} collective-permute-done((f16[2,32,1024]{2,1,0:T(8,128)(2,1)S(1)}, f16[2,32,1024]{2,1,0:T(8,128)(2,1)S(1)}, u32[]{:S(2)}, u32[]{:S(2)}) %collective-permute-start.40) | collective-permute-done | bytes 131104 | tf_op jit(solution)/shard_map/ppermute | solution.py:169
  154.6 3.8 %collective-permute-start.47 = (f32[4,64]{1,0:T(4,128)S(1)}, f32[4,64]{1,0:T(4,128)S(1)}, u32[]{:S(2)}, u32[]{:S(2)}) collective-permute-start(f32[4,64]{1,0:T(4,128)S(1)} %get-tuple-element.66), channel_id=1, source_target_pairs={{0,3},{1,0},{2,1},{3,2},{4,7},{5,4},{6,5},{7,6},{8,11},{9,8},{10,9... | collective-permute-start | bytes 3080 | tf_op jit(solution)/shard_map/ppermute | solution.py:212
  159.7 3.2 %collective-permute-done.46 = f32[4,64]{1,0:T(4,128)S(1)} collective-permute-done((f32[4,64]{1,0:T(4,128)S(1)}, f32[4,64]{1,0:T(4,128)S(1)}, u32[]{:S(2)}, u32[]{:S(2)}) %collective-permute-start.46) | collective-permute-done | bytes 1056 | tf_op jit(solution)/shard_map/ppermute | solution.py:212
  163.9 1.6 fusion
  (171 shorter events, 44.5 us)
Async XLA Ops:
  0.6 75.2 %collective-permute-start.12 = (bf16[1024,4096]{1,0:T(8,128)(2,1)}, bf16[1024,4096]{1,0:T(8,128)(2,1)}, u32[]{:S(2)}, u32[]{:S(2)}) collective-permute-start(bf16[1024,4096]{1,0:T(8,128)(2,1)} %weight_ref.7), channel_id=1, source_target_pairs={{0,16},{16,0},{1,17},{17,1},{2,18},{18,2},{3,19},{19,3},{4,20},{20... | collective-permute-start | bytes 25165832 | tf_op jit(solution)/shard_map/ppermute | solution.py:145
  3.1 10.9 %collective-permute-start = (bf16[2,32,1024]{2,1,0:T(8,128)(2,1)S(1)}, bf16[2,32,1024]{2,1,0:T(8,128)(2,1)S(1)}, u32[]{:S(2)}, u32[]{:S(2)}) collective-permute-start(bf16[2,32,1024]{2,1,0:T(8,128)(2,1)S(1)} %constant_dynamic-slice_fusion.15), channel_id=1, source_target_pairs={{0,4},{4,0},{8,12},{12,8},{1,5},{5,1},{9,13},{13,9},{2,6},{6,2},{1... | collective-permute-start | bytes 393224 | tf_op jit(solution)/shard_map/ppermute | solution.py:89
  14.0 8.3 %collective-permute-start.3 = (bf16[2,2,32,1024]{3,2,1,0:T(8,128)(2,1)S(1)}, bf16[2,2,32,1024]{3,2,1,0:T(8,128)(2,1)S(1)}, u32[]{:S(2)}, u32[]{:S(2)}) collective-permute-start(bf16[2,2,32,1024]{3,2,1,0:T(8,128)(2,1)S(1)} %pad_maximum_fusion.7), channel_id=1, source_target_pairs={{1,0},{2,1},{3,2},{5,4},{6,5},{7,6},{9,8},{10,9},{11,10},{13,12},{... | collective-permute-start | bytes 786440 | tf_op jit(solution)/shard_map/ppermute | solution.py:102
  15.3 8.4 %collective-permute-start.4 = (bf16[2,2,32,1024]{3,2,1,0:T(8,128)(2,1)S(1)}, bf16[2,2,32,1024]{3,2,1,0:T(8,128)(2,1)S(1)}, u32[]{:S(2)}, u32[]{:S(2)}) collective-permute-start(bf16[2,2,32,1024]{3,2,1,0:T(8,128)(2,1)S(1)} %pad_maximum_fusion.7), channel_id=1, source_target_pairs={{0,1},{1,2},{2,3},{4,5},{5,6},{6,7},{8,9},{9,10},{10,11},{12,13},{... | collective-permute-start | bytes 786440 | tf_op jit(solution)/shard_map/ppermute | solution.py:99
  20.4 42.8 %collective-permute-start.43 = (f32[64]{0:T(128)S(1)}, f32[64]{0:T(128)S(1)}, u32[]{:S(2)}, u32[]{:S(2)}) collective-permute-start(f32[64]{0:T(128)S(1)} %get-tuple-element.73), channel_id=1, source_target_pairs={{0,0},{4,8},{8,16},{12,24},{16,4},{20,12},{24,20},{28,28},{1,1},{5... | collective-permute-start | bytes 776 | tf_op jit(solution)/shard_map/ppermute | solution.py:149
  23.8 13.5 %collective-permute-start.5 = (bf16[2,2,32,1024]{3,2,1,0:T(8,128)(2,1)S(1)}, bf16[2,2,32,1024]{3,2,1,0:T(8,128)(2,1)S(1)}, u32[]{:S(2)}, u32[]{:S(2)}) collective-permute-start(bf16[2,2,32,1024]{3,2,1,0:T(8,128)(2,1)S(1)} %select_select_fusion.6), channel_id=1, source_target_pairs={{0,8},{8,0},{4,12},{12,4},{1,9},{9,1},{5,13},{13,5},{2,10},{10,2},... | collective-permute-start | bytes 786440 | tf_op jit(solution)/shard_map/ppermute | solution.py:113
  25.4 9.1 %collective-permute-start.6 = (bf16[2,2,32,1024]{3,2,1,0:T(8,128)(2,1)S(1)}, bf16[2,2,32,1024]{3,2,1,0:T(8,128)(2,1)S(1)}, u32[]{:S(2)}, u32[]{:S(2)}) collective-permute-start(bf16[2,2,32,1024]{3,2,1,0:T(8,128)(2,1)S(1)} %collective-permute-done.3), channel_id=1, source_target_pairs={{1,0},{2,1},{5,4},{6,5},{9,8},{10,9},{13,12},{14,13},{17,16},{18,1... | collective-permute-start | bytes 786440 | tf_op jit(solution)/shard_map/ppermute | solution.py:102
  26.7 9.3 %collective-permute-start.8 = (bf16[2,2,32,1024]{3,2,1,0:T(8,128)(2,1)S(1)}, bf16[2,2,32,1024]{3,2,1,0:T(8,128)(2,1)S(1)}, u32[]{:S(2)}, u32[]{:S(2)}) collective-permute-start(bf16[2,2,32,1024]{3,2,1,0:T(8,128)(2,1)S(1)} %collective-permute-done.4), channel_id=1, source_target_pairs={{1,2},{2,3},{5,6},{6,7},{9,10},{10,11},{13,14},{14,15},{17,18},{18... | collective-permute-start | bytes 786440 | tf_op jit(solution)/shard_map/ppermute | solution.py:99
  34.5 30.0 %collective-permute-start.44 = (f32[64]{0:T(128)S(1)}, f32[64]{0:T(128)S(1)}, u32[]{:S(2)}, u32[]{:S(2)}) collective-permute-start(f32[64]{0:T(128)S(1)} %get-tuple-element.74), channel_id=1, source_target_pairs={{0,4},{4,12},{8,20},{12,28},{16,0},{20,8},{24,16},{28,24},{1,5},{5... | collective-permute-start | bytes 776 | tf_op jit(solution)/shard_map/ppermute | solution.py:149
  36.0 9.1 %collective-permute-start.7 = (bf16[2,2,32,1024]{3,2,1,0:T(8,128)(2,1)S(1)}, bf16[2,2,32,1024]{3,2,1,0:T(8,128)(2,1)S(1)}, u32[]{:S(2)}, u32[]{:S(2)}) collective-permute-start(bf16[2,2,32,1024]{3,2,1,0:T(8,128)(2,1)S(1)} %collective-permute-done.6), channel_id=1, source_target_pairs={{1,0},{5,4},{9,8},{13,12},{17,16},{21,20},{25,24},{29,28}} | collective-permute-start | bytes 786440 | tf_op jit(solution)/shard_map/ppermute | solution.py:102
  37.3 9.1 %collective-permute-start.9 = (bf16[2,2,32,1024]{3,2,1,0:T(8,128)(2,1)S(1)}, bf16[2,2,32,1024]{3,2,1,0:T(8,128)(2,1)S(1)}, u32[]{:S(2)}, u32[]{:S(2)}) collective-permute-start(bf16[2,2,32,1024]{3,2,1,0:T(8,128)(2,1)S(1)} %collective-permute-done.8), channel_id=1, source_target_pairs={{2,3},{6,7},{10,11},{14,15},{18,19},{22,23},{26,27},{30,31}} | collective-permute-start | bytes 786440 | tf_op jit(solution)/shard_map/ppermute | solution.py:99
  45.1 8.3 %collective-permute-start.11 = (bf16[2,2,32,1024]{3,2,1,0:T(8,128)(2,1)S(1)}, bf16[2,2,32,1024]{3,2,1,0:T(8,128)(2,1)S(1)}, u32[]{:S(2)}, u32[]{:S(2)}) collective-permute-start(bf16[2,2,32,1024]{3,2,1,0:T(8,128)(2,1)S(1)} %get-tuple-element.49), channel_id=1, source_target_pairs={{1,9},{2,10},{3,11},{5,13},{6,14},{7,15},{8,0},{9,1},{10,2},{12,4}... | collective-permute-start | bytes 786440 | tf_op jit(solution)/shard_map/ppermute | solution.py:118
  46.4 8.4 %collective-permute-start.10 = (bf16[2,2,32,1024]{3,2,1,0:T(8,128)(2,1)S(1)}, bf16[2,2,32,1024]{3,2,1,0:T(8,128)(2,1)S(1)}, u32[]{:S(2)}, u32[]{:S(2)}) collective-permute-start(bf16[2,2,32,1024]{3,2,1,0:T(8,128)(2,1)S(1)} %broadcast_select_fusion.1), channel_id=1, source_target_pairs={{0,8},{4,12},{11,3},{15,7},{16,24},{20,28},{27,19},{31,23}} | collective-permute-start | bytes 786440 | tf_op jit(solution)/shard_map/ppermute | solution.py:121
  53.3 8.3 %collective-permute-start.23 = (bf16[2,2,32,1024]{3,2,1,0:T(8,128)(2,1)S(1)}, bf16[2,2,32,1024]{3,2,1,0:T(8,128)(2,1)S(1)}, u32[]{:S(2)}, u32[]{:S(2)}) collective-permute-start(bf16[2,2,32,1024]{3,2,1,0:T(8,128)(2,1)S(1)} %pad_maximum_fusion.8), channel_id=1, source_target_pairs={{1,0},{2,1},{3,2},{5,4},{6,5},{7,6},{9,8},{10,9},{11,10},{13,12},{... | collective-permute-start | bytes 786440 | tf_op jit(solution)/shard_map/ppermute | solution.py:102
  61.6 14.3 %collective-permute-start.17 = (bf16[2,2,2,2,32,1024]{5,4,3,2,1,0:T(8,128)(2,1)S(1)}, bf16[2,2,2,2,32,1024]{5,4,3,2,1,0:T(8,128)(2,1)S(1)}, u32[]{:S(2)}, u32[]{:S(2)}) collective-permute-start(bf16[2,2,2,2,32,1024]{5,4,3,2,1,0:T(8,128)(2,1)S(1)} %pad_maximum_fusion.1), channel_id=1, source_target_pairs={{0,16},{16,0},{1,17},{17,1},{2,18},{18,2},{3,19},{19,3},{4,20},{20... | collective-permute-start | bytes 3145736 | tf_op jit(solution)/shard_map/ppermute | solution.py:181
  63.1 9.2 %collective-permute-start.25 = (bf16[2,2,32,1024]{3,2,1,0:T(8,128)(2,1)S(1)}, bf16[2,2,32,1024]{3,2,1,0:T(8,128)(2,1)S(1)}, u32[]{:S(2)}, u32[]{:S(2)}) collective-permute-start(bf16[2,2,32,1024]{3,2,1,0:T(8,128)(2,1)S(1)} %select_select_fusion.2), channel_id=1, source_target_pairs={{0,8},{8,0},{4,12},{12,4},{1,9},{9,1},{5,13},{13,5},{2,10},{10,2},... | collective-permute-start | bytes 786440 | tf_op jit(solution)/shard_map/ppermute | solution.py:113
  63.2 9.1 %collective-permute-start.26 = (bf16[2,2,32,1024]{3,2,1,0:T(8,128)(2,1)S(1)}, bf16[2,2,32,1024]{3,2,1,0:T(8,128)(2,1)S(1)}, u32[]{:S(2)}, u32[]{:S(2)}) collective-permute-start(bf16[2,2,32,1024]{3,2,1,0:T(8,128)(2,1)S(1)} %collective-permute-done.23), channel_id=1, source_target_pairs={{1,0},{2,1},{5,4},{6,5},{9,8},{10,9},{13,12},{14,13},{17,16},{18,1... | collective-permute-start | bytes 786440 | tf_op jit(solution)/shard_map/ppermute | solution.py:102
  72.5 23.9 %collective-permute-start.31 = (bf16[2,2,32,1024]{3,2,1,0:T(8,128)(2,1)S(1)}, bf16[2,2,32,1024]{3,2,1,0:T(8,128)(2,1)S(1)}, u32[]{:S(2)}, u32[]{:S(2)}) collective-permute-start(bf16[2,2,32,1024]{3,2,1,0:T(8,128)(2,1)S(1)} %get-tuple-element.48), channel_id=1, source_target_pairs={{1,9},{2,10},{3,11},{5,13},{6,14},{7,15},{8,0},{9,1},{10,2},{12,4}... | collective-permute-start | bytes 786440 | tf_op jit(solution)/shard_map/ppermute | solution.py:118
  73.8 22.4 %collective-permute-start.27 = (bf16[2,2,32,1024]{3,2,1,0:T(8,128)(2,1)S(1)}, bf16[2,2,32,1024]{3,2,1,0:T(8,128)(2,1)S(1)}, u32[]{:S(2)}, u32[]{:S(2)}) collective-permute-start(bf16[2,2,32,1024]{3,2,1,0:T(8,128)(2,1)S(1)} %collective-permute-done.26), channel_id=1, source_target_pairs={{1,0},{5,4},{9,8},{13,12},{17,16},{21,20},{25,24},{29,28}} | collective-permute-start | bytes 786440 | tf_op jit(solution)/shard_map/ppermute | solution.py:102
  75.1 21.1 %collective-permute-start.29 = (bf16[2,2,32,1024]{3,2,1,0:T(8,128)(2,1)S(1)}, bf16[2,2,32,1024]{3,2,1,0:T(8,128)(2,1)S(1)}, u32[]{:S(2)}, u32[]{:S(2)}) collective-permute-start(bf16[2,2,32,1024]{3,2,1,0:T(8,128)(2,1)S(1)} %collective-permute-done.28), channel_id=1, source_target_pairs={{2,3},{6,7},{10,11},{14,15},{18,19},{22,23},{26,27},{30,31}} | collective-permute-start | bytes 786440 | tf_op jit(solution)/shard_map/ppermute | solution.py:99
  82.5 17.9 %collective-permute-start.20 = (f16[2,2,32,1024]{3,2,1,0:T(8,128)(2,1)S(1)}, f16[2,2,32,1024]{3,2,1,0:T(8,128)(2,1)S(1)}, u32[]{:S(2)}, u32[]{:S(2)}) collective-permute-start(f16[2,2,32,1024]{3,2,1,0:T(8,128)(2,1)S(1)} %fusion.8), channel_id=1, source_target_pairs={{0,8},{8,0},{4,12},{12,4},{1,9},{9,1},{5,13},{13,5},{2,10},{10,2},... | collective-permute-start | bytes 786440 | tf_op jit(solution)/shard_map/ppermute | solution.py:165
  85.4 17.2 %collective-permute-start.18 = (f16[2,2,32,1024]{3,2,0,1:T(8,128)(2,1)S(1)}, f16[2,2,32,1024]{3,2,0,1:T(8,128)(2,1)S(1)}, u32[]{:S(2)}, u32[]{:S(2)}) collective-permute-start(f16[2,2,32,1024]{3,2,0,1:T(8,128)(2,1)S(1)} %fusion.12), channel_id=1, source_target_pairs={{0,4},{4,0},{8,12},{12,8},{1,5},{5,1},{9,13},{13,9},{2,6},{6,2},{1... | collective-permute-start | bytes 786440 | tf_op jit(solution)/shard_map/ppermute | solution.py:164
  96.2 9.0 %collective-permute-start.13 = (f16[2,2,32,1024]{3,2,0,1:T(8,128)(2,1)S(1)}, f16[2,2,32,1024]{3,2,0,1:T(8,128)(2,1)S(1)}, u32[]{:S(2)}, u32[]{:S(2)}) collective-permute-start(f16[2,2,32,1024]{3,2,0,1:T(8,128)(2,1)S(1)} %fusion.10), channel_id=1, source_target_pairs={{0,4},{4,0},{8,12},{12,8},{1,5},{5,1},{9,13},{13,9},{2,6},{6,2},{1... | collective-permute-start | bytes 786440 | tf_op jit(solution)/shard_map/ppermute | solution.py:164
  96.4 11.8 %collective-permute-start.30 = (bf16[2,2,32,1024]{3,2,1,0:T(8,128)(2,1)S(1)}, bf16[2,2,32,1024]{3,2,1,0:T(8,128)(2,1)S(1)}, u32[]{:S(2)}, u32[]{:S(2)}) collective-permute-start(bf16[2,2,32,1024]{3,2,1,0:T(8,128)(2,1)S(1)} %broadcast_select_fusion), channel_id=1, source_target_pairs={{0,8},{4,12},{11,3},{15,7},{16,24},{20,28},{27,19},{31,23}} | collective-permute-start | bytes 786440 | tf_op jit(solution)/shard_map/ppermute | solution.py:121
  100.5 14.9 %collective-permute-start.21 = (f16[2,32,1024]{2,1,0:T(8,128)(2,1)S(1)}, f16[2,32,1024]{2,1,0:T(8,128)(2,1)S(1)}, u32[]{:S(2)}, u32[]{:S(2)}) collective-permute-start(f16[2,32,1024]{2,1,0:T(8,128)(2,1)S(1)} %fusion.28), channel_id=1, source_target_pairs={{0,4},{4,0},{8,12},{12,8},{1,5},{5,1},{9,13},{13,9},{2,6},{6,2},{1... | collective-permute-start | bytes 393224 | tf_op jit(solution)/shard_map/ppermute | solution.py:169
  102.7 15.3 %collective-permute-start.19 = (f16[2,32,1024]{2,1,0:T(8,128)(2,1)S(1)}, f16[2,32,1024]{2,1,0:T(8,128)(2,1)S(1)}, u32[]{:S(2)}, u32[]{:S(2)}) collective-permute-start(f16[2,32,1024]{2,1,0:T(8,128)(2,1)S(1)} %fusion.27), channel_id=1, source_target_pairs={{0,8},{8,0},{4,12},{12,4},{1,9},{9,1},{5,13},{13,5},{2,10},{10,2},... | collective-permute-start | bytes 393224 | tf_op jit(solution)/shard_map/ppermute | solution.py:168
  104.0 14.4 %collective-permute-start.16 = (f16[2,32,1024]{2,1,0:T(8,128)(2,1)S(1)}, f16[2,32,1024]{2,1,0:T(8,128)(2,1)S(1)}, u32[]{:S(2)}, u32[]{:S(2)}) collective-permute-start(f16[2,32,1024]{2,1,0:T(8,128)(2,1)S(1)} %fusion.26), channel_id=1, source_target_pairs={{0,4},{4,0},{8,12},{12,8},{1,5},{5,1},{9,13},{13,9},{2,6},{6,2},{1... | collective-permute-start | bytes 393224 | tf_op jit(solution)/shard_map/ppermute | solution.py:169
  105.3 13.2 %collective-permute-start.14 = (f16[2,32,1024]{2,1,0:T(8,128)(2,1)S(1)}, f16[2,32,1024]{2,1,0:T(8,128)(2,1)S(1)}, u32[]{:S(2)}, u32[]{:S(2)}) collective-permute-start(f16[2,32,1024]{2,1,0:T(8,128)(2,1)S(1)} %fusion.25), channel_id=1, source_target_pairs={{0,8},{8,0},{4,12},{12,4},{1,9},{9,1},{5,13},{13,5},{2,10},{10,2},... | collective-permute-start | bytes 393224 | tf_op jit(solution)/shard_map/ppermute | solution.py:168
  108.6 23.1 %collective-permute-start.36 = (bf16[2,2,2,2,32,1024]{5,4,3,2,1,0:T(8,128)(2,1)S(1)}, bf16[2,2,2,2,32,1024]{5,4,3,2,1,0:T(8,128)(2,1)S(1)}, u32[]{:S(2)}, u32[]{:S(2)}) collective-permute-start(bf16[2,2,2,2,32,1024]{5,4,3,2,1,0:T(8,128)(2,1)S(1)} %pad_maximum_fusion.2), channel_id=1, source_target_pairs={{0,16},{16,0},{1,17},{17,1},{2,18},{18,2},{3,19},{19,3},{4,20},{20... | collective-permute-start | bytes 3145736 | tf_op jit(solution)/shard_map/ppermute | solution.py:181
  115.4 9.5 %collective-permute-start.34 = (f16[2,2,32,1024]{3,2,0,1:T(8,128)(2,1)S(1)}, f16[2,2,32,1024]{3,2,0,1:T(8,128)(2,1)S(1)}, u32[]{:S(2)}, u32[]{:S(2)}) collective-permute-start(f16[2,2,32,1024]{3,2,0,1:T(8,128)(2,1)S(1)} %fusion.14), channel_id=1, source_target_pairs={{0,8},{8,0},{4,12},{12,4},{1,9},{9,1},{5,13},{13,5},{2,10},{10,2},... | collective-permute-start | bytes 786440 | tf_op jit(solution)/shard_map/ppermute | solution.py:165
  118.0 8.5 %collective-permute-start.32 = (f16[2,2,32,1024]{3,2,0,1:T(8,128)(2,1)S(1)}, f16[2,2,32,1024]{3,2,0,1:T(8,128)(2,1)S(1)}, u32[]{:S(2)}, u32[]{:S(2)}) collective-permute-start(f16[2,2,32,1024]{3,2,0,1:T(8,128)(2,1)S(1)} %fusion.13), channel_id=1, source_target_pairs={{0,4},{4,0},{8,12},{12,8},{1,5},{5,1},{9,13},{13,9},{2,6},{6,2},{1... | collective-permute-start | bytes 786440 | tf_op jit(solution)/shard_map/ppermute | solution.py:164
  118.9 32.7 %collective-permute-start.41 = (f16[2,32,2048]{2,1,0:T(8,128)(2,1)S(1)}, f16[2,32,2048]{2,1,0:T(8,128)(2,1)S(1)}, u32[]{:S(2)}, u32[]{:S(2)}) collective-permute-start(f16[2,32,2048]{2,1,0:T(8,128)(2,1)S(1)} %get-tuple-element.52), channel_id=1, source_target_pairs={{0,16},{16,0},{1,17},{17,1},{2,18},{18,2},{3,19},{19,3},{4,20},{20... | collective-permute-start | bytes 786440 | tf_op jit(solution)/shard_map/ppermute | solution.py:187
  (19 other events, 135.9 us)

commit v7 on v6

--- a/solution.py
+++ b/solution.py
@@ -10,7 +10,6 @@
 CHUNKS = 2
 SHRINK = 1.0 / 32.0
 SUM_TYPE = jnp.float16
-TILE = 512
 
 X_SWAP = [(0, 1), (1, 0), (2, 3), (3, 2)]
 Y_SWAP = [(0, 2), (2, 0), (1, 3), (3, 1)]
@@ -25,36 +24,30 @@
     return lax.optimization_barrier((value, *others))[0]
 
 
-def logits_kernel(place_ref, left_ref, weight_ref, take_ref, out_ref):
-    side, own = place_ref[0], place_ref[1]
+def columns_kernel(start_ref, weight_ref, out_ref, done):
     width = out_ref.shape[1]
-    tile = min(TILE, width)
-
-    @pl.loop(0, width // tile)
-    def _(t):
-        here = pl.ds(pl.multiple_of(t * tile, tile), tile)
-        there = pl.ds(pl.multiple_of(side * width + t * tile, tile), tile)
-        out = jnp.dot(left_ref[own], weight_ref[:, there], preferred_element_type=jnp.float32)
-        out += jnp.dot(left_ref[1 - own], take_ref[:, there], preferred_element_type=jnp.float32)
-        out_ref[:, here] = out * SHRINK
-
-
-def partial_logits(core, own, left, head_weight, take):
-    _, rows, block = left.shape
-    width = take.shape[1] // 2
-    whole = pl.BlockSpec(memory_space=pltpu.VMEM)
+    start = pl.multiple_of(start_ref[0] * width, width)
+    copy = pltpu.make_async_copy(weight_ref.at[:, pl.ds(start, width)], out_ref, done)
+    copy.start()
+    copy.wait()
+
+
+def half_columns(weight, side):
+    block, columns = weight.shape
     return pl.pallas_call(
-        logits_kernel,
-        in_specs=[pl.BlockSpec(memory_space=pltpu.SMEM), whole, whole, whole],
-        out_specs=whole,
-        out_shape=jax.ShapeDtypeStruct((rows, width), jnp.float32),
-        compiler_params=pltpu.CompilerParams(vmem_limit_bytes=32 * 1024 * 1024),
+        columns_kernel,
+        in_specs=[
+            pl.BlockSpec(memory_space=pltpu.SMEM),
+            pl.BlockSpec(memory_space=pl.ANY),
+        ],
+        out_specs=pl.BlockSpec(memory_space=pltpu.VMEM),
+        out_shape=jax.ShapeDtypeStruct((block, columns // 2), weight.dtype),
+        scratch_shapes=[pltpu.SemaphoreType.DMA],
         cost_estimate=pl.CostEstimate(
-            flops=4 * rows * block * width,
-            bytes_accessed=4 * block * width + 4 * rows * block + 4 * rows * width,
-            transcendentals=0,
+            flops=0, bytes_accessed=2 * block * columns, transcendentals=0
         ),
-    )(jnp.stack([core, own]).astype(jnp.int32), left, head_weight, take)
+        compiler_params=pltpu.CompilerParams(vmem_limit_bytes=16 * 1024 * 1024),
+    )(side.reshape(1).astype(jnp.int32), weight)
 
 
 def on_device(hidden, norm_gain, head_weight):
@@ -75,10 +68,13 @@
     gained = (wide * norm_gain.astype(jnp.float32)[None, :]).astype(jnp.bfloat16)
     gained = gained.reshape(2, seg, depth)
 
+    def paired(value, reach):
+        return lax.ppermute(value, "vocab", [(i, i ^ reach) for i in range(vocab)])
+
     squares = jnp.sum(wide * wide, axis=1)
     reach = 1
-    while reach < vocab:
-        squares += lax.ppermute(squares, "vocab", [(i, i ^ reach) for i in range(vocab)])
+    while 2 * reach < vocab:
+        squares += paired(squares, reach)
         reach *= 2
 
     first = level // 2 if vocab == 4 else 0
@@ -88,11 +84,11 @@
         sides = [lax.dynamic_slice_in_dim(piece, (1 - x) * block, block, 2) for piece in pieces]
         sides = [lax.ppermute(side, "batch", X_SWAP) for side in sides]
 
-    def line_features(c, held, *earlier):
+    def line_features(c):
         mine = lax.dynamic_slice_in_dim(pieces[c], x * block, block, 2)
         other = sides[c]
         own = jnp.stack([jnp.where(x == 0, mine, other), jnp.where(x == 0, other, mine)])
-        own = after(own, squares, *held)
+        own = after(own, squares)
         below, above = [own], [own]
         for k in range(1, vocab):
             below.append(
@@ -101,6 +97,8 @@
             above.append(
                 lax.ppermute(above[-1], "vocab", [(z + 1, z) for z in range(vocab - k)])
             )
+            if c == 0 and k == 2:
+                below[2], above[2] = after(below[2], *sides), after(above[2], *sides)
 
         def quarter(place, reach):
             part = own
@@ -115,6 +113,7 @@
         pairs = [(b * vocab + z, (b ^ 2) * vocab + z) for b in range(4) for z in range(vocab)]
         late = [pair for pair in pairs if (pair[0] // vocab // 2, pair[0] % vocab) in ends]
         early = [pair for pair in pairs if pair not in late]
+        earlier = yield below[1], above[1]
         got_early = after(lax.ppermute(quarter(far, 2), ("batch", "vocab"), early), *earlier)
         below[-1], above[-1] = after(below[-1], *earlier), after(above[-1], *earlier)
         last = jnp.where(level == 0, above[-1], below[-1])
@@ -129,36 +128,53 @@
             halves.append(
                 jnp.stack([jnp.where(y == 0, mine, other), jnp.where(y == 0, other, mine)])
             )
-        return jnp.stack(halves), (below[-1], above[-1], got_near, got_early)
-
-    def gathered_features(c, held, *earlier):
+        yield jnp.stack(halves)
+
+    def gathered_features(c):
+        earlier = yield (gained,)
         whole = lax.all_gather(pieces[c], "vocab", axis=2, tiled=True)
         whole = whole.reshape(2, step, 2, 4, block).transpose(3, 2, 0, 1, 4)
         whole = lax.all_to_all(whole, "batch", split_axis=0, concat_axis=0)
         whole = whole.reshape(2, 2, 2, 2, step, block).transpose(2, 0, 1, 3, 4, 5)
-        return after(whole, *earlier), (gained,)
+        yield after(whole, *earlier)
 
     features = line_features if lined else gathered_features
     own_half = core ^ first if lined else core
-    found, begun = features(0, ())
+    gathers = [features(c) for c in range(CHUNKS)]
+    begun = [next(gather) for gather in gathers]
+    found = gathers[0].send(())
+    for parts in begun[1:]:
+        found = after(found, *parts)
 
     take = lax.ppermute(head_weight, "pair", CORE_SWAP)
-
-    squares = squares.reshape(2, seg)
-    sent = [
-        lax.ppermute(
-            pick(squares, core ^ k, 0),
-            ("pair", "batch"),
-            [(4 * s + b, 2 * b + (s ^ k)) for s in range(2) for b in range(4)],
+    keep = half_columns(after(head_weight, *begun[0]), core)
+    take = half_columns(take, core)
+
+    more_squares = paired(after(squares, *begun[0]), reach)
+
+    def row_scale(*earlier):
+        total = (squares + after(more_squares, *earlier)).reshape(2, seg)
+        sent = [
+            lax.ppermute(
+                pick(total, core ^ k, 0),
+                ("pair", "batch"),
+                [(4 * s + b, 2 * b + (s ^ k)) for s in range(2) for b in range(4)],
+            )
+            for k in range(2)
+        ]
+        total = jnp.stack(
+            [jnp.where(x == 0, sent[0], sent[1]), jnp.where(x == 0, sent[1], sent[0])]
         )
-        for k in range(2)
-    ]
-    total_sq = jnp.stack([jnp.where(x == 0, sent[0], sent[1]), jnp.where(x == 0, sent[1], sent[0])])
-    scale = lax.rsqrt(total_sq / model + EPS) / SHRINK
+        return lax.rsqrt(total / model + EPS) / SHRINK
+
+    def partial(left):
+        out = jnp.dot(pick(left, own_half, 0), keep, preferred_element_type=jnp.float32)
+        out += jnp.dot(pick(left, 1 - own_half, 0), take, preferred_element_type=jnp.float32)
+        return out * SHRINK
 
     def reduced(left):
         middle = width // 2
-        parts = partial_logits(core, own_half, left.reshape(2, -1, block), head_weight, take)
+        parts = partial(left.reshape(2, -1, block))
         parts = parts.reshape(2, 2, 2, step, width)
         low, high = parts[..., :middle], parts[..., middle:]
         away_x = lax.ppermute(pick(low, 1 - x, 2).astype(SUM_TYPE), "batch", X_SWAP)
@@ -178,11 +194,15 @@
 
     done = []
     for c in range(CHUNKS):
-        other = lax.ppermute(found, "pair", CORE_SWAP)
+        found, other = lax.optimization_barrier(
+            (found, lax.ppermute(found, "pair", CORE_SWAP))
+        )
         own_sums, parts, _ = reduced(found)
-        other_sums, _, halfway = reduced(other)
+        other_sums, more_parts, halfway = reduced(other)
+        if c == 0:
+            scale = row_scale(more_parts)
         if c + 1 < CHUNKS:
-            found = after(features(c + 1, begun, parts)[0], halfway)
+            found = after(gathers[c + 1].send((parts,)), halfway)
         sums = jnp.stack([own_sums, other_sums])
         theirs = lax.ppermute(pick(sums, 1 - core, 1), "pair", CORE_SWAP)
         done.append((pick(sums, core, 1), theirs))

time: 166 us -> 156 us (0.940)
  Pallas kernels: 25.1 us -> 3.24 us
  waiting for transfers between devices: 62.4 us -> 45.2 us
  matrix products: 0 us -> 14 us
  starting transfers between devices: 66.3 us -> 71.6 us
  other arithmetic: 8.41 us -> 13.4 us
  local copies, waits for them, and re-layouts: 1.76 us -> 5.83 us
    pallas_call x4 -> x2, Pallas kernels: 25.1 us -> 3.24 us  [half_columns(): pl.pallas_call(columns_kernel, in_specs=[pl.BlockSpec(memory_space=pltpu....]
    dot_general x0 -> x8, matrix products: none -> 14 us  [the longest x4 7.57 us: partial(): jnp.dot(pick(left, 1 - own_half, 0), take, preferred_element_type=jnp.flo...]
    ppermute x6, waiting for transfers between devices: 24.3 us -> 15.9 us  [line_features(): lax.ppermute(above[-1], 'vocab', [(z + 1, z) for z in range(vocab - k)])]
    ppermute x4, starting transfers between devices: 3.38 us -> 8.92 us  [reduced(): lax.ppermute(pick(sum_x, 1 - y, 1).astype(SUM_TYPE), 'batch', Y_SWAP)]
    ppermute x4, waiting for transfers between devices: 11.3 us -> 6.04 us  [reduced(): lax.ppermute(pick(high, 1 - y, 1).astype(SUM_TYPE), 'batch', Y_SWAP)]
    unnamed x7 -> x13, local copies, waits for them, and re-layouts: 0.07 us -> 4.14 us
    ppermute x4, waiting for transfers between devices: 5.38 us -> 1.66 us  [reduced(): lax.ppermute(pick(sum_y, 1 - x, 1).astype(SUM_TYPE), 'batch', X_SWAP)]
    ppermute x4, starting transfers between devices: 3.53 us -> 6.75 us  [reduced(): lax.ppermute(pick(sum_y, 1 - x, 1).astype(SUM_TYPE), 'batch', X_SWAP)]
  transfers between devices with their start and end apart: 48 -> 48, of which waited for: 25 -> 24; matrix products, arithmetic and copies ran while one was open for 4% -> 14% of each run, Pallas kernels for 15% -> 2%
where the time goes in v7:
time: 156 us; the launch traced here: 155 us
  starting transfers between devices  71.6 us (46%)
  waiting for transfers between devices  45.2 us (29%)
  matrix products  14 us (9%)
  other arithmetic  13.4 us (9%)
  local copies, waits for them, and re-layouts  5.83 us (4%)
  Pallas kernels  3.24 us (2%)
  between operations  1.61 us (1%)
    ppermute x6, waiting for transfers between devices, line_features(): lax.ppermute(above[-1], 'vocab', [(z + 1, z) for z in range(vocab - k)])  15.9 us
    ppermute x6, starting transfers between devices, line_features(): lax.ppermute(below[-1], 'vocab', [(z, z + 1) for z in range(k - 1, vocab...  12.9 us
    ppermute x4, starting transfers between devices, reduced(): lax.ppermute(pick(sum_x, 1 - y, 1).astype(SUM_TYPE), 'batch', Y_SWAP)  8.92 us
    ppermute x6, starting transfers between devices, line_features(): lax.ppermute(above[-1], 'vocab', [(z + 1, z) for z in range(vocab - k)])  7.72 us
    dot_general x4, matrix products, partial(): jnp.dot(pick(left, 1 - own_half, 0), take, preferred_element_type=jnp.flo...  7.57 us
    ppermute x2, starting transfers between devices, line_features(): got_late = lax.ppermute(last, ('batch', 'vocab'), late)  7.05 us
    ppermute x2, starting transfers between devices, row_scale(): lax.ppermute(pick(total, core ^ k, 0), ('pair', 'batch'), [(4 * s + b, 2...  6.82 us
    ppermute x4, starting transfers between devices, reduced(): lax.ppermute(pick(sum_y, 1 - x, 1).astype(SUM_TYPE), 'batch', X_SWAP)  6.75 us
  transfers between devices with their start and end apart: 48, of which 24 were waited for; matrix products, arithmetic and copies ran while one was open for 14% of the time, Pallas kernels for 2%

profile of v7, /device:TPU:0, one launch (start us, length us, event | category | flops | bytes accessed | tf_op | source)
XLA Modules:
  0.0 154.9 jit_solution(10385716770466333676)
XLA Ops:
  3.1 2.6 %collective-permute-start = (bf16[2,32,1024]{2,1,0:T(8,128)(2,1)S(1)}, bf16[2,32,1024]{2,1,0:T(8,128)(2,1)S(1)}, u32[]{:S(2)}, u32[]{:S(2)}) collective-permute-start(bf16[2,32,1024]{2,1,0:T(8,128)(2,1)S(1)} %constant_dynamic-slice_fusion.15), channel_id=1, source_target_pairs={{0,4},{4,0},{8,12},{12,8},{1,5},{5,1},{9,13},{13,9},{2,6},{6,2},{1... | collective-permute-start | bytes 393224 | tf_op jit(solution)/shard_map/ppermute | solution.py:85
  9.9 4.2 %collective-permute-start.3 = (bf16[2,2,32,1024]{3,2,1,0:T(8,128)(2,1)S(1)}, bf16[2,2,32,1024]{3,2,1,0:T(8,128)(2,1)S(1)}, u32[]{:S(2)}, u32[]{:S(2)}) collective-permute-start(bf16[2,2,32,1024]{3,2,1,0:T(8,128)(2,1)S(1)} %pad_maximum_fusion.4), channel_id=1, source_target_pairs={{0,1},{1,2},{2,3},{4,5},{5,6},{6,7},{8,9},{9,10},{10,11},{12,13},{... | collective-permute-start | bytes 786440 | tf_op jit(solution)/shard_map/ppermute | solution.py:95
  15.5 4.6 %collective-permute-start.12 = (bf16[2,2,32,1024]{3,2,1,0:T(8,128)(2,1)S(1)}, bf16[2,2,32,1024]{3,2,1,0:T(8,128)(2,1)S(1)}, u32[]{:S(2)}, u32[]{:S(2)}) collective-permute-start(bf16[2,2,32,1024]{3,2,1,0:T(8,128)(2,1)S(1)} %pad_maximum_fusion.5), channel_id=1, source_target_pairs={{0,1},{1,2},{2,3},{4,5},{5,6},{6,7},{8,9},{9,10},{10,11},{12,13},{... | collective-permute-start | bytes 786440 | tf_op jit(solution)/shard_map/ppermute | solution.py:95
  21.4 1.8 %collective-permute-done.2 = bf16[2,2,32,1024]{3,2,1,0:T(8,128)(2,1)S(1)} collective-permute-done((bf16[2,2,32,1024]{3,2,1,0:T(8,128)(2,1)S(1)}, bf16[2,2,32,1024]{3,2,1,0:T(8,128)(2,1)S(1)}, u32[]{:S(2)}, u32[]{:S(2)}) %collective-permute-start.2) | collective-permute-done | bytes 262176 | tf_op jit(solution)/shard_map/ppermute | solution.py:98
  26.8 4.4 %collective-permute-done.13 = bf16[2,2,32,1024]{3,2,1,0:T(8,128)(2,1)S(1)} collective-permute-done((bf16[2,2,32,1024]{3,2,1,0:T(8,128)(2,1)S(1)}, bf16[2,2,32,1024]{3,2,1,0:T(8,128)(2,1)S(1)}, u32[]{:S(2)}, u32[]{:S(2)}) %collective-permute-start.13) | collective-permute-done | bytes 262176 | tf_op jit(solution)/shard_map/ppermute | solution.py:98
  32.6 3.5 %collective-permute-done.5 = bf16[2,2,32,1024]{3,2,1,0:T(8,128)(2,1)S(1)} collective-permute-done((bf16[2,2,32,1024]{3,2,1,0:T(8,128)(2,1)S(1)}, bf16[2,2,32,1024]{3,2,1,0:T(8,128)(2,1)S(1)}, u32[]{:S(2)}, u32[]{:S(2)}) %collective-permute-start.5) | collective-permute-done | bytes 262176 | tf_op jit(solution)/shard_map/ppermute | solution.py:98
  39.6 6.2 %collective-permute-done.7 = bf16[2,2,32,1024]{3,2,1,0:T(8,128)(2,1)S(1)} collective-permute-done((bf16[2,2,32,1024]{3,2,1,0:T(8,128)(2,1)S(1)}, bf16[2,2,32,1024]{3,2,1,0:T(8,128)(2,1)S(1)}, u32[]{:S(2)}, u32[]{:S(2)}) %collective-permute-start.7) | collective-permute-done | bytes 262176 | tf_op jit(solution)/shard_map/ppermute | solution.py:98
  47.1 4.6 %collective-permute-start.10 = (bf16[2,2,32,1024]{3,2,1,0:T(8,128)(2,1)S(1)}, bf16[2,2,32,1024]{3,2,1,0:T(8,128)(2,1)S(1)}, u32[]{:S(2)}, u32[]{:S(2)}) collective-permute-start(bf16[2,2,32,1024]{3,2,1,0:T(8,128)(2,1)S(1)} %broadcast_select_fusion.1), channel_id=1, source_target_pairs={{0,8},{4,12},{11,3},{15,7},{16,24},{20,28},{27,19},{31,23}} | collective-permute-start | bytes 786440 | tf_op jit(solution)/shard_map/ppermute | solution.py:120
  51.8 2.2 %collective-permute-done.11 = bf16[2,2,32,1024]{3,2,1,0:T(8,128)(2,1)S(1)} collective-permute-done((bf16[2,2,32,1024]{3,2,1,0:T(8,128)(2,1)S(1)}, bf16[2,2,32,1024]{3,2,1,0:T(8,128)(2,1)S(1)}, u32[]{:S(2)}, u32[]{:S(2)}) %collective-permute-start.11) | collective-permute-done | bytes 262176 | tf_op jit(solution)/shard_map/ppermute | solution.py:117
  56.8 2.5 %collective-permute-start.24 = (bf16[2,2,32,1024]{3,2,1,0:T(8,128)(2,1)S(1)}, bf16[2,2,32,1024]{3,2,1,0:T(8,128)(2,1)S(1)}, u32[]{:S(2)}, u32[]{:S(2)}) collective-permute-start(bf16[2,2,32,1024]{3,2,1,0:T(8,128)(2,1)S(1)} %select_select_fusion.2), channel_id=1, source_target_pairs={{0,8},{8,0},{4,12},{12,4},{1,9},{9,1},{5,13},{13,5},{2,10},{10,2},... | collective-permute-start | bytes 786440 | tf_op jit(solution)/shard_map/ppermute | solution.py:111
  59.4 3.4 %copy-done = bf16[1024,4096]{1,0:T(8,128)(2,1)S(1)} copy-done((bf16[1024,4096]{1,0:T(8,128)(2,1)S(1)}, bf16[1024,4096]{1,0:T(8,128)(2,1)}, u32[]{:S(2)}) %copy-start) | copy-done | bytes 8388632
  63.9 2.4 %collective-permute-done.24 = bf16[2,2,32,1024]{3,2,1,0:T(8,128)(2,1)S(1)} collective-permute-done((bf16[2,2,32,1024]{3,2,1,0:T(8,128)(2,1)S(1)}, bf16[2,2,32,1024]{3,2,1,0:T(8,128)(2,1)S(1)}, u32[]{:S(2)}, u32[]{:S(2)}) %collective-permute-start.24) | collective-permute-done | bytes 262176 | tf_op jit(solution)/shard_map/ppermute | solution.py:111
  71.2 2.2 %shard_map.51 = bf16[1024,2048]{1,0:T(8,128)(2,1)S(1)} custom-call(s32[1]{0:T(128)} %bitcast.13.start_ref, bf16[1024,4096]{1,0:T(8,128)(2,1)} %collective-permute-done.15.weight_ref), custom_call_target="tpu_custom_call" | custom-call | bytes 8388608 | tf_op jit(solution)/shard_map/pallas_call | solution.py:37
  77.7 6.2 %collective-permute-start.44 = (f32[64]{0:T(128)S(1)}, f32[64]{0:T(128)S(1)}, u32[]{:S(2)}, u32[]{:S(2)}) collective-permute-start(f32[64]{0:T(128)S(1)} %get-tuple-element.90), channel_id=1, source_target_pairs={{0,4},{4,12},{8,20},{12,28},{16,0},{20,8},{24,16},{28,24},{1,5},{5... | collective-permute-start | bytes 776 | tf_op jit(solution)/shard_map/ppermute | solution.py:158
  83.8 3.7 %fusion.21 = f32[256,2048]{1,0:T(8,128)S(1)} fusion(bf16[1024,2048]{1,0:T(8,128)(2,1)} %copy-done.3, bf16[2,256,1024]{2,1,0:T(8,128)(2,1)} %bitcast.11, s32[]{:T(128)S(6)} %select_n.401), kind=kOutput, calls=%fused_computation.56 | convolution fusion | flops 1073741824 | bytes 6815748 | tf_op jit(solution)/shard_map/dot_general | solution.py:172
  87.6 2.4 %fusion.3 = f32[256,2048]{1,0:T(8,128)S(1)} fusion(f32[256,2048]{1,0:T(8,128)S(1)} %fusion.21, bf16[1024,2048]{1,0:T(8,128)(2,1)S(1)} %copy-done.2, bf16[2,256,1024]{2,1,0:T(8,128)(2,1)} %bitcast.11, s32[]{:T(128)S(6)} %select_n.400), kind=kOutput, calls=%fused_computation.7 | convolution fusion | flops 1074790400 | bytes 8912900 | tf_op jit(solution)/shard_map/dot_general | solution.py:171
  92.8 2.5 %collective-permute-start.29 = (bf16[2,2,32,1024]{3,2,1,0:T(8,128)(2,1)S(1)}, bf16[2,2,32,1024]{3,2,1,0:T(8,128)(2,1)S(1)}, u32[]{:S(2)}, u32[]{:S(2)}) collective-permute-start(bf16[2,2,32,1024]{3,2,1,0:T(8,128)(2,1)S(1)} %broadcast_select_fusion), channel_id=1, source_target_pairs={{0,8},{4,12},{11,3},{15,7},{16,24},{20,28},{27,19},{31,23}} | collective-permute-start | bytes 786440 | tf_op jit(solution)/shard_map/ppermute | solution.py:120
  96.3 2.1 %collective-permute-done.22 = f16[2,2,32,1024]{3,2,0,1:T(8,128)(2,1)S(1)} collective-permute-done((f16[2,2,32,1024]{3,2,0,1:T(8,128)(2,1)S(1)}, f16[2,2,32,1024]{3,2,0,1:T(8,128)(2,1)S(1)}, u32[]{:S(2)}, u32[]{:S(2)}) %collective-permute-start.22) | collective-permute-done | bytes 262176 | tf_op jit(solution)/shard_map/ppermute | solution.py:181
  99.8 3.5 %collective-permute-done.29 = bf16[2,2,32,1024]{3,2,1,0:T(8,128)(2,1)S(1)} collective-permute-done((bf16[2,2,32,1024]{3,2,1,0:T(8,128)(2,1)S(1)}, bf16[2,2,32,1024]{3,2,1,0:T(8,128)(2,1)S(1)}, u32[]{:S(2)}, u32[]{:S(2)}) %collective-permute-start.29) | collective-permute-done | bytes 262176 | tf_op jit(solution)/shard_map/ppermute | solution.py:120
  106.3 1.9 %collective-permute-start.19 = (f16[2,32,1024]{2,1,0:T(8,128)(2,1)S(1)}, f16[2,32,1024]{2,1,0:T(8,128)(2,1)S(1)}, u32[]{:S(2)}, u32[]{:S(2)}) collective-permute-start(f16[2,32,1024]{2,1,0:T(8,128)(2,1)S(1)} %fusion.50), channel_id=1, source_target_pairs={{0,4},{4,0},{8,12},{12,8},{1,5},{5,1},{9,13},{13,9},{2,6},{6,2},{1... | collective-permute-start | bytes 393224 | tf_op jit(solution)/shard_map/ppermute | solution.py:185
  108.3 2.5 %collective-permute-start.17 = (f16[2,32,1024]{2,1,0:T(8,128)(2,1)S(1)}, f16[2,32,1024]{2,1,0:T(8,128)(2,1)S(1)}, u32[]{:S(2)}, u32[]{:S(2)}) collective-permute-start(f16[2,32,1024]{2,1,0:T(8,128)(2,1)S(1)} %fusion.49), channel_id=1, source_target_pairs={{0,8},{8,0},{4,12},{12,4},{1,9},{9,1},{5,13},{13,5},{2,10},{10,2},... | collective-permute-start | bytes 393224 | tf_op jit(solution)/shard_map/ppermute | solution.py:184
  111.9 1.9 %collective-permute-done.17 = f16[2,32,1024]{2,1,0:T(8,128)(2,1)S(1)} collective-permute-done((f16[2,32,1024]{2,1,0:T(8,128)(2,1)S(1)}, f16[2,32,1024]{2,1,0:T(8,128)(2,1)S(1)}, u32[]{:S(2)}, u32[]{:S(2)}) %collective-permute-start.17) | collective-permute-done | bytes 131104 | tf_op jit(solution)/shard_map/ppermute | solution.py:184
  120.3 1.9 %collective-permute-start.38 = (f16[2,2,32,1024]{3,2,1,0:T(8,128)(2,1)S(1)}, f16[2,2,32,1024]{3,2,1,0:T(8,128)(2,1)S(1)}, u32[]{:S(2)}, u32[]{:S(2)}) collective-permute-start(f16[2,2,32,1024]{3,2,1,0:T(8,128)(2,1)S(1)} %fusion.33), channel_id=1, source_target_pairs={{0,8},{8,0},{4,12},{12,4},{1,9},{9,1},{5,13},{13,5},{2,10},{10,2},... | collective-permute-start | bytes 786440 | tf_op jit(solution)/shard_map/ppermute | solution.py:181
  122.3 1.9 %collective-permute-start.36 = (f16[2,2,32,1024]{3,2,0,1:T(8,128)(2,1)S(1)}, f16[2,2,32,1024]{3,2,0,1:T(8,128)(2,1)S(1)}, u32[]{:S(2)}, u32[]{:S(2)}) collective-permute-start(f16[2,2,32,1024]{3,2,0,1:T(8,128)(2,1)S(1)} %fusion.39), channel_id=1, source_target_pairs={{0,4},{4,0},{8,12},{12,8},{1,5},{5,1},{9,13},{13,9},{2,6},{6,2},{1... | collective-permute-start | bytes 786440 | tf_op jit(solution)/shard_map/ppermute | solution.py:180
  125.0 2.6 %collective-permute-start.21 = (f16[2,32,1024]{2,1,0:T(8,128)(2,1)S(1)}, f16[2,32,1024]{2,1,0:T(8,128)(2,1)S(1)}, u32[]{:S(2)}, u32[]{:S(2)}) collective-permute-start(f16[2,32,1024]{2,1,0:T(8,128)(2,1)S(1)} %fusion.51), channel_id=1, source_target_pairs={{0,8},{8,0},{4,12},{12,4},{1,9},{9,1},{5,13},{13,5},{2,10},{10,2},... | collective-permute-start | bytes 393224 | tf_op jit(solution)/shard_map/ppermute | solution.py:184
  127.6 2.0 %collective-permute-done.38 = f16[2,2,32,1024]{3,2,1,0:T(8,128)(2,1)S(1)} collective-permute-done((f16[2,2,32,1024]{3,2,1,0:T(8,128)(2,1)S(1)}, f16[2,2,32,1024]{3,2,1,0:T(8,128)(2,1)S(1)}, u32[]{:S(2)}, u32[]{:S(2)}) %collective-permute-start.38) | collective-permute-done | bytes 262176 | tf_op jit(solution)/shard_map/ppermute | solution.py:181
  129.7 1.8 %collective-permute-start.39 = (f16[2,32,1024]{2,1,0:T(8,128)(2,1)S(1)}, f16[2,32,1024]{2,1,0:T(8,128)(2,1)S(1)}, u32[]{:S(2)}, u32[]{:S(2)}) collective-permute-start(f16[2,32,1024]{2,1,0:T(8,128)(2,1)S(1)} %fusion.56), channel_id=1, source_target_pairs={{0,4},{4,0},{8,12},{12,8},{1,5},{5,1},{9,13},{13,9},{2,6},{6,2},{1... | collective-permute-start | bytes 393224 | tf_op jit(solution)/shard_map/ppermute | solution.py:185
  131.8 1.9 %collective-permute-start.37 = (f16[2,32,1024]{2,1,0:T(8,128)(2,1)S(1)}, f16[2,32,1024]{2,1,0:T(8,128)(2,1)S(1)}, u32[]{:S(2)}, u32[]{:S(2)}) collective-permute-start(f16[2,32,1024]{2,1,0:T(8,128)(2,1)S(1)} %fusion.55), channel_id=1, source_target_pairs={{0,8},{8,0},{4,12},{12,4},{1,9},{9,1},{5,13},{13,5},{2,10},{10,2},... | collective-permute-start | bytes 393224 | tf_op jit(solution)/shard_map/ppermute | solution.py:184
  135.3 1.8 %collective-permute-start.35 = (f16[2,32,1024]{2,1,0:T(8,128)(2,1)S(1)}, f16[2,32,1024]{2,1,0:T(8,128)(2,1)S(1)}, u32[]{:S(2)}, u32[]{:S(2)}) collective-permute-start(f16[2,32,1024]{2,1,0:T(8,128)(2,1)S(1)} %fusion.54), channel_id=1, source_target_pairs={{0,4},{4,0},{8,12},{12,8},{1,5},{5,1},{9,13},{13,9},{2,6},{6,2},{1... | collective-permute-start | bytes 393224 | tf_op jit(solution)/shard_map/ppermute | solution.py:185
  137.4 1.9 %collective-permute-start.33 = (f16[2,32,1024]{2,1,0:T(8,128)(2,1)S(1)}, f16[2,32,1024]{2,1,0:T(8,128)(2,1)S(1)}, u32[]{:S(2)}, u32[]{:S(2)}) collective-permute-start(f16[2,32,1024]{2,1,0:T(8,128)(2,1)S(1)} %fusion.53), channel_id=1, source_target_pairs={{0,8},{8,0},{4,12},{12,4},{1,9},{9,1},{5,13},{13,5},{2,10},{10,2},... | collective-permute-start | bytes 393224 | tf_op jit(solution)/shard_map/ppermute | solution.py:184
  140.5 1.9 %collective-permute-done.33 = f16[2,32,1024]{2,1,0:T(8,128)(2,1)S(1)} collective-permute-done((f16[2,32,1024]{2,1,0:T(8,128)(2,1)S(1)}, f16[2,32,1024]{2,1,0:T(8,128)(2,1)S(1)}, u32[]{:S(2)}, u32[]{:S(2)}) %collective-permute-start.33) | collective-permute-done | bytes 131104 | tf_op jit(solution)/shard_map/ppermute | solution.py:184
  149.5 2.1 %collective-permute-done.46 = f32[4,64]{1,0:T(4,128)S(1)} collective-permute-done((f32[4,64]{1,0:T(4,128)S(1)}, f32[4,64]{1,0:T(4,128)S(1)}, u32[]{:S(2)}, u32[]{:S(2)}) %collective-permute-start.46) | collective-permute-done | bytes 1056 | tf_op jit(solution)/shard_map/ppermute | solution.py:232
  (180 shorter events, 62.0 us)
Async XLA Ops:
  0.6 70.6 %collective-permute-start.15 = (bf16[1024,4096]{1,0:T(8,128)(2,1)}, bf16[1024,4096]{1,0:T(8,128)(2,1)}, u32[]{:S(2)}, u32[]{:S(2)}) collective-permute-start(bf16[1024,4096]{1,0:T(8,128)(2,1)} %weight_ref), channel_id=1, source_target_pairs={{0,16},{16,0},{1,17},{17,1},{2,18},{18,2},{3,19},{19,3},{4,20},{20... | collective-permute-start | bytes 25165832 | tf_op jit(solution)/shard_map/ppermute | solution.py:149
  9.9 14.6 %collective-permute-start.3 = (bf16[2,2,32,1024]{3,2,1,0:T(8,128)(2,1)S(1)}, bf16[2,2,32,1024]{3,2,1,0:T(8,128)(2,1)S(1)}, u32[]{:S(2)}, u32[]{:S(2)}) collective-permute-start(bf16[2,2,32,1024]{3,2,1,0:T(8,128)(2,1)S(1)} %pad_maximum_fusion.4), channel_id=1, source_target_pairs={{0,1},{1,2},{2,3},{4,5},{5,6},{6,7},{8,9},{9,10},{10,11},{12,13},{... | collective-permute-start | bytes 786440 | tf_op jit(solution)/shard_map/ppermute | solution.py:95
  14.1 9.1 %collective-permute-start.2 = (bf16[2,2,32,1024]{3,2,1,0:T(8,128)(2,1)S(1)}, bf16[2,2,32,1024]{3,2,1,0:T(8,128)(2,1)S(1)}, u32[]{:S(2)}, u32[]{:S(2)}) collective-permute-start(bf16[2,2,32,1024]{3,2,1,0:T(8,128)(2,1)S(1)} %pad_maximum_fusion.4), channel_id=1, source_target_pairs={{1,0},{2,1},{3,2},{5,4},{6,5},{7,6},{9,8},{10,9},{11,10},{13,12},{... | collective-permute-start | bytes 786440 | tf_op jit(solution)/shard_map/ppermute | solution.py:98
  15.5 9.7 %collective-permute-start.12 = (bf16[2,2,32,1024]{3,2,1,0:T(8,128)(2,1)S(1)}, bf16[2,2,32,1024]{3,2,1,0:T(8,128)(2,1)S(1)}, u32[]{:S(2)}, u32[]{:S(2)}) collective-permute-start(bf16[2,2,32,1024]{3,2,1,0:T(8,128)(2,1)S(1)} %pad_maximum_fusion.5), channel_id=1, source_target_pairs={{0,1},{1,2},{2,3},{4,5},{5,6},{6,7},{8,9},{9,10},{10,11},{12,13},{... | collective-permute-start | bytes 786440 | tf_op jit(solution)/shard_map/ppermute | solution.py:95
  20.1 11.1 %collective-permute-start.13 = (bf16[2,2,32,1024]{3,2,1,0:T(8,128)(2,1)S(1)}, bf16[2,2,32,1024]{3,2,1,0:T(8,128)(2,1)S(1)}, u32[]{:S(2)}, u32[]{:S(2)}) collective-permute-start(bf16[2,2,32,1024]{3,2,1,0:T(8,128)(2,1)S(1)} %pad_maximum_fusion.5), channel_id=1, source_target_pairs={{1,0},{2,1},{3,2},{5,4},{6,5},{7,6},{9,8},{10,9},{11,10},{13,12},{... | collective-permute-start | bytes 786440 | tf_op jit(solution)/shard_map/ppermute | solution.py:98
  23.2 12.9 %collective-permute-start.5 = (bf16[2,2,32,1024]{3,2,1,0:T(8,128)(2,1)S(1)}, bf16[2,2,32,1024]{3,2,1,0:T(8,128)(2,1)S(1)}, u32[]{:S(2)}, u32[]{:S(2)}) collective-permute-start(bf16[2,2,32,1024]{3,2,1,0:T(8,128)(2,1)S(1)} %collective-permute-done.2), channel_id=1, source_target_pairs={{1,0},{2,1},{5,4},{6,5},{9,8},{10,9},{13,12},{14,13},{17,16},{18,1... | collective-permute-start | bytes 786440 | tf_op jit(solution)/shard_map/ppermute | solution.py:98
  24.5 13.0 %collective-permute-start.8 = (bf16[2,2,32,1024]{3,2,1,0:T(8,128)(2,1)S(1)}, bf16[2,2,32,1024]{3,2,1,0:T(8,128)(2,1)S(1)}, u32[]{:S(2)}, u32[]{:S(2)}) collective-permute-start(bf16[2,2,32,1024]{3,2,1,0:T(8,128)(2,1)S(1)} %collective-permute-done.3), channel_id=1, source_target_pairs={{1,2},{2,3},{5,6},{6,7},{9,10},{10,11},{13,14},{14,15},{17,18},{18... | collective-permute-start | bytes 786440 | tf_op jit(solution)/shard_map/ppermute | solution.py:95
  25.3 13.5 %collective-permute-start.4 = (bf16[2,2,32,1024]{3,2,1,0:T(8,128)(2,1)S(1)}, bf16[2,2,32,1024]{3,2,1,0:T(8,128)(2,1)S(1)}, u32[]{:S(2)}, u32[]{:S(2)}) collective-permute-start(bf16[2,2,32,1024]{3,2,1,0:T(8,128)(2,1)S(1)} %select_select_fusion.6), channel_id=1, source_target_pairs={{0,8},{8,0},{4,12},{12,4},{1,9},{9,1},{5,13},{13,5},{2,10},{10,2},... | collective-permute-start | bytes 786440 | tf_op jit(solution)/shard_map/ppermute | solution.py:111
  31.3 32.6 %collective-permute-start.25 = (bf16[2,2,32,1024]{3,2,1,0:T(8,128)(2,1)S(1)}, bf16[2,2,32,1024]{3,2,1,0:T(8,128)(2,1)}, u32[]{:S(2)}, u32[]{:S(2)}) collective-permute-start(bf16[2,2,32,1024]{3,2,1,0:T(8,128)(2,1)S(1)} %collective-permute-done.13), channel_id=1, source_target_pairs={{1,0},{2,1},{5,4},{6,5},{9,8},{10,9},{13,12},{14,13},{17,16},{18,1... | collective-permute-start | bytes 786440 | tf_op jit(solution)/shard_map/ppermute | solution.py:98
  36.1 27.8 %collective-permute-start.27 = (bf16[2,2,32,1024]{3,2,1,0:T(8,128)(2,1)S(1)}, bf16[2,2,32,1024]{3,2,1,0:T(8,128)(2,1)}, u32[]{:S(2)}, u32[]{:S(2)}) collective-permute-start(bf16[2,2,32,1024]{3,2,1,0:T(8,128)(2,1)S(1)} %collective-permute-done.12), channel_id=1, source_target_pairs={{1,2},{2,3},{5,6},{6,7},{9,10},{10,11},{13,14},{14,15},{17,18},{18... | collective-permute-start | bytes 786440 | tf_op jit(solution)/shard_map/ppermute | solution.py:95
  37.5 8.3 %collective-permute-start.7 = (bf16[2,2,32,1024]{3,2,1,0:T(8,128)(2,1)S(1)}, bf16[2,2,32,1024]{3,2,1,0:T(8,128)(2,1)S(1)}, u32[]{:S(2)}, u32[]{:S(2)}) collective-permute-start(bf16[2,2,32,1024]{3,2,1,0:T(8,128)(2,1)S(1)} %collective-permute-done.5), channel_id=1, source_target_pairs={{1,0},{5,4},{9,8},{13,12},{17,16},{21,20},{25,24},{29,28}} | collective-permute-start | bytes 786440 | tf_op jit(solution)/shard_map/ppermute | solution.py:98
  45.7 8.3 %collective-permute-start.11 = (bf16[2,2,32,1024]{3,2,1,0:T(8,128)(2,1)S(1)}, bf16[2,2,32,1024]{3,2,1,0:T(8,128)(2,1)S(1)}, u32[]{:S(2)}, u32[]{:S(2)}) collective-permute-start(bf16[2,2,32,1024]{3,2,1,0:T(8,128)(2,1)S(1)} %get-tuple-element.69), channel_id=1, source_target_pairs={{1,9},{2,10},{3,11},{5,13},{6,14},{7,15},{8,0},{9,1},{10,2},{12,4}... | collective-permute-start | bytes 786440 | tf_op jit(solution)/shard_map/ppermute | solution.py:117
  47.1 8.4 %collective-permute-start.10 = (bf16[2,2,32,1024]{3,2,1,0:T(8,128)(2,1)S(1)}, bf16[2,2,32,1024]{3,2,1,0:T(8,128)(2,1)S(1)}, u32[]{:S(2)}, u32[]{:S(2)}) collective-permute-start(bf16[2,2,32,1024]{3,2,1,0:T(8,128)(2,1)S(1)} %broadcast_select_fusion.1), channel_id=1, source_target_pairs={{0,8},{4,12},{11,3},{15,7},{16,24},{20,28},{27,19},{31,23}} | collective-permute-start | bytes 786440 | tf_op jit(solution)/shard_map/ppermute | solution.py:120
  56.8 13.0 %collective-permute-start.14 = (bf16[2,2,2,2,32,1024]{5,4,3,2,1,0:T(8,128)(2,1)}, bf16[2,2,2,2,32,1024]{5,4,3,2,1,0:T(8,128)(2,1)S(1)}, u32[]{:S(2)}, u32[]{:S(2)}) collective-permute-start(bf16[2,2,2,2,32,1024]{5,4,3,2,1,0:T(8,128)(2,1)} %pad_maximum_fusion), channel_id=1, source_target_pairs={{0,16},{16,0},{1,17},{17,1},{2,18},{18,2},{3,19},{19,3},{4,20},{20... | collective-permute-start | bytes 3145736 | tf_op jit(solution)/shard_map/ppermute | solution.py:198
  56.8 9.5 %collective-permute-start.24 = (bf16[2,2,32,1024]{3,2,1,0:T(8,128)(2,1)S(1)}, bf16[2,2,32,1024]{3,2,1,0:T(8,128)(2,1)S(1)}, u32[]{:S(2)}, u32[]{:S(2)}) collective-permute-start(bf16[2,2,32,1024]{3,2,1,0:T(8,128)(2,1)S(1)} %select_select_fusion.2), channel_id=1, source_target_pairs={{0,8},{8,0},{4,12},{12,4},{1,9},{9,1},{5,13},{13,5},{2,10},{10,2},... | collective-permute-start | bytes 786440 | tf_op jit(solution)/shard_map/ppermute | solution.py:111
  63.8 13.1 %collective-permute-start.42 = (f32[128]{0:T(128)S(1)}, f32[128]{0:T(128)S(1)}, u32[]{:S(2)}, u32[]{:S(2)}) collective-permute-start(f32[128]{0:T(128)S(1)} %add.186), channel_id=1, source_target_pairs={{0,2},{1,3},{2,0},{3,1},{4,6},{5,7},{6,4},{7,5},{8,10},{9,11},{10,... | collective-permute-start | bytes 1544 | tf_op jit(solution)/shard_map/ppermute | solution.py:72
  67.2 28.3 %collective-permute-start.30 = (bf16[2,2,32,1024]{3,2,1,0:T(8,128)(2,1)}, bf16[2,2,32,1024]{3,2,1,0:T(8,128)(2,1)}, u32[]{:S(2)}, u32[]{:S(2)}) collective-permute-start(bf16[2,2,32,1024]{3,2,1,0:T(8,128)(2,1)} %get-tuple-element.68), channel_id=1, source_target_pairs={{1,9},{2,10},{3,11},{5,13},{6,14},{7,15},{8,0},{9,1},{10,2},{12,4}... | collective-permute-start | bytes 786440 | tf_op jit(solution)/shard_map/ppermute | solution.py:117
  68.4 21.6 %collective-permute-start.26 = (bf16[2,2,32,1024]{3,2,1,0:T(8,128)(2,1)}, bf16[2,2,32,1024]{3,2,1,0:T(8,128)(2,1)}, u32[]{:S(2)}, u32[]{:S(2)}) collective-permute-start(bf16[2,2,32,1024]{3,2,1,0:T(8,128)(2,1)} %collective-permute-done.25), channel_id=1, source_target_pairs={{1,0},{5,4},{9,8},{13,12},{17,16},{21,20},{25,24},{29,28}} | collective-permute-start | bytes 786440 | tf_op jit(solution)/shard_map/ppermute | solution.py:98
  69.9 22.0 %collective-permute-start.28 = (bf16[2,2,32,1024]{3,2,1,0:T(8,128)(2,1)}, bf16[2,2,32,1024]{3,2,1,0:T(8,128)(2,1)}, u32[]{:S(2)}, u32[]{:S(2)}) collective-permute-start(bf16[2,2,32,1024]{3,2,1,0:T(8,128)(2,1)} %collective-permute-done.27), channel_id=1, source_target_pairs={{2,3},{6,7},{10,11},{14,15},{18,19},{22,23},{26,27},{30,31}} | collective-permute-start | bytes 786440 | tf_op jit(solution)/shard_map/ppermute | solution.py:95
  77.0 18.8 %collective-permute-start.43 = (f32[64]{0:T(128)S(1)}, f32[64]{0:T(128)S(1)}, u32[]{:S(2)}, u32[]{:S(2)}) collective-permute-start(f32[64]{0:T(128)S(1)} %get-tuple-element.89), channel_id=1, source_target_pairs={{0,0},{4,8},{8,16},{12,24},{16,4},{20,12},{24,20},{28,28},{1,1},{5... | collective-permute-start | bytes 776 | tf_op jit(solution)/shard_map/ppermute | solution.py:158
  77.7 18.7 %collective-permute-start.44 = (f32[64]{0:T(128)S(1)}, f32[64]{0:T(128)S(1)}, u32[]{:S(2)}, u32[]{:S(2)}) collective-permute-start(f32[64]{0:T(128)S(1)} %get-tuple-element.90), channel_id=1, source_target_pairs={{0,4},{4,12},{8,20},{12,28},{16,0},{20,8},{24,16},{28,24},{1,5},{5... | collective-permute-start | bytes 776 | tf_op jit(solution)/shard_map/ppermute | solution.py:158
  90.1 8.4 %collective-permute-start.22 = (f16[2,2,32,1024]{3,2,0,1:T(8,128)(2,1)S(1)}, f16[2,2,32,1024]{3,2,0,1:T(8,128)(2,1)S(1)}, u32[]{:S(2)}, u32[]{:S(2)}) collective-permute-start(f16[2,2,32,1024]{3,2,0,1:T(8,128)(2,1)S(1)} %fusion.36), channel_id=1, source_target_pairs={{0,8},{8,0},{4,12},{12,4},{1,9},{9,1},{5,13},{13,5},{2,10},{10,2},... | collective-permute-start | bytes 786440 | tf_op jit(solution)/shard_map/ppermute | solution.py:181
  92.8 10.5 %collective-permute-start.29 = (bf16[2,2,32,1024]{3,2,1,0:T(8,128)(2,1)S(1)}, bf16[2,2,32,1024]{3,2,1,0:T(8,128)(2,1)S(1)}, u32[]{:S(2)}, u32[]{:S(2)}) collective-permute-start(bf16[2,2,32,1024]{3,2,1,0:T(8,128)(2,1)S(1)} %broadcast_select_fusion), channel_id=1, source_target_pairs={{0,8},{4,12},{11,3},{15,7},{16,24},{20,28},{27,19},{31,23}} | collective-permute-start | bytes 786440 | tf_op jit(solution)/shard_map/ppermute | solution.py:120
  95.5 10.6 %collective-permute-start.18 = (f16[2,2,32,1024]{3,2,1,0:T(8,128)(2,1)S(1)}, f16[2,2,32,1024]{3,2,1,0:T(8,128)(2,1)S(1)}, u32[]{:S(2)}, u32[]{:S(2)}) collective-permute-start(f16[2,2,32,1024]{3,2,1,0:T(8,128)(2,1)S(1)} %fusion.32), channel_id=1, source_target_pairs={{0,8},{8,0},{4,12},{12,4},{1,9},{9,1},{5,13},{13,5},{2,10},{10,2},... | collective-permute-start | bytes 786440 | tf_op jit(solution)/shard_map/ppermute | solution.py:181
  95.8 12.4 %collective-permute-start.16 = (f16[2,2,32,1024]{3,2,0,1:T(8,128)(2,1)S(1)}, f16[2,2,32,1024]{3,2,0,1:T(8,128)(2,1)S(1)}, u32[]{:S(2)}, u32[]{:S(2)}) collective-permute-start(f16[2,2,32,1024]{3,2,0,1:T(8,128)(2,1)S(1)} %fusion.34), channel_id=1, source_target_pairs={{0,4},{4,0},{8,12},{12,8},{1,5},{5,1},{9,13},{13,9},{2,6},{6,2},{1... | collective-permute-start | bytes 786440 | tf_op jit(solution)/shard_map/ppermute | solution.py:180
  98.6 12.3 %collective-permute-start.23 = (f16[2,32,1024]{2,1,0:T(8,128)(2,1)S(1)}, f16[2,32,1024]{2,1,0:T(8,128)(2,1)S(1)}, u32[]{:S(2)}, u32[]{:S(2)}) collective-permute-start(f16[2,32,1024]{2,1,0:T(8,128)(2,1)S(1)} %fusion.52), channel_id=1, source_target_pairs={{0,4},{4,0},{8,12},{12,8},{1,5},{5,1},{9,13},{13,9},{2,6},{6,2},{1... | collective-permute-start | bytes 393224 | tf_op jit(solution)/shard_map/ppermute | solution.py:185
  120.3 9.3 %collective-permute-start.38 = (f16[2,2,32,1024]{3,2,1,0:T(8,128)(2,1)S(1)}, f16[2,2,32,1024]{3,2,1,0:T(8,128)(2,1)S(1)}, u32[]{:S(2)}, u32[]{:S(2)}) collective-permute-start(f16[2,2,32,1024]{3,2,1,0:T(8,128)(2,1)S(1)} %fusion.33), channel_id=1, source_target_pairs={{0,8},{8,0},{4,12},{12,4},{1,9},{9,1},{5,13},{13,5},{2,10},{10,2},... | collective-permute-start | bytes 786440 | tf_op jit(solution)/shard_map/ppermute | solution.py:181
  122.3 9.3 %collective-permute-start.36 = (f16[2,2,32,1024]{3,2,0,1:T(8,128)(2,1)S(1)}, f16[2,2,32,1024]{3,2,0,1:T(8,128)(2,1)S(1)}, u32[]{:S(2)}, u32[]{:S(2)}) collective-permute-start(f16[2,2,32,1024]{3,2,0,1:T(8,128)(2,1)S(1)} %fusion.39), channel_id=1, source_target_pairs={{0,4},{4,0},{8,12},{12,8},{1,5},{5,1},{9,13},{13,9},{2,6},{6,2},{1... | collective-permute-start | bytes 786440 | tf_op jit(solution)/shard_map/ppermute | solution.py:180
  124.4 10.8 %collective-permute-start.34 = (f16[2,2,32,1024]{3,2,0,1:T(8,128)(2,1)S(1)}, f16[2,2,32,1024]{3,2,0,1:T(8,128)(2,1)S(1)}, u32[]{:S(2)}, u32[]{:S(2)}) collective-permute-start(f16[2,2,32,1024]{3,2,0,1:T(8,128)(2,1)S(1)} %fusion.38), channel_id=1, source_target_pairs={{0,8},{8,0},{4,12},{12,4},{1,9},{9,1},{5,13},{13,5},{2,10},{10,2},... | collective-permute-start | bytes 786440 | tf_op jit(solution)/shard_map/ppermute | solution.py:181
  124.6 12.7 %collective-permute-start.32 = (f16[2,2,32,1024]{3,2,0,1:T(8,128)(2,1)S(1)}, f16[2,2,32,1024]{3,2,0,1:T(8,128)(2,1)S(1)}, u32[]{:S(2)}, u32[]{:S(2)}) collective-permute-start(f16[2,2,32,1024]{3,2,0,1:T(8,128)(2,1)S(1)} %fusion.37), channel_id=1, source_target_pairs={{0,4},{4,0},{8,12},{12,8},{1,5},{5,1},{9,13},{13,9},{2,6},{6,2},{1... | collective-permute-start | bytes 786440 | tf_op jit(solution)/shard_map/ppermute | solution.py:180
  125.0 14.3 %collective-permute-start.21 = (f16[2,32,1024]{2,1,0:T(8,128)(2,1)S(1)}, f16[2,32,1024]{2,1,0:T(8,128)(2,1)S(1)}, u32[]{:S(2)}, u32[]{:S(2)}) collective-permute-start(f16[2,32,1024]{2,1,0:T(8,128)(2,1)S(1)} %fusion.51), channel_id=1, source_target_pairs={{0,8},{8,0},{4,12},{12,4},{1,9},{9,1},{5,13},{13,5},{2,10},{10,2},... | collective-permute-start | bytes 393224 | tf_op jit(solution)/shard_map/ppermute | solution.py:184
  129.7 10.0 %collective-permute-start.39 = (f16[2,32,1024]{2,1,0:T(8,128)(2,1)S(1)}, f16[2,32,1024]{2,1,0:T(8,128)(2,1)S(1)}, u32[]{:S(2)}, u32[]{:S(2)}) collective-permute-start(f16[2,32,1024]{2,1,0:T(8,128)(2,1)S(1)} %fusion.56), channel_id=1, source_target_pairs={{0,4},{4,0},{8,12},{12,8},{1,5},{5,1},{9,13},{13,9},{2,6},{6,2},{1... | collective-permute-start | bytes 393224 | tf_op jit(solution)/shard_map/ppermute | solution.py:185
  (22 other events, 123.1 us)

commit v8 on v7

--- a/solution.py
+++ b/solution.py
@@ -38,7 +38,7 @@
         columns_kernel,
         in_specs=[
             pl.BlockSpec(memory_space=pltpu.SMEM),
-            pl.BlockSpec(memory_space=pl.ANY),
+            pl.BlockSpec(memory_space=pltpu.HBM),
         ],
         out_specs=pl.BlockSpec(memory_space=pltpu.VMEM),
         out_shape=jax.ShapeDtypeStruct((block, columns // 2), weight.dtype),
@@ -71,11 +71,12 @@
     def paired(value, reach):
         return lax.ppermute(value, "vocab", [(i, i ^ reach) for i in range(vocab)])
 
-    squares = jnp.sum(wide * wide, axis=1)
+    near_squares = jnp.sum(wide * wide, axis=1)
     reach = 1
     while 2 * reach < vocab:
-        squares += paired(squares, reach)
+        near_squares += paired(near_squares, reach)
         reach *= 2
+    squares = near_squares + paired(near_squares, reach)
 
     first = level // 2 if vocab == 4 else 0
     pieces = [gained[:, c * step : (c + 1) * step] for c in range(CHUNKS)]
@@ -84,11 +85,11 @@
         sides = [lax.dynamic_slice_in_dim(piece, (1 - x) * block, block, 2) for piece in pieces]
         sides = [lax.ppermute(side, "batch", X_SWAP) for side in sides]
 
-    def line_features(c):
+    def line_features(c, *held):
         mine = lax.dynamic_slice_in_dim(pieces[c], x * block, block, 2)
         other = sides[c]
         own = jnp.stack([jnp.where(x == 0, mine, other), jnp.where(x == 0, other, mine)])
-        own = after(own, squares)
+        own = after(own, near_squares, *held)
         below, above = [own], [own]
         for k in range(1, vocab):
             below.append(
@@ -97,8 +98,16 @@
             above.append(
                 lax.ppermute(above[-1], "vocab", [(z + 1, z) for z in range(vocab - k)])
             )
+            if c == 0 and k == 1:
+                side = after(core, below[1], above[1])
+                weights.append(half_columns(head_weight, side))
+                weights.append(half_columns(take, side))
             if c == 0 and k == 2:
-                below[2], above[2] = after(below[2], *sides), after(above[2], *sides)
+                ready = (*sides, *weights, squares)
+                below[2], above[2] = after(below[2], *ready), after(above[2], *ready)
+            if k == 2:
+                earlier = yield (below[1], above[1]), (below[2], above[2])
+                below[2], above[2] = after(below[2], *earlier), after(above[2], *earlier)
 
         def quarter(place, reach):
             part = own
@@ -113,9 +122,7 @@
         pairs = [(b * vocab + z, (b ^ 2) * vocab + z) for b in range(4) for z in range(vocab)]
         late = [pair for pair in pairs if (pair[0] // vocab // 2, pair[0] % vocab) in ends]
         early = [pair for pair in pairs if pair not in late]
-        earlier = yield below[1], above[1]
-        got_early = after(lax.ppermute(quarter(far, 2), ("batch", "vocab"), early), *earlier)
-        below[-1], above[-1] = after(below[-1], *earlier), after(above[-1], *earlier)
+        got_early = lax.ppermute(quarter(far, 2), ("batch", "vocab"), early)
         last = jnp.where(level == 0, above[-1], below[-1])
         got_late = lax.ppermute(last, ("batch", "vocab"), late)
         is_late = (level == 0) & (y == 1) | (level == vocab - 1) & (y == 0)
@@ -130,80 +137,73 @@
             )
         yield jnp.stack(halves)
 
-    def gathered_features(c):
-        earlier = yield (gained,)
+    def gathered_features(c, *held):
+        if c == 0:
+            weights.append(half_columns(head_weight, core))
+            weights.append(half_columns(take, core))
+        earlier = yield (gained,), (gained,)
         whole = lax.all_gather(pieces[c], "vocab", axis=2, tiled=True)
         whole = whole.reshape(2, step, 2, 4, block).transpose(3, 2, 0, 1, 4)
         whole = lax.all_to_all(whole, "batch", split_axis=0, concat_axis=0)
         whole = whole.reshape(2, 2, 2, 2, step, block).transpose(2, 0, 1, 3, 4, 5)
         yield after(whole, *earlier)
 
+    take = lax.ppermute(head_weight, "pair", CORE_SWAP)
+    weights = []
+
     features = line_features if lined else gathered_features
     own_half = core ^ first if lined else core
-    gathers = [features(c) for c in range(CHUNKS)]
-    begun = [next(gather) for gather in gathers]
-    found = gathers[0].send(())
-    for parts in begun[1:]:
-        found = after(found, *parts)
-
-    take = lax.ppermute(head_weight, "pair", CORE_SWAP)
-    keep = half_columns(after(head_weight, *begun[0]), core)
-    take = half_columns(take, core)
-
-    more_squares = paired(after(squares, *begun[0]), reach)
-
-    def row_scale(*earlier):
-        total = (squares + after(more_squares, *earlier)).reshape(2, seg)
-        sent = [
-            lax.ppermute(
-                pick(total, core ^ k, 0),
-                ("pair", "batch"),
-                [(4 * s + b, 2 * b + (s ^ k)) for s in range(2) for b in range(4)],
-            )
-            for k in range(2)
-        ]
-        total = jnp.stack(
-            [jnp.where(x == 0, sent[0], sent[1]), jnp.where(x == 0, sent[1], sent[0])]
+    gathers = [features(0)]
+    begun = next(gathers[0])[1]
+    for c in range(1, CHUNKS):
+        gathers.append(features(c, *begun))
+        first_step = next(gathers[c])[0]
+    squares = after(squares, *begun).reshape(2, seg)
+    sent = [
+        lax.ppermute(
+            pick(squares, core ^ k, 0),
+            ("pair", "batch"),
+            [(4 * s + b, 2 * b + (s ^ k)) for s in range(2) for b in range(4)],
         )
-        return lax.rsqrt(total / model + EPS) / SHRINK
+        for k in range(2)
+    ]
+    total_sq = jnp.stack([jnp.where(x == 0, sent[0], sent[1]), jnp.where(x == 0, sent[1], sent[0])])
+    scale = lax.rsqrt(total_sq / model + EPS) / SHRINK
+
+    found = after(gathers[0].send(()), scale, *first_step)
+    keep, take = weights
 
     def partial(left):
         out = jnp.dot(pick(left, own_half, 0), keep, preferred_element_type=jnp.float32)
         out += jnp.dot(pick(left, 1 - own_half, 0), take, preferred_element_type=jnp.float32)
         return out * SHRINK
 
-    def reduced(left):
+    def reduced(lefts):
         middle = width // 2
-        parts = partial(left.reshape(2, -1, block))
-        parts = parts.reshape(2, 2, 2, step, width)
-        low, high = parts[..., :middle], parts[..., middle:]
-        away_x = lax.ppermute(pick(low, 1 - x, 2).astype(SUM_TYPE), "batch", X_SWAP)
-        away_y = lax.ppermute(pick(high, 1 - y, 1).astype(SUM_TYPE), "batch", Y_SWAP)
-        sum_x = pick(low, x, 2) + away_x.astype(jnp.float32)
-        sum_y = pick(high, y, 1) + away_y.astype(jnp.float32)
-        next_y = lax.ppermute(pick(sum_x, 1 - y, 1).astype(SUM_TYPE), "batch", Y_SWAP)
-        next_x = lax.ppermute(pick(sum_y, 1 - x, 1).astype(SUM_TYPE), "batch", X_SWAP)
+        parts = [partial(left.reshape(2, -1, block)) for left in lefts]
+        whole = jnp.stack([part.reshape(2, 2, 2, step, width) for part in parts])
+        low, high = whole[..., :middle], whole[..., middle:]
+        away_x = lax.ppermute(pick(low, 1 - x, 3).astype(SUM_TYPE), "batch", X_SWAP)
+        away_y = lax.ppermute(pick(high, 1 - y, 2).astype(SUM_TYPE), "batch", Y_SWAP)
+        sum_x = pick(low, x, 3) + away_x.astype(jnp.float32)
+        sum_y = pick(high, y, 2) + away_y.astype(jnp.float32)
+        next_y = lax.ppermute(pick(sum_x, 1 - y, 2).astype(SUM_TYPE), "batch", Y_SWAP)
+        next_x = lax.ppermute(pick(sum_y, 1 - x, 2).astype(SUM_TYPE), "batch", X_SWAP)
         sums = jnp.concatenate(
             [
-                pick(sum_x, y, 1) + next_y.astype(jnp.float32),
-                pick(sum_y, x, 1) + next_x.astype(jnp.float32),
+                pick(sum_x, y, 2) + next_y.astype(jnp.float32),
+                pick(sum_y, x, 2) + next_x.astype(jnp.float32),
             ],
             axis=-1,
         ).astype(SUM_TYPE)
-        return sums, parts, sum_y
+        return sums, parts, (sum_x, sum_y)
 
     done = []
     for c in range(CHUNKS):
-        found, other = lax.optimization_barrier(
-            (found, lax.ppermute(found, "pair", CORE_SWAP))
-        )
-        own_sums, parts, _ = reduced(found)
-        other_sums, more_parts, halfway = reduced(other)
-        if c == 0:
-            scale = row_scale(more_parts)
+        lefts = lax.optimization_barrier((found, lax.ppermute(found, "pair", CORE_SWAP)))
+        sums, parts, halfway = reduced(lefts)
         if c + 1 < CHUNKS:
-            found = after(gathers[c + 1].send((parts,)), halfway)
-        sums = jnp.stack([own_sums, other_sums])
+            found = after(gathers[c + 1].send(parts), *halfway)
         theirs = lax.ppermute(pick(sums, 1 - core, 1), "pair", CORE_SWAP)
         done.append((pick(sums, core, 1), theirs))
 

time: 156 us -> 163 us (1.045)
  waiting for transfers between devices: 45.2 us -> 57 us
  starting transfers between devices: 71.6 us -> 63.5 us
  matrix products: 14 us -> 17.6 us
  other arithmetic: 13.4 us -> 10.1 us
  local copies, waits for them, and re-layouts: 5.83 us -> 8.89 us
    ppermute x20 -> x12, starting transfers between devices: 32.1 us -> 16.2 us  [the longest x2 5.26 us: reduced(): lax.ppermute(pick(high, 1 - y, 2).astype(SUM_TYPE), 'batch', Y_SWAP)]
    ppermute x20 -> x12, waiting for transfers between devices: 14.1 us -> 24.2 us  [the longest x2 11.1 us: reduced(): lax.ppermute(pick(high, 1 - y, 2).astype(SUM_TYPE), 'batch', Y_SWAP)]
    ppermute x2, waiting for transfers between devices: 5.05 us -> 13.5 us  [line_features(): got_late = lax.ppermute(last, ('batch', 'vocab'), late)]
    ppermute x6, waiting for transfers between devices: 15.9 us -> 11.6 us  [line_features(): lax.ppermute(above[-1], 'vocab', [(z + 1, z) for z in range(vocab - k)])]
    unnamed x13 -> x17, local copies, waits for them, and re-layouts: 4.14 us -> 8.31 us
    dot_general x4, matrix products: 6.4 us -> 10.1 us  [partial(): jnp.dot(pick(left, own_half, 0), keep, preferred_element_type=jnp.float32)]
    ppermute x2, starting transfers between devices: 1.71 us -> 4.22 us  [paired(): return lax.ppermute(value, 'vocab', [(i, i ^ reach) for i in range(vocab)])]
    ppermute x3, waiting for transfers between devices: 4.59 us -> 2.12 us  [on_device(): lax.ppermute(own, 'vocab', [(i, (i + k) % vocab) for i in range(vocab)])]
  transfers between devices with their start and end apart: 48 -> 40, of which waited for: 24 -> 15; matrix products, arithmetic and copies ran while one was open for 14% -> 15% of each run, Pallas kernels for 2% -> 2%
where the time goes in v8:
time: 163 us; the launch traced here: 162 us
  starting transfers between devices  63.5 us (39%)
  waiting for transfers between devices  57 us (35%)
  matrix products  17.6 us (11%)
  other arithmetic  10.1 us (6%)
  local copies, waits for them, and re-layouts  8.89 us (5%)
  Pallas kernels  3.24 us (2%)
    ppermute x6, starting transfers between devices, line_features(): lax.ppermute(below[-1], 'vocab', [(z, z + 1) for z in range(k - 1, vocab...  14.6 us
    ppermute x2, waiting for transfers between devices, line_features(): got_late = lax.ppermute(last, ('batch', 'vocab'), late)  13.5 us
    ppermute x6, waiting for transfers between devices, line_features(): lax.ppermute(above[-1], 'vocab', [(z + 1, z) for z in range(vocab - k)])  11.6 us
    ppermute x2, waiting for transfers between devices, reduced(): lax.ppermute(pick(high, 1 - y, 2).astype(SUM_TYPE), 'batch', Y_SWAP)  11.1 us
    ppermute x2, waiting for transfers between devices, reduced(): lax.ppermute(pick(sum_y, 1 - x, 2).astype(SUM_TYPE), 'batch', X_SWAP)  10.9 us
    dot_general x4, matrix products, partial(): jnp.dot(pick(left, own_half, 0), keep, preferred_element_type=jnp.float32)  10.1 us
    unnamed x17, local copies, waits for them, and re-layouts  8.31 us
    ppermute x6, starting transfers between devices, line_features(): lax.ppermute(above[-1], 'vocab', [(z + 1, z) for z in range(vocab - k)])  7.74 us
  transfers between devices with their start and end apart: 40, of which 15 were waited for; matrix products, arithmetic and copies ran while one was open for 15% of the time, Pallas kernels for 2%

profile of v8, /device:TPU:0, one launch (start us, length us, event | category | flops | bytes accessed | tf_op | source)
XLA Modules:
  0.0 161.9 jit_solution(13843052154565276713)
XLA Ops:
  3.1 2.6 %collective-permute-start = (bf16[2,32,1024]{2,1,0:T(8,128)(2,1)S(1)}, bf16[2,32,1024]{2,1,0:T(8,128)(2,1)S(1)}, u32[]{:S(2)}, u32[]{:S(2)}) collective-permute-start(bf16[2,32,1024]{2,1,0:T(8,128)(2,1)S(1)} %constant_dynamic-slice_fusion.7), channel_id=1, source_target_pairs={{0,4},{4,0},{8,12},{12,8},{1,5},{5,1},{9,13},{13,9},{2,6},{6,2},{1... | collective-permute-start | bytes 393224 | tf_op jit(solution)/shard_map/ppermute | solution.py:86
  5.9 1.6 %collective-permute-start.1 = (f32[128]{0:T(128)S(1)}, f32[128]{0:T(128)S(1)}, u32[]{:S(2)}, u32[]{:S(2)}) collective-permute-start(f32[128]{0:T(128)S(1)} %multiply_reduce_fusion), channel_id=1, source_target_pairs={{0,1},{1,0},{2,3},{3,2},{4,5},{5,4},{6,7},{7,6},{8,9},{9,8},{10,11... | collective-permute-start | bytes 1544 | tf_op jit(solution)/shard_map/ppermute | solution.py:72
  7.5 2.0 %collective-permute-done.1 = f32[128]{0:T(128)S(1)} collective-permute-done((f32[128]{0:T(128)S(1)}, f32[128]{0:T(128)S(1)}, u32[]{:S(2)}, u32[]{:S(2)}) %collective-permute-start.1) | collective-permute-done | bytes 544 | tf_op jit(solution)/shard_map/ppermute | solution.py:72
  11.2 4.6 %collective-permute-start.3 = (bf16[2,2,32,1024]{3,2,1,0:T(8,128)(2,1)S(1)}, bf16[2,2,32,1024]{3,2,1,0:T(8,128)(2,1)S(1)}, u32[]{:S(2)}, u32[]{:S(2)}) collective-permute-start(bf16[2,2,32,1024]{3,2,1,0:T(8,128)(2,1)S(1)} %pad_maximum_fusion.4), channel_id=1, source_target_pairs={{0,1},{1,2},{2,3},{4,5},{5,6},{6,7},{8,9},{9,10},{10,11},{12,13},{... | collective-permute-start | bytes 786440 | tf_op jit(solution)/shard_map/ppermute | solution.py:96
  15.8 1.8 %collective-permute-start.6 = (bf16[2,32,1024]{2,1,0:T(8,128)(2,1)S(1)}, bf16[2,32,1024]{2,1,0:T(8,128)(2,1)S(1)}, u32[]{:S(2)}, u32[]{:S(2)}) collective-permute-start(bf16[2,32,1024]{2,1,0:T(8,128)(2,1)S(1)} %constant_dynamic-slice_fusion.6), channel_id=1, source_target_pairs={{0,4},{4,0},{8,12},{12,8},{1,5},{5,1},{9,13},{13,9},{2,6},{6,2},{1... | collective-permute-start | bytes 393224 | tf_op jit(solution)/shard_map/ppermute | solution.py:86
  17.6 2.6 %collective-permute-start.8 = (f32[128]{0:T(128)S(1)}, f32[128]{0:T(128)S(1)}, u32[]{:S(2)}, u32[]{:S(2)}) collective-permute-start(f32[128]{0:T(128)S(1)} %add.146), channel_id=1, source_target_pairs={{0,2},{1,3},{2,0},{3,1},{4,6},{5,7},{6,4},{7,5},{8,10},{9,11},{10,... | collective-permute-start | bytes 1544 | tf_op jit(solution)/shard_map/ppermute | solution.py:72
  20.2 1.9 %collective-permute-done.8 = f32[128]{0:T(128)S(1)} collective-permute-done((f32[128]{0:T(128)S(1)}, f32[128]{0:T(128)S(1)}, u32[]{:S(2)}, u32[]{:S(2)}) %collective-permute-start.8) | collective-permute-done | bytes 544 | tf_op jit(solution)/shard_map/ppermute | solution.py:72
  25.8 3.4 %copy-done = bf16[1024,4096]{1,0:T(8,128)(2,1)S(1)} copy-done((bf16[1024,4096]{1,0:T(8,128)(2,1)S(1)}, bf16[1024,4096]{1,0:T(8,128)(2,1)}, u32[]{:S(2)}) %copy-start) | copy-done | bytes 8388632
  30.2 2.0 %copy-done.1 = bf16[1024,2048]{1,0:T(8,128)(2,1)} copy-done((bf16[1024,2048]{1,0:T(8,128)(2,1)}, bf16[1024,2048]{1,0:T(8,128)(2,1)S(1)}, u32[]{:S(2)}) %copy-start.1) | copy-done | bytes 4194328
  32.3 2.2 %shard_map.51 = bf16[1024,2048]{1,0:T(8,128)(2,1)S(1)} custom-call(s32[1]{0:T(128)} %bitcast.6.start_ref, bf16[1024,4096]{1,0:T(8,128)(2,1)} %collective-permute-done.7.weight_ref), custom_call_target="tpu_custom_call" | custom-call | bytes 8388608 | tf_op jit(solution)/shard_map/pallas_call | solution.py:37
  34.5 1.9 %copy-done.4 = bf16[1024,2048]{1,0:T(8,128)(2,1)} copy-done((bf16[1024,2048]{1,0:T(8,128)(2,1)}, bf16[1024,2048]{1,0:T(8,128)(2,1)S(1)}, u32[]{:S(2)}) %copy-start.4) | copy-done | bytes 4194328
  36.4 7.4 %collective-permute-start.16 = (bf16[2,2,32,1024]{3,2,1,0:T(8,128)(2,1)S(1)}, bf16[2,2,32,1024]{3,2,1,0:T(8,128)(2,1)S(1)}, u32[]{:S(2)}, u32[]{:S(2)}) collective-permute-start(bf16[2,2,32,1024]{3,2,1,0:T(8,128)(2,1)S(1)} %pad_maximum_fusion.5), channel_id=1, source_target_pairs={{0,1},{1,2},{2,3},{4,5},{5,6},{6,7},{8,9},{9,10},{10,11},{12,13},{... | collective-permute-start | bytes 786440 | tf_op jit(solution)/shard_map/ppermute | solution.py:96
  49.4 7.4 %collective-permute-done.9 = bf16[2,2,32,1024]{3,2,1,0:T(8,128)(2,1)S(1)} collective-permute-done((bf16[2,2,32,1024]{3,2,1,0:T(8,128)(2,1)S(1)}, bf16[2,2,32,1024]{3,2,1,0:T(8,128)(2,1)S(1)}, u32[]{:S(2)}, u32[]{:S(2)}) %collective-permute-start.9) | collective-permute-done | bytes 262176 | tf_op jit(solution)/shard_map/ppermute | solution.py:99
  57.5 3.4 %collective-permute-start.15 = (f32[64]{0:T(128)S(1)}, f32[64]{0:T(128)S(1)}, u32[]{:S(2)}, u32[]{:S(2)}) collective-permute-start(f32[64]{0:T(128)S(1)} %get-tuple-element.70), channel_id=1, source_target_pairs={{0,4},{4,12},{8,20},{12,28},{16,0},{20,8},{24,16},{28,24},{1,5},{5... | collective-permute-start | bytes 776 | tf_op jit(solution)/shard_map/ppermute | solution.py:163
  60.9 4.8 %collective-permute-start.12 = (bf16[2,2,32,1024]{3,2,1,0:T(8,128)(2,1)S(1)}, bf16[2,2,32,1024]{3,2,1,0:T(8,128)(2,1)S(1)}, u32[]{:S(2)}, u32[]{:S(2)}) collective-permute-start(bf16[2,2,32,1024]{3,2,1,0:T(8,128)(2,1)S(1)} %broadcast_select_fusion.1), channel_id=1, source_target_pairs={{0,8},{4,12},{11,3},{15,7},{16,24},{20,28},{27,19},{31,23}} | collective-permute-start | bytes 786440 | tf_op jit(solution)/shard_map/ppermute | solution.py:127
  65.7 4.0 %collective-permute-done.12 = bf16[2,2,32,1024]{3,2,1,0:T(8,128)(2,1)S(1)} collective-permute-done((bf16[2,2,32,1024]{3,2,1,0:T(8,128)(2,1)S(1)}, bf16[2,2,32,1024]{3,2,1,0:T(8,128)(2,1)S(1)}, u32[]{:S(2)}, u32[]{:S(2)}) %collective-permute-start.12) | collective-permute-done | bytes 262176 | tf_op jit(solution)/shard_map/ppermute | solution.py:127
  70.3 2.5 %collective-permute-start.23 = (bf16[2,2,32,1024]{3,2,1,0:T(8,128)(2,1)S(1)}, bf16[2,2,32,1024]{3,2,1,0:T(8,128)(2,1)S(1)}, u32[]{:S(2)}, u32[]{:S(2)}) collective-permute-start(bf16[2,2,32,1024]{3,2,1,0:T(8,128)(2,1)S(1)} %select_select_fusion.2), channel_id=1, source_target_pairs={{0,8},{8,0},{4,12},{12,4},{1,9},{9,1},{5,13},{13,5},{2,10},{10,2},... | collective-permute-start | bytes 786440 | tf_op jit(solution)/shard_map/ppermute | solution.py:120
  74.9 3.7 %fusion.35 = f32[256,2048]{1,0:T(8,128)S(1)} fusion(bf16[1024,2048]{1,0:T(8,128)(2,1)} %copy-done.1, bf16[2,256,1024]{2,1,0:T(8,128)(2,1)} %bitcast.20, s32[]{:T(128)S(6)} %select_n.389), kind=kOutput, calls=%fused_computation.82 | convolution fusion | flops 1073741824 | bytes 6815748 | tf_op jit(solution)/shard_map/dot_general | solution.py:177
  80.8 2.4 %fusion.2 = f32[256,2048]{1,0:T(8,128)S(1)} fusion(f32[256,2048]{1,0:T(8,128)S(1)} %fusion.35, bf16[1024,2048]{1,0:T(8,128)(2,1)S(1)} %copy-done.5, bf16[2,256,1024]{2,1,0:T(8,128)(2,1)} %bitcast.20, s32[]{:T(128)S(6)} %select_n.390), kind=kOutput, calls=%fused_computation.9 | convolution fusion | flops 1074790400 | bytes 8912900 | tf_op jit(solution)/shard_map/dot_general | solution.py:178
  88.2 2.7 %collective-permute-start.21 = (f16[2,2,2,32,1024]{4,3,2,1,0:T(8,128)(2,1)S(1)}, f16[2,2,2,32,1024]{4,3,2,1,0:T(8,128)(2,1)S(1)}, u32[]{:S(2)}, u32[]{:S(2)}) collective-permute-start(f16[2,2,2,32,1024]{4,3,2,1,0:T(8,128)(2,1)S(1)} %fusion.23), channel_id=1, source_target_pairs={{0,8},{8,0},{4,12},{12,4},{1,9},{9,1},{5,13},{13,5},{2,10},{10,2},... | collective-permute-start | bytes 1572872 | tf_op jit(solution)/shard_map/ppermute | solution.py:187
  91.3 4.2 %collective-permute-done.25 = bf16[2,2,32,1024]{3,2,1,0:T(8,128)(2,1)S(1)} collective-permute-done((bf16[2,2,32,1024]{3,2,1,0:T(8,128)(2,1)S(1)}, bf16[2,2,32,1024]{3,2,1,0:T(8,128)(2,1)S(1)}, u32[]{:S(2)}, u32[]{:S(2)}) %collective-permute-start.25) | collective-permute-done | bytes 262176 | tf_op jit(solution)/shard_map/ppermute | solution.py:99
  95.5 2.7 %collective-permute-start.28 = (bf16[2,2,32,1024]{3,2,1,0:T(8,128)(2,1)S(1)}, bf16[2,2,32,1024]{3,2,1,0:T(8,128)(2,1)S(1)}, u32[]{:S(2)}, u32[]{:S(2)}) collective-permute-start(bf16[2,2,32,1024]{3,2,1,0:T(8,128)(2,1)S(1)} %broadcast_select_fusion), channel_id=1, source_target_pairs={{0,8},{4,12},{11,3},{15,7},{16,24},{20,28},{27,19},{31,23}} | collective-permute-start | bytes 786440 | tf_op jit(solution)/shard_map/ppermute | solution.py:127
  98.3 9.5 %collective-permute-done.28 = bf16[2,2,32,1024]{3,2,1,0:T(8,128)(2,1)S(1)} collective-permute-done((bf16[2,2,32,1024]{3,2,1,0:T(8,128)(2,1)S(1)}, bf16[2,2,32,1024]{3,2,1,0:T(8,128)(2,1)S(1)}, u32[]{:S(2)}, u32[]{:S(2)}) %collective-permute-start.28) | collective-permute-done | bytes 262176 | tf_op jit(solution)/shard_map/ppermute | solution.py:127
  109.4 2.5 %collective-permute-start.20 = (f16[2,2,32,1024]{3,2,1,0:T(8,128)(2,1)S(1)}, f16[2,2,32,1024]{3,2,1,0:T(8,128)(2,1)S(1)}, u32[]{:S(2)}, u32[]{:S(2)}) collective-permute-start(f16[2,2,32,1024]{3,2,1,0:T(8,128)(2,1)S(1)} %fusion.48), channel_id=1, source_target_pairs={{0,8},{8,0},{4,12},{12,4},{1,9},{9,1},{5,13},{13,5},{2,10},{10,2},... | collective-permute-start | bytes 786440 | tf_op jit(solution)/shard_map/ppermute | solution.py:190
  112.0 6.3 %collective-permute-done.22 = f16[2,2,32,1024]{3,2,1,0:T(8,128)(2,1)S(1)} collective-permute-done((f16[2,2,32,1024]{3,2,1,0:T(8,128)(2,1)}, f16[2,2,32,1024]{3,2,1,0:T(8,128)(2,1)S(1)}, u32[]{:S(2)}, u32[]{:S(2)}) %collective-permute-start.22) | collective-permute-done | bytes 262176 | tf_op jit(solution)/shard_map/ppermute | solution.py:191
  118.4 3.7 %fusion.27 = f32[256,2048]{1,0:T(8,128)S(1)} fusion(bf16[1024,2048]{1,0:T(8,128)(2,1)} %copy-done.1, bf16[2,256,1024]{2,1,0:T(8,128)(2,1)} %bitcast.43, s32[]{:T(128)S(6)} %select_n.389), kind=kOutput, calls=%fused_computation.72 | convolution fusion | flops 1073741824 | bytes 6815748 | tf_op jit(solution)/shard_map/dot_general | solution.py:177
  122.2 2.5 %fusion = f32[256,2048]{1,0:T(8,128)S(1)} fusion(f32[256,2048]{1,0:T(8,128)S(1)} %fusion.27, bf16[1024,2048]{1,0:T(8,128)(2,1)S(1)} %copy-done.6, bf16[2,256,1024]{2,1,0:T(8,128)(2,1)} %bitcast.43, s32[]{:T(128)S(6)} %select_n.390), kind=kOutput, calls=%fused_computation.5 | convolution fusion | flops 1074790400 | bytes 8912900 | tf_op jit(solution)/shard_map/dot_general | solution.py:178
  127.6 2.5 %collective-permute-start.33 = (f16[2,2,2,32,1024]{4,3,2,1,0:T(8,128)(2,1)S(1)}, f16[2,2,2,32,1024]{4,3,2,1,0:T(8,128)(2,1)S(1)}, u32[]{:S(2)}, u32[]{:S(2)}) collective-permute-start(f16[2,2,2,32,1024]{4,3,2,1,0:T(8,128)(2,1)S(1)} %fusion.22), channel_id=1, source_target_pairs={{0,8},{8,0},{4,12},{12,4},{1,9},{9,1},{5,13},{13,5},{2,10},{10,2},... | collective-permute-start | bytes 1572872 | tf_op jit(solution)/shard_map/ppermute | solution.py:187
  130.9 11.1 %collective-permute-done.33 = f16[2,2,2,32,1024]{4,3,2,1,0:T(8,128)(2,1)S(1)} collective-permute-done((f16[2,2,2,32,1024]{4,3,2,1,0:T(8,128)(2,1)S(1)}, f16[2,2,2,32,1024]{4,3,2,1,0:T(8,128)(2,1)S(1)}, u32[]{:S(2)}, u32[]{:S(2)}) %collective-permute-start.33) | collective-permute-done | bytes 524320 | tf_op jit(solution)/shard_map/ppermute | solution.py:187
  145.0 4.6 %collective-permute-done.34 = f16[2,2,32,1024]{3,2,1,0:T(8,128)(2,1)S(1)} collective-permute-done((f16[2,2,32,1024]{3,2,1,0:T(8,128)(2,1)S(1)}, f16[2,2,32,1024]{3,2,1,0:T(8,128)(2,1)S(1)}, u32[]{:S(2)}, u32[]{:S(2)}) %collective-permute-start.34) | collective-permute-done | bytes 262176 | tf_op jit(solution)/shard_map/ppermute | solution.py:191
  155.1 3.0 %collective-permute-start.39 = (f32[4,64]{1,0:T(4,128)S(1)}, f32[4,64]{1,0:T(4,128)S(1)}, u32[]{:S(2)}, u32[]{:S(2)}) collective-permute-start(f32[4,64]{1,0:T(4,128)S(1)} %get-tuple-element.62), channel_id=1, source_target_pairs={{0,3},{1,0},{2,1},{3,2},{4,7},{5,4},{6,5},{7,6},{8,11},{9,8},{10,9... | collective-permute-start | bytes 3080 | tf_op jit(solution)/shard_map/ppermute | solution.py:232
  160.3 1.6 fusion.18
  (144 shorter events, 41.0 us)
Async XLA Ops:
  0.6 31.6 %collective-permute-start.7 = (bf16[1024,4096]{1,0:T(8,128)(2,1)}, bf16[1024,4096]{1,0:T(8,128)(2,1)}, u32[]{:S(2)}, u32[]{:S(2)}) collective-permute-start(bf16[1024,4096]{1,0:T(8,128)(2,1)} %weight_ref.1), channel_id=1, source_target_pairs={{0,16},{16,0},{1,17},{17,1},{2,18},{18,2},{3,19},{19,3},{4,20},{20... | collective-permute-start | bytes 25165832 | tf_op jit(solution)/shard_map/ppermute | solution.py:151
  3.1 6.7 %collective-permute-start = (bf16[2,32,1024]{2,1,0:T(8,128)(2,1)S(1)}, bf16[2,32,1024]{2,1,0:T(8,128)(2,1)S(1)}, u32[]{:S(2)}, u32[]{:S(2)}) collective-permute-start(bf16[2,32,1024]{2,1,0:T(8,128)(2,1)S(1)} %constant_dynamic-slice_fusion.7), channel_id=1, source_target_pairs={{0,4},{4,0},{8,12},{12,8},{1,5},{5,1},{9,13},{13,9},{2,6},{6,2},{1... | collective-permute-start | bytes 393224 | tf_op jit(solution)/shard_map/ppermute | solution.py:86
  9.9 12.2 %collective-permute-start.2 = (bf16[2,2,32,1024]{3,2,1,0:T(8,128)(2,1)S(1)}, bf16[2,2,32,1024]{3,2,1,0:T(8,128)(2,1)S(1)}, u32[]{:S(2)}, u32[]{:S(2)}) collective-permute-start(bf16[2,2,32,1024]{3,2,1,0:T(8,128)(2,1)S(1)} %pad_maximum_fusion.4), channel_id=1, source_target_pairs={{1,0},{2,1},{3,2},{5,4},{6,5},{7,6},{9,8},{10,9},{11,10},{13,12},{... | collective-permute-start | bytes 786440 | tf_op jit(solution)/shard_map/ppermute | solution.py:99
  11.2 10.9 %collective-permute-start.3 = (bf16[2,2,32,1024]{3,2,1,0:T(8,128)(2,1)S(1)}, bf16[2,2,32,1024]{3,2,1,0:T(8,128)(2,1)S(1)}, u32[]{:S(2)}, u32[]{:S(2)}) collective-permute-start(bf16[2,2,32,1024]{3,2,1,0:T(8,128)(2,1)S(1)} %pad_maximum_fusion.4), channel_id=1, source_target_pairs={{0,1},{1,2},{2,3},{4,5},{5,6},{6,7},{8,9},{9,10},{10,11},{12,13},{... | collective-permute-start | bytes 786440 | tf_op jit(solution)/shard_map/ppermute | solution.py:96
  15.8 9.9 %collective-permute-start.6 = (bf16[2,32,1024]{2,1,0:T(8,128)(2,1)S(1)}, bf16[2,32,1024]{2,1,0:T(8,128)(2,1)S(1)}, u32[]{:S(2)}, u32[]{:S(2)}) collective-permute-start(bf16[2,32,1024]{2,1,0:T(8,128)(2,1)S(1)} %constant_dynamic-slice_fusion.6), channel_id=1, source_target_pairs={{0,4},{4,0},{8,12},{12,8},{1,5},{5,1},{9,13},{13,9},{2,6},{6,2},{1... | collective-permute-start | bytes 393224 | tf_op jit(solution)/shard_map/ppermute | solution.py:86
  22.1 25.0 %collective-permute-start.4 = (bf16[2,2,32,1024]{3,2,1,0:T(8,128)(2,1)S(1)}, bf16[2,2,32,1024]{3,2,1,0:T(8,128)(2,1)S(1)}, u32[]{:S(2)}, u32[]{:S(2)}) collective-permute-start(bf16[2,2,32,1024]{3,2,1,0:T(8,128)(2,1)S(1)} %select_select_fusion.6), channel_id=1, source_target_pairs={{0,8},{8,0},{4,12},{12,4},{1,9},{9,1},{5,13},{13,5},{2,10},{10,2},... | collective-permute-start | bytes 786440 | tf_op jit(solution)/shard_map/ppermute | solution.py:120
  23.7 12.7 %collective-permute-start.5 = (bf16[2,2,32,1024]{3,2,1,0:T(8,128)(2,1)S(1)}, bf16[2,2,32,1024]{3,2,1,0:T(8,128)(2,1)S(1)}, u32[]{:S(2)}, u32[]{:S(2)}) collective-permute-start(bf16[2,2,32,1024]{3,2,1,0:T(8,128)(2,1)S(1)} %collective-permute-done.2), channel_id=1, source_target_pairs={{1,0},{2,1},{5,4},{6,5},{9,8},{10,9},{13,12},{14,13},{17,16},{18,1... | collective-permute-start | bytes 786440 | tf_op jit(solution)/shard_map/ppermute | solution.py:99
  25.0 11.5 %collective-permute-start.10 = (bf16[2,2,32,1024]{3,2,1,0:T(8,128)(2,1)S(1)}, bf16[2,2,32,1024]{3,2,1,0:T(8,128)(2,1)S(1)}, u32[]{:S(2)}, u32[]{:S(2)}) collective-permute-start(bf16[2,2,32,1024]{3,2,1,0:T(8,128)(2,1)S(1)} %collective-permute-done.3), channel_id=1, source_target_pairs={{1,2},{2,3},{5,6},{6,7},{9,10},{10,11},{13,14},{14,15},{17,18},{18... | collective-permute-start | bytes 786440 | tf_op jit(solution)/shard_map/ppermute | solution.py:96
  36.4 33.7 %collective-permute-start.16 = (bf16[2,2,32,1024]{3,2,1,0:T(8,128)(2,1)S(1)}, bf16[2,2,32,1024]{3,2,1,0:T(8,128)(2,1)S(1)}, u32[]{:S(2)}, u32[]{:S(2)}) collective-permute-start(bf16[2,2,32,1024]{3,2,1,0:T(8,128)(2,1)S(1)} %pad_maximum_fusion.5), channel_id=1, source_target_pairs={{0,1},{1,2},{2,3},{4,5},{5,6},{6,7},{8,9},{9,10},{10,11},{12,13},{... | collective-permute-start | bytes 786440 | tf_op jit(solution)/shard_map/ppermute | solution.py:96
  43.8 26.3 %collective-permute-start.17 = (bf16[2,2,32,1024]{3,2,1,0:T(8,128)(2,1)S(1)}, bf16[2,2,32,1024]{3,2,1,0:T(8,128)(2,1)S(1)}, u32[]{:S(2)}, u32[]{:S(2)}) collective-permute-start(bf16[2,2,32,1024]{3,2,1,0:T(8,128)(2,1)S(1)} %pad_maximum_fusion.5), channel_id=1, source_target_pairs={{1,0},{2,1},{3,2},{5,4},{6,5},{7,6},{9,8},{10,9},{11,10},{13,12},{... | collective-permute-start | bytes 786440 | tf_op jit(solution)/shard_map/ppermute | solution.py:99
  45.1 11.7 %collective-permute-start.9 = (bf16[2,2,32,1024]{3,2,1,0:T(8,128)(2,1)S(1)}, bf16[2,2,32,1024]{3,2,1,0:T(8,128)(2,1)S(1)}, u32[]{:S(2)}, u32[]{:S(2)}) collective-permute-start(bf16[2,2,32,1024]{3,2,1,0:T(8,128)(2,1)S(1)} %collective-permute-done.5), channel_id=1, source_target_pairs={{1,0},{5,4},{9,8},{13,12},{17,16},{21,20},{25,24},{29,28}} | collective-permute-start | bytes 786440 | tf_op jit(solution)/shard_map/ppermute | solution.py:99
  46.4 11.1 %collective-permute-start.11 = (bf16[2,2,32,1024]{3,2,1,0:T(8,128)(2,1)S(1)}, bf16[2,2,32,1024]{3,2,1,0:T(8,128)(2,1)S(1)}, u32[]{:S(2)}, u32[]{:S(2)}) collective-permute-start(bf16[2,2,32,1024]{3,2,1,0:T(8,128)(2,1)S(1)} %collective-permute-done.10), channel_id=1, source_target_pairs={{2,3},{6,7},{10,11},{14,15},{18,19},{22,23},{26,27},{30,31}} | collective-permute-start | bytes 786440 | tf_op jit(solution)/shard_map/ppermute | solution.py:96
  47.9 17.8 %collective-permute-start.13 = (bf16[2,2,32,1024]{3,2,1,0:T(8,128)(2,1)}, bf16[2,2,32,1024]{3,2,1,0:T(8,128)(2,1)S(1)}, u32[]{:S(2)}, u32[]{:S(2)}) collective-permute-start(bf16[2,2,32,1024]{3,2,1,0:T(8,128)(2,1)} %get-tuple-element.49), channel_id=1, source_target_pairs={{1,9},{2,10},{3,11},{5,13},{6,14},{7,15},{8,0},{9,1},{10,2},{12,4}... | collective-permute-start | bytes 786440 | tf_op jit(solution)/shard_map/ppermute | solution.py:125
  57.5 8.2 %collective-permute-start.15 = (f32[64]{0:T(128)S(1)}, f32[64]{0:T(128)S(1)}, u32[]{:S(2)}, u32[]{:S(2)}) collective-permute-start(f32[64]{0:T(128)S(1)} %get-tuple-element.70), channel_id=1, source_target_pairs={{0,4},{4,12},{8,20},{12,28},{16,0},{20,8},{24,16},{28,24},{1,5},{5... | collective-permute-start | bytes 776 | tf_op jit(solution)/shard_map/ppermute | solution.py:163
  60.9 8.9 %collective-permute-start.12 = (bf16[2,2,32,1024]{3,2,1,0:T(8,128)(2,1)S(1)}, bf16[2,2,32,1024]{3,2,1,0:T(8,128)(2,1)S(1)}, u32[]{:S(2)}, u32[]{:S(2)}) collective-permute-start(bf16[2,2,32,1024]{3,2,1,0:T(8,128)(2,1)S(1)} %broadcast_select_fusion.1), channel_id=1, source_target_pairs={{0,8},{4,12},{11,3},{15,7},{16,24},{20,28},{27,19},{31,23}} | collective-permute-start | bytes 786440 | tf_op jit(solution)/shard_map/ppermute | solution.py:127
  70.3 16.2 %collective-permute-start.23 = (bf16[2,2,32,1024]{3,2,1,0:T(8,128)(2,1)S(1)}, bf16[2,2,32,1024]{3,2,1,0:T(8,128)(2,1)S(1)}, u32[]{:S(2)}, u32[]{:S(2)}) collective-permute-start(bf16[2,2,32,1024]{3,2,1,0:T(8,128)(2,1)S(1)} %select_select_fusion.2), channel_id=1, source_target_pairs={{0,8},{8,0},{4,12},{12,4},{1,9},{9,1},{5,13},{13,5},{2,10},{10,2},... | collective-permute-start | bytes 786440 | tf_op jit(solution)/shard_map/ppermute | solution.py:120
  72.9 11.6 %collective-permute-start.26 = (bf16[2,2,32,1024]{3,2,1,0:T(8,128)(2,1)S(1)}, bf16[2,2,32,1024]{3,2,1,0:T(8,128)(2,1)S(1)}, u32[]{:S(2)}, u32[]{:S(2)}) collective-permute-start(bf16[2,2,32,1024]{3,2,1,0:T(8,128)(2,1)S(1)} %collective-permute-done.16), channel_id=1, source_target_pairs={{1,2},{2,3},{5,6},{6,7},{9,10},{10,11},{13,14},{14,15},{17,18},{18... | collective-permute-start | bytes 786440 | tf_op jit(solution)/shard_map/ppermute | solution.py:96
  73.5 11.0 %collective-permute-start.24 = (bf16[2,2,32,1024]{3,2,1,0:T(8,128)(2,1)S(1)}, bf16[2,2,32,1024]{3,2,1,0:T(8,128)(2,1)S(1)}, u32[]{:S(2)}, u32[]{:S(2)}) collective-permute-start(bf16[2,2,32,1024]{3,2,1,0:T(8,128)(2,1)S(1)} %collective-permute-done.17), channel_id=1, source_target_pairs={{1,0},{2,1},{5,4},{6,5},{9,8},{10,9},{13,12},{14,13},{17,16},{18,1... | collective-permute-start | bytes 786440 | tf_op jit(solution)/shard_map/ppermute | solution.py:99
  84.5 6.8 %collective-permute-start.27 = (bf16[2,2,32,1024]{3,2,1,0:T(8,128)(2,1)S(1)}, bf16[2,2,32,1024]{3,2,1,0:T(8,128)(2,1)S(1)}, u32[]{:S(2)}, u32[]{:S(2)}) collective-permute-start(bf16[2,2,32,1024]{3,2,1,0:T(8,128)(2,1)S(1)} %collective-permute-done.26), channel_id=1, source_target_pairs={{2,3},{6,7},{10,11},{14,15},{18,19},{22,23},{26,27},{30,31}} | collective-permute-start | bytes 786440 | tf_op jit(solution)/shard_map/ppermute | solution.py:96
  85.2 10.3 %collective-permute-start.25 = (bf16[2,2,32,1024]{3,2,1,0:T(8,128)(2,1)S(1)}, bf16[2,2,32,1024]{3,2,1,0:T(8,128)(2,1)S(1)}, u32[]{:S(2)}, u32[]{:S(2)}) collective-permute-start(bf16[2,2,32,1024]{3,2,1,0:T(8,128)(2,1)S(1)} %collective-permute-done.24), channel_id=1, source_target_pairs={{1,0},{5,4},{9,8},{13,12},{17,16},{21,20},{25,24},{29,28}} | collective-permute-start | bytes 786440 | tf_op jit(solution)/shard_map/ppermute | solution.py:99
  86.6 11.7 %collective-permute-start.29 = (bf16[2,2,32,1024]{3,2,1,0:T(8,128)(2,1)S(1)}, bf16[2,2,32,1024]{3,2,1,0:T(8,128)(2,1)S(1)}, u32[]{:S(2)}, u32[]{:S(2)}) collective-permute-start(bf16[2,2,32,1024]{3,2,1,0:T(8,128)(2,1)S(1)} %get-tuple-element.48), channel_id=1, source_target_pairs={{1,9},{2,10},{3,11},{5,13},{6,14},{7,15},{8,0},{9,1},{10,2},{12,4}... | collective-permute-start | bytes 786440 | tf_op jit(solution)/shard_map/ppermute | solution.py:125
  88.2 20.0 %collective-permute-start.21 = (f16[2,2,2,32,1024]{4,3,2,1,0:T(8,128)(2,1)S(1)}, f16[2,2,2,32,1024]{4,3,2,1,0:T(8,128)(2,1)S(1)}, u32[]{:S(2)}, u32[]{:S(2)}) collective-permute-start(f16[2,2,2,32,1024]{4,3,2,1,0:T(8,128)(2,1)S(1)} %fusion.23), channel_id=1, source_target_pairs={{0,8},{8,0},{4,12},{12,4},{1,9},{9,1},{5,13},{13,5},{2,10},{10,2},... | collective-permute-start | bytes 1572872 | tf_op jit(solution)/shard_map/ppermute | solution.py:187
  91.2 17.2 %collective-permute-start.19 = (f16[2,2,2,32,1024]{4,3,1,0,2:T(8,128)(2,1)S(1)}, f16[2,2,2,32,1024]{4,3,1,0,2:T(8,128)(2,1)S(1)}, u32[]{:S(2)}, u32[]{:S(2)}) collective-permute-start(f16[2,2,2,32,1024]{4,3,1,0,2:T(8,128)(2,1)S(1)} %fusion.20), channel_id=1, source_target_pairs={{0,4},{4,0},{8,12},{12,8},{1,5},{5,1},{9,13},{13,9},{2,6},{6,2},{1... | collective-permute-start | bytes 1572872 | tf_op jit(solution)/shard_map/ppermute | solution.py:186
  95.5 12.3 %collective-permute-start.28 = (bf16[2,2,32,1024]{3,2,1,0:T(8,128)(2,1)S(1)}, bf16[2,2,32,1024]{3,2,1,0:T(8,128)(2,1)S(1)}, u32[]{:S(2)}, u32[]{:S(2)}) collective-permute-start(bf16[2,2,32,1024]{3,2,1,0:T(8,128)(2,1)S(1)} %broadcast_select_fusion), channel_id=1, source_target_pairs={{0,8},{4,12},{11,3},{15,7},{16,24},{20,28},{27,19},{31,23}} | collective-permute-start | bytes 786440 | tf_op jit(solution)/shard_map/ppermute | solution.py:127
  108.6 9.8 %collective-permute-start.30 = (bf16[2,2,2,2,32,1024]{5,4,3,2,1,0:T(8,128)(2,1)S(1)}, bf16[2,2,2,2,32,1024]{5,4,3,2,1,0:T(8,128)(2,1)}, u32[]{:S(2)}, u32[]{:S(2)}) collective-permute-start(bf16[2,2,2,2,32,1024]{5,4,3,2,1,0:T(8,128)(2,1)S(1)} %pad_maximum_fusion.1), channel_id=1, source_target_pairs={{0,16},{16,0},{1,17},{17,1},{2,18},{18,2},{3,19},{19,3},{4,20},{20... | collective-permute-start | bytes 3145736 | tf_op jit(solution)/shard_map/ppermute | solution.py:203
  109.4 8.9 %collective-permute-start.22 = (f16[2,2,32,1024]{3,2,1,0:T(8,128)(2,1)}, f16[2,2,32,1024]{3,2,1,0:T(8,128)(2,1)S(1)}, u32[]{:S(2)}, u32[]{:S(2)}) collective-permute-start(f16[2,2,32,1024]{3,2,1,0:T(8,128)(2,1)} %fusion.49), channel_id=1, source_target_pairs={{0,4},{4,0},{8,12},{12,8},{1,5},{5,1},{9,13},{13,9},{2,6},{6,2},{1... | collective-permute-start | bytes 786440 | tf_op jit(solution)/shard_map/ppermute | solution.py:191
  109.4 21.4 %collective-permute-start.20 = (f16[2,2,32,1024]{3,2,1,0:T(8,128)(2,1)S(1)}, f16[2,2,32,1024]{3,2,1,0:T(8,128)(2,1)S(1)}, u32[]{:S(2)}, u32[]{:S(2)}) collective-permute-start(f16[2,2,32,1024]{3,2,1,0:T(8,128)(2,1)S(1)} %fusion.48), channel_id=1, source_target_pairs={{0,8},{8,0},{4,12},{12,4},{1,9},{9,1},{5,13},{13,5},{2,10},{10,2},... | collective-permute-start | bytes 786440 | tf_op jit(solution)/shard_map/ppermute | solution.py:190
  127.6 14.3 %collective-permute-start.33 = (f16[2,2,2,32,1024]{4,3,2,1,0:T(8,128)(2,1)S(1)}, f16[2,2,2,32,1024]{4,3,2,1,0:T(8,128)(2,1)S(1)}, u32[]{:S(2)}, u32[]{:S(2)}) collective-permute-start(f16[2,2,2,32,1024]{4,3,2,1,0:T(8,128)(2,1)S(1)} %fusion.22), channel_id=1, source_target_pairs={{0,8},{8,0},{4,12},{12,4},{1,9},{9,1},{5,13},{13,5},{2,10},{10,2},... | collective-permute-start | bytes 1572872 | tf_op jit(solution)/shard_map/ppermute | solution.py:187
  130.5 13.3 %collective-permute-start.31 = (f16[2,2,2,32,1024]{4,3,1,0,2:T(8,128)(2,1)S(1)}, f16[2,2,2,32,1024]{4,3,1,0,2:T(8,128)(2,1)S(1)}, u32[]{:S(2)}, u32[]{:S(2)}) collective-permute-start(f16[2,2,2,32,1024]{4,3,1,0,2:T(8,128)(2,1)S(1)} %fusion.21), channel_id=1, source_target_pairs={{0,4},{4,0},{8,12},{12,8},{1,5},{5,1},{9,13},{13,9},{2,6},{6,2},{1... | collective-permute-start | bytes 1572872 | tf_op jit(solution)/shard_map/ppermute | solution.py:186
  142.2 7.4 %collective-permute-start.34 = (f16[2,2,32,1024]{3,2,1,0:T(8,128)(2,1)S(1)}, f16[2,2,32,1024]{3,2,1,0:T(8,128)(2,1)S(1)}, u32[]{:S(2)}, u32[]{:S(2)}) collective-permute-start(f16[2,2,32,1024]{3,2,1,0:T(8,128)(2,1)S(1)} %fusion.51), channel_id=1, source_target_pairs={{0,4},{4,0},{8,12},{12,8},{1,5},{5,1},{9,13},{13,9},{2,6},{6,2},{1... | collective-permute-start | bytes 786440 | tf_op jit(solution)/shard_map/ppermute | solution.py:191
  144.0 6.8 %collective-permute-start.32 = (f16[2,2,32,1024]{3,2,1,0:T(8,128)(2,1)S(1)}, f16[2,2,32,1024]{3,2,1,0:T(8,128)(2,1)S(1)}, u32[]{:S(2)}, u32[]{:S(2)}) collective-permute-start(f16[2,2,32,1024]{3,2,1,0:T(8,128)(2,1)S(1)} %fusion.50), channel_id=1, source_target_pairs={{0,8},{8,0},{4,12},{12,4},{1,9},{9,1},{5,13},{13,5},{2,10},{10,2},... | collective-permute-start | bytes 786440 | tf_op jit(solution)/shard_map/ppermute | solution.py:190
  144.9 6.2 %collective-permute-start.35 = (f16[2,32,2048]{2,1,0:T(8,128)(2,1)S(1)}, f16[2,32,2048]{2,1,0:T(8,128)(2,1)S(1)}, u32[]{:S(2)}, u32[]{:S(2)}) collective-permute-start(f16[2,32,2048]{2,1,0:T(8,128)(2,1)S(1)} %get-tuple-element.52), channel_id=1, source_target_pairs={{0,16},{16,0},{1,17},{17,1},{2,18},{18,2},{3,19},{19,3},{4,20},{20... | collective-permute-start | bytes 786440 | tf_op jit(solution)/shard_map/ppermute | solution.py:207
  (16 other events, 58.3 us)

commit v9 on v8

v9 whole, which is shorter than its diff:
```python
import jax
import jax.numpy as jnp
from jax import lax
from jax.experimental import pallas as pl
from jax.experimental.pallas import tpu as pltpu
from jax.sharding import PartitionSpec as P

EPS = 1e-05
GUIDE = 1.5
CHUNKS = 2
SHRINK = 1.0 / 32.0
SUM_TYPE = jnp.float16

X_SWAP = [(0, 1), (1, 0), (2, 3), (3, 2)]
Y_SWAP = [(0, 2), (2, 0), (1, 3), (3, 1)]
CORE_SWAP = [(0, 1), (1, 0)]


def pick(array, index, axis):
    return lax.dynamic_index_in_dim(array, index, axis, keepdims=False)


def after(value, *others):
    return lax.optimization_barrier((value, *others))[0]


def columns_kernel(place_ref, own_ref, other_ref, near_ref, far_ref, done):
    width = near_ref.shape[1]
    start = pl.multiple_of(place_ref[0] * width, width)
    columns = pl.ds(start, width)

    def fetch(near, far):
        copies = [
            pltpu.make_async_copy(near.at[:, columns], near_ref, done.at[0]),
            pltpu.make_async_copy(far.at[:, columns], far_ref, done.at[1]),
        ]
        for copy in copies:
            copy.start()
        for copy in copies:
            copy.wait()

    @pl.when(place_ref[1] == 0)
    def _():
        fetch(own_ref, other_ref)

    @pl.when(place_ref[1] != 0)
    def _():
        fetch(other_ref, own_ref)


def half_columns(core, own_half, own, other):
    block, columns = own.shape
    shape = jax.ShapeDtypeStruct((block, columns // 2), own.dtype)
    return pl.pallas_call(
        columns_kernel,
        in_specs=[
            pl.BlockSpec(memory_space=pltpu.SMEM),
            pl.BlockSpec(memory_space=pltpu.HBM),
            pl.BlockSpec(memory_space=pltpu.HBM),
        ],
        out_specs=[pl.BlockSpec(memory_space=pltpu.VMEM)] * 2,
        out_shape=[shape, shape],
        scratch_shapes=[pltpu.SemaphoreType.DMA((2,))],
        cost_estimate=pl.CostEstimate(
            flops=0, bytes_accessed=4 * block * columns, transcendentals=0
        ),
        compiler_params=pltpu.CompilerParams(vmem_limit_bytes=24 * 1024 * 1024),
    )(jnp.stack([core, own_half]).astype(jnp.int32), own, other)


def on_device(hidden, norm_gain, head_weight):
    core = lax.axis_index("pair")
    place = lax.axis_index("batch")
    level = lax.axis_index("vocab")
    vocab = lax.axis_size("vocab")
    y, x = place // 2, place % 2
    rows = hidden[0]
    seg = rows.shape[0] // 2
    depth = rows.shape[1]
    block, columns = head_weight.shape
    width = columns // 2
    model = depth * vocab
    step = seg // CHUNKS

    wide = rows.astype(jnp.float32)
    gained = (wide * norm_gain.astype(jnp.float32)[None, :]).astype(jnp.bfloat16)
    gained = gained.reshape(2, CHUNKS, step, depth).transpose(1, 0, 2, 3)

    take = lax.ppermute(head_weight, "pair", CORE_SWAP)

    def paired(value, reach):
        return lax.ppermute(value, "vocab", [(i, i ^ reach) for i in range(vocab)])

    squares = jnp.sum(wide * wide, axis=1)
    reach = 1
    while reach < vocab:
        squares += paired(squares, reach)
        reach *= 2
    squares = squares.reshape(2, seg)

    def row_scale(*earlier):
        sent = [
            lax.ppermute(
                pick(after(squares, *earlier), core ^ k, 0),
                ("pair", "batch"),
                [(4 * s + b, 2 * b + (s ^ k)) for s in range(2) for b in range(4)],
            )
            for k in range(2)
        ]
        total = jnp.stack([jnp.where(x == 0, sent[0], sent[1]), jnp.where(x == 0, sent[1], sent[0])])
        return lax.rsqrt(total / model + EPS) / SHRINK

    def by_y(mine, other, axis):
        return jnp.stack([jnp.where(y == 0, mine, other), jnp.where(y == 0, other, mine)], axis)

    def swapped(value):
        return lax.ppermute(value, "pair", CORE_SWAP)

    def dots(lefts, weight):
        return [
            jnp.dot(left.reshape(-1, block), weight, preferred_element_type=jnp.float32)
            for left in lefts
        ]

    def line_parts():
        mine = lax.dynamic_slice_in_dim(gained, x * block, block, 3)
        other = lax.ppermute(
            lax.dynamic_slice_in_dim(gained, (1 - x) * block, block, 3), "batch", X_SWAP
        )
        own = jnp.stack([jnp.where(x == 0, mine, other), jnp.where(x == 0, other, mine)], axis=1)
        own = after(own, squares)

        def up(value, k):
            return lax.ppermute(value, "vocab", [(z, z + 1) for z in range(k - 1, vocab - 1)])

        def down(value, k):
            return lax.ppermute(value, "vocab", [(z + 1, z) for z in range(vocab - k)])

        below, above = [own, up(own, 1)], [own, down(own, 1)]

        def quarter(place, reach):
            part = own
            for k in range(1, reach + 1):
                part = jnp.where(level - place == k, below[k], part)
                part = jnp.where(place - level == k, above[k], part)
            return part

        first = level // 2
        got_near = lax.ppermute(quarter(1 - y + 2 * first, 1), "batch", Y_SWAP)
        below.append(up(below[1], 2))
        above.append(down(above[1], 2))
        weights = half_columns(after(core, below[1], above[1]), core ^ first, head_weight, take)
        scale = row_scale(*weights)
        near = by_y(quarter(y + 2 * first, 1), got_near, 1)
        ready = (near, scale, *weights)
        below[2], above[2] = after(below[2], *ready), after(above[2], *ready)
        nears = (near, swapped(near))

        far = 1 - y + 2 * (1 - first)
        tips = [(0, 0), (1, vocab - 1)]
        pairs = [(b * vocab + z, (b ^ 2) * vocab + z) for b in range(4) for z in range(vocab)]
        late = [pair for pair in pairs if (pair[0] // vocab // 2, pair[0] % vocab) in tips]
        early = [pair for pair in pairs if pair not in late]
        got_early = lax.ppermute(quarter(far, 2), ("batch", "vocab"), early)
        mine_early = quarter(y + 2 * (1 - first), 2)
        near_parts = [part.reshape(CHUNKS, -1, width) for part in dots(nears, weights[0])]
        is_late = (level == 0) & (y == 1) | (level == vocab - 1) & (y == 0)
        is_far = (level == 0) & (y == 1) | (level == vocab - 1) & (y == 0)
        ends = [(up(below[2][c], 3), down(above[2][c], 3)) for c in range(CHUNKS)]
        parts = []
        for c in range(CHUNKS):
            last = jnp.where(level == 0, ends[c][1], ends[c][0])
            earlier = parts[-1] if parts else sum(ends[1:], ())
            got_late = after(lax.ppermute(last, ("batch", "vocab"), late), *earlier)
            got = jnp.where(is_late, got_late, got_early[c])
            mine = jnp.where(is_far, last, mine_early[c])
            both = by_y(mine, got, 0)
            fars = lax.optimization_barrier((both, swapped(both)))
            parts.append(
                [
                    near_part[c] + far_part
                    for near_part, far_part in zip(near_parts, dots(fars, weights[1]))
                ]
            )
        return parts, scale

    def gathered_parts():
        weights = half_columns(core, core, head_weight, take)
        parts = []
        for c in range(CHUNKS):
            whole = lax.all_gather(gained[c], "vocab", axis=2, tiled=True)
            whole = whole.reshape(2, step, 2, 4, block).transpose(3, 2, 0, 1, 4)
            whole = lax.all_to_all(whole, "batch", split_axis=0, concat_axis=0)
            whole = whole.reshape(2, 2, 2, 2, step, block).transpose(2, 0, 1, 3, 4, 5)
            lefts = (whole, swapped(whole))
            parts.append(
                [
                    near + far
                    for near, far in zip(
                        dots([left[0] for left in lefts], weights[0]),
                        dots([left[1] for left in lefts], weights[1]),
                    )
                ]
            )
        return parts, row_scale()

    def reduced(parts):
        middle = width // 2
        whole = jnp.stack([(part * SHRINK).reshape(2, 2, 2, step, width) for part in parts])
        low, high = whole[..., :middle], whole[..., middle:]
        away_x = lax.ppermute(pick(low, 1 - x, 3).astype(SUM_TYPE), "batch", X_SWAP)
        away_y = lax.ppermute(pick(high, 1 - y, 2).astype(SUM_TYPE), "batch", Y_SWAP)
        sum_x = pick(low, x, 3) + away_x.astype(jnp.float32)
        sum_y = pick(high, y, 2) + away_y.astype(jnp.float32)
        next_y = lax.ppermute(pick(sum_x, 1 - y, 2).astype(SUM_TYPE), "batch", Y_SWAP)
        next_x = lax.ppermute(pick(sum_y, 1 - x, 2).astype(SUM_TYPE), "batch", X_SWAP)
        return jnp.concatenate(
            [
                pick(sum_x, y, 2) + next_y.astype(jnp.float32),
                pick(sum_y, x, 2) + next_x.astype(jnp.float32),
            ],
            axis=-1,
        ).astype(SUM_TYPE)

    lined = depth == 2 * block and vocab == 4
    parts, scale = line_parts() if lined else gathered_parts()
    done = []
    for c in range(CHUNKS):
        sums = reduced(parts[c])
        theirs = lax.ppermute(pick(sums, 1 - core, 1), "pair", CORE_SWAP)
        done.append((pick(sums, core, 1), theirs))

    mine = jnp.concatenate([part[0] for part in done], axis=1)
    theirs = jnp.concatenate([part[1] for part in done], axis=1)

    def scores(own, other, got_own, got_other, gain):
        low = jnp.where(core == 0, own, got_own)
        high = jnp.where(core == 0, got_other, other)
        return jnp.concatenate([low, high], axis=1).astype(jnp.float32) * gain[:, None]

    cond = scores(mine[0], mine[1], theirs[0], theirs[1], scale[0])
    uncond = scores(mine[1], mine[0], theirs[1], theirs[0], scale[1])
    guided = GUIDE * cond + (1.0 - GUIDE) * uncond

    def stats(values):
        peak = jnp.max(values, axis=1)
        return peak, jnp.sum(jnp.exp(values - peak[:, None]), axis=1)

    peak_c, sum_c = stats(cond)
    peak_g, sum_g = stats(guided)
    own = jnp.stack([peak_c, peak_g, sum_c, sum_g])
    every = jnp.stack(
        [own]
        + [
            lax.ppermute(own, "vocab", [(i, (i + k) % vocab) for i in range(vocab)])
            for k in range(1, vocab)
        ]
    )
    top = jnp.max(every[:, :2], axis=0)
    total = jnp.sum(every[:, 2:] * jnp.exp(every[:, :2] - top[None]), axis=0)
    norm = top + jnp.log(total)
    return (guided - norm[1][:, None], cond - norm[0][:, None])


def solution(mesh):
    in_specs = (P("pair", "batch", "vocab"), P("vocab"), P(("pair", "batch"), "vocab"))
    out_specs = (P(("pair", "batch"), "vocab"), P(("pair", "batch"), "vocab"))
    return jax.shard_map(
        on_device, mesh=mesh, in_specs=in_specs, out_specs=out_specs, check_vma=False
    )
```

time: 163 us -> 160 us (0.982)
  waiting for transfers between devices: 57 us -> 78.7 us
  starting transfers between devices: 63.5 us -> 50.6 us
  matrix products: 17.6 us -> 10.1 us
  local copies, waits for them, and re-layouts: 8.89 us -> 5.48 us
    ppermute x24 -> x18, starting transfers between devices: 45.2 us -> 29.6 us  [the longest x2 8.23 us: line_parts(): got_late = after(lax.ppermute(last, ('batch', 'vocab'), late), *earlier)]
    ppermute x24 -> x18, waiting for transfers between devices: 25.5 us -> 40.2 us  [the longest x4 14.9 us: down(): return lax.ppermute(value, 'vocab', [(z + 1, z) for z in range(vocab - k)])]
    dot_general x8 -> x6, matrix products: 17.6 us -> 10.1 us  [dots(): jnp.dot(left.reshape(-1, block), weight, preferred_element_type=jnp.float32)]
    ppermute x2, waiting for transfers between devices: 11.1 us -> 18 us  [reduced(): lax.ppermute(pick(high, 1 - y, 2).astype(SUM_TYPE), 'batch', Y_SWAP)]
    ppermute x2, waiting for transfers between devices: 10.9 us -> 5.2 us  [reduced(): lax.ppermute(pick(sum_y, 1 - x, 2).astype(SUM_TYPE), 'batch', X_SWAP)]
    ppermute x2, waiting for transfers between devices: 1.11 us -> 6.42 us  [reduced(): lax.ppermute(pick(sum_x, 1 - y, 2).astype(SUM_TYPE), 'batch', Y_SWAP)]
    unnamed x17 -> x3, local copies, waits for them, and re-layouts: 8.31 us -> 3.42 us
    ppermute x2, starting transfers between devices: 5.26 us -> 2.82 us  [reduced(): lax.ppermute(pick(high, 1 - y, 2).astype(SUM_TYPE), 'batch', Y_SWAP)]
  transfers between devices with their start and end apart: 40 -> 34, of which waited for: 15 -> 19; matrix products, arithmetic and copies ran while one was open for 15% -> 12% of each run, Pallas kernels for 2% -> 2%
where the time goes in v9:
time: 160 us
  waiting for transfers between devices  78.7 us (49%)
  starting transfers between devices  50.6 us (32%)
  matrix products  10.1 us (6%)
  other arithmetic  9.7 us (6%)
  local copies, waits for them, and re-layouts  5.48 us (3%)
  Pallas kernels  3.78 us (2%)
    ppermute x2, waiting for transfers between devices, reduced(): lax.ppermute(pick(high, 1 - y, 2).astype(SUM_TYPE), 'batch', Y_SWAP)  18 us
    ppermute x4, waiting for transfers between devices, down(): return lax.ppermute(value, 'vocab', [(z + 1, z) for z in range(vocab - k)])  14.9 us
    dot_general x6, matrix products, dots(): jnp.dot(left.reshape(-1, block), weight, preferred_element_type=jnp.float32)  10.1 us
    ppermute x1, waiting for transfers between devices, line_parts(): got_near = lax.ppermute(quarter(1 - y + 2 * first, 1), 'batch', Y_SWAP)  9.29 us
    ppermute x2, starting transfers between devices, line_parts(): got_late = after(lax.ppermute(last, ('batch', 'vocab'), late), *earlier)  8.23 us
    ppermute x4, waiting for transfers between devices, up(): lax.ppermute(value, 'vocab', [(z, z + 1) for z in range(k - 1, vocab - 1)])  8.15 us
    ppermute x2, waiting for transfers between devices, line_parts(): got_late = after(lax.ppermute(last, ('batch', 'vocab'), late), *earlier)  7.3 us
    ppermute x2, waiting for transfers between devices, reduced(): lax.ppermute(pick(sum_x, 1 - y, 2).astype(SUM_TYPE), 'batch', Y_SWAP)  6.42 us
  transfers between devices with their start and end apart: 34, of which 19 were waited for; matrix products, arithmetic and copies ran while one was open for 12% of the time, Pallas kernels for 2%

profile of v9, /device:TPU:0, one launch (start us, length us, event | category | flops | bytes accessed | tf_op | source)
XLA Modules:
  0.0 159.7 jit_solution(4198079982518150251)
XLA Ops:
  3.0 2.6 %collective-permute-start = (bf16[2,2,32,1024]{3,2,0,1:T(8,128)(2,1)S(1)}, bf16[2,2,32,1024]{3,2,0,1:T(8,128)(2,1)S(1)}, u32[]{:S(2)}, u32[]{:S(2)}) collective-permute-start(bf16[2,2,32,1024]{3,2,0,1:T(8,128)(2,1)S(1)} %dynamic-slice_bitcast_fusion), channel_id=1, source_target_pairs={{0,4},{4,0},{8,12},{12,8},{1,5},{5,1},{9,13},{13,9},{2,6},{6,2},{1... | collective-permute-start | bytes 786440 | tf_op jit(solution)/shard_map/ppermute | solution.py:127
  6.8 1.6 %collective-permute-start.1 = (f32[128]{0:T(128)S(1)}, f32[128]{0:T(128)S(1)}, u32[]{:S(2)}, u32[]{:S(2)}) collective-permute-start(f32[128]{0:T(128)S(1)} %multiply_reduce_fusion), channel_id=1, source_target_pairs={{0,1},{1,0},{2,3},{3,2},{4,5},{5,4},{6,7},{7,6},{8,9},{9,8},{10,11... | collective-permute-start | bytes 1544 | tf_op jit(solution)/shard_map/ppermute | solution.py:92
  8.5 2.0 %collective-permute-done.1 = f32[128]{0:T(128)S(1)} collective-permute-done((f32[128]{0:T(128)S(1)}, f32[128]{0:T(128)S(1)}, u32[]{:S(2)}, u32[]{:S(2)}) %collective-permute-start.1) | collective-permute-done | bytes 544 | tf_op jit(solution)/shard_map/ppermute | solution.py:92
  10.4 2.6 %collective-permute-start.2 = (f32[128]{0:T(128)S(1)}, f32[128]{0:T(128)S(1)}, u32[]{:S(2)}, u32[]{:S(2)}) collective-permute-start(f32[128]{0:T(128)S(1)} %add.126), channel_id=1, source_target_pairs={{0,2},{1,3},{2,0},{3,1},{4,6},{5,7},{6,4},{7,5},{8,10},{9,11},{10,... | collective-permute-start | bytes 1544 | tf_op jit(solution)/shard_map/ppermute | solution.py:92
  13.0 1.9 %collective-permute-done.2 = f32[128]{0:T(128)S(1)} collective-permute-done((f32[128]{0:T(128)S(1)}, f32[128]{0:T(128)S(1)}, u32[]{:S(2)}, u32[]{:S(2)}) %collective-permute-start.2) | collective-permute-done | bytes 544 | tf_op jit(solution)/shard_map/ppermute | solution.py:92
  15.2 3.5 %collective-permute-start.4 = (bf16[2,2,2,32,1024]{4,3,2,1,0:T(8,128)(2,1)S(1)}, bf16[2,2,2,32,1024]{4,3,2,1,0:T(8,128)(2,1)S(1)}, u32[]{:S(2)}, u32[]{:S(2)}) collective-permute-start(bf16[2,2,2,32,1024]{4,3,2,1,0:T(8,128)(2,1)S(1)} %copy.21), channel_id=1, source_target_pairs={{0,1},{1,2},{2,3},{4,5},{5,6},{6,7},{8,9},{9,10},{10,11},{12,13},{... | collective-permute-start | bytes 1572872 | tf_op jit(solution)/shard_map/ppermute | solution.py:134
  20.1 8.1 %collective-permute-done.4 = bf16[2,2,2,32,1024]{4,3,2,1,0:T(8,128)(2,1)S(1)} collective-permute-done((bf16[2,2,2,32,1024]{4,3,2,1,0:T(8,128)(2,1)S(1)}, bf16[2,2,2,32,1024]{4,3,2,1,0:T(8,128)(2,1)S(1)}, u32[]{:S(2)}, u32[]{:S(2)}) %collective-permute-start.4) | collective-permute-done | bytes 524320 | tf_op jit(solution)/shard_map/ppermute | solution.py:134
  28.2 4.1 %collective-permute-done.3 = bf16[2,2,2,32,1024]{4,3,2,1,0:T(8,128)(2,1)S(1)} collective-permute-done((bf16[2,2,2,32,1024]{4,3,2,1,0:T(8,128)(2,1)S(1)}, bf16[2,2,2,32,1024]{4,3,2,1,0:T(8,128)(2,1)S(1)}, u32[]{:S(2)}, u32[]{:S(2)}) %collective-permute-start.3) | collective-permute-done | bytes 524320 | tf_op jit(solution)/shard_map/ppermute | solution.py:137
  32.4 1.6 collective-permute-start.5
  34.0 9.3 %collective-permute-done.5 = bf16[2,2,2,32,1024]{4,3,2,1,0:T(8,128)(2,1)S(1)} collective-permute-done((bf16[2,2,2,32,1024]{4,3,2,1,0:T(8,128)(2,1)S(1)}, bf16[2,2,2,32,1024]{4,3,2,1,0:T(8,128)(2,1)S(1)}, u32[]{:S(2)}, u32[]{:S(2)}) %collective-permute-start.5) | collective-permute-done | bytes 524320 | tf_op jit(solution)/shard_map/ppermute | solution.py:149
  47.8 3.4 %copy-done = bf16[1024,4096]{1,0:T(8,128)(2,1)S(1)} copy-done((bf16[1024,4096]{1,0:T(8,128)(2,1)S(1)}, bf16[1024,4096]{1,0:T(8,128)(2,1)}, u32[]{:S(2)}) %copy-start) | copy-done | bytes 8388632
  51.2 3.8 %shard_map.50 = (bf16[1024,2048]{1,0:T(8,128)(2,1)S(1)}, bf16[1024,2048]{1,0:T(8,128)(2,1)S(1)}) custom-call(s32[2]{0:T(128)S(1)} %pad_add_fusion.place_ref, bf16[1024,4096]{1,0:T(8,128)(2,1)S(1)} %copy-done, bf16[1024,4096]{1,0:T(8,128)(2,1)} %collective-permute-done.6.other_ref), custom_call_target="tpu_custom_call" | custom-call | bytes 16777216 | tf_op jit(solution)/shard_map/pallas_call | solution.py:54
  55.6 4.3 %collective-permute-start.9 = (f32[64]{0:T(128)S(1)}, f32[64]{0:T(128)S(1)}, u32[]{:S(2)}, u32[]{:S(2)}) collective-permute-start(f32[64]{0:T(128)S(1)} %get-tuple-element.68), channel_id=1, source_target_pairs={{0,4},{4,12},{8,20},{12,28},{16,0},{20,8},{24,16},{28,24},{1,5},{5... | collective-permute-start | bytes 776 | tf_op jit(solution)/shard_map/ppermute | solution.py:103
  59.9 2.4 %fusion.56 = f32[512,2048]{1,0:T(8,128)S(1)} fusion(bf16[512,1024]{1,0:T(8,128)(2,1)S(1)} %bitcast.198, bf16[1024,2048]{1,0:T(8,128)(2,1)S(1)} %get-tuple-element.17), kind=kOutput, calls=%fused_computation.160 | convolution fusion | flops 2147483648 | bytes 9437184 | tf_op jit(solution)/shard_map/dot_general | solution.py:121
  68.4 10.2 %collective-permute-done.10 = bf16[2,2,32,1024]{3,2,1,0:T(8,128)(2,1)S(1)} collective-permute-done((bf16[2,2,32,1024]{3,2,1,0:T(8,128)(2,1)S(1)}, bf16[2,2,32,1024]{3,2,1,0:T(8,128)(2,1)S(1)}, u32[]{:S(2)}, u32[]{:S(2)}) %collective-permute-start.10) | collective-permute-done | bytes 262176 | tf_op jit(solution)/shard_map/ppermute | solution.py:137
  78.6 3.6 %collective-permute-start.13 = (bf16[2,2,32,1024]{3,2,1,0:T(8,128)(2,1)S(1)}, bf16[2,2,32,1024]{3,2,1,0:T(8,128)(2,1)S(1)}, u32[]{:S(2)}, u32[]{:S(2)}) collective-permute-start(bf16[2,2,32,1024]{3,2,1,0:T(8,128)(2,1)S(1)} %broadcast_select_fusion.1), channel_id=1, source_target_pairs={{0,8},{4,12},{11,3},{15,7},{16,24},{20,28},{27,19},{31,23}} | collective-permute-start | bytes 786440 | tf_op jit(solution)/shard_map/ppermute | solution.py:174
  82.5 4.0 %collective-permute-done.13 = bf16[2,2,32,1024]{3,2,1,0:T(8,128)(2,1)S(1)} collective-permute-done((bf16[2,2,32,1024]{3,2,1,0:T(8,128)(2,1)S(1)}, bf16[2,2,32,1024]{3,2,1,0:T(8,128)(2,1)S(1)}, u32[]{:S(2)}, u32[]{:S(2)}) %collective-permute-start.13) | collective-permute-done | bytes 262176 | tf_op jit(solution)/shard_map/ppermute | solution.py:174
  86.7 2.4 %fusion.55 = f32[512,2048]{1,0:T(8,128)S(1)} fusion(bf16[512,1024]{1,0:T(8,128)(2,1)S(1)} %bitcast.197, bf16[1024,2048]{1,0:T(8,128)(2,1)S(1)} %get-tuple-element.17), kind=kOutput, calls=%fused_computation.159 | convolution fusion | flops 2147483648 | bytes 9437184 | tf_op jit(solution)/shard_map/dot_general | solution.py:121
  89.1 4.6 %collective-permute-start.23 = (bf16[2,2,32,1024]{3,2,1,0:T(8,128)(2,1)S(1)}, bf16[2,2,32,1024]{3,2,1,0:T(8,128)(2,1)S(1)}, u32[]{:S(2)}, u32[]{:S(2)}) collective-permute-start(bf16[2,2,32,1024]{3,2,1,0:T(8,128)(2,1)S(1)} %broadcast_select_fusion), channel_id=1, source_target_pairs={{0,8},{4,12},{11,3},{15,7},{16,24},{20,28},{27,19},{31,23}} | collective-permute-start | bytes 786440 | tf_op jit(solution)/shard_map/ppermute | solution.py:174
  96.4 3.3 %collective-permute-done.23 = bf16[2,2,32,1024]{3,2,1,0:T(8,128)(2,1)S(1)} collective-permute-done((bf16[2,2,32,1024]{3,2,1,0:T(8,128)(2,1)S(1)}, bf16[2,2,32,1024]{3,2,1,0:T(8,128)(2,1)S(1)}, u32[]{:S(2)}, u32[]{:S(2)}) %collective-permute-start.23) | collective-permute-done | bytes 262176 | tf_op jit(solution)/shard_map/ppermute | solution.py:174
  99.8 2.5 %collective-permute-start.21 = (f16[2,2,2,32,1024]{4,3,2,1,0:T(8,128)(2,1)S(1)}, f16[2,2,2,32,1024]{4,3,2,1,0:T(8,128)(2,1)S(1)}, u32[]{:S(2)}, u32[]{:S(2)}) collective-permute-start(f16[2,2,2,32,1024]{4,3,2,1,0:T(8,128)(2,1)S(1)} %fusion.21), channel_id=1, source_target_pairs={{0,8},{8,0},{4,12},{12,4},{1,9},{9,1},{5,13},{13,5},{2,10},{10,2},... | collective-permute-start | bytes 1572872 | tf_op jit(solution)/shard_map/ppermute | solution.py:212
  103.1 2.0 %collective-permute-start.19 = (f16[2,2,2,32,1024]{4,3,1,0,2:T(8,128)(2,1)S(1)}, f16[2,2,2,32,1024]{4,3,1,0,2:T(8,128)(2,1)S(1)}, u32[]{:S(2)}, u32[]{:S(2)}) collective-permute-start(f16[2,2,2,32,1024]{4,3,1,0,2:T(8,128)(2,1)S(1)} %fusion.18), channel_id=1, source_target_pairs={{0,4},{4,0},{8,12},{12,8},{1,5},{5,1},{9,13},{13,9},{2,6},{6,2},{1... | collective-permute-start | bytes 1572872 | tf_op jit(solution)/shard_map/ppermute | solution.py:211
  105.1 9.0 %collective-permute-done.21 = f16[2,2,2,32,1024]{4,3,2,1,0:T(8,128)(2,1)S(1)} collective-permute-done((f16[2,2,2,32,1024]{4,3,2,1,0:T(8,128)(2,1)S(1)}, f16[2,2,2,32,1024]{4,3,2,1,0:T(8,128)(2,1)S(1)}, u32[]{:S(2)}, u32[]{:S(2)}) %collective-permute-start.21) | collective-permute-done | bytes 524320 | tf_op jit(solution)/shard_map/ppermute | solution.py:212
  114.4 2.0 %collective-permute-start.22 = (f16[2,2,32,1024]{3,2,1,0:T(8,128)(2,1)S(1)}, f16[2,2,32,1024]{3,2,1,0:T(8,128)(2,1)S(1)}, u32[]{:S(2)}, u32[]{:S(2)}) collective-permute-start(f16[2,2,32,1024]{3,2,1,0:T(8,128)(2,1)S(1)} %fusion.27), channel_id=1, source_target_pairs={{0,4},{4,0},{8,12},{12,8},{1,5},{5,1},{9,13},{13,9},{2,6},{6,2},{1... | collective-permute-start | bytes 786440 | tf_op jit(solution)/shard_map/ppermute | solution.py:216
  119.7 1.8 %collective-permute-start.20 = (f16[2,2,32,1024]{3,2,1,0:T(8,128)(2,1)S(1)}, f16[2,2,32,1024]{3,2,1,0:T(8,128)(2,1)S(1)}, u32[]{:S(2)}, u32[]{:S(2)}) collective-permute-start(f16[2,2,32,1024]{3,2,1,0:T(8,128)(2,1)S(1)} %fusion.26), channel_id=1, source_target_pairs={{0,8},{8,0},{4,12},{12,4},{1,9},{9,1},{5,13},{13,5},{2,10},{10,2},... | collective-permute-start | bytes 786440 | tf_op jit(solution)/shard_map/ppermute | solution.py:215
  123.6 5.4 %collective-permute-done.20 = f16[2,2,32,1024]{3,2,1,0:T(8,128)(2,1)S(1)} collective-permute-done((f16[2,2,32,1024]{3,2,1,0:T(8,128)(2,1)S(1)}, f16[2,2,32,1024]{3,2,1,0:T(8,128)(2,1)S(1)}, u32[]{:S(2)}, u32[]{:S(2)}) %collective-permute-start.20) | collective-permute-done | bytes 262176 | tf_op jit(solution)/shard_map/ppermute | solution.py:215
  129.1 9.0 %collective-permute-done.27 = f16[2,2,2,32,1024]{4,3,2,1,0:T(8,128)(2,1)S(1)} collective-permute-done((f16[2,2,2,32,1024]{4,3,2,1,0:T(8,128)(2,1)S(1)}, f16[2,2,2,32,1024]{4,3,2,1,0:T(8,128)(2,1)S(1)}, u32[]{:S(2)}, u32[]{:S(2)}) %collective-permute-start.27) | collective-permute-done | bytes 524320 | tf_op jit(solution)/shard_map/ppermute | solution.py:212
  140.6 4.1 %collective-permute-done.28 = f16[2,2,32,1024]{3,2,1,0:T(8,128)(2,1)S(1)} collective-permute-done((f16[2,2,32,1024]{3,2,1,0:T(8,128)(2,1)S(1)}, f16[2,2,32,1024]{3,2,1,0:T(8,128)(2,1)S(1)}, u32[]{:S(2)}, u32[]{:S(2)}) %collective-permute-start.28) | collective-permute-done | bytes 262176 | tf_op jit(solution)/shard_map/ppermute | solution.py:216
  146.2 1.4 collective-permute-done.30
  149.3 5.1 %collective-permute-start.31 = (f32[4,64]{1,0:T(4,128)S(1)}, f32[4,64]{1,0:T(4,128)S(1)}, u32[]{:S(2)}, u32[]{:S(2)}) collective-permute-start(f32[4,64]{1,0:T(4,128)S(1)} %get-tuple-element.60), channel_id=1, source_target_pairs={{0,1},{1,2},{2,3},{3,0},{4,5},{5,6},{6,7},{7,4},{8,9},{9,10},{10,1... | collective-permute-start | bytes 3080 | tf_op jit(solution)/shard_map/ppermute | solution.py:255
  155.7 2.3 %collective-permute-done.33 = f32[4,64]{1,0:T(4,128)S(1)} collective-permute-done((f32[4,64]{1,0:T(4,128)S(1)}, f32[4,64]{1,0:T(4,128)S(1)}, u32[]{:S(2)}, u32[]{:S(2)}) %collective-permute-start.33) | collective-permute-done | bytes 1056 | tf_op jit(solution)/shard_map/ppermute | solution.py:255
  158.1 1.6 %fusion.16 = (f32[64,4096]{1,0:T(8,128)}, f32[64,4096]{1,0:T(8,128)}) fusion(f32[64]{0:T(128)S(1)} %get-tuple-element.61, f32[64]{0:T(128)S(1)} %get-tuple-element.63, f16[64,2048]{1,0:T(8,128)(2,1)S(1)} %get-tuple-element.45, f16[64,2048]{1,0:T(8,128)(2,1)S(1)} %get-tuple-element.44, f32[64,4096]{1,0:T(8,128)S(1)} %get-tuple-element.29, ...), kind=kLoop, calls=%fused_computation.41 | loop fusion | flops 1310720 | bytes 3670784 | tf_op jit(solution)/shard_map/sub | solution.py:262
  (111 shorter events, 32.8 us)
Async XLA Ops:
  0.6 47.1 %collective-permute-start.6 = (bf16[1024,4096]{1,0:T(8,128)(2,1)}, bf16[1024,4096]{1,0:T(8,128)(2,1)}, u32[]{:S(2)}, u32[]{:S(2)}) collective-permute-start(bf16[1024,4096]{1,0:T(8,128)(2,1)} %own_ref.1), channel_id=1, source_target_pairs={{0,16},{16,0},{1,17},{17,1},{2,18},{18,2},{3,19},{19,3},{4,20},{20... | collective-permute-start | bytes 25165832 | tf_op jit(solution)/shard_map/ppermute | solution.py:89
  3.0 12.0 %collective-permute-start = (bf16[2,2,32,1024]{3,2,0,1:T(8,128)(2,1)S(1)}, bf16[2,2,32,1024]{3,2,0,1:T(8,128)(2,1)S(1)}, u32[]{:S(2)}, u32[]{:S(2)}) collective-permute-start(bf16[2,2,32,1024]{3,2,0,1:T(8,128)(2,1)S(1)} %dynamic-slice_bitcast_fusion), channel_id=1, source_target_pairs={{0,4},{4,0},{8,12},{12,8},{1,5},{5,1},{9,13},{13,9},{2,6},{6,2},{1... | collective-permute-start | bytes 786440 | tf_op jit(solution)/shard_map/ppermute | solution.py:127
  6.8 3.6 %collective-permute-start.1 = (f32[128]{0:T(128)S(1)}, f32[128]{0:T(128)S(1)}, u32[]{:S(2)}, u32[]{:S(2)}) collective-permute-start(f32[128]{0:T(128)S(1)} %multiply_reduce_fusion), channel_id=1, source_target_pairs={{0,1},{1,0},{2,3},{3,2},{4,5},{5,4},{6,7},{7,6},{8,9},{9,8},{10,11... | collective-permute-start | bytes 1544 | tf_op jit(solution)/shard_map/ppermute | solution.py:92
  10.4 4.4 %collective-permute-start.2 = (f32[128]{0:T(128)S(1)}, f32[128]{0:T(128)S(1)}, u32[]{:S(2)}, u32[]{:S(2)}) collective-permute-start(f32[128]{0:T(128)S(1)} %add.126), channel_id=1, source_target_pairs={{0,2},{1,3},{2,0},{3,1},{4,6},{5,7},{6,4},{7,5},{8,10},{9,11},{10,... | collective-permute-start | bytes 1544 | tf_op jit(solution)/shard_map/ppermute | solution.py:92
  15.2 13.0 %collective-permute-start.4 = (bf16[2,2,2,32,1024]{4,3,2,1,0:T(8,128)(2,1)S(1)}, bf16[2,2,2,32,1024]{4,3,2,1,0:T(8,128)(2,1)S(1)}, u32[]{:S(2)}, u32[]{:S(2)}) collective-permute-start(bf16[2,2,2,32,1024]{4,3,2,1,0:T(8,128)(2,1)S(1)} %copy.21), channel_id=1, source_target_pairs={{0,1},{1,2},{2,3},{4,5},{5,6},{6,7},{8,9},{9,10},{10,11},{12,13},{... | collective-permute-start | bytes 1572872 | tf_op jit(solution)/shard_map/ppermute | solution.py:134
  18.7 13.6 %collective-permute-start.3 = (bf16[2,2,2,32,1024]{4,3,2,1,0:T(8,128)(2,1)S(1)}, bf16[2,2,2,32,1024]{4,3,2,1,0:T(8,128)(2,1)S(1)}, u32[]{:S(2)}, u32[]{:S(2)}) collective-permute-start(bf16[2,2,2,32,1024]{4,3,2,1,0:T(8,128)(2,1)S(1)} %copy.21), channel_id=1, source_target_pairs={{1,0},{2,1},{3,2},{5,4},{6,5},{7,6},{9,8},{10,9},{11,10},{13,12},{... | collective-permute-start | bytes 1572872 | tf_op jit(solution)/shard_map/ppermute | solution.py:137
  32.4 10.9 %collective-permute-start.5 = (bf16[2,2,2,32,1024]{4,3,2,1,0:T(8,128)(2,1)S(1)}, bf16[2,2,2,32,1024]{4,3,2,1,0:T(8,128)(2,1)S(1)}, u32[]{:S(2)}, u32[]{:S(2)}) collective-permute-start(bf16[2,2,2,32,1024]{4,3,2,1,0:T(8,128)(2,1)S(1)} %select_select_fusion.1), channel_id=1, source_target_pairs={{0,8},{8,0},{4,12},{12,4},{1,9},{9,1},{5,13},{13,5},{2,10},{10,2},... | collective-permute-start | bytes 1572872 | tf_op jit(solution)/shard_map/ppermute | solution.py:149
  43.8 18.6 %collective-permute-start.11 = (bf16[2,2,2,32,1024]{4,3,2,1,0:T(8,128)(2,1)S(1)}, bf16[2,2,2,32,1024]{4,3,2,1,0:T(8,128)(2,1)S(1)}, u32[]{:S(2)}, u32[]{:S(2)}) collective-permute-start(bf16[2,2,2,32,1024]{4,3,2,1,0:T(8,128)(2,1)S(1)} %collective-permute-done.4), channel_id=1, source_target_pairs={{1,2},{2,3},{5,6},{6,7},{9,10},{10,11},{13,14},{14,15},{17,18},{18... | collective-permute-start | bytes 1572872 | tf_op jit(solution)/shard_map/ppermute | solution.py:134
  44.5 18.5 %collective-permute-start.7 = (bf16[2,2,2,32,1024]{4,3,2,1,0:T(8,128)(2,1)S(1)}, bf16[2,2,2,32,1024]{4,3,2,1,0:T(8,128)(2,1)S(1)}, u32[]{:S(2)}, u32[]{:S(2)}) collective-permute-start(bf16[2,2,2,32,1024]{4,3,2,1,0:T(8,128)(2,1)S(1)} %collective-permute-done.3), channel_id=1, source_target_pairs={{1,0},{2,1},{5,4},{6,5},{9,8},{10,9},{13,12},{14,13},{17,16},{18,1... | collective-permute-start | bytes 1572872 | tf_op jit(solution)/shard_map/ppermute | solution.py:137
  55.0 7.3 %collective-permute-start.8 = (f32[64]{0:T(128)S(1)}, f32[64]{0:T(128)S(1)}, u32[]{:S(2)}, u32[]{:S(2)}) collective-permute-start(f32[64]{0:T(128)S(1)} %get-tuple-element.67), channel_id=1, source_target_pairs={{0,0},{4,8},{8,16},{12,24},{16,4},{20,12},{24,20},{28,28},{1,1},{5... | collective-permute-start | bytes 776 | tf_op jit(solution)/shard_map/ppermute | solution.py:103
  55.6 6.7 %collective-permute-start.9 = (f32[64]{0:T(128)S(1)}, f32[64]{0:T(128)S(1)}, u32[]{:S(2)}, u32[]{:S(2)}) collective-permute-start(f32[64]{0:T(128)S(1)} %get-tuple-element.68), channel_id=1, source_target_pairs={{0,4},{4,12},{8,20},{12,28},{16,0},{20,8},{24,16},{28,24},{1,5},{5... | collective-permute-start | bytes 776 | tf_op jit(solution)/shard_map/ppermute | solution.py:103
  63.0 19.5 %collective-permute-start.15 = (bf16[2,2,32,1024]{3,2,1,0:T(8,128)(2,1)S(1)}, bf16[2,2,32,1024]{3,2,1,0:T(8,128)(2,1)S(1)}, u32[]{:S(2)}, u32[]{:S(2)}) collective-permute-start(bf16[2,2,32,1024]{3,2,1,0:T(8,128)(2,1)S(1)} %get-tuple-element.55), channel_id=1, source_target_pairs={{1,0},{5,4},{9,8},{13,12},{17,16},{21,20},{25,24},{29,28}} | collective-permute-start | bytes 786440 | tf_op jit(solution)/shard_map/ppermute | solution.py:137
  64.3 14.3 %collective-permute-start.10 = (bf16[2,2,32,1024]{3,2,1,0:T(8,128)(2,1)S(1)}, bf16[2,2,32,1024]{3,2,1,0:T(8,128)(2,1)S(1)}, u32[]{:S(2)}, u32[]{:S(2)}) collective-permute-start(bf16[2,2,32,1024]{3,2,1,0:T(8,128)(2,1)S(1)} %get-tuple-element.56), channel_id=1, source_target_pairs={{1,0},{5,4},{9,8},{13,12},{17,16},{21,20},{25,24},{29,28}} | collective-permute-start | bytes 786440 | tf_op jit(solution)/shard_map/ppermute | solution.py:137
  65.6 16.9 %collective-permute-start.14 = (bf16[2,2,32,1024]{3,2,1,0:T(8,128)(2,1)S(1)}, bf16[2,2,32,1024]{3,2,1,0:T(8,128)(2,1)S(1)}, u32[]{:S(2)}, u32[]{:S(2)}) collective-permute-start(bf16[2,2,32,1024]{3,2,1,0:T(8,128)(2,1)S(1)} %get-tuple-element.57), channel_id=1, source_target_pairs={{2,3},{6,7},{10,11},{14,15},{18,19},{22,23},{26,27},{30,31}} | collective-permute-start | bytes 786440 | tf_op jit(solution)/shard_map/ppermute | solution.py:134
  66.3 12.3 %collective-permute-start.12 = (bf16[2,2,32,1024]{3,2,1,0:T(8,128)(2,1)S(1)}, bf16[2,2,32,1024]{3,2,1,0:T(8,128)(2,1)S(1)}, u32[]{:S(2)}, u32[]{:S(2)}) collective-permute-start(bf16[2,2,32,1024]{3,2,1,0:T(8,128)(2,1)S(1)} %get-tuple-element.58), channel_id=1, source_target_pairs={{2,3},{6,7},{10,11},{14,15},{18,19},{22,23},{26,27},{30,31}} | collective-permute-start | bytes 786440 | tf_op jit(solution)/shard_map/ppermute | solution.py:134
  67.1 19.4 %collective-permute-start.16 = (bf16[2,2,2,32,1024]{4,3,0,2,1:T(8,128)(2,1)S(1)}, bf16[2,2,2,32,1024]{4,3,0,2,1:T(8,128)(2,1)S(1)}, u32[]{:S(2)}, u32[]{:S(2)}) collective-permute-start(bf16[2,2,2,32,1024]{4,3,0,2,1:T(8,128)(2,1)S(1)} %copy_select_fusion), channel_id=1, source_target_pairs={{1,9},{2,10},{3,11},{5,13},{6,14},{7,15},{8,0},{9,1},{10,2},{12,4}... | collective-permute-start | bytes 1572872 | tf_op jit(solution)/shard_map/ppermute | solution.py:164
  78.6 7.9 %collective-permute-start.13 = (bf16[2,2,32,1024]{3,2,1,0:T(8,128)(2,1)S(1)}, bf16[2,2,32,1024]{3,2,1,0:T(8,128)(2,1)S(1)}, u32[]{:S(2)}, u32[]{:S(2)}) collective-permute-start(bf16[2,2,32,1024]{3,2,1,0:T(8,128)(2,1)S(1)} %broadcast_select_fusion.1), channel_id=1, source_target_pairs={{0,8},{4,12},{11,3},{15,7},{16,24},{20,28},{27,19},{31,23}} | collective-permute-start | bytes 786440 | tf_op jit(solution)/shard_map/ppermute | solution.py:174
  86.6 7.1 %collective-permute-start.17 = (bf16[2,2,2,32,1024]{4,3,2,1,0:T(8,128)(2,1)S(1)}, bf16[2,2,2,32,1024]{4,3,2,1,0:T(8,128)(2,1)S(1)}, u32[]{:S(2)}, u32[]{:S(2)}) collective-permute-start(bf16[2,2,2,32,1024]{4,3,2,1,0:T(8,128)(2,1)S(1)} %pad_maximum_fusion.2), channel_id=1, source_target_pairs={{0,16},{16,0},{1,17},{17,1},{2,18},{18,2},{3,19},{19,3},{4,20},{20... | collective-permute-start | bytes 1572872 | tf_op jit(solution)/shard_map/ppermute | solution.py:117
  89.1 10.6 %collective-permute-start.23 = (bf16[2,2,32,1024]{3,2,1,0:T(8,128)(2,1)S(1)}, bf16[2,2,32,1024]{3,2,1,0:T(8,128)(2,1)S(1)}, u32[]{:S(2)}, u32[]{:S(2)}) collective-permute-start(bf16[2,2,32,1024]{3,2,1,0:T(8,128)(2,1)S(1)} %broadcast_select_fusion), channel_id=1, source_target_pairs={{0,8},{4,12},{11,3},{15,7},{16,24},{20,28},{27,19},{31,23}} | collective-permute-start | bytes 786440 | tf_op jit(solution)/shard_map/ppermute | solution.py:174
  99.8 14.4 %collective-permute-start.21 = (f16[2,2,2,32,1024]{4,3,2,1,0:T(8,128)(2,1)S(1)}, f16[2,2,2,32,1024]{4,3,2,1,0:T(8,128)(2,1)S(1)}, u32[]{:S(2)}, u32[]{:S(2)}) collective-permute-start(f16[2,2,2,32,1024]{4,3,2,1,0:T(8,128)(2,1)S(1)} %fusion.21), channel_id=1, source_target_pairs={{0,8},{8,0},{4,12},{12,4},{1,9},{9,1},{5,13},{13,5},{2,10},{10,2},... | collective-permute-start | bytes 1572872 | tf_op jit(solution)/shard_map/ppermute | solution.py:212
  102.5 13.9 %collective-permute-start.24 = (bf16[2,2,2,32,1024]{4,3,2,1,0:T(8,128)(2,1)S(1)}, bf16[2,2,2,32,1024]{4,3,2,1,0:T(8,128)(2,1)S(1)}, u32[]{:S(2)}, u32[]{:S(2)}) collective-permute-start(bf16[2,2,2,32,1024]{4,3,2,1,0:T(8,128)(2,1)S(1)} %pad_maximum_fusion.3), channel_id=1, source_target_pairs={{0,16},{16,0},{1,17},{17,1},{2,18},{18,2},{3,19},{19,3},{4,20},{20... | collective-permute-start | bytes 1572872 | tf_op jit(solution)/shard_map/ppermute | solution.py:117
  103.1 16.4 %collective-permute-start.19 = (f16[2,2,2,32,1024]{4,3,1,0,2:T(8,128)(2,1)S(1)}, f16[2,2,2,32,1024]{4,3,1,0,2:T(8,128)(2,1)S(1)}, u32[]{:S(2)}, u32[]{:S(2)}) collective-permute-start(f16[2,2,2,32,1024]{4,3,1,0,2:T(8,128)(2,1)S(1)} %fusion.18), channel_id=1, source_target_pairs={{0,4},{4,0},{8,12},{12,8},{1,5},{5,1},{9,13},{13,9},{2,6},{6,2},{1... | collective-permute-start | bytes 1572872 | tf_op jit(solution)/shard_map/ppermute | solution.py:211
  114.4 9.2 %collective-permute-start.22 = (f16[2,2,32,1024]{3,2,1,0:T(8,128)(2,1)S(1)}, f16[2,2,32,1024]{3,2,1,0:T(8,128)(2,1)S(1)}, u32[]{:S(2)}, u32[]{:S(2)}) collective-permute-start(f16[2,2,32,1024]{3,2,1,0:T(8,128)(2,1)S(1)} %fusion.27), channel_id=1, source_target_pairs={{0,4},{4,0},{8,12},{12,8},{1,5},{5,1},{9,13},{13,9},{2,6},{6,2},{1... | collective-permute-start | bytes 786440 | tf_op jit(solution)/shard_map/ppermute | solution.py:216
  119.7 9.3 %collective-permute-start.20 = (f16[2,2,32,1024]{3,2,1,0:T(8,128)(2,1)S(1)}, f16[2,2,32,1024]{3,2,1,0:T(8,128)(2,1)S(1)}, u32[]{:S(2)}, u32[]{:S(2)}) collective-permute-start(f16[2,2,32,1024]{3,2,1,0:T(8,128)(2,1)S(1)} %fusion.26), channel_id=1, source_target_pairs={{0,8},{8,0},{4,12},{12,4},{1,9},{9,1},{5,13},{13,5},{2,10},{10,2},... | collective-permute-start | bytes 786440 | tf_op jit(solution)/shard_map/ppermute | solution.py:215
  121.5 16.6 %collective-permute-start.27 = (f16[2,2,2,32,1024]{4,3,2,1,0:T(8,128)(2,1)S(1)}, f16[2,2,2,32,1024]{4,3,2,1,0:T(8,128)(2,1)S(1)}, u32[]{:S(2)}, u32[]{:S(2)}) collective-permute-start(f16[2,2,2,32,1024]{4,3,2,1,0:T(8,128)(2,1)S(1)} %fusion.20), channel_id=1, source_target_pairs={{0,8},{8,0},{4,12},{12,4},{1,9},{9,1},{5,13},{13,5},{2,10},{10,2},... | collective-permute-start | bytes 1572872 | tf_op jit(solution)/shard_map/ppermute | solution.py:212
  122.1 17.1 %collective-permute-start.25 = (f16[2,2,2,32,1024]{4,3,1,0,2:T(8,128)(2,1)S(1)}, f16[2,2,2,32,1024]{4,3,1,0,2:T(8,128)(2,1)S(1)}, u32[]{:S(2)}, u32[]{:S(2)}) collective-permute-start(f16[2,2,2,32,1024]{4,3,1,0,2:T(8,128)(2,1)S(1)} %fusion.19), channel_id=1, source_target_pairs={{0,4},{4,0},{8,12},{12,8},{1,5},{5,1},{9,13},{13,9},{2,6},{6,2},{1... | collective-permute-start | bytes 1572872 | tf_op jit(solution)/shard_map/ppermute | solution.py:211
  138.3 6.4 %collective-permute-start.28 = (f16[2,2,32,1024]{3,2,1,0:T(8,128)(2,1)S(1)}, f16[2,2,32,1024]{3,2,1,0:T(8,128)(2,1)S(1)}, u32[]{:S(2)}, u32[]{:S(2)}) collective-permute-start(f16[2,2,32,1024]{3,2,1,0:T(8,128)(2,1)S(1)} %fusion.29), channel_id=1, source_target_pairs={{0,4},{4,0},{8,12},{12,8},{1,5},{5,1},{9,13},{13,9},{2,6},{6,2},{1... | collective-permute-start | bytes 786440 | tf_op jit(solution)/shard_map/ppermute | solution.py:216
  139.4 6.4 %collective-permute-start.26 = (f16[2,2,32,1024]{3,2,1,0:T(8,128)(2,1)S(1)}, f16[2,2,32,1024]{3,2,1,0:T(8,128)(2,1)S(1)}, u32[]{:S(2)}, u32[]{:S(2)}) collective-permute-start(f16[2,2,32,1024]{3,2,1,0:T(8,128)(2,1)S(1)} %fusion.28), channel_id=1, source_target_pairs={{0,8},{8,0},{4,12},{12,4},{1,9},{9,1},{5,13},{13,5},{2,10},{10,2},... | collective-permute-start | bytes 786440 | tf_op jit(solution)/shard_map/ppermute | solution.py:215
  140.5 5.7 %collective-permute-start.29 = (f16[2,32,2048]{2,1,0:T(8,128)(2,1)S(1)}, f16[2,32,2048]{2,1,0:T(8,128)(2,1)S(1)}, u32[]{:S(2)}, u32[]{:S(2)}) collective-permute-start(f16[2,32,2048]{2,1,0:T(8,128)(2,1)S(1)} %get-tuple-element.52), channel_id=1, source_target_pairs={{0,16},{16,0},{1,17},{17,1},{2,18},{18,2},{3,19},{19,3},{4,20},{20... | collective-permute-start | bytes 786440 | tf_op jit(solution)/shard_map/ppermute | solution.py:230
  149.2 5.2 %collective-permute-start.32 = (f32[4,64]{1,0:T(4,128)S(1)}, f32[4,64]{1,0:T(4,128)S(1)}, u32[]{:S(2)}, u32[]{:S(2)}) collective-permute-start(f32[4,64]{1,0:T(4,128)S(1)} %get-tuple-element.60), channel_id=1, source_target_pairs={{0,2},{1,3},{2,0},{3,1},{4,6},{5,7},{6,4},{7,5},{8,10},{9,11},{10,... | collective-permute-start | bytes 3080 | tf_op jit(solution)/shard_map/ppermute | solution.py:255
  149.3 6.4 %collective-permute-start.31 = (f32[4,64]{1,0:T(4,128)S(1)}, f32[4,64]{1,0:T(4,128)S(1)}, u32[]{:S(2)}, u32[]{:S(2)}) collective-permute-start(f32[4,64]{1,0:T(4,128)S(1)} %get-tuple-element.60), channel_id=1, source_target_pairs={{0,1},{1,2},{2,3},{3,0},{4,5},{5,6},{6,7},{7,4},{8,9},{9,10},{10,1... | collective-permute-start | bytes 3080 | tf_op jit(solution)/shard_map/ppermute | solution.py:255
  154.4 3.6 %collective-permute-start.33 = (f32[4,64]{1,0:T(4,128)S(1)}, f32[4,64]{1,0:T(4,128)S(1)}, u32[]{:S(2)}, u32[]{:S(2)}) collective-permute-start(f32[4,64]{1,0:T(4,128)S(1)} %get-tuple-element.60), channel_id=1, source_target_pairs={{0,3},{1,0},{2,1},{3,2},{4,7},{5,4},{6,5},{7,6},{8,11},{9,8},{10,9... | collective-permute-start | bytes 3080 | tf_op jit(solution)/shard_map/ppermute | solution.py:255
  (3 other events, 7.8 us)

commit v10 on v9

--- a/solution.py
+++ b/solution.py
@@ -64,7 +64,7 @@
         cost_estimate=pl.CostEstimate(
             flops=0, bytes_accessed=4 * block * columns, transcendentals=0
         ),
-        compiler_params=pltpu.CompilerParams(vmem_limit_bytes=24 * 1024 * 1024),
+        compiler_params=pltpu.CompilerParams(vmem_limit_bytes=48 * 1024 * 1024),
     )(jnp.stack([core, own_half]).astype(jnp.int32), own, other)
 
 
@@ -146,14 +146,13 @@
             return part
 
         first = level // 2
+        weights = half_columns(after(core, own), core ^ first, head_weight, take)
+        scale = row_scale(*weights)
+        below[1], above[1] = after(below[1], scale, *weights), after(above[1], scale, *weights)
         got_near = lax.ppermute(quarter(1 - y + 2 * first, 1), "batch", Y_SWAP)
         below.append(up(below[1], 2))
         above.append(down(above[1], 2))
-        weights = half_columns(after(core, below[1], above[1]), core ^ first, head_weight, take)
-        scale = row_scale(*weights)
-        near = by_y(quarter(y + 2 * first, 1), got_near, 1)
-        ready = (near, scale, *weights)
-        below[2], above[2] = after(below[2], *ready), after(above[2], *ready)
+        near = by_y(quarter(y + 2 * first, 1), after(got_near, below[2], above[2]), 1)
         nears = (near, swapped(near))
 
         far = 1 - y + 2 * (1 - first)
@@ -165,68 +164,77 @@
         mine_early = quarter(y + 2 * (1 - first), 2)
         near_parts = [part.reshape(CHUNKS, -1, width) for part in dots(nears, weights[0])]
         is_late = (level == 0) & (y == 1) | (level == vocab - 1) & (y == 0)
-        is_far = (level == 0) & (y == 1) | (level == vocab - 1) & (y == 0)
-        ends = [(up(below[2][c], 3), down(above[2][c], 3)) for c in range(CHUNKS)]
-        parts = []
-        for c in range(CHUNKS):
-            last = jnp.where(level == 0, ends[c][1], ends[c][0])
-            earlier = parts[-1] if parts else sum(ends[1:], ())
-            got_late = after(lax.ppermute(last, ("batch", "vocab"), late), *earlier)
+        ends = [
+            (
+                up(after(below[2][c], *([near] if c else [])), 3),
+                down(after(above[2][c], *([near] if c else [])), 3),
+            )
+            for c in range(CHUNKS)
+        ]
+
+        lasts = [jnp.where(level == 0, above_3, below_3) for below_3, above_3 in ends]
+        lates = [lax.ppermute(last, ("batch", "vocab"), late) for last in lasts]
+
+        def parts(c, *earlier):
+            got_late = after(lates[c], *(earlier or lasts[1:]))
             got = jnp.where(is_late, got_late, got_early[c])
-            mine = jnp.where(is_far, last, mine_early[c])
+            mine = jnp.where(is_late, lasts[c], mine_early[c])
             both = by_y(mine, got, 0)
             fars = lax.optimization_barrier((both, swapped(both)))
-            parts.append(
-                [
-                    near_part[c] + far_part
-                    for near_part, far_part in zip(near_parts, dots(fars, weights[1]))
-                ]
-            )
+            found = [
+                near_part[c] + far_part
+                for near_part, far_part in zip(near_parts, dots(fars, weights[1]))
+            ]
+            return [after(part, *lates[c + 1 :]) for part in found]
+
         return parts, scale
 
     def gathered_parts():
         weights = half_columns(core, core, head_weight, take)
-        parts = []
-        for c in range(CHUNKS):
+
+        def parts(c, *earlier):
             whole = lax.all_gather(gained[c], "vocab", axis=2, tiled=True)
             whole = whole.reshape(2, step, 2, 4, block).transpose(3, 2, 0, 1, 4)
             whole = lax.all_to_all(whole, "batch", split_axis=0, concat_axis=0)
             whole = whole.reshape(2, 2, 2, 2, step, block).transpose(2, 0, 1, 3, 4, 5)
+            whole = after(whole, *earlier)
             lefts = (whole, swapped(whole))
-            parts.append(
-                [
-                    near + far
-                    for near, far in zip(
-                        dots([left[0] for left in lefts], weights[0]),
-                        dots([left[1] for left in lefts], weights[1]),
-                    )
-                ]
-            )
+            return [
+                near + far
+                for near, far in zip(
+                    dots([left[0] for left in lefts], weights[0]),
+                    dots([left[1] for left in lefts], weights[1]),
+                )
+            ]
+
         return parts, row_scale()
 
-    def reduced(parts):
-        middle = width // 2
-        whole = jnp.stack([(part * SHRINK).reshape(2, 2, 2, step, width) for part in parts])
-        low, high = whole[..., :middle], whole[..., middle:]
+    lined = depth == 2 * block and vocab == 4
+    parts, scale = line_parts() if lined else gathered_parts()
+    halfway, more_sends = [], []
+    for c in range(CHUNKS):
+        whole = [part * SHRINK for part in parts(c, *(more_sends[-1] if c else ()))]
+        whole = jnp.stack([part.reshape(2, 2, 2, step, width) for part in whole])
+        low, high = whole[..., : width // 2], whole[..., width // 2 :]
         away_x = lax.ppermute(pick(low, 1 - x, 3).astype(SUM_TYPE), "batch", X_SWAP)
         away_y = lax.ppermute(pick(high, 1 - y, 2).astype(SUM_TYPE), "batch", Y_SWAP)
         sum_x = pick(low, x, 3) + away_x.astype(jnp.float32)
         sum_y = pick(high, y, 2) + away_y.astype(jnp.float32)
-        next_y = lax.ppermute(pick(sum_x, 1 - y, 2).astype(SUM_TYPE), "batch", Y_SWAP)
-        next_x = lax.ppermute(pick(sum_y, 1 - x, 2).astype(SUM_TYPE), "batch", X_SWAP)
-        return jnp.concatenate(
+        halfway.append((pick(sum_x, y, 2), pick(sum_y, x, 2)))
+        more_sends.append(
+            (pick(sum_x, 1 - y, 2).astype(SUM_TYPE), pick(sum_y, 1 - x, 2).astype(SUM_TYPE))
+        )
+    done = []
+    for c in range(CHUNKS):
+        next_y = lax.ppermute(more_sends[c][0], "batch", Y_SWAP)
+        next_x = lax.ppermute(more_sends[c][1], "batch", X_SWAP)
+        sums = jnp.concatenate(
             [
-                pick(sum_x, y, 2) + next_y.astype(jnp.float32),
-                pick(sum_y, x, 2) + next_x.astype(jnp.float32),
+                halfway[c][0] + next_y.astype(jnp.float32),
+                halfway[c][1] + next_x.astype(jnp.float32),
             ],
             axis=-1,
         ).astype(SUM_TYPE)
-
-    lined = depth == 2 * block and vocab == 4
-    parts, scale = line_parts() if lined else gathered_parts()
-    done = []
-    for c in range(CHUNKS):
-        sums = reduced(parts[c])
         theirs = lax.ppermute(pick(sums, 1 - core, 1), "pair", CORE_SWAP)
         done.append((pick(sums, core, 1), theirs))
 

time: 160 us -> 164 us (1.025)
  waiting for transfers between devices: 78.7 us -> 67.8 us
  other arithmetic: 9.7 us -> 16.7 us
  matrix products: 10.1 us -> 12.9 us
  Pallas kernels: 3.78 us -> 6.07 us
    ppermute x4, waiting for transfers between devices: 8.15 us -> 0.01 us  [up(): lax.ppermute(value, 'vocab', [(z, z + 1) for z in range(k - 1, vocab - 1)])]
    ppermute x4, waiting for transfers between devices: 14.9 us -> 9.54 us  [down(): return lax.ppermute(value, 'vocab', [(z + 1, z) for z in range(vocab - k)])]
    dot_general x6, matrix products: 10.1 us -> 12.9 us  [dots(): jnp.dot(left.reshape(-1, block), weight, preferred_element_type=jnp.float32)]
    ppermute x1, waiting for transfers between devices: 0.01 us -> 2.76 us  [line_parts(): got_early = lax.ppermute(quarter(far, 2), ('batch', 'vocab'), early)]
    unnamed x3 -> x31, local copies, waits for them, and re-layouts: 3.42 us -> 6.15 us
    convert_element_type x8, other arithmetic: 0.45 us -> 2.76 us  [the longest x2 0.96 us: on_device(): pick(high, 1 - y, 2).astype(SUM_TYPE)]
    ppermute x3, starting transfers between devices: 5.15 us -> 7.45 us  [on_device(): lax.ppermute(own, 'vocab', [(i, (i + k) % vocab) for i in range(vocab)])]
    pallas_call x1, Pallas kernels: 3.78 us -> 6.07 us  [half_columns(): pl.pallas_call(columns_kernel, in_specs=[pl.BlockSpec(memory_space=pltpu....]
  transfers between devices with their start and end apart: 34 -> 34, of which waited for: 19 -> 17; matrix products, arithmetic and copies ran while one was open for 12% -> 13% of each run, Pallas kernels for 2% -> 4%
where the time goes in v10:
time: 164 us; the launch traced here: 163 us
  waiting for transfers between devices  67.8 us (41%)
  starting transfers between devices  51.4 us (31%)
  other arithmetic  16.7 us (10%)
  matrix products  12.9 us (8%)
  local copies, waits for them, and re-layouts  7.02 us (4%)
  Pallas kernels  6.07 us (4%)
    ppermute x2, waiting for transfers between devices, on_device(): lax.ppermute(pick(high, 1 - y, 2).astype(SUM_TYPE), 'batch', Y_SWAP)  20.9 us
    dot_general x6, matrix products, dots(): jnp.dot(left.reshape(-1, block), weight, preferred_element_type=jnp.float32)  12.9 us
    ppermute x2, waiting for transfers between devices, on_device(): next_x = lax.ppermute(more_sends[c][1], 'batch', X_SWAP)  11 us
    ppermute x4, waiting for transfers between devices, down(): return lax.ppermute(value, 'vocab', [(z + 1, z) for z in range(vocab - k)])  9.54 us
    ppermute x1, waiting for transfers between devices, line_parts(): got_near = lax.ppermute(quarter(1 - y + 2 * first, 1), 'batch', Y_SWAP)  9.13 us
    ppermute x3, starting transfers between devices, on_device(): lax.ppermute(own, 'vocab', [(i, (i + k) % vocab) for i in range(vocab)])  7.45 us
    unnamed x31, local copies, waits for them, and re-layouts  6.15 us
    ppermute x2, starting transfers between devices, line_parts(): lates = [lax.ppermute(last, ('batch', 'vocab'), late) for last in lasts]  6.08 us
  transfers between devices with their start and end apart: 34, of which 17 were waited for; matrix products, arithmetic and copies ran while one was open for 13% of the time, Pallas kernels for 4%

profile of v10, /device:TPU:0, one launch (start us, length us, event | category | flops | bytes accessed | tf_op | source)
XLA Modules:
  0.0 163.3 jit_solution(9648992451877484629)
XLA Ops:
  3.0 2.6 %collective-permute-start = (bf16[2,2,32,1024]{3,2,0,1:T(8,128)(2,1)S(1)}, bf16[2,2,32,1024]{3,2,0,1:T(8,128)(2,1)S(1)}, u32[]{:S(2)}, u32[]{:S(2)}) collective-permute-start(bf16[2,2,32,1024]{3,2,0,1:T(8,128)(2,1)S(1)} %dynamic-slice_bitcast_fusion), channel_id=1, source_target_pairs={{0,4},{4,0},{8,12},{12,8},{1,5},{5,1},{9,13},{13,9},{2,6},{6,2},{1... | collective-permute-start | bytes 786440 | tf_op jit(solution)/shard_map/ppermute | solution.py:127
  6.8 1.6 %collective-permute-start.1 = (f32[128]{0:T(128)S(1)}, f32[128]{0:T(128)S(1)}, u32[]{:S(2)}, u32[]{:S(2)}) collective-permute-start(f32[128]{0:T(128)S(1)} %multiply_reduce_fusion), channel_id=1, source_target_pairs={{0,1},{1,0},{2,3},{3,2},{4,5},{5,4},{6,7},{7,6},{8,9},{9,8},{10,11... | collective-permute-start | bytes 1544 | tf_op jit(solution)/shard_map/ppermute | solution.py:92
  8.5 2.0 %collective-permute-done.1 = f32[128]{0:T(128)S(1)} collective-permute-done((f32[128]{0:T(128)S(1)}, f32[128]{0:T(128)S(1)}, u32[]{:S(2)}, u32[]{:S(2)}) %collective-permute-start.1) | collective-permute-done | bytes 544 | tf_op jit(solution)/shard_map/ppermute | solution.py:92
  10.4 2.6 %collective-permute-start.2 = (f32[128]{0:T(128)S(1)}, f32[128]{0:T(128)S(1)}, u32[]{:S(2)}, u32[]{:S(2)}) collective-permute-start(f32[128]{0:T(128)S(1)} %add.126), channel_id=1, source_target_pairs={{0,2},{1,3},{2,0},{3,1},{4,6},{5,7},{6,4},{7,5},{8,10},{9,11},{10,... | collective-permute-start | bytes 1544 | tf_op jit(solution)/shard_map/ppermute | solution.py:92
  13.0 1.9 %collective-permute-done.2 = f32[128]{0:T(128)S(1)} collective-permute-done((f32[128]{0:T(128)S(1)}, f32[128]{0:T(128)S(1)}, u32[]{:S(2)}, u32[]{:S(2)}) %collective-permute-start.2) | collective-permute-done | bytes 544 | tf_op jit(solution)/shard_map/ppermute | solution.py:92
  15.2 3.5 %collective-permute-start.7 = (bf16[2,2,2,32,1024]{4,3,2,1,0:T(8,128)(2,1)S(1)}, bf16[2,2,2,32,1024]{4,3,2,1,0:T(8,128)(2,1)S(1)}, u32[]{:S(2)}, u32[]{:S(2)}) collective-permute-start(bf16[2,2,2,32,1024]{4,3,2,1,0:T(8,128)(2,1)S(1)} %copy.21), channel_id=1, source_target_pairs={{0,1},{1,2},{2,3},{4,5},{5,6},{6,7},{8,9},{9,10},{10,11},{12,13},{... | collective-permute-start | bytes 1572872 | tf_op jit(solution)/shard_map/ppermute | solution.py:134
  20.1 6.1 %shard_map.50 = (bf16[1024,2048]{1,0:T(8,128)(2,1)S(1)}, bf16[1024,2048]{1,0:T(8,128)(2,1)}) custom-call(s32[2]{0:T(128)S(1)} %pad_add_fusion.place_ref, bf16[1024,4096]{1,0:T(8,128)(2,1)} %own_ref.1, bf16[1024,4096]{1,0:T(8,128)(2,1)} %collective-permute-done.4.other_ref), custom_call_target="tpu_custom_call" | custom-call | bytes 16777216 | tf_op jit(solution)/shard_map/pallas_call | solution.py:54
  26.2 2.0 %copy-done = bf16[1024,2048]{1,0:T(8,128)(2,1)} copy-done((bf16[1024,2048]{1,0:T(8,128)(2,1)}, bf16[1024,2048]{1,0:T(8,128)(2,1)S(1)}, u32[]{:S(2)}) %copy-start) | copy-done | bytes 4194328
  28.8 4.3 %collective-permute-start.6 = (f32[64]{0:T(128)S(1)}, f32[64]{0:T(128)S(1)}, u32[]{:S(2)}, u32[]{:S(2)}) collective-permute-start(f32[64]{0:T(128)S(1)} %get-tuple-element.75), channel_id=1, source_target_pairs={{0,4},{4,12},{8,20},{12,28},{16,0},{20,8},{24,16},{28,24},{1,5},{5... | collective-permute-start | bytes 776 | tf_op jit(solution)/shard_map/ppermute | solution.py:103
  35.3 1.6 collective-permute-start.8
  39.0 9.1 %collective-permute-done.8 = bf16[2,2,2,32,1024]{4,3,2,1,0:T(8,128)(2,1)S(1)} collective-permute-done((bf16[2,2,2,32,1024]{4,3,2,1,0:T(8,128)(2,1)}, bf16[2,2,2,32,1024]{4,3,2,1,0:T(8,128)(2,1)S(1)}, u32[]{:S(2)}, u32[]{:S(2)}) %collective-permute-start.8) | collective-permute-done | bytes 524320 | tf_op jit(solution)/shard_map/ppermute | solution.py:152
  48.1 2.6 %collective-permute-done.10 = bf16[2,2,2,32,1024]{4,3,2,1,0:T(8,128)(2,1)S(1)} collective-permute-done((bf16[2,2,2,32,1024]{4,3,2,1,0:T(8,128)(2,1)S(1)}, bf16[2,2,2,32,1024]{4,3,2,1,0:T(8,128)(2,1)S(1)}, u32[]{:S(2)}, u32[]{:S(2)}) %collective-permute-start.10) | collective-permute-done | bytes 524320 | tf_op jit(solution)/shard_map/ppermute | solution.py:137
  52.6 1.6 collective-permute-start.14
  55.7 7.0 %collective-permute-done.11 = bf16[2,2,32,1024]{3,2,1,0:T(8,128)(2,1)S(1)} collective-permute-done((bf16[2,2,32,1024]{3,2,1,0:T(8,128)(2,1)S(1)}, bf16[2,2,32,1024]{3,2,1,0:T(8,128)(2,1)S(1)}, u32[]{:S(2)}, u32[]{:S(2)}) %collective-permute-start.11) | collective-permute-done | bytes 262176 | tf_op jit(solution)/shard_map/ppermute | solution.py:137
  64.0 4.6 %collective-permute-start.13 = (bf16[2,2,32,1024]{3,2,1,0:T(8,128)(2,1)S(1)}, bf16[2,2,32,1024]{3,2,1,0:T(8,128)(2,1)S(1)}, u32[]{:S(2)}, u32[]{:S(2)}) collective-permute-start(bf16[2,2,32,1024]{3,2,1,0:T(8,128)(2,1)S(1)} %broadcast_select_fusion.1), channel_id=1, source_target_pairs={{0,8},{4,12},{11,3},{15,7},{16,24},{20,28},{27,19},{31,23}} | collective-permute-start | bytes 786440 | tf_op jit(solution)/shard_map/ppermute | solution.py:176
  68.6 2.4 %fusion.53 = f32[512,2048]{1,0:T(8,128)S(1)} fusion(bf16[512,1024]{1,0:T(8,128)(2,1)S(1)} %bitcast.197, bf16[1024,2048]{1,0:T(8,128)(2,1)S(1)} %copy-done.1), kind=kOutput, calls=%fused_computation.159 | convolution fusion | flops 2147483648 | bytes 9437184 | tf_op jit(solution)/shard_map/dot_general | solution.py:121
  72.5 2.8 %collective-permute-done.13 = bf16[2,2,32,1024]{3,2,1,0:T(8,128)(2,1)S(1)} collective-permute-done((bf16[2,2,32,1024]{3,2,1,0:T(8,128)(2,1)S(1)}, bf16[2,2,32,1024]{3,2,1,0:T(8,128)(2,1)S(1)}, u32[]{:S(2)}, u32[]{:S(2)}) %collective-permute-start.13) | collective-permute-done | bytes 262176 | tf_op jit(solution)/shard_map/ppermute | solution.py:176
  75.3 2.8 %collective-permute-done.16 = bf16[2,2,2,32,1024]{4,3,0,2,1:T(8,128)(2,1)S(1)} collective-permute-done((bf16[2,2,2,32,1024]{4,3,0,2,1:T(8,128)(2,1)S(1)}, bf16[2,2,2,32,1024]{4,3,0,2,1:T(8,128)(2,1)S(1)}, u32[]{:S(2)}, u32[]{:S(2)}) %collective-permute-start.16) | collective-permute-done | bytes 524320 | tf_op jit(solution)/shard_map/ppermute | solution.py:163
  78.9 2.4 %fusion.54 = f32[512,2048]{1,0:T(8,128)S(1)} fusion(bf16[512,1024]{1,0:T(8,128)(2,1)S(1)} %bitcast.198, bf16[1024,2048]{1,0:T(8,128)(2,1)S(1)} %copy-done.1), kind=kOutput, calls=%fused_computation.160 | convolution fusion | flops 2147483648 | bytes 9437184 | tf_op jit(solution)/shard_map/dot_general | solution.py:121
  88.2 3.0 %collective-permute-start.20 = (f16[2,2,2,32,1024]{4,3,1,0,2:T(8,128)(2,1)}, f16[2,2,2,32,1024]{4,3,1,0,2:T(8,128)(2,1)}, u32[]{:S(2)}, u32[]{:S(2)}) collective-permute-start(f16[2,2,2,32,1024]{4,3,1,0,2:T(8,128)(2,1)} %fusion.16), channel_id=1, source_target_pairs={{0,4},{4,0},{8,12},{12,8},{1,5},{5,1},{9,13},{13,9},{2,6},{6,2},{1... | collective-permute-start | bytes 1572872 | tf_op jit(solution)/shard_map/ppermute | solution.py:219
  91.2 10.0 %collective-permute-done.22 = f16[2,2,2,32,1024]{4,3,2,1,0:T(8,128)(2,1)} collective-permute-done((f16[2,2,2,32,1024]{4,3,2,1,0:T(8,128)(2,1)}, f16[2,2,2,32,1024]{4,3,2,1,0:T(8,128)(2,1)}, u32[]{:S(2)}, u32[]{:S(2)}) %collective-permute-start.22) | collective-permute-done | bytes 524320 | tf_op jit(solution)/shard_map/ppermute | solution.py:220
  105.1 2.9 %collective-permute-start.23 = (f16[2,2,32,1024]{3,2,1,0:T(8,128)(2,1)}, f16[2,2,32,1024]{3,2,1,0:T(8,128)(2,1)S(1)}, u32[]{:S(2)}, u32[]{:S(2)}) collective-permute-start(f16[2,2,32,1024]{3,2,1,0:T(8,128)(2,1)} %fusion.25), channel_id=1, source_target_pairs={{0,4},{4,0},{8,12},{12,8},{1,5},{5,1},{9,13},{13,9},{2,6},{6,2},{1... | collective-permute-start | bytes 786440 | tf_op jit(solution)/shard_map/ppermute | solution.py:230
  108.7 6.5 %collective-permute-done.23 = f16[2,2,32,1024]{3,2,1,0:T(8,128)(2,1)S(1)} collective-permute-done((f16[2,2,32,1024]{3,2,1,0:T(8,128)(2,1)}, f16[2,2,32,1024]{3,2,1,0:T(8,128)(2,1)S(1)}, u32[]{:S(2)}, u32[]{:S(2)}) %collective-permute-start.23) | collective-permute-done | bytes 262176 | tf_op jit(solution)/shard_map/ppermute | solution.py:230
  116.3 4.3 %slice_add_fusion.1 = f32[256,2048]{1,0:T(8,128)S(1)} fusion(f32[512,2048]{1,0:T(8,128)} %copy-done.5, bf16[256,1024]{1,0:T(8,128)(2,1)S(1)} %bitcast.194, bf16[1024,2048]{1,0:T(8,128)(2,1)} %get-tuple-element.23), kind=kOutput, calls=%fused_computation.7 | convolution fusion | flops 1074266112 | bytes 8912896 | tf_op jit(solution)/shard_map/dot_general | solution.py:121
  120.8 1.9 %copy-done.3 = bf16[1024,2048]{1,0:T(8,128)(2,1)S(1)} copy-done((bf16[1024,2048]{1,0:T(8,128)(2,1)S(1)}, bf16[1024,2048]{1,0:T(8,128)(2,1)}, u32[]{:S(2)}) %copy-start.3) | copy-done | bytes 4194328
  125.6 1.8 %collective-permute-start.25 = (f16[2,2,2,32,1024]{4,3,1,0,2:T(8,128)(2,1)S(1)}, f16[2,2,2,32,1024]{4,3,1,0,2:T(8,128)(2,1)S(1)}, u32[]{:S(2)}, u32[]{:S(2)}) collective-permute-start(f16[2,2,2,32,1024]{4,3,1,0,2:T(8,128)(2,1)S(1)} %fusion.17), channel_id=1, source_target_pairs={{0,4},{4,0},{8,12},{12,8},{1,5},{5,1},{9,13},{13,9},{2,6},{6,2},{1... | collective-permute-start | bytes 1572872 | tf_op jit(solution)/shard_map/ppermute | solution.py:219
  127.5 10.9 %collective-permute-done.27 = f16[2,2,2,32,1024]{4,3,2,1,0:T(8,128)(2,1)S(1)} collective-permute-done((f16[2,2,2,32,1024]{4,3,2,1,0:T(8,128)(2,1)S(1)}, f16[2,2,2,32,1024]{4,3,2,1,0:T(8,128)(2,1)S(1)}, u32[]{:S(2)}, u32[]{:S(2)}) %collective-permute-start.27) | collective-permute-done | bytes 524320 | tf_op jit(solution)/shard_map/ppermute | solution.py:220
  138.6 1.6 collective-permute-start.28
  141.4 4.5 %collective-permute-done.28 = f16[2,2,32,1024]{3,2,1,0:T(8,128)(2,1)S(1)} collective-permute-done((f16[2,2,32,1024]{3,2,1,0:T(8,128)(2,1)S(1)}, f16[2,2,32,1024]{3,2,1,0:T(8,128)(2,1)S(1)}, u32[]{:S(2)}, u32[]{:S(2)}) %collective-permute-start.28) | collective-permute-done | bytes 262176 | tf_op jit(solution)/shard_map/ppermute | solution.py:230
  150.7 7.4 %collective-permute-start.31 = (f32[4,64]{1,0:T(4,128)S(1)}, f32[4,64]{1,0:T(4,128)S(1)}, u32[]{:S(2)}, u32[]{:S(2)}) collective-permute-start(f32[4,64]{1,0:T(4,128)S(1)} %get-tuple-element.67), channel_id=1, source_target_pairs={{0,1},{1,2},{2,3},{3,0},{4,5},{5,6},{6,7},{7,4},{8,9},{9,10},{10,1... | collective-permute-start | bytes 3080 | tf_op jit(solution)/shard_map/ppermute | solution.py:263
  159.4 2.3 %collective-permute-done.33 = f32[4,64]{1,0:T(4,128)S(1)} collective-permute-done((f32[4,64]{1,0:T(4,128)S(1)}, f32[4,64]{1,0:T(4,128)S(1)}, u32[]{:S(2)}, u32[]{:S(2)}) %collective-permute-start.33) | collective-permute-done | bytes 1056 | tf_op jit(solution)/shard_map/ppermute | solution.py:263
  161.7 1.6 fusion.14
  (142 shorter events, 40.0 us)
Async XLA Ops:
  0.6 19.5 %collective-permute-start.4 = (bf16[1024,4096]{1,0:T(8,128)(2,1)}, bf16[1024,4096]{1,0:T(8,128)(2,1)}, u32[]{:S(2)}, u32[]{:S(2)}) collective-permute-start(bf16[1024,4096]{1,0:T(8,128)(2,1)} %own_ref.1), channel_id=1, source_target_pairs={{0,16},{16,0},{1,17},{17,1},{2,18},{18,2},{3,19},{19,3},{4,20},{20... | collective-permute-start | bytes 25165832 | tf_op jit(solution)/shard_map/ppermute | solution.py:89
  3.0 12.0 %collective-permute-start = (bf16[2,2,32,1024]{3,2,0,1:T(8,128)(2,1)S(1)}, bf16[2,2,32,1024]{3,2,0,1:T(8,128)(2,1)S(1)}, u32[]{:S(2)}, u32[]{:S(2)}) collective-permute-start(bf16[2,2,32,1024]{3,2,0,1:T(8,128)(2,1)S(1)} %dynamic-slice_bitcast_fusion), channel_id=1, source_target_pairs={{0,4},{4,0},{8,12},{12,8},{1,5},{5,1},{9,13},{13,9},{2,6},{6,2},{1... | collective-permute-start | bytes 786440 | tf_op jit(solution)/shard_map/ppermute | solution.py:127
  6.8 3.6 %collective-permute-start.1 = (f32[128]{0:T(128)S(1)}, f32[128]{0:T(128)S(1)}, u32[]{:S(2)}, u32[]{:S(2)}) collective-permute-start(f32[128]{0:T(128)S(1)} %multiply_reduce_fusion), channel_id=1, source_target_pairs={{0,1},{1,0},{2,3},{3,2},{4,5},{5,4},{6,7},{7,6},{8,9},{9,8},{10,11... | collective-permute-start | bytes 1544 | tf_op jit(solution)/shard_map/ppermute | solution.py:92
  10.4 4.4 %collective-permute-start.2 = (f32[128]{0:T(128)S(1)}, f32[128]{0:T(128)S(1)}, u32[]{:S(2)}, u32[]{:S(2)}) collective-permute-start(f32[128]{0:T(128)S(1)} %add.126), channel_id=1, source_target_pairs={{0,2},{1,3},{2,0},{3,1},{4,6},{5,7},{6,4},{7,5},{8,10},{9,11},{10,... | collective-permute-start | bytes 1544 | tf_op jit(solution)/shard_map/ppermute | solution.py:92
  15.2 19.2 %collective-permute-start.7 = (bf16[2,2,2,32,1024]{4,3,2,1,0:T(8,128)(2,1)S(1)}, bf16[2,2,2,32,1024]{4,3,2,1,0:T(8,128)(2,1)S(1)}, u32[]{:S(2)}, u32[]{:S(2)}) collective-permute-start(bf16[2,2,2,32,1024]{4,3,2,1,0:T(8,128)(2,1)S(1)} %copy.21), channel_id=1, source_target_pairs={{0,1},{1,2},{2,3},{4,5},{5,6},{6,7},{8,9},{9,10},{10,11},{12,13},{... | collective-permute-start | bytes 1572872 | tf_op jit(solution)/shard_map/ppermute | solution.py:134
  18.7 15.7 %collective-permute-start.3 = (bf16[2,2,2,32,1024]{4,3,2,1,0:T(8,128)(2,1)S(1)}, bf16[2,2,2,32,1024]{4,3,2,1,0:T(8,128)(2,1)S(1)}, u32[]{:S(2)}, u32[]{:S(2)}) collective-permute-start(bf16[2,2,2,32,1024]{4,3,2,1,0:T(8,128)(2,1)S(1)} %copy.21), channel_id=1, source_target_pairs={{1,0},{2,1},{3,2},{5,4},{6,5},{7,6},{9,8},{10,9},{11,10},{13,12},{... | collective-permute-start | bytes 1572872 | tf_op jit(solution)/shard_map/ppermute | solution.py:137
  28.2 4.9 %collective-permute-start.5 = (f32[64]{0:T(128)S(1)}, f32[64]{0:T(128)S(1)}, u32[]{:S(2)}, u32[]{:S(2)}) collective-permute-start(f32[64]{0:T(128)S(1)} %get-tuple-element.74), channel_id=1, source_target_pairs={{0,0},{4,8},{8,16},{12,24},{16,4},{20,12},{24,20},{28,28},{1,1},{5... | collective-permute-start | bytes 776 | tf_op jit(solution)/shard_map/ppermute | solution.py:103
  28.8 5.6 %collective-permute-start.6 = (f32[64]{0:T(128)S(1)}, f32[64]{0:T(128)S(1)}, u32[]{:S(2)}, u32[]{:S(2)}) collective-permute-start(f32[64]{0:T(128)S(1)} %get-tuple-element.75), channel_id=1, source_target_pairs={{0,4},{4,12},{8,20},{12,28},{16,0},{20,8},{24,16},{28,24},{1,5},{5... | collective-permute-start | bytes 776 | tf_op jit(solution)/shard_map/ppermute | solution.py:103
  35.3 12.8 %collective-permute-start.8 = (bf16[2,2,2,32,1024]{4,3,2,1,0:T(8,128)(2,1)}, bf16[2,2,2,32,1024]{4,3,2,1,0:T(8,128)(2,1)S(1)}, u32[]{:S(2)}, u32[]{:S(2)}) collective-permute-start(bf16[2,2,2,32,1024]{4,3,2,1,0:T(8,128)(2,1)} %select_select_fusion.1), channel_id=1, source_target_pairs={{0,8},{8,0},{4,12},{12,4},{1,9},{9,1},{5,13},{13,5},{2,10},{10,2},... | collective-permute-start | bytes 1572872 | tf_op jit(solution)/shard_map/ppermute | solution.py:152
  36.9 13.8 %collective-permute-start.10 = (bf16[2,2,2,32,1024]{4,3,2,1,0:T(8,128)(2,1)S(1)}, bf16[2,2,2,32,1024]{4,3,2,1,0:T(8,128)(2,1)S(1)}, u32[]{:S(2)}, u32[]{:S(2)}) collective-permute-start(bf16[2,2,2,32,1024]{4,3,2,1,0:T(8,128)(2,1)S(1)} %collective-permute-done.3), channel_id=1, source_target_pairs={{1,0},{2,1},{5,4},{6,5},{9,8},{10,9},{13,12},{14,13},{17,16},{18,1... | collective-permute-start | bytes 1572872 | tf_op jit(solution)/shard_map/ppermute | solution.py:137
  38.2 12.5 %collective-permute-start.9 = (bf16[2,2,2,32,1024]{4,3,2,1,0:T(8,128)(2,1)S(1)}, bf16[2,2,2,32,1024]{4,3,2,1,0:T(8,128)(2,1)S(1)}, u32[]{:S(2)}, u32[]{:S(2)}) collective-permute-start(bf16[2,2,2,32,1024]{4,3,2,1,0:T(8,128)(2,1)S(1)} %collective-permute-done.7), channel_id=1, source_target_pairs={{1,2},{2,3},{5,6},{6,7},{9,10},{10,11},{13,14},{14,15},{17,18},{18... | collective-permute-start | bytes 1572872 | tf_op jit(solution)/shard_map/ppermute | solution.py:134
  51.1 27.1 %collective-permute-start.19 = (bf16[2,2,2,2,32,1024]{5,4,3,2,0,1:T(8,128)(2,1)S(1)}, bf16[2,2,2,2,32,1024]{5,4,3,2,0,1:T(8,128)(2,1)S(1)}, u32[]{:S(2)}, u32[]{:S(2)}) collective-permute-start(bf16[2,2,2,2,32,1024]{5,4,3,2,0,1:T(8,128)(2,1)S(1)} %pad_maximum_fusion), channel_id=1, source_target_pairs={{0,16},{16,0},{1,17},{17,1},{2,18},{18,2},{3,19},{19,3},{4,20},{20... | collective-permute-start | bytes 3145736 | tf_op jit(solution)/shard_map/ppermute | solution.py:117
  51.3 11.4 %collective-permute-start.11 = (bf16[2,2,32,1024]{3,2,1,0:T(8,128)(2,1)S(1)}, bf16[2,2,32,1024]{3,2,1,0:T(8,128)(2,1)S(1)}, u32[]{:S(2)}, u32[]{:S(2)}) collective-permute-start(bf16[2,2,32,1024]{3,2,1,0:T(8,128)(2,1)S(1)} %get-tuple-element.65), channel_id=1, source_target_pairs={{1,0},{5,4},{9,8},{13,12},{17,16},{21,20},{25,24},{29,28}} | collective-permute-start | bytes 786440 | tf_op jit(solution)/shard_map/ppermute | solution.py:137
  52.6 18.3 %collective-permute-start.14 = (bf16[2,2,32,1024]{3,2,1,0:T(8,128)(2,1)S(1)}, bf16[2,2,32,1024]{3,2,1,0:T(8,128)(2,1)S(1)}, u32[]{:S(2)}, u32[]{:S(2)}) collective-permute-start(bf16[2,2,32,1024]{3,2,1,0:T(8,128)(2,1)S(1)} %get-tuple-element.28), channel_id=1, source_target_pairs={{1,0},{5,4},{9,8},{13,12},{17,16},{21,20},{25,24},{29,28}} | collective-permute-start | bytes 786440 | tf_op jit(solution)/shard_map/ppermute | solution.py:137
  54.2 16.8 %collective-permute-start.15 = (bf16[2,2,32,1024]{3,2,1,0:T(8,128)(2,1)S(1)}, bf16[2,2,32,1024]{3,2,1,0:T(8,128)(2,1)S(1)}, u32[]{:S(2)}, u32[]{:S(2)}) collective-permute-start(bf16[2,2,32,1024]{3,2,1,0:T(8,128)(2,1)S(1)} %get-tuple-element.29), channel_id=1, source_target_pairs={{2,3},{6,7},{10,11},{14,15},{18,19},{22,23},{26,27},{30,31}} | collective-permute-start | bytes 786440 | tf_op jit(solution)/shard_map/ppermute | solution.py:134
  54.9 9.1 %collective-permute-start.12 = (bf16[2,2,32,1024]{3,2,1,0:T(8,128)(2,1)S(1)}, bf16[2,2,32,1024]{3,2,1,0:T(8,128)(2,1)S(1)}, u32[]{:S(2)}, u32[]{:S(2)}) collective-permute-start(bf16[2,2,32,1024]{3,2,1,0:T(8,128)(2,1)S(1)} %get-tuple-element.63), channel_id=1, source_target_pairs={{2,3},{6,7},{10,11},{14,15},{18,19},{22,23},{26,27},{30,31}} | collective-permute-start | bytes 786440 | tf_op jit(solution)/shard_map/ppermute | solution.py:134
  62.6 15.4 %collective-permute-start.16 = (bf16[2,2,2,32,1024]{4,3,0,2,1:T(8,128)(2,1)S(1)}, bf16[2,2,2,32,1024]{4,3,0,2,1:T(8,128)(2,1)S(1)}, u32[]{:S(2)}, u32[]{:S(2)}) collective-permute-start(bf16[2,2,2,32,1024]{4,3,0,2,1:T(8,128)(2,1)S(1)} %copy_select_fusion), channel_id=1, source_target_pairs={{1,9},{2,10},{3,11},{5,13},{6,14},{7,15},{8,0},{9,1},{10,2},{12,4}... | collective-permute-start | bytes 1572872 | tf_op jit(solution)/shard_map/ppermute | solution.py:163
  64.0 11.3 %collective-permute-start.13 = (bf16[2,2,32,1024]{3,2,1,0:T(8,128)(2,1)S(1)}, bf16[2,2,32,1024]{3,2,1,0:T(8,128)(2,1)S(1)}, u32[]{:S(2)}, u32[]{:S(2)}) collective-permute-start(bf16[2,2,32,1024]{3,2,1,0:T(8,128)(2,1)S(1)} %broadcast_select_fusion.1), channel_id=1, source_target_pairs={{0,8},{4,12},{11,3},{15,7},{16,24},{20,28},{27,19},{31,23}} | collective-permute-start | bytes 786440 | tf_op jit(solution)/shard_map/ppermute | solution.py:176
  71.0 11.6 %collective-permute-start.18 = (bf16[2,2,32,1024]{3,2,1,0:T(8,128)(2,1)S(1)}, bf16[2,2,32,1024]{3,2,1,0:T(8,128)(2,1)S(1)}, u32[]{:S(2)}, u32[]{:S(2)}) collective-permute-start(bf16[2,2,32,1024]{3,2,1,0:T(8,128)(2,1)S(1)} %broadcast_select_fusion), channel_id=1, source_target_pairs={{0,8},{4,12},{11,3},{15,7},{16,24},{20,28},{27,19},{31,23}} | collective-permute-start | bytes 786440 | tf_op jit(solution)/shard_map/ppermute | solution.py:176
  87.1 14.1 %collective-permute-start.22 = (f16[2,2,2,32,1024]{4,3,2,1,0:T(8,128)(2,1)}, f16[2,2,2,32,1024]{4,3,2,1,0:T(8,128)(2,1)}, u32[]{:S(2)}, u32[]{:S(2)}) collective-permute-start(f16[2,2,2,32,1024]{4,3,2,1,0:T(8,128)(2,1)} %fusion.19), channel_id=1, source_target_pairs={{0,8},{8,0},{4,12},{12,4},{1,9},{9,1},{5,13},{13,5},{2,10},{10,2},... | collective-permute-start | bytes 1572872 | tf_op jit(solution)/shard_map/ppermute | solution.py:220
  88.2 15.4 %collective-permute-start.20 = (f16[2,2,2,32,1024]{4,3,1,0,2:T(8,128)(2,1)}, f16[2,2,2,32,1024]{4,3,1,0,2:T(8,128)(2,1)}, u32[]{:S(2)}, u32[]{:S(2)}) collective-permute-start(f16[2,2,2,32,1024]{4,3,1,0,2:T(8,128)(2,1)} %fusion.16), channel_id=1, source_target_pairs={{0,4},{4,0},{8,12},{12,8},{1,5},{5,1},{9,13},{13,9},{2,6},{6,2},{1... | collective-permute-start | bytes 1572872 | tf_op jit(solution)/shard_map/ppermute | solution.py:219
  105.0 11.2 %collective-permute-start.24 = (bf16[2,2,2,32,1024]{4,3,2,1,0:T(8,128)(2,1)S(1)}, bf16[2,2,2,32,1024]{4,3,2,1,0:T(8,128)(2,1)S(1)}, u32[]{:S(2)}, u32[]{:S(2)}) collective-permute-start(bf16[2,2,2,32,1024]{4,3,2,1,0:T(8,128)(2,1)S(1)} %pad_maximum_fusion.3), channel_id=1, source_target_pairs={{0,16},{16,0},{1,17},{17,1},{2,18},{18,2},{3,19},{19,3},{4,20},{20... | collective-permute-start | bytes 1572872 | tf_op jit(solution)/shard_map/ppermute | solution.py:117
  105.1 10.0 %collective-permute-start.23 = (f16[2,2,32,1024]{3,2,1,0:T(8,128)(2,1)}, f16[2,2,32,1024]{3,2,1,0:T(8,128)(2,1)S(1)}, u32[]{:S(2)}, u32[]{:S(2)}) collective-permute-start(f16[2,2,32,1024]{3,2,1,0:T(8,128)(2,1)} %fusion.25), channel_id=1, source_target_pairs={{0,4},{4,0},{8,12},{12,8},{1,5},{5,1},{9,13},{13,9},{2,6},{6,2},{1... | collective-permute-start | bytes 786440 | tf_op jit(solution)/shard_map/ppermute | solution.py:230
  108.1 19.4 %collective-permute-start.21 = (f16[2,2,32,1024]{3,2,1,0:T(8,128)(2,1)S(1)}, f16[2,2,32,1024]{3,2,1,0:T(8,128)(2,1)S(1)}, u32[]{:S(2)}, u32[]{:S(2)}) collective-permute-start(f16[2,2,32,1024]{3,2,1,0:T(8,128)(2,1)S(1)} %fusion.24), channel_id=1, source_target_pairs={{0,8},{8,0},{4,12},{12,4},{1,9},{9,1},{5,13},{13,5},{2,10},{10,2},... | collective-permute-start | bytes 786440 | tf_op jit(solution)/shard_map/ppermute | solution.py:229
  124.6 13.7 %collective-permute-start.27 = (f16[2,2,2,32,1024]{4,3,2,1,0:T(8,128)(2,1)S(1)}, f16[2,2,2,32,1024]{4,3,2,1,0:T(8,128)(2,1)S(1)}, u32[]{:S(2)}, u32[]{:S(2)}) collective-permute-start(f16[2,2,2,32,1024]{4,3,2,1,0:T(8,128)(2,1)S(1)} %fusion.18), channel_id=1, source_target_pairs={{0,8},{8,0},{4,12},{12,4},{1,9},{9,1},{5,13},{13,5},{2,10},{10,2},... | collective-permute-start | bytes 1572872 | tf_op jit(solution)/shard_map/ppermute | solution.py:220
  125.6 14.6 %collective-permute-start.25 = (f16[2,2,2,32,1024]{4,3,1,0,2:T(8,128)(2,1)S(1)}, f16[2,2,2,32,1024]{4,3,1,0,2:T(8,128)(2,1)S(1)}, u32[]{:S(2)}, u32[]{:S(2)}) collective-permute-start(f16[2,2,2,32,1024]{4,3,1,0,2:T(8,128)(2,1)S(1)} %fusion.17), channel_id=1, source_target_pairs={{0,4},{4,0},{8,12},{12,8},{1,5},{5,1},{9,13},{13,9},{2,6},{6,2},{1... | collective-permute-start | bytes 1572872 | tf_op jit(solution)/shard_map/ppermute | solution.py:219
  138.6 7.3 %collective-permute-start.28 = (f16[2,2,32,1024]{3,2,1,0:T(8,128)(2,1)S(1)}, f16[2,2,32,1024]{3,2,1,0:T(8,128)(2,1)S(1)}, u32[]{:S(2)}, u32[]{:S(2)}) collective-permute-start(f16[2,2,32,1024]{3,2,1,0:T(8,128)(2,1)S(1)} %fusion.27), channel_id=1, source_target_pairs={{0,4},{4,0},{8,12},{12,8},{1,5},{5,1},{9,13},{13,9},{2,6},{6,2},{1... | collective-permute-start | bytes 786440 | tf_op jit(solution)/shard_map/ppermute | solution.py:230
  140.5 6.8 %collective-permute-start.26 = (f16[2,2,32,1024]{3,2,1,0:T(8,128)(2,1)S(1)}, f16[2,2,32,1024]{3,2,1,0:T(8,128)(2,1)S(1)}, u32[]{:S(2)}, u32[]{:S(2)}) collective-permute-start(f16[2,2,32,1024]{3,2,1,0:T(8,128)(2,1)S(1)} %fusion.26), channel_id=1, source_target_pairs={{0,8},{8,0},{4,12},{12,4},{1,9},{9,1},{5,13},{13,5},{2,10},{10,2},... | collective-permute-start | bytes 786440 | tf_op jit(solution)/shard_map/ppermute | solution.py:229
  141.3 6.3 %collective-permute-start.29 = (f16[2,32,2048]{2,1,0:T(8,128)(2,1)S(1)}, f16[2,32,2048]{2,1,0:T(8,128)(2,1)S(1)}, u32[]{:S(2)}, u32[]{:S(2)}) collective-permute-start(f16[2,32,2048]{2,1,0:T(8,128)(2,1)S(1)} %get-tuple-element.59), channel_id=1, source_target_pairs={{0,16},{16,0},{1,17},{17,1},{2,18},{18,2},{3,19},{19,3},{4,20},{20... | collective-permute-start | bytes 786440 | tf_op jit(solution)/shard_map/ppermute | solution.py:238
  150.6 7.5 %collective-permute-start.32 = (f32[4,64]{1,0:T(4,128)S(1)}, f32[4,64]{1,0:T(4,128)S(1)}, u32[]{:S(2)}, u32[]{:S(2)}) collective-permute-start(f32[4,64]{1,0:T(4,128)S(1)} %get-tuple-element.67), channel_id=1, source_target_pairs={{0,2},{1,3},{2,0},{3,1},{4,6},{5,7},{6,4},{7,5},{8,10},{9,11},{10,... | collective-permute-start | bytes 3080 | tf_op jit(solution)/shard_map/ppermute | solution.py:263
  150.7 8.7 %collective-permute-start.31 = (f32[4,64]{1,0:T(4,128)S(1)}, f32[4,64]{1,0:T(4,128)S(1)}, u32[]{:S(2)}, u32[]{:S(2)}) collective-permute-start(f32[4,64]{1,0:T(4,128)S(1)} %get-tuple-element.67), channel_id=1, source_target_pairs={{0,1},{1,2},{2,3},{3,0},{4,5},{5,6},{6,7},{7,4},{8,9},{9,10},{10,1... | collective-permute-start | bytes 3080 | tf_op jit(solution)/shard_map/ppermute | solution.py:263
  158.1 3.6 %collective-permute-start.33 = (f32[4,64]{1,0:T(4,128)S(1)}, f32[4,64]{1,0:T(4,128)S(1)}, u32[]{:S(2)}, u32[]{:S(2)}) collective-permute-start(f32[4,64]{1,0:T(4,128)S(1)} %get-tuple-element.67), channel_id=1, source_target_pairs={{0,3},{1,0},{2,1},{3,2},{4,7},{5,4},{6,5},{7,6},{8,11},{9,8},{10,9... | collective-permute-start | bytes 3080 | tf_op jit(solution)/shard_map/ppermute | solution.py:263
  (17 other events, 83.5 us)

commit v11 on v10

--- a/solution.py
+++ b/solution.py
@@ -1,8 +1,6 @@
 import jax
 import jax.numpy as jnp
 from jax import lax
-from jax.experimental import pallas as pl
-from jax.experimental.pallas import tpu as pltpu
 from jax.sharding import PartitionSpec as P
 
 EPS = 1e-05
@@ -22,50 +20,6 @@
 
 def after(value, *others):
     return lax.optimization_barrier((value, *others))[0]
-
-
-def columns_kernel(place_ref, own_ref, other_ref, near_ref, far_ref, done):
-    width = near_ref.shape[1]
-    start = pl.multiple_of(place_ref[0] * width, width)
-    columns = pl.ds(start, width)
-
-    def fetch(near, far):
-        copies = [
-            pltpu.make_async_copy(near.at[:, columns], near_ref, done.at[0]),
-            pltpu.make_async_copy(far.at[:, columns], far_ref, done.at[1]),
-        ]
-        for copy in copies:
-            copy.start()
-        for copy in copies:
-            copy.wait()
-
-    @pl.when(place_ref[1] == 0)
-    def _():
-        fetch(own_ref, other_ref)
-
-    @pl.when(place_ref[1] != 0)
-    def _():
-        fetch(other_ref, own_ref)
-
-
-def half_columns(core, own_half, own, other):
-    block, columns = own.shape
-    shape = jax.ShapeDtypeStruct((block, columns // 2), own.dtype)
-    return pl.pallas_call(
-        columns_kernel,
-        in_specs=[
-            pl.BlockSpec(memory_space=pltpu.SMEM),
-            pl.BlockSpec(memory_space=pltpu.HBM),
-            pl.BlockSpec(memory_space=pltpu.HBM),
-        ],
-        out_specs=[pl.BlockSpec(memory_space=pltpu.VMEM)] * 2,
-        out_shape=[shape, shape],
-        scratch_shapes=[pltpu.SemaphoreType.DMA((2,))],
-        cost_estimate=pl.CostEstimate(
-            flops=0, bytes_accessed=4 * block * columns, transcendentals=0
-        ),
-        compiler_params=pltpu.CompilerParams(vmem_limit_bytes=48 * 1024 * 1024),
-    )(jnp.stack([core, own_half]).astype(jnp.int32), own, other)
 
 
 def on_device(hidden, norm_gain, head_weight):
@@ -116,9 +70,21 @@
     def swapped(value):
         return lax.ppermute(value, "pair", CORE_SWAP)
 
-    def dots(lefts, weight):
+    def half_columns(weight, *earlier):
+        return lax.dynamic_slice_in_dim(weight, after(core, *earlier) * width, width, 1)
+
+    def dots(lefts, own_half, weights):
         return [
-            jnp.dot(left.reshape(-1, block), weight, preferred_element_type=jnp.float32)
+            jnp.dot(
+                pick(left, own_half, 0).reshape(-1, block),
+                weights[0],
+                preferred_element_type=jnp.float32,
+            )
+            + jnp.dot(
+                pick(left, 1 - own_half, 0).reshape(-1, block),
+                weights[1],
+                preferred_element_type=jnp.float32,
+            )
             for left in lefts
         ]
 
@@ -146,12 +112,14 @@
             return part
 
         first = level // 2
-        weights = half_columns(after(core, own), core ^ first, head_weight, take)
-        scale = row_scale(*weights)
-        below[1], above[1] = after(below[1], scale, *weights), after(above[1], scale, *weights)
+        weights = lax.optimization_barrier(
+            (half_columns(head_weight, own), half_columns(take, own))
+        )
+        below[1], above[1] = after(below[1], *weights), after(above[1], *weights)
         got_near = lax.ppermute(quarter(1 - y + 2 * first, 1), "batch", Y_SWAP)
         below.append(up(below[1], 2))
         above.append(down(above[1], 2))
+        below[2], above[2] = after(below[2], got_near), after(above[2], got_near)
         near = by_y(quarter(y + 2 * first, 1), after(got_near, below[2], above[2]), 1)
         nears = (near, swapped(near))
 
@@ -162,35 +130,25 @@
         early = [pair for pair in pairs if pair not in late]
         got_early = lax.ppermute(quarter(far, 2), ("batch", "vocab"), early)
         mine_early = quarter(y + 2 * (1 - first), 2)
-        near_parts = [part.reshape(CHUNKS, -1, width) for part in dots(nears, weights[0])]
         is_late = (level == 0) & (y == 1) | (level == vocab - 1) & (y == 0)
-        ends = [
-            (
-                up(after(below[2][c], *([near] if c else [])), 3),
-                down(after(above[2][c], *([near] if c else [])), 3),
-            )
-            for c in range(CHUNKS)
-        ]
-
-        lasts = [jnp.where(level == 0, above_3, below_3) for below_3, above_3 in ends]
+        below_3, above_3 = up(below[2], 3), down(above[2], 3)
+        last = after(jnp.where(level == 0, above_3, below_3), got_early)
+        lasts = [last[c] for c in range(CHUNKS)]
         lates = [lax.ppermute(last, ("batch", "vocab"), late) for last in lasts]
 
         def parts(c, *earlier):
-            got_late = after(lates[c], *(earlier or lasts[1:]))
+            got_late = after(lates[c], *earlier)
             got = jnp.where(is_late, got_late, got_early[c])
             mine = jnp.where(is_late, lasts[c], mine_early[c])
             both = by_y(mine, got, 0)
             fars = lax.optimization_barrier((both, swapped(both)))
-            found = [
-                near_part[c] + far_part
-                for near_part, far_part in zip(near_parts, dots(fars, weights[1]))
-            ]
-            return [after(part, *lates[c + 1 :]) for part in found]
-
-        return parts, scale
+            lefts = [jnp.stack([near[c], far]) for near, far in zip(nears, fars)]
+            return [after(part, *lates[c + 1 :]) for part in dots(lefts, core ^ first, weights)]
+
+        return parts
 
     def gathered_parts():
-        weights = half_columns(core, core, head_weight, take)
+        weights = (half_columns(head_weight), half_columns(take))
 
         def parts(c, *earlier):
             whole = lax.all_gather(gained[c], "vocab", axis=2, tiled=True)
@@ -198,28 +156,30 @@
             whole = lax.all_to_all(whole, "batch", split_axis=0, concat_axis=0)
             whole = whole.reshape(2, 2, 2, 2, step, block).transpose(2, 0, 1, 3, 4, 5)
             whole = after(whole, *earlier)
-            lefts = (whole, swapped(whole))
-            return [
-                near + far
-                for near, far in zip(
-                    dots([left[0] for left in lefts], weights[0]),
-                    dots([left[1] for left in lefts], weights[1]),
-                )
-            ]
-
-        return parts, row_scale()
+            return dots((whole, swapped(whole)), core, weights)
+
+        return parts
 
     lined = depth == 2 * block and vocab == 4
-    parts, scale = line_parts() if lined else gathered_parts()
+    parts = line_parts() if lined else gathered_parts()
+    kept, sends = [], []
+    for c in range(CHUNKS):
+        whole = [part * SHRINK for part in parts(c, *(sends[-1] if c else ()))]
+        whole = jnp.stack([part.reshape(2, 2, 2, step, width) for part in whole])
+        low, high = whole[..., : width // 2], whole[..., width // 2 :]
+        kept.append((pick(low, x, 3), pick(high, y, 2)))
+        sends.append(
+            (pick(low, 1 - x, 3).astype(SUM_TYPE), pick(high, 1 - y, 2).astype(SUM_TYPE))
+        )
+    scale = row_scale(*sends[-1])
     halfway, more_sends = [], []
     for c in range(CHUNKS):
-        whole = [part * SHRINK for part in parts(c, *(more_sends[-1] if c else ()))]
-        whole = jnp.stack([part.reshape(2, 2, 2, step, width) for part in whole])
-        low, high = whole[..., : width // 2], whole[..., width // 2 :]
-        away_x = lax.ppermute(pick(low, 1 - x, 3).astype(SUM_TYPE), "batch", X_SWAP)
-        away_y = lax.ppermute(pick(high, 1 - y, 2).astype(SUM_TYPE), "batch", Y_SWAP)
-        sum_x = pick(low, x, 3) + away_x.astype(jnp.float32)
-        sum_y = pick(high, y, 2) + away_y.astype(jnp.float32)
+        away_x = lax.ppermute(sends[c][0], "batch", X_SWAP)
+        away_y = lax.ppermute(sends[c][1], "batch", Y_SWAP)
+        if c + 1 < CHUNKS:
+            away_x, away_y = after(away_x, *sends[c + 1]), after(away_y, *sends[c + 1])
+        sum_x = kept[c][0] + away_x.astype(jnp.float32)
+        sum_y = kept[c][1] + away_y.astype(jnp.float32)
         halfway.append((pick(sum_x, y, 2), pick(sum_y, x, 2)))
         more_sends.append(
             (pick(sum_x, 1 - y, 2).astype(SUM_TYPE), pick(sum_y, 1 - x, 2).astype(SUM_TYPE))

time: 164 us -> 144 us (0.88)
  waiting for transfers between devices: 67.8 us -> 47.7 us
  local copies, waits for them, and re-layouts: 7.02 us -> 17.1 us
  Pallas kernels: 6.07 us -> 0 us
  matrix products: 12.9 us -> 10.3 us
  starting transfers between devices: 51.4 us -> 48.9 us
  other arithmetic: 16.7 us -> 18.4 us
    ppermute x4, waiting for transfers between devices: 21.1 us -> 0.01 us  [the longest x2 0.01 us: on_device(): away_y = lax.ppermute(sends[c][1], 'batch', Y_SWAP)]
    ppermute x2, waiting for transfers between devices: 1.29 us -> 11.7 us  [on_device(): next_y = lax.ppermute(more_sends[c][0], 'batch', Y_SWAP)]
    ppermute x2, waiting for transfers between devices: 11 us -> 0.93 us  [on_device(): next_x = lax.ppermute(more_sends[c][1], 'batch', X_SWAP)]
    dynamic_slice x0 -> x2, local copies, waits for them, and re-layouts: none -> 9.53 us  [half_columns(): lax.dynamic_slice_in_dim(weight, after(core, *earlier) * width, width, 1)]
    pallas_call x1 -> x0, Pallas kernels: 6.07 us -> none  [half_columns(): pl.pallas_call(columns_kernel, in_specs=[pl.BlockSpec(memory_space=pltpu....]
    ppermute x3, starting transfers between devices: 7.45 us -> 2.07 us  [on_device(): lax.ppermute(own, 'vocab', [(i, (i + k) % vocab) for i in range(vocab)])]
    ppermute x4 -> x3, waiting for transfers between devices: 9.54 us -> 14.2 us  [down(): return lax.ppermute(value, 'vocab', [(z + 1, z) for z in range(vocab - k)])]
    ppermute x2, starting transfers between devices: 1.31 us -> 4.34 us  [on_device(): next_y = lax.ppermute(more_sends[c][0], 'batch', Y_SWAP)]
  transfers between devices with their start and end apart: 34 -> 32, of which waited for: 17 -> 14; matrix products, arithmetic and copies ran while one was open for 13% -> 22% of each run, Pallas kernels for 4% -> 0%
where the time goes in v11:
time: 144 us
  starting transfers between devices  48.9 us (34%)
  waiting for transfers between devices  47.7 us (33%)
  other arithmetic  18.4 us (13%)
  local copies, waits for them, and re-layouts  17.1 us (12%)
  matrix products  10.3 us (7%)
    ppermute x3, waiting for transfers between devices, down(): return lax.ppermute(value, 'vocab', [(z + 1, z) for z in range(vocab - k)])  14.2 us
    ppermute x2, waiting for transfers between devices, on_device(): next_y = lax.ppermute(more_sends[c][0], 'batch', Y_SWAP)  11.7 us
    dynamic_slice x2, local copies, waits for them, and re-layouts, half_columns(): lax.dynamic_slice_in_dim(weight, after(core, *earlier) * width, width, 1)  9.53 us
    ppermute x1, waiting for transfers between devices, line_parts(): got_near = lax.ppermute(quarter(1 - y + 2 * first, 1), 'batch', Y_SWAP)  7.15 us
    ppermute x3, starting transfers between devices, up(): lax.ppermute(value, 'vocab', [(z, z + 1) for z in range(k - 1, vocab - 1)])  6.73 us
    ppermute x2, starting transfers between devices, line_parts(): lates = [lax.ppermute(last, ('batch', 'vocab'), late) for last in lasts]  6.3 us
    ppermute x2, starting transfers between devices, on_device(): next_x = lax.ppermute(more_sends[c][1], 'batch', X_SWAP)  5.66 us
    dot_general x4, matrix products, dots(): jnp.dot(pick(left, own_half, 0).reshape(-1, block), weights[0], preferred...  5.17 us
  transfers between devices with their start and end apart: 32, of which 14 were waited for; matrix products, arithmetic and copies ran while one was open for 22% of the time, Pallas kernels for 0%

profile of v11, /device:TPU:0, one launch (start us, length us, event | category | flops | bytes accessed | tf_op | source)
XLA Modules:
  0.0 143.7 jit_solution(942644475118591533)
XLA Ops:
  3.0 2.6 %collective-permute-start = (bf16[2,2,32,1024]{3,2,0,1:T(8,128)(2,1)S(1)}, bf16[2,2,32,1024]{3,2,0,1:T(8,128)(2,1)S(1)}, u32[]{:S(2)}, u32[]{:S(2)}) collective-permute-start(bf16[2,2,32,1024]{3,2,0,1:T(8,128)(2,1)S(1)} %dynamic-slice_bitcast_fusion), channel_id=1, source_target_pairs={{0,4},{4,0},{8,12},{12,8},{1,5},{5,1},{9,13},{13,9},{2,6},{6,2},{1... | collective-permute-start | bytes 786440 | tf_op jit(solution)/shard_map/ppermute | solution.py:93
  6.8 1.6 %collective-permute-start.1 = (f32[128]{0:T(128)S(1)}, f32[128]{0:T(128)S(1)}, u32[]{:S(2)}, u32[]{:S(2)}) collective-permute-start(f32[128]{0:T(128)S(1)} %multiply_reduce_fusion), channel_id=1, source_target_pairs={{0,1},{1,0},{2,3},{3,2},{4,5},{5,4},{6,7},{7,6},{8,9},{9,8},{10,11... | collective-permute-start | bytes 1544 | tf_op jit(solution)/shard_map/ppermute | solution.py:46
  8.5 2.0 %collective-permute-done.1 = f32[128]{0:T(128)S(1)} collective-permute-done((f32[128]{0:T(128)S(1)}, f32[128]{0:T(128)S(1)}, u32[]{:S(2)}, u32[]{:S(2)}) %collective-permute-start.1) | collective-permute-done | bytes 544 | tf_op jit(solution)/shard_map/ppermute | solution.py:46
  10.4 2.6 %collective-permute-start.2 = (f32[128]{0:T(128)S(1)}, f32[128]{0:T(128)S(1)}, u32[]{:S(2)}, u32[]{:S(2)}) collective-permute-start(f32[128]{0:T(128)S(1)} %add.144), channel_id=1, source_target_pairs={{0,2},{1,3},{2,0},{3,1},{4,6},{5,7},{6,4},{7,5},{8,10},{9,11},{10,... | collective-permute-start | bytes 1544 | tf_op jit(solution)/shard_map/ppermute | solution.py:46
  13.0 1.9 %collective-permute-done.2 = f32[128]{0:T(128)S(1)} collective-permute-done((f32[128]{0:T(128)S(1)}, f32[128]{0:T(128)S(1)}, u32[]{:S(2)}, u32[]{:S(2)}) %collective-permute-start.2) | collective-permute-done | bytes 544 | tf_op jit(solution)/shard_map/ppermute | solution.py:46
  16.5 4.6 %collective-permute-start.5 = (bf16[2,2,2,32,1024]{4,3,2,1,0:T(8,128)(2,1)S(1)}, bf16[2,2,2,32,1024]{4,3,2,1,0:T(8,128)(2,1)S(1)}, u32[]{:S(2)}, u32[]{:S(2)}) collective-permute-start(bf16[2,2,2,32,1024]{4,3,2,1,0:T(8,128)(2,1)S(1)} %copy.5), channel_id=1, source_target_pairs={{0,1},{1,2},{2,3},{4,5},{5,6},{6,7},{8,9},{9,10},{10,11},{12,13},{... | collective-permute-start | bytes 1572872 | tf_op jit(solution)/shard_map/ppermute | solution.py:100
  21.1 4.8 %constant_dynamic-slice_fusion.7 = bf16[1024,2048]{1,0:T(8,128)(2,1)} fusion(bf16[1024,4096]{1,0:T(8,128)(2,1)} %param.5, s32[]{:T(128)S(6)} %select_n.271), kind=kLoop, calls=%fused_computation.162 | loop fusion | bytes 8388612 | tf_op jit(solution)/shard_map/dynamic_slice | solution.py:74
  25.9 4.7 %constant_dynamic-slice_fusion.6 = bf16[1024,2048]{1,0:T(8,128)(2,1)} fusion(bf16[1024,4096]{1,0:T(8,128)(2,1)} %collective-permute-done.4, s32[]{:T(128)S(6)} %select_n.271), kind=kLoop, calls=%fused_computation.161 | loop fusion | bytes 8388612 | tf_op jit(solution)/shard_map/dynamic_slice | solution.py:74
  30.7 1.6 %collective-permute-start.6 = (bf16[2,2,2,32,1024]{4,3,2,1,0:T(8,128)(2,1)S(1)}, bf16[2,2,2,32,1024]{4,3,2,1,0:T(8,128)(2,1)S(1)}, u32[]{:S(2)}, u32[]{:S(2)}) collective-permute-start(bf16[2,2,2,32,1024]{4,3,2,1,0:T(8,128)(2,1)S(1)} %select_select_fusion.1), channel_id=1, source_target_pairs={{0,8},{8,0},{4,12},{12,4},{1,9},{9,1},{5,13},{13,5},{2,10},{10,2},... | collective-permute-start | bytes 1572872 | tf_op jit(solution)/shard_map/ppermute | solution.py:119
  32.3 1.5 %collective-permute-start.7 = (bf16[2,2,2,32,1024]{4,3,2,1,0:T(8,128)(2,1)S(1)}, bf16[2,2,2,32,1024]{4,3,2,1,0:T(8,128)(2,1)}, u32[]{:S(2)}, u32[]{:S(2)}) collective-permute-start(bf16[2,2,2,32,1024]{4,3,2,1,0:T(8,128)(2,1)S(1)} %collective-permute-done.5), channel_id=1, source_target_pairs={{1,2},{2,3},{5,6},{6,7},{9,10},{10,11},{13,14},{14,15},{17,18},{18... | collective-permute-start | bytes 1572872 | tf_op jit(solution)/shard_map/ppermute | solution.py:100
  35.1 7.1 %collective-permute-done.6 = bf16[2,2,2,32,1024]{4,3,2,1,0:T(8,128)(2,1)S(1)} collective-permute-done((bf16[2,2,2,32,1024]{4,3,2,1,0:T(8,128)(2,1)S(1)}, bf16[2,2,2,32,1024]{4,3,2,1,0:T(8,128)(2,1)S(1)}, u32[]{:S(2)}, u32[]{:S(2)}) %collective-permute-start.6) | collective-permute-done | bytes 524320 | tf_op jit(solution)/shard_map/ppermute | solution.py:119
  42.2 7.1 %collective-permute-done.8 = bf16[2,2,2,32,1024]{4,3,2,1,0:T(8,128)(2,1)} collective-permute-done((bf16[2,2,2,32,1024]{4,3,2,1,0:T(8,128)(2,1)S(1)}, bf16[2,2,2,32,1024]{4,3,2,1,0:T(8,128)(2,1)}, u32[]{:S(2)}, u32[]{:S(2)}) %collective-permute-start.8) | collective-permute-done | bytes 524320 | tf_op jit(solution)/shard_map/ppermute | solution.py:103
  53.9 7.2 %collective-permute-done.9 = bf16[2,2,2,32,1024]{4,3,2,1,0:T(8,128)(2,1)S(1)} collective-permute-done((bf16[2,2,2,32,1024]{4,3,2,1,0:T(8,128)(2,1)}, bf16[2,2,2,32,1024]{4,3,2,1,0:T(8,128)(2,1)S(1)}, u32[]{:S(2)}, u32[]{:S(2)}) %collective-permute-start.9) | collective-permute-done | bytes 524320 | tf_op jit(solution)/shard_map/ppermute | solution.py:103
  61.1 1.9 %collective-permute-done.11 = bf16[2,2,2,32,1024]{4,3,2,1,0:T(8,128)(2,1)S(1)} collective-permute-done((bf16[2,2,2,32,1024]{4,3,2,1,0:T(8,128)(2,1)S(1)}, bf16[2,2,2,32,1024]{4,3,2,1,0:T(8,128)(2,1)S(1)}, u32[]{:S(2)}, u32[]{:S(2)}) %collective-permute-start.11) | collective-permute-done | bytes 524320 | tf_op jit(solution)/shard_map/ppermute | solution.py:131
  63.1 1.5 %collective-permute-start.12 = (bf16[2,2,32,1024]{3,2,1,0:T(8,128)(2,1)S(1)}, bf16[2,2,32,1024]{3,2,1,0:T(8,128)(2,1)S(1)}, u32[]{:S(2)}, u32[]{:S(2)}) collective-permute-start(bf16[2,2,32,1024]{3,2,1,0:T(8,128)(2,1)S(1)} %get-tuple-element.78), channel_id=1, source_target_pairs={{0,8},{4,12},{11,3},{15,7},{16,24},{20,28},{27,19},{31,23}} | collective-permute-start | bytes 786440 | tf_op jit(solution)/shard_map/ppermute | solution.py:137
  64.6 1.3 copy_select_fusion
  65.9 2.5 %collective-permute-done.12 = bf16[2,2,32,1024]{3,2,1,0:T(8,128)(2,1)S(1)} collective-permute-done((bf16[2,2,32,1024]{3,2,1,0:T(8,128)(2,1)S(1)}, bf16[2,2,32,1024]{3,2,1,0:T(8,128)(2,1)S(1)}, u32[]{:S(2)}, u32[]{:S(2)}) %collective-permute-start.12) | collective-permute-done | bytes 262176 | tf_op jit(solution)/shard_map/ppermute | solution.py:137
  69.6 4.8 %collective-permute-start.14 = (bf16[2,2,32,1024]{3,2,1,0:T(8,128)(2,1)S(1)}, bf16[2,2,32,1024]{3,2,1,0:T(8,128)(2,1)S(1)}, u32[]{:S(2)}, u32[]{:S(2)}) collective-permute-start(bf16[2,2,32,1024]{3,2,1,0:T(8,128)(2,1)S(1)} %get-tuple-element.79), channel_id=1, source_target_pairs={{0,8},{4,12},{11,3},{15,7},{16,24},{20,28},{27,19},{31,23}} | collective-permute-start | bytes 786440 | tf_op jit(solution)/shard_map/ppermute | solution.py:137
  74.4 2.1 %fusion.63 = (bf16[1,2,2,2,32,1024]{5,4,3,2,1,0:T(8,128)(2,1)}, bf16[1,2,2,2,32,1024]{5,4,3,2,1,0:T(8,128)(2,1)S(1)}) fusion(bf16[2,2,2,2,32,1024]{5,4,3,2,1,0:T(8,128)(2,1)} %collective-permute-done.15), kind=kLoop, calls=%fused_computation.187 | loop fusion | bytes 2097152 | tf_op jit(solution)/shard_map/slice | solution.py:145
  84.9 1.4 constant_dynamic-slice_fusion.5
  88.9 1.3 collective-permute-start.16
  90.2 1.6 %collective-permute-start.19 = (f16[2,2,2,32,1024]{4,3,2,1,0:T(8,128)(2,1)}, f16[2,2,2,32,1024]{4,3,2,1,0:T(8,128)(2,1)S(1)}, u32[]{:S(2)}, u32[]{:S(2)}) collective-permute-start(f16[2,2,2,32,1024]{4,3,2,1,0:T(8,128)(2,1)} %fusion.19), channel_id=1, source_target_pairs={{0,8},{8,0},{4,12},{12,4},{1,9},{9,1},{5,13},{13,5},{2,10},{10,2},... | collective-permute-start | bytes 1572872 | tf_op jit(solution)/shard_map/ppermute | solution.py:178
  91.8 2.1 %fusion.21 = (bf16[1,2,2,2,32,1024]{5,4,3,2,1,0:T(8,128)(2,1)S(1)}, bf16[1,2,2,2,32,1024]{5,4,3,2,1,0:T(8,128)(2,1)S(1)}, bf16[1,2,2,2,32,1024]{5,4,3,2,1,0:T(8,128)(2,1)S(1)}, bf16[1,2,2,2,32,1024]{5,4,3,2,1,0:T(8,128)(2,1)S(1)}) fusion(s32[]{:T(128)S(6)} %select_n.305, bf16[1,2,2,2,32,1024]{5,4,3,2,1,0:T(8,128)(2,1)} %get-tuple-element.61, ...), kind=kLoop, calls=%fused_computation.80 | loop fusion | flops 1048576 | bytes 4194312 | tf_op jit(solution)/shard_map/stack | solution.py:145
  104.0 3.8 %collective-permute-start.28 = (f32[64]{0:T(128)S(1)}, f32[64]{0:T(128)S(1)}, u32[]{:S(2)}, u32[]{:S(2)}) collective-permute-start(f32[64]{0:T(128)S(1)} %get-tuple-element.89), channel_id=1, source_target_pairs={{0,4},{4,12},{8,20},{12,28},{16,0},{20,8},{24,16},{28,24},{1,5},{5... | collective-permute-start | bytes 776 | tf_op jit(solution)/shard_map/ppermute | solution.py:57
  109.4 5.3 %collective-permute-start.20 = (f16[2,2,32,1024]{3,2,1,0:T(8,128)(2,1)S(1)}, f16[2,2,32,1024]{3,2,1,0:T(8,128)(2,1)S(1)}, u32[]{:S(2)}, u32[]{:S(2)}) collective-permute-start(f16[2,2,32,1024]{3,2,1,0:T(8,128)(2,1)S(1)} %fusion.35), channel_id=1, source_target_pairs={{0,4},{4,0},{8,12},{12,8},{1,5},{5,1},{9,13},{13,9},{2,6},{6,2},{1... | collective-permute-start | bytes 786440 | tf_op jit(solution)/shard_map/ppermute | solution.py:190
  114.7 6.5 %collective-permute-done.18 = f16[2,2,32,1024]{3,2,1,0:T(8,128)(2,1)S(1)} collective-permute-done((f16[2,2,32,1024]{3,2,1,0:T(8,128)(2,1)S(1)}, f16[2,2,32,1024]{3,2,1,0:T(8,128)(2,1)S(1)}, u32[]{:S(2)}, u32[]{:S(2)}) %collective-permute-start.18) | collective-permute-done | bytes 262176 | tf_op jit(solution)/shard_map/ppermute | solution.py:189
  121.6 3.3 %collective-permute-start.22 = (f16[2,2,32,1024]{3,2,1,0:T(8,128)(2,1)S(1)}, f16[2,2,32,1024]{3,2,1,0:T(8,128)(2,1)S(1)}, u32[]{:S(2)}, u32[]{:S(2)}) collective-permute-start(f16[2,2,32,1024]{3,2,1,0:T(8,128)(2,1)S(1)} %fusion.36), channel_id=1, source_target_pairs={{0,8},{8,0},{4,12},{12,4},{1,9},{9,1},{5,13},{13,5},{2,10},{10,2},... | collective-permute-start | bytes 786440 | tf_op jit(solution)/shard_map/ppermute | solution.py:189
  125.7 5.2 %collective-permute-done.22 = f16[2,2,32,1024]{3,2,1,0:T(8,128)(2,1)S(1)} collective-permute-done((f16[2,2,32,1024]{3,2,1,0:T(8,128)(2,1)S(1)}, f16[2,2,32,1024]{3,2,1,0:T(8,128)(2,1)S(1)}, u32[]{:S(2)}, u32[]{:S(2)}) %collective-permute-start.22) | collective-permute-done | bytes 262176 | tf_op jit(solution)/shard_map/ppermute | solution.py:189
  132.3 1.4 %collective-permute-done.26 = f16[2,32,2048]{2,1,0:T(8,128)(2,1)S(1)} collective-permute-done((f16[2,32,2048]{2,1,0:T(8,128)(2,1)S(1)}, f16[2,32,2048]{2,1,0:T(8,128)(2,1)S(1)}, u32[]{:S(2)}, u32[]{:S(2)}) %collective-permute-start.26) | collective-permute-done | bytes 262176 | tf_op jit(solution)/shard_map/ppermute | solution.py:198
  135.5 1.9 %collective-permute-start.29 = (f32[4,64]{1,0:T(4,128)S(1)}, f32[4,64]{1,0:T(4,128)S(1)}, u32[]{:S(2)}, u32[]{:S(2)}) collective-permute-start(f32[4,64]{1,0:T(4,128)S(1)} %get-tuple-element.81), channel_id=1, source_target_pairs={{0,1},{1,2},{2,3},{3,0},{4,5},{5,6},{6,7},{7,4},{8,9},{9,10},{10,1... | collective-permute-start | bytes 3080 | tf_op jit(solution)/shard_map/ppermute | solution.py:223
  137.4 1.6 %collective-permute-done.31 = f32[4,64]{1,0:T(4,128)S(1)} collective-permute-done((f32[4,64]{1,0:T(4,128)S(1)}, f32[4,64]{1,0:T(4,128)S(1)}, u32[]{:S(2)}, u32[]{:S(2)}) %collective-permute-start.31) | collective-permute-done | bytes 1056 | tf_op jit(solution)/shard_map/ppermute | solution.py:223
  139.9 1.4 collective-permute-done.29
  (140 shorter events, 42.2 us)
Async XLA Ops:
  0.6 25.3 %collective-permute-start.4 = (bf16[1024,4096]{1,0:T(8,128)(2,1)}, bf16[1024,4096]{1,0:T(8,128)(2,1)}, u32[]{:S(2)}, u32[]{:S(2)}) collective-permute-start(bf16[1024,4096]{1,0:T(8,128)(2,1)} %param.5), channel_id=1, source_target_pairs={{0,16},{16,0},{1,17},{17,1},{2,18},{18,2},{3,19},{19,3},{4,20},{20... | collective-permute-start | bytes 25165832 | tf_op jit(solution)/shard_map/ppermute | solution.py:43
  3.0 11.9 %collective-permute-start = (bf16[2,2,32,1024]{3,2,0,1:T(8,128)(2,1)S(1)}, bf16[2,2,32,1024]{3,2,0,1:T(8,128)(2,1)S(1)}, u32[]{:S(2)}, u32[]{:S(2)}) collective-permute-start(bf16[2,2,32,1024]{3,2,0,1:T(8,128)(2,1)S(1)} %dynamic-slice_bitcast_fusion), channel_id=1, source_target_pairs={{0,4},{4,0},{8,12},{12,8},{1,5},{5,1},{9,13},{13,9},{2,6},{6,2},{1... | collective-permute-start | bytes 786440 | tf_op jit(solution)/shard_map/ppermute | solution.py:93
  6.8 3.6 %collective-permute-start.1 = (f32[128]{0:T(128)S(1)}, f32[128]{0:T(128)S(1)}, u32[]{:S(2)}, u32[]{:S(2)}) collective-permute-start(f32[128]{0:T(128)S(1)} %multiply_reduce_fusion), channel_id=1, source_target_pairs={{0,1},{1,0},{2,3},{3,2},{4,5},{5,4},{6,7},{7,6},{8,9},{9,8},{10,11... | collective-permute-start | bytes 1544 | tf_op jit(solution)/shard_map/ppermute | solution.py:46
  10.4 4.4 %collective-permute-start.2 = (f32[128]{0:T(128)S(1)}, f32[128]{0:T(128)S(1)}, u32[]{:S(2)}, u32[]{:S(2)}) collective-permute-start(f32[128]{0:T(128)S(1)} %add.144), channel_id=1, source_target_pairs={{0,2},{1,3},{2,0},{3,1},{4,6},{5,7},{6,4},{7,5},{8,10},{9,11},{10,... | collective-permute-start | bytes 1544 | tf_op jit(solution)/shard_map/ppermute | solution.py:46
  15.2 15.4 %collective-permute-start.3 = (bf16[2,2,2,32,1024]{4,3,2,1,0:T(8,128)(2,1)S(1)}, bf16[2,2,2,32,1024]{4,3,2,1,0:T(8,128)(2,1)S(1)}, u32[]{:S(2)}, u32[]{:S(2)}) collective-permute-start(bf16[2,2,2,32,1024]{4,3,2,1,0:T(8,128)(2,1)S(1)} %copy.5), channel_id=1, source_target_pairs={{1,0},{2,1},{3,2},{5,4},{6,5},{7,6},{9,8},{10,9},{11,10},{13,12},{... | collective-permute-start | bytes 1572872 | tf_op jit(solution)/shard_map/ppermute | solution.py:103
  16.5 14.1 %collective-permute-start.5 = (bf16[2,2,2,32,1024]{4,3,2,1,0:T(8,128)(2,1)S(1)}, bf16[2,2,2,32,1024]{4,3,2,1,0:T(8,128)(2,1)S(1)}, u32[]{:S(2)}, u32[]{:S(2)}) collective-permute-start(bf16[2,2,2,32,1024]{4,3,2,1,0:T(8,128)(2,1)S(1)} %copy.5), channel_id=1, source_target_pairs={{0,1},{1,2},{2,3},{4,5},{5,6},{6,7},{8,9},{9,10},{10,11},{12,13},{... | collective-permute-start | bytes 1572872 | tf_op jit(solution)/shard_map/ppermute | solution.py:100
  30.7 11.5 %collective-permute-start.6 = (bf16[2,2,2,32,1024]{4,3,2,1,0:T(8,128)(2,1)S(1)}, bf16[2,2,2,32,1024]{4,3,2,1,0:T(8,128)(2,1)S(1)}, u32[]{:S(2)}, u32[]{:S(2)}) collective-permute-start(bf16[2,2,2,32,1024]{4,3,2,1,0:T(8,128)(2,1)S(1)} %select_select_fusion.1), channel_id=1, source_target_pairs={{0,8},{8,0},{4,12},{12,4},{1,9},{9,1},{5,13},{13,5},{2,10},{10,2},... | collective-permute-start | bytes 1572872 | tf_op jit(solution)/shard_map/ppermute | solution.py:119
  32.3 9.9 %collective-permute-start.7 = (bf16[2,2,2,32,1024]{4,3,2,1,0:T(8,128)(2,1)S(1)}, bf16[2,2,2,32,1024]{4,3,2,1,0:T(8,128)(2,1)}, u32[]{:S(2)}, u32[]{:S(2)}) collective-permute-start(bf16[2,2,2,32,1024]{4,3,2,1,0:T(8,128)(2,1)S(1)} %collective-permute-done.5), channel_id=1, source_target_pairs={{1,2},{2,3},{5,6},{6,7},{9,10},{10,11},{13,14},{14,15},{17,18},{18... | collective-permute-start | bytes 1572872 | tf_op jit(solution)/shard_map/ppermute | solution.py:100
  33.7 15.6 %collective-permute-start.8 = (bf16[2,2,2,32,1024]{4,3,2,1,0:T(8,128)(2,1)S(1)}, bf16[2,2,2,32,1024]{4,3,2,1,0:T(8,128)(2,1)}, u32[]{:S(2)}, u32[]{:S(2)}) collective-permute-start(bf16[2,2,2,32,1024]{4,3,2,1,0:T(8,128)(2,1)S(1)} %collective-permute-done.3), channel_id=1, source_target_pairs={{1,0},{2,1},{5,4},{6,5},{9,8},{10,9},{13,12},{14,13},{17,16},{18,1... | collective-permute-start | bytes 1572872 | tf_op jit(solution)/shard_map/ppermute | solution.py:103
  49.3 11.8 %collective-permute-start.9 = (bf16[2,2,2,32,1024]{4,3,2,1,0:T(8,128)(2,1)}, bf16[2,2,2,32,1024]{4,3,2,1,0:T(8,128)(2,1)S(1)}, u32[]{:S(2)}, u32[]{:S(2)}) collective-permute-start(bf16[2,2,2,32,1024]{4,3,2,1,0:T(8,128)(2,1)} %collective-permute-done.8), channel_id=1, source_target_pairs={{1,0},{5,4},{9,8},{13,12},{17,16},{21,20},{25,24},{29,28}} | collective-permute-start | bytes 1572872 | tf_op jit(solution)/shard_map/ppermute | solution.py:103
  50.6 10.5 %collective-permute-start.10 = (bf16[2,2,2,32,1024]{4,3,2,1,0:T(8,128)(2,1)}, bf16[2,2,2,32,1024]{4,3,2,1,0:T(8,128)(2,1)S(1)}, u32[]{:S(2)}, u32[]{:S(2)}) collective-permute-start(bf16[2,2,2,32,1024]{4,3,2,1,0:T(8,128)(2,1)} %collective-permute-done.7), channel_id=1, source_target_pairs={{2,3},{6,7},{10,11},{14,15},{18,19},{22,23},{26,27},{30,31}} | collective-permute-start | bytes 1572872 | tf_op jit(solution)/shard_map/ppermute | solution.py:100
  51.5 11.6 %collective-permute-start.11 = (bf16[2,2,2,32,1024]{4,3,2,1,0:T(8,128)(2,1)S(1)}, bf16[2,2,2,32,1024]{4,3,2,1,0:T(8,128)(2,1)S(1)}, u32[]{:S(2)}, u32[]{:S(2)}) collective-permute-start(bf16[2,2,2,32,1024]{4,3,2,1,0:T(8,128)(2,1)S(1)} %get-tuple-element.54), channel_id=1, source_target_pairs={{1,9},{2,10},{3,11},{5,13},{6,14},{7,15},{8,0},{9,1},{10,2},{12,4}... | collective-permute-start | bytes 1572872 | tf_op jit(solution)/shard_map/ppermute | solution.py:131
  53.9 20.5 %collective-permute-start.15 = (bf16[2,2,2,2,32,1024]{5,4,3,2,1,0:T(8,128)(2,1)}, bf16[2,2,2,2,32,1024]{5,4,3,2,1,0:T(8,128)(2,1)}, u32[]{:S(2)}, u32[]{:S(2)}) collective-permute-start(bf16[2,2,2,2,32,1024]{5,4,3,2,1,0:T(8,128)(2,1)} %pad_maximum_fusion), channel_id=1, source_target_pairs={{0,16},{16,0},{1,17},{17,1},{2,18},{18,2},{3,19},{19,3},{4,20},{20... | collective-permute-start | bytes 3145736 | tf_op jit(solution)/shard_map/ppermute | solution.py:71
  63.1 5.3 %collective-permute-start.12 = (bf16[2,2,32,1024]{3,2,1,0:T(8,128)(2,1)S(1)}, bf16[2,2,32,1024]{3,2,1,0:T(8,128)(2,1)S(1)}, u32[]{:S(2)}, u32[]{:S(2)}) collective-permute-start(bf16[2,2,32,1024]{3,2,1,0:T(8,128)(2,1)S(1)} %get-tuple-element.78), channel_id=1, source_target_pairs={{0,8},{4,12},{11,3},{15,7},{16,24},{20,28},{27,19},{31,23}} | collective-permute-start | bytes 786440 | tf_op jit(solution)/shard_map/ppermute | solution.py:137
  68.6 7.9 %collective-permute-start.13 = (bf16[2,2,2,32,1024]{4,3,2,1,0:T(8,128)(2,1)S(1)}, bf16[2,2,2,32,1024]{4,3,2,1,0:T(8,128)(2,1)S(1)}, u32[]{:S(2)}, u32[]{:S(2)}) collective-permute-start(bf16[2,2,2,32,1024]{4,3,2,1,0:T(8,128)(2,1)S(1)} %pad_maximum_fusion.2), channel_id=1, source_target_pairs={{0,16},{16,0},{1,17},{17,1},{2,18},{18,2},{3,19},{19,3},{4,20},{20... | collective-permute-start | bytes 1572872 | tf_op jit(solution)/shard_map/ppermute | solution.py:71
  69.6 10.8 %collective-permute-start.14 = (bf16[2,2,32,1024]{3,2,1,0:T(8,128)(2,1)S(1)}, bf16[2,2,32,1024]{3,2,1,0:T(8,128)(2,1)S(1)}, u32[]{:S(2)}, u32[]{:S(2)}) collective-permute-start(bf16[2,2,32,1024]{3,2,1,0:T(8,128)(2,1)S(1)} %get-tuple-element.79), channel_id=1, source_target_pairs={{0,8},{4,12},{11,3},{15,7},{16,24},{20,28},{27,19},{31,23}} | collective-permute-start | bytes 786440 | tf_op jit(solution)/shard_map/ppermute | solution.py:137
  88.7 3.1 %collective-permute-start.17 = (bf16[2,2,2,32,1024]{4,3,2,1,0:T(8,128)(2,1)S(1)}, bf16[2,2,2,32,1024]{4,3,2,1,0:T(8,128)(2,1)}, u32[]{:S(2)}, u32[]{:S(2)}) collective-permute-start(bf16[2,2,2,32,1024]{4,3,2,1,0:T(8,128)(2,1)S(1)} %pad_maximum_fusion.3), channel_id=1, source_target_pairs={{0,16},{16,0},{1,17},{17,1},{2,18},{18,2},{3,19},{19,3},{4,20},{20... | collective-permute-start | bytes 1572872 | tf_op jit(solution)/shard_map/ppermute | solution.py:71
  88.9 15.1 %collective-permute-start.16 = (f16[2,2,2,32,1024]{4,3,1,0,2:T(8,128)(2,1)}, f16[2,2,2,32,1024]{4,3,1,0,2:T(8,128)(2,1)S(1)}, u32[]{:S(2)}, u32[]{:S(2)}) collective-permute-start(f16[2,2,2,32,1024]{4,3,1,0,2:T(8,128)(2,1)} %fusion.16), channel_id=1, source_target_pairs={{0,4},{4,0},{8,12},{12,8},{1,5},{5,1},{9,13},{13,9},{2,6},{6,2},{1... | collective-permute-start | bytes 1572872 | tf_op jit(solution)/shard_map/ppermute | solution.py:177
  90.2 17.9 %collective-permute-start.19 = (f16[2,2,2,32,1024]{4,3,2,1,0:T(8,128)(2,1)}, f16[2,2,2,32,1024]{4,3,2,1,0:T(8,128)(2,1)S(1)}, u32[]{:S(2)}, u32[]{:S(2)}) collective-permute-start(f16[2,2,2,32,1024]{4,3,2,1,0:T(8,128)(2,1)} %fusion.19), channel_id=1, source_target_pairs={{0,8},{8,0},{4,12},{12,4},{1,9},{9,1},{5,13},{13,5},{2,10},{10,2},... | collective-permute-start | bytes 1572872 | tf_op jit(solution)/shard_map/ppermute | solution.py:178
  101.3 20.0 %collective-permute-start.21 = (f16[2,2,2,32,1024]{4,3,1,0,2:T(8,128)(2,1)S(1)}, f16[2,2,2,32,1024]{4,3,1,0,2:T(8,128)(2,1)S(1)}, u32[]{:S(2)}, u32[]{:S(2)}) collective-permute-start(f16[2,2,2,32,1024]{4,3,1,0,2:T(8,128)(2,1)S(1)} %fusion.17), channel_id=1, source_target_pairs={{0,4},{4,0},{8,12},{12,8},{1,5},{5,1},{9,13},{13,9},{2,6},{6,2},{1... | collective-permute-start | bytes 1572872 | tf_op jit(solution)/shard_map/ppermute | solution.py:177
  102.1 22.8 %collective-permute-start.23 = (f16[2,2,2,32,1024]{4,3,2,1,0:T(8,128)(2,1)S(1)}, f16[2,2,2,32,1024]{4,3,2,1,0:T(8,128)(2,1)S(1)}, u32[]{:S(2)}, u32[]{:S(2)}) collective-permute-start(f16[2,2,2,32,1024]{4,3,2,1,0:T(8,128)(2,1)S(1)} %fusion.18), channel_id=1, source_target_pairs={{0,8},{8,0},{4,12},{12,4},{1,9},{9,1},{5,13},{13,5},{2,10},{10,2},... | collective-permute-start | bytes 1572872 | tf_op jit(solution)/shard_map/ppermute | solution.py:178
  103.3 6.0 %collective-permute-start.27 = (f32[64]{0:T(128)S(1)}, f32[64]{0:T(128)S(1)}, u32[]{:S(2)}, u32[]{:S(2)}) collective-permute-start(f32[64]{0:T(128)S(1)} %get-tuple-element.88), channel_id=1, source_target_pairs={{0,0},{4,8},{8,16},{12,24},{16,4},{20,12},{24,20},{28,28},{1,1},{5... | collective-permute-start | bytes 776 | tf_op jit(solution)/shard_map/ppermute | solution.py:57
  104.0 10.7 %collective-permute-start.28 = (f32[64]{0:T(128)S(1)}, f32[64]{0:T(128)S(1)}, u32[]{:S(2)}, u32[]{:S(2)}) collective-permute-start(f32[64]{0:T(128)S(1)} %get-tuple-element.89), channel_id=1, source_target_pairs={{0,4},{4,12},{8,20},{12,28},{16,0},{20,8},{24,16},{28,24},{1,5},{5... | collective-permute-start | bytes 776 | tf_op jit(solution)/shard_map/ppermute | solution.py:57
  108.1 13.1 %collective-permute-start.18 = (f16[2,2,32,1024]{3,2,1,0:T(8,128)(2,1)S(1)}, f16[2,2,32,1024]{3,2,1,0:T(8,128)(2,1)S(1)}, u32[]{:S(2)}, u32[]{:S(2)}) collective-permute-start(f16[2,2,32,1024]{3,2,1,0:T(8,128)(2,1)S(1)} %fusion.34), channel_id=1, source_target_pairs={{0,8},{8,0},{4,12},{12,4},{1,9},{9,1},{5,13},{13,5},{2,10},{10,2},... | collective-permute-start | bytes 786440 | tf_op jit(solution)/shard_map/ppermute | solution.py:189
  109.4 11.9 %collective-permute-start.20 = (f16[2,2,32,1024]{3,2,1,0:T(8,128)(2,1)S(1)}, f16[2,2,32,1024]{3,2,1,0:T(8,128)(2,1)S(1)}, u32[]{:S(2)}, u32[]{:S(2)}) collective-permute-start(f16[2,2,32,1024]{3,2,1,0:T(8,128)(2,1)S(1)} %fusion.35), channel_id=1, source_target_pairs={{0,4},{4,0},{8,12},{12,8},{1,5},{5,1},{9,13},{13,9},{2,6},{6,2},{1... | collective-permute-start | bytes 786440 | tf_op jit(solution)/shard_map/ppermute | solution.py:190
  121.6 9.3 %collective-permute-start.22 = (f16[2,2,32,1024]{3,2,1,0:T(8,128)(2,1)S(1)}, f16[2,2,32,1024]{3,2,1,0:T(8,128)(2,1)S(1)}, u32[]{:S(2)}, u32[]{:S(2)}) collective-permute-start(f16[2,2,32,1024]{3,2,1,0:T(8,128)(2,1)S(1)} %fusion.36), channel_id=1, source_target_pairs={{0,8},{8,0},{4,12},{12,4},{1,9},{9,1},{5,13},{13,5},{2,10},{10,2},... | collective-permute-start | bytes 786440 | tf_op jit(solution)/shard_map/ppermute | solution.py:189
  125.1 6.8 %collective-permute-start.24 = (f16[2,2,32,1024]{3,2,1,0:T(8,128)(2,1)S(1)}, f16[2,2,32,1024]{3,2,1,0:T(8,128)(2,1)S(1)}, u32[]{:S(2)}, u32[]{:S(2)}) collective-permute-start(f16[2,2,32,1024]{3,2,1,0:T(8,128)(2,1)S(1)} %fusion.37), channel_id=1, source_target_pairs={{0,4},{4,0},{8,12},{12,8},{1,5},{5,1},{9,13},{13,9},{2,6},{6,2},{1... | collective-permute-start | bytes 786440 | tf_op jit(solution)/shard_map/ppermute | solution.py:190
  125.6 6.7 %collective-permute-start.25 = (f16[2,32,2048]{2,1,0:T(8,128)(2,1)S(1)}, f16[2,32,2048]{2,1,0:T(8,128)(2,1)S(1)}, u32[]{:S(2)}, u32[]{:S(2)}) collective-permute-start(f16[2,32,2048]{2,1,0:T(8,128)(2,1)S(1)} %get-tuple-element.75), channel_id=1, source_target_pairs={{0,16},{16,0},{1,17},{17,1},{2,18},{18,2},{3,19},{19,3},{4,20},{20... | collective-permute-start | bytes 786440 | tf_op jit(solution)/shard_map/ppermute | solution.py:198
  132.2 1.6 %collective-permute-start.26 = (f16[2,32,2048]{2,1,0:T(8,128)(2,1)S(1)}, f16[2,32,2048]{2,1,0:T(8,128)(2,1)S(1)}, u32[]{:S(2)}, u32[]{:S(2)}) collective-permute-start(f16[2,32,2048]{2,1,0:T(8,128)(2,1)S(1)} %get-tuple-element.77), channel_id=1, source_target_pairs={{0,16},{16,0},{1,17},{17,1},{2,18},{18,2},{3,19},{19,3},{4,20},{20... | collective-permute-start | bytes 786440 | tf_op jit(solution)/shard_map/ppermute | solution.py:198
  135.3 3.6 %collective-permute-start.31 = (f32[4,64]{1,0:T(4,128)S(1)}, f32[4,64]{1,0:T(4,128)S(1)}, u32[]{:S(2)}, u32[]{:S(2)}) collective-permute-start(f32[4,64]{1,0:T(4,128)S(1)} %get-tuple-element.81), channel_id=1, source_target_pairs={{0,3},{1,0},{2,1},{3,2},{4,7},{5,4},{6,5},{7,6},{8,11},{9,8},{10,9... | collective-permute-start | bytes 3080 | tf_op jit(solution)/shard_map/ppermute | solution.py:223
  135.5 4.5 %collective-permute-start.30 = (f32[4,64]{1,0:T(4,128)S(1)}, f32[4,64]{1,0:T(4,128)S(1)}, u32[]{:S(2)}, u32[]{:S(2)}) collective-permute-start(f32[4,64]{1,0:T(4,128)S(1)} %get-tuple-element.81), channel_id=1, source_target_pairs={{0,2},{1,3},{2,0},{3,1},{4,6},{5,7},{6,4},{7,5},{8,10},{9,11},{10,... | collective-permute-start | bytes 3080 | tf_op jit(solution)/shard_map/ppermute | solution.py:223
  135.5 5.9 %collective-permute-start.29 = (f32[4,64]{1,0:T(4,128)S(1)}, f32[4,64]{1,0:T(4,128)S(1)}, u32[]{:S(2)}, u32[]{:S(2)}) collective-permute-start(f32[4,64]{1,0:T(4,128)S(1)} %get-tuple-element.81), channel_id=1, source_target_pairs={{0,1},{1,2},{2,3},{3,0},{4,5},{5,6},{6,7},{7,4},{8,9},{9,10},{10,1... | collective-permute-start | bytes 3080 | tf_op jit(solution)/shard_map/ppermute | solution.py:223
  (14 other events, 47.7 us)

commit v12 on v11

v12 whole, which is shorter than its diff:
```python
import jax
import jax.numpy as jnp
from jax import lax
from jax.sharding import PartitionSpec as P

EPS = 1e-05
GUIDE = 1.5
SHRINK = 1.0 / 32.0
SUM_TYPE = jnp.float16

X_SWAP = [(0, 1), (1, 0), (2, 3), (3, 2)]
Y_SWAP = [(0, 2), (2, 0), (1, 3), (3, 1)]
CORE_SWAP = [(0, 1), (1, 0)]


def pick(array, index, axis):
    return lax.dynamic_index_in_dim(array, index, axis, keepdims=False)


def after(value, *others):
    return lax.optimization_barrier((value, *others))[0]


def on_device(hidden, norm_gain, head_weight):
    core = lax.axis_index("pair")
    place = lax.axis_index("batch")
    level = lax.axis_index("vocab")
    vocab = lax.axis_size("vocab")
    y, x = place // 2, place % 2
    rows = hidden[0]
    seg = rows.shape[0] // 2
    depth = rows.shape[1]
    block, columns = head_weight.shape
    width = columns // 2
    model = depth * vocab

    wide = rows.astype(jnp.float32)
    gained = (wide * norm_gain.astype(jnp.float32)[None, :]).astype(jnp.bfloat16)
    gained = gained.reshape(2, seg, depth)

    take = lax.ppermute(head_weight, "pair", CORE_SWAP)

    def paired(value, reach):
        return lax.ppermute(value, "vocab", [(i, i ^ reach) for i in range(vocab)])

    squares = jnp.sum(wide * wide, axis=1)
    reach = 1
    while reach < vocab:
        squares += paired(squares, reach)
        reach *= 2
    squares = squares.reshape(2, seg)

    def row_scale(*earlier):
        sent = [
            lax.ppermute(
                pick(after(squares, *earlier), core ^ k, 0),
                ("pair", "batch"),
                [(4 * s + b, 2 * b + (s ^ k)) for s in range(2) for b in range(4)],
            )
            for k in range(2)
        ]
        total = jnp.stack([jnp.where(x == 0, sent[0], sent[1]), jnp.where(x == 0, sent[1], sent[0])])
        return lax.rsqrt(total / model + EPS) / SHRINK

    def by_y(mine, other, axis):
        return jnp.stack([jnp.where(y == 0, mine, other), jnp.where(y == 0, other, mine)], axis)

    def swapped(value):
        return lax.ppermute(value, "pair", CORE_SWAP)

    def half_columns(weight, *earlier):
        return lax.dynamic_slice_in_dim(weight, after(core, *earlier) * width, width, 1)

    def dot(left, weight):
        return jnp.dot(left.reshape(-1, block), weight, preferred_element_type=jnp.float32)

    def line_parts():
        mine = lax.dynamic_slice_in_dim(gained, x * block, block, 2)
        other = lax.ppermute(
            lax.dynamic_slice_in_dim(gained, (1 - x) * block, block, 2), "batch", X_SWAP
        )
        own = jnp.stack([jnp.where(x == 0, mine, other), jnp.where(x == 0, other, mine)])
        own = after(own, squares)

        def up(value, k):
            return lax.ppermute(value, "vocab", [(z, z + 1) for z in range(k - 1, vocab - 1)])

        def down(value, k):
            return lax.ppermute(value, "vocab", [(z + 1, z) for z in range(vocab - k)])

        below, above = [own, up(own, 1)], [own, down(own, 1)]

        def quarter(place, reach):
            part = own
            for k in range(1, reach + 1):
                part = jnp.where(level - place == k, below[k], part)
                part = jnp.where(place - level == k, above[k], part)
            return part

        first = level // 2
        scale = row_scale(own)
        below[1], above[1] = after(below[1], scale), after(above[1], scale)
        near_sent = quarter(1 - y + 2 * first, 1)
        got_near = lax.ppermute(near_sent, "batch", Y_SWAP)
        below.append(up(below[1], 2))
        above.append(down(above[1], 2))
        keep_near = (core ^ first) == 0
        kept, taken = half_columns(head_weight, near_sent), half_columns(take, near_sent)
        near_weight, far_weight = lax.optimization_barrier(
            (jnp.where(keep_near, kept, taken), jnp.where(keep_near, taken, kept))
        )
        ready = (got_near, near_weight, far_weight)
        below[2], above[2] = after(below[2], *ready), after(above[2], *ready)
        near = by_y(quarter(y + 2 * first, 1), after(got_near, below[2], above[2]), 0)
        swapped_near = swapped(near)

        far = 1 - y + 2 * (1 - first)
        tips = [(0, 0), (1, vocab - 1)]
        pairs = [(b * vocab + z, (b ^ 2) * vocab + z) for b in range(4) for z in range(vocab)]
        late = [pair for pair in pairs if (pair[0] // vocab // 2, pair[0] % vocab) in tips]
        early = [pair for pair in pairs if pair not in late]
        got_early = lax.ppermute(quarter(far, 2), ("batch", "vocab"), early)
        mine_early = quarter(y + 2 * (1 - first), 2)
        is_late = (level == 0) & (y == 1) | (level == vocab - 1) & (y == 0)
        below_3, above_3 = up(below[2], 3), down(above[2], 3)
        near_part = dot(near, near_weight)
        last = after(jnp.where(level == 0, above_3, below_3), got_early, near_part)
        got_late = lax.ppermute(last, ("batch", "vocab"), late)
        far = by_y(
            jnp.where(is_late, last, mine_early), jnp.where(is_late, got_late, got_early), 0
        )
        swapped_far = swapped(far)

        def own_part():
            return near_part + dot(far, far_weight)

        def other_part(*earlier):
            left = after(swapped_far, *earlier)
            return dot(swapped_near, near_weight) + dot(left, far_weight)

        return (own_part, other_part), scale

    def gathered_parts():
        near_weight, far_weight = half_columns(head_weight), half_columns(take)
        whole = lax.all_gather(gained, "vocab", axis=2, tiled=True)
        whole = whole.reshape(2, seg, 2, 4, block).transpose(3, 2, 0, 1, 4)
        whole = lax.all_to_all(whole, "batch", split_axis=0, concat_axis=0)
        whole = whole.reshape(2, 2, 2, 2, seg, block).transpose(2, 0, 1, 3, 4, 5)
        swapped_whole = swapped(whole)

        def part(left):
            return dot(pick(left, core, 0), near_weight) + dot(pick(left, 1 - core, 0), far_weight)

        return (lambda: part(whole), lambda *earlier: part(after(swapped_whole, *earlier))), row_scale()

    lined = depth == 2 * block and vocab == 4
    parts, scale = line_parts() if lined else gathered_parts()
    kept, sends = [], []
    for part in parts:
        whole = (part(*(sends[-1] if sends else ())) * SHRINK).reshape(2, 2, 2, seg, width)
        low, high = whole[..., : width // 2], whole[..., width // 2 :]
        kept.append((pick(low, x, 2), pick(high, y, 1)))
        sends.append(
            (pick(low, 1 - x, 2).astype(SUM_TYPE), pick(high, 1 - y, 1).astype(SUM_TYPE))
        )
    halfway, more_sends = [], []
    for i in range(2):
        away_x = lax.ppermute(sends[i][0], "batch", X_SWAP)
        away_y = lax.ppermute(sends[i][1], "batch", Y_SWAP)
        if i == 0:
            away_x, away_y = after(away_x, *sends[1]), after(away_y, *sends[1])
        sum_x = kept[i][0] + away_x.astype(jnp.float32)
        sum_y = kept[i][1] + away_y.astype(jnp.float32)
        halfway.append((pick(sum_x, y, 1), pick(sum_y, x, 1)))
        more_sends.append(
            (pick(sum_x, 1 - y, 1).astype(SUM_TYPE), pick(sum_y, 1 - x, 1).astype(SUM_TYPE))
        )
    mine, theirs = [], []
    for i in range(2):
        next_y = lax.ppermute(more_sends[i][0], "batch", Y_SWAP)
        next_x = lax.ppermute(more_sends[i][1], "batch", X_SWAP)
        if i == 0:
            next_y, next_x = after(next_y, *more_sends[1]), after(next_x, *more_sends[1])
        sums = jnp.concatenate(
            [
                halfway[i][0] + next_y.astype(jnp.float32),
                halfway[i][1] + next_x.astype(jnp.float32),
            ],
            axis=-1,
        ).astype(SUM_TYPE)
        mine.append(pick(sums, core, 0))
        theirs.append(swapped(pick(sums, 1 - core, 0)))

    def scores(own, other, got_own, got_other, gain):
        low = jnp.where(core == 0, own, got_own)
        high = jnp.where(core == 0, got_other, other)
        return jnp.concatenate([low, high], axis=1).astype(jnp.float32) * gain[:, None]

    cond = scores(mine[0], mine[1], theirs[0], theirs[1], scale[0])
    uncond = scores(mine[1], mine[0], theirs[1], theirs[0], scale[1])
    guided = GUIDE * cond + (1.0 - GUIDE) * uncond

    def stats(values):
        peak = jnp.max(values, axis=1)
        return peak, jnp.sum(jnp.exp(values - peak[:, None]), axis=1)

    peak_c, sum_c = stats(cond)
    peak_g, sum_g = stats(guided)
    own = jnp.stack([peak_c, peak_g, sum_c, sum_g])
    every = jnp.stack(
        [own]
        + [
            lax.ppermute(own, "vocab", [(i, (i + k) % vocab) for i in range(vocab)])
            for k in range(1, vocab)
        ]
    )
    top = jnp.max(every[:, :2], axis=0)
    total = jnp.sum(every[:, 2:] * jnp.exp(every[:, :2] - top[None]), axis=0)
    norm = top + jnp.log(total)
    return (guided - norm[1][:, None], cond - norm[0][:, None])


def solution(mesh):
    in_specs = (P("pair", "batch", "vocab"), P("vocab"), P(("pair", "batch"), "vocab"))
    out_specs = (P(("pair", "batch"), "vocab"), P(("pair", "batch"), "vocab"))
    return jax.shard_map(
        on_device, mesh=mesh, in_specs=in_specs, out_specs=out_specs, check_vma=False
    )
```

time: 144 us -> 127 us (0.88)
  local copies, waits for them, and re-layouts: 17.1 us -> 1.77 us
  starting transfers between devices: 48.9 us -> 40.7 us
  waiting for transfers between devices: 47.7 us -> 51.1 us
  other arithmetic: 18.4 us -> 20.1 us
    dynamic_slice x3 -> x1, local copies, waits for them, and re-layouts: 9.56 us -> 0.03 us  [line_parts(): lax.dynamic_slice_in_dim(gained, (1 - x) * block, block, 2)]
    ppermute x14 -> x11, starting transfers between devices: 25.5 us -> 16.8 us  [the longest x2 2.9 us: on_device(): next_x = lax.ppermute(more_sends[i][1], 'batch', X_SWAP)]
    select_n x1 -> x3, other arithmetic: 0.06 us -> 8.37 us  [the longest x1 8.17 us: line_parts(): jnp.where(keep_near, taken, kept)]
    ppermute x14 -> x11, waiting for transfers between devices: 23.8 us -> 27.6 us  [the longest x2 11.7 us: on_device(): away_y = lax.ppermute(sends[i][1], 'batch', Y_SWAP)]
    unnamed x29 -> x10, local copies, waits for them, and re-layouts: 3.66 us -> 0.02 us
    another operation x11 -> x6, other arithmetic: 3.86 us -> 0.52 us  [the longest x3 2.91 us: parts(): lefts = [jnp.stack([near[c], far]) for near, far in zip(nears, fars)]]
    ppermute x3, waiting for transfers between devices: 14.2 us -> 11.1 us  [down(): return lax.ppermute(value, 'vocab', [(z + 1, z) for z in range(vocab - k)])]
    ppermute x3, waiting for transfers between devices: 0.01 us -> 1.86 us  [up(): lax.ppermute(value, 'vocab', [(z, z + 1) for z in range(k - 1, vocab - 1)])]
  transfers between devices with their start and end apart: 32 -> 30, of which waited for: 14 -> 18; matrix products, arithmetic and copies ran while one was open for 22% -> 24% of each run, Pallas kernels for 0% -> 0%
where the time goes in v12:
time: 127 us; the launch traced here: 126 us
  waiting for transfers between devices  51.1 us (40%)
  starting transfers between devices  40.7 us (32%)
  other arithmetic  20.1 us (16%)
  matrix products  11.5 us (9%)
  local copies, waits for them, and re-layouts  1.77 us (1%)
    ppermute x2, waiting for transfers between devices, on_device(): away_y = lax.ppermute(sends[i][1], 'batch', Y_SWAP)  11.7 us
    dot_general x4, matrix products, dot(): jnp.dot(left.reshape(-1, block), weight, preferred_element_type=jnp.float32)  11.5 us
    ppermute x3, waiting for transfers between devices, down(): return lax.ppermute(value, 'vocab', [(z + 1, z) for z in range(vocab - k)])  11.1 us
    ppermute x2, waiting for transfers between devices, on_device(): next_x = lax.ppermute(more_sends[i][1], 'batch', X_SWAP)  8.54 us
    select_n x1, other arithmetic, line_parts(): jnp.where(keep_near, taken, kept)  8.17 us
    ppermute x1, waiting for transfers between devices, line_parts(): got_late = lax.ppermute(last, ('batch', 'vocab'), late)  5.97 us
    ppermute x2, starting transfers between devices, row_scale(): lax.ppermute(pick(after(squares, *earlier), core ^ k, 0), ('pair', 'batch...  4.95 us
    ppermute x3, starting transfers between devices, up(): lax.ppermute(value, 'vocab', [(z, z + 1) for z in range(k - 1, vocab - 1)])  4.9 us
  transfers between devices with their start and end apart: 30, of which 18 were waited for; matrix products, arithmetic and copies ran while one was open for 24% of the time, Pallas kernels for 0%

profile of v12, /device:TPU:0, one launch (start us, length us, event | category | flops | bytes accessed | tf_op | source)
XLA Modules:
  0.0 126.4 jit_solution(14627358611629984859)
XLA Ops:
  3.0 2.6 %collective-permute-start = (bf16[2,64,1024]{2,1,0:T(8,128)(2,1)S(1)}, bf16[2,64,1024]{2,1,0:T(8,128)(2,1)S(1)}, u32[]{:S(2)}, u32[]{:S(2)}) collective-permute-start(bf16[2,64,1024]{2,1,0:T(8,128)(2,1)S(1)} %constant_dynamic-slice_fusion.6), channel_id=1, source_target_pairs={{0,4},{4,0},{8,12},{12,8},{1,5},{5,1},{9,13},{13,9},{2,6},{6,2},{1... | collective-permute-start | bytes 786440 | tf_op jit(solution)/shard_map/ppermute | solution.py:79
  6.8 1.6 %collective-permute-start.1 = (f32[128]{0:T(128)S(1)}, f32[128]{0:T(128)S(1)}, u32[]{:S(2)}, u32[]{:S(2)}) collective-permute-start(f32[128]{0:T(128)S(1)} %multiply_reduce_fusion), channel_id=1, source_target_pairs={{0,1},{1,0},{2,3},{3,2},{4,5},{5,4},{6,7},{7,6},{8,9},{9,8},{10,11... | collective-permute-start | bytes 1544 | tf_op jit(solution)/shard_map/ppermute | solution.py:44
  8.5 2.0 %collective-permute-done.1 = f32[128]{0:T(128)S(1)} collective-permute-done((f32[128]{0:T(128)S(1)}, f32[128]{0:T(128)S(1)}, u32[]{:S(2)}, u32[]{:S(2)}) %collective-permute-start.1) | collective-permute-done | bytes 544 | tf_op jit(solution)/shard_map/ppermute | solution.py:44
  10.4 2.6 %collective-permute-start.2 = (f32[128]{0:T(128)S(1)}, f32[128]{0:T(128)S(1)}, u32[]{:S(2)}, u32[]{:S(2)}) collective-permute-start(f32[128]{0:T(128)S(1)} %add.124), channel_id=1, source_target_pairs={{0,2},{1,3},{2,0},{3,1},{4,6},{5,7},{6,4},{7,5},{8,10},{9,11},{10,... | collective-permute-start | bytes 1544 | tf_op jit(solution)/shard_map/ppermute | solution.py:44
  13.0 1.9 %collective-permute-done.2 = f32[128]{0:T(128)S(1)} collective-permute-done((f32[128]{0:T(128)S(1)}, f32[128]{0:T(128)S(1)}, u32[]{:S(2)}, u32[]{:S(2)}) %collective-permute-start.2) | collective-permute-done | bytes 544 | tf_op jit(solution)/shard_map/ppermute | solution.py:44
  15.2 3.5 %collective-permute-start.6 = (bf16[2,2,64,1024]{3,2,1,0:T(8,128)(2,1)S(1)}, bf16[2,2,64,1024]{3,2,1,0:T(8,128)(2,1)S(1)}, u32[]{:S(2)}, u32[]{:S(2)}) collective-permute-start(bf16[2,2,64,1024]{3,2,1,0:T(8,128)(2,1)S(1)} %pad_maximum_fusion.2), channel_id=1, source_target_pairs={{0,1},{1,2},{2,3},{4,5},{5,6},{6,7},{8,9},{9,10},{10,11},{12,13},{... | collective-permute-start | bytes 1572872 | tf_op jit(solution)/shard_map/ppermute | solution.py:86
  20.7 4.3 %collective-permute-start.5 = (f32[64]{0:T(128)S(1)}, f32[64]{0:T(128)S(1)}, u32[]{:S(2)}, u32[]{:S(2)}) collective-permute-start(f32[64]{0:T(128)S(1)} %get-tuple-element.67), channel_id=1, source_target_pairs={{0,4},{4,12},{8,20},{12,28},{16,0},{20,8},{24,16},{28,24},{1,5},{5... | collective-permute-start | bytes 776 | tf_op jit(solution)/shard_map/ppermute | solution.py:55
  26.3 1.9 %collective-permute-done.6 = bf16[2,2,64,1024]{3,2,1,0:T(8,128)(2,1)S(1)} collective-permute-done((bf16[2,2,64,1024]{3,2,1,0:T(8,128)(2,1)S(1)}, bf16[2,2,64,1024]{3,2,1,0:T(8,128)(2,1)S(1)}, u32[]{:S(2)}, u32[]{:S(2)}) %collective-permute-start.6) | collective-permute-done | bytes 524320 | tf_op jit(solution)/shard_map/ppermute | solution.py:86
  28.2 4.1 %collective-permute-done.3 = bf16[2,2,64,1024]{3,2,1,0:T(8,128)(2,1)S(1)} collective-permute-done((bf16[2,2,64,1024]{3,2,1,0:T(8,128)(2,1)S(1)}, bf16[2,2,64,1024]{3,2,1,0:T(8,128)(2,1)S(1)}, u32[]{:S(2)}, u32[]{:S(2)}) %collective-permute-start.3) | collective-permute-done | bytes 524320 | tf_op jit(solution)/shard_map/ppermute | solution.py:89
  33.2 1.5 %collective-permute-start.7 = (bf16[2,2,64,1024]{3,2,1,0:T(8,128)(2,1)}, bf16[2,2,64,1024]{3,2,1,0:T(8,128)(2,1)S(1)}, u32[]{:S(2)}, u32[]{:S(2)}) collective-permute-start(bf16[2,2,64,1024]{3,2,1,0:T(8,128)(2,1)} %select_select_fusion.2), channel_id=1, source_target_pairs={{0,8},{8,0},{4,12},{12,4},{1,9},{9,1},{5,13},{13,5},{2,10},{10,2},... | collective-permute-start | bytes 1572872 | tf_op jit(solution)/shard_map/ppermute | solution.py:104
  36.7 8.2 %broadcast_select_fusion = (bf16[1024,2048]{1,0:T(8,128)(2,1)}, bf16[1024,2048]{1,0:T(8,128)(2,1)S(1)}) fusion(pred[]{:T(512)S(6)} %eq.77, bf16[1024,4096]{1,0:T(8,128)(2,1)} %collective-permute-done.9, s32[]{:T(128)S(6)} %select_n.253, bf16[1024,4096]{1,0:T(8,128)(2,1)} %param.5), kind=kLoop, calls=%fused_computation.2 | loop fusion | flops 4194304 | bytes 16777220 | tf_op jit(solution)/shard_map/jit(_where)/select_n | solution.py:110
  44.9 2.2 %collective-permute-done.10 = bf16[2,2,64,1024]{3,2,1,0:T(8,128)(2,1)S(1)} collective-permute-done((bf16[2,2,64,1024]{3,2,1,0:T(8,128)(2,1)S(1)}, bf16[2,2,64,1024]{3,2,1,0:T(8,128)(2,1)S(1)}, u32[]{:S(2)}, u32[]{:S(2)}) %collective-permute-start.10) | collective-permute-done | bytes 524320 | tf_op jit(solution)/shard_map/ppermute | solution.py:89
  50.8 4.4 %fusion.36 = f32[512,2048]{1,0:T(8,128)} fusion(bf16[512,1024]{1,0:T(8,128)(2,1)S(1)} %bitcast.116, bf16[1024,2048]{1,0:T(8,128)(2,1)S(1)} %get-tuple-element.23), kind=kOutput, calls=%fused_computation.110 | convolution fusion | flops 2147483648 | bytes 9437184 | tf_op jit(solution)/shard_map/dot_general | solution.py:75
  55.1 4.7 %collective-permute-done.11 = bf16[2,2,64,1024]{3,2,1,0:T(8,128)(2,1)S(1)} collective-permute-done((bf16[2,2,64,1024]{3,2,1,0:T(8,128)(2,1)S(1)}, bf16[2,2,64,1024]{3,2,1,0:T(8,128)(2,1)S(1)}, u32[]{:S(2)}, u32[]{:S(2)}) %collective-permute-start.11) | collective-permute-done | bytes 524320 | tf_op jit(solution)/shard_map/ppermute | solution.py:89
  61.0 2.2 %collective-permute-start.14 = (bf16[2,2,64,1024]{3,2,1,0:T(8,128)(2,1)S(1)}, bf16[2,2,64,1024]{3,2,1,0:T(8,128)(2,1)}, u32[]{:S(2)}, u32[]{:S(2)}) collective-permute-start(bf16[2,2,64,1024]{3,2,1,0:T(8,128)(2,1)S(1)} %broadcast_select_fusion.2), channel_id=1, source_target_pairs={{0,8},{4,12},{11,3},{15,7},{16,24},{20,28},{27,19},{31,23}} | collective-permute-start | bytes 1572872 | tf_op jit(solution)/shard_map/ppermute | solution.py:128
  63.2 6.0 %collective-permute-done.14 = bf16[2,2,64,1024]{3,2,1,0:T(8,128)(2,1)} collective-permute-done((bf16[2,2,64,1024]{3,2,1,0:T(8,128)(2,1)S(1)}, bf16[2,2,64,1024]{3,2,1,0:T(8,128)(2,1)}, u32[]{:S(2)}, u32[]{:S(2)}) %collective-permute-start.14) | collective-permute-done | bytes 524320 | tf_op jit(solution)/shard_map/ppermute | solution.py:128
  71.8 2.4 %add_multiply_fusion.1 = f32[512,2048]{1,0:T(8,128)S(1)} fusion(f32[512,2048]{1,0:T(8,128)S(1)} %copy-done.4, bf16[512,1024]{1,0:T(8,128)(2,1)S(1)} %bitcast.117, bf16[1024,2048]{1,0:T(8,128)(2,1)S(1)} %copy-done.2), kind=kOutput, calls=%fused_computation.1 | convolution fusion | flops 2149580800 | bytes 13631488 | tf_op jit(solution)/shard_map/dot_general | solution.py:75
  74.9 2.7 %collective-permute-start.21 = (f16[2,2,64,1024]{3,2,1,0:T(8,128)(2,1)S(1)}, f16[2,2,64,1024]{3,2,1,0:T(8,128)(2,1)S(1)}, u32[]{:S(2)}, u32[]{:S(2)}) collective-permute-start(f16[2,2,64,1024]{3,2,1,0:T(8,128)(2,1)S(1)} %fusion.4), channel_id=1, source_target_pairs={{0,8},{8,0},{4,12},{12,4},{1,9},{9,1},{5,13},{13,5},{2,10},{10,2},... | collective-permute-start | bytes 1572872 | tf_op jit(solution)/shard_map/ppermute | solution.py:169
  77.9 1.5 %collective-permute-start.15 = (f16[2,2,64,1024]{3,2,0,1:T(8,128)(2,1)S(1)}, f16[2,2,64,1024]{3,2,0,1:T(8,128)(2,1)S(1)}, u32[]{:S(2)}, u32[]{:S(2)}) collective-permute-start(f16[2,2,64,1024]{3,2,0,1:T(8,128)(2,1)S(1)} %fusion.6), channel_id=1, source_target_pairs={{0,4},{4,0},{8,12},{12,8},{1,5},{5,1},{9,13},{13,9},{2,6},{6,2},{1... | collective-permute-start | bytes 1572872 | tf_op jit(solution)/shard_map/ppermute | solution.py:168
  79.4 2.3 %fusion.37 = f32[512,2048]{1,0:T(8,128)S(1)} fusion(bf16[512,1024]{1,0:T(8,128)(2,1)S(1)} %bitcast.126, bf16[1024,2048]{1,0:T(8,128)(2,1)S(1)} %copy-done.2), kind=kOutput, calls=%fused_computation.111 | convolution fusion | flops 2147483648 | bytes 9437184 | tf_op jit(solution)/shard_map/dot_general | solution.py:75
  81.7 2.4 %add_multiply_fusion = f32[512,2048]{1,0:T(8,128)S(1)} fusion(f32[512,2048]{1,0:T(8,128)S(1)} %fusion.37, bf16[512,1024]{1,0:T(8,128)(2,1)S(1)} %bitcast.125, bf16[1024,2048]{1,0:T(8,128)(2,1)S(1)} %copy-done.1), kind=kOutput, calls=%fused_computation | convolution fusion | flops 2149580800 | bytes 13631488 | tf_op jit(solution)/shard_map/dot_general | solution.py:75
  85.9 4.4 %collective-permute-done.21 = f16[2,2,64,1024]{3,2,1,0:T(8,128)(2,1)S(1)} collective-permute-done((f16[2,2,64,1024]{3,2,1,0:T(8,128)(2,1)S(1)}, f16[2,2,64,1024]{3,2,1,0:T(8,128)(2,1)S(1)}, u32[]{:S(2)}, u32[]{:S(2)}) %collective-permute-start.21) | collective-permute-done | bytes 524320 | tf_op jit(solution)/shard_map/ppermute | solution.py:169
  90.6 1.5 %collective-permute-start.22 = (f16[2,64,1024]{2,1,0:T(8,128)(2,1)S(1)}, f16[2,64,1024]{2,1,0:T(8,128)(2,1)S(1)}, u32[]{:S(2)}, u32[]{:S(2)}) collective-permute-start(f16[2,64,1024]{2,1,0:T(8,128)(2,1)S(1)} %fusion.15), channel_id=1, source_target_pairs={{0,4},{4,0},{8,12},{12,8},{1,5},{5,1},{9,13},{13,9},{2,6},{6,2},{1... | collective-permute-start | bytes 786440 | tf_op jit(solution)/shard_map/ppermute | solution.py:181
  94.3 7.3 %collective-permute-done.20 = f16[2,2,64,1024]{3,2,1,0:T(8,128)(2,1)S(1)} collective-permute-done((f16[2,2,64,1024]{3,2,1,0:T(8,128)(2,1)S(1)}, f16[2,2,64,1024]{3,2,1,0:T(8,128)(2,1)S(1)}, u32[]{:S(2)}, u32[]{:S(2)}) %collective-permute-start.20) | collective-permute-done | bytes 524320 | tf_op jit(solution)/shard_map/ppermute | solution.py:169
  101.8 1.5 %collective-permute-start.25 = (f16[2,64,1024]{2,1,0:T(8,128)(2,1)S(1)}, f16[2,64,1024]{2,1,0:T(8,128)(2,1)S(1)}, u32[]{:S(2)}, u32[]{:S(2)}) collective-permute-start(f16[2,64,1024]{2,1,0:T(8,128)(2,1)S(1)} %fusion.14), channel_id=1, source_target_pairs={{0,4},{4,0},{8,12},{12,8},{1,5},{5,1},{9,13},{13,9},{2,6},{6,2},{1... | collective-permute-start | bytes 786440 | tf_op jit(solution)/shard_map/ppermute | solution.py:181
  105.6 4.0 %collective-permute-done.22 = f16[2,64,1024]{2,1,0:T(8,128)(2,1)S(1)} collective-permute-done((f16[2,64,1024]{2,1,0:T(8,128)(2,1)S(1)}, f16[2,64,1024]{2,1,0:T(8,128)(2,1)S(1)}, u32[]{:S(2)}, u32[]{:S(2)}) %collective-permute-start.22) | collective-permute-done | bytes 262176 | tf_op jit(solution)/shard_map/ppermute | solution.py:181
  109.9 4.5 %collective-permute-done.25 = f16[2,64,1024]{2,1,0:T(8,128)(2,1)S(1)} collective-permute-done((f16[2,64,1024]{2,1,0:T(8,128)(2,1)S(1)}, f16[2,64,1024]{2,1,0:T(8,128)(2,1)S(1)}, u32[]{:S(2)}, u32[]{:S(2)}) %collective-permute-start.25) | collective-permute-done | bytes 262176 | tf_op jit(solution)/shard_map/ppermute | solution.py:181
  115.0 1.4 %collective-permute-done.26 = f16[64,2048]{1,0:T(8,128)(2,1)S(1)} collective-permute-done((f16[64,2048]{1,0:T(8,128)(2,1)S(1)}, f16[64,2048]{1,0:T(8,128)(2,1)S(1)}, u32[]{:S(2)}, u32[]{:S(2)}) %collective-permute-start.26) | collective-permute-done | bytes 262176 | tf_op jit(solution)/shard_map/ppermute | solution.py:69
  117.8 3.3 %collective-permute-start.28 = (f32[4,64]{1,0:T(4,128)S(1)}, f32[4,64]{1,0:T(4,128)S(1)}, u32[]{:S(2)}, u32[]{:S(2)}) collective-permute-start(f32[4,64]{1,0:T(4,128)S(1)} %get-tuple-element.59), channel_id=1, source_target_pairs={{0,2},{1,3},{2,0},{3,1},{4,6},{5,7},{6,4},{7,5},{8,10},{9,11},{10,... | collective-permute-start | bytes 3080 | tf_op jit(solution)/shard_map/ppermute | solution.py:213
  121.6 1.6 %collective-permute-done.27 = f32[4,64]{1,0:T(4,128)S(1)} collective-permute-done((f32[4,64]{1,0:T(4,128)S(1)}, f32[4,64]{1,0:T(4,128)S(1)}, u32[]{:S(2)}, u32[]{:S(2)}) %collective-permute-start.27) | collective-permute-done | bytes 1056 | tf_op jit(solution)/shard_map/ppermute | solution.py:213
  123.1 1.5 %collective-permute-done.29 = f32[4,64]{1,0:T(4,128)S(1)} collective-permute-done((f32[4,64]{1,0:T(4,128)S(1)}, f32[4,64]{1,0:T(4,128)S(1)}, u32[]{:S(2)}, u32[]{:S(2)}) %collective-permute-start.29) | collective-permute-done | bytes 1056 | tf_op jit(solution)/shard_map/ppermute | solution.py:213
  124.7 1.6 %fusion.2 = (f32[64,4096]{1,0:T(8,128)}, f32[64,4096]{1,0:T(8,128)}) fusion(f32[64]{0:T(128)S(1)} %get-tuple-element.60, f32[64]{0:T(128)S(1)} %get-tuple-element.62, f16[64,2048]{1,0:T(8,128)(2,1)S(1)} %get-tuple-element.53, f16[64,2048]{1,0:T(8,128)(2,1)S(1)} %get-tuple-element.51, f32[64,4096]{1,0:T(8,128)S(1)} %get-tuple-element.35, ...), kind=kLoop, calls=%fused_computation.18 | loop fusion | flops 1310720 | bytes 3670784 | tf_op jit(solution)/shard_map/sub | solution.py:220
  (98 shorter events, 27.8 us)
Async XLA Ops:
  0.6 36.1 %collective-permute-start.9 = (bf16[1024,4096]{1,0:T(8,128)(2,1)}, bf16[1024,4096]{1,0:T(8,128)(2,1)}, u32[]{:S(2)}, u32[]{:S(2)}) collective-permute-start(bf16[1024,4096]{1,0:T(8,128)(2,1)} %param.5), channel_id=1, source_target_pairs={{0,16},{16,0},{1,17},{17,1},{2,18},{18,2},{3,19},{19,3},{4,20},{20... | collective-permute-start | bytes 25165832 | tf_op jit(solution)/shard_map/ppermute | solution.py:41
  3.0 12.0 %collective-permute-start = (bf16[2,64,1024]{2,1,0:T(8,128)(2,1)S(1)}, bf16[2,64,1024]{2,1,0:T(8,128)(2,1)S(1)}, u32[]{:S(2)}, u32[]{:S(2)}) collective-permute-start(bf16[2,64,1024]{2,1,0:T(8,128)(2,1)S(1)} %constant_dynamic-slice_fusion.6), channel_id=1, source_target_pairs={{0,4},{4,0},{8,12},{12,8},{1,5},{5,1},{9,13},{13,9},{2,6},{6,2},{1... | collective-permute-start | bytes 786440 | tf_op jit(solution)/shard_map/ppermute | solution.py:79
  6.8 3.6 %collective-permute-start.1 = (f32[128]{0:T(128)S(1)}, f32[128]{0:T(128)S(1)}, u32[]{:S(2)}, u32[]{:S(2)}) collective-permute-start(f32[128]{0:T(128)S(1)} %multiply_reduce_fusion), channel_id=1, source_target_pairs={{0,1},{1,0},{2,3},{3,2},{4,5},{5,4},{6,7},{7,6},{8,9},{9,8},{10,11... | collective-permute-start | bytes 1544 | tf_op jit(solution)/shard_map/ppermute | solution.py:44
  10.4 4.4 %collective-permute-start.2 = (f32[128]{0:T(128)S(1)}, f32[128]{0:T(128)S(1)}, u32[]{:S(2)}, u32[]{:S(2)}) collective-permute-start(f32[128]{0:T(128)S(1)} %add.124), channel_id=1, source_target_pairs={{0,2},{1,3},{2,0},{3,1},{4,6},{5,7},{6,4},{7,5},{8,10},{9,11},{10,... | collective-permute-start | bytes 1544 | tf_op jit(solution)/shard_map/ppermute | solution.py:44
  15.2 13.0 %collective-permute-start.6 = (bf16[2,2,64,1024]{3,2,1,0:T(8,128)(2,1)S(1)}, bf16[2,2,64,1024]{3,2,1,0:T(8,128)(2,1)S(1)}, u32[]{:S(2)}, u32[]{:S(2)}) collective-permute-start(bf16[2,2,64,1024]{3,2,1,0:T(8,128)(2,1)S(1)} %pad_maximum_fusion.2), channel_id=1, source_target_pairs={{0,1},{1,2},{2,3},{4,5},{5,6},{6,7},{8,9},{9,10},{10,11},{12,13},{... | collective-permute-start | bytes 1572872 | tf_op jit(solution)/shard_map/ppermute | solution.py:86
  18.7 13.6 %collective-permute-start.3 = (bf16[2,2,64,1024]{3,2,1,0:T(8,128)(2,1)S(1)}, bf16[2,2,64,1024]{3,2,1,0:T(8,128)(2,1)S(1)}, u32[]{:S(2)}, u32[]{:S(2)}) collective-permute-start(bf16[2,2,64,1024]{3,2,1,0:T(8,128)(2,1)S(1)} %pad_maximum_fusion.2), channel_id=1, source_target_pairs={{1,0},{2,1},{3,2},{5,4},{6,5},{7,6},{9,8},{10,9},{11,10},{13,12},{... | collective-permute-start | bytes 1572872 | tf_op jit(solution)/shard_map/ppermute | solution.py:89
  20.0 5.0 %collective-permute-start.4 = (f32[64]{0:T(128)S(1)}, f32[64]{0:T(128)S(1)}, u32[]{:S(2)}, u32[]{:S(2)}) collective-permute-start(f32[64]{0:T(128)S(1)} %get-tuple-element.66), channel_id=1, source_target_pairs={{0,0},{4,8},{8,16},{12,24},{16,4},{20,12},{24,20},{28,28},{1,1},{5... | collective-permute-start | bytes 776 | tf_op jit(solution)/shard_map/ppermute | solution.py:55
  20.7 5.6 %collective-permute-start.5 = (f32[64]{0:T(128)S(1)}, f32[64]{0:T(128)S(1)}, u32[]{:S(2)}, u32[]{:S(2)}) collective-permute-start(f32[64]{0:T(128)S(1)} %get-tuple-element.67), channel_id=1, source_target_pairs={{0,4},{4,12},{8,20},{12,28},{16,0},{20,8},{24,16},{28,24},{1,5},{5... | collective-permute-start | bytes 776 | tf_op jit(solution)/shard_map/ppermute | solution.py:55
  33.2 11.7 %collective-permute-start.7 = (bf16[2,2,64,1024]{3,2,1,0:T(8,128)(2,1)}, bf16[2,2,64,1024]{3,2,1,0:T(8,128)(2,1)S(1)}, u32[]{:S(2)}, u32[]{:S(2)}) collective-permute-start(bf16[2,2,64,1024]{3,2,1,0:T(8,128)(2,1)} %select_select_fusion.2), channel_id=1, source_target_pairs={{0,8},{8,0},{4,12},{12,4},{1,9},{9,1},{5,13},{13,5},{2,10},{10,2},... | collective-permute-start | bytes 1572872 | tf_op jit(solution)/shard_map/ppermute | solution.py:104
  34.7 12.4 %collective-permute-start.10 = (bf16[2,2,64,1024]{3,2,1,0:T(8,128)(2,1)S(1)}, bf16[2,2,64,1024]{3,2,1,0:T(8,128)(2,1)S(1)}, u32[]{:S(2)}, u32[]{:S(2)}) collective-permute-start(bf16[2,2,64,1024]{3,2,1,0:T(8,128)(2,1)S(1)} %collective-permute-done.3), channel_id=1, source_target_pairs={{1,0},{2,1},{5,4},{6,5},{9,8},{10,9},{13,12},{14,13},{17,16},{18,1... | collective-permute-start | bytes 1572872 | tf_op jit(solution)/shard_map/ppermute | solution.py:89
  36.0 12.4 %collective-permute-start.8 = (bf16[2,2,64,1024]{3,2,1,0:T(8,128)(2,1)S(1)}, bf16[2,2,64,1024]{3,2,1,0:T(8,128)(2,1)S(1)}, u32[]{:S(2)}, u32[]{:S(2)}) collective-permute-start(bf16[2,2,64,1024]{3,2,1,0:T(8,128)(2,1)S(1)} %collective-permute-done.6), channel_id=1, source_target_pairs={{1,2},{2,3},{5,6},{6,7},{9,10},{10,11},{13,14},{14,15},{17,18},{18... | collective-permute-start | bytes 1572872 | tf_op jit(solution)/shard_map/ppermute | solution.py:86
  47.1 12.8 %collective-permute-start.11 = (bf16[2,2,64,1024]{3,2,1,0:T(8,128)(2,1)S(1)}, bf16[2,2,64,1024]{3,2,1,0:T(8,128)(2,1)S(1)}, u32[]{:S(2)}, u32[]{:S(2)}) collective-permute-start(bf16[2,2,64,1024]{3,2,1,0:T(8,128)(2,1)S(1)} %collective-permute-done.10), channel_id=1, source_target_pairs={{1,0},{5,4},{9,8},{13,12},{17,16},{21,20},{25,24},{29,28}} | collective-permute-start | bytes 1572872 | tf_op jit(solution)/shard_map/ppermute | solution.py:89
  48.4 11.5 %collective-permute-start.12 = (bf16[2,2,64,1024]{3,2,1,0:T(8,128)(2,1)S(1)}, bf16[2,2,64,1024]{3,2,1,0:T(8,128)(2,1)S(1)}, u32[]{:S(2)}, u32[]{:S(2)}) collective-permute-start(bf16[2,2,64,1024]{3,2,1,0:T(8,128)(2,1)S(1)} %collective-permute-done.8), channel_id=1, source_target_pairs={{2,3},{6,7},{10,11},{14,15},{18,19},{22,23},{26,27},{30,31}} | collective-permute-start | bytes 1572872 | tf_op jit(solution)/shard_map/ppermute | solution.py:86
  49.4 11.6 %collective-permute-start.13 = (bf16[2,2,64,1024]{3,2,1,0:T(8,128)(2,1)S(1)}, bf16[2,2,64,1024]{3,2,1,0:T(8,128)(2,1)}, u32[]{:S(2)}, u32[]{:S(2)}) collective-permute-start(bf16[2,2,64,1024]{3,2,1,0:T(8,128)(2,1)S(1)} %get-tuple-element.50), channel_id=1, source_target_pairs={{1,9},{2,10},{3,11},{5,13},{6,14},{7,15},{8,0},{9,1},{10,2},{12,4}... | collective-permute-start | bytes 1572872 | tf_op jit(solution)/shard_map/ppermute | solution.py:122
  61.0 8.2 %collective-permute-start.14 = (bf16[2,2,64,1024]{3,2,1,0:T(8,128)(2,1)S(1)}, bf16[2,2,64,1024]{3,2,1,0:T(8,128)(2,1)}, u32[]{:S(2)}, u32[]{:S(2)}) collective-permute-start(bf16[2,2,64,1024]{3,2,1,0:T(8,128)(2,1)S(1)} %broadcast_select_fusion.2), channel_id=1, source_target_pairs={{0,8},{4,12},{11,3},{15,7},{16,24},{20,28},{27,19},{31,23}} | collective-permute-start | bytes 1572872 | tf_op jit(solution)/shard_map/ppermute | solution.py:128
  63.2 8.7 %copy-start.2 = (bf16[1024,2048]{1,0:T(8,128)(2,1)S(1)}, bf16[1024,2048]{1,0:T(8,128)(2,1)}, u32[]{:S(2)}) copy-start(bf16[1024,2048]{1,0:T(8,128)(2,1)} %get-tuple-element.24) | copy-start | bytes 12582916
  63.2 8.7 %copy-start.4 = (f32[512,2048]{1,0:T(8,128)S(1)}, f32[512,2048]{1,0:T(8,128)}, u32[]{:S(2)}) copy-start(f32[512,2048]{1,0:T(8,128)} %fusion.36) | copy-start | bytes 12582916
  63.2 18.5 %collective-permute-start.16 = (bf16[2,2,2,64,1024]{4,3,2,1,0:T(8,128)(2,1)}, bf16[2,2,2,64,1024]{4,3,2,1,0:T(8,128)(2,1)S(1)}, u32[]{:S(2)}, u32[]{:S(2)}) collective-permute-start(bf16[2,2,2,64,1024]{4,3,2,1,0:T(8,128)(2,1)} %copy-done.3), channel_id=1, source_target_pairs={{0,16},{16,0},{1,17},{17,1},{2,18},{18,2},{3,19},{19,3},{4,20},{20... | collective-permute-start | bytes 3145736 | tf_op jit(solution)/shard_map/ppermute | solution.py:69
  71.7 7.6 %collective-permute-start.17 = (bf16[2,2,2,64,1024]{4,3,2,1,0:T(8,128)(2,1)S(1)}, bf16[2,2,2,64,1024]{4,3,2,1,0:T(8,128)(2,1)S(1)}, u32[]{:S(2)}, u32[]{:S(2)}) collective-permute-start(bf16[2,2,2,64,1024]{4,3,2,1,0:T(8,128)(2,1)S(1)} %pad_maximum_fusion.1), channel_id=1, source_target_pairs={{0,16},{16,0},{1,17},{17,1},{2,18},{18,2},{3,19},{19,3},{4,20},{20... | collective-permute-start | bytes 3145736 | tf_op jit(solution)/shard_map/ppermute | solution.py:69
  74.9 15.4 %collective-permute-start.21 = (f16[2,2,64,1024]{3,2,1,0:T(8,128)(2,1)S(1)}, f16[2,2,64,1024]{3,2,1,0:T(8,128)(2,1)S(1)}, u32[]{:S(2)}, u32[]{:S(2)}) collective-permute-start(f16[2,2,64,1024]{3,2,1,0:T(8,128)(2,1)S(1)} %fusion.4), channel_id=1, source_target_pairs={{0,8},{8,0},{4,12},{12,4},{1,9},{9,1},{5,13},{13,5},{2,10},{10,2},... | collective-permute-start | bytes 1572872 | tf_op jit(solution)/shard_map/ppermute | solution.py:169
  77.9 14.8 %collective-permute-start.15 = (f16[2,2,64,1024]{3,2,0,1:T(8,128)(2,1)S(1)}, f16[2,2,64,1024]{3,2,0,1:T(8,128)(2,1)S(1)}, u32[]{:S(2)}, u32[]{:S(2)}) collective-permute-start(f16[2,2,64,1024]{3,2,0,1:T(8,128)(2,1)S(1)} %fusion.6), channel_id=1, source_target_pairs={{0,4},{4,0},{8,12},{12,8},{1,5},{5,1},{9,13},{13,9},{2,6},{6,2},{1... | collective-permute-start | bytes 1572872 | tf_op jit(solution)/shard_map/ppermute | solution.py:168
  84.8 16.8 %collective-permute-start.20 = (f16[2,2,64,1024]{3,2,1,0:T(8,128)(2,1)S(1)}, f16[2,2,64,1024]{3,2,1,0:T(8,128)(2,1)S(1)}, u32[]{:S(2)}, u32[]{:S(2)}) collective-permute-start(f16[2,2,64,1024]{3,2,1,0:T(8,128)(2,1)S(1)} %fusion.5), channel_id=1, source_target_pairs={{0,8},{8,0},{4,12},{12,4},{1,9},{9,1},{5,13},{13,5},{2,10},{10,2},... | collective-permute-start | bytes 1572872 | tf_op jit(solution)/shard_map/ppermute | solution.py:169
  85.2 18.8 %collective-permute-start.19 = (f16[2,2,64,1024]{3,2,0,1:T(8,128)(2,1)S(1)}, f16[2,2,64,1024]{3,2,0,1:T(8,128)(2,1)S(1)}, u32[]{:S(2)}, u32[]{:S(2)}) collective-permute-start(f16[2,2,64,1024]{3,2,0,1:T(8,128)(2,1)S(1)} %fusion.7), channel_id=1, source_target_pairs={{0,4},{4,0},{8,12},{12,8},{1,5},{5,1},{9,13},{13,9},{2,6},{6,2},{1... | collective-permute-start | bytes 1572872 | tf_op jit(solution)/shard_map/ppermute | solution.py:168
  90.6 19.0 %collective-permute-start.22 = (f16[2,64,1024]{2,1,0:T(8,128)(2,1)S(1)}, f16[2,64,1024]{2,1,0:T(8,128)(2,1)S(1)}, u32[]{:S(2)}, u32[]{:S(2)}) collective-permute-start(f16[2,64,1024]{2,1,0:T(8,128)(2,1)S(1)} %fusion.15), channel_id=1, source_target_pairs={{0,4},{4,0},{8,12},{12,8},{1,5},{5,1},{9,13},{13,9},{2,6},{6,2},{1... | collective-permute-start | bytes 786440 | tf_op jit(solution)/shard_map/ppermute | solution.py:181
  93.0 16.7 %collective-permute-start.18 = (f16[2,64,1024]{2,1,0:T(8,128)(2,1)S(1)}, f16[2,64,1024]{2,1,0:T(8,128)(2,1)S(1)}, u32[]{:S(2)}, u32[]{:S(2)}) collective-permute-start(f16[2,64,1024]{2,1,0:T(8,128)(2,1)S(1)} %fusion.12), channel_id=1, source_target_pairs={{0,8},{8,0},{4,12},{12,4},{1,9},{9,1},{5,13},{13,5},{2,10},{10,2},... | collective-permute-start | bytes 786440 | tf_op jit(solution)/shard_map/ppermute | solution.py:180
  101.8 12.6 %collective-permute-start.25 = (f16[2,64,1024]{2,1,0:T(8,128)(2,1)S(1)}, f16[2,64,1024]{2,1,0:T(8,128)(2,1)S(1)}, u32[]{:S(2)}, u32[]{:S(2)}) collective-permute-start(f16[2,64,1024]{2,1,0:T(8,128)(2,1)S(1)} %fusion.14), channel_id=1, source_target_pairs={{0,4},{4,0},{8,12},{12,8},{1,5},{5,1},{9,13},{13,9},{2,6},{6,2},{1... | collective-permute-start | bytes 786440 | tf_op jit(solution)/shard_map/ppermute | solution.py:181
  104.2 10.3 %collective-permute-start.24 = (f16[2,64,1024]{2,1,0:T(8,128)(2,1)S(1)}, f16[2,64,1024]{2,1,0:T(8,128)(2,1)S(1)}, u32[]{:S(2)}, u32[]{:S(2)}) collective-permute-start(f16[2,64,1024]{2,1,0:T(8,128)(2,1)S(1)} %fusion.13), channel_id=1, source_target_pairs={{0,8},{8,0},{4,12},{12,4},{1,9},{9,1},{5,13},{13,5},{2,10},{10,2},... | collective-permute-start | bytes 786440 | tf_op jit(solution)/shard_map/ppermute | solution.py:180
  109.9 4.9 %collective-permute-start.23 = (f16[64,2048]{1,0:T(8,128)(2,1)S(1)}, f16[64,2048]{1,0:T(8,128)(2,1)S(1)}, u32[]{:S(2)}, u32[]{:S(2)}) collective-permute-start(f16[64,2048]{1,0:T(8,128)(2,1)S(1)} %fusion.21), channel_id=1, source_target_pairs={{0,16},{16,0},{1,17},{17,1},{2,18},{18,2},{3,19},{19,3},{4,20},{20... | collective-permute-start | bytes 786440 | tf_op jit(solution)/shard_map/ppermute | solution.py:69
  114.7 1.6 %collective-permute-start.26 = (f16[64,2048]{1,0:T(8,128)(2,1)S(1)}, f16[64,2048]{1,0:T(8,128)(2,1)S(1)}, u32[]{:S(2)}, u32[]{:S(2)}) collective-permute-start(f16[64,2048]{1,0:T(8,128)(2,1)S(1)} %fusion.19), channel_id=1, source_target_pairs={{0,16},{16,0},{1,17},{17,1},{2,18},{18,2},{3,19},{19,3},{4,20},{20... | collective-permute-start | bytes 786440 | tf_op jit(solution)/shard_map/ppermute | solution.py:69
  117.7 5.4 %collective-permute-start.27 = (f32[4,64]{1,0:T(4,128)S(1)}, f32[4,64]{1,0:T(4,128)S(1)}, u32[]{:S(2)}, u32[]{:S(2)}) collective-permute-start(f32[4,64]{1,0:T(4,128)S(1)} %get-tuple-element.59), channel_id=1, source_target_pairs={{0,1},{1,2},{2,3},{3,0},{4,5},{5,6},{6,7},{7,4},{8,9},{9,10},{10,1... | collective-permute-start | bytes 3080 | tf_op jit(solution)/shard_map/ppermute | solution.py:213
  117.8 5.4 %collective-permute-start.28 = (f32[4,64]{1,0:T(4,128)S(1)}, f32[4,64]{1,0:T(4,128)S(1)}, u32[]{:S(2)}, u32[]{:S(2)}) collective-permute-start(f32[4,64]{1,0:T(4,128)S(1)} %get-tuple-element.59), channel_id=1, source_target_pairs={{0,2},{1,3},{2,0},{3,1},{4,6},{5,7},{6,4},{7,5},{8,10},{9,11},{10,... | collective-permute-start | bytes 3080 | tf_op jit(solution)/shard_map/ppermute | solution.py:213
  121.1 3.6 %collective-permute-start.29 = (f32[4,64]{1,0:T(4,128)S(1)}, f32[4,64]{1,0:T(4,128)S(1)}, u32[]{:S(2)}, u32[]{:S(2)}) collective-permute-start(f32[4,64]{1,0:T(4,128)S(1)} %get-tuple-element.59), channel_id=1, source_target_pairs={{0,3},{1,0},{2,1},{3,2},{4,7},{5,4},{6,5},{7,6},{8,11},{9,8},{10,9... | collective-permute-start | bytes 3080 | tf_op jit(solution)/shard_map/ppermute | solution.py:213
  (3 other events, 12.6 us)

commit v13 on v11

--- a/solution.py
+++ b/solution.py
@@ -5,9 +5,9 @@
 
 EPS = 1e-05
 GUIDE = 1.5
-CHUNKS = 2
 SHRINK = 1.0 / 32.0
 SUM_TYPE = jnp.float16
+CHUNKS = 2
 
 X_SWAP = [(0, 1), (1, 0), (2, 3), (3, 2)]
 Y_SWAP = [(0, 2), (2, 0), (1, 3), (3, 1)]
@@ -73,20 +73,8 @@
     def half_columns(weight, *earlier):
         return lax.dynamic_slice_in_dim(weight, after(core, *earlier) * width, width, 1)
 
-    def dots(lefts, own_half, weights):
-        return [
-            jnp.dot(
-                pick(left, own_half, 0).reshape(-1, block),
-                weights[0],
-                preferred_element_type=jnp.float32,
-            )
-            + jnp.dot(
-                pick(left, 1 - own_half, 0).reshape(-1, block),
-                weights[1],
-                preferred_element_type=jnp.float32,
-            )
-            for left in lefts
-        ]
+    def dot(left, weight):
+        return jnp.dot(left.reshape(-1, block), weight, preferred_element_type=jnp.float32)
 
     def line_parts():
         mine = lax.dynamic_slice_in_dim(gained, x * block, block, 3)
@@ -102,53 +90,73 @@
         def down(value, k):
             return lax.ppermute(value, "vocab", [(z + 1, z) for z in range(vocab - k)])
 
-        below, above = [own, up(own, 1)], [own, down(own, 1)]
-
-        def quarter(place, reach):
-            part = own
+        first = level // 2
+        keep_near = (core ^ first) == 0
+        kept, taken = half_columns(head_weight, own), half_columns(take, own)
+        near_weight, far_weight = lax.optimization_barrier(
+            (jnp.where(keep_near, kept, taken), jnp.where(keep_near, taken, kept))
+        )
+        scale = row_scale(own)
+        ready = (scale, near_weight, far_weight)
+        below_1, above_1 = after(up(own, 1), *ready), after(down(own, 1), *ready)
+        belows, aboves = [], []
+        for c in range(CHUNKS):
+            below = [own[c], below_1[c], up(below_1[c], 2)]
+            above = [own[c], above_1[c], down(above_1[c], 2)]
+            if c:
+                below[2] = after(below[2], belows[-1][2], aboves[-1][2])
+                above[2] = after(above[2], belows[-1][2], aboves[-1][2])
+            belows.append(below)
+            aboves.append(above)
+
+        def quarter(c, place, reach):
+            part = own[c]
             for k in range(1, reach + 1):
-                part = jnp.where(level - place == k, below[k], part)
-                part = jnp.where(place - level == k, above[k], part)
+                part = jnp.where(level - place == k, belows[c][k], part)
+                part = jnp.where(place - level == k, aboves[c][k], part)
             return part
 
-        first = level // 2
-        weights = lax.optimization_barrier(
-            (half_columns(head_weight, own), half_columns(take, own))
-        )
-        below[1], above[1] = after(below[1], *weights), after(above[1], *weights)
-        got_near = lax.ppermute(quarter(1 - y + 2 * first, 1), "batch", Y_SWAP)
-        below.append(up(below[1], 2))
-        above.append(down(above[1], 2))
-        below[2], above[2] = after(below[2], got_near), after(above[2], got_near)
-        near = by_y(quarter(y + 2 * first, 1), after(got_near, below[2], above[2]), 1)
-        nears = (near, swapped(near))
-
+        def quarters(place, reach):
+            return jnp.stack([quarter(c, place, reach) for c in range(CHUNKS)])
+
+        got_near = lax.ppermute(quarters(1 - y + 2 * first, 1), "batch", Y_SWAP)
         far = 1 - y + 2 * (1 - first)
         tips = [(0, 0), (1, vocab - 1)]
         pairs = [(b * vocab + z, (b ^ 2) * vocab + z) for b in range(4) for z in range(vocab)]
         late = [pair for pair in pairs if (pair[0] // vocab // 2, pair[0] % vocab) in tips]
         early = [pair for pair in pairs if pair not in late]
-        got_early = lax.ppermute(quarter(far, 2), ("batch", "vocab"), early)
-        mine_early = quarter(y + 2 * (1 - first), 2)
+        far_sent = quarters(far, 2)
+        got_early = lax.ppermute(far_sent, ("batch", "vocab"), early)
         is_late = (level == 0) & (y == 1) | (level == vocab - 1) & (y == 0)
-        below_3, above_3 = up(below[2], 3), down(above[2], 3)
-        last = after(jnp.where(level == 0, above_3, below_3), got_early)
-        lasts = [last[c] for c in range(CHUNKS)]
-        lates = [lax.ppermute(last, ("batch", "vocab"), late) for last in lasts]
+        ends = []
+        for c in range(CHUNKS):
+            earlier = (got_near,) if c else ()
+            below_3 = up(after(belows[c][2], *earlier), 3)
+            above_3 = down(after(aboves[c][2], *earlier), 3)
+            earlier = (belows[1][2], aboves[1][2]) if c == 0 else ends[-1:]
+            ends.append(after(jnp.where(level == 0, above_3, below_3), got_near, *earlier))
+        lates = [lax.ppermute(end, ("batch", "vocab"), late) for end in ends]
+        near = by_y(quarters(y + 2 * first, 1), after(got_near, belows[1][2]), 1)
+        nears = (near, swapped(near))
+        near_parts = [dot(left, near_weight).reshape(CHUNKS, -1, width) for left in nears]
 
         def parts(c, *earlier):
-            got_late = after(lates[c], *earlier)
-            got = jnp.where(is_late, got_late, got_early[c])
-            mine = jnp.where(is_late, lasts[c], mine_early[c])
-            both = by_y(mine, got, 0)
-            fars = lax.optimization_barrier((both, swapped(both)))
-            lefts = [jnp.stack([near[c], far]) for near, far in zip(nears, fars)]
-            return [after(part, *lates[c + 1 :]) for part in dots(lefts, core ^ first, weights)]
-
-        return parts
+            got_late = after(lates[c], *(earlier or ends[1:]))
+            mine = jnp.where(is_late, ends[c], quarter(c, y + 2 * (1 - first), 2))
+            far = by_y(mine, jnp.where(is_late, got_late, got_early[c]), 0)
+            found = [
+                near_part[c] + dot(left, far_weight)
+                for near_part, left in zip(near_parts, (far, swapped(far)))
+            ]
+            return found
+
+        return parts, scale
 
     def gathered_parts():
-        weights = (half_columns(head_weight), half_columns(take))
+        near_weight, far_weight = half_columns(head_weight), half_columns(take)
+
+        def part(left):
+            return dot(pick(left, core, 0), near_weight) + dot(pick(left, 1 - core, 0), far_weight)
 
         def parts(c, *earlier):
             whole = lax.all_gather(gained[c], "vocab", axis=2, tiled=True)
@@ -156,12 +164,12 @@
             whole = lax.all_to_all(whole, "batch", split_axis=0, concat_axis=0)
             whole = whole.reshape(2, 2, 2, 2, step, block).transpose(2, 0, 1, 3, 4, 5)
             whole = after(whole, *earlier)
-            return dots((whole, swapped(whole)), core, weights)
-
-        return parts
+            return [part(whole), part(swapped(whole))]
+
+        return parts, row_scale()
 
     lined = depth == 2 * block and vocab == 4
-    parts = line_parts() if lined else gathered_parts()
+    parts, scale = line_parts() if lined else gathered_parts()
     kept, sends = [], []
     for c in range(CHUNKS):
         whole = [part * SHRINK for part in parts(c, *(sends[-1] if c else ()))]
@@ -171,7 +179,6 @@
         sends.append(
             (pick(low, 1 - x, 3).astype(SUM_TYPE), pick(high, 1 - y, 2).astype(SUM_TYPE))
         )
-    scale = row_scale(*sends[-1])
     halfway, more_sends = [], []
     for c in range(CHUNKS):
         away_x = lax.ppermute(sends[c][0], "batch", X_SWAP)
@@ -188,6 +195,8 @@
     for c in range(CHUNKS):
         next_y = lax.ppermute(more_sends[c][0], "batch", Y_SWAP)
         next_x = lax.ppermute(more_sends[c][1], "batch", X_SWAP)
+        if c + 1 < CHUNKS:
+            next_y, next_x = after(next_y, *more_sends[c + 1]), after(next_x, *more_sends[c + 1])
         sums = jnp.concatenate(
             [
                 halfway[c][0] + next_y.astype(jnp.float32),
@@ -195,9 +204,7 @@
             ],
             axis=-1,
         ).astype(SUM_TYPE)
-        theirs = lax.ppermute(pick(sums, 1 - core, 1), "pair", CORE_SWAP)
-        done.append((pick(sums, core, 1), theirs))
-
+        done.append((pick(sums, core, 1), swapped(pick(sums, 1 - core, 1))))
     mine = jnp.concatenate([part[0] for part in done], axis=1)
     theirs = jnp.concatenate([part[1] for part in done], axis=1)
 

time: 144 us -> 145 us (level)
  local copies, waits for them, and re-layouts: 17.1 us -> 5.48 us
  other arithmetic: 18.4 us -> 24.8 us
  matrix products: 10.3 us -> 14 us
  waiting for transfers between devices: 47.7 us -> 49.3 us
    ppermute x6 -> x4, waiting for transfers between devices: 13 us -> 0.01 us  [the longest x2 0.01 us: line_parts(): lates = [lax.ppermute(end, ('batch', 'vocab'), late) for end in ends]]
    ppermute x2, waiting for transfers between devices: 0.01 us -> 11.3 us  [on_device(): away_x = lax.ppermute(sends[c][0], 'batch', X_SWAP)]
    select_n x3 -> x4, other arithmetic: 1.46 us -> 11.2 us  [the longest x1 9.9 us: line_parts(): jnp.where(keep_near, taken, kept)]
    dynamic_slice x2 -> x0, local copies, waits for them, and re-layouts: 9.53 us -> none  [half_columns(): lax.dynamic_slice_in_dim(weight, after(core, *earlier) * width, width, 1)]
    ppermute x2, waiting for transfers between devices: 11.7 us -> 7.85 us  [on_device(): next_y = lax.ppermute(more_sends[c][0], 'batch', Y_SWAP)]
    ppermute x2, starting transfers between devices: 4.34 us -> 0.6 us  [on_device(): next_y = lax.ppermute(more_sends[c][0], 'batch', Y_SWAP)]
    dot_general x8 -> x6, matrix products: 10.3 us -> 14 us  [dot(): jnp.dot(left.reshape(-1, block), weight, preferred_element_type=jnp.float32)]
    ppermute x3 -> x5, waiting for transfers between devices: 14.2 us -> 17.9 us  [down(): return lax.ppermute(value, 'vocab', [(z + 1, z) for z in range(vocab - k)])]
  transfers between devices with their start and end apart: 32 -> 36, of which waited for: 14 -> 17; matrix products, arithmetic and copies ran while one was open for 22% -> 25% of each run, Pallas kernels for 0% -> 0%
where the time goes in v13:
time: 145 us; the launch traced here: 144 us
  waiting for transfers between devices  49.3 us (34%)
  starting transfers between devices  49.2 us (34%)
  other arithmetic  24.8 us (17%)
  matrix products  14 us (10%)
  local copies, waits for them, and re-layouts  5.48 us (4%)
    ppermute x5, waiting for transfers between devices, down(): return lax.ppermute(value, 'vocab', [(z + 1, z) for z in range(vocab - k)])  17.9 us
    dot_general x6, matrix products, dot(): jnp.dot(left.reshape(-1, block), weight, preferred_element_type=jnp.float32)  14 us
    ppermute x2, waiting for transfers between devices, on_device(): away_x = lax.ppermute(sends[c][0], 'batch', X_SWAP)  11.3 us
    select_n x1, other arithmetic, line_parts(): jnp.where(keep_near, taken, kept)  9.9 us
    ppermute x2, starting transfers between devices, line_parts(): lates = [lax.ppermute(end, ('batch', 'vocab'), late) for end in ends]  8.74 us
    ppermute x2, waiting for transfers between devices, on_device(): next_y = lax.ppermute(more_sends[c][0], 'batch', Y_SWAP)  7.85 us
    ppermute x5, starting transfers between devices, down(): return lax.ppermute(value, 'vocab', [(z + 1, z) for z in range(vocab - k)])  6.44 us
    ppermute x5, starting transfers between devices, up(): lax.ppermute(value, 'vocab', [(z, z + 1) for z in range(k - 1, vocab - 1)])  6.21 us
  transfers between devices with their start and end apart: 36, of which 17 were waited for; matrix products, arithmetic and copies ran while one was open for 25% of the time, Pallas kernels for 0%

profile of v13, /device:TPU:0, one launch (start us, length us, event | category | flops | bytes accessed | tf_op | source)
XLA Modules:
  0.0 144.1 jit_solution(11034593304131380038)
XLA Ops:
  3.0 2.6 %collective-permute-start = (bf16[2,2,32,1024]{3,2,0,1:T(8,128)(2,1)S(1)}, bf16[2,2,32,1024]{3,2,0,1:T(8,128)(2,1)S(1)}, u32[]{:S(2)}, u32[]{:S(2)}) collective-permute-start(bf16[2,2,32,1024]{3,2,0,1:T(8,128)(2,1)S(1)} %dynamic-slice_bitcast_fusion), channel_id=1, source_target_pairs={{0,4},{4,0},{8,12},{12,8},{1,5},{5,1},{9,13},{13,9},{2,6},{6,2},{1... | collective-permute-start | bytes 786440 | tf_op jit(solution)/shard_map/ppermute | solution.py:81
  6.8 1.6 %collective-permute-start.1 = (f32[128]{0:T(128)S(1)}, f32[128]{0:T(128)S(1)}, u32[]{:S(2)}, u32[]{:S(2)}) collective-permute-start(f32[128]{0:T(128)S(1)} %multiply_reduce_fusion), channel_id=1, source_target_pairs={{0,1},{1,0},{2,3},{3,2},{4,5},{5,4},{6,7},{7,6},{8,9},{9,8},{10,11... | collective-permute-start | bytes 1544 | tf_op jit(solution)/shard_map/ppermute | solution.py:46
  8.5 2.0 %collective-permute-done.1 = f32[128]{0:T(128)S(1)} collective-permute-done((f32[128]{0:T(128)S(1)}, f32[128]{0:T(128)S(1)}, u32[]{:S(2)}, u32[]{:S(2)}) %collective-permute-start.1) | collective-permute-done | bytes 544 | tf_op jit(solution)/shard_map/ppermute | solution.py:46
  10.4 2.6 %collective-permute-start.2 = (f32[128]{0:T(128)S(1)}, f32[128]{0:T(128)S(1)}, u32[]{:S(2)}, u32[]{:S(2)}) collective-permute-start(f32[128]{0:T(128)S(1)} %add.131), channel_id=1, source_target_pairs={{0,2},{1,3},{2,0},{3,1},{4,6},{5,7},{6,4},{7,5},{8,10},{9,11},{10,... | collective-permute-start | bytes 1544 | tf_op jit(solution)/shard_map/ppermute | solution.py:46
  13.0 1.9 %collective-permute-done.2 = f32[128]{0:T(128)S(1)} collective-permute-done((f32[128]{0:T(128)S(1)}, f32[128]{0:T(128)S(1)}, u32[]{:S(2)}, u32[]{:S(2)}) %collective-permute-start.2) | collective-permute-done | bytes 544 | tf_op jit(solution)/shard_map/ppermute | solution.py:46
  15.2 3.5 %collective-permute-start.7 = (bf16[2,2,2,32,1024]{4,3,2,1,0:T(8,128)(2,1)S(1)}, bf16[2,2,2,32,1024]{4,3,2,1,0:T(8,128)(2,1)S(1)}, u32[]{:S(2)}, u32[]{:S(2)}) collective-permute-start(bf16[2,2,2,32,1024]{4,3,2,1,0:T(8,128)(2,1)S(1)} %copy.16), channel_id=1, source_target_pairs={{0,1},{1,2},{2,3},{4,5},{5,6},{6,7},{8,9},{9,10},{10,11},{12,13},{... | collective-permute-start | bytes 1572872 | tf_op jit(solution)/shard_map/ppermute | solution.py:88
  18.7 1.3 collective-permute-start.3
  20.7 4.3 %collective-permute-start.5 = (f32[64]{0:T(128)S(1)}, f32[64]{0:T(128)S(1)}, u32[]{:S(2)}, u32[]{:S(2)}) collective-permute-start(f32[64]{0:T(128)S(1)} %get-tuple-element.87), channel_id=1, source_target_pairs={{0,4},{4,12},{8,20},{12,28},{16,0},{20,8},{24,16},{28,24},{1,5},{5... | collective-permute-start | bytes 776 | tf_op jit(solution)/shard_map/ppermute | solution.py:57
  26.3 9.9 %broadcast_select_fusion = (bf16[1024,2048]{1,0:T(8,128)(2,1)}, bf16[1024,2048]{1,0:T(8,128)(2,1)}) fusion(pred[]{:T(512)S(6)} %eq.44, bf16[1024,4096]{1,0:T(8,128)(2,1)} %collective-permute-done.6, s32[]{:T(128)S(6)} %select_n.336, bf16[1024,4096]{1,0:T(8,128)(2,1)} %param.5), kind=kLoop, calls=%fused_computation.4 | loop fusion | flops 4194304 | bytes 16777220 | tf_op jit(solution)/shard_map/jit(_where)/select_n | solution.py:97
  43.0 1.6 %collective-permute-start.8 = (bf16[2,2,2,32,1024]{4,3,2,1,0:T(8,128)(2,1)}, bf16[2,2,2,32,1024]{4,3,2,1,0:T(8,128)(2,1)}, u32[]{:S(2)}, u32[]{:S(2)}) collective-permute-start(bf16[2,2,2,32,1024]{4,3,2,1,0:T(8,128)(2,1)} %pad_maximum_fusion.3), channel_id=1, source_target_pairs={{0,8},{8,0},{4,12},{12,4},{1,9},{9,1},{5,13},{13,5},{2,10},{10,2},... | collective-permute-start | bytes 1572872 | tf_op jit(solution)/shard_map/ppermute | solution.py:122
  44.6 3.1 %collective-permute-done.11 = bf16[2,2,32,1024]{3,2,1,0:T(8,128)(2,1)S(1)} collective-permute-done((bf16[2,2,32,1024]{3,2,1,0:T(8,128)(2,1)}, bf16[2,2,32,1024]{3,2,1,0:T(8,128)(2,1)S(1)}, u32[]{:S(2)}, u32[]{:S(2)}) %collective-permute-start.11) | collective-permute-done | bytes 262176 | tf_op jit(solution)/shard_map/ppermute | solution.py:91
  49.7 8.0 %collective-permute-done.14 = bf16[2,2,32,1024]{3,2,1,0:T(8,128)(2,1)S(1)} collective-permute-done((bf16[2,2,32,1024]{3,2,1,0:T(8,128)(2,1)S(1)}, bf16[2,2,32,1024]{3,2,1,0:T(8,128)(2,1)S(1)}, u32[]{:S(2)}, u32[]{:S(2)}) %collective-permute-start.14) | collective-permute-done | bytes 262176 | tf_op jit(solution)/shard_map/ppermute | solution.py:91
  61.1 4.8 %collective-permute-start.15 = (bf16[2,2,32,1024]{3,2,1,0:T(8,128)(2,1)S(1)}, bf16[2,2,32,1024]{3,2,1,0:T(8,128)(2,1)S(1)}, u32[]{:S(2)}, u32[]{:S(2)}) collective-permute-start(bf16[2,2,32,1024]{3,2,1,0:T(8,128)(2,1)S(1)} %broadcast_select_fusion.3), channel_id=1, source_target_pairs={{0,8},{4,12},{11,3},{15,7},{16,24},{20,28},{27,19},{31,23}} | collective-permute-start | bytes 786440 | tf_op jit(solution)/shard_map/ppermute | solution.py:138
  67.9 2.4 %fusion.75 = f32[512,2048]{1,0:T(8,128)S(1)} fusion(bf16[512,1024]{1,0:T(8,128)(2,1)S(1)} %bitcast.249, bf16[1024,2048]{1,0:T(8,128)(2,1)S(1)} %copy-done.10), kind=kOutput, calls=%fused_computation.178 | convolution fusion | flops 2147483648 | bytes 9437184 | tf_op jit(solution)/shard_map/dot_general | solution.py:77
  70.3 6.7 %collective-permute-done.16 = bf16[2,2,32,1024]{3,2,1,0:T(8,128)(2,1)S(1)} collective-permute-done((bf16[2,2,32,1024]{3,2,1,0:T(8,128)(2,1)S(1)}, bf16[2,2,32,1024]{3,2,1,0:T(8,128)(2,1)S(1)}, u32[]{:S(2)}, u32[]{:S(2)}) %collective-permute-start.16) | collective-permute-done | bytes 262176 | tf_op jit(solution)/shard_map/ppermute | solution.py:91
  77.0 4.0 %collective-permute-start.22 = (bf16[2,2,32,1024]{3,2,1,0:T(8,128)(2,1)S(1)}, bf16[2,2,32,1024]{3,2,1,0:T(8,128)(2,1)S(1)}, u32[]{:S(2)}, u32[]{:S(2)}) collective-permute-start(bf16[2,2,32,1024]{3,2,1,0:T(8,128)(2,1)S(1)} %broadcast_select_fusion.2), channel_id=1, source_target_pairs={{0,8},{4,12},{11,3},{15,7},{16,24},{20,28},{27,19},{31,23}} | collective-permute-start | bytes 786440 | tf_op jit(solution)/shard_map/ppermute | solution.py:138
  81.6 1.3 fusion.1
  83.0 2.4 %fusion.76 = f32[512,2048]{1,0:T(8,128)S(1)} fusion(bf16[512,1024]{1,0:T(8,128)(2,1)S(1)} %bitcast.250, bf16[1024,2048]{1,0:T(8,128)(2,1)S(1)} %copy-done.10), kind=kOutput, calls=%fused_computation.179 | convolution fusion | flops 2147483648 | bytes 9437184 | tf_op jit(solution)/shard_map/dot_general | solution.py:77
  85.4 1.3 fusion.5
  93.2 4.3 %fusion = f32[256,2048]{1,0:T(8,128)S(1)} fusion(bf16[256,1024]{1,0:T(8,128)(2,1)S(1)} %bitcast.246, bf16[1024,2048]{1,0:T(8,128)(2,1)} %get-tuple-element.26, f32[512,2048]{1,0:T(8,128)} %copy-done.6), kind=kOutput, calls=%fused_computation.7 | convolution fusion | flops 1074790400 | bytes 8912896 | tf_op jit(solution)/shard_map/dot_general | solution.py:77
  98.6 2.4 %fusion.4 = f32[256,2048]{1,0:T(8,128)S(1)} fusion(f32[512,2048]{1,0:T(8,128)S(1)} %copy-done.8, bf16[256,1024]{1,0:T(8,128)(2,1)} %bitcast.38, bf16[1024,2048]{1,0:T(8,128)(2,1)S(1)} %copy-done.1), kind=kOutput, calls=%fused_computation.13 | convolution fusion | flops 1074790400 | bytes 8912896 | tf_op jit(solution)/shard_map/dot_general | solution.py:77
  101.5 1.4 %collective-permute-start.25 = (f16[2,2,2,32,1024]{4,3,1,0,2:T(8,128)(2,1)S(1)}, f16[2,2,2,32,1024]{4,3,1,0,2:T(8,128)(2,1)S(1)}, u32[]{:S(2)}, u32[]{:S(2)}) collective-permute-start(f16[2,2,2,32,1024]{4,3,1,0,2:T(8,128)(2,1)S(1)} %fusion.21), channel_id=1, source_target_pairs={{0,4},{4,0},{8,12},{12,8},{1,5},{5,1},{9,13},{13,9},{2,6},{6,2},{1... | collective-permute-start | bytes 1572872 | tf_op jit(solution)/shard_map/ppermute | solution.py:184
  103.0 2.1 %collective-permute-start.26 = (f16[2,2,2,32,1024]{4,3,2,1,0:T(8,128)(2,1)S(1)}, f16[2,2,2,32,1024]{4,3,2,1,0:T(8,128)(2,1)S(1)}, u32[]{:S(2)}, u32[]{:S(2)}) collective-permute-start(f16[2,2,2,32,1024]{4,3,2,1,0:T(8,128)(2,1)S(1)} %fusion.22), channel_id=1, source_target_pairs={{0,8},{8,0},{4,12},{12,4},{1,9},{9,1},{5,13},{13,5},{2,10},{10,2},... | collective-permute-start | bytes 1572872 | tf_op jit(solution)/shard_map/ppermute | solution.py:185
  105.1 2.5 %collective-permute-done.21 = f16[2,2,2,32,1024]{4,3,1,0,2:T(8,128)(2,1)S(1)} collective-permute-done((f16[2,2,2,32,1024]{4,3,1,0,2:T(8,128)(2,1)}, f16[2,2,2,32,1024]{4,3,1,0,2:T(8,128)(2,1)S(1)}, u32[]{:S(2)}, u32[]{:S(2)}) %collective-permute-start.21) | collective-permute-done | bytes 524320 | tf_op jit(solution)/shard_map/ppermute | solution.py:184
  108.5 1.4 %collective-permute-start.28 = (f16[2,2,32,1024]{3,2,1,0:T(8,128)(2,1)S(1)}, f16[2,2,32,1024]{3,2,1,0:T(8,128)(2,1)S(1)}, u32[]{:S(2)}, u32[]{:S(2)}) collective-permute-start(f16[2,2,32,1024]{3,2,1,0:T(8,128)(2,1)S(1)} %fusion.31), channel_id=1, source_target_pairs={{0,4},{4,0},{8,12},{12,8},{1,5},{5,1},{9,13},{13,9},{2,6},{6,2},{1... | collective-permute-start | bytes 786440 | tf_op jit(solution)/shard_map/ppermute | solution.py:197
  110.0 8.8 %collective-permute-done.25 = f16[2,2,2,32,1024]{4,3,1,0,2:T(8,128)(2,1)S(1)} collective-permute-done((f16[2,2,2,32,1024]{4,3,1,0,2:T(8,128)(2,1)S(1)}, f16[2,2,2,32,1024]{4,3,1,0,2:T(8,128)(2,1)S(1)}, u32[]{:S(2)}, u32[]{:S(2)}) %collective-permute-start.25) | collective-permute-done | bytes 524320 | tf_op jit(solution)/shard_map/ppermute | solution.py:184
  121.3 3.8 %collective-permute-done.24 = f16[2,2,32,1024]{3,2,1,0:T(8,128)(2,1)S(1)} collective-permute-done((f16[2,2,32,1024]{3,2,1,0:T(8,128)(2,1)S(1)}, f16[2,2,32,1024]{3,2,1,0:T(8,128)(2,1)S(1)}, u32[]{:S(2)}, u32[]{:S(2)}) %collective-permute-start.24) | collective-permute-done | bytes 262176 | tf_op jit(solution)/shard_map/ppermute | solution.py:196
  125.5 4.0 %collective-permute-done.29 = f16[2,2,32,1024]{3,2,1,0:T(8,128)(2,1)S(1)} collective-permute-done((f16[2,2,32,1024]{3,2,1,0:T(8,128)(2,1)S(1)}, f16[2,2,32,1024]{3,2,1,0:T(8,128)(2,1)S(1)}, u32[]{:S(2)}, u32[]{:S(2)}) %collective-permute-start.29) | collective-permute-done | bytes 262176 | tf_op jit(solution)/shard_map/ppermute | solution.py:196
  130.1 1.4 %collective-permute-done.32 = f16[2,32,2048]{2,1,0:T(8,128)(2,1)S(1)} collective-permute-done((f16[2,32,2048]{2,1,0:T(8,128)(2,1)S(1)}, f16[2,32,2048]{2,1,0:T(8,128)(2,1)S(1)}, u32[]{:S(2)}, u32[]{:S(2)}) %collective-permute-start.32) | collective-permute-done | bytes 262176 | tf_op jit(solution)/shard_map/ppermute | solution.py:71
  133.1 3.9 %collective-permute-start.35 = (f32[4,64]{1,0:T(4,128)S(1)}, f32[4,64]{1,0:T(4,128)S(1)}, u32[]{:S(2)}, u32[]{:S(2)}) collective-permute-start(f32[4,64]{1,0:T(4,128)S(1)} %get-tuple-element.79), channel_id=1, source_target_pairs={{0,3},{1,0},{2,1},{3,2},{4,7},{5,4},{6,5},{7,6},{8,11},{9,8},{10,9... | collective-permute-start | bytes 3080 | tf_op jit(solution)/shard_map/ppermute | solution.py:230
  138.3 3.2 %collective-permute-done.34 = f32[4,64]{1,0:T(4,128)S(1)} collective-permute-done((f32[4,64]{1,0:T(4,128)S(1)}, f32[4,64]{1,0:T(4,128)S(1)}, u32[]{:S(2)}, u32[]{:S(2)}) %collective-permute-start.34) | collective-permute-done | bytes 1056 | tf_op jit(solution)/shard_map/ppermute | solution.py:230
  142.5 1.6 %fusion.18 = (f32[64,4096]{1,0:T(8,128)}, f32[64,4096]{1,0:T(8,128)}) fusion(f32[64]{0:T(128)S(1)} %get-tuple-element.80, f32[64]{0:T(128)S(1)} %get-tuple-element.82, f16[64,2048]{1,0:T(8,128)(2,1)S(1)} %get-tuple-element.59, f16[64,2048]{1,0:T(8,128)(2,1)S(1)} %get-tuple-element.58, f32[64,4096]{1,0:T(8,128)S(1)} %get-tuple-element.43, ...), kind=kLoop, calls=%fused_computation.45 | loop fusion | flops 1310720 | bytes 3670784 | tf_op jit(solution)/shard_map/sub | solution.py:237
  (139 shorter events, 36.7 us)
Async XLA Ops:
  0.6 25.7 %collective-permute-start.6 = (bf16[1024,4096]{1,0:T(8,128)(2,1)}, bf16[1024,4096]{1,0:T(8,128)(2,1)}, u32[]{:S(2)}, u32[]{:S(2)}) collective-permute-start(bf16[1024,4096]{1,0:T(8,128)(2,1)} %param.5), channel_id=1, source_target_pairs={{0,16},{16,0},{1,17},{17,1},{2,18},{18,2},{3,19},{19,3},{4,20},{20... | collective-permute-start | bytes 25165832 | tf_op jit(solution)/shard_map/ppermute | solution.py:43
  3.0 11.9 %collective-permute-start = (bf16[2,2,32,1024]{3,2,0,1:T(8,128)(2,1)S(1)}, bf16[2,2,32,1024]{3,2,0,1:T(8,128)(2,1)S(1)}, u32[]{:S(2)}, u32[]{:S(2)}) collective-permute-start(bf16[2,2,32,1024]{3,2,0,1:T(8,128)(2,1)S(1)} %dynamic-slice_bitcast_fusion), channel_id=1, source_target_pairs={{0,4},{4,0},{8,12},{12,8},{1,5},{5,1},{9,13},{13,9},{2,6},{6,2},{1... | collective-permute-start | bytes 786440 | tf_op jit(solution)/shard_map/ppermute | solution.py:81
  15.2 21.0 %collective-permute-start.7 = (bf16[2,2,2,32,1024]{4,3,2,1,0:T(8,128)(2,1)S(1)}, bf16[2,2,2,32,1024]{4,3,2,1,0:T(8,128)(2,1)S(1)}, u32[]{:S(2)}, u32[]{:S(2)}) collective-permute-start(bf16[2,2,2,32,1024]{4,3,2,1,0:T(8,128)(2,1)S(1)} %copy.16), channel_id=1, source_target_pairs={{0,1},{1,2},{2,3},{4,5},{5,6},{6,7},{8,9},{9,10},{10,11},{12,13},{... | collective-permute-start | bytes 1572872 | tf_op jit(solution)/shard_map/ppermute | solution.py:88
  18.7 17.5 %collective-permute-start.3 = (bf16[2,2,2,32,1024]{4,3,2,1,0:T(8,128)(2,1)S(1)}, bf16[2,2,2,32,1024]{4,3,2,1,0:T(8,128)(2,1)S(1)}, u32[]{:S(2)}, u32[]{:S(2)}) collective-permute-start(bf16[2,2,2,32,1024]{4,3,2,1,0:T(8,128)(2,1)S(1)} %copy.16), channel_id=1, source_target_pairs={{1,0},{2,1},{3,2},{5,4},{6,5},{7,6},{9,8},{10,9},{11,10},{13,12},{... | collective-permute-start | bytes 1572872 | tf_op jit(solution)/shard_map/ppermute | solution.py:91
  20.0 5.0 %collective-permute-start.4 = (f32[64]{0:T(128)S(1)}, f32[64]{0:T(128)S(1)}, u32[]{:S(2)}, u32[]{:S(2)}) collective-permute-start(f32[64]{0:T(128)S(1)} %get-tuple-element.86), channel_id=1, source_target_pairs={{0,0},{4,8},{8,16},{12,24},{16,4},{20,12},{24,20},{28,28},{1,1},{5... | collective-permute-start | bytes 776 | tf_op jit(solution)/shard_map/ppermute | solution.py:57
  20.7 5.6 %collective-permute-start.5 = (f32[64]{0:T(128)S(1)}, f32[64]{0:T(128)S(1)}, u32[]{:S(2)}, u32[]{:S(2)}) collective-permute-start(f32[64]{0:T(128)S(1)} %get-tuple-element.87), channel_id=1, source_target_pairs={{0,4},{4,12},{8,20},{12,28},{16,0},{20,8},{24,16},{28,24},{1,5},{5... | collective-permute-start | bytes 776 | tf_op jit(solution)/shard_map/ppermute | solution.py:57
  37.5 10.3 %collective-permute-start.11 = (bf16[2,2,32,1024]{3,2,1,0:T(8,128)(2,1)}, bf16[2,2,32,1024]{3,2,1,0:T(8,128)(2,1)S(1)}, u32[]{:S(2)}, u32[]{:S(2)}) collective-permute-start(bf16[2,2,32,1024]{3,2,1,0:T(8,128)(2,1)} %get-tuple-element.75), channel_id=1, source_target_pairs={{1,0},{2,1},{5,4},{6,5},{9,8},{10,9},{13,12},{14,13},{17,16},{18,1... | collective-permute-start | bytes 786440 | tf_op jit(solution)/shard_map/ppermute | solution.py:91
  38.7 10.3 %collective-permute-start.10 = (bf16[2,2,32,1024]{3,2,1,0:T(8,128)(2,1)}, bf16[2,2,32,1024]{3,2,1,0:T(8,128)(2,1)S(1)}, u32[]{:S(2)}, u32[]{:S(2)}) collective-permute-start(bf16[2,2,32,1024]{3,2,1,0:T(8,128)(2,1)} %get-tuple-element.77), channel_id=1, source_target_pairs={{1,2},{2,3},{5,6},{6,7},{9,10},{10,11},{13,14},{14,15},{17,18},{18... | collective-permute-start | bytes 786440 | tf_op jit(solution)/shard_map/ppermute | solution.py:88
  40.2 9.5 %collective-permute-start.9 = (bf16[2,2,32,1024]{3,2,1,0:T(8,128)(2,1)}, bf16[2,2,32,1024]{3,2,1,0:T(8,128)(2,1)S(1)}, u32[]{:S(2)}, u32[]{:S(2)}) collective-permute-start(bf16[2,2,32,1024]{3,2,1,0:T(8,128)(2,1)} %slice_bitcast_fusion.2), channel_id=1, source_target_pairs={{1,2},{2,3},{5,6},{6,7},{9,10},{10,11},{13,14},{14,15},{17,18},{18... | collective-permute-start | bytes 786440 | tf_op jit(solution)/shard_map/ppermute | solution.py:88
  40.8 16.9 %collective-permute-start.14 = (bf16[2,2,32,1024]{3,2,1,0:T(8,128)(2,1)S(1)}, bf16[2,2,32,1024]{3,2,1,0:T(8,128)(2,1)S(1)}, u32[]{:S(2)}, u32[]{:S(2)}) collective-permute-start(bf16[2,2,32,1024]{3,2,1,0:T(8,128)(2,1)S(1)} %get-tuple-element.76), channel_id=1, source_target_pairs={{1,0},{2,1},{5,4},{6,5},{9,8},{10,9},{13,12},{14,13},{17,16},{18,1... | collective-permute-start | bytes 786440 | tf_op jit(solution)/shard_map/ppermute | solution.py:91
  43.0 16.6 %collective-permute-start.8 = (bf16[2,2,2,32,1024]{4,3,2,1,0:T(8,128)(2,1)}, bf16[2,2,2,32,1024]{4,3,2,1,0:T(8,128)(2,1)}, u32[]{:S(2)}, u32[]{:S(2)}) collective-permute-start(bf16[2,2,2,32,1024]{4,3,2,1,0:T(8,128)(2,1)} %pad_maximum_fusion.3), channel_id=1, source_target_pairs={{0,8},{8,0},{4,12},{12,4},{1,9},{9,1},{5,13},{13,5},{2,10},{10,2},... | collective-permute-start | bytes 1572872 | tf_op jit(solution)/shard_map/ppermute | solution.py:122
  47.7 13.4 %collective-permute-start.12 = (bf16[2,2,32,1024]{3,2,1,0:T(8,128)(2,1)S(1)}, bf16[2,2,32,1024]{3,2,1,0:T(8,128)(2,1)S(1)}, u32[]{:S(2)}, u32[]{:S(2)}) collective-permute-start(bf16[2,2,32,1024]{3,2,1,0:T(8,128)(2,1)S(1)} %collective-permute-done.11), channel_id=1, source_target_pairs={{1,0},{5,4},{9,8},{13,12},{17,16},{21,20},{25,24},{29,28}} | collective-permute-start | bytes 786440 | tf_op jit(solution)/shard_map/ppermute | solution.py:91
  49.0 12.1 %collective-permute-start.13 = (bf16[2,2,32,1024]{3,2,1,0:T(8,128)(2,1)S(1)}, bf16[2,2,32,1024]{3,2,1,0:T(8,128)(2,1)S(1)}, u32[]{:S(2)}, u32[]{:S(2)}) collective-permute-start(bf16[2,2,32,1024]{3,2,1,0:T(8,128)(2,1)S(1)} %collective-permute-done.10), channel_id=1, source_target_pairs={{2,3},{6,7},{10,11},{14,15},{18,19},{22,23},{26,27},{30,31}} | collective-permute-start | bytes 786440 | tf_op jit(solution)/shard_map/ppermute | solution.py:88
  58.3 22.7 %collective-permute-start.18 = (bf16[2,2,2,32,1024]{4,3,2,1,0:T(8,128)(2,1)S(1)}, bf16[2,2,2,32,1024]{4,3,2,1,0:T(8,128)(2,1)S(1)}, u32[]{:S(2)}, u32[]{:S(2)}) collective-permute-start(bf16[2,2,2,32,1024]{4,3,2,1,0:T(8,128)(2,1)S(1)} %pad_maximum_fusion.4), channel_id=1, source_target_pairs={{1,9},{2,10},{3,11},{5,13},{6,14},{7,15},{8,0},{9,1},{10,2},{12,4}... | collective-permute-start | bytes 1572872 | tf_op jit(solution)/shard_map/ppermute | solution.py:129
  60.9 22.0 %collective-permute-start.19 = (bf16[2,2,2,2,32,1024]{5,4,3,2,0,1:T(8,128)(2,1)S(1)}, bf16[2,2,2,2,32,1024]{5,4,3,2,0,1:T(8,128)(2,1)S(1)}, u32[]{:S(2)}, u32[]{:S(2)}) collective-permute-start(bf16[2,2,2,2,32,1024]{5,4,3,2,0,1:T(8,128)(2,1)S(1)} %pad_maximum_fusion), channel_id=1, source_target_pairs={{0,16},{16,0},{1,17},{17,1},{2,18},{18,2},{3,19},{19,3},{4,20},{20... | collective-permute-start | bytes 3145736 | tf_op jit(solution)/shard_map/ppermute | solution.py:71
  61.1 19.8 %collective-permute-start.15 = (bf16[2,2,32,1024]{3,2,1,0:T(8,128)(2,1)S(1)}, bf16[2,2,32,1024]{3,2,1,0:T(8,128)(2,1)S(1)}, u32[]{:S(2)}, u32[]{:S(2)}) collective-permute-start(bf16[2,2,32,1024]{3,2,1,0:T(8,128)(2,1)S(1)} %broadcast_select_fusion.3), channel_id=1, source_target_pairs={{0,8},{4,12},{11,3},{15,7},{16,24},{20,28},{27,19},{31,23}} | collective-permute-start | bytes 786440 | tf_op jit(solution)/shard_map/ppermute | solution.py:138
  65.9 11.0 %collective-permute-start.16 = (bf16[2,2,32,1024]{3,2,1,0:T(8,128)(2,1)S(1)}, bf16[2,2,32,1024]{3,2,1,0:T(8,128)(2,1)S(1)}, u32[]{:S(2)}, u32[]{:S(2)}) collective-permute-start(bf16[2,2,32,1024]{3,2,1,0:T(8,128)(2,1)S(1)} %collective-permute-done.14), channel_id=1, source_target_pairs={{1,0},{5,4},{9,8},{13,12},{17,16},{21,20},{25,24},{29,28}} | collective-permute-start | bytes 786440 | tf_op jit(solution)/shard_map/ppermute | solution.py:91
  67.2 9.7 %collective-permute-start.17 = (bf16[2,2,32,1024]{3,2,1,0:T(8,128)(2,1)S(1)}, bf16[2,2,32,1024]{3,2,1,0:T(8,128)(2,1)S(1)}, u32[]{:S(2)}, u32[]{:S(2)}) collective-permute-start(bf16[2,2,32,1024]{3,2,1,0:T(8,128)(2,1)S(1)} %collective-permute-done.9), channel_id=1, source_target_pairs={{2,3},{6,7},{10,11},{14,15},{18,19},{22,23},{26,27},{30,31}} | collective-permute-start | bytes 786440 | tf_op jit(solution)/shard_map/ppermute | solution.py:88
  77.0 14.7 %collective-permute-start.22 = (bf16[2,2,32,1024]{3,2,1,0:T(8,128)(2,1)S(1)}, bf16[2,2,32,1024]{3,2,1,0:T(8,128)(2,1)S(1)}, u32[]{:S(2)}, u32[]{:S(2)}) collective-permute-start(bf16[2,2,32,1024]{3,2,1,0:T(8,128)(2,1)S(1)} %broadcast_select_fusion.2), channel_id=1, source_target_pairs={{0,8},{4,12},{11,3},{15,7},{16,24},{20,28},{27,19},{31,23}} | collective-permute-start | bytes 786440 | tf_op jit(solution)/shard_map/ppermute | solution.py:138
  92.0 5.5 %collective-permute-start.23 = (bf16[2,2,2,32,1024]{4,3,2,1,0:T(8,128)(2,1)S(1)}, bf16[2,2,2,32,1024]{4,3,2,1,0:T(8,128)(2,1)}, u32[]{:S(2)}, u32[]{:S(2)}) collective-permute-start(bf16[2,2,2,32,1024]{4,3,2,1,0:T(8,128)(2,1)S(1)} %pad_maximum_fusion.6), channel_id=1, source_target_pairs={{0,16},{16,0},{1,17},{17,1},{2,18},{18,2},{3,19},{19,3},{4,20},{20... | collective-permute-start | bytes 1572872 | tf_op jit(solution)/shard_map/ppermute | solution.py:71
  92.6 15.0 %collective-permute-start.21 = (f16[2,2,2,32,1024]{4,3,1,0,2:T(8,128)(2,1)}, f16[2,2,2,32,1024]{4,3,1,0,2:T(8,128)(2,1)S(1)}, u32[]{:S(2)}, u32[]{:S(2)}) collective-permute-start(f16[2,2,2,32,1024]{4,3,1,0,2:T(8,128)(2,1)} %fusion.20), channel_id=1, source_target_pairs={{0,4},{4,0},{8,12},{12,8},{1,5},{5,1},{9,13},{13,9},{2,6},{6,2},{1... | collective-permute-start | bytes 1572872 | tf_op jit(solution)/shard_map/ppermute | solution.py:184
  93.2 15.0 %collective-permute-start.27 = (f16[2,2,2,32,1024]{4,3,2,1,0:T(8,128)(2,1)}, f16[2,2,2,32,1024]{4,3,2,1,0:T(8,128)(2,1)S(1)}, u32[]{:S(2)}, u32[]{:S(2)}) collective-permute-start(f16[2,2,2,32,1024]{4,3,2,1,0:T(8,128)(2,1)} %fusion.23), channel_id=1, source_target_pairs={{0,8},{8,0},{4,12},{12,4},{1,9},{9,1},{5,13},{13,5},{2,10},{10,2},... | collective-permute-start | bytes 1572872 | tf_op jit(solution)/shard_map/ppermute | solution.py:185
  101.5 17.3 %collective-permute-start.25 = (f16[2,2,2,32,1024]{4,3,1,0,2:T(8,128)(2,1)S(1)}, f16[2,2,2,32,1024]{4,3,1,0,2:T(8,128)(2,1)S(1)}, u32[]{:S(2)}, u32[]{:S(2)}) collective-permute-start(f16[2,2,2,32,1024]{4,3,1,0,2:T(8,128)(2,1)S(1)} %fusion.21), channel_id=1, source_target_pairs={{0,4},{4,0},{8,12},{12,8},{1,5},{5,1},{9,13},{13,9},{2,6},{6,2},{1... | collective-permute-start | bytes 1572872 | tf_op jit(solution)/shard_map/ppermute | solution.py:184
  103.0 16.5 %collective-permute-start.26 = (f16[2,2,2,32,1024]{4,3,2,1,0:T(8,128)(2,1)S(1)}, f16[2,2,2,32,1024]{4,3,2,1,0:T(8,128)(2,1)S(1)}, u32[]{:S(2)}, u32[]{:S(2)}) collective-permute-start(f16[2,2,2,32,1024]{4,3,2,1,0:T(8,128)(2,1)S(1)} %fusion.22), channel_id=1, source_target_pairs={{0,8},{8,0},{4,12},{12,4},{1,9},{9,1},{5,13},{13,5},{2,10},{10,2},... | collective-permute-start | bytes 1572872 | tf_op jit(solution)/shard_map/ppermute | solution.py:185
  107.8 17.3 %collective-permute-start.24 = (f16[2,2,32,1024]{3,2,1,0:T(8,128)(2,1)S(1)}, f16[2,2,32,1024]{3,2,1,0:T(8,128)(2,1)S(1)}, u32[]{:S(2)}, u32[]{:S(2)}) collective-permute-start(f16[2,2,32,1024]{3,2,1,0:T(8,128)(2,1)S(1)} %fusion.28), channel_id=1, source_target_pairs={{0,8},{8,0},{4,12},{12,4},{1,9},{9,1},{5,13},{13,5},{2,10},{10,2},... | collective-permute-start | bytes 786440 | tf_op jit(solution)/shard_map/ppermute | solution.py:196
  108.5 16.7 %collective-permute-start.28 = (f16[2,2,32,1024]{3,2,1,0:T(8,128)(2,1)S(1)}, f16[2,2,32,1024]{3,2,1,0:T(8,128)(2,1)S(1)}, u32[]{:S(2)}, u32[]{:S(2)}) collective-permute-start(f16[2,2,32,1024]{3,2,1,0:T(8,128)(2,1)S(1)} %fusion.31), channel_id=1, source_target_pairs={{0,4},{4,0},{8,12},{12,8},{1,5},{5,1},{9,13},{13,9},{2,6},{6,2},{1... | collective-permute-start | bytes 786440 | tf_op jit(solution)/shard_map/ppermute | solution.py:197
  119.8 9.8 %collective-permute-start.29 = (f16[2,2,32,1024]{3,2,1,0:T(8,128)(2,1)S(1)}, f16[2,2,32,1024]{3,2,1,0:T(8,128)(2,1)S(1)}, u32[]{:S(2)}, u32[]{:S(2)}) collective-permute-start(f16[2,2,32,1024]{3,2,1,0:T(8,128)(2,1)S(1)} %fusion.29), channel_id=1, source_target_pairs={{0,8},{8,0},{4,12},{12,4},{1,9},{9,1},{5,13},{13,5},{2,10},{10,2},... | collective-permute-start | bytes 786440 | tf_op jit(solution)/shard_map/ppermute | solution.py:196
  120.3 9.4 %collective-permute-start.30 = (f16[2,2,32,1024]{3,2,1,0:T(8,128)(2,1)S(1)}, f16[2,2,32,1024]{3,2,1,0:T(8,128)(2,1)S(1)}, u32[]{:S(2)}, u32[]{:S(2)}) collective-permute-start(f16[2,2,32,1024]{3,2,1,0:T(8,128)(2,1)S(1)} %fusion.30), channel_id=1, source_target_pairs={{0,4},{4,0},{8,12},{12,8},{1,5},{5,1},{9,13},{13,9},{2,6},{6,2},{1... | collective-permute-start | bytes 786440 | tf_op jit(solution)/shard_map/ppermute | solution.py:197
  125.4 4.6 %collective-permute-start.31 = (f16[2,32,2048]{2,1,0:T(8,128)(2,1)S(1)}, f16[2,32,2048]{2,1,0:T(8,128)(2,1)S(1)}, u32[]{:S(2)}, u32[]{:S(2)}) collective-permute-start(f16[2,32,2048]{2,1,0:T(8,128)(2,1)S(1)} %get-tuple-element.72), channel_id=1, source_target_pairs={{0,16},{16,0},{1,17},{17,1},{2,18},{18,2},{3,19},{19,3},{4,20},{20... | collective-permute-start | bytes 786440 | tf_op jit(solution)/shard_map/ppermute | solution.py:71
  133.1 5.2 %collective-permute-start.35 = (f32[4,64]{1,0:T(4,128)S(1)}, f32[4,64]{1,0:T(4,128)S(1)}, u32[]{:S(2)}, u32[]{:S(2)}) collective-permute-start(f32[4,64]{1,0:T(4,128)S(1)} %get-tuple-element.79), channel_id=1, source_target_pairs={{0,3},{1,0},{2,1},{3,2},{4,7},{5,4},{6,5},{7,6},{8,11},{9,8},{10,9... | collective-permute-start | bytes 3080 | tf_op jit(solution)/shard_map/ppermute | solution.py:230
  137.0 4.5 %collective-permute-start.34 = (f32[4,64]{1,0:T(4,128)S(1)}, f32[4,64]{1,0:T(4,128)S(1)}, u32[]{:S(2)}, u32[]{:S(2)}) collective-permute-start(f32[4,64]{1,0:T(4,128)S(1)} %get-tuple-element.79), channel_id=1, source_target_pairs={{0,2},{1,3},{2,0},{3,1},{4,6},{5,7},{6,4},{7,5},{8,10},{9,11},{10,... | collective-permute-start | bytes 3080 | tf_op jit(solution)/shard_map/ppermute | solution.py:230
  137.0 5.4 %collective-permute-start.33 = (f32[4,64]{1,0:T(4,128)S(1)}, f32[4,64]{1,0:T(4,128)S(1)}, u32[]{:S(2)}, u32[]{:S(2)}) collective-permute-start(f32[4,64]{1,0:T(4,128)S(1)} %get-tuple-element.79), channel_id=1, source_target_pairs={{0,1},{1,2},{2,3},{3,0},{4,5},{5,6},{6,7},{7,4},{8,9},{9,10},{10,1... | collective-permute-start | bytes 3080 | tf_op jit(solution)/shard_map/ppermute | solution.py:230
  (17 other events, 118.1 us)

commit v14 on v12

--- a/solution.py
+++ b/solution.py
@@ -35,22 +35,27 @@
     model = depth * vocab
 
     wide = rows.astype(jnp.float32)
-    gained = (wide * norm_gain.astype(jnp.float32)[None, :]).astype(jnp.bfloat16)
-    gained = gained.reshape(2, seg, depth)
+    gain = norm_gain.astype(jnp.float32)
+
+    def gained(value, factor):
+        return (value.astype(jnp.float32) * factor).astype(jnp.bfloat16)
 
     take = lax.ppermute(head_weight, "pair", CORE_SWAP)
 
     def paired(value, reach):
         return lax.ppermute(value, "vocab", [(i, i ^ reach) for i in range(vocab)])
 
-    squares = jnp.sum(wide * wide, axis=1)
+    near_squares = jnp.sum(wide * wide, axis=1)
     reach = 1
-    while reach < vocab:
-        squares += paired(squares, reach)
+    while 2 * reach < vocab:
+        near_squares += paired(near_squares, reach)
         reach *= 2
-    squares = squares.reshape(2, seg)
-
-    def row_scale(*earlier):
+
+    def far_squares(*earlier):
+        return paired(after(near_squares, *earlier), reach)
+
+    def row_scale(squares, *earlier):
+        squares = squares.reshape(2, seg)
         sent = [
             lax.ppermute(
                 pick(after(squares, *earlier), core ^ k, 0),
@@ -74,13 +79,24 @@
     def dot(left, weight):
         return jnp.dot(left.reshape(-1, block), weight, preferred_element_type=jnp.float32)
 
+    def pieces(left, weight):
+        low, high = weight[:, : width // 2], weight[:, width // 2 :]
+        return [
+            dot(pick(left, 1 - x, 2), low),
+            dot(pick(left, 1 - y, 1), high),
+            dot(pick(left, x, 2), low),
+            dot(pick(left, y, 1), high),
+        ]
+
     def line_parts():
-        mine = lax.dynamic_slice_in_dim(gained, x * block, block, 2)
+        raw = rows.reshape(2, seg, depth)
+        mine = lax.dynamic_slice_in_dim(raw, x * block, block, 2)
         other = lax.ppermute(
-            lax.dynamic_slice_in_dim(gained, (1 - x) * block, block, 2), "batch", X_SWAP
+            lax.dynamic_slice_in_dim(raw, (1 - x) * block, block, 2), "batch", X_SWAP
         )
         own = jnp.stack([jnp.where(x == 0, mine, other), jnp.where(x == 0, other, mine)])
-        own = after(own, squares)
+        own = gained(own, lax.dynamic_slice_in_dim(gain, x * block, block, 0))
+        own = after(own, near_squares)
 
         def up(value, k):
             return lax.ppermute(value, "vocab", [(z, z + 1) for z in range(k - 1, vocab - 1)])
@@ -98,18 +114,20 @@
             return part
 
         first = level // 2
-        scale = row_scale(own)
-        below[1], above[1] = after(below[1], scale), after(above[1], scale)
-        near_sent = quarter(1 - y + 2 * first, 1)
-        got_near = lax.ppermute(near_sent, "batch", Y_SWAP)
+        more_squares = far_squares(own)
+        keep_near = (core ^ first) == 0
+        kept, taken = half_columns(head_weight, own), half_columns(take, own)
+        near_weight, far_weight = lax.optimization_barrier(
+            (jnp.where(keep_near, kept, taken), jnp.where(keep_near, taken, kept))
+        )
+        squares = near_squares + after(more_squares, near_weight, far_weight)
+        ready = (near_weight, far_weight)
+        below[1], above[1] = after(below[1], *ready), after(above[1], *ready)
+        scale = row_scale(squares, below[1], above[1])
+        got_near = lax.ppermute(quarter(1 - y + 2 * first, 1), "batch", Y_SWAP)
         below.append(up(below[1], 2))
         above.append(down(above[1], 2))
-        keep_near = (core ^ first) == 0
-        kept, taken = half_columns(head_weight, near_sent), half_columns(take, near_sent)
-        near_weight, far_weight = lax.optimization_barrier(
-            (jnp.where(keep_near, kept, taken), jnp.where(keep_near, taken, kept))
-        )
-        ready = (got_near, near_weight, far_weight)
+        ready = (got_near, scale)
         below[2], above[2] = after(below[2], *ready), after(above[2], *ready)
         near = by_y(quarter(y + 2 * first, 1), after(got_near, below[2], above[2]), 0)
         swapped_near = swapped(near)
@@ -123,46 +141,50 @@
         mine_early = quarter(y + 2 * (1 - first), 2)
         is_late = (level == 0) & (y == 1) | (level == vocab - 1) & (y == 0)
         below_3, above_3 = up(below[2], 3), down(above[2], 3)
-        near_part = dot(near, near_weight)
-        last = after(jnp.where(level == 0, above_3, below_3), got_early, near_part)
+        near_pieces = pieces(near, near_weight)
+        mine_early, last = after(mine_early, got_early), jnp.where(level == 0, above_3, below_3)
+        last = after(last, got_early, mine_early, *near_pieces)
         got_late = lax.ppermute(last, ("batch", "vocab"), late)
         far = by_y(
             jnp.where(is_late, last, mine_early), jnp.where(is_late, got_late, got_early), 0
         )
         swapped_far = swapped(far)
 
-        def own_part():
-            return near_part + dot(far, far_weight)
-
-        def other_part(*earlier):
+        def own_pieces():
+            return [a + b for a, b in zip(near_pieces, pieces(far, far_weight))]
+
+        def other_pieces(*earlier):
             left = after(swapped_far, *earlier)
-            return dot(swapped_near, near_weight) + dot(left, far_weight)
-
-        return (own_part, other_part), scale
+            return [
+                a + b
+                for a, b in zip(pieces(swapped_near, near_weight), pieces(left, far_weight))
+            ]
+
+        return (own_pieces, other_pieces), scale
 
     def gathered_parts():
         near_weight, far_weight = half_columns(head_weight), half_columns(take)
-        whole = lax.all_gather(gained, "vocab", axis=2, tiled=True)
+        whole = lax.all_gather(gained(rows, gain).reshape(2, seg, depth), "vocab", axis=2, tiled=True)
         whole = whole.reshape(2, seg, 2, 4, block).transpose(3, 2, 0, 1, 4)
         whole = lax.all_to_all(whole, "batch", split_axis=0, concat_axis=0)
         whole = whole.reshape(2, 2, 2, 2, seg, block).transpose(2, 0, 1, 3, 4, 5)
         swapped_whole = swapped(whole)
 
-        def part(left):
-            return dot(pick(left, core, 0), near_weight) + dot(pick(left, 1 - core, 0), far_weight)
-
-        return (lambda: part(whole), lambda *earlier: part(after(swapped_whole, *earlier))), row_scale()
+        def found(left):
+            near, far = pick(left, core, 0), pick(left, 1 - core, 0)
+            return [a + b for a, b in zip(pieces(near, near_weight), pieces(far, far_weight))]
+
+        branches = (lambda: found(whole), lambda *earlier: found(after(swapped_whole, *earlier)))
+        return branches, row_scale(near_squares + far_squares())
 
     lined = depth == 2 * block and vocab == 4
-    parts, scale = line_parts() if lined else gathered_parts()
+    branches, scale = line_parts() if lined else gathered_parts()
     kept, sends = [], []
-    for part in parts:
-        whole = (part(*(sends[-1] if sends else ())) * SHRINK).reshape(2, 2, 2, seg, width)
-        low, high = whole[..., : width // 2], whole[..., width // 2 :]
-        kept.append((pick(low, x, 2), pick(high, y, 1)))
-        sends.append(
-            (pick(low, 1 - x, 2).astype(SUM_TYPE), pick(high, 1 - y, 1).astype(SUM_TYPE))
-        )
+    for branch in branches:
+        found = branch(*(sends[-1] if sends else ()))
+        found = [(piece * SHRINK).reshape(2, 2, seg, width // 2) for piece in found]
+        sends.append((found[0].astype(SUM_TYPE), found[1].astype(SUM_TYPE)))
+        kept.append((found[2], found[3]))
     halfway, more_sends = [], []
     for i in range(2):
         away_x = lax.ppermute(sends[i][0], "batch", X_SWAP)

time: 127 us -> 147 us (1.16)
  waiting for transfers between devices: 51.1 us -> 59.8 us
  starting transfers between devices: 40.7 us -> 44.8 us
  matrix products: 11.5 us -> 15.5 us
  local copies, waits for them, and re-layouts: 1.77 us -> 4.22 us
    ppermute x2, waiting for transfers between devices: 11.7 us -> 0.01 us  [on_device(): away_y = lax.ppermute(sends[i][1], 'batch', Y_SWAP)]
    ppermute x2, waiting for transfers between devices: 1.32 us -> 12.6 us  [on_device(): away_x = lax.ppermute(sends[i][0], 'batch', X_SWAP)]
    ppermute x1, waiting for transfers between devices: 1.02 us -> 8.98 us  [line_parts(): got_early = lax.ppermute(quarter(far, 2), ('batch', 'vocab'), early)]
    ppermute x3, waiting for transfers between devices: 11.1 us -> 3.93 us  [down(): return lax.ppermute(value, 'vocab', [(z + 1, z) for z in range(vocab - k)])]
    ppermute x2, waiting for transfers between devices: 8.54 us -> 4.49 us  [on_device(): next_x = lax.ppermute(more_sends[i][1], 'batch', X_SWAP)]
    ppermute x2, waiting for transfers between devices: 3.81 us -> 7.8 us  [paired(): return lax.ppermute(value, 'vocab', [(i, i ^ reach) for i in range(vocab)])]
    dot_general x4 -> x16, matrix products: 11.5 us -> 15.5 us  [dot(): jnp.dot(left.reshape(-1, block), weight, preferred_element_type=jnp.float32)]
    ppermute x1, waiting for transfers between devices: 5.97 us -> 9.9 us  [line_parts(): got_late = lax.ppermute(last, ('batch', 'vocab'), late)]
  transfers between devices with their start and end apart: 30 -> 30, of which waited for: 18 -> 17; matrix products, arithmetic and copies ran while one was open for 24% -> 23% of each run, Pallas kernels for 0% -> 0%
where the time goes in v14:
time: 147 us
  waiting for transfers between devices  59.8 us (41%)
  starting transfers between devices  44.8 us (30%)
  other arithmetic  21.1 us (14%)
  matrix products  15.5 us (11%)
  local copies, waits for them, and re-layouts  4.22 us (3%)
    dot_general x16, matrix products, dot(): jnp.dot(left.reshape(-1, block), weight, preferred_element_type=jnp.float32)  15.5 us
    ppermute x2, waiting for transfers between devices, on_device(): away_x = lax.ppermute(sends[i][0], 'batch', X_SWAP)  12.6 us
    ppermute x1, waiting for transfers between devices, line_parts(): got_late = lax.ppermute(last, ('batch', 'vocab'), late)  9.9 us
    select_n x1, other arithmetic, line_parts(): jnp.where(keep_near, taken, kept)  9.84 us
    ppermute x1, waiting for transfers between devices, line_parts(): got_early = lax.ppermute(quarter(far, 2), ('batch', 'vocab'), early)  8.98 us
    ppermute x2, waiting for transfers between devices, paired(): return lax.ppermute(value, 'vocab', [(i, i ^ reach) for i in range(vocab)])  7.8 us
    ppermute x3, starting transfers between devices, up(): lax.ppermute(value, 'vocab', [(z, z + 1) for z in range(k - 1, vocab - 1)])  5.9 us
    ppermute x2, starting transfers between devices, paired(): return lax.ppermute(value, 'vocab', [(i, i ^ reach) for i in range(vocab)])  5.88 us
  transfers between devices with their start and end apart: 30, of which 17 were waited for; matrix products, arithmetic and copies ran while one was open for 23% of the time, Pallas kernels for 0%

profile of v14, /device:TPU:0, one launch (start us, length us, event | category | flops | bytes accessed | tf_op | source)
XLA Modules:
  0.0 146.7 jit_solution(10513972741465894546)
XLA Ops:
  2.1 2.6 %collective-permute-start = (bf16[2,64,1024]{2,1,0:T(8,128)(2,1)S(1)}, bf16[2,64,1024]{2,1,0:T(8,128)(2,1)S(1)}, u32[]{:S(2)}, u32[]{:S(2)}) collective-permute-start(bf16[2,64,1024]{2,1,0:T(8,128)(2,1)S(1)} %constant_dynamic-slice_fusion.10), channel_id=1, source_target_pairs={{0,4},{4,0},{8,12},{12,8},{1,5},{5,1},{9,13},{13,9},{2,6},{6,2},{1... | collective-permute-start | bytes 786440 | tf_op jit(solution)/shard_map/ppermute | solution.py:94
  5.9 1.6 %collective-permute-start.1 = (f32[128]{0:T(128)S(1)}, f32[128]{0:T(128)S(1)}, u32[]{:S(2)}, u32[]{:S(2)}) collective-permute-start(f32[128]{0:T(128)S(1)} %multiply_reduce_fusion), channel_id=1, source_target_pairs={{0,1},{1,0},{2,3},{3,2},{4,5},{5,4},{6,7},{7,6},{8,9},{9,8},{10,11... | collective-permute-start | bytes 1544 | tf_op jit(solution)/shard_map/ppermute | solution.py:46
  9.5 2.1 %collective-permute-done = bf16[2,64,1024]{2,1,0:T(8,128)(2,1)S(1)} collective-permute-done((bf16[2,64,1024]{2,1,0:T(8,128)(2,1)S(1)}, bf16[2,64,1024]{2,1,0:T(8,128)(2,1)S(1)}, u32[]{:S(2)}, u32[]{:S(2)}) %collective-permute-start) | collective-permute-done | bytes 262176 | tf_op jit(solution)/shard_map/ppermute | solution.py:94
  12.8 3.8 %collective-permute-start.4 = (bf16[2,2,64,1024]{3,2,1,0:T(8,128)(2,1)S(1)}, bf16[2,2,64,1024]{3,2,1,0:T(8,128)(2,1)S(1)}, u32[]{:S(2)}, u32[]{:S(2)}) collective-permute-start(bf16[2,2,64,1024]{3,2,1,0:T(8,128)(2,1)S(1)} %multiply_convert_fusion), channel_id=1, source_target_pairs={{0,1},{1,2},{2,3},{4,5},{5,6},{6,7},{8,9},{9,10},{10,11},{12,13},{... | collective-permute-start | bytes 1572872 | tf_op jit(solution)/shard_map/ppermute | solution.py:102
  18.0 9.8 %broadcast_select_fusion = (bf16[1024,2048]{1,0:T(8,128)(2,1)}, bf16[1024,2048]{1,0:T(8,128)(2,1)}) fusion(pred[]{:T(512)S(6)} %eq.74, bf16[1024,4096]{1,0:T(8,128)(2,1)} %collective-permute-done.3, s32[]{:T(128)S(6)} %select_n.250, bf16[1024,4096]{1,0:T(8,128)(2,1)} %param.5), kind=kLoop, calls=%fused_computation | loop fusion | flops 4194304 | bytes 16777220 | tf_op jit(solution)/shard_map/jit(_where)/select_n | solution.py:121
  27.8 3.9 %collective-permute-done.2 = bf16[2,2,64,1024]{3,2,1,0:T(8,128)(2,1)S(1)} collective-permute-done((bf16[2,2,64,1024]{3,2,1,0:T(8,128)(2,1)S(1)}, bf16[2,2,64,1024]{3,2,1,0:T(8,128)(2,1)S(1)}, u32[]{:S(2)}, u32[]{:S(2)}) %collective-permute-start.2) | collective-permute-done | bytes 524320 | tf_op jit(solution)/shard_map/ppermute | solution.py:105
  33.1 1.6 %collective-permute-start.5 = (bf16[2,2,64,1024]{3,2,1,0:T(8,128)(2,1)S(1)}, bf16[2,2,64,1024]{3,2,1,0:T(8,128)(2,1)S(1)}, u32[]{:S(2)}, u32[]{:S(2)}) collective-permute-start(bf16[2,2,64,1024]{3,2,1,0:T(8,128)(2,1)S(1)} %select_select_fusion.2), channel_id=1, source_target_pairs={{0,8},{8,0},{4,12},{12,4},{1,9},{9,1},{5,13},{13,5},{2,10},{10,2},... | collective-permute-start | bytes 1572872 | tf_op jit(solution)/shard_map/ppermute | solution.py:127
  34.7 1.4 collective-permute-start.6
  36.1 4.2 %collective-permute-start.7 = (f32[128]{0:T(128)S(1)}, f32[128]{0:T(128)S(1)}, u32[]{:S(2)}, u32[]{:S(2)}) collective-permute-start(f32[128]{0:T(128)S(1)} %add.151), channel_id=1, source_target_pairs={{0,2},{1,3},{2,0},{3,1},{4,6},{5,7},{6,4},{7,5},{8,10},{9,11},{10,... | collective-permute-start | bytes 1544 | tf_op jit(solution)/shard_map/ppermute | solution.py:46
  40.4 6.5 %collective-permute-done.7 = f32[128]{0:T(128)S(1)} collective-permute-done((f32[128]{0:T(128)S(1)}, f32[128]{0:T(128)S(1)}, u32[]{:S(2)}, u32[]{:S(2)}) %collective-permute-start.7) | collective-permute-done | bytes 544 | tf_op jit(solution)/shard_map/ppermute | solution.py:46
  47.7 4.3 %collective-permute-start.9 = (f32[64]{0:T(128)S(1)}, f32[64]{0:T(128)S(1)}, u32[]{:S(2)}, u32[]{:S(2)}) collective-permute-start(f32[64]{0:T(128)S(1)} %get-tuple-element.84), channel_id=1, source_target_pairs={{0,4},{4,12},{8,20},{12,28},{16,0},{20,8},{24,16},{28,24},{1,5},{5... | collective-permute-start | bytes 776 | tf_op jit(solution)/shard_map/ppermute | solution.py:60
  57.8 1.3 copy-done
  59.1 1.7 %fusion.30 = f32[256,1024]{1,0:T(8,128)} fusion(bf16[256,1024]{1,0:T(8,128)(2,1)S(1)} %bitcast.141, bf16[1024,2048]{1,0:T(8,128)(2,1)S(1)} %copy-done), kind=kOutput, calls=%fused_computation.58 | convolution fusion | flops 536870912 | bytes 3670016 | tf_op jit(solution)/shard_map/dot_general | solution.py:80
  62.1 1.7 %fusion.28 = f32[256,1024]{1,0:T(8,128)} fusion(bf16[256,1024]{1,0:T(8,128)(2,1)S(1)} %bitcast.137, bf16[1024,2048]{1,0:T(8,128)(2,1)S(1)} %copy-done), kind=kOutput, calls=%fused_computation.56 | convolution fusion | flops 536870912 | bytes 3670016 | tf_op jit(solution)/shard_map/dot_general | solution.py:80
  63.9 1.7 %fusion.24 = f32[256,1024]{1,0:T(8,128)} fusion(bf16[256,1024]{1,0:T(8,128)(2,1)S(1)} %bitcast.139, bf16[1024,2048]{1,0:T(8,128)(2,1)S(1)} %copy-done), kind=kOutput, calls=%fused_computation.52 | convolution fusion | flops 536870912 | bytes 3670016 | tf_op jit(solution)/shard_map/dot_general | solution.py:80
  65.6 1.7 %fusion.22 = f32[256,1024]{1,0:T(8,128)} fusion(bf16[256,1024]{1,0:T(8,128)(2,1)S(1)} %bitcast.138, bf16[1024,2048]{1,0:T(8,128)(2,1)S(1)} %copy-done), kind=kOutput, calls=%fused_computation.50 | convolution fusion | flops 536870912 | bytes 3670016 | tf_op jit(solution)/shard_map/dot_general | solution.py:80
  67.2 9.0 %collective-permute-done.13 = bf16[2,2,64,1024]{3,2,1,0:T(8,128)(2,1)S(1)} collective-permute-done((bf16[2,2,64,1024]{3,2,1,0:T(8,128)(2,1)S(1)}, bf16[2,2,64,1024]{3,2,1,0:T(8,128)(2,1)S(1)}, u32[]{:S(2)}, u32[]{:S(2)}) %collective-permute-start.13) | collective-permute-done | bytes 524320 | tf_op jit(solution)/shard_map/ppermute | solution.py:140
  76.3 1.7 %collective-permute-start.14 = (bf16[2,2,64,1024]{3,2,1,0:T(8,128)(2,1)S(1)}, bf16[2,2,64,1024]{3,2,1,0:T(8,128)(2,1)S(1)}, u32[]{:S(2)}, u32[]{:S(2)}) collective-permute-start(bf16[2,2,64,1024]{3,2,1,0:T(8,128)(2,1)S(1)} %broadcast_select_fusion.2), channel_id=1, source_target_pairs={{0,8},{4,12},{11,3},{15,7},{16,24},{20,28},{27,19},{31,23}} | collective-permute-start | bytes 1572872 | tf_op jit(solution)/shard_map/ppermute | solution.py:147
  78.1 9.9 %collective-permute-done.14 = bf16[2,2,64,1024]{3,2,1,0:T(8,128)(2,1)S(1)} collective-permute-done((bf16[2,2,64,1024]{3,2,1,0:T(8,128)(2,1)S(1)}, bf16[2,2,64,1024]{3,2,1,0:T(8,128)(2,1)S(1)}, u32[]{:S(2)}, u32[]{:S(2)}) %collective-permute-start.14) | collective-permute-done | bytes 524320 | tf_op jit(solution)/shard_map/ppermute | solution.py:147
  89.3 3.9 %collective-permute-start.15 = (f16[2,2,64,1024]{3,2,1,0:T(8,128)(2,1)S(1)}, f16[2,2,64,1024]{3,2,1,0:T(8,128)(2,1)S(1)}, u32[]{:S(2)}, u32[]{:S(2)}) collective-permute-start(f16[2,2,64,1024]{3,2,1,0:T(8,128)(2,1)S(1)} %bitcast.149), channel_id=1, source_target_pairs={{0,4},{4,0},{8,12},{12,8},{1,5},{5,1},{9,13},{13,9},{2,6},{6,2},{1... | collective-permute-start | bytes 1572872 | tf_op jit(solution)/shard_map/ppermute | solution.py:190
  94.1 2.5 %collective-permute-start.21 = (f16[2,2,64,1024]{3,2,0,1:T(8,128)(2,1)S(1)}, f16[2,2,64,1024]{3,2,0,1:T(8,128)(2,1)S(1)}, u32[]{:S(2)}, u32[]{:S(2)}) collective-permute-start(f16[2,2,64,1024]{3,2,0,1:T(8,128)(2,1)S(1)} %copy.7), channel_id=1, source_target_pairs={{0,8},{8,0},{4,12},{12,4},{1,9},{9,1},{5,13},{13,5},{2,10},{10,2},... | collective-permute-start | bytes 1572872 | tf_op jit(solution)/shard_map/ppermute | solution.py:191
  102.8 3.0 %collective-permute-done.15 = f16[2,2,64,1024]{3,2,1,0:T(8,128)(2,1)S(1)} collective-permute-done((f16[2,2,64,1024]{3,2,1,0:T(8,128)(2,1)S(1)}, f16[2,2,64,1024]{3,2,1,0:T(8,128)(2,1)S(1)}, u32[]{:S(2)}, u32[]{:S(2)}) %collective-permute-start.15) | collective-permute-done | bytes 524320 | tf_op jit(solution)/shard_map/ppermute | solution.py:190
  106.0 2.5 %collective-permute-start.18 = (f16[2,64,1024]{2,1,0:T(8,128)(2,1)S(1)}, f16[2,64,1024]{2,1,0:T(8,128)(2,1)S(1)}, u32[]{:S(2)}, u32[]{:S(2)}) collective-permute-start(f16[2,64,1024]{2,1,0:T(8,128)(2,1)S(1)} %fusion.58), channel_id=1, source_target_pairs={{0,8},{8,0},{4,12},{12,4},{1,9},{9,1},{5,13},{13,5},{2,10},{10,2},... | collective-permute-start | bytes 786440 | tf_op jit(solution)/shard_map/ppermute | solution.py:202
  108.6 1.7 %collective-permute-start.19 = (f16[2,2,64,1024]{3,2,0,1:T(8,128)(2,1)S(1)}, f16[2,2,64,1024]{3,2,0,1:T(8,128)(2,1)S(1)}, u32[]{:S(2)}, u32[]{:S(2)}) collective-permute-start(f16[2,2,64,1024]{3,2,0,1:T(8,128)(2,1)S(1)} %copy.5), channel_id=1, source_target_pairs={{0,4},{4,0},{8,12},{12,8},{1,5},{5,1},{9,13},{13,9},{2,6},{6,2},{1... | collective-permute-start | bytes 1572872 | tf_op jit(solution)/shard_map/ppermute | solution.py:190
  113.8 9.6 %collective-permute-done.19 = f16[2,2,64,1024]{3,2,0,1:T(8,128)(2,1)S(1)} collective-permute-done((f16[2,2,64,1024]{3,2,0,1:T(8,128)(2,1)S(1)}, f16[2,2,64,1024]{3,2,0,1:T(8,128)(2,1)S(1)}, u32[]{:S(2)}, u32[]{:S(2)}) %collective-permute-start.19) | collective-permute-done | bytes 524320 | tf_op jit(solution)/shard_map/ppermute | solution.py:190
  123.9 1.8 %collective-permute-start.25 = (f16[2,64,1024]{2,1,0:T(8,128)(2,1)S(1)}, f16[2,64,1024]{2,1,0:T(8,128)(2,1)S(1)}, u32[]{:S(2)}, u32[]{:S(2)}) collective-permute-start(f16[2,64,1024]{2,1,0:T(8,128)(2,1)S(1)} %fusion.60), channel_id=1, source_target_pairs={{0,4},{4,0},{8,12},{12,8},{1,5},{5,1},{9,13},{13,9},{2,6},{6,2},{1... | collective-permute-start | bytes 786440 | tf_op jit(solution)/shard_map/ppermute | solution.py:203
  126.3 2.7 %collective-permute-done.22 = f16[2,64,1024]{2,1,0:T(8,128)(2,1)S(1)} collective-permute-done((f16[2,64,1024]{2,1,0:T(8,128)(2,1)S(1)}, f16[2,64,1024]{2,1,0:T(8,128)(2,1)S(1)}, u32[]{:S(2)}, u32[]{:S(2)}) %collective-permute-start.22) | collective-permute-done | bytes 262176 | tf_op jit(solution)/shard_map/ppermute | solution.py:203
  129.3 2.2 %collective-permute-done.24 = f16[2,64,1024]{2,1,0:T(8,128)(2,1)S(1)} collective-permute-done((f16[2,64,1024]{2,1,0:T(8,128)(2,1)S(1)}, f16[2,64,1024]{2,1,0:T(8,128)(2,1)S(1)}, u32[]{:S(2)}, u32[]{:S(2)}) %collective-permute-start.24) | collective-permute-done | bytes 262176 | tf_op jit(solution)/shard_map/ppermute | solution.py:202
  131.5 1.7 %collective-permute-done.25 = f16[2,64,1024]{2,1,0:T(8,128)(2,1)S(1)} collective-permute-done((f16[2,64,1024]{2,1,0:T(8,128)(2,1)S(1)}, f16[2,64,1024]{2,1,0:T(8,128)(2,1)S(1)}, u32[]{:S(2)}, u32[]{:S(2)}) %collective-permute-start.25) | collective-permute-done | bytes 262176 | tf_op jit(solution)/shard_map/ppermute | solution.py:203
  133.7 1.4 collective-permute-done.26
  136.4 2.6 %collective-permute-start.29 = (f32[4,64]{1,0:T(4,128)S(1)}, f32[4,64]{1,0:T(4,128)S(1)}, u32[]{:S(2)}, u32[]{:S(2)}) collective-permute-start(f32[4,64]{1,0:T(4,128)S(1)} %get-tuple-element.76), channel_id=1, source_target_pairs={{0,3},{1,0},{2,1},{3,2},{4,7},{5,4},{6,5},{7,6},{8,11},{9,8},{10,9... | collective-permute-start | bytes 3080 | tf_op jit(solution)/shard_map/ppermute | solution.py:235
  140.3 3.2 %collective-permute-done.28 = f32[4,64]{1,0:T(4,128)S(1)} collective-permute-done((f32[4,64]{1,0:T(4,128)S(1)}, f32[4,64]{1,0:T(4,128)S(1)}, u32[]{:S(2)}, u32[]{:S(2)}) %collective-permute-start.28) | collective-permute-done | bytes 1056 | tf_op jit(solution)/shard_map/ppermute | solution.py:235
  (114 shorter events, 36.0 us)
Async XLA Ops:
  0.6 17.3 %collective-permute-start.3 = (bf16[1024,4096]{1,0:T(8,128)(2,1)}, bf16[1024,4096]{1,0:T(8,128)(2,1)}, u32[]{:S(2)}, u32[]{:S(2)}) collective-permute-start(bf16[1024,4096]{1,0:T(8,128)(2,1)} %param.5), channel_id=1, source_target_pairs={{0,16},{16,0},{1,17},{17,1},{2,18},{18,2},{3,19},{19,3},{4,20},{20... | collective-permute-start | bytes 25165832 | tf_op jit(solution)/shard_map/ppermute | solution.py:43
  2.1 9.5 %collective-permute-start = (bf16[2,64,1024]{2,1,0:T(8,128)(2,1)S(1)}, bf16[2,64,1024]{2,1,0:T(8,128)(2,1)S(1)}, u32[]{:S(2)}, u32[]{:S(2)}) collective-permute-start(bf16[2,64,1024]{2,1,0:T(8,128)(2,1)S(1)} %constant_dynamic-slice_fusion.10), channel_id=1, source_target_pairs={{0,4},{4,0},{8,12},{12,8},{1,5},{5,1},{9,13},{13,9},{2,6},{6,2},{1... | collective-permute-start | bytes 786440 | tf_op jit(solution)/shard_map/ppermute | solution.py:94
  5.9 3.6 %collective-permute-start.1 = (f32[128]{0:T(128)S(1)}, f32[128]{0:T(128)S(1)}, u32[]{:S(2)}, u32[]{:S(2)}) collective-permute-start(f32[128]{0:T(128)S(1)} %multiply_reduce_fusion), channel_id=1, source_target_pairs={{0,1},{1,0},{2,3},{3,2},{4,5},{5,4},{6,7},{7,6},{8,9},{9,8},{10,11... | collective-permute-start | bytes 1544 | tf_op jit(solution)/shard_map/ppermute | solution.py:46
  12.8 15.0 %collective-permute-start.4 = (bf16[2,2,64,1024]{3,2,1,0:T(8,128)(2,1)S(1)}, bf16[2,2,64,1024]{3,2,1,0:T(8,128)(2,1)S(1)}, u32[]{:S(2)}, u32[]{:S(2)}) collective-permute-start(bf16[2,2,64,1024]{3,2,1,0:T(8,128)(2,1)S(1)} %multiply_convert_fusion), channel_id=1, source_target_pairs={{0,1},{1,2},{2,3},{4,5},{5,6},{6,7},{8,9},{9,10},{10,11},{12,13},{... | collective-permute-start | bytes 1572872 | tf_op jit(solution)/shard_map/ppermute | solution.py:102
  16.6 15.1 %collective-permute-start.2 = (bf16[2,2,64,1024]{3,2,1,0:T(8,128)(2,1)S(1)}, bf16[2,2,64,1024]{3,2,1,0:T(8,128)(2,1)S(1)}, u32[]{:S(2)}, u32[]{:S(2)}) collective-permute-start(bf16[2,2,64,1024]{3,2,1,0:T(8,128)(2,1)S(1)} %multiply_convert_fusion), channel_id=1, source_target_pairs={{1,0},{2,1},{3,2},{5,4},{6,5},{7,6},{9,8},{10,9},{11,10},{13,12},{... | collective-permute-start | bytes 1572872 | tf_op jit(solution)/shard_map/ppermute | solution.py:105
  31.7 21.5 %collective-permute-start.10 = (bf16[2,2,64,1024]{3,2,1,0:T(8,128)(2,1)S(1)}, bf16[2,2,64,1024]{3,2,1,0:T(8,128)(2,1)S(1)}, u32[]{:S(2)}, u32[]{:S(2)}) collective-permute-start(bf16[2,2,64,1024]{3,2,1,0:T(8,128)(2,1)S(1)} %collective-permute-done.2), channel_id=1, source_target_pairs={{1,0},{2,1},{5,4},{6,5},{9,8},{10,9},{13,12},{14,13},{17,16},{18,1... | collective-permute-start | bytes 1572872 | tf_op jit(solution)/shard_map/ppermute | solution.py:105
  33.1 20.2 %collective-permute-start.5 = (bf16[2,2,64,1024]{3,2,1,0:T(8,128)(2,1)S(1)}, bf16[2,2,64,1024]{3,2,1,0:T(8,128)(2,1)S(1)}, u32[]{:S(2)}, u32[]{:S(2)}) collective-permute-start(bf16[2,2,64,1024]{3,2,1,0:T(8,128)(2,1)S(1)} %select_select_fusion.2), channel_id=1, source_target_pairs={{0,8},{8,0},{4,12},{12,4},{1,9},{9,1},{5,13},{13,5},{2,10},{10,2},... | collective-permute-start | bytes 1572872 | tf_op jit(solution)/shard_map/ppermute | solution.py:127
  34.7 18.6 %collective-permute-start.6 = (bf16[2,2,64,1024]{3,2,1,0:T(8,128)(2,1)S(1)}, bf16[2,2,64,1024]{3,2,1,0:T(8,128)(2,1)}, u32[]{:S(2)}, u32[]{:S(2)}) collective-permute-start(bf16[2,2,64,1024]{3,2,1,0:T(8,128)(2,1)S(1)} %collective-permute-done.4), channel_id=1, source_target_pairs={{1,2},{2,3},{5,6},{6,7},{9,10},{10,11},{13,14},{14,15},{17,18},{18... | collective-permute-start | bytes 1572872 | tf_op jit(solution)/shard_map/ppermute | solution.py:102
  36.1 10.8 %collective-permute-start.7 = (f32[128]{0:T(128)S(1)}, f32[128]{0:T(128)S(1)}, u32[]{:S(2)}, u32[]{:S(2)}) collective-permute-start(f32[128]{0:T(128)S(1)} %add.151), channel_id=1, source_target_pairs={{0,2},{1,3},{2,0},{3,1},{4,6},{5,7},{6,4},{7,5},{8,10},{9,11},{10,... | collective-permute-start | bytes 1544 | tf_op jit(solution)/shard_map/ppermute | solution.py:46
  47.0 4.9 %collective-permute-start.8 = (f32[64]{0:T(128)S(1)}, f32[64]{0:T(128)S(1)}, u32[]{:S(2)}, u32[]{:S(2)}) collective-permute-start(f32[64]{0:T(128)S(1)} %get-tuple-element.83), channel_id=1, source_target_pairs={{0,0},{4,8},{8,16},{12,24},{16,4},{20,12},{24,20},{28,28},{1,1},{5... | collective-permute-start | bytes 776 | tf_op jit(solution)/shard_map/ppermute | solution.py:60
  47.7 5.6 %collective-permute-start.9 = (f32[64]{0:T(128)S(1)}, f32[64]{0:T(128)S(1)}, u32[]{:S(2)}, u32[]{:S(2)}) collective-permute-start(f32[64]{0:T(128)S(1)} %get-tuple-element.84), channel_id=1, source_target_pairs={{0,4},{4,12},{8,20},{12,28},{16,0},{20,8},{24,16},{28,24},{1,5},{5... | collective-permute-start | bytes 776 | tf_op jit(solution)/shard_map/ppermute | solution.py:60
  53.3 22.9 %collective-permute-start.11 = (bf16[2,2,64,1024]{3,2,1,0:T(8,128)(2,1)S(1)}, bf16[2,2,64,1024]{3,2,1,0:T(8,128)(2,1)S(1)}, u32[]{:S(2)}, u32[]{:S(2)}) collective-permute-start(bf16[2,2,64,1024]{3,2,1,0:T(8,128)(2,1)S(1)} %collective-permute-done.10), channel_id=1, source_target_pairs={{1,0},{5,4},{9,8},{13,12},{17,16},{21,20},{25,24},{29,28}} | collective-permute-start | bytes 1572872 | tf_op jit(solution)/shard_map/ppermute | solution.py:105
  54.6 21.7 %collective-permute-start.12 = (bf16[2,2,64,1024]{3,2,1,0:T(8,128)(2,1)}, bf16[2,2,64,1024]{3,2,1,0:T(8,128)(2,1)S(1)}, u32[]{:S(2)}, u32[]{:S(2)}) collective-permute-start(bf16[2,2,64,1024]{3,2,1,0:T(8,128)(2,1)} %collective-permute-done.6), channel_id=1, source_target_pairs={{2,3},{6,7},{10,11},{14,15},{18,19},{22,23},{26,27},{30,31}} | collective-permute-start | bytes 1572872 | tf_op jit(solution)/shard_map/ppermute | solution.py:102
  60.8 15.4 %collective-permute-start.13 = (bf16[2,2,64,1024]{3,2,1,0:T(8,128)(2,1)S(1)}, bf16[2,2,64,1024]{3,2,1,0:T(8,128)(2,1)S(1)}, u32[]{:S(2)}, u32[]{:S(2)}) collective-permute-start(bf16[2,2,64,1024]{3,2,1,0:T(8,128)(2,1)S(1)} %get-tuple-element.47), channel_id=1, source_target_pairs={{1,9},{2,10},{3,11},{5,13},{6,14},{7,15},{8,0},{9,1},{10,2},{12,4}... | collective-permute-start | bytes 1572872 | tf_op jit(solution)/shard_map/ppermute | solution.py:140
  63.8 14.2 %collective-permute-start.16 = (bf16[2,2,2,64,1024]{4,3,2,1,0:T(8,128)(2,1)}, bf16[2,2,2,64,1024]{4,3,2,1,0:T(8,128)(2,1)S(1)}, u32[]{:S(2)}, u32[]{:S(2)}) collective-permute-start(bf16[2,2,2,64,1024]{4,3,2,1,0:T(8,128)(2,1)} %pad_maximum_fusion), channel_id=1, source_target_pairs={{0,16},{16,0},{1,17},{17,1},{2,18},{18,2},{3,19},{19,3},{4,20},{20... | collective-permute-start | bytes 3145736 | tf_op jit(solution)/shard_map/ppermute | solution.py:74
  76.3 11.7 %collective-permute-start.14 = (bf16[2,2,64,1024]{3,2,1,0:T(8,128)(2,1)S(1)}, bf16[2,2,64,1024]{3,2,1,0:T(8,128)(2,1)S(1)}, u32[]{:S(2)}, u32[]{:S(2)}) collective-permute-start(bf16[2,2,64,1024]{3,2,1,0:T(8,128)(2,1)S(1)} %broadcast_select_fusion.2), channel_id=1, source_target_pairs={{0,8},{4,12},{11,3},{15,7},{16,24},{20,28},{27,19},{31,23}} | collective-permute-start | bytes 1572872 | tf_op jit(solution)/shard_map/ppermute | solution.py:147
  78.1 10.3 %copy-start.2 = (bf16[1024,2048]{1,0:T(8,128)(2,1)S(1)}, bf16[1024,2048]{1,0:T(8,128)(2,1)}, u32[]{:S(2)}) copy-start(bf16[1024,2048]{1,0:T(8,128)(2,1)} %get-tuple-element.24) | copy-start | bytes 12582916
  78.1 10.3 %copy-start.6 = (f32[256,1024]{1,0:T(8,128)S(1)}, f32[256,1024]{1,0:T(8,128)}, u32[]{:S(2)}) copy-start(f32[256,1024]{1,0:T(8,128)} %fusion.28) | copy-start | bytes 3145732
  89.2 9.0 %collective-permute-start.17 = (bf16[2,2,2,64,1024]{4,3,2,1,0:T(8,128)(2,1)S(1)}, bf16[2,2,2,64,1024]{4,3,2,1,0:T(8,128)(2,1)S(1)}, u32[]{:S(2)}, u32[]{:S(2)}) collective-permute-start(bf16[2,2,2,64,1024]{4,3,2,1,0:T(8,128)(2,1)S(1)} %pad_maximum_fusion.1), channel_id=1, source_target_pairs={{0,16},{16,0},{1,17},{17,1},{2,18},{18,2},{3,19},{19,3},{4,20},{20... | collective-permute-start | bytes 3145736 | tf_op jit(solution)/shard_map/ppermute | solution.py:74
  89.3 16.5 %collective-permute-start.15 = (f16[2,2,64,1024]{3,2,1,0:T(8,128)(2,1)S(1)}, f16[2,2,64,1024]{3,2,1,0:T(8,128)(2,1)S(1)}, u32[]{:S(2)}, u32[]{:S(2)}) collective-permute-start(f16[2,2,64,1024]{3,2,1,0:T(8,128)(2,1)S(1)} %bitcast.149), channel_id=1, source_target_pairs={{0,4},{4,0},{8,12},{12,8},{1,5},{5,1},{9,13},{13,9},{2,6},{6,2},{1... | collective-permute-start | bytes 1572872 | tf_op jit(solution)/shard_map/ppermute | solution.py:190
  94.1 16.9 %collective-permute-start.21 = (f16[2,2,64,1024]{3,2,0,1:T(8,128)(2,1)S(1)}, f16[2,2,64,1024]{3,2,0,1:T(8,128)(2,1)S(1)}, u32[]{:S(2)}, u32[]{:S(2)}) collective-permute-start(f16[2,2,64,1024]{3,2,0,1:T(8,128)(2,1)S(1)} %copy.7), channel_id=1, source_target_pairs={{0,8},{8,0},{4,12},{12,4},{1,9},{9,1},{5,13},{13,5},{2,10},{10,2},... | collective-permute-start | bytes 1572872 | tf_op jit(solution)/shard_map/ppermute | solution.py:191
  102.7 20.8 %collective-permute-start.20 = (f16[2,2,64,1024]{3,2,1,0:T(8,128)(2,1)S(1)}, f16[2,2,64,1024]{3,2,1,0:T(8,128)(2,1)S(1)}, u32[]{:S(2)}, u32[]{:S(2)}) collective-permute-start(f16[2,2,64,1024]{3,2,1,0:T(8,128)(2,1)S(1)} %bitcast.150), channel_id=1, source_target_pairs={{0,8},{8,0},{4,12},{12,4},{1,9},{9,1},{5,13},{13,5},{2,10},{10,2},... | collective-permute-start | bytes 1572872 | tf_op jit(solution)/shard_map/ppermute | solution.py:191
  106.0 20.2 %collective-permute-start.18 = (f16[2,64,1024]{2,1,0:T(8,128)(2,1)S(1)}, f16[2,64,1024]{2,1,0:T(8,128)(2,1)S(1)}, u32[]{:S(2)}, u32[]{:S(2)}) collective-permute-start(f16[2,64,1024]{2,1,0:T(8,128)(2,1)S(1)} %fusion.58), channel_id=1, source_target_pairs={{0,8},{8,0},{4,12},{12,4},{1,9},{9,1},{5,13},{13,5},{2,10},{10,2},... | collective-permute-start | bytes 786440 | tf_op jit(solution)/shard_map/ppermute | solution.py:202
  108.6 14.8 %collective-permute-start.19 = (f16[2,2,64,1024]{3,2,0,1:T(8,128)(2,1)S(1)}, f16[2,2,64,1024]{3,2,0,1:T(8,128)(2,1)S(1)}, u32[]{:S(2)}, u32[]{:S(2)}) collective-permute-start(f16[2,2,64,1024]{3,2,0,1:T(8,128)(2,1)S(1)} %copy.5), channel_id=1, source_target_pairs={{0,4},{4,0},{8,12},{12,8},{1,5},{5,1},{9,13},{13,9},{2,6},{6,2},{1... | collective-permute-start | bytes 1572872 | tf_op jit(solution)/shard_map/ppermute | solution.py:190
  111.3 17.7 %collective-permute-start.22 = (f16[2,64,1024]{2,1,0:T(8,128)(2,1)S(1)}, f16[2,64,1024]{2,1,0:T(8,128)(2,1)S(1)}, u32[]{:S(2)}, u32[]{:S(2)}) collective-permute-start(f16[2,64,1024]{2,1,0:T(8,128)(2,1)S(1)} %fusion.61), channel_id=1, source_target_pairs={{0,4},{4,0},{8,12},{12,8},{1,5},{5,1},{9,13},{13,9},{2,6},{6,2},{1... | collective-permute-start | bytes 786440 | tf_op jit(solution)/shard_map/ppermute | solution.py:203
  123.8 7.6 %collective-permute-start.24 = (f16[2,64,1024]{2,1,0:T(8,128)(2,1)S(1)}, f16[2,64,1024]{2,1,0:T(8,128)(2,1)S(1)}, u32[]{:S(2)}, u32[]{:S(2)}) collective-permute-start(f16[2,64,1024]{2,1,0:T(8,128)(2,1)S(1)} %fusion.59), channel_id=1, source_target_pairs={{0,8},{8,0},{4,12},{12,4},{1,9},{9,1},{5,13},{13,5},{2,10},{10,2},... | collective-permute-start | bytes 786440 | tf_op jit(solution)/shard_map/ppermute | solution.py:202
  123.9 9.3 %collective-permute-start.25 = (f16[2,64,1024]{2,1,0:T(8,128)(2,1)S(1)}, f16[2,64,1024]{2,1,0:T(8,128)(2,1)S(1)}, u32[]{:S(2)}, u32[]{:S(2)}) collective-permute-start(f16[2,64,1024]{2,1,0:T(8,128)(2,1)S(1)} %fusion.60), channel_id=1, source_target_pairs={{0,4},{4,0},{8,12},{12,8},{1,5},{5,1},{9,13},{13,9},{2,6},{6,2},{1... | collective-permute-start | bytes 786440 | tf_op jit(solution)/shard_map/ppermute | solution.py:203
  129.2 4.3 %collective-permute-start.23 = (f16[64,2048]{1,0:T(8,128)(2,1)S(1)}, f16[64,2048]{1,0:T(8,128)(2,1)S(1)}, u32[]{:S(2)}, u32[]{:S(2)}) collective-permute-start(f16[64,2048]{1,0:T(8,128)(2,1)S(1)} %fusion.67), channel_id=1, source_target_pairs={{0,16},{16,0},{1,17},{17,1},{2,18},{18,2},{3,19},{19,3},{4,20},{20... | collective-permute-start | bytes 786440 | tf_op jit(solution)/shard_map/ppermute | solution.py:74
  133.4 1.6 %collective-permute-start.26 = (f16[64,2048]{1,0:T(8,128)(2,1)S(1)}, f16[64,2048]{1,0:T(8,128)(2,1)S(1)}, u32[]{:S(2)}, u32[]{:S(2)}) collective-permute-start(f16[64,2048]{1,0:T(8,128)(2,1)S(1)} %fusion.65), channel_id=1, source_target_pairs={{0,16},{16,0},{1,17},{17,1},{2,18},{18,2},{3,19},{19,3},{4,20},{20... | collective-permute-start | bytes 786440 | tf_op jit(solution)/shard_map/ppermute | solution.py:74
  136.4 3.9 %collective-permute-start.29 = (f32[4,64]{1,0:T(4,128)S(1)}, f32[4,64]{1,0:T(4,128)S(1)}, u32[]{:S(2)}, u32[]{:S(2)}) collective-permute-start(f32[4,64]{1,0:T(4,128)S(1)} %get-tuple-element.76), channel_id=1, source_target_pairs={{0,3},{1,0},{2,1},{3,2},{4,7},{5,4},{6,5},{7,6},{8,11},{9,8},{10,9... | collective-permute-start | bytes 3080 | tf_op jit(solution)/shard_map/ppermute | solution.py:235
  139.0 4.5 %collective-permute-start.28 = (f32[4,64]{1,0:T(4,128)S(1)}, f32[4,64]{1,0:T(4,128)S(1)}, u32[]{:S(2)}, u32[]{:S(2)}) collective-permute-start(f32[4,64]{1,0:T(4,128)S(1)} %get-tuple-element.76), channel_id=1, source_target_pairs={{0,2},{1,3},{2,0},{3,1},{4,6},{5,7},{6,4},{7,5},{8,10},{9,11},{10,... | collective-permute-start | bytes 3080 | tf_op jit(solution)/shard_map/ppermute | solution.py:235
  139.0 5.4 %collective-permute-start.27 = (f32[4,64]{1,0:T(4,128)S(1)}, f32[4,64]{1,0:T(4,128)S(1)}, u32[]{:S(2)}, u32[]{:S(2)}) collective-permute-start(f32[4,64]{1,0:T(4,128)S(1)} %get-tuple-element.76), channel_id=1, source_target_pairs={{0,1},{1,2},{2,3},{3,0},{4,5},{5,6},{6,7},{7,4},{8,9},{9,10},{10,1... | collective-permute-start | bytes 3080 | tf_op jit(solution)/shard_map/ppermute | solution.py:235
  (5 other events, 21.4 us)

commit v15 on v12

--- a/solution.py
+++ b/solution.py
@@ -40,14 +40,20 @@
 
     take = lax.ppermute(head_weight, "pair", CORE_SWAP)
 
+    def shifted(value, k):
+        return lax.ppermute(value, "vocab", [(i, (i + k) % vocab) for i in range(vocab)])
+
     def paired(value, reach):
         return lax.ppermute(value, "vocab", [(i, i ^ reach) for i in range(vocab)])
 
     squares = jnp.sum(wide * wide, axis=1)
-    reach = 1
-    while reach < vocab:
-        squares += paired(squares, reach)
-        reach *= 2
+    if vocab == 4:
+        squares += sum(shifted(squares, k) for k in range(1, vocab))
+    else:
+        reach = 1
+        while reach < vocab:
+            squares += paired(squares, reach)
+            reach *= 2
     squares = squares.reshape(2, seg)
 
     def row_scale(*earlier):
@@ -115,19 +121,26 @@
         swapped_near = swapped(near)
 
         far = 1 - y + 2 * (1 - first)
-        tips = [(0, 0), (1, vocab - 1)]
         pairs = [(b * vocab + z, (b ^ 2) * vocab + z) for b in range(4) for z in range(vocab)]
-        late = [pair for pair in pairs if (pair[0] // vocab // 2, pair[0] % vocab) in tips]
-        early = [pair for pair in pairs if pair not in late]
+        lone = [b * vocab + (vocab - 1) * (b // 2) for b in range(4)]
+        early = [pair for pair in pairs if pair[0] not in lone]
         got_early = lax.ppermute(quarter(far, 2), ("batch", "vocab"), early)
-        mine_early = quarter(y + 2 * (1 - first), 2)
+        mine_early = lax.optimization_barrier(quarter(y + 2 * (1 - first), 2))
         is_late = (level == 0) & (y == 1) | (level == vocab - 1) & (y == 0)
-        below_3, above_3 = up(below[2], 3), down(above[2], 3)
         near_part = dot(near, near_weight)
-        last = after(jnp.where(level == 0, above_3, below_3), got_early, near_part)
-        got_late = lax.ppermute(last, ("batch", "vocab"), late)
+        sent = after(own, below[2], above[2])
+        ends = []
+        for cross in (0, 2):
+            moves = []
+            for place in lone:
+                b, z = divmod(place, vocab)
+                moves.append(((b ^ cross) * vocab + z, b * vocab + vocab - 1 - z))
+            ends.append(lax.ppermute(sent, ("batch", "vocab"), sorted(moves)))
+        mine_late, got_late, got_early, _ = lax.optimization_barrier(
+            (ends[0], ends[1], got_early, near_part)
+        )
         far = by_y(
-            jnp.where(is_late, last, mine_early), jnp.where(is_late, got_late, got_early), 0
+            jnp.where(is_late, mine_late, mine_early), jnp.where(is_late, got_late, got_early), 0
         )
         swapped_far = swapped(far)
 
@@ -210,8 +223,7 @@
     every = jnp.stack(
         [own]
         + [
-            lax.ppermute(own, "vocab", [(i, (i + k) % vocab) for i in range(vocab)])
-            for k in range(1, vocab)
+            shifted(own, k) for k in range(1, vocab)
         ]
     )
     top = jnp.max(every[:, :2], axis=0)

time: 127 us -> 119 us (0.937)
  waiting for transfers between devices: 51.1 us -> 45.3 us
  starting transfers between devices: 40.7 us -> 45.2 us
  other arithmetic: 20.1 us -> 15.7 us
  matrix products: 11.5 us -> 9.41 us
    ppermute x3 -> x2, waiting for transfers between devices: 11.1 us -> 4.15 us  [down(): return lax.ppermute(value, 'vocab', [(z + 1, z) for z in range(vocab - k)])]
    ppermute x6 -> x8, waiting for transfers between devices: 12.9 us -> 6.21 us  [the longest x6 4.31 us: shifted(): lax.ppermute(value, 'vocab', [(i, (i + k) % vocab) for i in range(vocab)])]
    ppermute x1, waiting for transfers between devices: 1.02 us -> 6.17 us  [line_parts(): got_early = lax.ppermute(quarter(far, 2), ('batch', 'vocab'), early)]
    ppermute x6 -> x8, starting transfers between devices: 10.3 us -> 15.2 us  [the longest x6 9.44 us: shifted(): lax.ppermute(value, 'vocab', [(i, (i + k) % vocab) for i in range(vocab)])]
    ppermute x1, waiting for transfers between devices: 0.01 us -> 4.37 us  [line_parts(): got_near = lax.ppermute(near_sent, 'batch', Y_SWAP)]
    ppermute x2, starting transfers between devices: 2.9 us -> 6.56 us  [on_device(): next_x = lax.ppermute(more_sends[i][1], 'batch', X_SWAP)]
    another operation x6 -> x4, other arithmetic: 2.84 us -> 0.39 us  [by_y(): jnp.stack([jnp.where(y == 0, mine, other), jnp.where(y == 0, other, mine)...]
    ppermute x2, starting transfers between devices: 2.7 us -> 0.3 us  [on_device(): next_y = lax.ppermute(more_sends[i][0], 'batch', Y_SWAP)]
  transfers between devices with their start and end apart: 30 -> 30, of which waited for: 18 -> 16; matrix products, arithmetic and copies ran while one was open for 24% -> 20% of each run, Pallas kernels for 0% -> 0%
where the time goes in v15:
time: 119 us
  waiting for transfers between devices  45.3 us (38%)
  starting transfers between devices  45.2 us (38%)
  other arithmetic  15.7 us (13%)
  matrix products  9.41 us (8%)
  local copies, waits for them, and re-layouts  1.76 us (1%)
    ppermute x2, waiting for transfers between devices, on_device(): away_y = lax.ppermute(sends[i][1], 'batch', Y_SWAP)  10.5 us
    ppermute x6, starting transfers between devices, shifted(): lax.ppermute(value, 'vocab', [(i, (i + k) % vocab) for i in range(vocab)])  9.44 us
    dot_general x4, matrix products, dot(): jnp.dot(left.reshape(-1, block), weight, preferred_element_type=jnp.float32)  9.41 us
    ppermute x2, waiting for transfers between devices, on_device(): next_x = lax.ppermute(more_sends[i][1], 'batch', X_SWAP)  8.47 us
    ppermute x2, starting transfers between devices, on_device(): next_x = lax.ppermute(more_sends[i][1], 'batch', X_SWAP)  6.56 us
    ppermute x1, waiting for transfers between devices, line_parts(): got_early = lax.ppermute(quarter(far, 2), ('batch', 'vocab'), early)  6.17 us
    select_n x1, other arithmetic, line_parts(): jnp.where(keep_near, taken, kept)  5.88 us
    ppermute x2, starting transfers between devices, line_parts(): ends.append(lax.ppermute(sent, ('batch', 'vocab'), sorted(moves)))  5.72 us
  transfers between devices with their start and end apart: 30, of which 16 were waited for; matrix products, arithmetic and copies ran while one was open for 20% of the time, Pallas kernels for 0%

profile of v15, /device:TPU:0, one launch (start us, length us, event | category | flops | bytes accessed | tf_op | source)
XLA Modules:
  0.0 118.6 jit_solution(2269682755212634536)
XLA Ops:
  3.0 2.6 %collective-permute-start = (bf16[2,64,1024]{2,1,0:T(8,128)(2,1)S(1)}, bf16[2,64,1024]{2,1,0:T(8,128)(2,1)S(1)}, u32[]{:S(2)}, u32[]{:S(2)}) collective-permute-start(bf16[2,64,1024]{2,1,0:T(8,128)(2,1)S(1)} %constant_dynamic-slice_fusion.6), channel_id=1, source_target_pairs={{0,4},{4,0},{8,12},{12,8},{1,5},{5,1},{9,13},{13,9},{2,6},{6,2},{1... | collective-permute-start | bytes 786440 | tf_op jit(solution)/shard_map/ppermute | solution.py:85
  6.8 1.6 %collective-permute-start.1 = (f32[128]{0:T(128)S(1)}, f32[128]{0:T(128)S(1)}, u32[]{:S(2)}, u32[]{:S(2)}) collective-permute-start(f32[128]{0:T(128)S(1)} %multiply_reduce_fusion), channel_id=1, source_target_pairs={{0,1},{1,2},{2,3},{3,0},{4,5},{5,6},{6,7},{7,4},{8,9},{9,10},{10,1... | collective-permute-start | bytes 1544 | tf_op jit(solution)/shard_map/ppermute | solution.py:44
  8.5 2.6 %collective-permute-start.2 = (f32[128]{0:T(128)S(1)}, f32[128]{0:T(128)S(1)}, u32[]{:S(2)}, u32[]{:S(2)}) collective-permute-start(f32[128]{0:T(128)S(1)} %multiply_reduce_fusion), channel_id=1, source_target_pairs={{0,2},{1,3},{2,0},{3,1},{4,6},{5,7},{6,4},{7,5},{8,10},{9,11},{10,... | collective-permute-start | bytes 1544 | tf_op jit(solution)/shard_map/ppermute | solution.py:44
  12.9 1.7 %collective-permute-done.3 = f32[128]{0:T(128)S(1)} collective-permute-done((f32[128]{0:T(128)S(1)}, f32[128]{0:T(128)S(1)}, u32[]{:S(2)}, u32[]{:S(2)}) %collective-permute-start.3) | collective-permute-done | bytes 544 | tf_op jit(solution)/shard_map/ppermute | solution.py:44
  14.9 2.2 %collective-permute-start.7 = (bf16[2,2,64,1024]{3,2,1,0:T(8,128)(2,1)S(1)}, bf16[2,2,64,1024]{3,2,1,0:T(8,128)(2,1)S(1)}, u32[]{:S(2)}, u32[]{:S(2)}) collective-permute-start(bf16[2,2,64,1024]{3,2,1,0:T(8,128)(2,1)S(1)} %pad_maximum_fusion.2), channel_id=1, source_target_pairs={{0,1},{1,2},{2,3},{4,5},{5,6},{6,7},{8,9},{9,10},{10,11},{12,13},{... | collective-permute-start | bytes 1572872 | tf_op jit(solution)/shard_map/ppermute | solution.py:92
  19.1 4.3 %collective-permute-start.6 = (f32[64]{0:T(128)S(1)}, f32[64]{0:T(128)S(1)}, u32[]{:S(2)}, u32[]{:S(2)}) collective-permute-start(f32[64]{0:T(128)S(1)} %get-tuple-element.76), channel_id=1, source_target_pairs={{0,4},{4,12},{8,20},{12,28},{16,0},{20,8},{24,16},{28,24},{1,5},{5... | collective-permute-start | bytes 776 | tf_op jit(solution)/shard_map/ppermute | solution.py:61
  24.7 2.8 %collective-permute-done.7 = bf16[2,2,64,1024]{3,2,1,0:T(8,128)(2,1)S(1)} collective-permute-done((bf16[2,2,64,1024]{3,2,1,0:T(8,128)(2,1)S(1)}, bf16[2,2,64,1024]{3,2,1,0:T(8,128)(2,1)S(1)}, u32[]{:S(2)}, u32[]{:S(2)}) %collective-permute-start.7) | collective-permute-done | bytes 524320 | tf_op jit(solution)/shard_map/ppermute | solution.py:92
  27.5 4.1 %collective-permute-done.4 = bf16[2,2,64,1024]{3,2,1,0:T(8,128)(2,1)S(1)} collective-permute-done((bf16[2,2,64,1024]{3,2,1,0:T(8,128)(2,1)S(1)}, bf16[2,2,64,1024]{3,2,1,0:T(8,128)(2,1)S(1)}, u32[]{:S(2)}, u32[]{:S(2)}) %collective-permute-start.4) | collective-permute-done | bytes 524320 | tf_op jit(solution)/shard_map/ppermute | solution.py:95
  32.9 1.5 %collective-permute-start.9 = (bf16[2,2,64,1024]{3,2,1,0:T(8,128)(2,1)S(1)}, bf16[2,2,64,1024]{3,2,1,0:T(8,128)(2,1)}, u32[]{:S(2)}, u32[]{:S(2)}) collective-permute-start(bf16[2,2,64,1024]{3,2,1,0:T(8,128)(2,1)S(1)} %collective-permute-done.7), channel_id=1, source_target_pairs={{1,2},{2,3},{5,6},{6,7},{9,10},{10,11},{13,14},{14,15},{17,18},{18... | collective-permute-start | bytes 1572872 | tf_op jit(solution)/shard_map/ppermute | solution.py:92
  34.5 1.6 %collective-permute-start.8 = (bf16[2,2,64,1024]{3,2,1,0:T(8,128)(2,1)S(1)}, bf16[2,2,64,1024]{3,2,1,0:T(8,128)(2,1)S(1)}, u32[]{:S(2)}, u32[]{:S(2)}) collective-permute-start(bf16[2,2,64,1024]{3,2,1,0:T(8,128)(2,1)S(1)} %select_select_fusion.2), channel_id=1, source_target_pairs={{0,8},{8,0},{4,12},{12,4},{1,9},{9,1},{5,13},{13,5},{2,10},{10,2},... | collective-permute-start | bytes 1572872 | tf_op jit(solution)/shard_map/ppermute | solution.py:110
  36.1 5.9 %broadcast_select_fusion = (bf16[1024,2048]{1,0:T(8,128)(2,1)S(1)}, bf16[1024,2048]{1,0:T(8,128)(2,1)S(1)}) fusion(pred[]{:T(512)S(6)} %eq.76, bf16[1024,4096]{1,0:T(8,128)(2,1)} %collective-permute-done.10, s32[]{:T(128)S(6)} %select_n.247, bf16[1024,4096]{1,0:T(8,128)(2,1)} %param.5), kind=kLoop, calls=%fused_computation.2 | loop fusion | flops 4194304 | bytes 16777220 | tf_op jit(solution)/shard_map/jit(_where)/select_n | solution.py:116
  42.0 4.4 %collective-permute-done.8 = bf16[2,2,64,1024]{3,2,1,0:T(8,128)(2,1)S(1)} collective-permute-done((bf16[2,2,64,1024]{3,2,1,0:T(8,128)(2,1)S(1)}, bf16[2,2,64,1024]{3,2,1,0:T(8,128)(2,1)S(1)}, u32[]{:S(2)}, u32[]{:S(2)}) %collective-permute-start.8) | collective-permute-done | bytes 524320 | tf_op jit(solution)/shard_map/ppermute | solution.py:110
  46.4 5.0 %collective-permute-start.12 = (bf16[2,2,64,1024]{3,2,1,0:T(8,128)(2,1)S(1)}, bf16[2,2,64,1024]{3,2,1,0:T(8,128)(2,1)S(1)}, u32[]{:S(2)}, u32[]{:S(2)}) collective-permute-start(bf16[2,2,64,1024]{3,2,1,0:T(8,128)(2,1)S(1)} %pad_maximum_fusion.2), channel_id=1, source_target_pairs={{0,3},{4,7},{11,8},{15,12},{16,19},{20,23},{27,24},{31,28}} | collective-permute-start | bytes 1572872 | tf_op jit(solution)/shard_map/ppermute | solution.py:138
  53.4 1.5 %collective-permute-start.14 = (bf16[2,2,64,1024]{3,2,1,0:T(8,128)(2,1)S(1)}, bf16[2,2,64,1024]{3,2,1,0:T(8,128)(2,1)S(1)}, u32[]{:S(2)}, u32[]{:S(2)}) collective-permute-start(bf16[2,2,64,1024]{3,2,1,0:T(8,128)(2,1)S(1)} %get-tuple-element.51), channel_id=1, source_target_pairs={{1,9},{2,10},{3,11},{5,13},{6,14},{7,15},{8,0},{9,1},{10,2},{12,4}... | collective-permute-start | bytes 1572872 | tf_op jit(solution)/shard_map/ppermute | solution.py:127
  55.1 2.3 %fusion.36 = f32[512,2048]{1,0:T(8,128)S(1)} fusion(bf16[512,1024]{1,0:T(8,128)(2,1)S(1)} %bitcast.116, bf16[1024,2048]{1,0:T(8,128)(2,1)S(1)} %get-tuple-element.26), kind=kOutput, calls=%fused_computation.111 | convolution fusion | flops 2147483648 | bytes 9437184 | tf_op jit(solution)/shard_map/dot_general | solution.py:81
  57.5 1.9 %collective-permute-done.12 = bf16[2,2,64,1024]{3,2,1,0:T(8,128)(2,1)S(1)} collective-permute-done((bf16[2,2,64,1024]{3,2,1,0:T(8,128)(2,1)S(1)}, bf16[2,2,64,1024]{3,2,1,0:T(8,128)(2,1)S(1)}, u32[]{:S(2)}, u32[]{:S(2)}) %collective-permute-start.12) | collective-permute-done | bytes 524320 | tf_op jit(solution)/shard_map/ppermute | solution.py:138
  59.4 6.2 %collective-permute-done.14 = bf16[2,2,64,1024]{3,2,1,0:T(8,128)(2,1)S(1)} collective-permute-done((bf16[2,2,64,1024]{3,2,1,0:T(8,128)(2,1)S(1)}, bf16[2,2,64,1024]{3,2,1,0:T(8,128)(2,1)S(1)}, u32[]{:S(2)}, u32[]{:S(2)}) %collective-permute-start.14) | collective-permute-done | bytes 524320 | tf_op jit(solution)/shard_map/ppermute | solution.py:127
  65.9 2.4 %add_multiply_fusion.1 = f32[512,2048]{1,0:T(8,128)S(1)} fusion(f32[512,2048]{1,0:T(8,128)S(1)} %fusion.36, bf16[512,1024]{1,0:T(8,128)(2,1)S(1)} %bitcast.117, bf16[1024,2048]{1,0:T(8,128)(2,1)S(1)} %get-tuple-element.27), kind=kOutput, calls=%fused_computation.1 | convolution fusion | flops 2149580800 | bytes 13631488 | tf_op jit(solution)/shard_map/dot_general | solution.py:81
  69.3 3.3 %collective-permute-start.15 = (f16[2,2,64,1024]{3,2,0,1:T(8,128)(2,1)S(1)}, f16[2,2,64,1024]{3,2,0,1:T(8,128)(2,1)S(1)}, u32[]{:S(2)}, u32[]{:S(2)}) collective-permute-start(f16[2,2,64,1024]{3,2,0,1:T(8,128)(2,1)S(1)} %fusion.6), channel_id=1, source_target_pairs={{0,4},{4,0},{8,12},{12,8},{1,5},{5,1},{9,13},{13,9},{2,6},{6,2},{1... | collective-permute-start | bytes 1572872 | tf_op jit(solution)/shard_map/ppermute | solution.py:181
  72.6 2.3 %fusion.37 = f32[512,2048]{1,0:T(8,128)S(1)} fusion(bf16[512,1024]{1,0:T(8,128)(2,1)S(1)} %bitcast.126, bf16[1024,2048]{1,0:T(8,128)(2,1)S(1)} %get-tuple-element.27), kind=kOutput, calls=%fused_computation.112 | convolution fusion | flops 2147483648 | bytes 9437184 | tf_op jit(solution)/shard_map/dot_general | solution.py:81
  75.0 2.3 %add_multiply_fusion = f32[512,2048]{1,0:T(8,128)S(1)} fusion(f32[512,2048]{1,0:T(8,128)S(1)} %fusion.37, bf16[512,1024]{1,0:T(8,128)(2,1)S(1)} %bitcast.125, bf16[1024,2048]{1,0:T(8,128)(2,1)S(1)} %get-tuple-element.26), kind=kOutput, calls=%fused_computation | convolution fusion | flops 2149580800 | bytes 13631488 | tf_op jit(solution)/shard_map/dot_general | solution.py:81
  78.0 2.1 %collective-permute-start.20 = (f16[2,2,64,1024]{3,2,1,0:T(8,128)(2,1)S(1)}, f16[2,2,64,1024]{3,2,1,0:T(8,128)(2,1)S(1)}, u32[]{:S(2)}, u32[]{:S(2)}) collective-permute-start(f16[2,2,64,1024]{3,2,1,0:T(8,128)(2,1)S(1)} %fusion.5), channel_id=1, source_target_pairs={{0,8},{8,0},{4,12},{12,4},{1,9},{9,1},{5,13},{13,5},{2,10},{10,2},... | collective-permute-start | bytes 1572872 | tf_op jit(solution)/shard_map/ppermute | solution.py:182
  80.5 3.2 %collective-permute-done.21 = f16[2,2,64,1024]{3,2,1,0:T(8,128)(2,1)S(1)} collective-permute-done((f16[2,2,64,1024]{3,2,1,0:T(8,128)(2,1)S(1)}, f16[2,2,64,1024]{3,2,1,0:T(8,128)(2,1)S(1)}, u32[]{:S(2)}, u32[]{:S(2)}) %collective-permute-start.21) | collective-permute-done | bytes 524320 | tf_op jit(solution)/shard_map/ppermute | solution.py:182
  84.0 3.3 %collective-permute-start.22 = (f16[2,64,1024]{2,1,0:T(8,128)(2,1)S(1)}, f16[2,64,1024]{2,1,0:T(8,128)(2,1)S(1)}, u32[]{:S(2)}, u32[]{:S(2)}) collective-permute-start(f16[2,64,1024]{2,1,0:T(8,128)(2,1)S(1)} %fusion.15), channel_id=1, source_target_pairs={{0,4},{4,0},{8,12},{12,8},{1,5},{5,1},{9,13},{13,9},{2,6},{6,2},{1... | collective-permute-start | bytes 786440 | tf_op jit(solution)/shard_map/ppermute | solution.py:194
  87.6 7.3 %collective-permute-done.20 = f16[2,2,64,1024]{3,2,1,0:T(8,128)(2,1)S(1)} collective-permute-done((f16[2,2,64,1024]{3,2,1,0:T(8,128)(2,1)S(1)}, f16[2,2,64,1024]{3,2,1,0:T(8,128)(2,1)S(1)}, u32[]{:S(2)}, u32[]{:S(2)}) %collective-permute-start.20) | collective-permute-done | bytes 524320 | tf_op jit(solution)/shard_map/ppermute | solution.py:182
  95.2 3.3 %collective-permute-start.25 = (f16[2,64,1024]{2,1,0:T(8,128)(2,1)S(1)}, f16[2,64,1024]{2,1,0:T(8,128)(2,1)S(1)}, u32[]{:S(2)}, u32[]{:S(2)}) collective-permute-start(f16[2,64,1024]{2,1,0:T(8,128)(2,1)S(1)} %fusion.14), channel_id=1, source_target_pairs={{0,4},{4,0},{8,12},{12,8},{1,5},{5,1},{9,13},{13,9},{2,6},{6,2},{1... | collective-permute-start | bytes 786440 | tf_op jit(solution)/shard_map/ppermute | solution.py:194
  98.9 3.4 %collective-permute-done.22 = f16[2,64,1024]{2,1,0:T(8,128)(2,1)S(1)} collective-permute-done((f16[2,64,1024]{2,1,0:T(8,128)(2,1)S(1)}, f16[2,64,1024]{2,1,0:T(8,128)(2,1)S(1)}, u32[]{:S(2)}, u32[]{:S(2)}) %collective-permute-start.22) | collective-permute-done | bytes 262176 | tf_op jit(solution)/shard_map/ppermute | solution.py:194
  102.6 5.1 %collective-permute-done.25 = f16[2,64,1024]{2,1,0:T(8,128)(2,1)S(1)} collective-permute-done((f16[2,64,1024]{2,1,0:T(8,128)(2,1)S(1)}, f16[2,64,1024]{2,1,0:T(8,128)(2,1)S(1)}, u32[]{:S(2)}, u32[]{:S(2)}) %collective-permute-start.25) | collective-permute-done | bytes 262176 | tf_op jit(solution)/shard_map/ppermute | solution.py:194
  108.2 1.4 %collective-permute-done.26 = f16[64,2048]{1,0:T(8,128)(2,1)S(1)} collective-permute-done((f16[64,2048]{1,0:T(8,128)(2,1)S(1)}, f16[64,2048]{1,0:T(8,128)(2,1)S(1)}, u32[]{:S(2)}, u32[]{:S(2)}) %collective-permute-start.26) | collective-permute-done | bytes 262176 | tf_op jit(solution)/shard_map/ppermute | solution.py:75
  113.2 1.6 %collective-permute-start.29 = (f32[4,64]{1,0:T(4,128)S(1)}, f32[4,64]{1,0:T(4,128)S(1)}, u32[]{:S(2)}, u32[]{:S(2)}) collective-permute-start(f32[4,64]{1,0:T(4,128)S(1)} %get-tuple-element.68), channel_id=1, source_target_pairs={{0,3},{1,0},{2,1},{3,2},{4,7},{5,4},{6,5},{7,6},{8,11},{9,8},{10,9... | collective-permute-start | bytes 3080 | tf_op jit(solution)/shard_map/ppermute | solution.py:44
  114.8 1.6 %collective-permute-done.27 = f32[4,64]{1,0:T(4,128)S(1)} collective-permute-done((f32[4,64]{1,0:T(4,128)S(1)}, f32[4,64]{1,0:T(4,128)S(1)}, u32[]{:S(2)}, u32[]{:S(2)}) %collective-permute-start.27) | collective-permute-done | bytes 1056 | tf_op jit(solution)/shard_map/ppermute | solution.py:44
  117.0 1.6 %fusion.2 = (f32[64,4096]{1,0:T(8,128)}, f32[64,4096]{1,0:T(8,128)}) fusion(f32[64]{0:T(128)S(1)} %get-tuple-element.69, f32[64]{0:T(128)S(1)} %get-tuple-element.71, f16[64,2048]{1,0:T(8,128)(2,1)S(1)} %get-tuple-element.62, f16[64,2048]{1,0:T(8,128)(2,1)S(1)} %get-tuple-element.60, f32[64,4096]{1,0:T(8,128)S(1)} %get-tuple-element.41, ...), kind=kLoop, calls=%fused_computation.18 | loop fusion | flops 1310720 | bytes 3670784 | tf_op jit(solution)/shard_map/sub | solution.py:232
  (85 shorter events, 21.2 us)
Async XLA Ops:
  0.6 35.5 %collective-permute-start.10 = (bf16[1024,4096]{1,0:T(8,128)(2,1)}, bf16[1024,4096]{1,0:T(8,128)(2,1)}, u32[]{:S(2)}, u32[]{:S(2)}) collective-permute-start(bf16[1024,4096]{1,0:T(8,128)(2,1)} %param.5), channel_id=1, source_target_pairs={{0,16},{16,0},{1,17},{17,1},{2,18},{18,2},{3,19},{19,3},{4,20},{20... | collective-permute-start | bytes 25165832 | tf_op jit(solution)/shard_map/ppermute | solution.py:41
  3.0 11.7 %collective-permute-start = (bf16[2,64,1024]{2,1,0:T(8,128)(2,1)S(1)}, bf16[2,64,1024]{2,1,0:T(8,128)(2,1)S(1)}, u32[]{:S(2)}, u32[]{:S(2)}) collective-permute-start(bf16[2,64,1024]{2,1,0:T(8,128)(2,1)S(1)} %constant_dynamic-slice_fusion.6), channel_id=1, source_target_pairs={{0,4},{4,0},{8,12},{12,8},{1,5},{5,1},{9,13},{13,9},{2,6},{6,2},{1... | collective-permute-start | bytes 786440 | tf_op jit(solution)/shard_map/ppermute | solution.py:85
  6.8 5.6 %collective-permute-start.1 = (f32[128]{0:T(128)S(1)}, f32[128]{0:T(128)S(1)}, u32[]{:S(2)}, u32[]{:S(2)}) collective-permute-start(f32[128]{0:T(128)S(1)} %multiply_reduce_fusion), channel_id=1, source_target_pairs={{0,1},{1,2},{2,3},{3,0},{4,5},{5,6},{6,7},{7,4},{8,9},{9,10},{10,1... | collective-permute-start | bytes 1544 | tf_op jit(solution)/shard_map/ppermute | solution.py:44
  8.5 4.4 %collective-permute-start.2 = (f32[128]{0:T(128)S(1)}, f32[128]{0:T(128)S(1)}, u32[]{:S(2)}, u32[]{:S(2)}) collective-permute-start(f32[128]{0:T(128)S(1)} %multiply_reduce_fusion), channel_id=1, source_target_pairs={{0,2},{1,3},{2,0},{3,1},{4,6},{5,7},{6,4},{7,5},{8,10},{9,11},{10,... | collective-permute-start | bytes 1544 | tf_op jit(solution)/shard_map/ppermute | solution.py:44
  11.0 3.5 %collective-permute-start.3 = (f32[128]{0:T(128)S(1)}, f32[128]{0:T(128)S(1)}, u32[]{:S(2)}, u32[]{:S(2)}) collective-permute-start(f32[128]{0:T(128)S(1)} %multiply_reduce_fusion), channel_id=1, source_target_pairs={{0,3},{1,0},{2,1},{3,2},{4,7},{5,4},{6,5},{7,6},{8,11},{9,8},{10,9... | collective-permute-start | bytes 1544 | tf_op jit(solution)/shard_map/ppermute | solution.py:44
  14.9 12.6 %collective-permute-start.7 = (bf16[2,2,64,1024]{3,2,1,0:T(8,128)(2,1)S(1)}, bf16[2,2,64,1024]{3,2,1,0:T(8,128)(2,1)S(1)}, u32[]{:S(2)}, u32[]{:S(2)}) collective-permute-start(bf16[2,2,64,1024]{3,2,1,0:T(8,128)(2,1)S(1)} %pad_maximum_fusion.2), channel_id=1, source_target_pairs={{0,1},{1,2},{2,3},{4,5},{5,6},{6,7},{8,9},{9,10},{10,11},{12,13},{... | collective-permute-start | bytes 1572872 | tf_op jit(solution)/shard_map/ppermute | solution.py:92
  17.0 14.6 %collective-permute-start.4 = (bf16[2,2,64,1024]{3,2,1,0:T(8,128)(2,1)S(1)}, bf16[2,2,64,1024]{3,2,1,0:T(8,128)(2,1)S(1)}, u32[]{:S(2)}, u32[]{:S(2)}) collective-permute-start(bf16[2,2,64,1024]{3,2,1,0:T(8,128)(2,1)S(1)} %pad_maximum_fusion.2), channel_id=1, source_target_pairs={{1,0},{2,1},{3,2},{5,4},{6,5},{7,6},{9,8},{10,9},{11,10},{13,12},{... | collective-permute-start | bytes 1572872 | tf_op jit(solution)/shard_map/ppermute | solution.py:95
  18.5 5.0 %collective-permute-start.5 = (f32[64]{0:T(128)S(1)}, f32[64]{0:T(128)S(1)}, u32[]{:S(2)}, u32[]{:S(2)}) collective-permute-start(f32[64]{0:T(128)S(1)} %get-tuple-element.75), channel_id=1, source_target_pairs={{0,0},{4,8},{8,16},{12,24},{16,4},{20,12},{24,20},{28,28},{1,1},{5... | collective-permute-start | bytes 776 | tf_op jit(solution)/shard_map/ppermute | solution.py:61
  19.1 5.6 %collective-permute-start.6 = (f32[64]{0:T(128)S(1)}, f32[64]{0:T(128)S(1)}, u32[]{:S(2)}, u32[]{:S(2)}) collective-permute-start(f32[64]{0:T(128)S(1)} %get-tuple-element.76), channel_id=1, source_target_pairs={{0,4},{4,12},{8,20},{12,28},{16,0},{20,8},{24,16},{28,24},{1,5},{5... | collective-permute-start | bytes 776 | tf_op jit(solution)/shard_map/ppermute | solution.py:61
  31.6 14.7 %collective-permute-start.11 = (bf16[2,2,64,1024]{3,2,1,0:T(8,128)(2,1)S(1)}, bf16[2,2,64,1024]{3,2,1,0:T(8,128)(2,1)S(1)}, u32[]{:S(2)}, u32[]{:S(2)}) collective-permute-start(bf16[2,2,64,1024]{3,2,1,0:T(8,128)(2,1)S(1)} %collective-permute-done.4), channel_id=1, source_target_pairs={{1,0},{2,1},{5,4},{6,5},{9,8},{10,9},{13,12},{14,13},{17,16},{18,1... | collective-permute-start | bytes 1572872 | tf_op jit(solution)/shard_map/ppermute | solution.py:95
  32.9 13.5 %collective-permute-start.9 = (bf16[2,2,64,1024]{3,2,1,0:T(8,128)(2,1)S(1)}, bf16[2,2,64,1024]{3,2,1,0:T(8,128)(2,1)}, u32[]{:S(2)}, u32[]{:S(2)}) collective-permute-start(bf16[2,2,64,1024]{3,2,1,0:T(8,128)(2,1)S(1)} %collective-permute-done.7), channel_id=1, source_target_pairs={{1,2},{2,3},{5,6},{6,7},{9,10},{10,11},{13,14},{14,15},{17,18},{18... | collective-permute-start | bytes 1572872 | tf_op jit(solution)/shard_map/ppermute | solution.py:92
  34.5 11.8 %collective-permute-start.8 = (bf16[2,2,64,1024]{3,2,1,0:T(8,128)(2,1)S(1)}, bf16[2,2,64,1024]{3,2,1,0:T(8,128)(2,1)S(1)}, u32[]{:S(2)}, u32[]{:S(2)}) collective-permute-start(bf16[2,2,64,1024]{3,2,1,0:T(8,128)(2,1)S(1)} %select_select_fusion.2), channel_id=1, source_target_pairs={{0,8},{8,0},{4,12},{12,4},{1,9},{9,1},{5,13},{13,5},{2,10},{10,2},... | collective-permute-start | bytes 1572872 | tf_op jit(solution)/shard_map/ppermute | solution.py:110
  46.4 13.0 %collective-permute-start.12 = (bf16[2,2,64,1024]{3,2,1,0:T(8,128)(2,1)S(1)}, bf16[2,2,64,1024]{3,2,1,0:T(8,128)(2,1)S(1)}, u32[]{:S(2)}, u32[]{:S(2)}) collective-permute-start(bf16[2,2,64,1024]{3,2,1,0:T(8,128)(2,1)S(1)} %pad_maximum_fusion.2), channel_id=1, source_target_pairs={{0,3},{4,7},{11,8},{15,12},{16,19},{20,23},{27,24},{31,28}} | collective-permute-start | bytes 1572872 | tf_op jit(solution)/shard_map/ppermute | solution.py:138
  51.4 7.9 %collective-permute-start.13 = (bf16[2,2,64,1024]{3,2,1,0:T(8,128)(2,1)S(1)}, bf16[2,2,64,1024]{3,2,1,0:T(8,128)(2,1)S(1)}, u32[]{:S(2)}, u32[]{:S(2)}) collective-permute-start(bf16[2,2,64,1024]{3,2,1,0:T(8,128)(2,1)S(1)} %pad_maximum_fusion.2), channel_id=1, source_target_pairs={{3,8},{7,12},{8,3},{12,7},{19,24},{23,28},{24,19},{28,23}} | collective-permute-start | bytes 1572872 | tf_op jit(solution)/shard_map/ppermute | solution.py:138
  53.4 12.1 %collective-permute-start.14 = (bf16[2,2,64,1024]{3,2,1,0:T(8,128)(2,1)S(1)}, bf16[2,2,64,1024]{3,2,1,0:T(8,128)(2,1)S(1)}, u32[]{:S(2)}, u32[]{:S(2)}) collective-permute-start(bf16[2,2,64,1024]{3,2,1,0:T(8,128)(2,1)S(1)} %get-tuple-element.51), channel_id=1, source_target_pairs={{1,9},{2,10},{3,11},{5,13},{6,14},{7,15},{8,0},{9,1},{10,2},{12,4}... | collective-permute-start | bytes 1572872 | tf_op jit(solution)/shard_map/ppermute | solution.py:127
  55.0 19.9 %collective-permute-start.16 = (bf16[2,2,2,64,1024]{4,3,2,1,0:T(8,128)(2,1)S(1)}, bf16[2,2,2,64,1024]{4,3,2,1,0:T(8,128)(2,1)S(1)}, u32[]{:S(2)}, u32[]{:S(2)}) collective-permute-start(bf16[2,2,2,64,1024]{4,3,2,1,0:T(8,128)(2,1)S(1)} %pad_maximum_fusion), channel_id=1, source_target_pairs={{0,16},{16,0},{1,17},{17,1},{2,18},{18,2},{3,19},{19,3},{4,20},{20... | collective-permute-start | bytes 3145736 | tf_op jit(solution)/shard_map/ppermute | solution.py:75
  65.8 6.9 %collective-permute-start.17 = (bf16[2,2,2,64,1024]{4,3,2,1,0:T(8,128)(2,1)S(1)}, bf16[2,2,2,64,1024]{4,3,2,1,0:T(8,128)(2,1)S(1)}, u32[]{:S(2)}, u32[]{:S(2)}) collective-permute-start(bf16[2,2,2,64,1024]{4,3,2,1,0:T(8,128)(2,1)S(1)} %pad_maximum_fusion.1), channel_id=1, source_target_pairs={{0,16},{16,0},{1,17},{17,1},{2,18},{18,2},{3,19},{19,3},{4,20},{20... | collective-permute-start | bytes 3145736 | tf_op jit(solution)/shard_map/ppermute | solution.py:75
  68.9 14.8 %collective-permute-start.21 = (f16[2,2,64,1024]{3,2,1,0:T(8,128)(2,1)S(1)}, f16[2,2,64,1024]{3,2,1,0:T(8,128)(2,1)S(1)}, u32[]{:S(2)}, u32[]{:S(2)}) collective-permute-start(f16[2,2,64,1024]{3,2,1,0:T(8,128)(2,1)S(1)} %fusion.4), channel_id=1, source_target_pairs={{0,8},{8,0},{4,12},{12,4},{1,9},{9,1},{5,13},{13,5},{2,10},{10,2},... | collective-permute-start | bytes 1572872 | tf_op jit(solution)/shard_map/ppermute | solution.py:182
  69.3 17.9 %collective-permute-start.15 = (f16[2,2,64,1024]{3,2,0,1:T(8,128)(2,1)S(1)}, f16[2,2,64,1024]{3,2,0,1:T(8,128)(2,1)S(1)}, u32[]{:S(2)}, u32[]{:S(2)}) collective-permute-start(f16[2,2,64,1024]{3,2,0,1:T(8,128)(2,1)S(1)} %fusion.6), channel_id=1, source_target_pairs={{0,4},{4,0},{8,12},{12,8},{1,5},{5,1},{9,13},{13,9},{2,6},{6,2},{1... | collective-permute-start | bytes 1572872 | tf_op jit(solution)/shard_map/ppermute | solution.py:181
  78.0 17.0 %collective-permute-start.20 = (f16[2,2,64,1024]{3,2,1,0:T(8,128)(2,1)S(1)}, f16[2,2,64,1024]{3,2,1,0:T(8,128)(2,1)S(1)}, u32[]{:S(2)}, u32[]{:S(2)}) collective-permute-start(f16[2,2,64,1024]{3,2,1,0:T(8,128)(2,1)S(1)} %fusion.5), channel_id=1, source_target_pairs={{0,8},{8,0},{4,12},{12,4},{1,9},{9,1},{5,13},{13,5},{2,10},{10,2},... | collective-permute-start | bytes 1572872 | tf_op jit(solution)/shard_map/ppermute | solution.py:182
  80.4 18.1 %collective-permute-start.19 = (f16[2,2,64,1024]{3,2,0,1:T(8,128)(2,1)S(1)}, f16[2,2,64,1024]{3,2,0,1:T(8,128)(2,1)S(1)}, u32[]{:S(2)}, u32[]{:S(2)}) collective-permute-start(f16[2,2,64,1024]{3,2,0,1:T(8,128)(2,1)S(1)} %fusion.7), channel_id=1, source_target_pairs={{0,4},{4,0},{8,12},{12,8},{1,5},{5,1},{9,13},{13,9},{2,6},{6,2},{1... | collective-permute-start | bytes 1572872 | tf_op jit(solution)/shard_map/ppermute | solution.py:181
  84.0 18.3 %collective-permute-start.22 = (f16[2,64,1024]{2,1,0:T(8,128)(2,1)S(1)}, f16[2,64,1024]{2,1,0:T(8,128)(2,1)S(1)}, u32[]{:S(2)}, u32[]{:S(2)}) collective-permute-start(f16[2,64,1024]{2,1,0:T(8,128)(2,1)S(1)} %fusion.15), channel_id=1, source_target_pairs={{0,4},{4,0},{8,12},{12,8},{1,5},{5,1},{9,13},{13,9},{2,6},{6,2},{1... | collective-permute-start | bytes 786440 | tf_op jit(solution)/shard_map/ppermute | solution.py:194
  87.5 14.8 %collective-permute-start.18 = (f16[2,64,1024]{2,1,0:T(8,128)(2,1)S(1)}, f16[2,64,1024]{2,1,0:T(8,128)(2,1)S(1)}, u32[]{:S(2)}, u32[]{:S(2)}) collective-permute-start(f16[2,64,1024]{2,1,0:T(8,128)(2,1)S(1)} %fusion.12), channel_id=1, source_target_pairs={{0,8},{8,0},{4,12},{12,4},{1,9},{9,1},{5,13},{13,5},{2,10},{10,2},... | collective-permute-start | bytes 786440 | tf_op jit(solution)/shard_map/ppermute | solution.py:193
  95.2 12.5 %collective-permute-start.25 = (f16[2,64,1024]{2,1,0:T(8,128)(2,1)S(1)}, f16[2,64,1024]{2,1,0:T(8,128)(2,1)S(1)}, u32[]{:S(2)}, u32[]{:S(2)}) collective-permute-start(f16[2,64,1024]{2,1,0:T(8,128)(2,1)S(1)} %fusion.14), channel_id=1, source_target_pairs={{0,4},{4,0},{8,12},{12,8},{1,5},{5,1},{9,13},{13,9},{2,6},{6,2},{1... | collective-permute-start | bytes 786440 | tf_op jit(solution)/shard_map/ppermute | solution.py:194
  98.7 9.0 %collective-permute-start.24 = (f16[2,64,1024]{2,1,0:T(8,128)(2,1)S(1)}, f16[2,64,1024]{2,1,0:T(8,128)(2,1)S(1)}, u32[]{:S(2)}, u32[]{:S(2)}) collective-permute-start(f16[2,64,1024]{2,1,0:T(8,128)(2,1)S(1)} %fusion.13), channel_id=1, source_target_pairs={{0,8},{8,0},{4,12},{12,4},{1,9},{9,1},{5,13},{13,5},{2,10},{10,2},... | collective-permute-start | bytes 786440 | tf_op jit(solution)/shard_map/ppermute | solution.py:193
  102.5 5.5 %collective-permute-start.23 = (f16[64,2048]{1,0:T(8,128)(2,1)S(1)}, f16[64,2048]{1,0:T(8,128)(2,1)S(1)}, u32[]{:S(2)}, u32[]{:S(2)}) collective-permute-start(f16[64,2048]{1,0:T(8,128)(2,1)S(1)} %fusion.21), channel_id=1, source_target_pairs={{0,16},{16,0},{1,17},{17,1},{2,18},{18,2},{3,19},{19,3},{4,20},{20... | collective-permute-start | bytes 786440 | tf_op jit(solution)/shard_map/ppermute | solution.py:75
  108.0 1.6 %collective-permute-start.26 = (f16[64,2048]{1,0:T(8,128)(2,1)S(1)}, f16[64,2048]{1,0:T(8,128)(2,1)S(1)}, u32[]{:S(2)}, u32[]{:S(2)}) collective-permute-start(f16[64,2048]{1,0:T(8,128)(2,1)S(1)} %fusion.19), channel_id=1, source_target_pairs={{0,16},{16,0},{1,17},{17,1},{2,18},{18,2},{3,19},{19,3},{4,20},{20... | collective-permute-start | bytes 786440 | tf_op jit(solution)/shard_map/ppermute | solution.py:75
  110.9 5.4 %collective-permute-start.27 = (f32[4,64]{1,0:T(4,128)S(1)}, f32[4,64]{1,0:T(4,128)S(1)}, u32[]{:S(2)}, u32[]{:S(2)}) collective-permute-start(f32[4,64]{1,0:T(4,128)S(1)} %get-tuple-element.68), channel_id=1, source_target_pairs={{0,1},{1,2},{2,3},{3,0},{4,5},{5,6},{6,7},{7,4},{8,9},{9,10},{10,1... | collective-permute-start | bytes 3080 | tf_op jit(solution)/shard_map/ppermute | solution.py:44
  112.2 4.5 %collective-permute-start.28 = (f32[4,64]{1,0:T(4,128)S(1)}, f32[4,64]{1,0:T(4,128)S(1)}, u32[]{:S(2)}, u32[]{:S(2)}) collective-permute-start(f32[4,64]{1,0:T(4,128)S(1)} %get-tuple-element.68), channel_id=1, source_target_pairs={{0,2},{1,3},{2,0},{3,1},{4,6},{5,7},{6,4},{7,5},{8,10},{9,11},{10,... | collective-permute-start | bytes 3080 | tf_op jit(solution)/shard_map/ppermute | solution.py:44
  113.2 3.7 %collective-permute-start.29 = (f32[4,64]{1,0:T(4,128)S(1)}, f32[4,64]{1,0:T(4,128)S(1)}, u32[]{:S(2)}, u32[]{:S(2)}) collective-permute-start(f32[4,64]{1,0:T(4,128)S(1)} %get-tuple-element.68), channel_id=1, source_target_pairs={{0,3},{1,0},{2,1},{3,2},{4,7},{5,4},{6,5},{7,6},{8,11},{9,8},{10,9... | collective-permute-start | bytes 3080 | tf_op jit(solution)/shard_map/ppermute | solution.py:44

commit v16 on v15

--- a/solution.py
+++ b/solution.py
@@ -46,26 +46,27 @@
     def paired(value, reach):
         return lax.ppermute(value, "vocab", [(i, i ^ reach) for i in range(vocab)])
 
-    squares = jnp.sum(wide * wide, axis=1)
-    if vocab == 4:
-        squares += sum(shifted(squares, k) for k in range(1, vocab))
-    else:
-        reach = 1
-        while reach < vocab:
-            squares += paired(squares, reach)
-            reach *= 2
-    squares = squares.reshape(2, seg)
+    squares = jnp.sum(wide * wide, axis=1).reshape(2, seg)
+    ending = [
+        lax.ppermute(
+            pick(squares, core ^ k, 0),
+            ("pair", "batch"),
+            [(4 * s + b, 2 * b + (s ^ k)) for s in range(2) for b in range(4)],
+        )
+        for k in range(2)
+    ]
 
     def row_scale(*earlier):
-        sent = [
-            lax.ppermute(
-                pick(after(squares, *earlier), core ^ k, 0),
-                ("pair", "batch"),
-                [(4 * s + b, 2 * b + (s ^ k)) for s in range(2) for b in range(4)],
-            )
-            for k in range(2)
-        ]
-        total = jnp.stack([jnp.where(x == 0, sent[0], sent[1]), jnp.where(x == 0, sent[1], sent[0])])
+        total = jnp.stack(
+            [jnp.where(x == 0, ending[0], ending[1]), jnp.where(x == 0, ending[1], ending[0])]
+        )
+        if vocab == 4:
+            total += sum(after(shifted(total, k), *earlier) for k in range(1, vocab))
+        else:
+            reach = 1
+            while reach < vocab:
+                total += paired(total, reach)
+                reach *= 2
         return lax.rsqrt(total / model + EPS) / SHRINK
 
     def by_y(mine, other, axis):
@@ -82,19 +83,25 @@
 
     def line_parts():
         mine = lax.dynamic_slice_in_dim(gained, x * block, block, 2)
+
+        def by_x(mine, other):
+            return jnp.stack([jnp.where(x == 0, mine, other), jnp.where(x == 0, other, mine)])
+
+        def up(value, k):
+            return lax.ppermute(value, "vocab", [(z, z + 1) for z in range(k - 1, vocab - 1)])
+
+        def down(value, k):
+            return lax.ppermute(value, "vocab", [(z + 1, z) for z in range(vocab - k)])
+
+        mine = after(mine, squares)
+        mine_up, mine_down = up(mine, 1), down(mine, 1)
         other = lax.ppermute(
             lax.dynamic_slice_in_dim(gained, (1 - x) * block, block, 2), "batch", X_SWAP
         )
-        own = jnp.stack([jnp.where(x == 0, mine, other), jnp.where(x == 0, other, mine)])
-        own = after(own, squares)
-
-        def up(value, k):
-            return lax.ppermute(value, "vocab", [(z, z + 1) for z in range(k - 1, vocab - 1)])
-
-        def down(value, k):
-            return lax.ppermute(value, "vocab", [(z + 1, z) for z in range(vocab - k)])
-
-        below, above = [own, up(own, 1)], [own, down(own, 1)]
+        other = after(other, mine_up, mine_down)
+        own = by_x(mine, other)
+        below = [own, by_x(mine_up, up(other, 1))]
+        above = [own, by_x(mine_down, down(other, 1))]
 
         def quarter(place, reach):
             part = own
@@ -104,8 +111,7 @@
             return part
 
         first = level // 2
-        scale = row_scale(own)
-        below[1], above[1] = after(below[1], scale), after(above[1], scale)
+        scale = row_scale(below[1], above[1])
         near_sent = quarter(1 - y + 2 * first, 1)
         got_near = lax.ppermute(near_sent, "batch", Y_SWAP)
         below.append(up(below[1], 2))
@@ -115,7 +121,7 @@
         near_weight, far_weight = lax.optimization_barrier(
             (jnp.where(keep_near, kept, taken), jnp.where(keep_near, taken, kept))
         )
-        ready = (got_near, near_weight, far_weight)
+        ready = (got_near, near_weight, far_weight, scale)
         below[2], above[2] = after(below[2], *ready), after(above[2], *ready)
         near = by_y(quarter(y + 2 * first, 1), after(got_near, below[2], above[2]), 0)
         swapped_near = swapped(near)
@@ -124,11 +130,11 @@
         pairs = [(b * vocab + z, (b ^ 2) * vocab + z) for b in range(4) for z in range(vocab)]
         lone = [b * vocab + (vocab - 1) * (b // 2) for b in range(4)]
         early = [pair for pair in pairs if pair[0] not in lone]
-        got_early = lax.ppermute(quarter(far, 2), ("batch", "vocab"), early)
+        far_sent = quarter(far, 2)
         mine_early = lax.optimization_barrier(quarter(y + 2 * (1 - first), 2))
         is_late = (level == 0) & (y == 1) | (level == vocab - 1) & (y == 0)
         near_part = dot(near, near_weight)
-        sent = after(own, below[2], above[2])
+        sent = after(own, below[2], above[2], far_sent, swapped_near)
         ends = []
         for cross in (0, 2):
             moves = []
@@ -136,6 +142,7 @@
                 b, z = divmod(place, vocab)
                 moves.append(((b ^ cross) * vocab + z, b * vocab + vocab - 1 - z))
             ends.append(lax.ppermute(sent, ("batch", "vocab"), sorted(moves)))
+        got_early = lax.ppermute(far_sent, ("batch", "vocab"), early)
         mine_late, got_late, got_early, _ = lax.optimization_barrier(
             (ends[0], ends[1], got_early, near_part)
         )

time: 119 us -> 133 us (1.12)
  starting transfers between devices: 45.2 us -> 59.9 us
  waiting for transfers between devices: 45.3 us -> 36.9 us
  other arithmetic: 15.7 us -> 21 us
  matrix products: 9.41 us -> 12 us
    ppermute x1, waiting for transfers between devices: 4.37 us -> 0.01 us  [line_parts(): got_near = lax.ppermute(near_sent, 'batch', Y_SWAP)]
    ppermute x2 -> x3, starting transfers between devices: 3.68 us -> 7.77 us  [up(): lax.ppermute(value, 'vocab', [(z, z + 1) for z in range(k - 1, vocab - 1)])]
    select_n x1, other arithmetic: 5.88 us -> 9.83 us  [line_parts(): jnp.where(keep_near, taken, kept)]
    ppermute x2, starting transfers between devices: 0.3 us -> 4.02 us  [on_device(): next_y = lax.ppermute(more_sends[i][0], 'batch', Y_SWAP)]
    ppermute x3, waiting for transfers between devices: 7.47 us -> 3.95 us  [the longest x1 2.65 us: line_parts(): got_early = lax.ppermute(far_sent, ('batch', 'vocab'), early)]
    dot_general x4, matrix products: 9.41 us -> 12 us  [dot(): jnp.dot(left.reshape(-1, block), weight, preferred_element_type=jnp.float32)]
    ppermute x2, waiting for transfers between devices: 1.9 us -> 4.31 us  [line_parts(): ends.append(lax.ppermute(sent, ('batch', 'vocab'), sorted(moves)))]
    ppermute x2, waiting for transfers between devices: 10.5 us -> 8.19 us  [on_device(): away_y = lax.ppermute(sends[i][1], 'batch', Y_SWAP)]
  transfers between devices with their start and end apart: 30 -> 32, of which waited for: 16 -> 14; matrix products, arithmetic and copies ran while one was open for 20% -> 23% of each run, Pallas kernels for 0% -> 0%
where the time goes in v16:
time: 133 us
  starting transfers between devices  59.9 us (45%)
  waiting for transfers between devices  36.9 us (28%)
  other arithmetic  21 us (16%)
  matrix products  12 us (9%)
  local copies, waits for them, and re-layouts  1.78 us (1%)
    dot_general x4, matrix products, dot(): jnp.dot(left.reshape(-1, block), weight, preferred_element_type=jnp.float32)  12 us
    ppermute x6, starting transfers between devices, shifted(): lax.ppermute(value, 'vocab', [(i, (i + k) % vocab) for i in range(vocab)])  10.8 us
    select_n x1, other arithmetic, line_parts(): jnp.where(keep_near, taken, kept)  9.83 us
    ppermute x2, waiting for transfers between devices, on_device(): next_x = lax.ppermute(more_sends[i][1], 'batch', X_SWAP)  8.24 us
    ppermute x2, waiting for transfers between devices, on_device(): away_y = lax.ppermute(sends[i][1], 'batch', Y_SWAP)  8.19 us
    ppermute x3, starting transfers between devices, up(): lax.ppermute(value, 'vocab', [(z, z + 1) for z in range(k - 1, vocab - 1)])  7.77 us
    ppermute x2, starting transfers between devices, line_parts(): ends.append(lax.ppermute(sent, ('batch', 'vocab'), sorted(moves)))  7.39 us
    ppermute x2, starting transfers between devices, on_device(): lax.ppermute(pick(squares, core ^ k, 0), ('pair', 'batch'), [(4 * s + b,...  6.96 us
  transfers between devices with their start and end apart: 32, of which 14 were waited for; matrix products, arithmetic and copies ran while one was open for 23% of the time, Pallas kernels for 0%

profile of v16, /device:TPU:0, one launch (start us, length us, event | category | flops | bytes accessed | tf_op | source)
XLA Modules:
  0.0 132.7 jit_solution(16205087600272737018)
XLA Ops:
  5.6 5.2 %collective-permute-start.2 = (bf16[2,64,1024]{2,1,0:T(8,128)(2,1)S(1)}, bf16[2,64,1024]{2,1,0:T(8,128)(2,1)S(1)}, u32[]{:S(2)}, u32[]{:S(2)}) collective-permute-start(bf16[2,64,1024]{2,1,0:T(8,128)(2,1)S(1)} %get-tuple-element.22), channel_id=1, source_target_pairs={{0,1},{1,2},{2,3},{4,5},{5,6},{6,7},{8,9},{9,10},{10,11},{12,13},{... | collective-permute-start | bytes 786440 | tf_op jit(solution)/shard_map/ppermute | solution.py:91
  10.8 2.0 %collective-permute-start.1 = (bf16[2,64,1024]{2,1,0:T(8,128)(2,1)S(1)}, bf16[2,64,1024]{2,1,0:T(8,128)(2,1)S(1)}, u32[]{:S(2)}, u32[]{:S(2)}) collective-permute-start(bf16[2,64,1024]{2,1,0:T(8,128)(2,1)S(1)} %get-tuple-element.75), channel_id=1, source_target_pairs={{0,4},{4,0},{8,12},{12,8},{1,5},{5,1},{9,13},{13,9},{2,6},{6,2},{1... | collective-permute-start | bytes 786440 | tf_op jit(solution)/shard_map/ppermute | solution.py:98
  13.5 6.3 %collective-permute-start.9 = (f32[64]{0:T(128)S(1)}, f32[64]{0:T(128)S(1)}, u32[]{:S(2)}, u32[]{:S(2)}) collective-permute-start(f32[64]{0:T(128)S(1)} %get-tuple-element.85), channel_id=1, source_target_pairs={{0,4},{4,12},{8,20},{12,28},{16,0},{20,8},{24,16},{28,24},{1,5},{5... | collective-permute-start | bytes 776 | tf_op jit(solution)/shard_map/ppermute | solution.py:51
  22.5 3.7 %collective-permute-start.11 = (f32[2,64]{1,0:T(2,128)S(1)}, f32[2,64]{1,0:T(2,128)S(1)}, u32[]{:S(2)}, u32[]{:S(2)}) collective-permute-start(f32[2,64]{1,0:T(2,128)S(1)} %pad_maximum_fusion.8), channel_id=1, source_target_pairs={{0,2},{1,3},{2,0},{3,1},{4,6},{5,7},{6,4},{7,5},{8,10},{9,11},{10,... | collective-permute-start | bytes 1544 | tf_op jit(solution)/shard_map/ppermute | solution.py:44
  26.2 1.6 %collective-permute-start.10 = (f32[2,64]{1,0:T(2,128)S(1)}, f32[2,64]{1,0:T(2,128)S(1)}, u32[]{:S(2)}, u32[]{:S(2)}) collective-permute-start(f32[2,64]{1,0:T(2,128)S(1)} %pad_maximum_fusion.8), channel_id=1, source_target_pairs={{0,1},{1,2},{2,3},{3,0},{4,5},{5,6},{6,7},{7,4},{8,9},{9,10},{10,1... | collective-permute-start | bytes 1544 | tf_op jit(solution)/shard_map/ppermute | solution.py:44
  27.8 1.9 %collective-permute-start.4 = (bf16[2,64,1024]{2,1,0:T(8,128)(2,1)S(1)}, bf16[2,64,1024]{2,1,0:T(8,128)(2,1)S(1)}, u32[]{:S(2)}, u32[]{:S(2)}) collective-permute-start(bf16[2,64,1024]{2,1,0:T(8,128)(2,1)S(1)} %collective-permute-done.1), channel_id=1, source_target_pairs={{0,1},{1,2},{2,3},{4,5},{5,6},{6,7},{8,9},{9,10},{10,11},{12,13},{... | collective-permute-start | bytes 786440 | tf_op jit(solution)/shard_map/ppermute | solution.py:91
  29.8 2.1 %collective-permute-done.3 = bf16[2,64,1024]{2,1,0:T(8,128)(2,1)S(1)} collective-permute-done((bf16[2,64,1024]{2,1,0:T(8,128)(2,1)S(1)}, bf16[2,64,1024]{2,1,0:T(8,128)(2,1)S(1)}, u32[]{:S(2)}, u32[]{:S(2)}) %collective-permute-start.3) | collective-permute-done | bytes 262176 | tf_op jit(solution)/shard_map/ppermute | solution.py:94
  31.8 1.6 %collective-permute-start.12 = (f32[2,64]{1,0:T(2,128)S(1)}, f32[2,64]{1,0:T(2,128)S(1)}, u32[]{:S(2)}, u32[]{:S(2)}) collective-permute-start(f32[2,64]{1,0:T(2,128)S(1)} %pad_maximum_fusion.8), channel_id=1, source_target_pairs={{0,3},{1,0},{2,1},{3,2},{4,7},{5,4},{6,5},{7,6},{8,11},{9,8},{10,9... | collective-permute-start | bytes 1544 | tf_op jit(solution)/shard_map/ppermute | solution.py:44
  33.5 1.9 %collective-permute-done.4 = bf16[2,64,1024]{2,1,0:T(8,128)(2,1)S(1)} collective-permute-done((bf16[2,64,1024]{2,1,0:T(8,128)(2,1)S(1)}, bf16[2,64,1024]{2,1,0:T(8,128)(2,1)S(1)}, u32[]{:S(2)}, u32[]{:S(2)}) %collective-permute-start.4) | collective-permute-done | bytes 262176 | tf_op jit(solution)/shard_map/ppermute | solution.py:91
  38.7 1.8 %collective-permute-start.5 = (bf16[2,2,64,1024]{3,2,1,0:T(8,128)(2,1)}, bf16[2,2,64,1024]{3,2,1,0:T(8,128)(2,1)S(1)}, u32[]{:S(2)}, u32[]{:S(2)}) collective-permute-start(bf16[2,2,64,1024]{3,2,1,0:T(8,128)(2,1)} %get-tuple-element.65), channel_id=1, source_target_pairs={{0,8},{8,0},{4,12},{12,4},{1,9},{9,1},{5,13},{13,5},{2,10},{10,2},... | collective-permute-start | bytes 1572872 | tf_op jit(solution)/shard_map/ppermute | solution.py:116
  40.6 9.8 %broadcast_select_fusion = (bf16[1024,2048]{1,0:T(8,128)(2,1)}, bf16[1024,2048]{1,0:T(8,128)(2,1)}) fusion(pred[]{:T(512)S(6)} %eq.80, bf16[1024,4096]{1,0:T(8,128)(2,1)} %collective-permute-done.7, s32[]{:T(128)S(6)} %select_n.262, bf16[1024,4096]{1,0:T(8,128)(2,1)} %param.5), kind=kLoop, calls=%fused_computation.2 | loop fusion | flops 4194304 | bytes 16777220 | tf_op jit(solution)/shard_map/jit(_where)/select_n | solution.py:122
  50.4 2.1 %collective-permute-done.13 = bf16[2,2,64,1024]{3,2,1,0:T(8,128)(2,1)S(1)} collective-permute-done((bf16[2,2,64,1024]{3,2,1,0:T(8,128)(2,1)}, bf16[2,2,64,1024]{3,2,1,0:T(8,128)(2,1)S(1)}, u32[]{:S(2)}, u32[]{:S(2)}) %collective-permute-start.13) | collective-permute-done | bytes 524320 | tf_op jit(solution)/shard_map/ppermute | solution.py:94
  56.8 6.5 %collective-permute-start.15 = (bf16[2,2,64,1024]{3,2,1,0:T(8,128)(2,1)S(1)}, bf16[2,2,64,1024]{3,2,1,0:T(8,128)(2,1)S(1)}, u32[]{:S(2)}, u32[]{:S(2)}) collective-permute-start(bf16[2,2,64,1024]{3,2,1,0:T(8,128)(2,1)S(1)} %get-tuple-element.33), channel_id=1, source_target_pairs={{0,3},{4,7},{11,8},{15,12},{16,19},{20,23},{27,24},{31,28}} | collective-permute-start | bytes 1572872 | tf_op jit(solution)/shard_map/ppermute | solution.py:144
  64.2 3.6 %fusion.33 = f32[512,2048]{1,0:T(8,128)S(1)} fusion(bf16[512,1024]{1,0:T(8,128)(2,1)} %bitcast.13, bf16[1024,2048]{1,0:T(8,128)(2,1)S(1)} %copy-done), kind=kOutput, calls=%fused_computation.115 | convolution fusion | flops 2147483648 | bytes 9437184 | tf_op jit(solution)/shard_map/dot_general | solution.py:82
  67.8 2.7 %collective-permute-done.17 = bf16[2,2,64,1024]{3,2,1,0:T(8,128)(2,1)S(1)} collective-permute-done((bf16[2,2,64,1024]{3,2,1,0:T(8,128)(2,1)S(1)}, bf16[2,2,64,1024]{3,2,1,0:T(8,128)(2,1)S(1)}, u32[]{:S(2)}, u32[]{:S(2)}) %collective-permute-start.17) | collective-permute-done | bytes 524320 | tf_op jit(solution)/shard_map/ppermute | solution.py:145
  70.5 4.3 %collective-permute-done.15 = bf16[2,2,64,1024]{3,2,1,0:T(8,128)(2,1)S(1)} collective-permute-done((bf16[2,2,64,1024]{3,2,1,0:T(8,128)(2,1)S(1)}, bf16[2,2,64,1024]{3,2,1,0:T(8,128)(2,1)S(1)}, u32[]{:S(2)}, u32[]{:S(2)}) %collective-permute-start.15) | collective-permute-done | bytes 524320 | tf_op jit(solution)/shard_map/ppermute | solution.py:144
  75.1 2.4 %add_multiply_fusion.1 = f32[512,2048]{1,0:T(8,128)S(1)} fusion(f32[512,2048]{1,0:T(8,128)S(1)} %fusion.33, bf16[512,1024]{1,0:T(8,128)(2,1)S(1)} %bitcast.124, bf16[1024,2048]{1,0:T(8,128)(2,1)S(1)} %copy-done.1), kind=kOutput, calls=%fused_computation.1 | convolution fusion | flops 2149580800 | bytes 13631488 | tf_op jit(solution)/shard_map/dot_general | solution.py:82
  78.2 3.6 %collective-permute-start.23 = (f16[2,2,64,1024]{3,2,1,0:T(8,128)(2,1)S(1)}, f16[2,2,64,1024]{3,2,1,0:T(8,128)(2,1)S(1)}, u32[]{:S(2)}, u32[]{:S(2)}) collective-permute-start(f16[2,2,64,1024]{3,2,1,0:T(8,128)(2,1)S(1)} %fusion.4), channel_id=1, source_target_pairs={{0,8},{8,0},{4,12},{12,4},{1,9},{9,1},{5,13},{13,5},{2,10},{10,2},... | collective-permute-start | bytes 1572872 | tf_op jit(solution)/shard_map/ppermute | solution.py:189
  82.1 3.5 %collective-permute-start.18 = (f16[2,2,64,1024]{3,2,0,1:T(8,128)(2,1)S(1)}, f16[2,2,64,1024]{3,2,0,1:T(8,128)(2,1)S(1)}, u32[]{:S(2)}, u32[]{:S(2)}) collective-permute-start(f16[2,2,64,1024]{3,2,0,1:T(8,128)(2,1)S(1)} %fusion.6), channel_id=1, source_target_pairs={{0,4},{4,0},{8,12},{12,8},{1,5},{5,1},{9,13},{13,9},{2,6},{6,2},{1... | collective-permute-start | bytes 1572872 | tf_op jit(solution)/shard_map/ppermute | solution.py:188
  85.6 2.4 %fusion.34 = f32[512,2048]{1,0:T(8,128)S(1)} fusion(bf16[512,1024]{1,0:T(8,128)(2,1)S(1)} %bitcast.132, bf16[1024,2048]{1,0:T(8,128)(2,1)S(1)} %copy-done.1), kind=kOutput, calls=%fused_computation.116 | convolution fusion | flops 2147483648 | bytes 9437184 | tf_op jit(solution)/shard_map/dot_general | solution.py:82
  87.9 3.6 %add_multiply_fusion = f32[512,2048]{1,0:T(8,128)S(1)} fusion(f32[512,2048]{1,0:T(8,128)S(1)} %fusion.34, bf16[512,1024]{1,0:T(8,128)(2,1)} %bitcast.20, bf16[1024,2048]{1,0:T(8,128)(2,1)S(1)} %copy-done), kind=kOutput, calls=%fused_computation | convolution fusion | flops 2149580800 | bytes 13631488 | tf_op jit(solution)/shard_map/dot_general | solution.py:82
  92.8 1.6 %collective-permute-done.23 = f16[2,2,64,1024]{3,2,1,0:T(8,128)(2,1)S(1)} collective-permute-done((f16[2,2,64,1024]{3,2,1,0:T(8,128)(2,1)S(1)}, f16[2,2,64,1024]{3,2,1,0:T(8,128)(2,1)S(1)}, u32[]{:S(2)}, u32[]{:S(2)}) %collective-permute-start.23) | collective-permute-done | bytes 524320 | tf_op jit(solution)/shard_map/ppermute | solution.py:189
  94.6 3.7 %collective-permute-start.24 = (f16[2,64,1024]{2,1,0:T(8,128)(2,1)S(1)}, f16[2,64,1024]{2,1,0:T(8,128)(2,1)S(1)}, u32[]{:S(2)}, u32[]{:S(2)}) collective-permute-start(f16[2,64,1024]{2,1,0:T(8,128)(2,1)S(1)} %fusion.15), channel_id=1, source_target_pairs={{0,4},{4,0},{8,12},{12,8},{1,5},{5,1},{9,13},{13,9},{2,6},{6,2},{1... | collective-permute-start | bytes 786440 | tf_op jit(solution)/shard_map/ppermute | solution.py:201
  98.5 2.0 %collective-permute-start.20 = (f16[2,64,1024]{2,1,0:T(8,128)(2,1)S(1)}, f16[2,64,1024]{2,1,0:T(8,128)(2,1)S(1)}, u32[]{:S(2)}, u32[]{:S(2)}) collective-permute-start(f16[2,64,1024]{2,1,0:T(8,128)(2,1)S(1)} %fusion.12), channel_id=1, source_target_pairs={{0,8},{8,0},{4,12},{12,4},{1,9},{9,1},{5,13},{13,5},{2,10},{10,2},... | collective-permute-start | bytes 786440 | tf_op jit(solution)/shard_map/ppermute | solution.py:200
  100.5 6.6 %collective-permute-done.22 = f16[2,2,64,1024]{3,2,1,0:T(8,128)(2,1)S(1)} collective-permute-done((f16[2,2,64,1024]{3,2,1,0:T(8,128)(2,1)S(1)}, f16[2,2,64,1024]{3,2,1,0:T(8,128)(2,1)S(1)}, u32[]{:S(2)}, u32[]{:S(2)}) %collective-permute-start.22) | collective-permute-done | bytes 524320 | tf_op jit(solution)/shard_map/ppermute | solution.py:189
  107.4 2.1 %collective-permute-start.27 = (f16[2,64,1024]{2,1,0:T(8,128)(2,1)S(1)}, f16[2,64,1024]{2,1,0:T(8,128)(2,1)S(1)}, u32[]{:S(2)}, u32[]{:S(2)}) collective-permute-start(f16[2,64,1024]{2,1,0:T(8,128)(2,1)S(1)} %fusion.14), channel_id=1, source_target_pairs={{0,4},{4,0},{8,12},{12,8},{1,5},{5,1},{9,13},{13,9},{2,6},{6,2},{1... | collective-permute-start | bytes 786440 | tf_op jit(solution)/shard_map/ppermute | solution.py:201
  109.8 2.0 %collective-permute-start.26 = (f16[2,64,1024]{2,1,0:T(8,128)(2,1)S(1)}, f16[2,64,1024]{2,1,0:T(8,128)(2,1)S(1)}, u32[]{:S(2)}, u32[]{:S(2)}) collective-permute-start(f16[2,64,1024]{2,1,0:T(8,128)(2,1)S(1)} %fusion.13), channel_id=1, source_target_pairs={{0,8},{8,0},{4,12},{12,4},{1,9},{9,1},{5,13},{13,5},{2,10},{10,2},... | collective-permute-start | bytes 786440 | tf_op jit(solution)/shard_map/ppermute | solution.py:200
  111.8 3.4 %collective-permute-done.24 = f16[2,64,1024]{2,1,0:T(8,128)(2,1)S(1)} collective-permute-done((f16[2,64,1024]{2,1,0:T(8,128)(2,1)S(1)}, f16[2,64,1024]{2,1,0:T(8,128)(2,1)S(1)}, u32[]{:S(2)}, u32[]{:S(2)}) %collective-permute-start.24) | collective-permute-done | bytes 262176 | tf_op jit(solution)/shard_map/ppermute | solution.py:201
  115.5 4.9 %collective-permute-done.27 = f16[2,64,1024]{2,1,0:T(8,128)(2,1)S(1)} collective-permute-done((f16[2,64,1024]{2,1,0:T(8,128)(2,1)S(1)}, f16[2,64,1024]{2,1,0:T(8,128)(2,1)S(1)}, u32[]{:S(2)}, u32[]{:S(2)}) %collective-permute-start.27) | collective-permute-done | bytes 262176 | tf_op jit(solution)/shard_map/ppermute | solution.py:201
  123.6 3.8 %collective-permute-start.30 = (f32[4,64]{1,0:T(4,128)S(1)}, f32[4,64]{1,0:T(4,128)S(1)}, u32[]{:S(2)}, u32[]{:S(2)}) collective-permute-start(f32[4,64]{1,0:T(4,128)S(1)} %get-tuple-element.77), channel_id=1, source_target_pairs={{0,2},{1,3},{2,0},{3,1},{4,6},{5,7},{6,4},{7,5},{8,10},{9,11},{10,... | collective-permute-start | bytes 3080 | tf_op jit(solution)/shard_map/ppermute | solution.py:44
  129.0 2.0 %collective-permute-done.31 = f32[4,64]{1,0:T(4,128)S(1)} collective-permute-done((f32[4,64]{1,0:T(4,128)S(1)}, f32[4,64]{1,0:T(4,128)S(1)}, u32[]{:S(2)}, u32[]{:S(2)}) %collective-permute-start.31) | collective-permute-done | bytes 1056 | tf_op jit(solution)/shard_map/ppermute | solution.py:44
  131.1 1.6 %fusion.2 = (f32[64,4096]{1,0:T(8,128)}, f32[64,4096]{1,0:T(8,128)}) fusion(f32[64]{0:T(128)S(1)} %get-tuple-element.78, f32[64]{0:T(128)S(1)} %get-tuple-element.80, f16[64,2048]{1,0:T(8,128)(2,1)S(1)} %get-tuple-element.60, f16[64,2048]{1,0:T(8,128)(2,1)S(1)} %get-tuple-element.58, f32[64,4096]{1,0:T(8,128)S(1)} %get-tuple-element.43, ...), kind=kLoop, calls=%fused_computation.18 | loop fusion | flops 1310720 | bytes 3670784 | tf_op jit(solution)/shard_map/sub | solution.py:239
  (96 shorter events, 25.3 us)
Async XLA Ops:
  0.6 39.9 %collective-permute-start.7 = (bf16[1024,4096]{1,0:T(8,128)(2,1)}, bf16[1024,4096]{1,0:T(8,128)(2,1)}, u32[]{:S(2)}, u32[]{:S(2)}) collective-permute-start(bf16[1024,4096]{1,0:T(8,128)(2,1)} %param.5), channel_id=1, source_target_pairs={{0,16},{16,0},{1,17},{17,1},{2,18},{18,2},{3,19},{19,3},{4,20},{20... | collective-permute-start | bytes 25165832 | tf_op jit(solution)/shard_map/ppermute | solution.py:41
  4.3 16.8 %collective-permute-start = (bf16[2,64,1024]{2,1,0:T(8,128)(2,1)S(1)}, bf16[2,64,1024]{2,1,0:T(8,128)(2,1)S(1)}, u32[]{:S(2)}, u32[]{:S(2)}) collective-permute-start(bf16[2,64,1024]{2,1,0:T(8,128)(2,1)S(1)} %get-tuple-element.22), channel_id=1, source_target_pairs={{1,0},{2,1},{3,2},{5,4},{6,5},{7,6},{9,8},{10,9},{11,10},{13,12},{... | collective-permute-start | bytes 786440 | tf_op jit(solution)/shard_map/ppermute | solution.py:94
  5.6 15.5 %collective-permute-start.2 = (bf16[2,64,1024]{2,1,0:T(8,128)(2,1)S(1)}, bf16[2,64,1024]{2,1,0:T(8,128)(2,1)S(1)}, u32[]{:S(2)}, u32[]{:S(2)}) collective-permute-start(bf16[2,64,1024]{2,1,0:T(8,128)(2,1)S(1)} %get-tuple-element.22), channel_id=1, source_target_pairs={{0,1},{1,2},{2,3},{4,5},{5,6},{6,7},{8,9},{9,10},{10,11},{12,13},{... | collective-permute-start | bytes 786440 | tf_op jit(solution)/shard_map/ppermute | solution.py:91
  10.8 10.3 %collective-permute-start.1 = (bf16[2,64,1024]{2,1,0:T(8,128)(2,1)S(1)}, bf16[2,64,1024]{2,1,0:T(8,128)(2,1)S(1)}, u32[]{:S(2)}, u32[]{:S(2)}) collective-permute-start(bf16[2,64,1024]{2,1,0:T(8,128)(2,1)S(1)} %get-tuple-element.75), channel_id=1, source_target_pairs={{0,4},{4,0},{8,12},{12,8},{1,5},{5,1},{9,13},{13,9},{2,6},{6,2},{1... | collective-permute-start | bytes 786440 | tf_op jit(solution)/shard_map/ppermute | solution.py:98
  12.8 0.7 collective-permute-start.8
  13.5 7.6 %collective-permute-start.9 = (f32[64]{0:T(128)S(1)}, f32[64]{0:T(128)S(1)}, u32[]{:S(2)}, u32[]{:S(2)}) collective-permute-start(f32[64]{0:T(128)S(1)} %get-tuple-element.85), channel_id=1, source_target_pairs={{0,4},{4,12},{8,20},{12,28},{16,0},{20,8},{24,16},{28,24},{1,5},{5... | collective-permute-start | bytes 776 | tf_op jit(solution)/shard_map/ppermute | solution.py:51
  21.2 10.7 %collective-permute-start.3 = (bf16[2,64,1024]{2,1,0:T(8,128)(2,1)S(1)}, bf16[2,64,1024]{2,1,0:T(8,128)(2,1)S(1)}, u32[]{:S(2)}, u32[]{:S(2)}) collective-permute-start(bf16[2,64,1024]{2,1,0:T(8,128)(2,1)S(1)} %collective-permute-done.1), channel_id=1, source_target_pairs={{1,0},{2,1},{3,2},{5,4},{6,5},{7,6},{9,8},{10,9},{11,10},{13,12},{... | collective-permute-start | bytes 786440 | tf_op jit(solution)/shard_map/ppermute | solution.py:94
  22.5 15.5 %collective-permute-start.11 = (f32[2,64]{1,0:T(2,128)S(1)}, f32[2,64]{1,0:T(2,128)S(1)}, u32[]{:S(2)}, u32[]{:S(2)}) collective-permute-start(f32[2,64]{1,0:T(2,128)S(1)} %pad_maximum_fusion.8), channel_id=1, source_target_pairs={{0,2},{1,3},{2,0},{3,1},{4,6},{5,7},{6,4},{7,5},{8,10},{9,11},{10,... | collective-permute-start | bytes 1544 | tf_op jit(solution)/shard_map/ppermute | solution.py:44
  26.2 12.5 %collective-permute-start.10 = (f32[2,64]{1,0:T(2,128)S(1)}, f32[2,64]{1,0:T(2,128)S(1)}, u32[]{:S(2)}, u32[]{:S(2)}) collective-permute-start(f32[2,64]{1,0:T(2,128)S(1)} %pad_maximum_fusion.8), channel_id=1, source_target_pairs={{0,1},{1,2},{2,3},{3,0},{4,5},{5,6},{6,7},{7,4},{8,9},{9,10},{10,1... | collective-permute-start | bytes 1544 | tf_op jit(solution)/shard_map/ppermute | solution.py:44
  27.8 7.6 %collective-permute-start.4 = (bf16[2,64,1024]{2,1,0:T(8,128)(2,1)S(1)}, bf16[2,64,1024]{2,1,0:T(8,128)(2,1)S(1)}, u32[]{:S(2)}, u32[]{:S(2)}) collective-permute-start(bf16[2,64,1024]{2,1,0:T(8,128)(2,1)S(1)} %collective-permute-done.1), channel_id=1, source_target_pairs={{0,1},{1,2},{2,3},{4,5},{5,6},{6,7},{8,9},{9,10},{10,11},{12,13},{... | collective-permute-start | bytes 786440 | tf_op jit(solution)/shard_map/ppermute | solution.py:91
  31.8 8.7 %collective-permute-start.12 = (f32[2,64]{1,0:T(2,128)S(1)}, f32[2,64]{1,0:T(2,128)S(1)}, u32[]{:S(2)}, u32[]{:S(2)}) collective-permute-start(f32[2,64]{1,0:T(2,128)S(1)} %pad_maximum_fusion.8), channel_id=1, source_target_pairs={{0,3},{1,0},{2,1},{3,2},{4,7},{5,4},{6,5},{7,6},{8,11},{9,8},{10,9... | collective-permute-start | bytes 1544 | tf_op jit(solution)/shard_map/ppermute | solution.py:44
  36.7 15.8 %collective-permute-start.13 = (bf16[2,2,64,1024]{3,2,1,0:T(8,128)(2,1)}, bf16[2,2,64,1024]{3,2,1,0:T(8,128)(2,1)S(1)}, u32[]{:S(2)}, u32[]{:S(2)}) collective-permute-start(bf16[2,2,64,1024]{3,2,1,0:T(8,128)(2,1)} %get-tuple-element.66), channel_id=1, source_target_pairs={{1,0},{2,1},{5,4},{6,5},{9,8},{10,9},{13,12},{14,13},{17,16},{18,1... | collective-permute-start | bytes 1572872 | tf_op jit(solution)/shard_map/ppermute | solution.py:94
  38.0 14.5 %collective-permute-start.6 = (bf16[2,2,64,1024]{3,2,1,0:T(8,128)(2,1)}, bf16[2,2,64,1024]{3,2,1,0:T(8,128)(2,1)S(1)}, u32[]{:S(2)}, u32[]{:S(2)}) collective-permute-start(bf16[2,2,64,1024]{3,2,1,0:T(8,128)(2,1)} %get-tuple-element.67), channel_id=1, source_target_pairs={{1,2},{2,3},{5,6},{6,7},{9,10},{10,11},{13,14},{14,15},{17,18},{18... | collective-permute-start | bytes 1572872 | tf_op jit(solution)/shard_map/ppermute | solution.py:91
  38.7 13.8 %collective-permute-start.5 = (bf16[2,2,64,1024]{3,2,1,0:T(8,128)(2,1)}, bf16[2,2,64,1024]{3,2,1,0:T(8,128)(2,1)S(1)}, u32[]{:S(2)}, u32[]{:S(2)}) collective-permute-start(bf16[2,2,64,1024]{3,2,1,0:T(8,128)(2,1)} %get-tuple-element.65), channel_id=1, source_target_pairs={{0,8},{8,0},{4,12},{12,4},{1,9},{9,1},{5,13},{13,5},{2,10},{10,2},... | collective-permute-start | bytes 1572872 | tf_op jit(solution)/shard_map/ppermute | solution.py:116
  53.8 3.0 %collective-permute-start.14 = (bf16[2,2,2,64,1024]{4,3,2,1,0:T(8,128)(2,1)}, bf16[2,2,2,64,1024]{4,3,2,1,0:T(8,128)(2,1)}, u32[]{:S(2)}, u32[]{:S(2)}) collective-permute-start(bf16[2,2,2,64,1024]{4,3,2,1,0:T(8,128)(2,1)} %pad_maximum_fusion), channel_id=1, source_target_pairs={{0,16},{16,0},{1,17},{17,1},{2,18},{18,2},{3,19},{19,3},{4,20},{20... | collective-permute-start | bytes 3145736 | tf_op jit(solution)/shard_map/ppermute | solution.py:76
  54.0 16.5 %collective-permute-start.17 = (bf16[2,2,64,1024]{3,2,1,0:T(8,128)(2,1)S(1)}, bf16[2,2,64,1024]{3,2,1,0:T(8,128)(2,1)S(1)}, u32[]{:S(2)}, u32[]{:S(2)}) collective-permute-start(bf16[2,2,64,1024]{3,2,1,0:T(8,128)(2,1)S(1)} %select_select_fusion.1), channel_id=1, source_target_pairs={{1,9},{2,10},{3,11},{5,13},{6,14},{7,15},{8,0},{9,1},{10,2},{12,4}... | collective-permute-start | bytes 1572872 | tf_op jit(solution)/shard_map/ppermute | solution.py:145
  56.8 18.0 %collective-permute-start.15 = (bf16[2,2,64,1024]{3,2,1,0:T(8,128)(2,1)S(1)}, bf16[2,2,64,1024]{3,2,1,0:T(8,128)(2,1)S(1)}, u32[]{:S(2)}, u32[]{:S(2)}) collective-permute-start(bf16[2,2,64,1024]{3,2,1,0:T(8,128)(2,1)S(1)} %get-tuple-element.33), channel_id=1, source_target_pairs={{0,3},{4,7},{11,8},{15,12},{16,19},{20,23},{27,24},{31,28}} | collective-permute-start | bytes 1572872 | tf_op jit(solution)/shard_map/ppermute | solution.py:144
  63.3 11.4 %collective-permute-start.16 = (bf16[2,2,64,1024]{3,2,1,0:T(8,128)(2,1)S(1)}, bf16[2,2,64,1024]{3,2,1,0:T(8,128)(2,1)S(1)}, u32[]{:S(2)}, u32[]{:S(2)}) collective-permute-start(bf16[2,2,64,1024]{3,2,1,0:T(8,128)(2,1)S(1)} %get-tuple-element.33), channel_id=1, source_target_pairs={{3,8},{7,12},{8,3},{12,7},{19,24},{23,28},{24,19},{28,23}} | collective-permute-start | bytes 1572872 | tf_op jit(solution)/shard_map/ppermute | solution.py:144
  75.0 10.6 %collective-permute-start.19 = (bf16[2,2,2,64,1024]{4,3,2,1,0:T(8,128)(2,1)S(1)}, bf16[2,2,2,64,1024]{4,3,2,1,0:T(8,128)(2,1)S(1)}, u32[]{:S(2)}, u32[]{:S(2)}) collective-permute-start(bf16[2,2,2,64,1024]{4,3,2,1,0:T(8,128)(2,1)S(1)} %pad_maximum_fusion.1), channel_id=1, source_target_pairs={{0,16},{16,0},{1,17},{17,1},{2,18},{18,2},{3,19},{19,3},{4,20},{20... | collective-permute-start | bytes 3145736 | tf_op jit(solution)/shard_map/ppermute | solution.py:76
  78.2 16.2 %collective-permute-start.23 = (f16[2,2,64,1024]{3,2,1,0:T(8,128)(2,1)S(1)}, f16[2,2,64,1024]{3,2,1,0:T(8,128)(2,1)S(1)}, u32[]{:S(2)}, u32[]{:S(2)}) collective-permute-start(f16[2,2,64,1024]{3,2,1,0:T(8,128)(2,1)S(1)} %fusion.4), channel_id=1, source_target_pairs={{0,8},{8,0},{4,12},{12,4},{1,9},{9,1},{5,13},{13,5},{2,10},{10,2},... | collective-permute-start | bytes 1572872 | tf_op jit(solution)/shard_map/ppermute | solution.py:189
  82.1 16.2 %collective-permute-start.18 = (f16[2,2,64,1024]{3,2,0,1:T(8,128)(2,1)S(1)}, f16[2,2,64,1024]{3,2,0,1:T(8,128)(2,1)S(1)}, u32[]{:S(2)}, u32[]{:S(2)}) collective-permute-start(f16[2,2,64,1024]{3,2,0,1:T(8,128)(2,1)S(1)} %fusion.6), channel_id=1, source_target_pairs={{0,4},{4,0},{8,12},{12,8},{1,5},{5,1},{9,13},{13,9},{2,6},{6,2},{1... | collective-permute-start | bytes 1572872 | tf_op jit(solution)/shard_map/ppermute | solution.py:188
  92.2 14.9 %collective-permute-start.22 = (f16[2,2,64,1024]{3,2,1,0:T(8,128)(2,1)S(1)}, f16[2,2,64,1024]{3,2,1,0:T(8,128)(2,1)S(1)}, u32[]{:S(2)}, u32[]{:S(2)}) collective-permute-start(f16[2,2,64,1024]{3,2,1,0:T(8,128)(2,1)S(1)} %fusion.5), channel_id=1, source_target_pairs={{0,8},{8,0},{4,12},{12,4},{1,9},{9,1},{5,13},{13,5},{2,10},{10,2},... | collective-permute-start | bytes 1572872 | tf_op jit(solution)/shard_map/ppermute | solution.py:189
  92.7 16.9 %collective-permute-start.21 = (f16[2,2,64,1024]{3,2,0,1:T(8,128)(2,1)S(1)}, f16[2,2,64,1024]{3,2,0,1:T(8,128)(2,1)S(1)}, u32[]{:S(2)}, u32[]{:S(2)}) collective-permute-start(f16[2,2,64,1024]{3,2,0,1:T(8,128)(2,1)S(1)} %fusion.7), channel_id=1, source_target_pairs={{0,4},{4,0},{8,12},{12,8},{1,5},{5,1},{9,13},{13,9},{2,6},{6,2},{1... | collective-permute-start | bytes 1572872 | tf_op jit(solution)/shard_map/ppermute | solution.py:188
  94.6 20.5 %collective-permute-start.24 = (f16[2,64,1024]{2,1,0:T(8,128)(2,1)S(1)}, f16[2,64,1024]{2,1,0:T(8,128)(2,1)S(1)}, u32[]{:S(2)}, u32[]{:S(2)}) collective-permute-start(f16[2,64,1024]{2,1,0:T(8,128)(2,1)S(1)} %fusion.15), channel_id=1, source_target_pairs={{0,4},{4,0},{8,12},{12,8},{1,5},{5,1},{9,13},{13,9},{2,6},{6,2},{1... | collective-permute-start | bytes 786440 | tf_op jit(solution)/shard_map/ppermute | solution.py:201
  98.5 16.7 %collective-permute-start.20 = (f16[2,64,1024]{2,1,0:T(8,128)(2,1)S(1)}, f16[2,64,1024]{2,1,0:T(8,128)(2,1)S(1)}, u32[]{:S(2)}, u32[]{:S(2)}) collective-permute-start(f16[2,64,1024]{2,1,0:T(8,128)(2,1)S(1)} %fusion.12), channel_id=1, source_target_pairs={{0,8},{8,0},{4,12},{12,4},{1,9},{9,1},{5,13},{13,5},{2,10},{10,2},... | collective-permute-start | bytes 786440 | tf_op jit(solution)/shard_map/ppermute | solution.py:200
  107.4 13.0 %collective-permute-start.27 = (f16[2,64,1024]{2,1,0:T(8,128)(2,1)S(1)}, f16[2,64,1024]{2,1,0:T(8,128)(2,1)S(1)}, u32[]{:S(2)}, u32[]{:S(2)}) collective-permute-start(f16[2,64,1024]{2,1,0:T(8,128)(2,1)S(1)} %fusion.14), channel_id=1, source_target_pairs={{0,4},{4,0},{8,12},{12,8},{1,5},{5,1},{9,13},{13,9},{2,6},{6,2},{1... | collective-permute-start | bytes 786440 | tf_op jit(solution)/shard_map/ppermute | solution.py:201
  109.8 10.7 %collective-permute-start.26 = (f16[2,64,1024]{2,1,0:T(8,128)(2,1)S(1)}, f16[2,64,1024]{2,1,0:T(8,128)(2,1)S(1)}, u32[]{:S(2)}, u32[]{:S(2)}) collective-permute-start(f16[2,64,1024]{2,1,0:T(8,128)(2,1)S(1)} %fusion.13), channel_id=1, source_target_pairs={{0,8},{8,0},{4,12},{12,4},{1,9},{9,1},{5,13},{13,5},{2,10},{10,2},... | collective-permute-start | bytes 786440 | tf_op jit(solution)/shard_map/ppermute | solution.py:200
  115.4 5.3 %collective-permute-start.25 = (f16[64,2048]{1,0:T(8,128)(2,1)S(1)}, f16[64,2048]{1,0:T(8,128)(2,1)S(1)}, u32[]{:S(2)}, u32[]{:S(2)}) collective-permute-start(f16[64,2048]{1,0:T(8,128)(2,1)S(1)} %fusion.21), channel_id=1, source_target_pairs={{0,16},{16,0},{1,17},{17,1},{2,18},{18,2},{3,19},{19,3},{4,20},{20... | collective-permute-start | bytes 786440 | tf_op jit(solution)/shard_map/ppermute | solution.py:76
  120.6 1.6 %collective-permute-start.28 = (f16[64,2048]{1,0:T(8,128)(2,1)S(1)}, f16[64,2048]{1,0:T(8,128)(2,1)S(1)}, u32[]{:S(2)}, u32[]{:S(2)}) collective-permute-start(f16[64,2048]{1,0:T(8,128)(2,1)S(1)} %fusion.19), channel_id=1, source_target_pairs={{0,16},{16,0},{1,17},{17,1},{2,18},{18,2},{3,19},{19,3},{4,20},{20... | collective-permute-start | bytes 786440 | tf_op jit(solution)/shard_map/ppermute | solution.py:76
  123.6 5.4 %collective-permute-start.29 = (f32[4,64]{1,0:T(4,128)S(1)}, f32[4,64]{1,0:T(4,128)S(1)}, u32[]{:S(2)}, u32[]{:S(2)}) collective-permute-start(f32[4,64]{1,0:T(4,128)S(1)} %get-tuple-element.77), channel_id=1, source_target_pairs={{0,1},{1,2},{2,3},{3,0},{4,5},{5,6},{6,7},{7,4},{8,9},{9,10},{10,1... | collective-permute-start | bytes 3080 | tf_op jit(solution)/shard_map/ppermute | solution.py:44
  123.6 5.4 %collective-permute-start.30 = (f32[4,64]{1,0:T(4,128)S(1)}, f32[4,64]{1,0:T(4,128)S(1)}, u32[]{:S(2)}, u32[]{:S(2)}) collective-permute-start(f32[4,64]{1,0:T(4,128)S(1)} %get-tuple-element.77), channel_id=1, source_target_pairs={{0,2},{1,3},{2,0},{3,1},{4,6},{5,7},{6,4},{7,5},{8,10},{9,11},{10,... | collective-permute-start | bytes 3080 | tf_op jit(solution)/shard_map/ppermute | solution.py:44
  127.4 3.6 %collective-permute-start.31 = (f32[4,64]{1,0:T(4,128)S(1)}, f32[4,64]{1,0:T(4,128)S(1)}, u32[]{:S(2)}, u32[]{:S(2)}) collective-permute-start(f32[4,64]{1,0:T(4,128)S(1)} %get-tuple-element.77), channel_id=1, source_target_pairs={{0,3},{1,0},{2,1},{3,2},{4,7},{5,4},{6,5},{7,6},{8,11},{9,8},{10,9... | collective-permute-start | bytes 3080 | tf_op jit(solution)/shard_map/ppermute | solution.py:44
  (2 other events, 17.7 us)

commit v17 on v15

--- a/solution.py
+++ b/solution.py
@@ -128,7 +128,7 @@
         mine_early = lax.optimization_barrier(quarter(y + 2 * (1 - first), 2))
         is_late = (level == 0) & (y == 1) | (level == vocab - 1) & (y == 0)
         near_part = dot(near, near_weight)
-        sent = after(own, below[2], above[2])
+        sent = after(own, near_weight, far_weight)
         ends = []
         for cross in (0, 2):
             moves = []

time: 119 us -> 127 us (1.067)
  waiting for transfers between devices: 45.3 us -> 51.4 us
  starting transfers between devices: 45.2 us -> 47.5 us
    ppermute x1, waiting for transfers between devices: 6.17 us -> 14.6 us  [line_parts(): got_early = lax.ppermute(quarter(far, 2), ('batch', 'vocab'), early)]
    ppermute x6, starting transfers between devices: 9.44 us -> 17.5 us  [shifted(): lax.ppermute(value, 'vocab', [(i, (i + k) % vocab) for i in range(vocab)])]
    ppermute x1, waiting for transfers between devices: 4.37 us -> 0.77 us  [line_parts(): got_near = lax.ppermute(near_sent, 'batch', Y_SWAP)]
    ppermute x2, waiting for transfers between devices: 10.5 us -> 12.9 us  [on_device(): away_y = lax.ppermute(sends[i][1], 'batch', Y_SWAP)]
    ppermute x2, starting transfers between devices: 6.56 us -> 4.17 us  [on_device(): next_x = lax.ppermute(more_sends[i][1], 'batch', X_SWAP)]
    ppermute x2, starting transfers between devices: 5.72 us -> 3.59 us  [line_parts(): ends.append(lax.ppermute(sent, ('batch', 'vocab'), sorted(moves)))]
  transfers between devices with their start and end apart: 30 -> 30, of which waited for: 16 -> 14; matrix products, arithmetic and copies ran while one was open for 20% -> 19% of each run, Pallas kernels for 0% -> 0%
where the time goes in v17:
time: 127 us
  waiting for transfers between devices  51.4 us (40%)
  starting transfers between devices  47.5 us (37%)
  other arithmetic  15.7 us (12%)
  matrix products  9.42 us (7%)
  local copies, waits for them, and re-layouts  1.76 us (1%)
    ppermute x6, starting transfers between devices, shifted(): lax.ppermute(value, 'vocab', [(i, (i + k) % vocab) for i in range(vocab)])  17.5 us
    ppermute x1, waiting for transfers between devices, line_parts(): got_early = lax.ppermute(quarter(far, 2), ('batch', 'vocab'), early)  14.6 us
    ppermute x2, waiting for transfers between devices, on_device(): away_y = lax.ppermute(sends[i][1], 'batch', Y_SWAP)  12.9 us
    dot_general x4, matrix products, dot(): jnp.dot(left.reshape(-1, block), weight, preferred_element_type=jnp.float32)  9.42 us
    ppermute x2, waiting for transfers between devices, on_device(): next_x = lax.ppermute(more_sends[i][1], 'batch', X_SWAP)  8.47 us
    select_n x1, other arithmetic, line_parts(): jnp.where(keep_near, taken, kept)  5.88 us
    ppermute x2, starting transfers between devices, row_scale(): lax.ppermute(pick(after(squares, *earlier), core ^ k, 0), ('pair', 'batch...  4.95 us
    ppermute x2, starting transfers between devices, on_device(): next_x = lax.ppermute(more_sends[i][1], 'batch', X_SWAP)  4.17 us
  transfers between devices with their start and end apart: 30, of which 14 were waited for; matrix products, arithmetic and copies ran while one was open for 19% of the time, Pallas kernels for 0%

profile of v17, /device:TPU:0, one launch (start us, length us, event | category | flops | bytes accessed | tf_op | source)
XLA Modules:
  0.0 127.0 jit_solution(5210734415427313861)
XLA Ops:
  3.0 2.6 %collective-permute-start = (bf16[2,64,1024]{2,1,0:T(8,128)(2,1)S(1)}, bf16[2,64,1024]{2,1,0:T(8,128)(2,1)S(1)}, u32[]{:S(2)}, u32[]{:S(2)}) collective-permute-start(bf16[2,64,1024]{2,1,0:T(8,128)(2,1)S(1)} %constant_dynamic-slice_fusion.6), channel_id=1, source_target_pairs={{0,4},{4,0},{8,12},{12,8},{1,5},{5,1},{9,13},{13,9},{2,6},{6,2},{1... | collective-permute-start | bytes 786440 | tf_op jit(solution)/shard_map/ppermute | solution.py:85
  6.8 1.6 %collective-permute-start.1 = (f32[128]{0:T(128)S(1)}, f32[128]{0:T(128)S(1)}, u32[]{:S(2)}, u32[]{:S(2)}) collective-permute-start(f32[128]{0:T(128)S(1)} %multiply_reduce_fusion), channel_id=1, source_target_pairs={{0,1},{1,2},{2,3},{3,0},{4,5},{5,6},{6,7},{7,4},{8,9},{9,10},{10,1... | collective-permute-start | bytes 1544 | tf_op jit(solution)/shard_map/ppermute | solution.py:44
  8.5 2.6 %collective-permute-start.2 = (f32[128]{0:T(128)S(1)}, f32[128]{0:T(128)S(1)}, u32[]{:S(2)}, u32[]{:S(2)}) collective-permute-start(f32[128]{0:T(128)S(1)} %multiply_reduce_fusion), channel_id=1, source_target_pairs={{0,2},{1,3},{2,0},{3,1},{4,6},{5,7},{6,4},{7,5},{8,10},{9,11},{10,... | collective-permute-start | bytes 1544 | tf_op jit(solution)/shard_map/ppermute | solution.py:44
  12.9 1.7 %collective-permute-done.3 = f32[128]{0:T(128)S(1)} collective-permute-done((f32[128]{0:T(128)S(1)}, f32[128]{0:T(128)S(1)}, u32[]{:S(2)}, u32[]{:S(2)}) %collective-permute-start.3) | collective-permute-done | bytes 544 | tf_op jit(solution)/shard_map/ppermute | solution.py:44
  14.9 2.2 %collective-permute-start.7 = (bf16[2,2,64,1024]{3,2,1,0:T(8,128)(2,1)S(1)}, bf16[2,2,64,1024]{3,2,1,0:T(8,128)(2,1)S(1)}, u32[]{:S(2)}, u32[]{:S(2)}) collective-permute-start(bf16[2,2,64,1024]{3,2,1,0:T(8,128)(2,1)S(1)} %pad_maximum_fusion.2), channel_id=1, source_target_pairs={{0,1},{1,2},{2,3},{4,5},{5,6},{6,7},{8,9},{9,10},{10,11},{12,13},{... | collective-permute-start | bytes 1572872 | tf_op jit(solution)/shard_map/ppermute | solution.py:92
  19.1 4.3 %collective-permute-start.6 = (f32[64]{0:T(128)S(1)}, f32[64]{0:T(128)S(1)}, u32[]{:S(2)}, u32[]{:S(2)}) collective-permute-start(f32[64]{0:T(128)S(1)} %get-tuple-element.76), channel_id=1, source_target_pairs={{0,4},{4,12},{8,20},{12,28},{16,0},{20,8},{24,16},{28,24},{1,5},{5... | collective-permute-start | bytes 776 | tf_op jit(solution)/shard_map/ppermute | solution.py:61
  24.7 2.8 %collective-permute-done.7 = bf16[2,2,64,1024]{3,2,1,0:T(8,128)(2,1)S(1)} collective-permute-done((bf16[2,2,64,1024]{3,2,1,0:T(8,128)(2,1)S(1)}, bf16[2,2,64,1024]{3,2,1,0:T(8,128)(2,1)S(1)}, u32[]{:S(2)}, u32[]{:S(2)}) %collective-permute-start.7) | collective-permute-done | bytes 524320 | tf_op jit(solution)/shard_map/ppermute | solution.py:92
  27.5 4.1 %collective-permute-done.4 = bf16[2,2,64,1024]{3,2,1,0:T(8,128)(2,1)S(1)} collective-permute-done((bf16[2,2,64,1024]{3,2,1,0:T(8,128)(2,1)S(1)}, bf16[2,2,64,1024]{3,2,1,0:T(8,128)(2,1)S(1)}, u32[]{:S(2)}, u32[]{:S(2)}) %collective-permute-start.4) | collective-permute-done | bytes 524320 | tf_op jit(solution)/shard_map/ppermute | solution.py:95
  32.9 1.5 %collective-permute-start.9 = (bf16[2,2,64,1024]{3,2,1,0:T(8,128)(2,1)S(1)}, bf16[2,2,64,1024]{3,2,1,0:T(8,128)(2,1)}, u32[]{:S(2)}, u32[]{:S(2)}) collective-permute-start(bf16[2,2,64,1024]{3,2,1,0:T(8,128)(2,1)S(1)} %collective-permute-done.7), channel_id=1, source_target_pairs={{1,2},{2,3},{5,6},{6,7},{9,10},{10,11},{13,14},{14,15},{17,18},{18... | collective-permute-start | bytes 1572872 | tf_op jit(solution)/shard_map/ppermute | solution.py:92
  34.5 1.6 %collective-permute-start.8 = (bf16[2,2,64,1024]{3,2,1,0:T(8,128)(2,1)S(1)}, bf16[2,2,64,1024]{3,2,1,0:T(8,128)(2,1)S(1)}, u32[]{:S(2)}, u32[]{:S(2)}) collective-permute-start(bf16[2,2,64,1024]{3,2,1,0:T(8,128)(2,1)S(1)} %select_select_fusion.2), channel_id=1, source_target_pairs={{0,8},{8,0},{4,12},{12,4},{1,9},{9,1},{5,13},{13,5},{2,10},{10,2},... | collective-permute-start | bytes 1572872 | tf_op jit(solution)/shard_map/ppermute | solution.py:110
  36.1 5.9 %broadcast_select_fusion = (bf16[1024,2048]{1,0:T(8,128)(2,1)S(1)}, bf16[1024,2048]{1,0:T(8,128)(2,1)S(1)}) fusion(pred[]{:T(512)S(6)} %eq.76, bf16[1024,4096]{1,0:T(8,128)(2,1)} %collective-permute-done.10, s32[]{:T(128)S(6)} %select_n.247, bf16[1024,4096]{1,0:T(8,128)(2,1)} %param.5), kind=kLoop, calls=%fused_computation.2 | loop fusion | flops 4194304 | bytes 16777220 | tf_op jit(solution)/shard_map/jit(_where)/select_n | solution.py:116
  42.0 2.9 %collective-permute-start.12 = (bf16[2,2,64,1024]{3,2,1,0:T(8,128)(2,1)S(1)}, bf16[2,2,64,1024]{3,2,1,0:T(8,128)(2,1)S(1)}, u32[]{:S(2)}, u32[]{:S(2)}) collective-permute-start(bf16[2,2,64,1024]{3,2,1,0:T(8,128)(2,1)S(1)} %pad_maximum_fusion.2), channel_id=1, source_target_pairs={{0,3},{4,7},{11,8},{15,12},{16,19},{20,23},{27,24},{31,28}} | collective-permute-start | bytes 1572872 | tf_op jit(solution)/shard_map/ppermute | solution.py:138
  47.7 1.5 %collective-permute-start.14 = (bf16[2,2,64,1024]{3,2,1,0:T(8,128)(2,1)S(1)}, bf16[2,2,64,1024]{3,2,1,0:T(8,128)(2,1)S(1)}, u32[]{:S(2)}, u32[]{:S(2)}) collective-permute-start(bf16[2,2,64,1024]{3,2,1,0:T(8,128)(2,1)S(1)} %get-tuple-element.51), channel_id=1, source_target_pairs={{1,9},{2,10},{3,11},{5,13},{6,14},{7,15},{8,0},{9,1},{10,2},{12,4}... | collective-permute-start | bytes 1572872 | tf_op jit(solution)/shard_map/ppermute | solution.py:127
  49.4 2.3 %fusion.36 = f32[512,2048]{1,0:T(8,128)S(1)} fusion(bf16[512,1024]{1,0:T(8,128)(2,1)S(1)} %bitcast.116, bf16[1024,2048]{1,0:T(8,128)(2,1)S(1)} %get-tuple-element.26), kind=kOutput, calls=%fused_computation.111 | convolution fusion | flops 2147483648 | bytes 9437184 | tf_op jit(solution)/shard_map/dot_general | solution.py:81
  51.7 1.5 %collective-permute-done.12 = bf16[2,2,64,1024]{3,2,1,0:T(8,128)(2,1)S(1)} collective-permute-done((bf16[2,2,64,1024]{3,2,1,0:T(8,128)(2,1)S(1)}, bf16[2,2,64,1024]{3,2,1,0:T(8,128)(2,1)S(1)}, u32[]{:S(2)}, u32[]{:S(2)}) %collective-permute-start.12) | collective-permute-done | bytes 524320 | tf_op jit(solution)/shard_map/ppermute | solution.py:138
  53.2 14.6 %collective-permute-done.14 = bf16[2,2,64,1024]{3,2,1,0:T(8,128)(2,1)S(1)} collective-permute-done((bf16[2,2,64,1024]{3,2,1,0:T(8,128)(2,1)S(1)}, bf16[2,2,64,1024]{3,2,1,0:T(8,128)(2,1)S(1)}, u32[]{:S(2)}, u32[]{:S(2)}) %collective-permute-start.14) | collective-permute-done | bytes 524320 | tf_op jit(solution)/shard_map/ppermute | solution.py:127
  68.1 2.4 %add_multiply_fusion.1 = f32[512,2048]{1,0:T(8,128)S(1)} fusion(f32[512,2048]{1,0:T(8,128)S(1)} %fusion.36, bf16[512,1024]{1,0:T(8,128)(2,1)S(1)} %bitcast.117, bf16[1024,2048]{1,0:T(8,128)(2,1)S(1)} %get-tuple-element.27), kind=kOutput, calls=%fused_computation.1 | convolution fusion | flops 2149580800 | bytes 13631488 | tf_op jit(solution)/shard_map/dot_general | solution.py:81
  71.6 2.1 %collective-permute-start.15 = (f16[2,2,64,1024]{3,2,0,1:T(8,128)(2,1)S(1)}, f16[2,2,64,1024]{3,2,0,1:T(8,128)(2,1)S(1)}, u32[]{:S(2)}, u32[]{:S(2)}) collective-permute-start(f16[2,2,64,1024]{3,2,0,1:T(8,128)(2,1)S(1)} %fusion.6), channel_id=1, source_target_pairs={{0,4},{4,0},{8,12},{12,8},{1,5},{5,1},{9,13},{13,9},{2,6},{6,2},{1... | collective-permute-start | bytes 1572872 | tf_op jit(solution)/shard_map/ppermute | solution.py:181
  73.7 2.3 %fusion.37 = f32[512,2048]{1,0:T(8,128)S(1)} fusion(bf16[512,1024]{1,0:T(8,128)(2,1)S(1)} %bitcast.126, bf16[1024,2048]{1,0:T(8,128)(2,1)S(1)} %get-tuple-element.27), kind=kOutput, calls=%fused_computation.112 | convolution fusion | flops 2147483648 | bytes 9437184 | tf_op jit(solution)/shard_map/dot_general | solution.py:81
  76.1 2.3 %add_multiply_fusion = f32[512,2048]{1,0:T(8,128)S(1)} fusion(f32[512,2048]{1,0:T(8,128)S(1)} %fusion.37, bf16[512,1024]{1,0:T(8,128)(2,1)S(1)} %bitcast.125, bf16[1024,2048]{1,0:T(8,128)(2,1)S(1)} %get-tuple-element.26), kind=kOutput, calls=%fused_computation | convolution fusion | flops 2149580800 | bytes 13631488 | tf_op jit(solution)/shard_map/dot_general | solution.py:81
  79.1 2.1 %collective-permute-start.20 = (f16[2,2,64,1024]{3,2,1,0:T(8,128)(2,1)S(1)}, f16[2,2,64,1024]{3,2,1,0:T(8,128)(2,1)S(1)}, u32[]{:S(2)}, u32[]{:S(2)}) collective-permute-start(f16[2,2,64,1024]{3,2,1,0:T(8,128)(2,1)S(1)} %fusion.5), channel_id=1, source_target_pairs={{0,8},{8,0},{4,12},{12,4},{1,9},{9,1},{5,13},{13,5},{2,10},{10,2},... | collective-permute-start | bytes 1572872 | tf_op jit(solution)/shard_map/ppermute | solution.py:182
  81.6 4.4 %collective-permute-done.21 = f16[2,2,64,1024]{3,2,1,0:T(8,128)(2,1)S(1)} collective-permute-done((f16[2,2,64,1024]{3,2,1,0:T(8,128)(2,1)S(1)}, f16[2,2,64,1024]{3,2,1,0:T(8,128)(2,1)S(1)}, u32[]{:S(2)}, u32[]{:S(2)}) %collective-permute-start.21) | collective-permute-done | bytes 524320 | tf_op jit(solution)/shard_map/ppermute | solution.py:182
  86.3 2.1 %collective-permute-start.22 = (f16[2,64,1024]{2,1,0:T(8,128)(2,1)S(1)}, f16[2,64,1024]{2,1,0:T(8,128)(2,1)S(1)}, u32[]{:S(2)}, u32[]{:S(2)}) collective-permute-start(f16[2,64,1024]{2,1,0:T(8,128)(2,1)S(1)} %fusion.15), channel_id=1, source_target_pairs={{0,4},{4,0},{8,12},{12,8},{1,5},{5,1},{9,13},{13,9},{2,6},{6,2},{1... | collective-permute-start | bytes 786440 | tf_op jit(solution)/shard_map/ppermute | solution.py:194
  88.8 8.5 %collective-permute-done.20 = f16[2,2,64,1024]{3,2,1,0:T(8,128)(2,1)S(1)} collective-permute-done((f16[2,2,64,1024]{3,2,1,0:T(8,128)(2,1)S(1)}, f16[2,2,64,1024]{3,2,1,0:T(8,128)(2,1)S(1)}, u32[]{:S(2)}, u32[]{:S(2)}) %collective-permute-start.20) | collective-permute-done | bytes 524320 | tf_op jit(solution)/shard_map/ppermute | solution.py:182
  97.5 2.1 %collective-permute-start.25 = (f16[2,64,1024]{2,1,0:T(8,128)(2,1)S(1)}, f16[2,64,1024]{2,1,0:T(8,128)(2,1)S(1)}, u32[]{:S(2)}, u32[]{:S(2)}) collective-permute-start(f16[2,64,1024]{2,1,0:T(8,128)(2,1)S(1)} %fusion.14), channel_id=1, source_target_pairs={{0,4},{4,0},{8,12},{12,8},{1,5},{5,1},{9,13},{13,9},{2,6},{6,2},{1... | collective-permute-start | bytes 786440 | tf_op jit(solution)/shard_map/ppermute | solution.py:194
  100.0 3.4 %collective-permute-done.22 = f16[2,64,1024]{2,1,0:T(8,128)(2,1)S(1)} collective-permute-done((f16[2,64,1024]{2,1,0:T(8,128)(2,1)S(1)}, f16[2,64,1024]{2,1,0:T(8,128)(2,1)S(1)}, u32[]{:S(2)}, u32[]{:S(2)}) %collective-permute-start.22) | collective-permute-done | bytes 262176 | tf_op jit(solution)/shard_map/ppermute | solution.py:194
  103.7 5.1 %collective-permute-done.25 = f16[2,64,1024]{2,1,0:T(8,128)(2,1)S(1)} collective-permute-done((f16[2,64,1024]{2,1,0:T(8,128)(2,1)S(1)}, f16[2,64,1024]{2,1,0:T(8,128)(2,1)S(1)}, u32[]{:S(2)}, u32[]{:S(2)}) %collective-permute-start.25) | collective-permute-done | bytes 262176 | tf_op jit(solution)/shard_map/ppermute | solution.py:194
  109.3 1.4 %collective-permute-done.26 = f16[64,2048]{1,0:T(8,128)(2,1)S(1)} collective-permute-done((f16[64,2048]{1,0:T(8,128)(2,1)S(1)}, f16[64,2048]{1,0:T(8,128)(2,1)S(1)}, u32[]{:S(2)}, u32[]{:S(2)}) %collective-permute-start.26) | collective-permute-done | bytes 262176 | tf_op jit(solution)/shard_map/ppermute | solution.py:75
  112.0 6.9 %collective-permute-start.27 = (f32[4,64]{1,0:T(4,128)S(1)}, f32[4,64]{1,0:T(4,128)S(1)}, u32[]{:S(2)}, u32[]{:S(2)}) collective-permute-start(f32[4,64]{1,0:T(4,128)S(1)} %get-tuple-element.68), channel_id=1, source_target_pairs={{0,1},{1,2},{2,3},{3,0},{4,5},{5,6},{6,7},{7,4},{8,9},{9,10},{10,1... | collective-permute-start | bytes 3080 | tf_op jit(solution)/shard_map/ppermute | solution.py:44
  118.9 2.2 %collective-permute-start.28 = (f32[4,64]{1,0:T(4,128)S(1)}, f32[4,64]{1,0:T(4,128)S(1)}, u32[]{:S(2)}, u32[]{:S(2)}) collective-permute-start(f32[4,64]{1,0:T(4,128)S(1)} %get-tuple-element.68), channel_id=1, source_target_pairs={{0,2},{1,3},{2,0},{3,1},{4,6},{5,7},{6,4},{7,5},{8,10},{9,11},{10,... | collective-permute-start | bytes 3080 | tf_op jit(solution)/shard_map/ppermute | solution.py:44
  121.1 2.8 %collective-permute-start.29 = (f32[4,64]{1,0:T(4,128)S(1)}, f32[4,64]{1,0:T(4,128)S(1)}, u32[]{:S(2)}, u32[]{:S(2)}) collective-permute-start(f32[4,64]{1,0:T(4,128)S(1)} %get-tuple-element.68), channel_id=1, source_target_pairs={{0,3},{1,0},{2,1},{3,2},{4,7},{5,4},{6,5},{7,6},{8,11},{9,8},{10,9... | collective-permute-start | bytes 3080 | tf_op jit(solution)/shard_map/ppermute | solution.py:44
  125.4 1.6 %fusion.2 = (f32[64,4096]{1,0:T(8,128)}, f32[64,4096]{1,0:T(8,128)}) fusion(f32[64]{0:T(128)S(1)} %get-tuple-element.69, f32[64]{0:T(128)S(1)} %get-tuple-element.71, f16[64,2048]{1,0:T(8,128)(2,1)S(1)} %get-tuple-element.62, f16[64,2048]{1,0:T(8,128)(2,1)S(1)} %get-tuple-element.60, f32[64,4096]{1,0:T(8,128)S(1)} %get-tuple-element.41, ...), kind=kLoop, calls=%fused_computation.18 | loop fusion | flops 1310720 | bytes 3670784 | tf_op jit(solution)/shard_map/sub | solution.py:232
  (85 shorter events, 20.4 us)
Async XLA Ops:
  0.6 35.5 %collective-permute-start.10 = (bf16[1024,4096]{1,0:T(8,128)(2,1)}, bf16[1024,4096]{1,0:T(8,128)(2,1)}, u32[]{:S(2)}, u32[]{:S(2)}) collective-permute-start(bf16[1024,4096]{1,0:T(8,128)(2,1)} %param.5), channel_id=1, source_target_pairs={{0,16},{16,0},{1,17},{17,1},{2,18},{18,2},{3,19},{19,3},{4,20},{20... | collective-permute-start | bytes 25165832 | tf_op jit(solution)/shard_map/ppermute | solution.py:41
  3.0 11.7 %collective-permute-start = (bf16[2,64,1024]{2,1,0:T(8,128)(2,1)S(1)}, bf16[2,64,1024]{2,1,0:T(8,128)(2,1)S(1)}, u32[]{:S(2)}, u32[]{:S(2)}) collective-permute-start(bf16[2,64,1024]{2,1,0:T(8,128)(2,1)S(1)} %constant_dynamic-slice_fusion.6), channel_id=1, source_target_pairs={{0,4},{4,0},{8,12},{12,8},{1,5},{5,1},{9,13},{13,9},{2,6},{6,2},{1... | collective-permute-start | bytes 786440 | tf_op jit(solution)/shard_map/ppermute | solution.py:85
  6.8 5.6 %collective-permute-start.1 = (f32[128]{0:T(128)S(1)}, f32[128]{0:T(128)S(1)}, u32[]{:S(2)}, u32[]{:S(2)}) collective-permute-start(f32[128]{0:T(128)S(1)} %multiply_reduce_fusion), channel_id=1, source_target_pairs={{0,1},{1,2},{2,3},{3,0},{4,5},{5,6},{6,7},{7,4},{8,9},{9,10},{10,1... | collective-permute-start | bytes 1544 | tf_op jit(solution)/shard_map/ppermute | solution.py:44
  8.5 4.4 %collective-permute-start.2 = (f32[128]{0:T(128)S(1)}, f32[128]{0:T(128)S(1)}, u32[]{:S(2)}, u32[]{:S(2)}) collective-permute-start(f32[128]{0:T(128)S(1)} %multiply_reduce_fusion), channel_id=1, source_target_pairs={{0,2},{1,3},{2,0},{3,1},{4,6},{5,7},{6,4},{7,5},{8,10},{9,11},{10,... | collective-permute-start | bytes 1544 | tf_op jit(solution)/shard_map/ppermute | solution.py:44
  11.0 3.5 %collective-permute-start.3 = (f32[128]{0:T(128)S(1)}, f32[128]{0:T(128)S(1)}, u32[]{:S(2)}, u32[]{:S(2)}) collective-permute-start(f32[128]{0:T(128)S(1)} %multiply_reduce_fusion), channel_id=1, source_target_pairs={{0,3},{1,0},{2,1},{3,2},{4,7},{5,4},{6,5},{7,6},{8,11},{9,8},{10,9... | collective-permute-start | bytes 1544 | tf_op jit(solution)/shard_map/ppermute | solution.py:44
  14.9 12.6 %collective-permute-start.7 = (bf16[2,2,64,1024]{3,2,1,0:T(8,128)(2,1)S(1)}, bf16[2,2,64,1024]{3,2,1,0:T(8,128)(2,1)S(1)}, u32[]{:S(2)}, u32[]{:S(2)}) collective-permute-start(bf16[2,2,64,1024]{3,2,1,0:T(8,128)(2,1)S(1)} %pad_maximum_fusion.2), channel_id=1, source_target_pairs={{0,1},{1,2},{2,3},{4,5},{5,6},{6,7},{8,9},{9,10},{10,11},{12,13},{... | collective-permute-start | bytes 1572872 | tf_op jit(solution)/shard_map/ppermute | solution.py:92
  17.0 14.6 %collective-permute-start.4 = (bf16[2,2,64,1024]{3,2,1,0:T(8,128)(2,1)S(1)}, bf16[2,2,64,1024]{3,2,1,0:T(8,128)(2,1)S(1)}, u32[]{:S(2)}, u32[]{:S(2)}) collective-permute-start(bf16[2,2,64,1024]{3,2,1,0:T(8,128)(2,1)S(1)} %pad_maximum_fusion.2), channel_id=1, source_target_pairs={{1,0},{2,1},{3,2},{5,4},{6,5},{7,6},{9,8},{10,9},{11,10},{13,12},{... | collective-permute-start | bytes 1572872 | tf_op jit(solution)/shard_map/ppermute | solution.py:95
  18.5 5.0 %collective-permute-start.5 = (f32[64]{0:T(128)S(1)}, f32[64]{0:T(128)S(1)}, u32[]{:S(2)}, u32[]{:S(2)}) collective-permute-start(f32[64]{0:T(128)S(1)} %get-tuple-element.75), channel_id=1, source_target_pairs={{0,0},{4,8},{8,16},{12,24},{16,4},{20,12},{24,20},{28,28},{1,1},{5... | collective-permute-start | bytes 776 | tf_op jit(solution)/shard_map/ppermute | solution.py:61
  19.1 5.6 %collective-permute-start.6 = (f32[64]{0:T(128)S(1)}, f32[64]{0:T(128)S(1)}, u32[]{:S(2)}, u32[]{:S(2)}) collective-permute-start(f32[64]{0:T(128)S(1)} %get-tuple-element.76), channel_id=1, source_target_pairs={{0,4},{4,12},{8,20},{12,28},{16,0},{20,8},{24,16},{28,24},{1,5},{5... | collective-permute-start | bytes 776 | tf_op jit(solution)/shard_map/ppermute | solution.py:61
  31.6 14.7 %collective-permute-start.11 = (bf16[2,2,64,1024]{3,2,1,0:T(8,128)(2,1)S(1)}, bf16[2,2,64,1024]{3,2,1,0:T(8,128)(2,1)S(1)}, u32[]{:S(2)}, u32[]{:S(2)}) collective-permute-start(bf16[2,2,64,1024]{3,2,1,0:T(8,128)(2,1)S(1)} %collective-permute-done.4), channel_id=1, source_target_pairs={{1,0},{2,1},{5,4},{6,5},{9,8},{10,9},{13,12},{14,13},{17,16},{18,1... | collective-permute-start | bytes 1572872 | tf_op jit(solution)/shard_map/ppermute | solution.py:95
  32.9 13.5 %collective-permute-start.9 = (bf16[2,2,64,1024]{3,2,1,0:T(8,128)(2,1)S(1)}, bf16[2,2,64,1024]{3,2,1,0:T(8,128)(2,1)}, u32[]{:S(2)}, u32[]{:S(2)}) collective-permute-start(bf16[2,2,64,1024]{3,2,1,0:T(8,128)(2,1)S(1)} %collective-permute-done.7), channel_id=1, source_target_pairs={{1,2},{2,3},{5,6},{6,7},{9,10},{10,11},{13,14},{14,15},{17,18},{18... | collective-permute-start | bytes 1572872 | tf_op jit(solution)/shard_map/ppermute | solution.py:92
  34.5 11.8 %collective-permute-start.8 = (bf16[2,2,64,1024]{3,2,1,0:T(8,128)(2,1)S(1)}, bf16[2,2,64,1024]{3,2,1,0:T(8,128)(2,1)S(1)}, u32[]{:S(2)}, u32[]{:S(2)}) collective-permute-start(bf16[2,2,64,1024]{3,2,1,0:T(8,128)(2,1)S(1)} %select_select_fusion.2), channel_id=1, source_target_pairs={{0,8},{8,0},{4,12},{12,4},{1,9},{9,1},{5,13},{13,5},{2,10},{10,2},... | collective-permute-start | bytes 1572872 | tf_op jit(solution)/shard_map/ppermute | solution.py:110
  42.0 11.2 %collective-permute-start.12 = (bf16[2,2,64,1024]{3,2,1,0:T(8,128)(2,1)S(1)}, bf16[2,2,64,1024]{3,2,1,0:T(8,128)(2,1)S(1)}, u32[]{:S(2)}, u32[]{:S(2)}) collective-permute-start(bf16[2,2,64,1024]{3,2,1,0:T(8,128)(2,1)S(1)} %pad_maximum_fusion.2), channel_id=1, source_target_pairs={{0,3},{4,7},{11,8},{15,12},{16,19},{20,23},{27,24},{31,28}} | collective-permute-start | bytes 1572872 | tf_op jit(solution)/shard_map/ppermute | solution.py:138
  44.9 8.3 %collective-permute-start.13 = (bf16[2,2,64,1024]{3,2,1,0:T(8,128)(2,1)S(1)}, bf16[2,2,64,1024]{3,2,1,0:T(8,128)(2,1)S(1)}, u32[]{:S(2)}, u32[]{:S(2)}) collective-permute-start(bf16[2,2,64,1024]{3,2,1,0:T(8,128)(2,1)S(1)} %pad_maximum_fusion.2), channel_id=1, source_target_pairs={{3,8},{7,12},{8,3},{12,7},{19,24},{23,28},{24,19},{28,23}} | collective-permute-start | bytes 1572872 | tf_op jit(solution)/shard_map/ppermute | solution.py:138
  47.7 20.1 %collective-permute-start.14 = (bf16[2,2,64,1024]{3,2,1,0:T(8,128)(2,1)S(1)}, bf16[2,2,64,1024]{3,2,1,0:T(8,128)(2,1)S(1)}, u32[]{:S(2)}, u32[]{:S(2)}) collective-permute-start(bf16[2,2,64,1024]{3,2,1,0:T(8,128)(2,1)S(1)} %get-tuple-element.51), channel_id=1, source_target_pairs={{1,9},{2,10},{3,11},{5,13},{6,14},{7,15},{8,0},{9,1},{10,2},{12,4}... | collective-permute-start | bytes 1572872 | tf_op jit(solution)/shard_map/ppermute | solution.py:127
  49.3 26.8 %collective-permute-start.16 = (bf16[2,2,2,64,1024]{4,3,2,1,0:T(8,128)(2,1)S(1)}, bf16[2,2,2,64,1024]{4,3,2,1,0:T(8,128)(2,1)S(1)}, u32[]{:S(2)}, u32[]{:S(2)}) collective-permute-start(bf16[2,2,2,64,1024]{4,3,2,1,0:T(8,128)(2,1)S(1)} %pad_maximum_fusion), channel_id=1, source_target_pairs={{0,16},{16,0},{1,17},{17,1},{2,18},{18,2},{3,19},{19,3},{4,20},{20... | collective-permute-start | bytes 3145736 | tf_op jit(solution)/shard_map/ppermute | solution.py:75
  68.1 5.7 %collective-permute-start.17 = (bf16[2,2,2,64,1024]{4,3,2,1,0:T(8,128)(2,1)S(1)}, bf16[2,2,2,64,1024]{4,3,2,1,0:T(8,128)(2,1)S(1)}, u32[]{:S(2)}, u32[]{:S(2)}) collective-permute-start(bf16[2,2,2,64,1024]{4,3,2,1,0:T(8,128)(2,1)S(1)} %pad_maximum_fusion.1), channel_id=1, source_target_pairs={{0,16},{16,0},{1,17},{17,1},{2,18},{18,2},{3,19},{19,3},{4,20},{20... | collective-permute-start | bytes 3145736 | tf_op jit(solution)/shard_map/ppermute | solution.py:75
  71.2 14.8 %collective-permute-start.21 = (f16[2,2,64,1024]{3,2,1,0:T(8,128)(2,1)S(1)}, f16[2,2,64,1024]{3,2,1,0:T(8,128)(2,1)S(1)}, u32[]{:S(2)}, u32[]{:S(2)}) collective-permute-start(f16[2,2,64,1024]{3,2,1,0:T(8,128)(2,1)S(1)} %fusion.4), channel_id=1, source_target_pairs={{0,8},{8,0},{4,12},{12,4},{1,9},{9,1},{5,13},{13,5},{2,10},{10,2},... | collective-permute-start | bytes 1572872 | tf_op jit(solution)/shard_map/ppermute | solution.py:182
  71.6 16.7 %collective-permute-start.15 = (f16[2,2,64,1024]{3,2,0,1:T(8,128)(2,1)S(1)}, f16[2,2,64,1024]{3,2,0,1:T(8,128)(2,1)S(1)}, u32[]{:S(2)}, u32[]{:S(2)}) collective-permute-start(f16[2,2,64,1024]{3,2,0,1:T(8,128)(2,1)S(1)} %fusion.6), channel_id=1, source_target_pairs={{0,4},{4,0},{8,12},{12,8},{1,5},{5,1},{9,13},{13,9},{2,6},{6,2},{1... | collective-permute-start | bytes 1572872 | tf_op jit(solution)/shard_map/ppermute | solution.py:181
  79.1 18.1 %collective-permute-start.20 = (f16[2,2,64,1024]{3,2,1,0:T(8,128)(2,1)S(1)}, f16[2,2,64,1024]{3,2,1,0:T(8,128)(2,1)S(1)}, u32[]{:S(2)}, u32[]{:S(2)}) collective-permute-start(f16[2,2,64,1024]{3,2,1,0:T(8,128)(2,1)S(1)} %fusion.5), channel_id=1, source_target_pairs={{0,8},{8,0},{4,12},{12,4},{1,9},{9,1},{5,13},{13,5},{2,10},{10,2},... | collective-permute-start | bytes 1572872 | tf_op jit(solution)/shard_map/ppermute | solution.py:182
  81.5 18.1 %collective-permute-start.19 = (f16[2,2,64,1024]{3,2,0,1:T(8,128)(2,1)S(1)}, f16[2,2,64,1024]{3,2,0,1:T(8,128)(2,1)S(1)}, u32[]{:S(2)}, u32[]{:S(2)}) collective-permute-start(f16[2,2,64,1024]{3,2,0,1:T(8,128)(2,1)S(1)} %fusion.7), channel_id=1, source_target_pairs={{0,4},{4,0},{8,12},{12,8},{1,5},{5,1},{9,13},{13,9},{2,6},{6,2},{1... | collective-permute-start | bytes 1572872 | tf_op jit(solution)/shard_map/ppermute | solution.py:181
  86.3 17.1 %collective-permute-start.22 = (f16[2,64,1024]{2,1,0:T(8,128)(2,1)S(1)}, f16[2,64,1024]{2,1,0:T(8,128)(2,1)S(1)}, u32[]{:S(2)}, u32[]{:S(2)}) collective-permute-start(f16[2,64,1024]{2,1,0:T(8,128)(2,1)S(1)} %fusion.15), channel_id=1, source_target_pairs={{0,4},{4,0},{8,12},{12,8},{1,5},{5,1},{9,13},{13,9},{2,6},{6,2},{1... | collective-permute-start | bytes 786440 | tf_op jit(solution)/shard_map/ppermute | solution.py:194
  88.6 14.8 %collective-permute-start.18 = (f16[2,64,1024]{2,1,0:T(8,128)(2,1)S(1)}, f16[2,64,1024]{2,1,0:T(8,128)(2,1)S(1)}, u32[]{:S(2)}, u32[]{:S(2)}) collective-permute-start(f16[2,64,1024]{2,1,0:T(8,128)(2,1)S(1)} %fusion.12), channel_id=1, source_target_pairs={{0,8},{8,0},{4,12},{12,4},{1,9},{9,1},{5,13},{13,5},{2,10},{10,2},... | collective-permute-start | bytes 786440 | tf_op jit(solution)/shard_map/ppermute | solution.py:193
  97.5 11.3 %collective-permute-start.25 = (f16[2,64,1024]{2,1,0:T(8,128)(2,1)S(1)}, f16[2,64,1024]{2,1,0:T(8,128)(2,1)S(1)}, u32[]{:S(2)}, u32[]{:S(2)}) collective-permute-start(f16[2,64,1024]{2,1,0:T(8,128)(2,1)S(1)} %fusion.14), channel_id=1, source_target_pairs={{0,4},{4,0},{8,12},{12,8},{1,5},{5,1},{9,13},{13,9},{2,6},{6,2},{1... | collective-permute-start | bytes 786440 | tf_op jit(solution)/shard_map/ppermute | solution.py:194
  99.8 9.0 %collective-permute-start.24 = (f16[2,64,1024]{2,1,0:T(8,128)(2,1)S(1)}, f16[2,64,1024]{2,1,0:T(8,128)(2,1)S(1)}, u32[]{:S(2)}, u32[]{:S(2)}) collective-permute-start(f16[2,64,1024]{2,1,0:T(8,128)(2,1)S(1)} %fusion.13), channel_id=1, source_target_pairs={{0,8},{8,0},{4,12},{12,4},{1,9},{9,1},{5,13},{13,5},{2,10},{10,2},... | collective-permute-start | bytes 786440 | tf_op jit(solution)/shard_map/ppermute | solution.py:193
  103.6 5.5 %collective-permute-start.23 = (f16[64,2048]{1,0:T(8,128)(2,1)S(1)}, f16[64,2048]{1,0:T(8,128)(2,1)S(1)}, u32[]{:S(2)}, u32[]{:S(2)}) collective-permute-start(f16[64,2048]{1,0:T(8,128)(2,1)S(1)} %fusion.21), channel_id=1, source_target_pairs={{0,16},{16,0},{1,17},{17,1},{2,18},{18,2},{3,19},{19,3},{4,20},{20... | collective-permute-start | bytes 786440 | tf_op jit(solution)/shard_map/ppermute | solution.py:75
  109.1 1.6 %collective-permute-start.26 = (f16[64,2048]{1,0:T(8,128)(2,1)S(1)}, f16[64,2048]{1,0:T(8,128)(2,1)S(1)}, u32[]{:S(2)}, u32[]{:S(2)}) collective-permute-start(f16[64,2048]{1,0:T(8,128)(2,1)S(1)} %fusion.19), channel_id=1, source_target_pairs={{0,16},{16,0},{1,17},{17,1},{2,18},{18,2},{3,19},{19,3},{4,20},{20... | collective-permute-start | bytes 786440 | tf_op jit(solution)/shard_map/ppermute | solution.py:75
  112.0 11.9 %collective-permute-start.27 = (f32[4,64]{1,0:T(4,128)S(1)}, f32[4,64]{1,0:T(4,128)S(1)}, u32[]{:S(2)}, u32[]{:S(2)}) collective-permute-start(f32[4,64]{1,0:T(4,128)S(1)} %get-tuple-element.68), channel_id=1, source_target_pairs={{0,1},{1,2},{2,3},{3,0},{4,5},{5,6},{6,7},{7,4},{8,9},{9,10},{10,1... | collective-permute-start | bytes 3080 | tf_op jit(solution)/shard_map/ppermute | solution.py:44
  118.9 5.1 %collective-permute-start.28 = (f32[4,64]{1,0:T(4,128)S(1)}, f32[4,64]{1,0:T(4,128)S(1)}, u32[]{:S(2)}, u32[]{:S(2)}) collective-permute-start(f32[4,64]{1,0:T(4,128)S(1)} %get-tuple-element.68), channel_id=1, source_target_pairs={{0,2},{1,3},{2,0},{3,1},{4,6},{5,7},{6,4},{7,5},{8,10},{9,11},{10,... | collective-permute-start | bytes 3080 | tf_op jit(solution)/shard_map/ppermute | solution.py:44
  121.1 4.2 %collective-permute-start.29 = (f32[4,64]{1,0:T(4,128)S(1)}, f32[4,64]{1,0:T(4,128)S(1)}, u32[]{:S(2)}, u32[]{:S(2)}) collective-permute-start(f32[4,64]{1,0:T(4,128)S(1)} %get-tuple-element.68), channel_id=1, source_target_pairs={{0,3},{1,0},{2,1},{3,2},{4,7},{5,4},{6,5},{7,6},{8,11},{9,8},{10,9... | collective-permute-start | bytes 3080 | tf_op jit(solution)/shard_map/ppermute | solution.py:44

commit v18 on v15

--- a/solution.py
+++ b/solution.py
@@ -1,3 +1,5 @@
+import functools
+
 import jax
 import jax.numpy as jnp
 from jax import lax
@@ -7,6 +9,7 @@
 GUIDE = 1.5
 SHRINK = 1.0 / 32.0
 SUM_TYPE = jnp.float16
+CHUNKS = 2
 
 X_SWAP = [(0, 1), (1, 0), (2, 3), (3, 2)]
 Y_SWAP = [(0, 2), (2, 0), (1, 3), (3, 1)]
@@ -33,10 +36,11 @@
     block, columns = head_weight.shape
     width = columns // 2
     model = depth * vocab
+    step = seg // CHUNKS
 
     wide = rows.astype(jnp.float32)
     gained = (wide * norm_gain.astype(jnp.float32)[None, :]).astype(jnp.bfloat16)
-    gained = gained.reshape(2, seg, depth)
+    gained = gained.reshape(2, CHUNKS, step, depth).transpose(1, 0, 2, 3)
 
     take = lax.ppermute(head_weight, "pair", CORE_SWAP)
 
@@ -81,11 +85,11 @@
         return jnp.dot(left.reshape(-1, block), weight, preferred_element_type=jnp.float32)
 
     def line_parts():
-        mine = lax.dynamic_slice_in_dim(gained, x * block, block, 2)
+        mine = lax.dynamic_slice_in_dim(gained, x * block, block, 3)
         other = lax.ppermute(
-            lax.dynamic_slice_in_dim(gained, (1 - x) * block, block, 2), "batch", X_SWAP
-        )
-        own = jnp.stack([jnp.where(x == 0, mine, other), jnp.where(x == 0, other, mine)])
+            lax.dynamic_slice_in_dim(gained, (1 - x) * block, block, 3), "batch", X_SWAP
+        )
+        own = jnp.stack([jnp.where(x == 0, mine, other), jnp.where(x == 0, other, mine)], axis=1)
         own = after(own, squares)
 
         def up(value, k):
@@ -117,17 +121,20 @@
         )
         ready = (got_near, near_weight, far_weight)
         below[2], above[2] = after(below[2], *ready), after(above[2], *ready)
-        near = by_y(quarter(y + 2 * first, 1), after(got_near, below[2], above[2]), 0)
+        near = by_y(quarter(y + 2 * first, 1), after(got_near, below[2], above[2]), 1)
         swapped_near = swapped(near)
 
         far = 1 - y + 2 * (1 - first)
         pairs = [(b * vocab + z, (b ^ 2) * vocab + z) for b in range(4) for z in range(vocab)]
         lone = [b * vocab + (vocab - 1) * (b // 2) for b in range(4)]
         early = [pair for pair in pairs if pair[0] not in lone]
-        got_early = lax.ppermute(quarter(far, 2), ("batch", "vocab"), early)
+        far_sent = quarter(far, 2)
+        got_early = [
+            lax.ppermute(far_sent[c], ("batch", "vocab"), early) for c in range(CHUNKS)
+        ]
         mine_early = lax.optimization_barrier(quarter(y + 2 * (1 - first), 2))
         is_late = (level == 0) & (y == 1) | (level == vocab - 1) & (y == 0)
-        near_part = dot(near, near_weight)
+        near_part = dot(near, near_weight).reshape(CHUNKS, -1, width)
         sent = after(own, below[2], above[2])
         ends = []
         for cross in (0, 2):
@@ -136,64 +143,88 @@
                 b, z = divmod(place, vocab)
                 moves.append(((b ^ cross) * vocab + z, b * vocab + vocab - 1 - z))
             ends.append(lax.ppermute(sent, ("batch", "vocab"), sorted(moves)))
-        mine_late, got_late, got_early, _ = lax.optimization_barrier(
-            (ends[0], ends[1], got_early, near_part)
-        )
-        far = by_y(
-            jnp.where(is_late, mine_late, mine_early), jnp.where(is_late, got_late, got_early), 0
-        )
-        swapped_far = swapped(far)
-
-        def own_part():
-            return near_part + dot(far, far_weight)
+        mine_late, got_late, got_early[0], _ = lax.optimization_barrier(
+            (ends[0], ends[1], got_early[0], near_part)
+        )
+
+        def far_rows(c, *earlier):
+            got = after(got_early[c], *earlier)
+            return by_y(
+                jnp.where(is_late, mine_late[c], mine_early[c]),
+                jnp.where(is_late, got_late[c], got),
+                0,
+            )
+
+        swapped_far = []
+
+        def own_part(c, *earlier):
+            rows = far_rows(c, *earlier)
+            swapped_far.append(swapped(rows))
+            return (near_part[c] + dot(rows, far_weight))[None]
 
         def other_part(*earlier):
-            left = after(swapped_far, *earlier)
-            return dot(swapped_near, near_weight) + dot(left, far_weight)
-
-        return (own_part, other_part), scale
+            near_other = dot(swapped_near, near_weight).reshape(CHUNKS, -1, width)
+            found = [
+                near_other[c] + dot(after(swapped_far[c], *earlier), far_weight)
+                for c in range(CHUNKS)
+            ]
+            return jnp.stack(found)
+
+        own_parts = [functools.partial(own_part, c) for c in range(CHUNKS)]
+        return (*own_parts, other_part), scale
 
     def gathered_parts():
         near_weight, far_weight = half_columns(head_weight), half_columns(take)
-        whole = lax.all_gather(gained, "vocab", axis=2, tiled=True)
-        whole = whole.reshape(2, seg, 2, 4, block).transpose(3, 2, 0, 1, 4)
+        whole = lax.all_gather(gained, "vocab", axis=3, tiled=True)
+        whole = whole.reshape(CHUNKS, 2, step, 2, 4, block).transpose(4, 3, 0, 1, 2, 5)
         whole = lax.all_to_all(whole, "batch", split_axis=0, concat_axis=0)
-        whole = whole.reshape(2, 2, 2, 2, seg, block).transpose(2, 0, 1, 3, 4, 5)
+        whole = whole.reshape(2, 2, 2, CHUNKS, 2, step, block).transpose(2, 3, 0, 1, 4, 5, 6)
         swapped_whole = swapped(whole)
 
         def part(left):
-            return dot(pick(left, core, 0), near_weight) + dot(pick(left, 1 - core, 0), far_weight)
-
-        return (lambda: part(whole), lambda *earlier: part(after(swapped_whole, *earlier))), row_scale()
+            near, far = pick(left, core, 0), pick(left, 1 - core, 0)
+            found = dot(near, near_weight) + dot(far, far_weight)
+            return found.reshape(near.shape[0], -1, width)
+
+        def own_part(c, *earlier):
+            return part(after(whole, *earlier)[:, c : c + 1])
+
+        def other_part(*earlier):
+            return part(after(swapped_whole, *earlier))
+
+        own_parts = [functools.partial(own_part, c) for c in range(CHUNKS)]
+        return (*own_parts, other_part), row_scale()
 
     lined = depth == 2 * block and vocab == 4
     parts, scale = line_parts() if lined else gathered_parts()
+    groups = len(parts)
     kept, sends = [], []
     for part in parts:
-        whole = (part(*(sends[-1] if sends else ())) * SHRINK).reshape(2, 2, 2, seg, width)
+        whole = part(*(sends[-1] if sends else ())) * SHRINK
+        whole = whole.reshape(-1, 2, 2, 2, step, width)
         low, high = whole[..., : width // 2], whole[..., width // 2 :]
-        kept.append((pick(low, x, 2), pick(high, y, 1)))
+        kept.append((pick(low, x, 3), pick(high, y, 2)))
         sends.append(
-            (pick(low, 1 - x, 2).astype(SUM_TYPE), pick(high, 1 - y, 1).astype(SUM_TYPE))
+            (pick(low, 1 - x, 3).astype(SUM_TYPE), pick(high, 1 - y, 2).astype(SUM_TYPE))
         )
     halfway, more_sends = [], []
-    for i in range(2):
+    for i in range(groups):
         away_x = lax.ppermute(sends[i][0], "batch", X_SWAP)
         away_y = lax.ppermute(sends[i][1], "batch", Y_SWAP)
-        if i == 0:
-            away_x, away_y = after(away_x, *sends[1]), after(away_y, *sends[1])
+        if i + 1 < groups:
+            away_x, away_y = after(away_x, *sends[i + 1]), after(away_y, *sends[i + 1])
         sum_x = kept[i][0] + away_x.astype(jnp.float32)
         sum_y = kept[i][1] + away_y.astype(jnp.float32)
-        halfway.append((pick(sum_x, y, 1), pick(sum_y, x, 1)))
+        halfway.append((pick(sum_x, y, 2), pick(sum_y, x, 2)))
         more_sends.append(
-            (pick(sum_x, 1 - y, 1).astype(SUM_TYPE), pick(sum_y, 1 - x, 1).astype(SUM_TYPE))
+            (pick(sum_x, 1 - y, 2).astype(SUM_TYPE), pick(sum_y, 1 - x, 2).astype(SUM_TYPE))
         )
     mine, theirs = [], []
-    for i in range(2):
+    for i in range(groups):
         next_y = lax.ppermute(more_sends[i][0], "batch", Y_SWAP)
         next_x = lax.ppermute(more_sends[i][1], "batch", X_SWAP)
-        if i == 0:
-            next_y, next_x = after(next_y, *more_sends[1]), after(next_x, *more_sends[1])
+        if i + 1 < groups:
+            next_y, next_x = after(next_y, *more_sends[i + 1]), after(next_x, *more_sends[i + 1])
         sums = jnp.concatenate(
             [
                 halfway[i][0] + next_y.astype(jnp.float32),
@@ -201,8 +232,14 @@
             ],
             axis=-1,
         ).astype(SUM_TYPE)
-        mine.append(pick(sums, core, 0))
-        theirs.append(swapped(pick(sums, 1 - core, 0)))
+        mine.append(pick(sums, core, 1))
+        theirs.append(swapped(pick(sums, 1 - core, 1)))
+
+    def by_branch(found):
+        own = jnp.concatenate(found[:-1]).reshape(seg, width)
+        return own, found[-1].reshape(seg, width)
+
+    mine, theirs = by_branch(mine), by_branch(theirs)
 
     def scores(own, other, got_own, got_other, gain):
         low = jnp.where(core == 0, own, got_own)

time: 119 us -> 133 us (1.12)
  starting transfers between devices: 45.2 us -> 50.8 us
  waiting for transfers between devices: 45.3 us -> 50.2 us
  other arithmetic: 15.7 us -> 18.8 us
    ppermute x2 -> x3, waiting for transfers between devices: 0.01 us -> 11.5 us  [on_device(): away_x = lax.ppermute(sends[i][0], 'batch', X_SWAP)]
    ppermute x2 -> x3, waiting for transfers between devices: 10.5 us -> 1.78 us  [on_device(): away_y = lax.ppermute(sends[i][1], 'batch', Y_SWAP)]
    ppermute x2 -> x3, starting transfers between devices: 6.56 us -> 1.16 us  [on_device(): next_x = lax.ppermute(more_sends[i][1], 'batch', X_SWAP)]
    ppermute x2 -> x3, starting transfers between devices: 2.14 us -> 7.18 us  [on_device(): away_y = lax.ppermute(sends[i][1], 'batch', Y_SWAP)]
    ppermute x6, waiting for transfers between devices: 4.31 us -> 9.07 us  [shifted(): lax.ppermute(value, 'vocab', [(i, (i + k) % vocab) for i in range(vocab)])]
    ppermute x2 -> x3, waiting for transfers between devices: 0.01 us -> 4.09 us  [on_device(): next_y = lax.ppermute(more_sends[i][0], 'batch', Y_SWAP)]
    ppermute x2, starting transfers between devices: 5.72 us -> 8.89 us  [line_parts(): ends.append(lax.ppermute(sent, ('batch', 'vocab'), sorted(moves)))]
    ppermute x1, waiting for transfers between devices: 4.37 us -> 1.64 us  [line_parts(): got_near = lax.ppermute(near_sent, 'batch', Y_SWAP)]
  transfers between devices with their start and end apart: 30 -> 37, of which waited for: 16 -> 21; matrix products, arithmetic and copies ran while one was open for 20% -> 20% of each run, Pallas kernels for 0% -> 0%
where the time goes in v18:
time: 133 us
  starting transfers between devices  50.8 us (38%)
  waiting for transfers between devices  50.2 us (38%)
  other arithmetic  18.8 us (14%)
  matrix products  9.84 us (7%)
  local copies, waits for them, and re-layouts  1.89 us (1%)
  between operations  1.41 us (1%)
    ppermute x3, waiting for transfers between devices, on_device(): away_x = lax.ppermute(sends[i][0], 'batch', X_SWAP)  11.5 us
    dot_general x6, matrix products, dot(): jnp.dot(left.reshape(-1, block), weight, preferred_element_type=jnp.float32)  9.84 us
    ppermute x6, waiting for transfers between devices, shifted(): lax.ppermute(value, 'vocab', [(i, (i + k) % vocab) for i in range(vocab)])  9.07 us
    ppermute x2, starting transfers between devices, line_parts(): ends.append(lax.ppermute(sent, ('batch', 'vocab'), sorted(moves)))  8.89 us
    ppermute x6, starting transfers between devices, shifted(): lax.ppermute(value, 'vocab', [(i, (i + k) % vocab) for i in range(vocab)])  8.35 us
    select_n x1, other arithmetic, line_parts(): jnp.where(keep_near, taken, kept)  8.23 us
    ppermute x3, starting transfers between devices, on_device(): away_y = lax.ppermute(sends[i][1], 'batch', Y_SWAP)  7.18 us
    ppermute x2, waiting for transfers between devices, line_parts(): lax.ppermute(far_sent[c], ('batch', 'vocab'), early)  5.94 us
  transfers between devices with their start and end apart: 37, of which 21 were waited for; matrix products, arithmetic and copies ran while one was open for 20% of the time, Pallas kernels for 0%

profile of v18, /device:TPU:0, one launch (start us, length us, event | category | flops | bytes accessed | tf_op | source)
XLA Modules:
  0.0 133.0 jit_solution(10568079667090686124)
XLA Ops:
  3.0 2.6 %collective-permute-start = (bf16[2,2,32,1024]{3,2,0,1:T(8,128)(2,1)S(1)}, bf16[2,2,32,1024]{3,2,0,1:T(8,128)(2,1)S(1)}, u32[]{:S(2)}, u32[]{:S(2)}) collective-permute-start(bf16[2,2,32,1024]{3,2,0,1:T(8,128)(2,1)S(1)} %dynamic-slice_bitcast_fusion), channel_id=1, source_target_pairs={{0,4},{4,0},{8,12},{12,8},{1,5},{5,1},{9,13},{13,9},{2,6},{6,2},{1... | collective-permute-start | bytes 786440 | tf_op jit(solution)/shard_map/ppermute | solution.py:89
  6.8 3.6 %collective-permute-start.3 = (f32[128]{0:T(128)S(1)}, f32[128]{0:T(128)S(1)}, u32[]{:S(2)}, u32[]{:S(2)}) collective-permute-start(f32[128]{0:T(128)S(1)} %multiply_reduce_fusion), channel_id=1, source_target_pairs={{0,3},{1,0},{2,1},{3,2},{4,7},{5,4},{6,5},{7,6},{8,11},{9,8},{10,9... | collective-permute-start | bytes 1544 | tf_op jit(solution)/shard_map/ppermute | solution.py:48
  11.8 4.0 %collective-permute-done.1 = f32[128]{0:T(128)S(1)} collective-permute-done((f32[128]{0:T(128)S(1)}, f32[128]{0:T(128)S(1)}, u32[]{:S(2)}, u32[]{:S(2)}) %collective-permute-start.1) | collective-permute-done | bytes 544 | tf_op jit(solution)/shard_map/ppermute | solution.py:48
  16.1 2.5 %collective-permute-start.7 = (bf16[2,2,2,32,1024]{4,3,2,1,0:T(8,128)(2,1)S(1)}, bf16[2,2,2,32,1024]{4,3,2,1,0:T(8,128)(2,1)S(1)}, u32[]{:S(2)}, u32[]{:S(2)}) collective-permute-start(bf16[2,2,2,32,1024]{4,3,2,1,0:T(8,128)(2,1)S(1)} %copy.21), channel_id=1, source_target_pairs={{0,1},{1,2},{2,3},{4,5},{5,6},{6,7},{8,9},{9,10},{10,11},{12,13},{... | collective-permute-start | bytes 1572872 | tf_op jit(solution)/shard_map/ppermute | solution.py:96
  20.7 4.3 %collective-permute-start.6 = (f32[64]{0:T(128)S(1)}, f32[64]{0:T(128)S(1)}, u32[]{:S(2)}, u32[]{:S(2)}) collective-permute-start(f32[64]{0:T(128)S(1)} %get-tuple-element.104), channel_id=1, source_target_pairs={{0,4},{4,12},{8,20},{12,28},{16,0},{20,8},{24,16},{28,24},{1,5},{5... | collective-permute-start | bytes 776 | tf_op jit(solution)/shard_map/ppermute | solution.py:65
  26.3 2.4 %collective-permute-done.7 = bf16[2,2,2,32,1024]{4,3,2,1,0:T(8,128)(2,1)S(1)} collective-permute-done((bf16[2,2,2,32,1024]{4,3,2,1,0:T(8,128)(2,1)S(1)}, bf16[2,2,2,32,1024]{4,3,2,1,0:T(8,128)(2,1)S(1)}, u32[]{:S(2)}, u32[]{:S(2)}) %collective-permute-start.7) | collective-permute-done | bytes 524320 | tf_op jit(solution)/shard_map/ppermute | solution.py:96
  29.4 3.5 %collective-permute-done.4 = bf16[2,2,2,32,1024]{4,3,2,1,0:T(8,128)(2,1)S(1)} collective-permute-done((bf16[2,2,2,32,1024]{4,3,2,1,0:T(8,128)(2,1)S(1)}, bf16[2,2,2,32,1024]{4,3,2,1,0:T(8,128)(2,1)S(1)}, u32[]{:S(2)}, u32[]{:S(2)}) %collective-permute-start.4) | collective-permute-done | bytes 524320 | tf_op jit(solution)/shard_map/ppermute | solution.py:99
  34.2 1.6 %collective-permute-start.8 = (bf16[2,2,2,32,1024]{4,3,2,1,0:T(8,128)(2,1)S(1)}, bf16[2,2,2,32,1024]{4,3,2,1,0:T(8,128)(2,1)S(1)}, u32[]{:S(2)}, u32[]{:S(2)}) collective-permute-start(bf16[2,2,2,32,1024]{4,3,2,1,0:T(8,128)(2,1)S(1)} %select_select_fusion.2), channel_id=1, source_target_pairs={{0,8},{8,0},{4,12},{12,4},{1,9},{9,1},{5,13},{13,5},{2,10},{10,2},... | collective-permute-start | bytes 1572872 | tf_op jit(solution)/shard_map/ppermute | solution.py:114
  35.8 8.2 %broadcast_select_fusion = (bf16[1024,2048]{1,0:T(8,128)(2,1)S(1)}, bf16[1024,2048]{1,0:T(8,128)(2,1)}) fusion(pred[]{:T(512)S(6)} %eq.78, bf16[1024,4096]{1,0:T(8,128)(2,1)} %collective-permute-done.10, s32[]{:T(128)S(6)} %select_n.295, bf16[1024,4096]{1,0:T(8,128)(2,1)} %param.5), kind=kLoop, calls=%fused_computation.1 | loop fusion | flops 4194304 | bytes 16777220 | tf_op jit(solution)/shard_map/jit(_where)/select_n | solution.py:120
  44.1 1.6 %collective-permute-done.8 = bf16[2,2,2,32,1024]{4,3,2,1,0:T(8,128)(2,1)S(1)} collective-permute-done((bf16[2,2,2,32,1024]{4,3,2,1,0:T(8,128)(2,1)S(1)}, bf16[2,2,2,32,1024]{4,3,2,1,0:T(8,128)(2,1)S(1)}, u32[]{:S(2)}, u32[]{:S(2)}) %collective-permute-start.8) | collective-permute-done | bytes 524320 | tf_op jit(solution)/shard_map/ppermute | solution.py:114
  48.6 8.2 %collective-permute-start.12 = (bf16[2,2,2,32,1024]{4,3,2,1,0:T(8,128)(2,1)S(1)}, bf16[2,2,2,32,1024]{4,3,2,1,0:T(8,128)(2,1)S(1)}, u32[]{:S(2)}, u32[]{:S(2)}) collective-permute-start(bf16[2,2,2,32,1024]{4,3,2,1,0:T(8,128)(2,1)S(1)} %copy.26), channel_id=1, source_target_pairs={{0,3},{4,7},{11,8},{15,12},{16,19},{20,23},{27,24},{31,28}} | collective-permute-start | bytes 1572872 | tf_op jit(solution)/shard_map/ppermute | solution.py:145
  58.2 2.3 %fusion.54 = f32[512,2048]{1,0:T(8,128)S(1)} fusion(bf16[512,1024]{1,0:T(8,128)(2,1)S(1)} %bitcast.198, bf16[1024,2048]{1,0:T(8,128)(2,1)S(1)} %copy-done), kind=kOutput, calls=%fused_computation.156 | convolution fusion | flops 2147483648 | bytes 9437184 | tf_op jit(solution)/shard_map/dot_general | solution.py:85
  60.5 1.5 %collective-permute-start.16 = (bf16[2,2,32,1024]{3,2,1,0:T(8,128)(2,1)S(1)}, bf16[2,2,32,1024]{3,2,1,0:T(8,128)(2,1)S(1)}, u32[]{:S(2)}, u32[]{:S(2)}) collective-permute-start(bf16[2,2,32,1024]{3,2,1,0:T(8,128)(2,1)S(1)} %get-tuple-element.89), channel_id=1, source_target_pairs={{1,9},{2,10},{3,11},{5,13},{6,14},{7,15},{8,0},{9,1},{10,2},{12,4}... | collective-permute-start | bytes 786440 | tf_op jit(solution)/shard_map/ppermute | solution.py:133
  62.0 5.9 %collective-permute-done.14 = bf16[2,2,32,1024]{3,2,1,0:T(8,128)(2,1)S(1)} collective-permute-done((bf16[2,2,32,1024]{3,2,1,0:T(8,128)(2,1)S(1)}, bf16[2,2,32,1024]{3,2,1,0:T(8,128)(2,1)S(1)}, u32[]{:S(2)}, u32[]{:S(2)}) %collective-permute-start.14) | collective-permute-done | bytes 262176 | tf_op jit(solution)/shard_map/ppermute | solution.py:133
  70.3 1.5 %collective-permute-start.15 = (f16[1,2,2,32,1024]{4,3,1,2,0:T(8,128)(2,1)S(1)}, f16[1,2,2,32,1024]{4,3,1,2,0:T(8,128)(2,1)S(1)}, u32[]{:S(2)}, u32[]{:S(2)}) collective-permute-start(f16[1,2,2,32,1024]{4,3,1,2,0:T(8,128)(2,1)S(1)} %fusion.15), channel_id=1, source_target_pairs={{0,4},{4,0},{8,12},{12,8},{1,5},{5,1},{9,13},{13,9},{2,6},{6,2},{1... | collective-permute-start | bytes 786440 | tf_op jit(solution)/shard_map/ppermute | solution.py:212
  71.9 3.3 %collective-permute-start.23 = (f16[1,2,2,32,1024]{4,3,2,1,0:T(8,128)(2,1)S(1)}, f16[1,2,2,32,1024]{4,3,2,1,0:T(8,128)(2,1)S(1)}, u32[]{:S(2)}, u32[]{:S(2)}) collective-permute-start(f16[1,2,2,32,1024]{4,3,2,1,0:T(8,128)(2,1)S(1)} %fusion.11), channel_id=1, source_target_pairs={{0,8},{8,0},{4,12},{12,4},{1,9},{9,1},{5,13},{13,5},{2,10},{10,2},... | collective-permute-start | bytes 786440 | tf_op jit(solution)/shard_map/ppermute | solution.py:213
  75.3 1.3 fusion
  77.1 2.0 %collective-permute-done.15 = f16[1,2,2,32,1024]{4,3,1,2,0:T(8,128)(2,1)S(1)} collective-permute-done((f16[1,2,2,32,1024]{4,3,1,2,0:T(8,128)(2,1)S(1)}, f16[1,2,2,32,1024]{4,3,1,2,0:T(8,128)(2,1)S(1)}, u32[]{:S(2)}, u32[]{:S(2)}) %collective-permute-start.15) | collective-permute-done | bytes 262176 | tf_op jit(solution)/shard_map/ppermute | solution.py:212
  79.1 1.4 %collective-permute-start.18 = (f16[1,2,2,32,1024]{4,3,1,2,0:T(8,128)(2,1)S(1)}, f16[1,2,2,32,1024]{4,3,1,2,0:T(8,128)(2,1)S(1)}, u32[]{:S(2)}, u32[]{:S(2)}) collective-permute-start(f16[1,2,2,32,1024]{4,3,1,2,0:T(8,128)(2,1)S(1)} %fusion.16), channel_id=1, source_target_pairs={{0,4},{4,0},{8,12},{12,8},{1,5},{5,1},{9,13},{13,9},{2,6},{6,2},{1... | collective-permute-start | bytes 786440 | tf_op jit(solution)/shard_map/ppermute | solution.py:212
  81.8 1.9 %collective-permute-start.22 = (f16[1,2,2,32,1024]{4,3,2,1,0:T(8,128)(2,1)S(1)}, f16[1,2,2,32,1024]{4,3,2,1,0:T(8,128)(2,1)S(1)}, u32[]{:S(2)}, u32[]{:S(2)}) collective-permute-start(f16[1,2,2,32,1024]{4,3,2,1,0:T(8,128)(2,1)S(1)} %fusion.12), channel_id=1, source_target_pairs={{0,8},{8,0},{4,12},{12,4},{1,9},{9,1},{5,13},{13,5},{2,10},{10,2},... | collective-permute-start | bytes 786440 | tf_op jit(solution)/shard_map/ppermute | solution.py:213
  84.2 2.3 %fusion.55 = f32[512,2048]{1,0:T(8,128)S(1)} fusion(bf16[512,1024]{1,0:T(8,128)(2,1)S(1)} %bitcast.199, bf16[1024,2048]{1,0:T(8,128)(2,1)S(1)} %copy-done), kind=kOutput, calls=%fused_computation.157 | convolution fusion | flops 2147483648 | bytes 9437184 | tf_op jit(solution)/shard_map/dot_general | solution.py:85
  91.0 1.8 %collective-permute-start.26 = (f16[2,2,2,32,1024]{4,3,1,0,2:T(8,128)(2,1)S(1)}, f16[2,2,2,32,1024]{4,3,1,0,2:T(8,128)(2,1)S(1)}, u32[]{:S(2)}, u32[]{:S(2)}) collective-permute-start(f16[2,2,2,32,1024]{4,3,1,0,2:T(8,128)(2,1)S(1)} %fusion.6), channel_id=1, source_target_pairs={{0,4},{4,0},{8,12},{12,8},{1,5},{5,1},{9,13},{13,9},{2,6},{6,2},{1... | collective-permute-start | bytes 1572872 | tf_op jit(solution)/shard_map/ppermute | solution.py:212
  92.9 2.0 %collective-permute-start.27 = (f16[2,2,2,32,1024]{4,3,2,1,0:T(8,128)(2,1)S(1)}, f16[2,2,2,32,1024]{4,3,2,1,0:T(8,128)(2,1)S(1)}, u32[]{:S(2)}, u32[]{:S(2)}) collective-permute-start(f16[2,2,2,32,1024]{4,3,2,1,0:T(8,128)(2,1)S(1)} %fusion.5), channel_id=1, source_target_pairs={{0,8},{8,0},{4,12},{12,4},{1,9},{9,1},{5,13},{13,5},{2,10},{10,2},... | collective-permute-start | bytes 1572872 | tf_op jit(solution)/shard_map/ppermute | solution.py:213
  95.9 9.5 %collective-permute-done.26 = f16[2,2,2,32,1024]{4,3,1,0,2:T(8,128)(2,1)S(1)} collective-permute-done((f16[2,2,2,32,1024]{4,3,1,0,2:T(8,128)(2,1)S(1)}, f16[2,2,2,32,1024]{4,3,1,0,2:T(8,128)(2,1)S(1)}, u32[]{:S(2)}, u32[]{:S(2)}) %collective-permute-start.26) | collective-permute-done | bytes 524320 | tf_op jit(solution)/shard_map/ppermute | solution.py:212
  105.6 1.7 %collective-permute-start.31 = (f16[2,2,32,1024]{3,2,1,0:T(8,128)(2,1)S(1)}, f16[2,2,32,1024]{3,2,1,0:T(8,128)(2,1)S(1)}, u32[]{:S(2)}, u32[]{:S(2)}) collective-permute-start(f16[2,2,32,1024]{3,2,1,0:T(8,128)(2,1)S(1)} %fusion.13), channel_id=1, source_target_pairs={{0,8},{8,0},{4,12},{12,4},{1,9},{9,1},{5,13},{13,5},{2,10},{10,2},... | collective-permute-start | bytes 786440 | tf_op jit(solution)/shard_map/ppermute | solution.py:224
  108.0 2.5 %collective-permute-done.25 = f16[1,2,32,1024]{3,2,1,0:T(8,128)(2,1)S(1)} collective-permute-done((f16[1,2,32,1024]{3,2,1,0:T(8,128)(2,1)S(1)}, f16[1,2,32,1024]{3,2,1,0:T(8,128)(2,1)S(1)}, u32[]{:S(2)}, u32[]{:S(2)}) %collective-permute-start.25) | collective-permute-done | bytes 131104 | tf_op jit(solution)/shard_map/ppermute | solution.py:224
  112.2 1.5 %collective-permute-done.31 = f16[2,2,32,1024]{3,2,1,0:T(8,128)(2,1)S(1)} collective-permute-done((f16[2,2,32,1024]{3,2,1,0:T(8,128)(2,1)S(1)}, f16[2,2,32,1024]{3,2,1,0:T(8,128)(2,1)S(1)}, u32[]{:S(2)}, u32[]{:S(2)}) %collective-permute-start.31) | collective-permute-done | bytes 262176 | tf_op jit(solution)/shard_map/ppermute | solution.py:224
  113.9 5.8 %collective-permute-done.32 = f16[2,2,32,1024]{3,2,1,0:T(8,128)(2,1)S(1)} collective-permute-done((f16[2,2,32,1024]{3,2,1,0:T(8,128)(2,1)S(1)}, f16[2,2,32,1024]{3,2,1,0:T(8,128)(2,1)S(1)}, u32[]{:S(2)}, u32[]{:S(2)}) %collective-permute-start.32) | collective-permute-done | bytes 262176 | tf_op jit(solution)/shard_map/ppermute | solution.py:225
  120.1 1.4 %collective-permute-done.33 = f16[2,32,2048]{2,1,0:T(8,128)(2,1)S(1)} collective-permute-done((f16[2,32,2048]{2,1,0:T(8,128)(2,1)S(1)}, f16[2,32,2048]{2,1,0:T(8,128)(2,1)S(1)}, u32[]{:S(2)}, u32[]{:S(2)}) %collective-permute-start.33) | collective-permute-done | bytes 262176 | tf_op jit(solution)/shard_map/ppermute | solution.py:79
  122.9 3.0 %collective-permute-start.36 = (f32[4,64]{1,0:T(4,128)S(1)}, f32[4,64]{1,0:T(4,128)S(1)}, u32[]{:S(2)}, u32[]{:S(2)}) collective-permute-start(f32[4,64]{1,0:T(4,128)S(1)} %get-tuple-element.96), channel_id=1, source_target_pairs={{0,3},{1,0},{2,1},{3,2},{4,7},{5,4},{6,5},{7,6},{8,11},{9,8},{10,9... | collective-permute-start | bytes 3080 | tf_op jit(solution)/shard_map/ppermute | solution.py:48
  127.2 3.2 %collective-permute-done.35 = f32[4,64]{1,0:T(4,128)S(1)} collective-permute-done((f32[4,64]{1,0:T(4,128)S(1)}, f32[4,64]{1,0:T(4,128)S(1)}, u32[]{:S(2)}, u32[]{:S(2)}) %collective-permute-start.35) | collective-permute-done | bytes 1056 | tf_op jit(solution)/shard_map/ppermute | solution.py:48
  131.4 1.6 %fusion.3 = (f32[64,4096]{1,0:T(8,128)}, f32[64,4096]{1,0:T(8,128)}) fusion(f32[64]{0:T(128)S(1)} %get-tuple-element.97, f32[64]{0:T(128)S(1)} %get-tuple-element.99, f16[64,2048]{1,0:T(8,128)(2,1)S(1)} %get-tuple-element.85, f16[64,2048]{1,0:T(8,128)(2,1)S(1)} %bitcast.194, f32[64,4096]{1,0:T(8,128)S(1)} %get-tuple-element.53, f32[64]{0:T(128)S(1)} %get-tuple-element.98), kind=kLoop, calls=%fused_computation.18 | loop fusion | flops 1310720 | bytes 3670784 | tf_op jit(solution)/shard_map/sub | solution.py:269
  (124 shorter events, 31.5 us)
Async XLA Ops:
  0.6 35.2 %collective-permute-start.10 = (bf16[1024,4096]{1,0:T(8,128)(2,1)}, bf16[1024,4096]{1,0:T(8,128)(2,1)}, u32[]{:S(2)}, u32[]{:S(2)}) collective-permute-start(bf16[1024,4096]{1,0:T(8,128)(2,1)} %param.5), channel_id=1, source_target_pairs={{0,16},{16,0},{1,17},{17,1},{2,18},{18,2},{3,19},{19,3},{4,20},{20... | collective-permute-start | bytes 25165832 | tf_op jit(solution)/shard_map/ppermute | solution.py:45
  3.0 12.9 %collective-permute-start = (bf16[2,2,32,1024]{3,2,0,1:T(8,128)(2,1)S(1)}, bf16[2,2,32,1024]{3,2,0,1:T(8,128)(2,1)S(1)}, u32[]{:S(2)}, u32[]{:S(2)}) collective-permute-start(bf16[2,2,32,1024]{3,2,0,1:T(8,128)(2,1)S(1)} %dynamic-slice_bitcast_fusion), channel_id=1, source_target_pairs={{0,4},{4,0},{8,12},{12,8},{1,5},{5,1},{9,13},{13,9},{2,6},{6,2},{1... | collective-permute-start | bytes 786440 | tf_op jit(solution)/shard_map/ppermute | solution.py:89
  10.5 5.3 %collective-permute-start.1 = (f32[128]{0:T(128)S(1)}, f32[128]{0:T(128)S(1)}, u32[]{:S(2)}, u32[]{:S(2)}) collective-permute-start(f32[128]{0:T(128)S(1)} %multiply_reduce_fusion), channel_id=1, source_target_pairs={{0,1},{1,2},{2,3},{3,0},{4,5},{5,6},{6,7},{7,4},{8,9},{9,10},{10,1... | collective-permute-start | bytes 1544 | tf_op jit(solution)/shard_map/ppermute | solution.py:48
  10.5 5.3 %collective-permute-start.2 = (f32[128]{0:T(128)S(1)}, f32[128]{0:T(128)S(1)}, u32[]{:S(2)}, u32[]{:S(2)}) collective-permute-start(f32[128]{0:T(128)S(1)} %multiply_reduce_fusion), channel_id=1, source_target_pairs={{0,2},{1,3},{2,0},{3,1},{4,6},{5,7},{6,4},{7,5},{8,10},{9,11},{10,... | collective-permute-start | bytes 1544 | tf_op jit(solution)/shard_map/ppermute | solution.py:48
  16.1 12.6 %collective-permute-start.7 = (bf16[2,2,2,32,1024]{4,3,2,1,0:T(8,128)(2,1)S(1)}, bf16[2,2,2,32,1024]{4,3,2,1,0:T(8,128)(2,1)S(1)}, u32[]{:S(2)}, u32[]{:S(2)}) collective-permute-start(bf16[2,2,2,32,1024]{4,3,2,1,0:T(8,128)(2,1)S(1)} %copy.21), channel_id=1, source_target_pairs={{0,1},{1,2},{2,3},{4,5},{5,6},{6,7},{8,9},{9,10},{10,11},{12,13},{... | collective-permute-start | bytes 1572872 | tf_op jit(solution)/shard_map/ppermute | solution.py:96
  18.7 14.2 %collective-permute-start.4 = (bf16[2,2,2,32,1024]{4,3,2,1,0:T(8,128)(2,1)S(1)}, bf16[2,2,2,32,1024]{4,3,2,1,0:T(8,128)(2,1)S(1)}, u32[]{:S(2)}, u32[]{:S(2)}) collective-permute-start(bf16[2,2,2,32,1024]{4,3,2,1,0:T(8,128)(2,1)S(1)} %copy.21), channel_id=1, source_target_pairs={{1,0},{2,1},{3,2},{5,4},{6,5},{7,6},{9,8},{10,9},{11,10},{13,12},{... | collective-permute-start | bytes 1572872 | tf_op jit(solution)/shard_map/ppermute | solution.py:99
  20.1 5.0 %collective-permute-start.5 = (f32[64]{0:T(128)S(1)}, f32[64]{0:T(128)S(1)}, u32[]{:S(2)}, u32[]{:S(2)}) collective-permute-start(f32[64]{0:T(128)S(1)} %get-tuple-element.103), channel_id=1, source_target_pairs={{0,0},{4,8},{8,16},{12,24},{16,4},{20,12},{24,20},{28,28},{1,1},{5... | collective-permute-start | bytes 776 | tf_op jit(solution)/shard_map/ppermute | solution.py:65
  20.7 5.6 %collective-permute-start.6 = (f32[64]{0:T(128)S(1)}, f32[64]{0:T(128)S(1)}, u32[]{:S(2)}, u32[]{:S(2)}) collective-permute-start(f32[64]{0:T(128)S(1)} %get-tuple-element.104), channel_id=1, source_target_pairs={{0,4},{4,12},{8,20},{12,28},{16,0},{20,8},{24,16},{28,24},{1,5},{5... | collective-permute-start | bytes 776 | tf_op jit(solution)/shard_map/ppermute | solution.py:65
  28.7 15.3 %collective-permute-start.9 = (bf16[2,2,2,32,1024]{4,3,2,1,0:T(8,128)(2,1)S(1)}, bf16[2,2,2,32,1024]{4,3,2,1,0:T(8,128)(2,1)S(1)}, u32[]{:S(2)}, u32[]{:S(2)}) collective-permute-start(bf16[2,2,2,32,1024]{4,3,2,1,0:T(8,128)(2,1)S(1)} %collective-permute-done.7), channel_id=1, source_target_pairs={{1,2},{2,3},{5,6},{6,7},{9,10},{10,11},{13,14},{14,15},{17,18},{18... | collective-permute-start | bytes 1572872 | tf_op jit(solution)/shard_map/ppermute | solution.py:96
  32.9 13.4 %collective-permute-start.11 = (bf16[2,2,2,32,1024]{4,3,2,1,0:T(8,128)(2,1)S(1)}, bf16[2,2,2,32,1024]{4,3,2,1,0:T(8,128)(2,1)}, u32[]{:S(2)}, u32[]{:S(2)}) collective-permute-start(bf16[2,2,2,32,1024]{4,3,2,1,0:T(8,128)(2,1)S(1)} %collective-permute-done.4), channel_id=1, source_target_pairs={{1,0},{2,1},{5,4},{6,5},{9,8},{10,9},{13,12},{14,13},{17,16},{18,1... | collective-permute-start | bytes 1572872 | tf_op jit(solution)/shard_map/ppermute | solution.py:99
  34.2 11.5 %collective-permute-start.8 = (bf16[2,2,2,32,1024]{4,3,2,1,0:T(8,128)(2,1)S(1)}, bf16[2,2,2,32,1024]{4,3,2,1,0:T(8,128)(2,1)S(1)}, u32[]{:S(2)}, u32[]{:S(2)}) collective-permute-start(bf16[2,2,2,32,1024]{4,3,2,1,0:T(8,128)(2,1)S(1)} %select_select_fusion.2), channel_id=1, source_target_pairs={{0,8},{8,0},{4,12},{12,4},{1,9},{9,1},{5,13},{13,5},{2,10},{10,2},... | collective-permute-start | bytes 1572872 | tf_op jit(solution)/shard_map/ppermute | solution.py:114
  46.3 22.0 %collective-permute-start.13 = (bf16[2,2,2,32,1024]{4,3,0,2,1:T(8,128)(2,1)S(1)}, bf16[2,2,2,32,1024]{4,3,0,2,1:T(8,128)(2,1)S(1)}, u32[]{:S(2)}, u32[]{:S(2)}) collective-permute-start(bf16[2,2,2,32,1024]{4,3,0,2,1:T(8,128)(2,1)S(1)} %pad_maximum_fusion.1), channel_id=1, source_target_pairs={{3,8},{7,12},{8,3},{12,7},{19,24},{23,28},{24,19},{28,23}} | collective-permute-start | bytes 1572872 | tf_op jit(solution)/shard_map/ppermute | solution.py:145
  48.5 35.4 %collective-permute-start.19 = (bf16[2,2,2,2,32,1024]{5,4,3,2,0,1:T(8,128)(2,1)S(1)}, bf16[2,2,2,2,32,1024]{5,4,3,2,0,1:T(8,128)(2,1)S(1)}, u32[]{:S(2)}, u32[]{:S(2)}) collective-permute-start(bf16[2,2,2,2,32,1024]{5,4,3,2,0,1:T(8,128)(2,1)S(1)} %pad_maximum_fusion), channel_id=1, source_target_pairs={{0,16},{16,0},{1,17},{17,1},{2,18},{18,2},{3,19},{19,3},{4,20},{20... | collective-permute-start | bytes 3145736 | tf_op jit(solution)/shard_map/ppermute | solution.py:79
  48.6 19.7 %collective-permute-start.12 = (bf16[2,2,2,32,1024]{4,3,2,1,0:T(8,128)(2,1)S(1)}, bf16[2,2,2,32,1024]{4,3,2,1,0:T(8,128)(2,1)S(1)}, u32[]{:S(2)}, u32[]{:S(2)}) collective-permute-start(bf16[2,2,2,32,1024]{4,3,2,1,0:T(8,128)(2,1)S(1)} %copy.26), channel_id=1, source_target_pairs={{0,3},{4,7},{11,8},{15,12},{16,19},{20,23},{27,24},{31,28}} | collective-permute-start | bytes 1572872 | tf_op jit(solution)/shard_map/ppermute | solution.py:145
  56.8 11.1 %collective-permute-start.14 = (bf16[2,2,32,1024]{3,2,1,0:T(8,128)(2,1)S(1)}, bf16[2,2,32,1024]{3,2,1,0:T(8,128)(2,1)S(1)}, u32[]{:S(2)}, u32[]{:S(2)}) collective-permute-start(bf16[2,2,32,1024]{3,2,1,0:T(8,128)(2,1)S(1)} %get-tuple-element.90), channel_id=1, source_target_pairs={{1,9},{2,10},{3,11},{5,13},{6,14},{7,15},{8,0},{9,1},{10,2},{12,4}... | collective-permute-start | bytes 786440 | tf_op jit(solution)/shard_map/ppermute | solution.py:133
  60.5 14.6 %collective-permute-start.16 = (bf16[2,2,32,1024]{3,2,1,0:T(8,128)(2,1)S(1)}, bf16[2,2,32,1024]{3,2,1,0:T(8,128)(2,1)S(1)}, u32[]{:S(2)}, u32[]{:S(2)}) collective-permute-start(bf16[2,2,32,1024]{3,2,1,0:T(8,128)(2,1)S(1)} %get-tuple-element.89), channel_id=1, source_target_pairs={{1,9},{2,10},{3,11},{5,13},{6,14},{7,15},{8,0},{9,1},{10,2},{12,4}... | collective-permute-start | bytes 786440 | tf_op jit(solution)/shard_map/ppermute | solution.py:133
  68.6 19.6 %collective-permute-start.20 = (bf16[2,2,2,32,1024]{4,3,2,1,0:T(8,128)(2,1)S(1)}, bf16[2,2,2,32,1024]{4,3,2,1,0:T(8,128)(2,1)S(1)}, u32[]{:S(2)}, u32[]{:S(2)}) collective-permute-start(bf16[2,2,2,32,1024]{4,3,2,1,0:T(8,128)(2,1)S(1)} %pad_maximum_fusion.2), channel_id=1, source_target_pairs={{0,16},{16,0},{1,17},{17,1},{2,18},{18,2},{3,19},{19,3},{4,20},{20... | collective-permute-start | bytes 1572872 | tf_op jit(solution)/shard_map/ppermute | solution.py:79
  70.3 8.8 %collective-permute-start.15 = (f16[1,2,2,32,1024]{4,3,1,2,0:T(8,128)(2,1)S(1)}, f16[1,2,2,32,1024]{4,3,1,2,0:T(8,128)(2,1)S(1)}, u32[]{:S(2)}, u32[]{:S(2)}) collective-permute-start(f16[1,2,2,32,1024]{4,3,1,2,0:T(8,128)(2,1)S(1)} %fusion.15), channel_id=1, source_target_pairs={{0,4},{4,0},{8,12},{12,8},{1,5},{5,1},{9,13},{13,9},{2,6},{6,2},{1... | collective-permute-start | bytes 786440 | tf_op jit(solution)/shard_map/ppermute | solution.py:212
  71.9 10.0 %collective-permute-start.23 = (f16[1,2,2,32,1024]{4,3,2,1,0:T(8,128)(2,1)S(1)}, f16[1,2,2,32,1024]{4,3,2,1,0:T(8,128)(2,1)S(1)}, u32[]{:S(2)}, u32[]{:S(2)}) collective-permute-start(f16[1,2,2,32,1024]{4,3,2,1,0:T(8,128)(2,1)S(1)} %fusion.11), channel_id=1, source_target_pairs={{0,8},{8,0},{4,12},{12,4},{1,9},{9,1},{5,13},{13,5},{2,10},{10,2},... | collective-permute-start | bytes 786440 | tf_op jit(solution)/shard_map/ppermute | solution.py:213
  75.2 11.3 %collective-permute-start.21 = (bf16[2,2,2,32,1024]{4,3,2,1,0:T(8,128)(2,1)S(1)}, bf16[2,2,2,32,1024]{4,3,2,1,0:T(8,128)(2,1)S(1)}, u32[]{:S(2)}, u32[]{:S(2)}) collective-permute-start(bf16[2,2,2,32,1024]{4,3,2,1,0:T(8,128)(2,1)S(1)} %pad_maximum_fusion.3), channel_id=1, source_target_pairs={{0,16},{16,0},{1,17},{17,1},{2,18},{18,2},{3,19},{19,3},{4,20},{20... | collective-permute-start | bytes 1572872 | tf_op jit(solution)/shard_map/ppermute | solution.py:79
  79.1 13.7 %collective-permute-start.18 = (f16[1,2,2,32,1024]{4,3,1,2,0:T(8,128)(2,1)S(1)}, f16[1,2,2,32,1024]{4,3,1,2,0:T(8,128)(2,1)S(1)}, u32[]{:S(2)}, u32[]{:S(2)}) collective-permute-start(f16[1,2,2,32,1024]{4,3,1,2,0:T(8,128)(2,1)S(1)} %fusion.16), channel_id=1, source_target_pairs={{0,4},{4,0},{8,12},{12,8},{1,5},{5,1},{9,13},{13,9},{2,6},{6,2},{1... | collective-permute-start | bytes 786440 | tf_op jit(solution)/shard_map/ppermute | solution.py:212
  81.8 13.0 %collective-permute-start.22 = (f16[1,2,2,32,1024]{4,3,2,1,0:T(8,128)(2,1)S(1)}, f16[1,2,2,32,1024]{4,3,2,1,0:T(8,128)(2,1)S(1)}, u32[]{:S(2)}, u32[]{:S(2)}) collective-permute-start(f16[1,2,2,32,1024]{4,3,2,1,0:T(8,128)(2,1)S(1)} %fusion.12), channel_id=1, source_target_pairs={{0,8},{8,0},{4,12},{12,4},{1,9},{9,1},{5,13},{13,5},{2,10},{10,2},... | collective-permute-start | bytes 786440 | tf_op jit(solution)/shard_map/ppermute | solution.py:213
  84.0 11.3 %collective-permute-start.17 = (f16[1,2,32,1024]{3,2,1,0:T(8,128)(2,1)S(1)}, f16[1,2,32,1024]{3,2,1,0:T(8,128)(2,1)S(1)}, u32[]{:S(2)}, u32[]{:S(2)}) collective-permute-start(f16[1,2,32,1024]{3,2,1,0:T(8,128)(2,1)S(1)} %fusion.29), channel_id=1, source_target_pairs={{0,8},{8,0},{4,12},{12,4},{1,9},{9,1},{5,13},{13,5},{2,10},{10,2},... | collective-permute-start | bytes 393224 | tf_op jit(solution)/shard_map/ppermute | solution.py:224
  86.6 9.1 %collective-permute-start.24 = (f16[1,2,32,1024]{3,2,1,0:T(8,128)(2,1)S(1)}, f16[1,2,32,1024]{3,2,1,0:T(8,128)(2,1)S(1)}, u32[]{:S(2)}, u32[]{:S(2)}) collective-permute-start(f16[1,2,32,1024]{3,2,1,0:T(8,128)(2,1)S(1)} %fusion.32), channel_id=1, source_target_pairs={{0,4},{4,0},{8,12},{12,8},{1,5},{5,1},{9,13},{13,9},{2,6},{6,2},{1... | collective-permute-start | bytes 393224 | tf_op jit(solution)/shard_map/ppermute | solution.py:225
  91.0 14.4 %collective-permute-start.26 = (f16[2,2,2,32,1024]{4,3,1,0,2:T(8,128)(2,1)S(1)}, f16[2,2,2,32,1024]{4,3,1,0,2:T(8,128)(2,1)S(1)}, u32[]{:S(2)}, u32[]{:S(2)}) collective-permute-start(f16[2,2,2,32,1024]{4,3,1,0,2:T(8,128)(2,1)S(1)} %fusion.6), channel_id=1, source_target_pairs={{0,4},{4,0},{8,12},{12,8},{1,5},{5,1},{9,13},{13,9},{2,6},{6,2},{1... | collective-permute-start | bytes 1572872 | tf_op jit(solution)/shard_map/ppermute | solution.py:212
  92.9 14.9 %collective-permute-start.27 = (f16[2,2,2,32,1024]{4,3,2,1,0:T(8,128)(2,1)S(1)}, f16[2,2,2,32,1024]{4,3,2,1,0:T(8,128)(2,1)S(1)}, u32[]{:S(2)}, u32[]{:S(2)}) collective-permute-start(f16[2,2,2,32,1024]{4,3,2,1,0:T(8,128)(2,1)S(1)} %fusion.5), channel_id=1, source_target_pairs={{0,8},{8,0},{4,12},{12,4},{1,9},{9,1},{5,13},{13,5},{2,10},{10,2},... | collective-permute-start | bytes 1572872 | tf_op jit(solution)/shard_map/ppermute | solution.py:213
  95.0 15.6 %collective-permute-start.25 = (f16[1,2,32,1024]{3,2,1,0:T(8,128)(2,1)S(1)}, f16[1,2,32,1024]{3,2,1,0:T(8,128)(2,1)S(1)}, u32[]{:S(2)}, u32[]{:S(2)}) collective-permute-start(f16[1,2,32,1024]{3,2,1,0:T(8,128)(2,1)S(1)} %fusion.30), channel_id=1, source_target_pairs={{0,8},{8,0},{4,12},{12,4},{1,9},{9,1},{5,13},{13,5},{2,10},{10,2},... | collective-permute-start | bytes 393224 | tf_op jit(solution)/shard_map/ppermute | solution.py:224
  95.2 15.4 %collective-permute-start.28 = (f16[1,2,32,1024]{3,2,1,0:T(8,128)(2,1)S(1)}, f16[1,2,32,1024]{3,2,1,0:T(8,128)(2,1)S(1)}, u32[]{:S(2)}, u32[]{:S(2)}) collective-permute-start(f16[1,2,32,1024]{3,2,1,0:T(8,128)(2,1)S(1)} %fusion.31), channel_id=1, source_target_pairs={{0,4},{4,0},{8,12},{12,8},{1,5},{5,1},{9,13},{13,9},{2,6},{6,2},{1... | collective-permute-start | bytes 393224 | tf_op jit(solution)/shard_map/ppermute | solution.py:225
  95.8 15.1 %collective-permute-start.29 = (f16[1,32,2048]{2,1,0:T(8,128)(2,1)S(1)}, f16[1,32,2048]{2,1,0:T(8,128)(2,1)S(1)}, u32[]{:S(2)}, u32[]{:S(2)}) collective-permute-start(f16[1,32,2048]{2,1,0:T(8,128)(2,1)S(1)} %get-tuple-element.92), channel_id=1, source_target_pairs={{0,16},{16,0},{1,17},{17,1},{2,18},{18,2},{3,19},{19,3},{4,20},{20... | collective-permute-start | bytes 393224 | tf_op jit(solution)/shard_map/ppermute | solution.py:79
  105.6 8.2 %collective-permute-start.31 = (f16[2,2,32,1024]{3,2,1,0:T(8,128)(2,1)S(1)}, f16[2,2,32,1024]{3,2,1,0:T(8,128)(2,1)S(1)}, u32[]{:S(2)}, u32[]{:S(2)}) collective-permute-start(f16[2,2,32,1024]{3,2,1,0:T(8,128)(2,1)S(1)} %fusion.13), channel_id=1, source_target_pairs={{0,8},{8,0},{4,12},{12,4},{1,9},{9,1},{5,13},{13,5},{2,10},{10,2},... | collective-permute-start | bytes 786440 | tf_op jit(solution)/shard_map/ppermute | solution.py:224
  110.9 8.8 %collective-permute-start.32 = (f16[2,2,32,1024]{3,2,1,0:T(8,128)(2,1)S(1)}, f16[2,2,32,1024]{3,2,1,0:T(8,128)(2,1)S(1)}, u32[]{:S(2)}, u32[]{:S(2)}) collective-permute-start(f16[2,2,32,1024]{3,2,1,0:T(8,128)(2,1)S(1)} %fusion.14), channel_id=1, source_target_pairs={{0,4},{4,0},{8,12},{12,8},{1,5},{5,1},{9,13},{13,9},{2,6},{6,2},{1... | collective-permute-start | bytes 786440 | tf_op jit(solution)/shard_map/ppermute | solution.py:225
  125.9 5.4 %collective-permute-start.34 = (f32[4,64]{1,0:T(4,128)S(1)}, f32[4,64]{1,0:T(4,128)S(1)}, u32[]{:S(2)}, u32[]{:S(2)}) collective-permute-start(f32[4,64]{1,0:T(4,128)S(1)} %get-tuple-element.96), channel_id=1, source_target_pairs={{0,1},{1,2},{2,3},{3,0},{4,5},{5,6},{6,7},{7,4},{8,9},{9,10},{10,1... | collective-permute-start | bytes 3080 | tf_op jit(solution)/shard_map/ppermute | solution.py:48
  (6 other events, 26.7 us)

commit v19 on v17

--- a/solution.py
+++ b/solution.py
@@ -124,11 +124,12 @@
         pairs = [(b * vocab + z, (b ^ 2) * vocab + z) for b in range(4) for z in range(vocab)]
         lone = [b * vocab + (vocab - 1) * (b // 2) for b in range(4)]
         early = [pair for pair in pairs if pair[0] not in lone]
-        got_early = lax.ppermute(quarter(far, 2), ("batch", "vocab"), early)
+        far_sent = quarter(far, 2)
+        got_early = lax.ppermute(far_sent, ("batch", "vocab"), early)
         mine_early = lax.optimization_barrier(quarter(y + 2 * (1 - first), 2))
         is_late = (level == 0) & (y == 1) | (level == vocab - 1) & (y == 0)
         near_part = dot(near, near_weight)
-        sent = after(own, near_weight, far_weight)
+        sent = after(own, below[2], above[2], far_sent)
         ends = []
         for cross in (0, 2):
             moves = []
@@ -136,9 +137,8 @@
                 b, z = divmod(place, vocab)
                 moves.append(((b ^ cross) * vocab + z, b * vocab + vocab - 1 - z))
             ends.append(lax.ppermute(sent, ("batch", "vocab"), sorted(moves)))
-        mine_late, got_late, got_early, _ = lax.optimization_barrier(
-            (ends[0], ends[1], got_early, near_part)
-        )
+        got_early = after(got_early, near_part)
+        mine_late, got_late = after(ends[0], got_early), after(ends[1], got_early)
         far = by_y(
             jnp.where(is_late, mine_late, mine_early), jnp.where(is_late, got_late, got_early), 0
         )

time: 127 us -> 124 us (0.976)
  waiting for transfers between devices: 51.4 us -> 40.2 us
  starting transfers between devices: 47.5 us -> 55.6 us
    ppermute x1, waiting for transfers between devices: 14.6 us -> 0.01 us  [line_parts(): got_early = lax.ppermute(far_sent, ('batch', 'vocab'), early)]
    ppermute x6, starting transfers between devices: 17.5 us -> 9.43 us  [shifted(): lax.ppermute(value, 'vocab', [(i, (i + k) % vocab) for i in range(vocab)])]
    ppermute x2, starting transfers between devices: 3.59 us -> 9.96 us  [line_parts(): ends.append(lax.ppermute(sent, ('batch', 'vocab'), sorted(moves)))]
    ppermute x2, waiting for transfers between devices: 12.9 us -> 8.75 us  [on_device(): away_y = lax.ppermute(sends[i][1], 'batch', Y_SWAP)]
    ppermute x2, starting transfers between devices: 0.3 us -> 4.02 us  [on_device(): next_y = lax.ppermute(more_sends[i][0], 'batch', Y_SWAP)]
    ppermute x1, waiting for transfers between devices: 0.77 us -> 4.37 us  [line_parts(): got_near = lax.ppermute(near_sent, 'batch', Y_SWAP)]
    ppermute x2, waiting for transfers between devices: 1.53 us -> 4.98 us  [line_parts(): ends.append(lax.ppermute(sent, ('batch', 'vocab'), sorted(moves)))]
    ppermute x2, starting transfers between devices: 2.14 us -> 4.83 us  [on_device(): away_y = lax.ppermute(sends[i][1], 'batch', Y_SWAP)]
  transfers between devices with their start and end apart: 30 -> 30, of which waited for: 14 -> 14; matrix products, arithmetic and copies ran while one was open for 19% -> 18% of each run, Pallas kernels for 0% -> 0%
where the time goes in v19:
time: 124 us
  starting transfers between devices  55.6 us (45%)
  waiting for transfers between devices  40.2 us (32%)
  other arithmetic  15.7 us (13%)
  matrix products  9.42 us (8%)
  local copies, waits for them, and re-layouts  1.75 us (1%)
    ppermute x2, starting transfers between devices, line_parts(): ends.append(lax.ppermute(sent, ('batch', 'vocab'), sorted(moves)))  9.96 us
    ppermute x6, starting transfers between devices, shifted(): lax.ppermute(value, 'vocab', [(i, (i + k) % vocab) for i in range(vocab)])  9.43 us
    dot_general x4, matrix products, dot(): jnp.dot(left.reshape(-1, block), weight, preferred_element_type=jnp.float32)  9.42 us
    ppermute x2, waiting for transfers between devices, on_device(): away_y = lax.ppermute(sends[i][1], 'batch', Y_SWAP)  8.75 us
    ppermute x2, waiting for transfers between devices, on_device(): next_x = lax.ppermute(more_sends[i][1], 'batch', X_SWAP)  8.24 us
    ppermute x2, starting transfers between devices, on_device(): next_x = lax.ppermute(more_sends[i][1], 'batch', X_SWAP)  6.55 us
    select_n x1, other arithmetic, line_parts(): jnp.where(keep_near, taken, kept)  5.88 us
    ppermute x2, waiting for transfers between devices, line_parts(): ends.append(lax.ppermute(sent, ('batch', 'vocab'), sorted(moves)))  4.98 us
  transfers between devices with their start and end apart: 30, of which 14 were waited for; matrix products, arithmetic and copies ran while one was open for 18% of the time, Pallas kernels for 0%

profile of v19, /device:TPU:0, one launch (start us, length us, event | category | flops | bytes accessed | tf_op | source)
XLA Modules:
  0.0 123.9 jit_solution(5286044360397147394)
XLA Ops:
  3.0 2.6 %collective-permute-start = (bf16[2,64,1024]{2,1,0:T(8,128)(2,1)S(1)}, bf16[2,64,1024]{2,1,0:T(8,128)(2,1)S(1)}, u32[]{:S(2)}, u32[]{:S(2)}) collective-permute-start(bf16[2,64,1024]{2,1,0:T(8,128)(2,1)S(1)} %constant_dynamic-slice_fusion.6), channel_id=1, source_target_pairs={{0,4},{4,0},{8,12},{12,8},{1,5},{5,1},{9,13},{13,9},{2,6},{6,2},{1... | collective-permute-start | bytes 786440 | tf_op jit(solution)/shard_map/ppermute | solution.py:85
  6.8 1.6 %collective-permute-start.1 = (f32[128]{0:T(128)S(1)}, f32[128]{0:T(128)S(1)}, u32[]{:S(2)}, u32[]{:S(2)}) collective-permute-start(f32[128]{0:T(128)S(1)} %multiply_reduce_fusion), channel_id=1, source_target_pairs={{0,1},{1,2},{2,3},{3,0},{4,5},{5,6},{6,7},{7,4},{8,9},{9,10},{10,1... | collective-permute-start | bytes 1544 | tf_op jit(solution)/shard_map/ppermute | solution.py:44
  8.5 2.6 %collective-permute-start.2 = (f32[128]{0:T(128)S(1)}, f32[128]{0:T(128)S(1)}, u32[]{:S(2)}, u32[]{:S(2)}) collective-permute-start(f32[128]{0:T(128)S(1)} %multiply_reduce_fusion), channel_id=1, source_target_pairs={{0,2},{1,3},{2,0},{3,1},{4,6},{5,7},{6,4},{7,5},{8,10},{9,11},{10,... | collective-permute-start | bytes 1544 | tf_op jit(solution)/shard_map/ppermute | solution.py:44
  12.9 1.7 %collective-permute-done.3 = f32[128]{0:T(128)S(1)} collective-permute-done((f32[128]{0:T(128)S(1)}, f32[128]{0:T(128)S(1)}, u32[]{:S(2)}, u32[]{:S(2)}) %collective-permute-start.3) | collective-permute-done | bytes 544 | tf_op jit(solution)/shard_map/ppermute | solution.py:44
  14.9 2.2 %collective-permute-start.7 = (bf16[2,2,64,1024]{3,2,1,0:T(8,128)(2,1)S(1)}, bf16[2,2,64,1024]{3,2,1,0:T(8,128)(2,1)S(1)}, u32[]{:S(2)}, u32[]{:S(2)}) collective-permute-start(bf16[2,2,64,1024]{3,2,1,0:T(8,128)(2,1)S(1)} %pad_maximum_fusion.2), channel_id=1, source_target_pairs={{0,1},{1,2},{2,3},{4,5},{5,6},{6,7},{8,9},{9,10},{10,11},{12,13},{... | collective-permute-start | bytes 1572872 | tf_op jit(solution)/shard_map/ppermute | solution.py:92
  19.1 4.3 %collective-permute-start.6 = (f32[64]{0:T(128)S(1)}, f32[64]{0:T(128)S(1)}, u32[]{:S(2)}, u32[]{:S(2)}) collective-permute-start(f32[64]{0:T(128)S(1)} %get-tuple-element.76), channel_id=1, source_target_pairs={{0,4},{4,12},{8,20},{12,28},{16,0},{20,8},{24,16},{28,24},{1,5},{5... | collective-permute-start | bytes 776 | tf_op jit(solution)/shard_map/ppermute | solution.py:61
  24.7 2.8 %collective-permute-done.7 = bf16[2,2,64,1024]{3,2,1,0:T(8,128)(2,1)S(1)} collective-permute-done((bf16[2,2,64,1024]{3,2,1,0:T(8,128)(2,1)S(1)}, bf16[2,2,64,1024]{3,2,1,0:T(8,128)(2,1)S(1)}, u32[]{:S(2)}, u32[]{:S(2)}) %collective-permute-start.7) | collective-permute-done | bytes 524320 | tf_op jit(solution)/shard_map/ppermute | solution.py:92
  27.5 4.1 %collective-permute-done.4 = bf16[2,2,64,1024]{3,2,1,0:T(8,128)(2,1)S(1)} collective-permute-done((bf16[2,2,64,1024]{3,2,1,0:T(8,128)(2,1)S(1)}, bf16[2,2,64,1024]{3,2,1,0:T(8,128)(2,1)S(1)}, u32[]{:S(2)}, u32[]{:S(2)}) %collective-permute-start.4) | collective-permute-done | bytes 524320 | tf_op jit(solution)/shard_map/ppermute | solution.py:95
  32.9 1.5 %collective-permute-start.9 = (bf16[2,2,64,1024]{3,2,1,0:T(8,128)(2,1)S(1)}, bf16[2,2,64,1024]{3,2,1,0:T(8,128)(2,1)}, u32[]{:S(2)}, u32[]{:S(2)}) collective-permute-start(bf16[2,2,64,1024]{3,2,1,0:T(8,128)(2,1)S(1)} %collective-permute-done.7), channel_id=1, source_target_pairs={{1,2},{2,3},{5,6},{6,7},{9,10},{10,11},{13,14},{14,15},{17,18},{18... | collective-permute-start | bytes 1572872 | tf_op jit(solution)/shard_map/ppermute | solution.py:92
  34.5 1.6 %collective-permute-start.8 = (bf16[2,2,64,1024]{3,2,1,0:T(8,128)(2,1)S(1)}, bf16[2,2,64,1024]{3,2,1,0:T(8,128)(2,1)S(1)}, u32[]{:S(2)}, u32[]{:S(2)}) collective-permute-start(bf16[2,2,64,1024]{3,2,1,0:T(8,128)(2,1)S(1)} %select_select_fusion.2), channel_id=1, source_target_pairs={{0,8},{8,0},{4,12},{12,4},{1,9},{9,1},{5,13},{13,5},{2,10},{10,2},... | collective-permute-start | bytes 1572872 | tf_op jit(solution)/shard_map/ppermute | solution.py:110
  36.1 5.9 %broadcast_select_fusion = (bf16[1024,2048]{1,0:T(8,128)(2,1)S(1)}, bf16[1024,2048]{1,0:T(8,128)(2,1)S(1)}) fusion(pred[]{:T(512)S(6)} %eq.76, bf16[1024,4096]{1,0:T(8,128)(2,1)} %collective-permute-done.10, s32[]{:T(128)S(6)} %select_n.247, bf16[1024,4096]{1,0:T(8,128)(2,1)} %param.5), kind=kLoop, calls=%fused_computation.2 | loop fusion | flops 4194304 | bytes 16777220 | tf_op jit(solution)/shard_map/jit(_where)/select_n | solution.py:116
  42.0 4.4 %collective-permute-done.8 = bf16[2,2,64,1024]{3,2,1,0:T(8,128)(2,1)S(1)} collective-permute-done((bf16[2,2,64,1024]{3,2,1,0:T(8,128)(2,1)S(1)}, bf16[2,2,64,1024]{3,2,1,0:T(8,128)(2,1)S(1)}, u32[]{:S(2)}, u32[]{:S(2)}) %collective-permute-start.8) | collective-permute-done | bytes 524320 | tf_op jit(solution)/shard_map/ppermute | solution.py:110
  49.6 9.3 %collective-permute-start.12 = (bf16[2,2,64,1024]{3,2,1,0:T(8,128)(2,1)S(1)}, bf16[2,2,64,1024]{3,2,1,0:T(8,128)(2,1)S(1)}, u32[]{:S(2)}, u32[]{:S(2)}) collective-permute-start(bf16[2,2,64,1024]{3,2,1,0:T(8,128)(2,1)S(1)} %pad_maximum_fusion.2), channel_id=1, source_target_pairs={{0,3},{4,7},{11,8},{15,12},{16,19},{20,23},{27,24},{31,28}} | collective-permute-start | bytes 1572872 | tf_op jit(solution)/shard_map/ppermute | solution.py:139
  59.2 2.3 %fusion.36 = f32[512,2048]{1,0:T(8,128)S(1)} fusion(bf16[512,1024]{1,0:T(8,128)(2,1)S(1)} %bitcast.116, bf16[1024,2048]{1,0:T(8,128)(2,1)S(1)} %get-tuple-element.26), kind=kOutput, calls=%fused_computation.111 | convolution fusion | flops 2147483648 | bytes 9437184 | tf_op jit(solution)/shard_map/dot_general | solution.py:81
  61.5 5.0 %collective-permute-done.12 = bf16[2,2,64,1024]{3,2,1,0:T(8,128)(2,1)S(1)} collective-permute-done((bf16[2,2,64,1024]{3,2,1,0:T(8,128)(2,1)S(1)}, bf16[2,2,64,1024]{3,2,1,0:T(8,128)(2,1)S(1)}, u32[]{:S(2)}, u32[]{:S(2)}) %collective-permute-start.12) | collective-permute-done | bytes 524320 | tf_op jit(solution)/shard_map/ppermute | solution.py:139
  66.8 2.4 %add_multiply_fusion.1 = f32[512,2048]{1,0:T(8,128)S(1)} fusion(f32[512,2048]{1,0:T(8,128)S(1)} %fusion.36, bf16[512,1024]{1,0:T(8,128)(2,1)S(1)} %bitcast.117, bf16[1024,2048]{1,0:T(8,128)(2,1)S(1)} %get-tuple-element.27), kind=kOutput, calls=%fused_computation.1 | convolution fusion | flops 2149580800 | bytes 13631488 | tf_op jit(solution)/shard_map/dot_general | solution.py:81
  69.9 4.7 %collective-permute-start.21 = (f16[2,2,64,1024]{3,2,1,0:T(8,128)(2,1)S(1)}, f16[2,2,64,1024]{3,2,1,0:T(8,128)(2,1)S(1)}, u32[]{:S(2)}, u32[]{:S(2)}) collective-permute-start(f16[2,2,64,1024]{3,2,1,0:T(8,128)(2,1)S(1)} %fusion.4), channel_id=1, source_target_pairs={{0,8},{8,0},{4,12},{12,4},{1,9},{9,1},{5,13},{13,5},{2,10},{10,2},... | collective-permute-start | bytes 1572872 | tf_op jit(solution)/shard_map/ppermute | solution.py:182
  75.0 3.3 %collective-permute-start.15 = (f16[2,2,64,1024]{3,2,0,1:T(8,128)(2,1)S(1)}, f16[2,2,64,1024]{3,2,0,1:T(8,128)(2,1)S(1)}, u32[]{:S(2)}, u32[]{:S(2)}) collective-permute-start(f16[2,2,64,1024]{3,2,0,1:T(8,128)(2,1)S(1)} %fusion.6), channel_id=1, source_target_pairs={{0,4},{4,0},{8,12},{12,8},{1,5},{5,1},{9,13},{13,9},{2,6},{6,2},{1... | collective-permute-start | bytes 1572872 | tf_op jit(solution)/shard_map/ppermute | solution.py:181
  78.2 2.3 %fusion.37 = f32[512,2048]{1,0:T(8,128)S(1)} fusion(bf16[512,1024]{1,0:T(8,128)(2,1)S(1)} %bitcast.126, bf16[1024,2048]{1,0:T(8,128)(2,1)S(1)} %get-tuple-element.27), kind=kOutput, calls=%fused_computation.112 | convolution fusion | flops 2147483648 | bytes 9437184 | tf_op jit(solution)/shard_map/dot_general | solution.py:81
  80.6 2.3 %add_multiply_fusion = f32[512,2048]{1,0:T(8,128)S(1)} fusion(f32[512,2048]{1,0:T(8,128)S(1)} %fusion.37, bf16[512,1024]{1,0:T(8,128)(2,1)S(1)} %bitcast.125, bf16[1024,2048]{1,0:T(8,128)(2,1)S(1)} %get-tuple-element.26), kind=kOutput, calls=%fused_computation | convolution fusion | flops 2149580800 | bytes 13631488 | tf_op jit(solution)/shard_map/dot_general | solution.py:81
  84.1 3.3 %collective-permute-done.21 = f16[2,2,64,1024]{3,2,1,0:T(8,128)(2,1)S(1)} collective-permute-done((f16[2,2,64,1024]{3,2,1,0:T(8,128)(2,1)S(1)}, f16[2,2,64,1024]{3,2,1,0:T(8,128)(2,1)S(1)}, u32[]{:S(2)}, u32[]{:S(2)}) %collective-permute-start.21) | collective-permute-done | bytes 524320 | tf_op jit(solution)/shard_map/ppermute | solution.py:182
  87.7 3.3 %collective-permute-start.22 = (f16[2,64,1024]{2,1,0:T(8,128)(2,1)S(1)}, f16[2,64,1024]{2,1,0:T(8,128)(2,1)S(1)}, u32[]{:S(2)}, u32[]{:S(2)}) collective-permute-start(f16[2,64,1024]{2,1,0:T(8,128)(2,1)S(1)} %fusion.15), channel_id=1, source_target_pairs={{0,4},{4,0},{8,12},{12,8},{1,5},{5,1},{9,13},{13,9},{2,6},{6,2},{1... | collective-permute-start | bytes 786440 | tf_op jit(solution)/shard_map/ppermute | solution.py:194
  91.2 2.0 %collective-permute-start.18 = (f16[2,64,1024]{2,1,0:T(8,128)(2,1)S(1)}, f16[2,64,1024]{2,1,0:T(8,128)(2,1)S(1)}, u32[]{:S(2)}, u32[]{:S(2)}) collective-permute-start(f16[2,64,1024]{2,1,0:T(8,128)(2,1)S(1)} %fusion.12), channel_id=1, source_target_pairs={{0,8},{8,0},{4,12},{12,4},{1,9},{9,1},{5,13},{13,5},{2,10},{10,2},... | collective-permute-start | bytes 786440 | tf_op jit(solution)/shard_map/ppermute | solution.py:193
  93.2 5.5 %collective-permute-done.20 = f16[2,2,64,1024]{3,2,1,0:T(8,128)(2,1)S(1)} collective-permute-done((f16[2,2,64,1024]{3,2,1,0:T(8,128)(2,1)S(1)}, f16[2,2,64,1024]{3,2,1,0:T(8,128)(2,1)S(1)}, u32[]{:S(2)}, u32[]{:S(2)}) %collective-permute-start.20) | collective-permute-done | bytes 524320 | tf_op jit(solution)/shard_map/ppermute | solution.py:182
  98.9 3.3 %collective-permute-start.25 = (f16[2,64,1024]{2,1,0:T(8,128)(2,1)S(1)}, f16[2,64,1024]{2,1,0:T(8,128)(2,1)S(1)}, u32[]{:S(2)}, u32[]{:S(2)}) collective-permute-start(f16[2,64,1024]{2,1,0:T(8,128)(2,1)S(1)} %fusion.14), channel_id=1, source_target_pairs={{0,4},{4,0},{8,12},{12,8},{1,5},{5,1},{9,13},{13,9},{2,6},{6,2},{1... | collective-permute-start | bytes 786440 | tf_op jit(solution)/shard_map/ppermute | solution.py:194
  102.4 2.0 %collective-permute-start.24 = (f16[2,64,1024]{2,1,0:T(8,128)(2,1)S(1)}, f16[2,64,1024]{2,1,0:T(8,128)(2,1)S(1)}, u32[]{:S(2)}, u32[]{:S(2)}) collective-permute-start(f16[2,64,1024]{2,1,0:T(8,128)(2,1)S(1)} %fusion.13), channel_id=1, source_target_pairs={{0,8},{8,0},{4,12},{12,4},{1,9},{9,1},{5,13},{13,5},{2,10},{10,2},... | collective-permute-start | bytes 786440 | tf_op jit(solution)/shard_map/ppermute | solution.py:193
  104.4 3.4 %collective-permute-done.22 = f16[2,64,1024]{2,1,0:T(8,128)(2,1)S(1)} collective-permute-done((f16[2,64,1024]{2,1,0:T(8,128)(2,1)S(1)}, f16[2,64,1024]{2,1,0:T(8,128)(2,1)S(1)}, u32[]{:S(2)}, u32[]{:S(2)}) %collective-permute-start.22) | collective-permute-done | bytes 262176 | tf_op jit(solution)/shard_map/ppermute | solution.py:194
  108.1 4.9 %collective-permute-done.25 = f16[2,64,1024]{2,1,0:T(8,128)(2,1)S(1)} collective-permute-done((f16[2,64,1024]{2,1,0:T(8,128)(2,1)S(1)}, f16[2,64,1024]{2,1,0:T(8,128)(2,1)S(1)}, u32[]{:S(2)}, u32[]{:S(2)}) %collective-permute-start.25) | collective-permute-done | bytes 262176 | tf_op jit(solution)/shard_map/ppermute | solution.py:194
  113.5 1.4 %collective-permute-done.26 = f16[64,2048]{1,0:T(8,128)(2,1)S(1)} collective-permute-done((f16[64,2048]{1,0:T(8,128)(2,1)S(1)}, f16[64,2048]{1,0:T(8,128)(2,1)S(1)}, u32[]{:S(2)}, u32[]{:S(2)}) %collective-permute-start.26) | collective-permute-done | bytes 262176 | tf_op jit(solution)/shard_map/ppermute | solution.py:75
  116.4 3.7 %collective-permute-start.29 = (f32[4,64]{1,0:T(4,128)S(1)}, f32[4,64]{1,0:T(4,128)S(1)}, u32[]{:S(2)}, u32[]{:S(2)}) collective-permute-start(f32[4,64]{1,0:T(4,128)S(1)} %get-tuple-element.68), channel_id=1, source_target_pairs={{0,3},{1,0},{2,1},{3,2},{4,7},{5,4},{6,5},{7,6},{8,11},{9,8},{10,9... | collective-permute-start | bytes 3080 | tf_op jit(solution)/shard_map/ppermute | solution.py:44
  120.1 1.6 %collective-permute-done.27 = f32[4,64]{1,0:T(4,128)S(1)} collective-permute-done((f32[4,64]{1,0:T(4,128)S(1)}, f32[4,64]{1,0:T(4,128)S(1)}, u32[]{:S(2)}, u32[]{:S(2)}) %collective-permute-start.27) | collective-permute-done | bytes 1056 | tf_op jit(solution)/shard_map/ppermute | solution.py:44
  122.3 1.6 %fusion.2 = (f32[64,4096]{1,0:T(8,128)}, f32[64,4096]{1,0:T(8,128)}) fusion(f32[64]{0:T(128)S(1)} %get-tuple-element.69, f32[64]{0:T(128)S(1)} %get-tuple-element.71, f16[64,2048]{1,0:T(8,128)(2,1)S(1)} %get-tuple-element.62, f16[64,2048]{1,0:T(8,128)(2,1)S(1)} %get-tuple-element.60, f32[64,4096]{1,0:T(8,128)S(1)} %get-tuple-element.41, ...), kind=kLoop, calls=%fused_computation.18 | loop fusion | flops 1310720 | bytes 3670784 | tf_op jit(solution)/shard_map/sub | solution.py:232
  (85 shorter events, 20.1 us)
Async XLA Ops:
  0.6 35.5 %collective-permute-start.10 = (bf16[1024,4096]{1,0:T(8,128)(2,1)}, bf16[1024,4096]{1,0:T(8,128)(2,1)}, u32[]{:S(2)}, u32[]{:S(2)}) collective-permute-start(bf16[1024,4096]{1,0:T(8,128)(2,1)} %param.5), channel_id=1, source_target_pairs={{0,16},{16,0},{1,17},{17,1},{2,18},{18,2},{3,19},{19,3},{4,20},{20... | collective-permute-start | bytes 25165832 | tf_op jit(solution)/shard_map/ppermute | solution.py:41
  3.0 11.7 %collective-permute-start = (bf16[2,64,1024]{2,1,0:T(8,128)(2,1)S(1)}, bf16[2,64,1024]{2,1,0:T(8,128)(2,1)S(1)}, u32[]{:S(2)}, u32[]{:S(2)}) collective-permute-start(bf16[2,64,1024]{2,1,0:T(8,128)(2,1)S(1)} %constant_dynamic-slice_fusion.6), channel_id=1, source_target_pairs={{0,4},{4,0},{8,12},{12,8},{1,5},{5,1},{9,13},{13,9},{2,6},{6,2},{1... | collective-permute-start | bytes 786440 | tf_op jit(solution)/shard_map/ppermute | solution.py:85
  6.8 5.6 %collective-permute-start.1 = (f32[128]{0:T(128)S(1)}, f32[128]{0:T(128)S(1)}, u32[]{:S(2)}, u32[]{:S(2)}) collective-permute-start(f32[128]{0:T(128)S(1)} %multiply_reduce_fusion), channel_id=1, source_target_pairs={{0,1},{1,2},{2,3},{3,0},{4,5},{5,6},{6,7},{7,4},{8,9},{9,10},{10,1... | collective-permute-start | bytes 1544 | tf_op jit(solution)/shard_map/ppermute | solution.py:44
  8.5 4.4 %collective-permute-start.2 = (f32[128]{0:T(128)S(1)}, f32[128]{0:T(128)S(1)}, u32[]{:S(2)}, u32[]{:S(2)}) collective-permute-start(f32[128]{0:T(128)S(1)} %multiply_reduce_fusion), channel_id=1, source_target_pairs={{0,2},{1,3},{2,0},{3,1},{4,6},{5,7},{6,4},{7,5},{8,10},{9,11},{10,... | collective-permute-start | bytes 1544 | tf_op jit(solution)/shard_map/ppermute | solution.py:44
  11.0 3.5 %collective-permute-start.3 = (f32[128]{0:T(128)S(1)}, f32[128]{0:T(128)S(1)}, u32[]{:S(2)}, u32[]{:S(2)}) collective-permute-start(f32[128]{0:T(128)S(1)} %multiply_reduce_fusion), channel_id=1, source_target_pairs={{0,3},{1,0},{2,1},{3,2},{4,7},{5,4},{6,5},{7,6},{8,11},{9,8},{10,9... | collective-permute-start | bytes 1544 | tf_op jit(solution)/shard_map/ppermute | solution.py:44
  14.9 12.6 %collective-permute-start.7 = (bf16[2,2,64,1024]{3,2,1,0:T(8,128)(2,1)S(1)}, bf16[2,2,64,1024]{3,2,1,0:T(8,128)(2,1)S(1)}, u32[]{:S(2)}, u32[]{:S(2)}) collective-permute-start(bf16[2,2,64,1024]{3,2,1,0:T(8,128)(2,1)S(1)} %pad_maximum_fusion.2), channel_id=1, source_target_pairs={{0,1},{1,2},{2,3},{4,5},{5,6},{6,7},{8,9},{9,10},{10,11},{12,13},{... | collective-permute-start | bytes 1572872 | tf_op jit(solution)/shard_map/ppermute | solution.py:92
  17.0 14.6 %collective-permute-start.4 = (bf16[2,2,64,1024]{3,2,1,0:T(8,128)(2,1)S(1)}, bf16[2,2,64,1024]{3,2,1,0:T(8,128)(2,1)S(1)}, u32[]{:S(2)}, u32[]{:S(2)}) collective-permute-start(bf16[2,2,64,1024]{3,2,1,0:T(8,128)(2,1)S(1)} %pad_maximum_fusion.2), channel_id=1, source_target_pairs={{1,0},{2,1},{3,2},{5,4},{6,5},{7,6},{9,8},{10,9},{11,10},{13,12},{... | collective-permute-start | bytes 1572872 | tf_op jit(solution)/shard_map/ppermute | solution.py:95
  18.5 5.0 %collective-permute-start.5 = (f32[64]{0:T(128)S(1)}, f32[64]{0:T(128)S(1)}, u32[]{:S(2)}, u32[]{:S(2)}) collective-permute-start(f32[64]{0:T(128)S(1)} %get-tuple-element.75), channel_id=1, source_target_pairs={{0,0},{4,8},{8,16},{12,24},{16,4},{20,12},{24,20},{28,28},{1,1},{5... | collective-permute-start | bytes 776 | tf_op jit(solution)/shard_map/ppermute | solution.py:61
  19.1 5.6 %collective-permute-start.6 = (f32[64]{0:T(128)S(1)}, f32[64]{0:T(128)S(1)}, u32[]{:S(2)}, u32[]{:S(2)}) collective-permute-start(f32[64]{0:T(128)S(1)} %get-tuple-element.76), channel_id=1, source_target_pairs={{0,4},{4,12},{8,20},{12,28},{16,0},{20,8},{24,16},{28,24},{1,5},{5... | collective-permute-start | bytes 776 | tf_op jit(solution)/shard_map/ppermute | solution.py:61
  31.6 14.7 %collective-permute-start.11 = (bf16[2,2,64,1024]{3,2,1,0:T(8,128)(2,1)S(1)}, bf16[2,2,64,1024]{3,2,1,0:T(8,128)(2,1)S(1)}, u32[]{:S(2)}, u32[]{:S(2)}) collective-permute-start(bf16[2,2,64,1024]{3,2,1,0:T(8,128)(2,1)S(1)} %collective-permute-done.4), channel_id=1, source_target_pairs={{1,0},{2,1},{5,4},{6,5},{9,8},{10,9},{13,12},{14,13},{17,16},{18,1... | collective-permute-start | bytes 1572872 | tf_op jit(solution)/shard_map/ppermute | solution.py:95
  32.9 13.5 %collective-permute-start.9 = (bf16[2,2,64,1024]{3,2,1,0:T(8,128)(2,1)S(1)}, bf16[2,2,64,1024]{3,2,1,0:T(8,128)(2,1)}, u32[]{:S(2)}, u32[]{:S(2)}) collective-permute-start(bf16[2,2,64,1024]{3,2,1,0:T(8,128)(2,1)S(1)} %collective-permute-done.7), channel_id=1, source_target_pairs={{1,2},{2,3},{5,6},{6,7},{9,10},{10,11},{13,14},{14,15},{17,18},{18... | collective-permute-start | bytes 1572872 | tf_op jit(solution)/shard_map/ppermute | solution.py:92
  34.5 11.8 %collective-permute-start.8 = (bf16[2,2,64,1024]{3,2,1,0:T(8,128)(2,1)S(1)}, bf16[2,2,64,1024]{3,2,1,0:T(8,128)(2,1)S(1)}, u32[]{:S(2)}, u32[]{:S(2)}) collective-permute-start(bf16[2,2,64,1024]{3,2,1,0:T(8,128)(2,1)S(1)} %select_select_fusion.2), channel_id=1, source_target_pairs={{0,8},{8,0},{4,12},{12,4},{1,9},{9,1},{5,13},{13,5},{2,10},{10,2},... | collective-permute-start | bytes 1572872 | tf_op jit(solution)/shard_map/ppermute | solution.py:110
  47.6 13.9 %collective-permute-start.13 = (bf16[2,2,64,1024]{3,2,1,0:T(8,128)(2,1)S(1)}, bf16[2,2,64,1024]{3,2,1,0:T(8,128)(2,1)S(1)}, u32[]{:S(2)}, u32[]{:S(2)}) collective-permute-start(bf16[2,2,64,1024]{3,2,1,0:T(8,128)(2,1)S(1)} %get-tuple-element.51), channel_id=1, source_target_pairs={{1,9},{2,10},{3,11},{5,13},{6,14},{7,15},{8,0},{9,1},{10,2},{12,4}... | collective-permute-start | bytes 1572872 | tf_op jit(solution)/shard_map/ppermute | solution.py:128
  48.9 12.6 %collective-permute-start.14 = (bf16[2,2,64,1024]{3,2,1,0:T(8,128)(2,1)S(1)}, bf16[2,2,64,1024]{3,2,1,0:T(8,128)(2,1)S(1)}, u32[]{:S(2)}, u32[]{:S(2)}) collective-permute-start(bf16[2,2,64,1024]{3,2,1,0:T(8,128)(2,1)S(1)} %pad_maximum_fusion.2), channel_id=1, source_target_pairs={{3,8},{7,12},{8,3},{12,7},{19,24},{23,28},{24,19},{28,23}} | collective-permute-start | bytes 1572872 | tf_op jit(solution)/shard_map/ppermute | solution.py:139
  49.6 16.9 %collective-permute-start.12 = (bf16[2,2,64,1024]{3,2,1,0:T(8,128)(2,1)S(1)}, bf16[2,2,64,1024]{3,2,1,0:T(8,128)(2,1)S(1)}, u32[]{:S(2)}, u32[]{:S(2)}) collective-permute-start(bf16[2,2,64,1024]{3,2,1,0:T(8,128)(2,1)S(1)} %pad_maximum_fusion.2), channel_id=1, source_target_pairs={{0,3},{4,7},{11,8},{15,12},{16,19},{20,23},{27,24},{31,28}} | collective-permute-start | bytes 1572872 | tf_op jit(solution)/shard_map/ppermute | solution.py:139
  59.1 21.5 %collective-permute-start.16 = (bf16[2,2,2,64,1024]{4,3,2,1,0:T(8,128)(2,1)S(1)}, bf16[2,2,2,64,1024]{4,3,2,1,0:T(8,128)(2,1)S(1)}, u32[]{:S(2)}, u32[]{:S(2)}) collective-permute-start(bf16[2,2,2,64,1024]{4,3,2,1,0:T(8,128)(2,1)S(1)} %pad_maximum_fusion), channel_id=1, source_target_pairs={{0,16},{16,0},{1,17},{17,1},{2,18},{18,2},{3,19},{19,3},{4,20},{20... | collective-permute-start | bytes 3145736 | tf_op jit(solution)/shard_map/ppermute | solution.py:75
  66.7 11.5 %collective-permute-start.17 = (bf16[2,2,2,64,1024]{4,3,2,1,0:T(8,128)(2,1)S(1)}, bf16[2,2,2,64,1024]{4,3,2,1,0:T(8,128)(2,1)S(1)}, u32[]{:S(2)}, u32[]{:S(2)}) collective-permute-start(bf16[2,2,2,64,1024]{4,3,2,1,0:T(8,128)(2,1)S(1)} %pad_maximum_fusion.1), channel_id=1, source_target_pairs={{0,16},{16,0},{1,17},{17,1},{2,18},{18,2},{3,19},{19,3},{4,20},{20... | collective-permute-start | bytes 3145736 | tf_op jit(solution)/shard_map/ppermute | solution.py:75
  69.9 17.5 %collective-permute-start.21 = (f16[2,2,64,1024]{3,2,1,0:T(8,128)(2,1)S(1)}, f16[2,2,64,1024]{3,2,1,0:T(8,128)(2,1)S(1)}, u32[]{:S(2)}, u32[]{:S(2)}) collective-permute-start(f16[2,2,64,1024]{3,2,1,0:T(8,128)(2,1)S(1)} %fusion.4), channel_id=1, source_target_pairs={{0,8},{8,0},{4,12},{12,4},{1,9},{9,1},{5,13},{13,5},{2,10},{10,2},... | collective-permute-start | bytes 1572872 | tf_op jit(solution)/shard_map/ppermute | solution.py:182
  75.0 16.0 %collective-permute-start.15 = (f16[2,2,64,1024]{3,2,0,1:T(8,128)(2,1)S(1)}, f16[2,2,64,1024]{3,2,0,1:T(8,128)(2,1)S(1)}, u32[]{:S(2)}, u32[]{:S(2)}) collective-permute-start(f16[2,2,64,1024]{3,2,0,1:T(8,128)(2,1)S(1)} %fusion.6), channel_id=1, source_target_pairs={{0,4},{4,0},{8,12},{12,8},{1,5},{5,1},{9,13},{13,9},{2,6},{6,2},{1... | collective-permute-start | bytes 1572872 | tf_op jit(solution)/shard_map/ppermute | solution.py:181
  83.6 15.0 %collective-permute-start.20 = (f16[2,2,64,1024]{3,2,1,0:T(8,128)(2,1)S(1)}, f16[2,2,64,1024]{3,2,1,0:T(8,128)(2,1)S(1)}, u32[]{:S(2)}, u32[]{:S(2)}) collective-permute-start(f16[2,2,64,1024]{3,2,1,0:T(8,128)(2,1)S(1)} %fusion.5), channel_id=1, source_target_pairs={{0,8},{8,0},{4,12},{12,4},{1,9},{9,1},{5,13},{13,5},{2,10},{10,2},... | collective-permute-start | bytes 1572872 | tf_op jit(solution)/shard_map/ppermute | solution.py:182
  84.0 18.1 %collective-permute-start.19 = (f16[2,2,64,1024]{3,2,0,1:T(8,128)(2,1)S(1)}, f16[2,2,64,1024]{3,2,0,1:T(8,128)(2,1)S(1)}, u32[]{:S(2)}, u32[]{:S(2)}) collective-permute-start(f16[2,2,64,1024]{3,2,0,1:T(8,128)(2,1)S(1)} %fusion.7), channel_id=1, source_target_pairs={{0,4},{4,0},{8,12},{12,8},{1,5},{5,1},{9,13},{13,9},{2,6},{6,2},{1... | collective-permute-start | bytes 1572872 | tf_op jit(solution)/shard_map/ppermute | solution.py:181
  87.7 20.1 %collective-permute-start.22 = (f16[2,64,1024]{2,1,0:T(8,128)(2,1)S(1)}, f16[2,64,1024]{2,1,0:T(8,128)(2,1)S(1)}, u32[]{:S(2)}, u32[]{:S(2)}) collective-permute-start(f16[2,64,1024]{2,1,0:T(8,128)(2,1)S(1)} %fusion.15), channel_id=1, source_target_pairs={{0,4},{4,0},{8,12},{12,8},{1,5},{5,1},{9,13},{13,9},{2,6},{6,2},{1... | collective-permute-start | bytes 786440 | tf_op jit(solution)/shard_map/ppermute | solution.py:194
  91.2 16.7 %collective-permute-start.18 = (f16[2,64,1024]{2,1,0:T(8,128)(2,1)S(1)}, f16[2,64,1024]{2,1,0:T(8,128)(2,1)S(1)}, u32[]{:S(2)}, u32[]{:S(2)}) collective-permute-start(f16[2,64,1024]{2,1,0:T(8,128)(2,1)S(1)} %fusion.12), channel_id=1, source_target_pairs={{0,8},{8,0},{4,12},{12,4},{1,9},{9,1},{5,13},{13,5},{2,10},{10,2},... | collective-permute-start | bytes 786440 | tf_op jit(solution)/shard_map/ppermute | solution.py:193
  98.9 14.1 %collective-permute-start.25 = (f16[2,64,1024]{2,1,0:T(8,128)(2,1)S(1)}, f16[2,64,1024]{2,1,0:T(8,128)(2,1)S(1)}, u32[]{:S(2)}, u32[]{:S(2)}) collective-permute-start(f16[2,64,1024]{2,1,0:T(8,128)(2,1)S(1)} %fusion.14), channel_id=1, source_target_pairs={{0,4},{4,0},{8,12},{12,8},{1,5},{5,1},{9,13},{13,9},{2,6},{6,2},{1... | collective-permute-start | bytes 786440 | tf_op jit(solution)/shard_map/ppermute | solution.py:194
  102.4 10.7 %collective-permute-start.24 = (f16[2,64,1024]{2,1,0:T(8,128)(2,1)S(1)}, f16[2,64,1024]{2,1,0:T(8,128)(2,1)S(1)}, u32[]{:S(2)}, u32[]{:S(2)}) collective-permute-start(f16[2,64,1024]{2,1,0:T(8,128)(2,1)S(1)} %fusion.13), channel_id=1, source_target_pairs={{0,8},{8,0},{4,12},{12,4},{1,9},{9,1},{5,13},{13,5},{2,10},{10,2},... | collective-permute-start | bytes 786440 | tf_op jit(solution)/shard_map/ppermute | solution.py:193
  108.0 5.3 %collective-permute-start.23 = (f16[64,2048]{1,0:T(8,128)(2,1)S(1)}, f16[64,2048]{1,0:T(8,128)(2,1)S(1)}, u32[]{:S(2)}, u32[]{:S(2)}) collective-permute-start(f16[64,2048]{1,0:T(8,128)(2,1)S(1)} %fusion.21), channel_id=1, source_target_pairs={{0,16},{16,0},{1,17},{17,1},{2,18},{18,2},{3,19},{19,3},{4,20},{20... | collective-permute-start | bytes 786440 | tf_op jit(solution)/shard_map/ppermute | solution.py:75
  113.3 1.6 %collective-permute-start.26 = (f16[64,2048]{1,0:T(8,128)(2,1)S(1)}, f16[64,2048]{1,0:T(8,128)(2,1)S(1)}, u32[]{:S(2)}, u32[]{:S(2)}) collective-permute-start(f16[64,2048]{1,0:T(8,128)(2,1)S(1)} %fusion.19), channel_id=1, source_target_pairs={{0,16},{16,0},{1,17},{17,1},{2,18},{18,2},{3,19},{19,3},{4,20},{20... | collective-permute-start | bytes 786440 | tf_op jit(solution)/shard_map/ppermute | solution.py:75
  116.3 5.4 %collective-permute-start.27 = (f32[4,64]{1,0:T(4,128)S(1)}, f32[4,64]{1,0:T(4,128)S(1)}, u32[]{:S(2)}, u32[]{:S(2)}) collective-permute-start(f32[4,64]{1,0:T(4,128)S(1)} %get-tuple-element.68), channel_id=1, source_target_pairs={{0,1},{1,2},{2,3},{3,0},{4,5},{5,6},{6,7},{7,4},{8,9},{9,10},{10,1... | collective-permute-start | bytes 3080 | tf_op jit(solution)/shard_map/ppermute | solution.py:44
  116.3 5.4 %collective-permute-start.28 = (f32[4,64]{1,0:T(4,128)S(1)}, f32[4,64]{1,0:T(4,128)S(1)}, u32[]{:S(2)}, u32[]{:S(2)}) collective-permute-start(f32[4,64]{1,0:T(4,128)S(1)} %get-tuple-element.68), channel_id=1, source_target_pairs={{0,2},{1,3},{2,0},{3,1},{4,6},{5,7},{6,4},{7,5},{8,10},{9,11},{10,... | collective-permute-start | bytes 3080 | tf_op jit(solution)/shard_map/ppermute | solution.py:44
  116.4 5.8 %collective-permute-start.29 = (f32[4,64]{1,0:T(4,128)S(1)}, f32[4,64]{1,0:T(4,128)S(1)}, u32[]{:S(2)}, u32[]{:S(2)}) collective-permute-start(f32[4,64]{1,0:T(4,128)S(1)} %get-tuple-element.68), channel_id=1, source_target_pairs={{0,3},{1,0},{2,1},{3,2},{4,7},{5,4},{6,5},{7,6},{8,11},{9,8},{10,9... | collective-permute-start | bytes 3080 | tf_op jit(solution)/shard_map/ppermute | solution.py:44

commit v20 on v19

--- a/solution.py
+++ b/solution.py
@@ -46,18 +46,10 @@
     def paired(value, reach):
         return lax.ppermute(value, "vocab", [(i, i ^ reach) for i in range(vocab)])
 
-    squares = jnp.sum(wide * wide, axis=1)
-    if vocab == 4:
-        squares += sum(shifted(squares, k) for k in range(1, vocab))
-    else:
-        reach = 1
-        while reach < vocab:
-            squares += paired(squares, reach)
-            reach *= 2
-    squares = squares.reshape(2, seg)
-
-    def row_scale(*earlier):
-        sent = [
+    squares = jnp.sum(wide * wide, axis=1).reshape(2, seg)
+
+    def row_squares(*earlier):
+        ending = [
             lax.ppermute(
                 pick(after(squares, *earlier), core ^ k, 0),
                 ("pair", "batch"),
@@ -65,7 +57,18 @@
             )
             for k in range(2)
         ]
-        total = jnp.stack([jnp.where(x == 0, sent[0], sent[1]), jnp.where(x == 0, sent[1], sent[0])])
+        return jnp.stack(
+            [jnp.where(x == 0, ending[0], ending[1]), jnp.where(x == 0, ending[1], ending[0])]
+        )
+
+    def row_scale(total):
+        if vocab == 4:
+            total += sum(shifted(total, k) for k in range(1, vocab))
+        else:
+            reach = 1
+            while reach < vocab:
+                total += paired(total, reach)
+                reach *= 2
         return lax.rsqrt(total / model + EPS) / SHRINK
 
     def by_y(mine, other, axis):
@@ -86,7 +89,6 @@
             lax.dynamic_slice_in_dim(gained, (1 - x) * block, block, 2), "batch", X_SWAP
         )
         own = jnp.stack([jnp.where(x == 0, mine, other), jnp.where(x == 0, other, mine)])
-        own = after(own, squares)
 
         def up(value, k):
             return lax.ppermute(value, "vocab", [(z, z + 1) for z in range(k - 1, vocab - 1)])
@@ -104,8 +106,8 @@
             return part
 
         first = level // 2
-        scale = row_scale(own)
-        below[1], above[1] = after(below[1], scale), after(above[1], scale)
+        ending = row_squares(own)
+        below[1], above[1] = after(below[1], ending), after(above[1], ending)
         near_sent = quarter(1 - y + 2 * first, 1)
         got_near = lax.ppermute(near_sent, "batch", Y_SWAP)
         below.append(up(below[1], 2))
@@ -115,7 +117,7 @@
         near_weight, far_weight = lax.optimization_barrier(
             (jnp.where(keep_near, kept, taken), jnp.where(keep_near, taken, kept))
         )
-        ready = (got_near, near_weight, far_weight)
+        ready = (near_weight, far_weight)
         below[2], above[2] = after(below[2], *ready), after(above[2], *ready)
         near = by_y(quarter(y + 2 * first, 1), after(got_near, below[2], above[2]), 0)
         swapped_near = swapped(near)
@@ -129,7 +131,7 @@
         mine_early = lax.optimization_barrier(quarter(y + 2 * (1 - first), 2))
         is_late = (level == 0) & (y == 1) | (level == vocab - 1) & (y == 0)
         near_part = dot(near, near_weight)
-        sent = after(own, below[2], above[2], far_sent)
+        sent = after(own, below[2], above[2])
         ends = []
         for cross in (0, 2):
             moves = []
@@ -137,8 +139,10 @@
                 b, z = divmod(place, vocab)
                 moves.append(((b ^ cross) * vocab + z, b * vocab + vocab - 1 - z))
             ends.append(lax.ppermute(sent, ("batch", "vocab"), sorted(moves)))
-        got_early = after(got_early, near_part)
-        mine_late, got_late = after(ends[0], got_early), after(ends[1], got_early)
+        scale = row_scale(after(ending, far_sent))
+        mine_late, got_late, got_early, _, _ = lax.optimization_barrier(
+            (ends[0], ends[1], got_early, near_part, scale)
+        )
         far = by_y(
             jnp.where(is_late, mine_late, mine_early), jnp.where(is_late, got_late, got_early), 0
         )
@@ -164,7 +168,7 @@
         def part(left):
             return dot(pick(left, core, 0), near_weight) + dot(pick(left, 1 - core, 0), far_weight)
 
-        return (lambda: part(whole), lambda *earlier: part(after(swapped_whole, *earlier))), row_scale()
+        return (lambda: part(whole), lambda *earlier: part(after(swapped_whole, *earlier))), row_scale(row_squares())
 
     lined = depth == 2 * block and vocab == 4
     parts, scale = line_parts() if lined else gathered_parts()

time: 124 us -> 124 us (level)
  waiting for transfers between devices: 40.2 us -> 54.5 us
  starting transfers between devices: 55.6 us -> 42.2 us
    ppermute x2, waiting for transfers between devices: 4.15 us -> 11.9 us  [down(): return lax.ppermute(value, 'vocab', [(z + 1, z) for z in range(vocab - k)])]
    ppermute x1, waiting for transfers between devices: 0.01 us -> 6.9 us  [line_parts(): lax.ppermute(lax.dynamic_slice_in_dim(gained, (1 - x) * block, block, 2),...]
    ppermute x2, waiting for transfers between devices: 4.98 us -> 0.01 us  [line_parts(): ends.append(lax.ppermute(sent, ('batch', 'vocab'), sorted(moves)))]
    ppermute x1, waiting for transfers between devices: 4.37 us -> 0.01 us  [line_parts(): got_near = lax.ppermute(near_sent, 'batch', Y_SWAP)]
    ppermute x2, waiting for transfers between devices: 8.75 us -> 12.9 us  [on_device(): away_y = lax.ppermute(sends[i][1], 'batch', Y_SWAP)]
    ppermute x6, starting transfers between devices: 9.43 us -> 5.75 us  [shifted(): lax.ppermute(value, 'vocab', [(i, (i + k) % vocab) for i in range(vocab)])]
    ppermute x2, starting transfers between devices: 6.55 us -> 3.1 us  [on_device(): next_x = lax.ppermute(more_sends[i][1], 'batch', X_SWAP)]
    ppermute x6, waiting for transfers between devices: 4.31 us -> 7.46 us  [shifted(): lax.ppermute(value, 'vocab', [(i, (i + k) % vocab) for i in range(vocab)])]
  transfers between devices with their start and end apart: 30 -> 30, of which waited for: 14 -> 15; matrix products, arithmetic and copies ran while one was open for 18% -> 19% of each run, Pallas kernels for 0% -> 0%
where the time goes in v20:
time: 124 us
  waiting for transfers between devices  54.5 us (44%)
  starting transfers between devices  42.2 us (34%)
  other arithmetic  14.9 us (12%)
  matrix products  9.43 us (8%)
  local copies, waits for them, and re-layouts  1.76 us (1%)
    ppermute x2, waiting for transfers between devices, on_device(): away_y = lax.ppermute(sends[i][1], 'batch', Y_SWAP)  12.9 us
    ppermute x2, waiting for transfers between devices, down(): return lax.ppermute(value, 'vocab', [(z + 1, z) for z in range(vocab - k)])  11.9 us
    dot_general x4, matrix products, dot(): jnp.dot(left.reshape(-1, block), weight, preferred_element_type=jnp.float32)  9.43 us
    ppermute x2, starting transfers between devices, line_parts(): ends.append(lax.ppermute(sent, ('batch', 'vocab'), sorted(moves)))  8.61 us
    ppermute x2, waiting for transfers between devices, on_device(): next_x = lax.ppermute(more_sends[i][1], 'batch', X_SWAP)  8.18 us
    ppermute x6, waiting for transfers between devices, shifted(): lax.ppermute(value, 'vocab', [(i, (i + k) % vocab) for i in range(vocab)])  7.46 us
    ppermute x1, waiting for transfers between devices, line_parts(): lax.ppermute(lax.dynamic_slice_in_dim(gained, (1 - x) * block, block, 2),...  6.9 us
    select_n x1, other arithmetic, line_parts(): jnp.where(keep_near, taken, kept)  5.88 us
  transfers between devices with their start and end apart: 30, of which 15 were waited for; matrix products, arithmetic and copies ran while one was open for 19% of the time, Pallas kernels for 0%

profile of v20, /device:TPU:0, one launch (start us, length us, event | category | flops | bytes accessed | tf_op | source)
XLA Modules:
  0.0 124.0 jit_solution(13545949073210261745)
XLA Ops:
  3.0 2.6 %collective-permute-start = (bf16[2,64,1024]{2,1,0:T(8,128)(2,1)S(1)}, bf16[2,64,1024]{2,1,0:T(8,128)(2,1)S(1)}, u32[]{:S(2)}, u32[]{:S(2)}) collective-permute-start(bf16[2,64,1024]{2,1,0:T(8,128)(2,1)S(1)} %constant_dynamic-slice_fusion.6), channel_id=1, source_target_pairs={{0,4},{4,0},{8,12},{12,8},{1,5},{5,1},{9,13},{13,9},{2,6},{6,2},{1... | collective-permute-start | bytes 786440 | tf_op jit(solution)/shard_map/ppermute | solution.py:88
  5.7 6.9 %collective-permute-done = bf16[2,64,1024]{2,1,0:T(8,128)(2,1)S(1)} collective-permute-done((bf16[2,64,1024]{2,1,0:T(8,128)(2,1)S(1)}, bf16[2,64,1024]{2,1,0:T(8,128)(2,1)S(1)}, u32[]{:S(2)}, u32[]{:S(2)}) %collective-permute-start) | collective-permute-done | bytes 262176 | tf_op jit(solution)/shard_map/ppermute | solution.py:88
  12.7 3.8 %collective-permute-start.4 = (bf16[2,2,64,1024]{3,2,1,0:T(8,128)(2,1)S(1)}, bf16[2,2,64,1024]{3,2,1,0:T(8,128)(2,1)S(1)}, u32[]{:S(2)}, u32[]{:S(2)}) collective-permute-start(bf16[2,2,64,1024]{3,2,1,0:T(8,128)(2,1)S(1)} %pad_maximum_fusion.2), channel_id=1, source_target_pairs={{0,1},{1,2},{2,3},{4,5},{5,6},{6,7},{8,9},{9,10},{10,11},{12,13},{... | collective-permute-start | bytes 1572872 | tf_op jit(solution)/shard_map/ppermute | solution.py:94
  18.8 4.3 %collective-permute-start.3 = (f32[64]{0:T(128)S(1)}, f32[64]{0:T(128)S(1)}, u32[]{:S(2)}, u32[]{:S(2)}) collective-permute-start(f32[64]{0:T(128)S(1)} %get-tuple-element.74), channel_id=1, source_target_pairs={{0,4},{4,12},{8,20},{12,28},{16,0},{20,8},{24,16},{28,24},{1,5},{5... | collective-permute-start | bytes 776 | tf_op jit(solution)/shard_map/ppermute | solution.py:53
  24.4 3.1 %collective-permute-done.4 = bf16[2,2,64,1024]{3,2,1,0:T(8,128)(2,1)S(1)} collective-permute-done((bf16[2,2,64,1024]{3,2,1,0:T(8,128)(2,1)S(1)}, bf16[2,2,64,1024]{3,2,1,0:T(8,128)(2,1)S(1)}, u32[]{:S(2)}, u32[]{:S(2)}) %collective-permute-start.4) | collective-permute-done | bytes 524320 | tf_op jit(solution)/shard_map/ppermute | solution.py:94
  27.5 4.1 %collective-permute-done.1 = bf16[2,2,64,1024]{3,2,1,0:T(8,128)(2,1)S(1)} collective-permute-done((bf16[2,2,64,1024]{3,2,1,0:T(8,128)(2,1)S(1)}, bf16[2,2,64,1024]{3,2,1,0:T(8,128)(2,1)S(1)}, u32[]{:S(2)}, u32[]{:S(2)}) %collective-permute-start.1) | collective-permute-done | bytes 524320 | tf_op jit(solution)/shard_map/ppermute | solution.py:97
  31.6 1.5 %collective-permute-start.6 = (bf16[2,2,64,1024]{3,2,1,0:T(8,128)(2,1)S(1)}, bf16[2,2,64,1024]{3,2,1,0:T(8,128)(2,1)}, u32[]{:S(2)}, u32[]{:S(2)}) collective-permute-start(bf16[2,2,64,1024]{3,2,1,0:T(8,128)(2,1)S(1)} %collective-permute-done.4), channel_id=1, source_target_pairs={{1,2},{2,3},{5,6},{6,7},{9,10},{10,11},{13,14},{14,15},{17,18},{18... | collective-permute-start | bytes 1572872 | tf_op jit(solution)/shard_map/ppermute | solution.py:94
  34.4 1.6 %collective-permute-start.5 = (bf16[2,2,64,1024]{3,2,1,0:T(8,128)(2,1)S(1)}, bf16[2,2,64,1024]{3,2,1,0:T(8,128)(2,1)S(1)}, u32[]{:S(2)}, u32[]{:S(2)}) collective-permute-start(bf16[2,2,64,1024]{3,2,1,0:T(8,128)(2,1)S(1)} %select_select_fusion.2), channel_id=1, source_target_pairs={{0,8},{8,0},{4,12},{12,4},{1,9},{9,1},{5,13},{13,5},{2,10},{10,2},... | collective-permute-start | bytes 1572872 | tf_op jit(solution)/shard_map/ppermute | solution.py:112
  36.0 5.9 %broadcast_select_fusion = (bf16[1024,2048]{1,0:T(8,128)(2,1)S(1)}, bf16[1024,2048]{1,0:T(8,128)(2,1)S(1)}) fusion(pred[]{:T(512)S(6)} %eq.76, bf16[1024,4096]{1,0:T(8,128)(2,1)} %collective-permute-done.7, s32[]{:T(128)S(6)} %select_n.247, bf16[1024,4096]{1,0:T(8,128)(2,1)} %param.5), kind=kLoop, calls=%fused_computation.2 | loop fusion | flops 4194304 | bytes 16777220 | tf_op jit(solution)/shard_map/jit(_where)/select_n | solution.py:118
  41.9 7.8 %collective-permute-done.8 = bf16[2,2,64,1024]{3,2,1,0:T(8,128)(2,1)} collective-permute-done((bf16[2,2,64,1024]{3,2,1,0:T(8,128)(2,1)S(1)}, bf16[2,2,64,1024]{3,2,1,0:T(8,128)(2,1)}, u32[]{:S(2)}, u32[]{:S(2)}) %collective-permute-start.8) | collective-permute-done | bytes 524320 | tf_op jit(solution)/shard_map/ppermute | solution.py:97
  50.4 7.9 %collective-permute-start.9 = (bf16[2,2,64,1024]{3,2,1,0:T(8,128)(2,1)S(1)}, bf16[2,2,64,1024]{3,2,1,0:T(8,128)(2,1)S(1)}, u32[]{:S(2)}, u32[]{:S(2)}) collective-permute-start(bf16[2,2,64,1024]{3,2,1,0:T(8,128)(2,1)S(1)} %pad_maximum_fusion.2), channel_id=1, source_target_pairs={{0,3},{4,7},{11,8},{15,12},{16,19},{20,23},{27,24},{31,28}} | collective-permute-start | bytes 1572872 | tf_op jit(solution)/shard_map/ppermute | solution.py:141
  58.3 1.4 %select_select_fusion = (bf16[2,2,64,1024]{3,2,1,0:T(8,128)(2,1)S(1)}, bf16[2,2,64,1024]{3,2,1,0:T(8,128)(2,1)S(1)}) fusion(bf16[2,2,64,1024]{3,2,1,0:T(8,128)(2,1)} %collective-permute-done.8, bf16[2,2,64,1024]{3,2,1,0:T(8,128)(2,1)} %collective-permute-done.6, bf16[2,2,64,1024]{3,2,1,0:T(8,128)(2,1)S(1)} %collective-permute-done.1, ...), kind=kLoop, calls=%fused_computation.53 | loop fusion | flops 2359296 | bytes 3670024 | tf_op jit(solution)/shard_map/jit(_where)/select_n | solution.py:105
  61.1 1.8 %collective-permute-start.13 = (f32[2,64]{1,0:T(2,128)S(1)}, f32[2,64]{1,0:T(2,128)S(1)}, u32[]{:S(2)}, u32[]{:S(2)}) collective-permute-start(f32[2,64]{1,0:T(2,128)S(1)} %pad_maximum_fusion.6), channel_id=1, source_target_pairs={{0,2},{1,3},{2,0},{3,1},{4,6},{5,7},{6,4},{7,5},{8,10},{9,11},{10,... | collective-permute-start | bytes 1544 | tf_op jit(solution)/shard_map/ppermute | solution.py:44
  63.1 3.8 %collective-permute-done.12 = f32[2,64]{1,0:T(2,128)S(1)} collective-permute-done((f32[2,64]{1,0:T(2,128)S(1)}, f32[2,64]{1,0:T(2,128)S(1)}, u32[]{:S(2)}, u32[]{:S(2)}) %collective-permute-start.12) | collective-permute-done | bytes 544 | tf_op jit(solution)/shard_map/ppermute | solution.py:44
  66.9 2.3 %fusion.33 = f32[512,2048]{1,0:T(8,128)S(1)} fusion(bf16[512,1024]{1,0:T(8,128)(2,1)S(1)} %bitcast.116, bf16[1024,2048]{1,0:T(8,128)(2,1)S(1)} %get-tuple-element.25), kind=kOutput, calls=%fused_computation.108 | convolution fusion | flops 2147483648 | bytes 9437184 | tf_op jit(solution)/shard_map/dot_general | solution.py:84
  69.4 1.6 %collective-permute-done.14 = f32[2,64]{1,0:T(2,128)S(1)} collective-permute-done((f32[2,64]{1,0:T(2,128)S(1)}, f32[2,64]{1,0:T(2,128)S(1)}, u32[]{:S(2)}, u32[]{:S(2)}) %collective-permute-start.14) | collective-permute-done | bytes 544 | tf_op jit(solution)/shard_map/ppermute | solution.py:44
  71.0 1.4 %collective-permute-done.11 = bf16[2,2,64,1024]{3,2,1,0:T(8,128)(2,1)S(1)} collective-permute-done((bf16[2,2,64,1024]{3,2,1,0:T(8,128)(2,1)S(1)}, bf16[2,2,64,1024]{3,2,1,0:T(8,128)(2,1)S(1)}, u32[]{:S(2)}, u32[]{:S(2)}) %collective-permute-start.11) | collective-permute-done | bytes 524320 | tf_op jit(solution)/shard_map/ppermute | solution.py:130
  72.7 2.4 %add_multiply_fusion.1 = f32[512,2048]{1,0:T(8,128)S(1)} fusion(f32[512,2048]{1,0:T(8,128)S(1)} %fusion.33, bf16[512,1024]{1,0:T(8,128)(2,1)S(1)} %bitcast.117, bf16[1024,2048]{1,0:T(8,128)(2,1)S(1)} %get-tuple-element.26), kind=kOutput, calls=%fused_computation.1 | convolution fusion | flops 2149580800 | bytes 13631488 | tf_op jit(solution)/shard_map/dot_general | solution.py:84
  76.5 1.6 %collective-permute-start.15 = (f16[2,2,64,1024]{3,2,0,1:T(8,128)(2,1)S(1)}, f16[2,2,64,1024]{3,2,0,1:T(8,128)(2,1)S(1)}, u32[]{:S(2)}, u32[]{:S(2)}) collective-permute-start(f16[2,2,64,1024]{3,2,0,1:T(8,128)(2,1)S(1)} %fusion.6), channel_id=1, source_target_pairs={{0,4},{4,0},{8,12},{12,8},{1,5},{5,1},{9,13},{13,9},{2,6},{6,2},{1... | collective-permute-start | bytes 1572872 | tf_op jit(solution)/shard_map/ppermute | solution.py:185
  78.0 2.3 %fusion.34 = f32[512,2048]{1,0:T(8,128)S(1)} fusion(bf16[512,1024]{1,0:T(8,128)(2,1)S(1)} %bitcast.126, bf16[1024,2048]{1,0:T(8,128)(2,1)S(1)} %get-tuple-element.26), kind=kOutput, calls=%fused_computation.109 | convolution fusion | flops 2147483648 | bytes 9437184 | tf_op jit(solution)/shard_map/dot_general | solution.py:84
  80.4 2.3 %add_multiply_fusion = f32[512,2048]{1,0:T(8,128)S(1)} fusion(f32[512,2048]{1,0:T(8,128)S(1)} %fusion.34, bf16[512,1024]{1,0:T(8,128)(2,1)S(1)} %bitcast.125, bf16[1024,2048]{1,0:T(8,128)(2,1)S(1)} %get-tuple-element.25), kind=kOutput, calls=%fused_computation | convolution fusion | flops 2149580800 | bytes 13631488 | tf_op jit(solution)/shard_map/dot_general | solution.py:84
  83.4 1.8 %collective-permute-start.20 = (f16[2,2,64,1024]{3,2,1,0:T(8,128)(2,1)S(1)}, f16[2,2,64,1024]{3,2,1,0:T(8,128)(2,1)S(1)}, u32[]{:S(2)}, u32[]{:S(2)}) collective-permute-start(f16[2,2,64,1024]{3,2,1,0:T(8,128)(2,1)S(1)} %fusion.5), channel_id=1, source_target_pairs={{0,8},{8,0},{4,12},{12,4},{1,9},{9,1},{5,13},{13,5},{2,10},{10,2},... | collective-permute-start | bytes 1572872 | tf_op jit(solution)/shard_map/ppermute | solution.py:186
  86.1 4.4 %collective-permute-done.21 = f16[2,2,64,1024]{3,2,1,0:T(8,128)(2,1)S(1)} collective-permute-done((f16[2,2,64,1024]{3,2,1,0:T(8,128)(2,1)S(1)}, f16[2,2,64,1024]{3,2,1,0:T(8,128)(2,1)S(1)}, u32[]{:S(2)}, u32[]{:S(2)}) %collective-permute-start.21) | collective-permute-done | bytes 524320 | tf_op jit(solution)/shard_map/ppermute | solution.py:186
  90.8 1.6 %collective-permute-start.22 = (f16[2,64,1024]{2,1,0:T(8,128)(2,1)S(1)}, f16[2,64,1024]{2,1,0:T(8,128)(2,1)S(1)}, u32[]{:S(2)}, u32[]{:S(2)}) collective-permute-start(f16[2,64,1024]{2,1,0:T(8,128)(2,1)S(1)} %fusion.15), channel_id=1, source_target_pairs={{0,4},{4,0},{8,12},{12,8},{1,5},{5,1},{9,13},{13,9},{2,6},{6,2},{1... | collective-permute-start | bytes 786440 | tf_op jit(solution)/shard_map/ppermute | solution.py:198
  93.3 8.5 %collective-permute-done.20 = f16[2,2,64,1024]{3,2,1,0:T(8,128)(2,1)S(1)} collective-permute-done((f16[2,2,64,1024]{3,2,1,0:T(8,128)(2,1)S(1)}, f16[2,2,64,1024]{3,2,1,0:T(8,128)(2,1)S(1)}, u32[]{:S(2)}, u32[]{:S(2)}) %collective-permute-start.20) | collective-permute-done | bytes 524320 | tf_op jit(solution)/shard_map/ppermute | solution.py:186
  102.1 1.6 %collective-permute-start.25 = (f16[2,64,1024]{2,1,0:T(8,128)(2,1)S(1)}, f16[2,64,1024]{2,1,0:T(8,128)(2,1)S(1)}, u32[]{:S(2)}, u32[]{:S(2)}) collective-permute-start(f16[2,64,1024]{2,1,0:T(8,128)(2,1)S(1)} %fusion.14), channel_id=1, source_target_pairs={{0,4},{4,0},{8,12},{12,8},{1,5},{5,1},{9,13},{13,9},{2,6},{6,2},{1... | collective-permute-start | bytes 786440 | tf_op jit(solution)/shard_map/ppermute | solution.py:198
  104.6 3.6 %collective-permute-done.22 = f16[2,64,1024]{2,1,0:T(8,128)(2,1)S(1)} collective-permute-done((f16[2,64,1024]{2,1,0:T(8,128)(2,1)S(1)}, f16[2,64,1024]{2,1,0:T(8,128)(2,1)S(1)}, u32[]{:S(2)}, u32[]{:S(2)}) %collective-permute-start.22) | collective-permute-done | bytes 262176 | tf_op jit(solution)/shard_map/ppermute | solution.py:198
  108.5 4.6 %collective-permute-done.25 = f16[2,64,1024]{2,1,0:T(8,128)(2,1)S(1)} collective-permute-done((f16[2,64,1024]{2,1,0:T(8,128)(2,1)S(1)}, f16[2,64,1024]{2,1,0:T(8,128)(2,1)S(1)}, u32[]{:S(2)}, u32[]{:S(2)}) %collective-permute-start.25) | collective-permute-done | bytes 262176 | tf_op jit(solution)/shard_map/ppermute | solution.py:198
  117.3 1.5 %collective-permute-start.28 = (f32[4,64]{1,0:T(4,128)S(1)}, f32[4,64]{1,0:T(4,128)S(1)}, u32[]{:S(2)}, u32[]{:S(2)}) collective-permute-start(f32[4,64]{1,0:T(4,128)S(1)} %get-tuple-element.66), channel_id=1, source_target_pairs={{0,2},{1,3},{2,0},{3,1},{4,6},{5,7},{6,4},{7,5},{8,10},{9,11},{10,... | collective-permute-start | bytes 3080 | tf_op jit(solution)/shard_map/ppermute | solution.py:44
  118.7 1.5 %collective-permute-start.29 = (f32[4,64]{1,0:T(4,128)S(1)}, f32[4,64]{1,0:T(4,128)S(1)}, u32[]{:S(2)}, u32[]{:S(2)}) collective-permute-start(f32[4,64]{1,0:T(4,128)S(1)} %get-tuple-element.66), channel_id=1, source_target_pairs={{0,3},{1,0},{2,1},{3,2},{4,7},{5,4},{6,5},{7,6},{8,11},{9,8},{10,9... | collective-permute-start | bytes 3080 | tf_op jit(solution)/shard_map/ppermute | solution.py:44
  120.2 1.5 %collective-permute-done.27 = f32[4,64]{1,0:T(4,128)S(1)} collective-permute-done((f32[4,64]{1,0:T(4,128)S(1)}, f32[4,64]{1,0:T(4,128)S(1)}, u32[]{:S(2)}, u32[]{:S(2)}) %collective-permute-start.27) | collective-permute-done | bytes 1056 | tf_op jit(solution)/shard_map/ppermute | solution.py:44
  122.4 1.6 %fusion.2 = (f32[64,4096]{1,0:T(8,128)}, f32[64,4096]{1,0:T(8,128)}) fusion(f32[64]{0:T(128)S(1)} %get-tuple-element.67, f32[64]{0:T(128)S(1)} %get-tuple-element.69, f16[64,2048]{1,0:T(8,128)(2,1)S(1)} %get-tuple-element.60, f16[64,2048]{1,0:T(8,128)(2,1)S(1)} %get-tuple-element.58, f32[64,4096]{1,0:T(8,128)S(1)} %get-tuple-element.41, ...), kind=kLoop, calls=%fused_computation.18 | loop fusion | flops 1310720 | bytes 3670784 | tf_op jit(solution)/shard_map/sub | solution.py:236
  (88 shorter events, 20.5 us)
Async XLA Ops:
  0.6 17.2 %copy-start = (bf16[1,128,2048]{2,1,0:T(8,128)(2,1)S(1)}, bf16[1,128,2048]{2,1,0:T(8,128)(2,1)}, u32[]{:S(2)}) copy-start(bf16[1,128,2048]{2,1,0:T(8,128)(2,1)} %param.3) | copy-start | bytes 1572868
  0.6 35.4 %collective-permute-start.7 = (bf16[1024,4096]{1,0:T(8,128)(2,1)}, bf16[1024,4096]{1,0:T(8,128)(2,1)}, u32[]{:S(2)}, u32[]{:S(2)}) collective-permute-start(bf16[1024,4096]{1,0:T(8,128)(2,1)} %param.5), channel_id=1, source_target_pairs={{0,16},{16,0},{1,17},{17,1},{2,18},{18,2},{3,19},{19,3},{4,20},{20... | collective-permute-start | bytes 25165832 | tf_op jit(solution)/shard_map/ppermute | solution.py:41
  3.0 9.5 %collective-permute-start = (bf16[2,64,1024]{2,1,0:T(8,128)(2,1)S(1)}, bf16[2,64,1024]{2,1,0:T(8,128)(2,1)S(1)}, u32[]{:S(2)}, u32[]{:S(2)}) collective-permute-start(bf16[2,64,1024]{2,1,0:T(8,128)(2,1)S(1)} %constant_dynamic-slice_fusion.6), channel_id=1, source_target_pairs={{0,4},{4,0},{8,12},{12,8},{1,5},{5,1},{9,13},{13,9},{2,6},{6,2},{1... | collective-permute-start | bytes 786440 | tf_op jit(solution)/shard_map/ppermute | solution.py:88
  12.7 14.7 %collective-permute-start.4 = (bf16[2,2,64,1024]{3,2,1,0:T(8,128)(2,1)S(1)}, bf16[2,2,64,1024]{3,2,1,0:T(8,128)(2,1)S(1)}, u32[]{:S(2)}, u32[]{:S(2)}) collective-permute-start(bf16[2,2,64,1024]{3,2,1,0:T(8,128)(2,1)S(1)} %pad_maximum_fusion.2), channel_id=1, source_target_pairs={{0,1},{1,2},{2,3},{4,5},{5,6},{6,7},{8,9},{9,10},{10,11},{12,13},{... | collective-permute-start | bytes 1572872 | tf_op jit(solution)/shard_map/ppermute | solution.py:94
  16.5 15.1 %collective-permute-start.1 = (bf16[2,2,64,1024]{3,2,1,0:T(8,128)(2,1)S(1)}, bf16[2,2,64,1024]{3,2,1,0:T(8,128)(2,1)S(1)}, u32[]{:S(2)}, u32[]{:S(2)}) collective-permute-start(bf16[2,2,64,1024]{3,2,1,0:T(8,128)(2,1)S(1)} %pad_maximum_fusion.2), channel_id=1, source_target_pairs={{1,0},{2,1},{3,2},{5,4},{6,5},{7,6},{9,8},{10,9},{11,10},{13,12},{... | collective-permute-start | bytes 1572872 | tf_op jit(solution)/shard_map/ppermute | solution.py:97
  18.1 5.0 %collective-permute-start.2 = (f32[64]{0:T(128)S(1)}, f32[64]{0:T(128)S(1)}, u32[]{:S(2)}, u32[]{:S(2)}) collective-permute-start(f32[64]{0:T(128)S(1)} %get-tuple-element.73), channel_id=1, source_target_pairs={{0,0},{4,8},{8,16},{12,24},{16,4},{20,12},{24,20},{28,28},{1,1},{5... | collective-permute-start | bytes 776 | tf_op jit(solution)/shard_map/ppermute | solution.py:53
  18.8 5.6 %collective-permute-start.3 = (f32[64]{0:T(128)S(1)}, f32[64]{0:T(128)S(1)}, u32[]{:S(2)}, u32[]{:S(2)}) collective-permute-start(f32[64]{0:T(128)S(1)} %get-tuple-element.74), channel_id=1, source_target_pairs={{0,4},{4,12},{8,20},{12,28},{16,0},{20,8},{24,16},{28,24},{1,5},{5... | collective-permute-start | bytes 776 | tf_op jit(solution)/shard_map/ppermute | solution.py:53
  31.6 10.3 %collective-permute-start.6 = (bf16[2,2,64,1024]{3,2,1,0:T(8,128)(2,1)S(1)}, bf16[2,2,64,1024]{3,2,1,0:T(8,128)(2,1)}, u32[]{:S(2)}, u32[]{:S(2)}) collective-permute-start(bf16[2,2,64,1024]{3,2,1,0:T(8,128)(2,1)S(1)} %collective-permute-done.4), channel_id=1, source_target_pairs={{1,2},{2,3},{5,6},{6,7},{9,10},{10,11},{13,14},{14,15},{17,18},{18... | collective-permute-start | bytes 1572872 | tf_op jit(solution)/shard_map/ppermute | solution.py:94
  33.1 16.6 %collective-permute-start.8 = (bf16[2,2,64,1024]{3,2,1,0:T(8,128)(2,1)S(1)}, bf16[2,2,64,1024]{3,2,1,0:T(8,128)(2,1)}, u32[]{:S(2)}, u32[]{:S(2)}) collective-permute-start(bf16[2,2,64,1024]{3,2,1,0:T(8,128)(2,1)S(1)} %collective-permute-done.1), channel_id=1, source_target_pairs={{1,0},{2,1},{5,4},{6,5},{9,8},{10,9},{13,12},{14,13},{17,16},{18,1... | collective-permute-start | bytes 1572872 | tf_op jit(solution)/shard_map/ppermute | solution.py:97
  34.4 26.6 %collective-permute-start.5 = (bf16[2,2,64,1024]{3,2,1,0:T(8,128)(2,1)S(1)}, bf16[2,2,64,1024]{3,2,1,0:T(8,128)(2,1)S(1)}, u32[]{:S(2)}, u32[]{:S(2)}) collective-permute-start(bf16[2,2,64,1024]{3,2,1,0:T(8,128)(2,1)S(1)} %select_select_fusion.2), channel_id=1, source_target_pairs={{0,8},{8,0},{4,12},{12,4},{1,9},{9,1},{5,13},{13,5},{2,10},{10,2},... | collective-permute-start | bytes 1572872 | tf_op jit(solution)/shard_map/ppermute | solution.py:112
  49.7 21.3 %collective-permute-start.10 = (bf16[2,2,64,1024]{3,2,1,0:T(8,128)(2,1)S(1)}, bf16[2,2,64,1024]{3,2,1,0:T(8,128)(2,1)S(1)}, u32[]{:S(2)}, u32[]{:S(2)}) collective-permute-start(bf16[2,2,64,1024]{3,2,1,0:T(8,128)(2,1)S(1)} %pad_maximum_fusion.2), channel_id=1, source_target_pairs={{3,8},{7,12},{8,3},{12,7},{19,24},{23,28},{24,19},{28,23}} | collective-permute-start | bytes 1572872 | tf_op jit(solution)/shard_map/ppermute | solution.py:141
  50.4 20.6 %collective-permute-start.9 = (bf16[2,2,64,1024]{3,2,1,0:T(8,128)(2,1)S(1)}, bf16[2,2,64,1024]{3,2,1,0:T(8,128)(2,1)S(1)}, u32[]{:S(2)}, u32[]{:S(2)}) collective-permute-start(bf16[2,2,64,1024]{3,2,1,0:T(8,128)(2,1)S(1)} %pad_maximum_fusion.2), channel_id=1, source_target_pairs={{0,3},{4,7},{11,8},{15,12},{16,19},{20,23},{27,24},{31,28}} | collective-permute-start | bytes 1572872 | tf_op jit(solution)/shard_map/ppermute | solution.py:141
  59.7 12.7 %collective-permute-start.11 = (bf16[2,2,64,1024]{3,2,1,0:T(8,128)(2,1)S(1)}, bf16[2,2,64,1024]{3,2,1,0:T(8,128)(2,1)S(1)}, u32[]{:S(2)}, u32[]{:S(2)}) collective-permute-start(bf16[2,2,64,1024]{3,2,1,0:T(8,128)(2,1)S(1)} %get-tuple-element.51), channel_id=1, source_target_pairs={{1,9},{2,10},{3,11},{5,13},{6,14},{7,15},{8,0},{9,1},{10,2},{12,4}... | collective-permute-start | bytes 1572872 | tf_op jit(solution)/shard_map/ppermute | solution.py:130
  61.0 5.9 %collective-permute-start.12 = (f32[2,64]{1,0:T(2,128)S(1)}, f32[2,64]{1,0:T(2,128)S(1)}, u32[]{:S(2)}, u32[]{:S(2)}) collective-permute-start(f32[2,64]{1,0:T(2,128)S(1)} %pad_maximum_fusion.6), channel_id=1, source_target_pairs={{0,1},{1,2},{2,3},{3,0},{4,5},{5,6},{6,7},{7,4},{8,9},{9,10},{10,1... | collective-permute-start | bytes 1544 | tf_op jit(solution)/shard_map/ppermute | solution.py:44
  61.1 8.2 %collective-permute-start.13 = (f32[2,64]{1,0:T(2,128)S(1)}, f32[2,64]{1,0:T(2,128)S(1)}, u32[]{:S(2)}, u32[]{:S(2)}) collective-permute-start(f32[2,64]{1,0:T(2,128)S(1)} %pad_maximum_fusion.6), channel_id=1, source_target_pairs={{0,2},{1,3},{2,0},{3,1},{4,6},{5,7},{6,4},{7,5},{8,10},{9,11},{10,... | collective-permute-start | bytes 1544 | tf_op jit(solution)/shard_map/ppermute | solution.py:44
  66.9 4.0 %collective-permute-start.14 = (f32[2,64]{1,0:T(2,128)S(1)}, f32[2,64]{1,0:T(2,128)S(1)}, u32[]{:S(2)}, u32[]{:S(2)}) collective-permute-start(f32[2,64]{1,0:T(2,128)S(1)} %pad_maximum_fusion.6), channel_id=1, source_target_pairs={{0,3},{1,0},{2,1},{3,2},{4,7},{5,4},{6,5},{7,6},{8,11},{9,8},{10,9... | collective-permute-start | bytes 1544 | tf_op jit(solution)/shard_map/ppermute | solution.py:44
  69.3 11.1 %collective-permute-start.16 = (bf16[2,2,2,64,1024]{4,3,2,1,0:T(8,128)(2,1)S(1)}, bf16[2,2,2,64,1024]{4,3,2,1,0:T(8,128)(2,1)S(1)}, u32[]{:S(2)}, u32[]{:S(2)}) collective-permute-start(bf16[2,2,2,64,1024]{4,3,2,1,0:T(8,128)(2,1)S(1)} %pad_maximum_fusion), channel_id=1, source_target_pairs={{0,16},{16,0},{1,17},{17,1},{2,18},{18,2},{3,19},{19,3},{4,20},{20... | collective-permute-start | bytes 3145736 | tf_op jit(solution)/shard_map/ppermute | solution.py:78
  72.6 5.4 %collective-permute-start.17 = (bf16[2,2,2,64,1024]{4,3,2,1,0:T(8,128)(2,1)S(1)}, bf16[2,2,2,64,1024]{4,3,2,1,0:T(8,128)(2,1)S(1)}, u32[]{:S(2)}, u32[]{:S(2)}) collective-permute-start(bf16[2,2,2,64,1024]{4,3,2,1,0:T(8,128)(2,1)S(1)} %pad_maximum_fusion.1), channel_id=1, source_target_pairs={{0,16},{16,0},{1,17},{17,1},{2,18},{18,2},{3,19},{19,3},{4,20},{20... | collective-permute-start | bytes 3145736 | tf_op jit(solution)/shard_map/ppermute | solution.py:78
  75.8 14.8 %collective-permute-start.21 = (f16[2,2,64,1024]{3,2,1,0:T(8,128)(2,1)S(1)}, f16[2,2,64,1024]{3,2,1,0:T(8,128)(2,1)S(1)}, u32[]{:S(2)}, u32[]{:S(2)}) collective-permute-start(f16[2,2,64,1024]{3,2,1,0:T(8,128)(2,1)S(1)} %fusion.4), channel_id=1, source_target_pairs={{0,8},{8,0},{4,12},{12,4},{1,9},{9,1},{5,13},{13,5},{2,10},{10,2},... | collective-permute-start | bytes 1572872 | tf_op jit(solution)/shard_map/ppermute | solution.py:186
  76.5 15.9 %collective-permute-start.15 = (f16[2,2,64,1024]{3,2,0,1:T(8,128)(2,1)S(1)}, f16[2,2,64,1024]{3,2,0,1:T(8,128)(2,1)S(1)}, u32[]{:S(2)}, u32[]{:S(2)}) collective-permute-start(f16[2,2,64,1024]{3,2,0,1:T(8,128)(2,1)S(1)} %fusion.6), channel_id=1, source_target_pairs={{0,4},{4,0},{8,12},{12,8},{1,5},{5,1},{9,13},{13,9},{2,6},{6,2},{1... | collective-permute-start | bytes 1572872 | tf_op jit(solution)/shard_map/ppermute | solution.py:185
  83.4 18.4 %collective-permute-start.20 = (f16[2,2,64,1024]{3,2,1,0:T(8,128)(2,1)S(1)}, f16[2,2,64,1024]{3,2,1,0:T(8,128)(2,1)S(1)}, u32[]{:S(2)}, u32[]{:S(2)}) collective-permute-start(f16[2,2,64,1024]{3,2,1,0:T(8,128)(2,1)S(1)} %fusion.5), channel_id=1, source_target_pairs={{0,8},{8,0},{4,12},{12,4},{1,9},{9,1},{5,13},{13,5},{2,10},{10,2},... | collective-permute-start | bytes 1572872 | tf_op jit(solution)/shard_map/ppermute | solution.py:186
  85.5 18.1 %collective-permute-start.19 = (f16[2,2,64,1024]{3,2,0,1:T(8,128)(2,1)S(1)}, f16[2,2,64,1024]{3,2,0,1:T(8,128)(2,1)S(1)}, u32[]{:S(2)}, u32[]{:S(2)}) collective-permute-start(f16[2,2,64,1024]{3,2,0,1:T(8,128)(2,1)S(1)} %fusion.7), channel_id=1, source_target_pairs={{0,4},{4,0},{8,12},{12,8},{1,5},{5,1},{9,13},{13,9},{2,6},{6,2},{1... | collective-permute-start | bytes 1572872 | tf_op jit(solution)/shard_map/ppermute | solution.py:185
  90.8 17.3 %collective-permute-start.22 = (f16[2,64,1024]{2,1,0:T(8,128)(2,1)S(1)}, f16[2,64,1024]{2,1,0:T(8,128)(2,1)S(1)}, u32[]{:S(2)}, u32[]{:S(2)}) collective-permute-start(f16[2,64,1024]{2,1,0:T(8,128)(2,1)S(1)} %fusion.15), channel_id=1, source_target_pairs={{0,4},{4,0},{8,12},{12,8},{1,5},{5,1},{9,13},{13,9},{2,6},{6,2},{1... | collective-permute-start | bytes 786440 | tf_op jit(solution)/shard_map/ppermute | solution.py:198
  92.6 15.6 %collective-permute-start.18 = (f16[2,64,1024]{2,1,0:T(8,128)(2,1)S(1)}, f16[2,64,1024]{2,1,0:T(8,128)(2,1)S(1)}, u32[]{:S(2)}, u32[]{:S(2)}) collective-permute-start(f16[2,64,1024]{2,1,0:T(8,128)(2,1)S(1)} %fusion.12), channel_id=1, source_target_pairs={{0,8},{8,0},{4,12},{12,4},{1,9},{9,1},{5,13},{13,5},{2,10},{10,2},... | collective-permute-start | bytes 786440 | tf_op jit(solution)/shard_map/ppermute | solution.py:197
  102.1 11.0 %collective-permute-start.25 = (f16[2,64,1024]{2,1,0:T(8,128)(2,1)S(1)}, f16[2,64,1024]{2,1,0:T(8,128)(2,1)S(1)}, u32[]{:S(2)}, u32[]{:S(2)}) collective-permute-start(f16[2,64,1024]{2,1,0:T(8,128)(2,1)S(1)} %fusion.14), channel_id=1, source_target_pairs={{0,4},{4,0},{8,12},{12,8},{1,5},{5,1},{9,13},{13,9},{2,6},{6,2},{1... | collective-permute-start | bytes 786440 | tf_op jit(solution)/shard_map/ppermute | solution.py:198
  103.8 9.3 %collective-permute-start.24 = (f16[2,64,1024]{2,1,0:T(8,128)(2,1)S(1)}, f16[2,64,1024]{2,1,0:T(8,128)(2,1)S(1)}, u32[]{:S(2)}, u32[]{:S(2)}) collective-permute-start(f16[2,64,1024]{2,1,0:T(8,128)(2,1)S(1)} %fusion.13), channel_id=1, source_target_pairs={{0,8},{8,0},{4,12},{12,4},{1,9},{9,1},{5,13},{13,5},{2,10},{10,2},... | collective-permute-start | bytes 786440 | tf_op jit(solution)/shard_map/ppermute | solution.py:197
  108.4 5.0 %collective-permute-start.23 = (f16[64,2048]{1,0:T(8,128)(2,1)S(1)}, f16[64,2048]{1,0:T(8,128)(2,1)S(1)}, u32[]{:S(2)}, u32[]{:S(2)}) collective-permute-start(f16[64,2048]{1,0:T(8,128)(2,1)S(1)} %fusion.21), channel_id=1, source_target_pairs={{0,16},{16,0},{1,17},{17,1},{2,18},{18,2},{3,19},{19,3},{4,20},{20... | collective-permute-start | bytes 786440 | tf_op jit(solution)/shard_map/ppermute | solution.py:78
  113.3 1.6 %collective-permute-start.26 = (f16[64,2048]{1,0:T(8,128)(2,1)S(1)}, f16[64,2048]{1,0:T(8,128)(2,1)S(1)}, u32[]{:S(2)}, u32[]{:S(2)}) collective-permute-start(f16[64,2048]{1,0:T(8,128)(2,1)S(1)} %fusion.19), channel_id=1, source_target_pairs={{0,16},{16,0},{1,17},{17,1},{2,18},{18,2},{3,19},{19,3},{4,20},{20... | collective-permute-start | bytes 786440 | tf_op jit(solution)/shard_map/ppermute | solution.py:78
  116.3 5.4 %collective-permute-start.27 = (f32[4,64]{1,0:T(4,128)S(1)}, f32[4,64]{1,0:T(4,128)S(1)}, u32[]{:S(2)}, u32[]{:S(2)}) collective-permute-start(f32[4,64]{1,0:T(4,128)S(1)} %get-tuple-element.66), channel_id=1, source_target_pairs={{0,1},{1,2},{2,3},{3,0},{4,5},{5,6},{6,7},{7,4},{8,9},{9,10},{10,1... | collective-permute-start | bytes 3080 | tf_op jit(solution)/shard_map/ppermute | solution.py:44
  117.3 4.5 %collective-permute-start.28 = (f32[4,64]{1,0:T(4,128)S(1)}, f32[4,64]{1,0:T(4,128)S(1)}, u32[]{:S(2)}, u32[]{:S(2)}) collective-permute-start(f32[4,64]{1,0:T(4,128)S(1)} %get-tuple-element.66), channel_id=1, source_target_pairs={{0,2},{1,3},{2,0},{3,1},{4,6},{5,7},{6,4},{7,5},{8,10},{9,11},{10,... | collective-permute-start | bytes 3080 | tf_op jit(solution)/shard_map/ppermute | solution.py:44
  118.7 3.6 %collective-permute-start.29 = (f32[4,64]{1,0:T(4,128)S(1)}, f32[4,64]{1,0:T(4,128)S(1)}, u32[]{:S(2)}, u32[]{:S(2)}) collective-permute-start(f32[4,64]{1,0:T(4,128)S(1)} %get-tuple-element.66), channel_id=1, source_target_pairs={{0,3},{1,0},{2,1},{3,2},{4,7},{5,4},{6,5},{7,6},{8,11},{9,8},{10,9... | collective-permute-start | bytes 3080 | tf_op jit(solution)/shard_map/ppermute | solution.py:44

commit v21 on v15

--- a/solution.py
+++ b/solution.py
@@ -144,12 +144,18 @@
         )
         swapped_far = swapped(far)
 
+        def halves(near, left):
+            return [
+                near[:, low : low + width // 2] + dot(left, far_weight[:, low : low + width // 2])
+                for low in (0, width // 2)
+            ]
+
         def own_part():
-            return near_part + dot(far, far_weight)
+            return halves(near_part, far)
 
         def other_part(*earlier):
             left = after(swapped_far, *earlier)
-            return dot(swapped_near, near_weight) + dot(left, far_weight)
+            return halves(dot(swapped_near, near_weight), left)
 
         return (own_part, other_part), scale
 
@@ -162,7 +168,9 @@
         swapped_whole = swapped(whole)
 
         def part(left):
-            return dot(pick(left, core, 0), near_weight) + dot(pick(left, 1 - core, 0), far_weight)
+            near, far = pick(left, core, 0), pick(left, 1 - core, 0)
+            found = dot(near, near_weight) + dot(far, far_weight)
+            return found[:, : width // 2], found[:, width // 2 :]
 
         return (lambda: part(whole), lambda *earlier: part(after(swapped_whole, *earlier))), row_scale()
 
@@ -170,8 +178,10 @@
     parts, scale = line_parts() if lined else gathered_parts()
     kept, sends = [], []
     for part in parts:
-        whole = (part(*(sends[-1] if sends else ())) * SHRINK).reshape(2, 2, 2, seg, width)
-        low, high = whole[..., : width // 2], whole[..., width // 2 :]
+        low, high = (
+            (half * SHRINK).reshape(2, 2, 2, seg, width // 2)
+            for half in part(*(sends[-1] if sends else ()))
+        )
         kept.append((pick(low, x, 2), pick(high, y, 1)))
         sends.append(
             (pick(low, 1 - x, 2).astype(SUM_TYPE), pick(high, 1 - y, 1).astype(SUM_TYPE))

time: 119 us -> 119 us (level)
  local copies, waits for them, and re-layouts: 1.76 us -> 0.5 us
    dot_general x4 -> x6, matrix products: 9.41 us -> 9.72 us  [dot(): jnp.dot(left.reshape(-1, block), weight, preferred_element_type=jnp.float32)]
  transfers between devices with their start and end apart: 30 -> 30, of which waited for: 16 -> 16; matrix products, arithmetic and copies ran while one was open for 20% -> 19% of each run, Pallas kernels for 0% -> 0%
where the time goes in v21:
time: 119 us; the launch traced here: 118 us
  waiting for transfers between devices  45.9 us (39%)
  starting transfers between devices  45.1 us (38%)
  other arithmetic  15.6 us (13%)
  matrix products  9.72 us (8%)
    ppermute x2, waiting for transfers between devices, on_device(): away_y = lax.ppermute(sends[i][1], 'batch', Y_SWAP)  11.2 us
    dot_general x6, matrix products, dot(): jnp.dot(left.reshape(-1, block), weight, preferred_element_type=jnp.float32)  9.72 us
    ppermute x6, starting transfers between devices, shifted(): lax.ppermute(value, 'vocab', [(i, (i + k) % vocab) for i in range(vocab)])  9.44 us
    ppermute x2, waiting for transfers between devices, on_device(): next_x = lax.ppermute(more_sends[i][1], 'batch', X_SWAP)  8.42 us
    ppermute x2, starting transfers between devices, on_device(): next_x = lax.ppermute(more_sends[i][1], 'batch', X_SWAP)  6.54 us
    ppermute x1, waiting for transfers between devices, line_parts(): got_early = lax.ppermute(quarter(far, 2), ('batch', 'vocab'), early)  6.17 us
    select_n x1, other arithmetic, line_parts(): jnp.where(keep_near, taken, kept)  5.88 us
    ppermute x2, starting transfers between devices, line_parts(): ends.append(lax.ppermute(sent, ('batch', 'vocab'), sorted(moves)))  5.71 us
  transfers between devices with their start and end apart: 30, of which 16 were waited for; matrix products, arithmetic and copies ran while one was open for 19% of the time, Pallas kernels for 0%

profile of v21, /device:TPU:0, one launch (start us, length us, event | category | flops | bytes accessed | tf_op | source)
XLA Modules:
  0.0 118.1 jit_solution(5997863274009974873)
XLA Ops:
  3.0 2.6 %collective-permute-start = (bf16[2,64,1024]{2,1,0:T(8,128)(2,1)S(1)}, bf16[2,64,1024]{2,1,0:T(8,128)(2,1)S(1)}, u32[]{:S(2)}, u32[]{:S(2)}) collective-permute-start(bf16[2,64,1024]{2,1,0:T(8,128)(2,1)S(1)} %constant_dynamic-slice_fusion.6), channel_id=1, source_target_pairs={{0,4},{4,0},{8,12},{12,8},{1,5},{5,1},{9,13},{13,9},{2,6},{6,2},{1... | collective-permute-start | bytes 786440 | tf_op jit(solution)/shard_map/ppermute | solution.py:85
  6.8 1.6 %collective-permute-start.1 = (f32[128]{0:T(128)S(1)}, f32[128]{0:T(128)S(1)}, u32[]{:S(2)}, u32[]{:S(2)}) collective-permute-start(f32[128]{0:T(128)S(1)} %multiply_reduce_fusion), channel_id=1, source_target_pairs={{0,1},{1,2},{2,3},{3,0},{4,5},{5,6},{6,7},{7,4},{8,9},{9,10},{10,1... | collective-permute-start | bytes 1544 | tf_op jit(solution)/shard_map/ppermute | solution.py:44
  8.5 2.6 %collective-permute-start.2 = (f32[128]{0:T(128)S(1)}, f32[128]{0:T(128)S(1)}, u32[]{:S(2)}, u32[]{:S(2)}) collective-permute-start(f32[128]{0:T(128)S(1)} %multiply_reduce_fusion), channel_id=1, source_target_pairs={{0,2},{1,3},{2,0},{3,1},{4,6},{5,7},{6,4},{7,5},{8,10},{9,11},{10,... | collective-permute-start | bytes 1544 | tf_op jit(solution)/shard_map/ppermute | solution.py:44
  11.0 1.3 %collective-permute-start.3 = (f32[128]{0:T(128)S(1)}, f32[128]{0:T(128)S(1)}, u32[]{:S(2)}, u32[]{:S(2)}) collective-permute-start(f32[128]{0:T(128)S(1)} %multiply_reduce_fusion), channel_id=1, source_target_pairs={{0,3},{1,0},{2,1},{3,2},{4,7},{5,4},{6,5},{7,6},{8,11},{9,8},{10,9... | collective-permute-start | bytes 1544 | tf_op jit(solution)/shard_map/ppermute | solution.py:44
  12.9 1.7 %collective-permute-done.3 = f32[128]{0:T(128)S(1)} collective-permute-done((f32[128]{0:T(128)S(1)}, f32[128]{0:T(128)S(1)}, u32[]{:S(2)}, u32[]{:S(2)}) %collective-permute-start.3) | collective-permute-done | bytes 544 | tf_op jit(solution)/shard_map/ppermute | solution.py:44
  14.9 2.2 %collective-permute-start.7 = (bf16[2,2,64,1024]{3,2,1,0:T(8,128)(2,1)S(1)}, bf16[2,2,64,1024]{3,2,1,0:T(8,128)(2,1)S(1)}, u32[]{:S(2)}, u32[]{:S(2)}) collective-permute-start(bf16[2,2,64,1024]{3,2,1,0:T(8,128)(2,1)S(1)} %pad_maximum_fusion.2), channel_id=1, source_target_pairs={{0,1},{1,2},{2,3},{4,5},{5,6},{6,7},{8,9},{9,10},{10,11},{12,13},{... | collective-permute-start | bytes 1572872 | tf_op jit(solution)/shard_map/ppermute | solution.py:92
  17.0 1.3 %collective-permute-start.4 = (bf16[2,2,64,1024]{3,2,1,0:T(8,128)(2,1)S(1)}, bf16[2,2,64,1024]{3,2,1,0:T(8,128)(2,1)S(1)}, u32[]{:S(2)}, u32[]{:S(2)}) collective-permute-start(bf16[2,2,64,1024]{3,2,1,0:T(8,128)(2,1)S(1)} %pad_maximum_fusion.2), channel_id=1, source_target_pairs={{1,0},{2,1},{3,2},{5,4},{6,5},{7,6},{9,8},{10,9},{11,10},{13,12},{... | collective-permute-start | bytes 1572872 | tf_op jit(solution)/shard_map/ppermute | solution.py:95
  19.1 4.3 %collective-permute-start.6 = (f32[64]{0:T(128)S(1)}, f32[64]{0:T(128)S(1)}, u32[]{:S(2)}, u32[]{:S(2)}) collective-permute-start(f32[64]{0:T(128)S(1)} %get-tuple-element.72), channel_id=1, source_target_pairs={{0,4},{4,12},{8,20},{12,28},{16,0},{20,8},{24,16},{28,24},{1,5},{5... | collective-permute-start | bytes 776 | tf_op jit(solution)/shard_map/ppermute | solution.py:61
  24.7 2.8 %collective-permute-done.7 = bf16[2,2,64,1024]{3,2,1,0:T(8,128)(2,1)S(1)} collective-permute-done((bf16[2,2,64,1024]{3,2,1,0:T(8,128)(2,1)S(1)}, bf16[2,2,64,1024]{3,2,1,0:T(8,128)(2,1)S(1)}, u32[]{:S(2)}, u32[]{:S(2)}) %collective-permute-start.7) | collective-permute-done | bytes 524320 | tf_op jit(solution)/shard_map/ppermute | solution.py:92
  27.5 4.1 %collective-permute-done.4 = bf16[2,2,64,1024]{3,2,1,0:T(8,128)(2,1)S(1)} collective-permute-done((bf16[2,2,64,1024]{3,2,1,0:T(8,128)(2,1)S(1)}, bf16[2,2,64,1024]{3,2,1,0:T(8,128)(2,1)S(1)}, u32[]{:S(2)}, u32[]{:S(2)}) %collective-permute-start.4) | collective-permute-done | bytes 524320 | tf_op jit(solution)/shard_map/ppermute | solution.py:95
  32.9 1.5 %collective-permute-start.9 = (bf16[2,2,64,1024]{3,2,1,0:T(8,128)(2,1)S(1)}, bf16[2,2,64,1024]{3,2,1,0:T(8,128)(2,1)}, u32[]{:S(2)}, u32[]{:S(2)}) collective-permute-start(bf16[2,2,64,1024]{3,2,1,0:T(8,128)(2,1)S(1)} %collective-permute-done.7), channel_id=1, source_target_pairs={{1,2},{2,3},{5,6},{6,7},{9,10},{10,11},{13,14},{14,15},{17,18},{18... | collective-permute-start | bytes 1572872 | tf_op jit(solution)/shard_map/ppermute | solution.py:92
  34.5 1.6 %collective-permute-start.8 = (bf16[2,2,64,1024]{3,2,1,0:T(8,128)(2,1)S(1)}, bf16[2,2,64,1024]{3,2,1,0:T(8,128)(2,1)S(1)}, u32[]{:S(2)}, u32[]{:S(2)}) collective-permute-start(bf16[2,2,64,1024]{3,2,1,0:T(8,128)(2,1)S(1)} %select_select_fusion.2), channel_id=1, source_target_pairs={{0,8},{8,0},{4,12},{12,4},{1,9},{9,1},{5,13},{13,5},{2,10},{10,2},... | collective-permute-start | bytes 1572872 | tf_op jit(solution)/shard_map/ppermute | solution.py:110
  36.1 5.9 %broadcast_select_fusion = (bf16[1024,2048]{1,0:T(8,128)(2,1)S(1)}, bf16[1024,2048]{1,0:T(8,128)(2,1)S(1)}) fusion(pred[]{:T(512)S(6)} %eq.76, bf16[1024,4096]{1,0:T(8,128)(2,1)} %collective-permute-done.10, s32[]{:T(128)S(6)} %select_n.247, bf16[1024,4096]{1,0:T(8,128)(2,1)} %param.5), kind=kLoop, calls=%fused_computation | loop fusion | flops 4194304 | bytes 16777220 | tf_op jit(solution)/shard_map/jit(_where)/select_n | solution.py:116
  42.0 4.4 %collective-permute-done.8 = bf16[2,2,64,1024]{3,2,1,0:T(8,128)(2,1)S(1)} collective-permute-done((bf16[2,2,64,1024]{3,2,1,0:T(8,128)(2,1)S(1)}, bf16[2,2,64,1024]{3,2,1,0:T(8,128)(2,1)S(1)}, u32[]{:S(2)}, u32[]{:S(2)}) %collective-permute-start.8) | collective-permute-done | bytes 524320 | tf_op jit(solution)/shard_map/ppermute | solution.py:110
  46.4 5.0 %collective-permute-start.12 = (bf16[2,2,64,1024]{3,2,1,0:T(8,128)(2,1)S(1)}, bf16[2,2,64,1024]{3,2,1,0:T(8,128)(2,1)S(1)}, u32[]{:S(2)}, u32[]{:S(2)}) collective-permute-start(bf16[2,2,64,1024]{3,2,1,0:T(8,128)(2,1)S(1)} %pad_maximum_fusion.2), channel_id=1, source_target_pairs={{0,3},{4,7},{11,8},{15,12},{16,19},{20,23},{27,24},{31,28}} | collective-permute-start | bytes 1572872 | tf_op jit(solution)/shard_map/ppermute | solution.py:138
  53.4 1.5 %collective-permute-start.14 = (bf16[2,2,64,1024]{3,2,1,0:T(8,128)(2,1)S(1)}, bf16[2,2,64,1024]{3,2,1,0:T(8,128)(2,1)S(1)}, u32[]{:S(2)}, u32[]{:S(2)}) collective-permute-start(bf16[2,2,64,1024]{3,2,1,0:T(8,128)(2,1)S(1)} %get-tuple-element.47), channel_id=1, source_target_pairs={{1,9},{2,10},{3,11},{5,13},{6,14},{7,15},{8,0},{9,1},{10,2},{12,4}... | collective-permute-start | bytes 1572872 | tf_op jit(solution)/shard_map/ppermute | solution.py:127
  55.1 2.3 %fusion.52 = f32[512,2048]{1,0:T(8,128)S(1)} fusion(bf16[512,1024]{1,0:T(8,128)(2,1)S(1)} %bitcast.118, bf16[1024,2048]{1,0:T(8,128)(2,1)S(1)} %get-tuple-element.26), kind=kOutput, calls=%fused_computation.121 | convolution fusion | flops 2147483648 | bytes 9437184 | tf_op jit(solution)/shard_map/dot_general | solution.py:81
  57.5 1.9 %collective-permute-done.12 = bf16[2,2,64,1024]{3,2,1,0:T(8,128)(2,1)S(1)} collective-permute-done((bf16[2,2,64,1024]{3,2,1,0:T(8,128)(2,1)S(1)}, bf16[2,2,64,1024]{3,2,1,0:T(8,128)(2,1)S(1)}, u32[]{:S(2)}, u32[]{:S(2)}) %collective-permute-start.12) | collective-permute-done | bytes 524320 | tf_op jit(solution)/shard_map/ppermute | solution.py:138
  59.4 6.2 %collective-permute-done.14 = bf16[2,2,64,1024]{3,2,1,0:T(8,128)(2,1)S(1)} collective-permute-done((bf16[2,2,64,1024]{3,2,1,0:T(8,128)(2,1)S(1)}, bf16[2,2,64,1024]{3,2,1,0:T(8,128)(2,1)S(1)}, u32[]{:S(2)}, u32[]{:S(2)}) %collective-permute-start.14) | collective-permute-done | bytes 524320 | tf_op jit(solution)/shard_map/ppermute | solution.py:127
  68.8 3.3 %collective-permute-start.15 = (f16[2,2,64,1024]{3,2,0,1:T(8,128)(2,1)S(1)}, f16[2,2,64,1024]{3,2,0,1:T(8,128)(2,1)S(1)}, u32[]{:S(2)}, u32[]{:S(2)}) collective-permute-start(f16[2,2,64,1024]{3,2,0,1:T(8,128)(2,1)S(1)} %fusion.24), channel_id=1, source_target_pairs={{0,4},{4,0},{8,12},{12,8},{1,5},{5,1},{9,13},{13,9},{2,6},{6,2},{1... | collective-permute-start | bytes 1572872 | tf_op jit(solution)/shard_map/ppermute | solution.py:191
  72.1 2.3 %fusion.53 = f32[512,2048]{1,0:T(8,128)S(1)} fusion(bf16[512,1024]{1,0:T(8,128)(2,1)S(1)} %bitcast.128, bf16[1024,2048]{1,0:T(8,128)(2,1)S(1)} %get-tuple-element.26), kind=kOutput, calls=%fused_computation.122 | convolution fusion | flops 2147483648 | bytes 9437184 | tf_op jit(solution)/shard_map/dot_general | solution.py:81
  77.1 2.1 %collective-permute-start.20 = (f16[2,2,64,1024]{3,2,1,0:T(8,128)(2,1)S(1)}, f16[2,2,64,1024]{3,2,1,0:T(8,128)(2,1)S(1)}, u32[]{:S(2)}, u32[]{:S(2)}) collective-permute-start(f16[2,2,64,1024]{3,2,1,0:T(8,128)(2,1)S(1)} %fusion.23), channel_id=1, source_target_pairs={{0,8},{8,0},{4,12},{12,4},{1,9},{9,1},{5,13},{13,5},{2,10},{10,2},... | collective-permute-start | bytes 1572872 | tf_op jit(solution)/shard_map/ppermute | solution.py:192
  79.5 3.8 %collective-permute-done.21 = f16[2,2,64,1024]{3,2,1,0:T(8,128)(2,1)S(1)} collective-permute-done((f16[2,2,64,1024]{3,2,1,0:T(8,128)(2,1)S(1)}, f16[2,2,64,1024]{3,2,1,0:T(8,128)(2,1)S(1)}, u32[]{:S(2)}, u32[]{:S(2)}) %collective-permute-start.21) | collective-permute-done | bytes 524320 | tf_op jit(solution)/shard_map/ppermute | solution.py:192
  83.5 3.3 %collective-permute-start.22 = (f16[2,64,1024]{2,1,0:T(8,128)(2,1)S(1)}, f16[2,64,1024]{2,1,0:T(8,128)(2,1)S(1)}, u32[]{:S(2)}, u32[]{:S(2)}) collective-permute-start(f16[2,64,1024]{2,1,0:T(8,128)(2,1)S(1)} %fusion.33), channel_id=1, source_target_pairs={{0,4},{4,0},{8,12},{12,8},{1,5},{5,1},{9,13},{13,9},{2,6},{6,2},{1... | collective-permute-start | bytes 786440 | tf_op jit(solution)/shard_map/ppermute | solution.py:204
  87.1 7.4 %collective-permute-done.20 = f16[2,2,64,1024]{3,2,1,0:T(8,128)(2,1)S(1)} collective-permute-done((f16[2,2,64,1024]{3,2,1,0:T(8,128)(2,1)S(1)}, f16[2,2,64,1024]{3,2,1,0:T(8,128)(2,1)S(1)}, u32[]{:S(2)}, u32[]{:S(2)}) %collective-permute-start.20) | collective-permute-done | bytes 524320 | tf_op jit(solution)/shard_map/ppermute | solution.py:192
  94.7 3.3 %collective-permute-start.25 = (f16[2,64,1024]{2,1,0:T(8,128)(2,1)S(1)}, f16[2,64,1024]{2,1,0:T(8,128)(2,1)S(1)}, u32[]{:S(2)}, u32[]{:S(2)}) collective-permute-start(f16[2,64,1024]{2,1,0:T(8,128)(2,1)S(1)} %fusion.32), channel_id=1, source_target_pairs={{0,4},{4,0},{8,12},{12,8},{1,5},{5,1},{9,13},{13,9},{2,6},{6,2},{1... | collective-permute-start | bytes 786440 | tf_op jit(solution)/shard_map/ppermute | solution.py:204
  98.4 3.4 %collective-permute-done.22 = f16[2,64,1024]{2,1,0:T(8,128)(2,1)S(1)} collective-permute-done((f16[2,64,1024]{2,1,0:T(8,128)(2,1)S(1)}, f16[2,64,1024]{2,1,0:T(8,128)(2,1)S(1)}, u32[]{:S(2)}, u32[]{:S(2)}) %collective-permute-start.22) | collective-permute-done | bytes 262176 | tf_op jit(solution)/shard_map/ppermute | solution.py:204
  102.1 5.1 %collective-permute-done.25 = f16[2,64,1024]{2,1,0:T(8,128)(2,1)S(1)} collective-permute-done((f16[2,64,1024]{2,1,0:T(8,128)(2,1)S(1)}, f16[2,64,1024]{2,1,0:T(8,128)(2,1)S(1)}, u32[]{:S(2)}, u32[]{:S(2)}) %collective-permute-start.25) | collective-permute-done | bytes 262176 | tf_op jit(solution)/shard_map/ppermute | solution.py:204
  107.7 1.4 %collective-permute-done.26 = f16[64,2048]{1,0:T(8,128)(2,1)S(1)} collective-permute-done((f16[64,2048]{1,0:T(8,128)(2,1)S(1)}, f16[64,2048]{1,0:T(8,128)(2,1)S(1)}, u32[]{:S(2)}, u32[]{:S(2)}) %collective-permute-start.26) | collective-permute-done | bytes 262176 | tf_op jit(solution)/shard_map/ppermute | solution.py:75
  112.7 1.6 %collective-permute-start.29 = (f32[4,64]{1,0:T(4,128)S(1)}, f32[4,64]{1,0:T(4,128)S(1)}, u32[]{:S(2)}, u32[]{:S(2)}) collective-permute-start(f32[4,64]{1,0:T(4,128)S(1)} %get-tuple-element.64), channel_id=1, source_target_pairs={{0,3},{1,0},{2,1},{3,2},{4,7},{5,4},{6,5},{7,6},{8,11},{9,8},{10,9... | collective-permute-start | bytes 3080 | tf_op jit(solution)/shard_map/ppermute | solution.py:44
  114.3 1.6 %collective-permute-done.27 = f32[4,64]{1,0:T(4,128)S(1)} collective-permute-done((f32[4,64]{1,0:T(4,128)S(1)}, f32[4,64]{1,0:T(4,128)S(1)}, u32[]{:S(2)}, u32[]{:S(2)}) %collective-permute-start.27) | collective-permute-done | bytes 1056 | tf_op jit(solution)/shard_map/ppermute | solution.py:44
  116.5 1.6 %fusion.20 = (f32[64,4096]{1,0:T(8,128)}, f32[64,4096]{1,0:T(8,128)}) fusion(f32[64]{0:T(128)S(1)} %get-tuple-element.65, f32[64]{0:T(128)S(1)} %get-tuple-element.67, f16[64,2048]{1,0:T(8,128)(2,1)S(1)} %get-tuple-element.58, f16[64,2048]{1,0:T(8,128)(2,1)S(1)} %get-tuple-element.56, f32[64,4096]{1,0:T(8,128)S(1)} %get-tuple-element.41, ...), kind=kLoop, calls=%fused_computation.30 | loop fusion | flops 1310720 | bytes 3670784 | tf_op jit(solution)/shard_map/sub | solution.py:242
  (85 shorter events, 22.3 us)
Async XLA Ops:
  0.6 35.5 %collective-permute-start.10 = (bf16[1024,4096]{1,0:T(8,128)(2,1)}, bf16[1024,4096]{1,0:T(8,128)(2,1)}, u32[]{:S(2)}, u32[]{:S(2)}) collective-permute-start(bf16[1024,4096]{1,0:T(8,128)(2,1)} %param.5), channel_id=1, source_target_pairs={{0,16},{16,0},{1,17},{17,1},{2,18},{18,2},{3,19},{19,3},{4,20},{20... | collective-permute-start | bytes 25165832 | tf_op jit(solution)/shard_map/ppermute | solution.py:41
  3.0 11.7 %collective-permute-start = (bf16[2,64,1024]{2,1,0:T(8,128)(2,1)S(1)}, bf16[2,64,1024]{2,1,0:T(8,128)(2,1)S(1)}, u32[]{:S(2)}, u32[]{:S(2)}) collective-permute-start(bf16[2,64,1024]{2,1,0:T(8,128)(2,1)S(1)} %constant_dynamic-slice_fusion.6), channel_id=1, source_target_pairs={{0,4},{4,0},{8,12},{12,8},{1,5},{5,1},{9,13},{13,9},{2,6},{6,2},{1... | collective-permute-start | bytes 786440 | tf_op jit(solution)/shard_map/ppermute | solution.py:85
  6.8 5.6 %collective-permute-start.1 = (f32[128]{0:T(128)S(1)}, f32[128]{0:T(128)S(1)}, u32[]{:S(2)}, u32[]{:S(2)}) collective-permute-start(f32[128]{0:T(128)S(1)} %multiply_reduce_fusion), channel_id=1, source_target_pairs={{0,1},{1,2},{2,3},{3,0},{4,5},{5,6},{6,7},{7,4},{8,9},{9,10},{10,1... | collective-permute-start | bytes 1544 | tf_op jit(solution)/shard_map/ppermute | solution.py:44
  8.5 4.4 %collective-permute-start.2 = (f32[128]{0:T(128)S(1)}, f32[128]{0:T(128)S(1)}, u32[]{:S(2)}, u32[]{:S(2)}) collective-permute-start(f32[128]{0:T(128)S(1)} %multiply_reduce_fusion), channel_id=1, source_target_pairs={{0,2},{1,3},{2,0},{3,1},{4,6},{5,7},{6,4},{7,5},{8,10},{9,11},{10,... | collective-permute-start | bytes 1544 | tf_op jit(solution)/shard_map/ppermute | solution.py:44
  11.0 3.5 %collective-permute-start.3 = (f32[128]{0:T(128)S(1)}, f32[128]{0:T(128)S(1)}, u32[]{:S(2)}, u32[]{:S(2)}) collective-permute-start(f32[128]{0:T(128)S(1)} %multiply_reduce_fusion), channel_id=1, source_target_pairs={{0,3},{1,0},{2,1},{3,2},{4,7},{5,4},{6,5},{7,6},{8,11},{9,8},{10,9... | collective-permute-start | bytes 1544 | tf_op jit(solution)/shard_map/ppermute | solution.py:44
  14.9 12.6 %collective-permute-start.7 = (bf16[2,2,64,1024]{3,2,1,0:T(8,128)(2,1)S(1)}, bf16[2,2,64,1024]{3,2,1,0:T(8,128)(2,1)S(1)}, u32[]{:S(2)}, u32[]{:S(2)}) collective-permute-start(bf16[2,2,64,1024]{3,2,1,0:T(8,128)(2,1)S(1)} %pad_maximum_fusion.2), channel_id=1, source_target_pairs={{0,1},{1,2},{2,3},{4,5},{5,6},{6,7},{8,9},{9,10},{10,11},{12,13},{... | collective-permute-start | bytes 1572872 | tf_op jit(solution)/shard_map/ppermute | solution.py:92
  17.0 14.6 %collective-permute-start.4 = (bf16[2,2,64,1024]{3,2,1,0:T(8,128)(2,1)S(1)}, bf16[2,2,64,1024]{3,2,1,0:T(8,128)(2,1)S(1)}, u32[]{:S(2)}, u32[]{:S(2)}) collective-permute-start(bf16[2,2,64,1024]{3,2,1,0:T(8,128)(2,1)S(1)} %pad_maximum_fusion.2), channel_id=1, source_target_pairs={{1,0},{2,1},{3,2},{5,4},{6,5},{7,6},{9,8},{10,9},{11,10},{13,12},{... | collective-permute-start | bytes 1572872 | tf_op jit(solution)/shard_map/ppermute | solution.py:95
  18.5 5.0 %collective-permute-start.5 = (f32[64]{0:T(128)S(1)}, f32[64]{0:T(128)S(1)}, u32[]{:S(2)}, u32[]{:S(2)}) collective-permute-start(f32[64]{0:T(128)S(1)} %get-tuple-element.71), channel_id=1, source_target_pairs={{0,0},{4,8},{8,16},{12,24},{16,4},{20,12},{24,20},{28,28},{1,1},{5... | collective-permute-start | bytes 776 | tf_op jit(solution)/shard_map/ppermute | solution.py:61
  19.1 5.6 %collective-permute-start.6 = (f32[64]{0:T(128)S(1)}, f32[64]{0:T(128)S(1)}, u32[]{:S(2)}, u32[]{:S(2)}) collective-permute-start(f32[64]{0:T(128)S(1)} %get-tuple-element.72), channel_id=1, source_target_pairs={{0,4},{4,12},{8,20},{12,28},{16,0},{20,8},{24,16},{28,24},{1,5},{5... | collective-permute-start | bytes 776 | tf_op jit(solution)/shard_map/ppermute | solution.py:61
  31.6 14.7 %collective-permute-start.11 = (bf16[2,2,64,1024]{3,2,1,0:T(8,128)(2,1)S(1)}, bf16[2,2,64,1024]{3,2,1,0:T(8,128)(2,1)S(1)}, u32[]{:S(2)}, u32[]{:S(2)}) collective-permute-start(bf16[2,2,64,1024]{3,2,1,0:T(8,128)(2,1)S(1)} %collective-permute-done.4), channel_id=1, source_target_pairs={{1,0},{2,1},{5,4},{6,5},{9,8},{10,9},{13,12},{14,13},{17,16},{18,1... | collective-permute-start | bytes 1572872 | tf_op jit(solution)/shard_map/ppermute | solution.py:95
  32.9 13.5 %collective-permute-start.9 = (bf16[2,2,64,1024]{3,2,1,0:T(8,128)(2,1)S(1)}, bf16[2,2,64,1024]{3,2,1,0:T(8,128)(2,1)}, u32[]{:S(2)}, u32[]{:S(2)}) collective-permute-start(bf16[2,2,64,1024]{3,2,1,0:T(8,128)(2,1)S(1)} %collective-permute-done.7), channel_id=1, source_target_pairs={{1,2},{2,3},{5,6},{6,7},{9,10},{10,11},{13,14},{14,15},{17,18},{18... | collective-permute-start | bytes 1572872 | tf_op jit(solution)/shard_map/ppermute | solution.py:92
  34.5 11.8 %collective-permute-start.8 = (bf16[2,2,64,1024]{3,2,1,0:T(8,128)(2,1)S(1)}, bf16[2,2,64,1024]{3,2,1,0:T(8,128)(2,1)S(1)}, u32[]{:S(2)}, u32[]{:S(2)}) collective-permute-start(bf16[2,2,64,1024]{3,2,1,0:T(8,128)(2,1)S(1)} %select_select_fusion.2), channel_id=1, source_target_pairs={{0,8},{8,0},{4,12},{12,4},{1,9},{9,1},{5,13},{13,5},{2,10},{10,2},... | collective-permute-start | bytes 1572872 | tf_op jit(solution)/shard_map/ppermute | solution.py:110
  46.4 13.0 %collective-permute-start.12 = (bf16[2,2,64,1024]{3,2,1,0:T(8,128)(2,1)S(1)}, bf16[2,2,64,1024]{3,2,1,0:T(8,128)(2,1)S(1)}, u32[]{:S(2)}, u32[]{:S(2)}) collective-permute-start(bf16[2,2,64,1024]{3,2,1,0:T(8,128)(2,1)S(1)} %pad_maximum_fusion.2), channel_id=1, source_target_pairs={{0,3},{4,7},{11,8},{15,12},{16,19},{20,23},{27,24},{31,28}} | collective-permute-start | bytes 1572872 | tf_op jit(solution)/shard_map/ppermute | solution.py:138
  51.4 7.9 %collective-permute-start.13 = (bf16[2,2,64,1024]{3,2,1,0:T(8,128)(2,1)S(1)}, bf16[2,2,64,1024]{3,2,1,0:T(8,128)(2,1)S(1)}, u32[]{:S(2)}, u32[]{:S(2)}) collective-permute-start(bf16[2,2,64,1024]{3,2,1,0:T(8,128)(2,1)S(1)} %pad_maximum_fusion.2), channel_id=1, source_target_pairs={{3,8},{7,12},{8,3},{12,7},{19,24},{23,28},{24,19},{28,23}} | collective-permute-start | bytes 1572872 | tf_op jit(solution)/shard_map/ppermute | solution.py:138
  53.4 12.1 %collective-permute-start.14 = (bf16[2,2,64,1024]{3,2,1,0:T(8,128)(2,1)S(1)}, bf16[2,2,64,1024]{3,2,1,0:T(8,128)(2,1)S(1)}, u32[]{:S(2)}, u32[]{:S(2)}) collective-permute-start(bf16[2,2,64,1024]{3,2,1,0:T(8,128)(2,1)S(1)} %get-tuple-element.47), channel_id=1, source_target_pairs={{1,9},{2,10},{3,11},{5,13},{6,14},{7,15},{8,0},{9,1},{10,2},{12,4}... | collective-permute-start | bytes 1572872 | tf_op jit(solution)/shard_map/ppermute | solution.py:127
  55.0 17.1 %collective-permute-start.16 = (bf16[2,2,2,64,1024]{4,3,2,1,0:T(8,128)(2,1)S(1)}, bf16[2,2,2,64,1024]{4,3,2,1,0:T(8,128)(2,1)S(1)}, u32[]{:S(2)}, u32[]{:S(2)}) collective-permute-start(bf16[2,2,2,64,1024]{4,3,2,1,0:T(8,128)(2,1)S(1)} %pad_maximum_fusion), channel_id=1, source_target_pairs={{0,16},{16,0},{1,17},{17,1},{2,18},{18,2},{3,19},{19,3},{4,20},{20... | collective-permute-start | bytes 3145736 | tf_op jit(solution)/shard_map/ppermute | solution.py:75
  65.8 8.7 %collective-permute-start.17 = (bf16[2,2,2,64,1024]{4,3,2,1,0:T(8,128)(2,1)S(1)}, bf16[2,2,2,64,1024]{4,3,2,1,0:T(8,128)(2,1)S(1)}, u32[]{:S(2)}, u32[]{:S(2)}) collective-permute-start(bf16[2,2,2,64,1024]{4,3,2,1,0:T(8,128)(2,1)S(1)} %pad_maximum_fusion.1), channel_id=1, source_target_pairs={{0,16},{16,0},{1,17},{17,1},{2,18},{18,2},{3,19},{19,3},{4,20},{20... | collective-permute-start | bytes 3145736 | tf_op jit(solution)/shard_map/ppermute | solution.py:75
  68.5 14.8 %collective-permute-start.21 = (f16[2,2,64,1024]{3,2,1,0:T(8,128)(2,1)S(1)}, f16[2,2,64,1024]{3,2,1,0:T(8,128)(2,1)S(1)}, u32[]{:S(2)}, u32[]{:S(2)}) collective-permute-start(f16[2,2,64,1024]{3,2,1,0:T(8,128)(2,1)S(1)} %fusion.22), channel_id=1, source_target_pairs={{0,8},{8,0},{4,12},{12,4},{1,9},{9,1},{5,13},{13,5},{2,10},{10,2},... | collective-permute-start | bytes 1572872 | tf_op jit(solution)/shard_map/ppermute | solution.py:192
  68.8 17.9 %collective-permute-start.15 = (f16[2,2,64,1024]{3,2,0,1:T(8,128)(2,1)S(1)}, f16[2,2,64,1024]{3,2,0,1:T(8,128)(2,1)S(1)}, u32[]{:S(2)}, u32[]{:S(2)}) collective-permute-start(f16[2,2,64,1024]{3,2,0,1:T(8,128)(2,1)S(1)} %fusion.24), channel_id=1, source_target_pairs={{0,4},{4,0},{8,12},{12,8},{1,5},{5,1},{9,13},{13,9},{2,6},{6,2},{1... | collective-permute-start | bytes 1572872 | tf_op jit(solution)/shard_map/ppermute | solution.py:191
  77.1 17.4 %collective-permute-start.20 = (f16[2,2,64,1024]{3,2,1,0:T(8,128)(2,1)S(1)}, f16[2,2,64,1024]{3,2,1,0:T(8,128)(2,1)S(1)}, u32[]{:S(2)}, u32[]{:S(2)}) collective-permute-start(f16[2,2,64,1024]{3,2,1,0:T(8,128)(2,1)S(1)} %fusion.23), channel_id=1, source_target_pairs={{0,8},{8,0},{4,12},{12,4},{1,9},{9,1},{5,13},{13,5},{2,10},{10,2},... | collective-permute-start | bytes 1572872 | tf_op jit(solution)/shard_map/ppermute | solution.py:192
  79.4 18.6 %collective-permute-start.19 = (f16[2,2,64,1024]{3,2,0,1:T(8,128)(2,1)S(1)}, f16[2,2,64,1024]{3,2,0,1:T(8,128)(2,1)S(1)}, u32[]{:S(2)}, u32[]{:S(2)}) collective-permute-start(f16[2,2,64,1024]{3,2,0,1:T(8,128)(2,1)S(1)} %fusion.25), channel_id=1, source_target_pairs={{0,4},{4,0},{8,12},{12,8},{1,5},{5,1},{9,13},{13,9},{2,6},{6,2},{1... | collective-permute-start | bytes 1572872 | tf_op jit(solution)/shard_map/ppermute | solution.py:191
  83.5 18.3 %collective-permute-start.22 = (f16[2,64,1024]{2,1,0:T(8,128)(2,1)S(1)}, f16[2,64,1024]{2,1,0:T(8,128)(2,1)S(1)}, u32[]{:S(2)}, u32[]{:S(2)}) collective-permute-start(f16[2,64,1024]{2,1,0:T(8,128)(2,1)S(1)} %fusion.33), channel_id=1, source_target_pairs={{0,4},{4,0},{8,12},{12,8},{1,5},{5,1},{9,13},{13,9},{2,6},{6,2},{1... | collective-permute-start | bytes 786440 | tf_op jit(solution)/shard_map/ppermute | solution.py:204
  87.0 14.9 %collective-permute-start.18 = (f16[2,64,1024]{2,1,0:T(8,128)(2,1)S(1)}, f16[2,64,1024]{2,1,0:T(8,128)(2,1)S(1)}, u32[]{:S(2)}, u32[]{:S(2)}) collective-permute-start(f16[2,64,1024]{2,1,0:T(8,128)(2,1)S(1)} %fusion.30), channel_id=1, source_target_pairs={{0,8},{8,0},{4,12},{12,4},{1,9},{9,1},{5,13},{13,5},{2,10},{10,2},... | collective-permute-start | bytes 786440 | tf_op jit(solution)/shard_map/ppermute | solution.py:203
  94.7 12.5 %collective-permute-start.25 = (f16[2,64,1024]{2,1,0:T(8,128)(2,1)S(1)}, f16[2,64,1024]{2,1,0:T(8,128)(2,1)S(1)}, u32[]{:S(2)}, u32[]{:S(2)}) collective-permute-start(f16[2,64,1024]{2,1,0:T(8,128)(2,1)S(1)} %fusion.32), channel_id=1, source_target_pairs={{0,4},{4,0},{8,12},{12,8},{1,5},{5,1},{9,13},{13,9},{2,6},{6,2},{1... | collective-permute-start | bytes 786440 | tf_op jit(solution)/shard_map/ppermute | solution.py:204
  98.2 9.0 %collective-permute-start.24 = (f16[2,64,1024]{2,1,0:T(8,128)(2,1)S(1)}, f16[2,64,1024]{2,1,0:T(8,128)(2,1)S(1)}, u32[]{:S(2)}, u32[]{:S(2)}) collective-permute-start(f16[2,64,1024]{2,1,0:T(8,128)(2,1)S(1)} %fusion.31), channel_id=1, source_target_pairs={{0,8},{8,0},{4,12},{12,4},{1,9},{9,1},{5,13},{13,5},{2,10},{10,2},... | collective-permute-start | bytes 786440 | tf_op jit(solution)/shard_map/ppermute | solution.py:203
  102.0 5.5 %collective-permute-start.23 = (f16[64,2048]{1,0:T(8,128)(2,1)S(1)}, f16[64,2048]{1,0:T(8,128)(2,1)S(1)}, u32[]{:S(2)}, u32[]{:S(2)}) collective-permute-start(f16[64,2048]{1,0:T(8,128)(2,1)S(1)} %fusion.39), channel_id=1, source_target_pairs={{0,16},{16,0},{1,17},{17,1},{2,18},{18,2},{3,19},{19,3},{4,20},{20... | collective-permute-start | bytes 786440 | tf_op jit(solution)/shard_map/ppermute | solution.py:75
  107.4 1.6 %collective-permute-start.26 = (f16[64,2048]{1,0:T(8,128)(2,1)S(1)}, f16[64,2048]{1,0:T(8,128)(2,1)S(1)}, u32[]{:S(2)}, u32[]{:S(2)}) collective-permute-start(f16[64,2048]{1,0:T(8,128)(2,1)S(1)} %fusion.37), channel_id=1, source_target_pairs={{0,16},{16,0},{1,17},{17,1},{2,18},{18,2},{3,19},{19,3},{4,20},{20... | collective-permute-start | bytes 786440 | tf_op jit(solution)/shard_map/ppermute | solution.py:75
  110.4 5.4 %collective-permute-start.27 = (f32[4,64]{1,0:T(4,128)S(1)}, f32[4,64]{1,0:T(4,128)S(1)}, u32[]{:S(2)}, u32[]{:S(2)}) collective-permute-start(f32[4,64]{1,0:T(4,128)S(1)} %get-tuple-element.64), channel_id=1, source_target_pairs={{0,1},{1,2},{2,3},{3,0},{4,5},{5,6},{6,7},{7,4},{8,9},{9,10},{10,1... | collective-permute-start | bytes 3080 | tf_op jit(solution)/shard_map/ppermute | solution.py:44
  111.7 4.5 %collective-permute-start.28 = (f32[4,64]{1,0:T(4,128)S(1)}, f32[4,64]{1,0:T(4,128)S(1)}, u32[]{:S(2)}, u32[]{:S(2)}) collective-permute-start(f32[4,64]{1,0:T(4,128)S(1)} %get-tuple-element.64), channel_id=1, source_target_pairs={{0,2},{1,3},{2,0},{3,1},{4,6},{5,7},{6,4},{7,5},{8,10},{9,11},{10,... | collective-permute-start | bytes 3080 | tf_op jit(solution)/shard_map/ppermute | solution.py:44
  112.7 3.7 %collective-permute-start.29 = (f32[4,64]{1,0:T(4,128)S(1)}, f32[4,64]{1,0:T(4,128)S(1)}, u32[]{:S(2)}, u32[]{:S(2)}) collective-permute-start(f32[4,64]{1,0:T(4,128)S(1)} %get-tuple-element.64), channel_id=1, source_target_pairs={{0,3},{1,0},{2,1},{3,2},{4,7},{5,4},{6,5},{7,6},{8,11},{9,8},{10,9... | collective-permute-start | bytes 3080 | tf_op jit(solution)/shard_map/ppermute | solution.py:44

commit v22 on v21

--- a/solution.py
+++ b/solution.py
@@ -96,9 +96,11 @@
 
         below, above = [own, up(own, 1)], [own, down(own, 1)]
 
-        def quarter(place, reach):
-            part = own
-            for k in range(1, reach + 1):
+        def quarter(place, reach, least=0):
+            part = below[least]
+            if least:
+                part = jnp.where(level > place, part, above[least])
+            for k in range(least + 1, reach + 1):
                 part = jnp.where(level - place == k, below[k], part)
                 part = jnp.where(place - level == k, above[k], part)
             return part
@@ -124,8 +126,8 @@
         pairs = [(b * vocab + z, (b ^ 2) * vocab + z) for b in range(4) for z in range(vocab)]
         lone = [b * vocab + (vocab - 1) * (b // 2) for b in range(4)]
         early = [pair for pair in pairs if pair[0] not in lone]
-        got_early = lax.ppermute(quarter(far, 2), ("batch", "vocab"), early)
-        mine_early = lax.optimization_barrier(quarter(y + 2 * (1 - first), 2))
+        got_early = lax.ppermute(quarter(far, 2, 1), ("batch", "vocab"), early)
+        mine_early = lax.optimization_barrier(quarter(y + 2 * (1 - first), 2, 1))
         is_late = (level == 0) & (y == 1) | (level == vocab - 1) & (y == 0)
         near_part = dot(near, near_weight)
         sent = after(own, below[2], above[2])

time: 119 us -> 117 us (0.983)
  no operation moved by 1% of the time
where the time goes in v22:
time: 117 us
  waiting for transfers between devices  45.8 us (39%)
  starting transfers between devices  44.5 us (38%)
  other arithmetic  15.3 us (13%)
  matrix products  9.73 us (8%)
  between operations  1.17 us (1%)
    ppermute x2, waiting for transfers between devices, on_device(): away_y = lax.ppermute(sends[i][1], 'batch', Y_SWAP)  11.2 us
    ppermute x6, starting transfers between devices, shifted(): lax.ppermute(value, 'vocab', [(i, (i + k) % vocab) for i in range(vocab)])  9.91 us
    dot_general x6, matrix products, dot(): jnp.dot(left.reshape(-1, block), weight, preferred_element_type=jnp.float32)  9.73 us
    ppermute x2, waiting for transfers between devices, on_device(): next_x = lax.ppermute(more_sends[i][1], 'batch', X_SWAP)  8.42 us
    ppermute x2, starting transfers between devices, on_device(): next_x = lax.ppermute(more_sends[i][1], 'batch', X_SWAP)  6.53 us
    select_n x1, other arithmetic, line_parts(): jnp.where(keep_near, taken, kept)  5.87 us
    ppermute x2, starting transfers between devices, line_parts(): ends.append(lax.ppermute(sent, ('batch', 'vocab'), sorted(moves)))  5.5 us
    ppermute x1, waiting for transfers between devices, line_parts(): got_early = lax.ppermute(quarter(far, 2, 1), ('batch', 'vocab'), early)  5.11 us
  transfers between devices with their start and end apart: 30, of which 16 were waited for; matrix products, arithmetic and copies ran while one was open for 19% of the time, Pallas kernels for 0%

profile of v22, /device:TPU:0, one launch (start us, length us, event | category | flops | bytes accessed | tf_op | source)
XLA Modules:
  0.0 117.0 jit_solution(13919643282745560545)
XLA Ops:
  3.0 2.6 %collective-permute-start = (bf16[2,64,1024]{2,1,0:T(8,128)(2,1)S(1)}, bf16[2,64,1024]{2,1,0:T(8,128)(2,1)S(1)}, u32[]{:S(2)}, u32[]{:S(2)}) collective-permute-start(bf16[2,64,1024]{2,1,0:T(8,128)(2,1)S(1)} %constant_dynamic-slice_fusion.6), channel_id=1, source_target_pairs={{0,4},{4,0},{8,12},{12,8},{1,5},{5,1},{9,13},{13,9},{2,6},{6,2},{1... | collective-permute-start | bytes 786440 | tf_op jit(solution)/shard_map/ppermute | solution.py:85
  6.8 1.6 %collective-permute-start.1 = (f32[128]{0:T(128)S(1)}, f32[128]{0:T(128)S(1)}, u32[]{:S(2)}, u32[]{:S(2)}) collective-permute-start(f32[128]{0:T(128)S(1)} %multiply_reduce_fusion), channel_id=1, source_target_pairs={{0,1},{1,2},{2,3},{3,0},{4,5},{5,6},{6,7},{7,4},{8,9},{9,10},{10,1... | collective-permute-start | bytes 1544 | tf_op jit(solution)/shard_map/ppermute | solution.py:44
  8.5 2.6 %collective-permute-start.2 = (f32[128]{0:T(128)S(1)}, f32[128]{0:T(128)S(1)}, u32[]{:S(2)}, u32[]{:S(2)}) collective-permute-start(f32[128]{0:T(128)S(1)} %multiply_reduce_fusion), channel_id=1, source_target_pairs={{0,2},{1,3},{2,0},{3,1},{4,6},{5,7},{6,4},{7,5},{8,10},{9,11},{10,... | collective-permute-start | bytes 1544 | tf_op jit(solution)/shard_map/ppermute | solution.py:44
  11.0 1.3 %collective-permute-start.3 = (f32[128]{0:T(128)S(1)}, f32[128]{0:T(128)S(1)}, u32[]{:S(2)}, u32[]{:S(2)}) collective-permute-start(f32[128]{0:T(128)S(1)} %multiply_reduce_fusion), channel_id=1, source_target_pairs={{0,3},{1,0},{2,1},{3,2},{4,7},{5,4},{6,5},{7,6},{8,11},{9,8},{10,9... | collective-permute-start | bytes 1544 | tf_op jit(solution)/shard_map/ppermute | solution.py:44
  12.9 1.7 %collective-permute-done.3 = f32[128]{0:T(128)S(1)} collective-permute-done((f32[128]{0:T(128)S(1)}, f32[128]{0:T(128)S(1)}, u32[]{:S(2)}, u32[]{:S(2)}) %collective-permute-start.3) | collective-permute-done | bytes 544 | tf_op jit(solution)/shard_map/ppermute | solution.py:44
  14.9 2.2 %collective-permute-start.7 = (bf16[2,2,64,1024]{3,2,1,0:T(8,128)(2,1)S(1)}, bf16[2,2,64,1024]{3,2,1,0:T(8,128)(2,1)S(1)}, u32[]{:S(2)}, u32[]{:S(2)}) collective-permute-start(bf16[2,2,64,1024]{3,2,1,0:T(8,128)(2,1)S(1)} %pad_maximum_fusion.2), channel_id=1, source_target_pairs={{0,1},{1,2},{2,3},{4,5},{5,6},{6,7},{8,9},{9,10},{10,11},{12,13},{... | collective-permute-start | bytes 1572872 | tf_op jit(solution)/shard_map/ppermute | solution.py:92
  17.0 1.3 %collective-permute-start.4 = (bf16[2,2,64,1024]{3,2,1,0:T(8,128)(2,1)S(1)}, bf16[2,2,64,1024]{3,2,1,0:T(8,128)(2,1)S(1)}, u32[]{:S(2)}, u32[]{:S(2)}) collective-permute-start(bf16[2,2,64,1024]{3,2,1,0:T(8,128)(2,1)S(1)} %pad_maximum_fusion.2), channel_id=1, source_target_pairs={{1,0},{2,1},{3,2},{5,4},{6,5},{7,6},{9,8},{10,9},{11,10},{13,12},{... | collective-permute-start | bytes 1572872 | tf_op jit(solution)/shard_map/ppermute | solution.py:95
  19.1 4.3 %collective-permute-start.6 = (f32[64]{0:T(128)S(1)}, f32[64]{0:T(128)S(1)}, u32[]{:S(2)}, u32[]{:S(2)}) collective-permute-start(f32[64]{0:T(128)S(1)} %get-tuple-element.72), channel_id=1, source_target_pairs={{0,4},{4,12},{8,20},{12,28},{16,0},{20,8},{24,16},{28,24},{1,5},{5... | collective-permute-start | bytes 776 | tf_op jit(solution)/shard_map/ppermute | solution.py:61
  23.4 1.3 %collective-permute-done.6 = f32[64]{0:T(128)S(1)} collective-permute-done((f32[64]{0:T(128)S(1)}, f32[64]{0:T(128)S(1)}, u32[]{:S(2)}, u32[]{:S(2)}) %collective-permute-start.6) | collective-permute-done | bytes 288 | tf_op jit(solution)/shard_map/ppermute | solution.py:61
  24.7 2.8 %collective-permute-done.7 = bf16[2,2,64,1024]{3,2,1,0:T(8,128)(2,1)S(1)} collective-permute-done((bf16[2,2,64,1024]{3,2,1,0:T(8,128)(2,1)S(1)}, bf16[2,2,64,1024]{3,2,1,0:T(8,128)(2,1)S(1)}, u32[]{:S(2)}, u32[]{:S(2)}) %collective-permute-start.7) | collective-permute-done | bytes 524320 | tf_op jit(solution)/shard_map/ppermute | solution.py:92
  27.5 4.1 %collective-permute-done.4 = bf16[2,2,64,1024]{3,2,1,0:T(8,128)(2,1)S(1)} collective-permute-done((bf16[2,2,64,1024]{3,2,1,0:T(8,128)(2,1)S(1)}, bf16[2,2,64,1024]{3,2,1,0:T(8,128)(2,1)S(1)}, u32[]{:S(2)}, u32[]{:S(2)}) %collective-permute-start.4) | collective-permute-done | bytes 524320 | tf_op jit(solution)/shard_map/ppermute | solution.py:95
  34.5 1.5 %collective-permute-start.8 = (bf16[2,2,64,1024]{3,2,1,0:T(8,128)(2,1)}, bf16[2,2,64,1024]{3,2,1,0:T(8,128)(2,1)S(1)}, u32[]{:S(2)}, u32[]{:S(2)}) collective-permute-start(bf16[2,2,64,1024]{3,2,1,0:T(8,128)(2,1)} %select_select_fusion.2), channel_id=1, source_target_pairs={{0,8},{8,0},{4,12},{12,4},{1,9},{9,1},{5,13},{13,5},{2,10},{10,2},... | collective-permute-start | bytes 1572872 | tf_op jit(solution)/shard_map/ppermute | solution.py:112
  36.0 5.9 %broadcast_select_fusion = (bf16[1024,2048]{1,0:T(8,128)(2,1)S(1)}, bf16[1024,2048]{1,0:T(8,128)(2,1)S(1)}) fusion(pred[]{:T(512)S(6)} %eq.64, bf16[1024,4096]{1,0:T(8,128)(2,1)} %collective-permute-done.10, s32[]{:T(128)S(6)} %select_n.235, bf16[1024,4096]{1,0:T(8,128)(2,1)} %param.5), kind=kLoop, calls=%fused_computation | loop fusion | flops 4194304 | bytes 16777220 | tf_op jit(solution)/shard_map/jit(_where)/select_n | solution.py:118
  41.9 4.6 %collective-permute-done.8 = bf16[2,2,64,1024]{3,2,1,0:T(8,128)(2,1)S(1)} collective-permute-done((bf16[2,2,64,1024]{3,2,1,0:T(8,128)(2,1)}, bf16[2,2,64,1024]{3,2,1,0:T(8,128)(2,1)S(1)}, u32[]{:S(2)}, u32[]{:S(2)}) %collective-permute-start.8) | collective-permute-done | bytes 524320 | tf_op jit(solution)/shard_map/ppermute | solution.py:112
  46.5 4.8 %collective-permute-start.12 = (bf16[2,2,64,1024]{3,2,1,0:T(8,128)(2,1)S(1)}, bf16[2,2,64,1024]{3,2,1,0:T(8,128)(2,1)S(1)}, u32[]{:S(2)}, u32[]{:S(2)}) collective-permute-start(bf16[2,2,64,1024]{3,2,1,0:T(8,128)(2,1)S(1)} %pad_maximum_fusion.2), channel_id=1, source_target_pairs={{0,3},{4,7},{11,8},{15,12},{16,19},{20,23},{27,24},{31,28}} | collective-permute-start | bytes 1572872 | tf_op jit(solution)/shard_map/ppermute | solution.py:140
  52.3 1.5 %collective-permute-start.14 = (bf16[2,2,64,1024]{3,2,1,0:T(8,128)(2,1)S(1)}, bf16[2,2,64,1024]{3,2,1,0:T(8,128)(2,1)S(1)}, u32[]{:S(2)}, u32[]{:S(2)}) collective-permute-start(bf16[2,2,64,1024]{3,2,1,0:T(8,128)(2,1)S(1)} %get-tuple-element.53), channel_id=1, source_target_pairs={{1,9},{2,10},{3,11},{5,13},{6,14},{7,15},{8,0},{9,1},{10,2},{12,4}... | collective-permute-start | bytes 1572872 | tf_op jit(solution)/shard_map/ppermute | solution.py:129
  53.9 2.3 %fusion.52 = f32[512,2048]{1,0:T(8,128)S(1)} fusion(bf16[512,1024]{1,0:T(8,128)(2,1)S(1)} %bitcast.118, bf16[1024,2048]{1,0:T(8,128)(2,1)S(1)} %get-tuple-element.26), kind=kOutput, calls=%fused_computation.121 | convolution fusion | flops 2147483648 | bytes 9437184 | tf_op jit(solution)/shard_map/dot_general | solution.py:81
  56.3 3.0 %collective-permute-done.12 = bf16[2,2,64,1024]{3,2,1,0:T(8,128)(2,1)S(1)} collective-permute-done((bf16[2,2,64,1024]{3,2,1,0:T(8,128)(2,1)S(1)}, bf16[2,2,64,1024]{3,2,1,0:T(8,128)(2,1)S(1)}, u32[]{:S(2)}, u32[]{:S(2)}) %collective-permute-start.12) | collective-permute-done | bytes 524320 | tf_op jit(solution)/shard_map/ppermute | solution.py:140
  59.2 5.1 %collective-permute-done.14 = bf16[2,2,64,1024]{3,2,1,0:T(8,128)(2,1)S(1)} collective-permute-done((bf16[2,2,64,1024]{3,2,1,0:T(8,128)(2,1)S(1)}, bf16[2,2,64,1024]{3,2,1,0:T(8,128)(2,1)S(1)}, u32[]{:S(2)}, u32[]{:S(2)}) %collective-permute-start.14) | collective-permute-done | bytes 524320 | tf_op jit(solution)/shard_map/ppermute | solution.py:129
  68.0 2.9 %collective-permute-start.15 = (f16[2,2,64,1024]{3,2,0,1:T(8,128)(2,1)S(1)}, f16[2,2,64,1024]{3,2,0,1:T(8,128)(2,1)S(1)}, u32[]{:S(2)}, u32[]{:S(2)}) collective-permute-start(f16[2,2,64,1024]{3,2,0,1:T(8,128)(2,1)S(1)} %fusion.24), channel_id=1, source_target_pairs={{0,4},{4,0},{8,12},{12,8},{1,5},{5,1},{9,13},{13,9},{2,6},{6,2},{1... | collective-permute-start | bytes 1572872 | tf_op jit(solution)/shard_map/ppermute | solution.py:193
  70.9 2.3 %fusion.53 = f32[512,2048]{1,0:T(8,128)S(1)} fusion(bf16[512,1024]{1,0:T(8,128)(2,1)S(1)} %bitcast.128, bf16[1024,2048]{1,0:T(8,128)(2,1)S(1)} %get-tuple-element.26), kind=kOutput, calls=%fused_computation.122 | convolution fusion | flops 2147483648 | bytes 9437184 | tf_op jit(solution)/shard_map/dot_general | solution.py:81
  75.9 2.1 %collective-permute-start.20 = (f16[2,2,64,1024]{3,2,1,0:T(8,128)(2,1)S(1)}, f16[2,2,64,1024]{3,2,1,0:T(8,128)(2,1)S(1)}, u32[]{:S(2)}, u32[]{:S(2)}) collective-permute-start(f16[2,2,64,1024]{3,2,1,0:T(8,128)(2,1)S(1)} %fusion.23), channel_id=1, source_target_pairs={{0,8},{8,0},{4,12},{12,4},{1,9},{9,1},{5,13},{13,5},{2,10},{10,2},... | collective-permute-start | bytes 1572872 | tf_op jit(solution)/shard_map/ppermute | solution.py:194
  78.3 3.7 %collective-permute-done.21 = f16[2,2,64,1024]{3,2,1,0:T(8,128)(2,1)S(1)} collective-permute-done((f16[2,2,64,1024]{3,2,1,0:T(8,128)(2,1)S(1)}, f16[2,2,64,1024]{3,2,1,0:T(8,128)(2,1)S(1)}, u32[]{:S(2)}, u32[]{:S(2)}) %collective-permute-start.21) | collective-permute-done | bytes 524320 | tf_op jit(solution)/shard_map/ppermute | solution.py:194
  82.3 3.3 %collective-permute-start.22 = (f16[2,64,1024]{2,1,0:T(8,128)(2,1)S(1)}, f16[2,64,1024]{2,1,0:T(8,128)(2,1)S(1)}, u32[]{:S(2)}, u32[]{:S(2)}) collective-permute-start(f16[2,64,1024]{2,1,0:T(8,128)(2,1)S(1)} %fusion.33), channel_id=1, source_target_pairs={{0,4},{4,0},{8,12},{12,8},{1,5},{5,1},{9,13},{13,9},{2,6},{6,2},{1... | collective-permute-start | bytes 786440 | tf_op jit(solution)/shard_map/ppermute | solution.py:206
  85.9 7.4 %collective-permute-done.20 = f16[2,2,64,1024]{3,2,1,0:T(8,128)(2,1)S(1)} collective-permute-done((f16[2,2,64,1024]{3,2,1,0:T(8,128)(2,1)S(1)}, f16[2,2,64,1024]{3,2,1,0:T(8,128)(2,1)S(1)}, u32[]{:S(2)}, u32[]{:S(2)}) %collective-permute-start.20) | collective-permute-done | bytes 524320 | tf_op jit(solution)/shard_map/ppermute | solution.py:194
  93.5 3.3 %collective-permute-start.25 = (f16[2,64,1024]{2,1,0:T(8,128)(2,1)S(1)}, f16[2,64,1024]{2,1,0:T(8,128)(2,1)S(1)}, u32[]{:S(2)}, u32[]{:S(2)}) collective-permute-start(f16[2,64,1024]{2,1,0:T(8,128)(2,1)S(1)} %fusion.32), channel_id=1, source_target_pairs={{0,4},{4,0},{8,12},{12,8},{1,5},{5,1},{9,13},{13,9},{2,6},{6,2},{1... | collective-permute-start | bytes 786440 | tf_op jit(solution)/shard_map/ppermute | solution.py:206
  97.2 3.4 %collective-permute-done.22 = f16[2,64,1024]{2,1,0:T(8,128)(2,1)S(1)} collective-permute-done((f16[2,64,1024]{2,1,0:T(8,128)(2,1)S(1)}, f16[2,64,1024]{2,1,0:T(8,128)(2,1)S(1)}, u32[]{:S(2)}, u32[]{:S(2)}) %collective-permute-start.22) | collective-permute-done | bytes 262176 | tf_op jit(solution)/shard_map/ppermute | solution.py:206
  100.9 5.1 %collective-permute-done.25 = f16[2,64,1024]{2,1,0:T(8,128)(2,1)S(1)} collective-permute-done((f16[2,64,1024]{2,1,0:T(8,128)(2,1)S(1)}, f16[2,64,1024]{2,1,0:T(8,128)(2,1)S(1)}, u32[]{:S(2)}, u32[]{:S(2)}) %collective-permute-start.25) | collective-permute-done | bytes 262176 | tf_op jit(solution)/shard_map/ppermute | solution.py:206
  106.5 1.4 %collective-permute-done.26 = f16[64,2048]{1,0:T(8,128)(2,1)S(1)} collective-permute-done((f16[64,2048]{1,0:T(8,128)(2,1)S(1)}, f16[64,2048]{1,0:T(8,128)(2,1)S(1)}, u32[]{:S(2)}, u32[]{:S(2)}) %collective-permute-start.26) | collective-permute-done | bytes 262176 | tf_op jit(solution)/shard_map/ppermute | solution.py:75
  109.2 1.4 %collective-permute-start.27 = (f32[4,64]{1,0:T(4,128)S(1)}, f32[4,64]{1,0:T(4,128)S(1)}, u32[]{:S(2)}, u32[]{:S(2)}) collective-permute-start(f32[4,64]{1,0:T(4,128)S(1)} %get-tuple-element.64), channel_id=1, source_target_pairs={{0,1},{1,2},{2,3},{3,0},{4,5},{5,6},{6,7},{7,4},{8,9},{9,10},{10,1... | collective-permute-start | bytes 3080 | tf_op jit(solution)/shard_map/ppermute | solution.py:44
  111.8 1.8 %collective-permute-start.29 = (f32[4,64]{1,0:T(4,128)S(1)}, f32[4,64]{1,0:T(4,128)S(1)}, u32[]{:S(2)}, u32[]{:S(2)}) collective-permute-start(f32[4,64]{1,0:T(4,128)S(1)} %get-tuple-element.64), channel_id=1, source_target_pairs={{0,3},{1,0},{2,1},{3,2},{4,7},{5,4},{6,5},{7,6},{8,11},{9,8},{10,9... | collective-permute-start | bytes 3080 | tf_op jit(solution)/shard_map/ppermute | solution.py:44
  115.4 1.6 %fusion.20 = (f32[64,4096]{1,0:T(8,128)}, f32[64,4096]{1,0:T(8,128)}) fusion(f32[64]{0:T(128)S(1)} %get-tuple-element.65, f32[64]{0:T(128)S(1)} %get-tuple-element.67, f16[64,2048]{1,0:T(8,128)(2,1)S(1)} %get-tuple-element.58, f16[64,2048]{1,0:T(8,128)(2,1)S(1)} %get-tuple-element.56, f32[64,4096]{1,0:T(8,128)S(1)} %get-tuple-element.41, ...), kind=kLoop, calls=%fused_computation.30 | loop fusion | flops 1310720 | bytes 3670784 | tf_op jit(solution)/shard_map/sub | solution.py:244
  (85 shorter events, 21.8 us)
Async XLA Ops:
  0.6 35.4 %collective-permute-start.10 = (bf16[1024,4096]{1,0:T(8,128)(2,1)}, bf16[1024,4096]{1,0:T(8,128)(2,1)}, u32[]{:S(2)}, u32[]{:S(2)}) collective-permute-start(bf16[1024,4096]{1,0:T(8,128)(2,1)} %param.5), channel_id=1, source_target_pairs={{0,16},{16,0},{1,17},{17,1},{2,18},{18,2},{3,19},{19,3},{4,20},{20... | collective-permute-start | bytes 25165832 | tf_op jit(solution)/shard_map/ppermute | solution.py:41
  3.0 11.7 %collective-permute-start = (bf16[2,64,1024]{2,1,0:T(8,128)(2,1)S(1)}, bf16[2,64,1024]{2,1,0:T(8,128)(2,1)S(1)}, u32[]{:S(2)}, u32[]{:S(2)}) collective-permute-start(bf16[2,64,1024]{2,1,0:T(8,128)(2,1)S(1)} %constant_dynamic-slice_fusion.6), channel_id=1, source_target_pairs={{0,4},{4,0},{8,12},{12,8},{1,5},{5,1},{9,13},{13,9},{2,6},{6,2},{1... | collective-permute-start | bytes 786440 | tf_op jit(solution)/shard_map/ppermute | solution.py:85
  6.8 5.6 %collective-permute-start.1 = (f32[128]{0:T(128)S(1)}, f32[128]{0:T(128)S(1)}, u32[]{:S(2)}, u32[]{:S(2)}) collective-permute-start(f32[128]{0:T(128)S(1)} %multiply_reduce_fusion), channel_id=1, source_target_pairs={{0,1},{1,2},{2,3},{3,0},{4,5},{5,6},{6,7},{7,4},{8,9},{9,10},{10,1... | collective-permute-start | bytes 1544 | tf_op jit(solution)/shard_map/ppermute | solution.py:44
  8.5 4.4 %collective-permute-start.2 = (f32[128]{0:T(128)S(1)}, f32[128]{0:T(128)S(1)}, u32[]{:S(2)}, u32[]{:S(2)}) collective-permute-start(f32[128]{0:T(128)S(1)} %multiply_reduce_fusion), channel_id=1, source_target_pairs={{0,2},{1,3},{2,0},{3,1},{4,6},{5,7},{6,4},{7,5},{8,10},{9,11},{10,... | collective-permute-start | bytes 1544 | tf_op jit(solution)/shard_map/ppermute | solution.py:44
  11.0 3.5 %collective-permute-start.3 = (f32[128]{0:T(128)S(1)}, f32[128]{0:T(128)S(1)}, u32[]{:S(2)}, u32[]{:S(2)}) collective-permute-start(f32[128]{0:T(128)S(1)} %multiply_reduce_fusion), channel_id=1, source_target_pairs={{0,3},{1,0},{2,1},{3,2},{4,7},{5,4},{6,5},{7,6},{8,11},{9,8},{10,9... | collective-permute-start | bytes 1544 | tf_op jit(solution)/shard_map/ppermute | solution.py:44
  14.9 12.6 %collective-permute-start.7 = (bf16[2,2,64,1024]{3,2,1,0:T(8,128)(2,1)S(1)}, bf16[2,2,64,1024]{3,2,1,0:T(8,128)(2,1)S(1)}, u32[]{:S(2)}, u32[]{:S(2)}) collective-permute-start(bf16[2,2,64,1024]{3,2,1,0:T(8,128)(2,1)S(1)} %pad_maximum_fusion.2), channel_id=1, source_target_pairs={{0,1},{1,2},{2,3},{4,5},{5,6},{6,7},{8,9},{9,10},{10,11},{12,13},{... | collective-permute-start | bytes 1572872 | tf_op jit(solution)/shard_map/ppermute | solution.py:92
  17.0 14.6 %collective-permute-start.4 = (bf16[2,2,64,1024]{3,2,1,0:T(8,128)(2,1)S(1)}, bf16[2,2,64,1024]{3,2,1,0:T(8,128)(2,1)S(1)}, u32[]{:S(2)}, u32[]{:S(2)}) collective-permute-start(bf16[2,2,64,1024]{3,2,1,0:T(8,128)(2,1)S(1)} %pad_maximum_fusion.2), channel_id=1, source_target_pairs={{1,0},{2,1},{3,2},{5,4},{6,5},{7,6},{9,8},{10,9},{11,10},{13,12},{... | collective-permute-start | bytes 1572872 | tf_op jit(solution)/shard_map/ppermute | solution.py:95
  18.5 5.0 %collective-permute-start.5 = (f32[64]{0:T(128)S(1)}, f32[64]{0:T(128)S(1)}, u32[]{:S(2)}, u32[]{:S(2)}) collective-permute-start(f32[64]{0:T(128)S(1)} %get-tuple-element.71), channel_id=1, source_target_pairs={{0,0},{4,8},{8,16},{12,24},{16,4},{20,12},{24,20},{28,28},{1,1},{5... | collective-permute-start | bytes 776 | tf_op jit(solution)/shard_map/ppermute | solution.py:61
  19.1 5.6 %collective-permute-start.6 = (f32[64]{0:T(128)S(1)}, f32[64]{0:T(128)S(1)}, u32[]{:S(2)}, u32[]{:S(2)}) collective-permute-start(f32[64]{0:T(128)S(1)} %get-tuple-element.72), channel_id=1, source_target_pairs={{0,4},{4,12},{8,20},{12,28},{16,0},{20,8},{24,16},{28,24},{1,5},{5... | collective-permute-start | bytes 776 | tf_op jit(solution)/shard_map/ppermute | solution.py:61
  31.6 14.9 %collective-permute-start.11 = (bf16[2,2,64,1024]{3,2,1,0:T(8,128)(2,1)S(1)}, bf16[2,2,64,1024]{3,2,1,0:T(8,128)(2,1)S(1)}, u32[]{:S(2)}, u32[]{:S(2)}) collective-permute-start(bf16[2,2,64,1024]{3,2,1,0:T(8,128)(2,1)S(1)} %collective-permute-done.4), channel_id=1, source_target_pairs={{1,0},{2,1},{5,4},{6,5},{9,8},{10,9},{13,12},{14,13},{17,16},{18,1... | collective-permute-start | bytes 1572872 | tf_op jit(solution)/shard_map/ppermute | solution.py:95
  32.9 13.6 %collective-permute-start.9 = (bf16[2,2,64,1024]{3,2,1,0:T(8,128)(2,1)S(1)}, bf16[2,2,64,1024]{3,2,1,0:T(8,128)(2,1)S(1)}, u32[]{:S(2)}, u32[]{:S(2)}) collective-permute-start(bf16[2,2,64,1024]{3,2,1,0:T(8,128)(2,1)S(1)} %collective-permute-done.7), channel_id=1, source_target_pairs={{1,2},{2,3},{5,6},{6,7},{9,10},{10,11},{13,14},{14,15},{17,18},{18... | collective-permute-start | bytes 1572872 | tf_op jit(solution)/shard_map/ppermute | solution.py:92
  34.5 12.0 %collective-permute-start.8 = (bf16[2,2,64,1024]{3,2,1,0:T(8,128)(2,1)}, bf16[2,2,64,1024]{3,2,1,0:T(8,128)(2,1)S(1)}, u32[]{:S(2)}, u32[]{:S(2)}) collective-permute-start(bf16[2,2,64,1024]{3,2,1,0:T(8,128)(2,1)} %select_select_fusion.2), channel_id=1, source_target_pairs={{0,8},{8,0},{4,12},{12,4},{1,9},{9,1},{5,13},{13,5},{2,10},{10,2},... | collective-permute-start | bytes 1572872 | tf_op jit(solution)/shard_map/ppermute | solution.py:112
  46.5 12.7 %collective-permute-start.12 = (bf16[2,2,64,1024]{3,2,1,0:T(8,128)(2,1)S(1)}, bf16[2,2,64,1024]{3,2,1,0:T(8,128)(2,1)S(1)}, u32[]{:S(2)}, u32[]{:S(2)}) collective-permute-start(bf16[2,2,64,1024]{3,2,1,0:T(8,128)(2,1)S(1)} %pad_maximum_fusion.2), channel_id=1, source_target_pairs={{0,3},{4,7},{11,8},{15,12},{16,19},{20,23},{27,24},{31,28}} | collective-permute-start | bytes 1572872 | tf_op jit(solution)/shard_map/ppermute | solution.py:140
  51.3 7.9 %collective-permute-start.13 = (bf16[2,2,64,1024]{3,2,1,0:T(8,128)(2,1)S(1)}, bf16[2,2,64,1024]{3,2,1,0:T(8,128)(2,1)S(1)}, u32[]{:S(2)}, u32[]{:S(2)}) collective-permute-start(bf16[2,2,64,1024]{3,2,1,0:T(8,128)(2,1)S(1)} %pad_maximum_fusion.2), channel_id=1, source_target_pairs={{3,8},{7,12},{8,3},{12,7},{19,24},{23,28},{24,19},{28,23}} | collective-permute-start | bytes 1572872 | tf_op jit(solution)/shard_map/ppermute | solution.py:140
  52.3 12.1 %collective-permute-start.14 = (bf16[2,2,64,1024]{3,2,1,0:T(8,128)(2,1)S(1)}, bf16[2,2,64,1024]{3,2,1,0:T(8,128)(2,1)S(1)}, u32[]{:S(2)}, u32[]{:S(2)}) collective-permute-start(bf16[2,2,64,1024]{3,2,1,0:T(8,128)(2,1)S(1)} %get-tuple-element.53), channel_id=1, source_target_pairs={{1,9},{2,10},{3,11},{5,13},{6,14},{7,15},{8,0},{9,1},{10,2},{12,4}... | collective-permute-start | bytes 1572872 | tf_op jit(solution)/shard_map/ppermute | solution.py:129
  53.9 17.1 %collective-permute-start.16 = (bf16[2,2,2,64,1024]{4,3,2,1,0:T(8,128)(2,1)S(1)}, bf16[2,2,2,64,1024]{4,3,2,1,0:T(8,128)(2,1)S(1)}, u32[]{:S(2)}, u32[]{:S(2)}) collective-permute-start(bf16[2,2,2,64,1024]{4,3,2,1,0:T(8,128)(2,1)S(1)} %pad_maximum_fusion), channel_id=1, source_target_pairs={{0,16},{16,0},{1,17},{17,1},{2,18},{18,2},{3,19},{19,3},{4,20},{20... | collective-permute-start | bytes 3145736 | tf_op jit(solution)/shard_map/ppermute | solution.py:75
  64.6 8.7 %collective-permute-start.17 = (bf16[2,2,2,64,1024]{4,3,2,1,0:T(8,128)(2,1)S(1)}, bf16[2,2,2,64,1024]{4,3,2,1,0:T(8,128)(2,1)S(1)}, u32[]{:S(2)}, u32[]{:S(2)}) collective-permute-start(bf16[2,2,2,64,1024]{4,3,2,1,0:T(8,128)(2,1)S(1)} %pad_maximum_fusion.1), channel_id=1, source_target_pairs={{0,16},{16,0},{1,17},{17,1},{2,18},{18,2},{3,19},{19,3},{4,20},{20... | collective-permute-start | bytes 3145736 | tf_op jit(solution)/shard_map/ppermute | solution.py:75
  67.3 14.8 %collective-permute-start.21 = (f16[2,2,64,1024]{3,2,1,0:T(8,128)(2,1)S(1)}, f16[2,2,64,1024]{3,2,1,0:T(8,128)(2,1)S(1)}, u32[]{:S(2)}, u32[]{:S(2)}) collective-permute-start(f16[2,2,64,1024]{3,2,1,0:T(8,128)(2,1)S(1)} %fusion.22), channel_id=1, source_target_pairs={{0,8},{8,0},{4,12},{12,4},{1,9},{9,1},{5,13},{13,5},{2,10},{10,2},... | collective-permute-start | bytes 1572872 | tf_op jit(solution)/shard_map/ppermute | solution.py:194
  68.0 17.5 %collective-permute-start.15 = (f16[2,2,64,1024]{3,2,0,1:T(8,128)(2,1)S(1)}, f16[2,2,64,1024]{3,2,0,1:T(8,128)(2,1)S(1)}, u32[]{:S(2)}, u32[]{:S(2)}) collective-permute-start(f16[2,2,64,1024]{3,2,0,1:T(8,128)(2,1)S(1)} %fusion.24), channel_id=1, source_target_pairs={{0,4},{4,0},{8,12},{12,8},{1,5},{5,1},{9,13},{13,9},{2,6},{6,2},{1... | collective-permute-start | bytes 1572872 | tf_op jit(solution)/shard_map/ppermute | solution.py:193
  75.9 17.4 %collective-permute-start.20 = (f16[2,2,64,1024]{3,2,1,0:T(8,128)(2,1)S(1)}, f16[2,2,64,1024]{3,2,1,0:T(8,128)(2,1)S(1)}, u32[]{:S(2)}, u32[]{:S(2)}) collective-permute-start(f16[2,2,64,1024]{3,2,1,0:T(8,128)(2,1)S(1)} %fusion.23), channel_id=1, source_target_pairs={{0,8},{8,0},{4,12},{12,4},{1,9},{9,1},{5,13},{13,5},{2,10},{10,2},... | collective-permute-start | bytes 1572872 | tf_op jit(solution)/shard_map/ppermute | solution.py:194
  78.2 18.5 %collective-permute-start.19 = (f16[2,2,64,1024]{3,2,0,1:T(8,128)(2,1)S(1)}, f16[2,2,64,1024]{3,2,0,1:T(8,128)(2,1)S(1)}, u32[]{:S(2)}, u32[]{:S(2)}) collective-permute-start(f16[2,2,64,1024]{3,2,0,1:T(8,128)(2,1)S(1)} %fusion.25), channel_id=1, source_target_pairs={{0,4},{4,0},{8,12},{12,8},{1,5},{5,1},{9,13},{13,9},{2,6},{6,2},{1... | collective-permute-start | bytes 1572872 | tf_op jit(solution)/shard_map/ppermute | solution.py:193
  82.3 18.3 %collective-permute-start.22 = (f16[2,64,1024]{2,1,0:T(8,128)(2,1)S(1)}, f16[2,64,1024]{2,1,0:T(8,128)(2,1)S(1)}, u32[]{:S(2)}, u32[]{:S(2)}) collective-permute-start(f16[2,64,1024]{2,1,0:T(8,128)(2,1)S(1)} %fusion.33), channel_id=1, source_target_pairs={{0,4},{4,0},{8,12},{12,8},{1,5},{5,1},{9,13},{13,9},{2,6},{6,2},{1... | collective-permute-start | bytes 786440 | tf_op jit(solution)/shard_map/ppermute | solution.py:206
  85.8 14.9 %collective-permute-start.18 = (f16[2,64,1024]{2,1,0:T(8,128)(2,1)S(1)}, f16[2,64,1024]{2,1,0:T(8,128)(2,1)S(1)}, u32[]{:S(2)}, u32[]{:S(2)}) collective-permute-start(f16[2,64,1024]{2,1,0:T(8,128)(2,1)S(1)} %fusion.30), channel_id=1, source_target_pairs={{0,8},{8,0},{4,12},{12,4},{1,9},{9,1},{5,13},{13,5},{2,10},{10,2},... | collective-permute-start | bytes 786440 | tf_op jit(solution)/shard_map/ppermute | solution.py:205
  93.5 12.5 %collective-permute-start.25 = (f16[2,64,1024]{2,1,0:T(8,128)(2,1)S(1)}, f16[2,64,1024]{2,1,0:T(8,128)(2,1)S(1)}, u32[]{:S(2)}, u32[]{:S(2)}) collective-permute-start(f16[2,64,1024]{2,1,0:T(8,128)(2,1)S(1)} %fusion.32), channel_id=1, source_target_pairs={{0,4},{4,0},{8,12},{12,8},{1,5},{5,1},{9,13},{13,9},{2,6},{6,2},{1... | collective-permute-start | bytes 786440 | tf_op jit(solution)/shard_map/ppermute | solution.py:206
  97.0 9.0 %collective-permute-start.24 = (f16[2,64,1024]{2,1,0:T(8,128)(2,1)S(1)}, f16[2,64,1024]{2,1,0:T(8,128)(2,1)S(1)}, u32[]{:S(2)}, u32[]{:S(2)}) collective-permute-start(f16[2,64,1024]{2,1,0:T(8,128)(2,1)S(1)} %fusion.31), channel_id=1, source_target_pairs={{0,8},{8,0},{4,12},{12,4},{1,9},{9,1},{5,13},{13,5},{2,10},{10,2},... | collective-permute-start | bytes 786440 | tf_op jit(solution)/shard_map/ppermute | solution.py:205
  100.8 5.5 %collective-permute-start.23 = (f16[64,2048]{1,0:T(8,128)(2,1)S(1)}, f16[64,2048]{1,0:T(8,128)(2,1)S(1)}, u32[]{:S(2)}, u32[]{:S(2)}) collective-permute-start(f16[64,2048]{1,0:T(8,128)(2,1)S(1)} %fusion.39), channel_id=1, source_target_pairs={{0,16},{16,0},{1,17},{17,1},{2,18},{18,2},{3,19},{19,3},{4,20},{20... | collective-permute-start | bytes 786440 | tf_op jit(solution)/shard_map/ppermute | solution.py:75
  106.2 1.6 %collective-permute-start.26 = (f16[64,2048]{1,0:T(8,128)(2,1)S(1)}, f16[64,2048]{1,0:T(8,128)(2,1)S(1)}, u32[]{:S(2)}, u32[]{:S(2)}) collective-permute-start(f16[64,2048]{1,0:T(8,128)(2,1)S(1)} %fusion.37), channel_id=1, source_target_pairs={{0,16},{16,0},{1,17},{17,1},{2,18},{18,2},{3,19},{19,3},{4,20},{20... | collective-permute-start | bytes 786440 | tf_op jit(solution)/shard_map/ppermute | solution.py:75
  109.2 5.4 %collective-permute-start.27 = (f32[4,64]{1,0:T(4,128)S(1)}, f32[4,64]{1,0:T(4,128)S(1)}, u32[]{:S(2)}, u32[]{:S(2)}) collective-permute-start(f32[4,64]{1,0:T(4,128)S(1)} %get-tuple-element.64), channel_id=1, source_target_pairs={{0,1},{1,2},{2,3},{3,0},{4,5},{5,6},{6,7},{7,4},{8,9},{9,10},{10,1... | collective-permute-start | bytes 3080 | tf_op jit(solution)/shard_map/ppermute | solution.py:44
  110.7 4.5 %collective-permute-start.28 = (f32[4,64]{1,0:T(4,128)S(1)}, f32[4,64]{1,0:T(4,128)S(1)}, u32[]{:S(2)}, u32[]{:S(2)}) collective-permute-start(f32[4,64]{1,0:T(4,128)S(1)} %get-tuple-element.64), channel_id=1, source_target_pairs={{0,2},{1,3},{2,0},{3,1},{4,6},{5,7},{6,4},{7,5},{8,10},{9,11},{10,... | collective-permute-start | bytes 3080 | tf_op jit(solution)/shard_map/ppermute | solution.py:44
  111.8 3.6 %collective-permute-start.29 = (f32[4,64]{1,0:T(4,128)S(1)}, f32[4,64]{1,0:T(4,128)S(1)}, u32[]{:S(2)}, u32[]{:S(2)}) collective-permute-start(f32[4,64]{1,0:T(4,128)S(1)} %get-tuple-element.64), channel_id=1, source_target_pairs={{0,3},{1,0},{2,1},{3,2},{4,7},{5,4},{6,5},{7,6},{8,11},{9,8},{10,9... | collective-permute-start | bytes 3080 | tf_op jit(solution)/shard_map/ppermute | solution.py:44

commit v23 on v22

--- a/solution.py
+++ b/solution.py
@@ -147,10 +147,10 @@
         swapped_far = swapped(far)
 
         def halves(near, left):
-            return [
-                near[:, low : low + width // 2] + dot(left, far_weight[:, low : low + width // 2])
-                for low in (0, width // 2)
-            ]
+            middle = width // 2
+            high = near[:, middle:] + dot(left, far_weight[:, middle:])
+            low = near[:, :middle] + dot(after(left, high), far_weight[:, :middle])
+            return low, high
 
         def own_part():
             return halves(near_part, far)

time: 117 us -> 117 us (level)
  no operation moved by 1% of the time
where the time goes in v23:
time: 117 us
  waiting for transfers between devices  45.8 us (39%)
  starting transfers between devices  44.5 us (38%)
  other arithmetic  15.3 us (13%)
  matrix products  9.73 us (8%)
  between operations  1.17 us (1%)
    ppermute x2, waiting for transfers between devices, on_device(): away_y = lax.ppermute(sends[i][1], 'batch', Y_SWAP)  11.1 us
    ppermute x6, starting transfers between devices, shifted(): lax.ppermute(value, 'vocab', [(i, (i + k) % vocab) for i in range(vocab)])  9.91 us
    dot_general x6, matrix products, dot(): jnp.dot(left.reshape(-1, block), weight, preferred_element_type=jnp.float32)  9.73 us
    ppermute x2, waiting for transfers between devices, on_device(): next_x = lax.ppermute(more_sends[i][1], 'batch', X_SWAP)  8.42 us
    ppermute x2, starting transfers between devices, on_device(): next_x = lax.ppermute(more_sends[i][1], 'batch', X_SWAP)  6.53 us
    select_n x1, other arithmetic, line_parts(): jnp.where(keep_near, taken, kept)  5.87 us
    ppermute x2, starting transfers between devices, line_parts(): ends.append(lax.ppermute(sent, ('batch', 'vocab'), sorted(moves)))  5.5 us
    ppermute x1, waiting for transfers between devices, line_parts(): got_early = lax.ppermute(quarter(far, 2, 1), ('batch', 'vocab'), early)  5.11 us
  transfers between devices with their start and end apart: 30, of which 16 were waited for; matrix products, arithmetic and copies ran while one was open for 19% of the time, Pallas kernels for 0%

profile of v23, /device:TPU:0, one launch (start us, length us, event | category | flops | bytes accessed | tf_op | source)
XLA Modules:
  0.0 117.0 jit_solution(10114603906367296899)
XLA Ops:
  3.0 2.6 %collective-permute-start = (bf16[2,64,1024]{2,1,0:T(8,128)(2,1)S(1)}, bf16[2,64,1024]{2,1,0:T(8,128)(2,1)S(1)}, u32[]{:S(2)}, u32[]{:S(2)}) collective-permute-start(bf16[2,64,1024]{2,1,0:T(8,128)(2,1)S(1)} %constant_dynamic-slice_fusion.6), channel_id=1, source_target_pairs={{0,4},{4,0},{8,12},{12,8},{1,5},{5,1},{9,13},{13,9},{2,6},{6,2},{1... | collective-permute-start | bytes 786440 | tf_op jit(solution)/shard_map/ppermute | solution.py:85
  6.8 1.6 %collective-permute-start.1 = (f32[128]{0:T(128)S(1)}, f32[128]{0:T(128)S(1)}, u32[]{:S(2)}, u32[]{:S(2)}) collective-permute-start(f32[128]{0:T(128)S(1)} %multiply_reduce_fusion), channel_id=1, source_target_pairs={{0,1},{1,2},{2,3},{3,0},{4,5},{5,6},{6,7},{7,4},{8,9},{9,10},{10,1... | collective-permute-start | bytes 1544 | tf_op jit(solution)/shard_map/ppermute | solution.py:44
  8.5 2.6 %collective-permute-start.2 = (f32[128]{0:T(128)S(1)}, f32[128]{0:T(128)S(1)}, u32[]{:S(2)}, u32[]{:S(2)}) collective-permute-start(f32[128]{0:T(128)S(1)} %multiply_reduce_fusion), channel_id=1, source_target_pairs={{0,2},{1,3},{2,0},{3,1},{4,6},{5,7},{6,4},{7,5},{8,10},{9,11},{10,... | collective-permute-start | bytes 1544 | tf_op jit(solution)/shard_map/ppermute | solution.py:44
  11.0 1.3 %collective-permute-start.3 = (f32[128]{0:T(128)S(1)}, f32[128]{0:T(128)S(1)}, u32[]{:S(2)}, u32[]{:S(2)}) collective-permute-start(f32[128]{0:T(128)S(1)} %multiply_reduce_fusion), channel_id=1, source_target_pairs={{0,3},{1,0},{2,1},{3,2},{4,7},{5,4},{6,5},{7,6},{8,11},{9,8},{10,9... | collective-permute-start | bytes 1544 | tf_op jit(solution)/shard_map/ppermute | solution.py:44
  12.9 1.7 %collective-permute-done.3 = f32[128]{0:T(128)S(1)} collective-permute-done((f32[128]{0:T(128)S(1)}, f32[128]{0:T(128)S(1)}, u32[]{:S(2)}, u32[]{:S(2)}) %collective-permute-start.3) | collective-permute-done | bytes 544 | tf_op jit(solution)/shard_map/ppermute | solution.py:44
  14.9 2.2 %collective-permute-start.7 = (bf16[2,2,64,1024]{3,2,1,0:T(8,128)(2,1)S(1)}, bf16[2,2,64,1024]{3,2,1,0:T(8,128)(2,1)S(1)}, u32[]{:S(2)}, u32[]{:S(2)}) collective-permute-start(bf16[2,2,64,1024]{3,2,1,0:T(8,128)(2,1)S(1)} %pad_maximum_fusion.2), channel_id=1, source_target_pairs={{0,1},{1,2},{2,3},{4,5},{5,6},{6,7},{8,9},{9,10},{10,11},{12,13},{... | collective-permute-start | bytes 1572872 | tf_op jit(solution)/shard_map/ppermute | solution.py:92
  17.0 1.3 %collective-permute-start.4 = (bf16[2,2,64,1024]{3,2,1,0:T(8,128)(2,1)S(1)}, bf16[2,2,64,1024]{3,2,1,0:T(8,128)(2,1)S(1)}, u32[]{:S(2)}, u32[]{:S(2)}) collective-permute-start(bf16[2,2,64,1024]{3,2,1,0:T(8,128)(2,1)S(1)} %pad_maximum_fusion.2), channel_id=1, source_target_pairs={{1,0},{2,1},{3,2},{5,4},{6,5},{7,6},{9,8},{10,9},{11,10},{13,12},{... | collective-permute-start | bytes 1572872 | tf_op jit(solution)/shard_map/ppermute | solution.py:95
  19.1 4.3 %collective-permute-start.6 = (f32[64]{0:T(128)S(1)}, f32[64]{0:T(128)S(1)}, u32[]{:S(2)}, u32[]{:S(2)}) collective-permute-start(f32[64]{0:T(128)S(1)} %get-tuple-element.76), channel_id=1, source_target_pairs={{0,4},{4,12},{8,20},{12,28},{16,0},{20,8},{24,16},{28,24},{1,5},{5... | collective-permute-start | bytes 776 | tf_op jit(solution)/shard_map/ppermute | solution.py:61
  23.4 1.3 %collective-permute-done.6 = f32[64]{0:T(128)S(1)} collective-permute-done((f32[64]{0:T(128)S(1)}, f32[64]{0:T(128)S(1)}, u32[]{:S(2)}, u32[]{:S(2)}) %collective-permute-start.6) | collective-permute-done | bytes 288 | tf_op jit(solution)/shard_map/ppermute | solution.py:61
  24.7 2.8 %collective-permute-done.7 = bf16[2,2,64,1024]{3,2,1,0:T(8,128)(2,1)S(1)} collective-permute-done((bf16[2,2,64,1024]{3,2,1,0:T(8,128)(2,1)S(1)}, bf16[2,2,64,1024]{3,2,1,0:T(8,128)(2,1)S(1)}, u32[]{:S(2)}, u32[]{:S(2)}) %collective-permute-start.7) | collective-permute-done | bytes 524320 | tf_op jit(solution)/shard_map/ppermute | solution.py:92
  27.5 4.1 %collective-permute-done.4 = bf16[2,2,64,1024]{3,2,1,0:T(8,128)(2,1)S(1)} collective-permute-done((bf16[2,2,64,1024]{3,2,1,0:T(8,128)(2,1)S(1)}, bf16[2,2,64,1024]{3,2,1,0:T(8,128)(2,1)S(1)}, u32[]{:S(2)}, u32[]{:S(2)}) %collective-permute-start.4) | collective-permute-done | bytes 524320 | tf_op jit(solution)/shard_map/ppermute | solution.py:95
  34.5 1.5 %collective-permute-start.8 = (bf16[2,2,64,1024]{3,2,1,0:T(8,128)(2,1)}, bf16[2,2,64,1024]{3,2,1,0:T(8,128)(2,1)S(1)}, u32[]{:S(2)}, u32[]{:S(2)}) collective-permute-start(bf16[2,2,64,1024]{3,2,1,0:T(8,128)(2,1)} %select_select_fusion.2), channel_id=1, source_target_pairs={{0,8},{8,0},{4,12},{12,4},{1,9},{9,1},{5,13},{13,5},{2,10},{10,2},... | collective-permute-start | bytes 1572872 | tf_op jit(solution)/shard_map/ppermute | solution.py:112
  36.0 5.9 %broadcast_select_fusion = (bf16[1024,2048]{1,0:T(8,128)(2,1)S(1)}, bf16[1024,2048]{1,0:T(8,128)(2,1)S(1)}) fusion(pred[]{:T(512)S(6)} %eq.64, bf16[1024,4096]{1,0:T(8,128)(2,1)} %collective-permute-done.10, s32[]{:T(128)S(6)} %select_n.235, bf16[1024,4096]{1,0:T(8,128)(2,1)} %param.5), kind=kLoop, calls=%fused_computation | loop fusion | flops 4194304 | bytes 16777220 | tf_op jit(solution)/shard_map/jit(_where)/select_n | solution.py:118
  41.9 4.6 %collective-permute-done.8 = bf16[2,2,64,1024]{3,2,1,0:T(8,128)(2,1)S(1)} collective-permute-done((bf16[2,2,64,1024]{3,2,1,0:T(8,128)(2,1)}, bf16[2,2,64,1024]{3,2,1,0:T(8,128)(2,1)S(1)}, u32[]{:S(2)}, u32[]{:S(2)}) %collective-permute-start.8) | collective-permute-done | bytes 524320 | tf_op jit(solution)/shard_map/ppermute | solution.py:112
  46.5 4.8 %collective-permute-start.12 = (bf16[2,2,64,1024]{3,2,1,0:T(8,128)(2,1)S(1)}, bf16[2,2,64,1024]{3,2,1,0:T(8,128)(2,1)S(1)}, u32[]{:S(2)}, u32[]{:S(2)}) collective-permute-start(bf16[2,2,64,1024]{3,2,1,0:T(8,128)(2,1)S(1)} %pad_maximum_fusion.2), channel_id=1, source_target_pairs={{0,3},{4,7},{11,8},{15,12},{16,19},{20,23},{27,24},{31,28}} | collective-permute-start | bytes 1572872 | tf_op jit(solution)/shard_map/ppermute | solution.py:140
  52.3 1.5 %collective-permute-start.14 = (bf16[2,2,64,1024]{3,2,1,0:T(8,128)(2,1)S(1)}, bf16[2,2,64,1024]{3,2,1,0:T(8,128)(2,1)S(1)}, u32[]{:S(2)}, u32[]{:S(2)}) collective-permute-start(bf16[2,2,64,1024]{3,2,1,0:T(8,128)(2,1)S(1)} %get-tuple-element.57), channel_id=1, source_target_pairs={{1,9},{2,10},{3,11},{5,13},{6,14},{7,15},{8,0},{9,1},{10,2},{12,4}... | collective-permute-start | bytes 1572872 | tf_op jit(solution)/shard_map/ppermute | solution.py:129
  53.9 2.3 %fusion.50 = f32[512,2048]{1,0:T(8,128)S(1)} fusion(bf16[512,1024]{1,0:T(8,128)(2,1)S(1)} %bitcast.120, bf16[1024,2048]{1,0:T(8,128)(2,1)S(1)} %get-tuple-element.28), kind=kOutput, calls=%fused_computation.121 | convolution fusion | flops 2147483648 | bytes 9437184 | tf_op jit(solution)/shard_map/dot_general | solution.py:81
  56.3 3.0 %collective-permute-done.12 = bf16[2,2,64,1024]{3,2,1,0:T(8,128)(2,1)S(1)} collective-permute-done((bf16[2,2,64,1024]{3,2,1,0:T(8,128)(2,1)S(1)}, bf16[2,2,64,1024]{3,2,1,0:T(8,128)(2,1)S(1)}, u32[]{:S(2)}, u32[]{:S(2)}) %collective-permute-start.12) | collective-permute-done | bytes 524320 | tf_op jit(solution)/shard_map/ppermute | solution.py:140
  59.2 5.1 %collective-permute-done.14 = bf16[2,2,64,1024]{3,2,1,0:T(8,128)(2,1)S(1)} collective-permute-done((bf16[2,2,64,1024]{3,2,1,0:T(8,128)(2,1)S(1)}, bf16[2,2,64,1024]{3,2,1,0:T(8,128)(2,1)S(1)}, u32[]{:S(2)}, u32[]{:S(2)}) %collective-permute-start.14) | collective-permute-done | bytes 524320 | tf_op jit(solution)/shard_map/ppermute | solution.py:129
  68.0 2.9 %collective-permute-start.15 = (f16[2,2,64,1024]{3,2,0,1:T(8,128)(2,1)S(1)}, f16[2,2,64,1024]{3,2,0,1:T(8,128)(2,1)S(1)}, u32[]{:S(2)}, u32[]{:S(2)}) collective-permute-start(f16[2,2,64,1024]{3,2,0,1:T(8,128)(2,1)S(1)} %fusion.22), channel_id=1, source_target_pairs={{0,4},{4,0},{8,12},{12,8},{1,5},{5,1},{9,13},{13,9},{2,6},{6,2},{1... | collective-permute-start | bytes 1572872 | tf_op jit(solution)/shard_map/ppermute | solution.py:193
  70.9 2.3 %fusion.51 = f32[512,2048]{1,0:T(8,128)S(1)} fusion(bf16[512,1024]{1,0:T(8,128)(2,1)S(1)} %bitcast.130, bf16[1024,2048]{1,0:T(8,128)(2,1)S(1)} %get-tuple-element.28), kind=kOutput, calls=%fused_computation.122 | convolution fusion | flops 2147483648 | bytes 9437184 | tf_op jit(solution)/shard_map/dot_general | solution.py:81
  74.6 2.1 %collective-permute-start.20 = (f16[2,2,64,1024]{3,2,1,0:T(8,128)(2,1)S(1)}, f16[2,2,64,1024]{3,2,1,0:T(8,128)(2,1)S(1)}, u32[]{:S(2)}, u32[]{:S(2)}) collective-permute-start(f16[2,2,64,1024]{3,2,1,0:T(8,128)(2,1)S(1)} %fusion.21), channel_id=1, source_target_pairs={{0,8},{8,0},{4,12},{12,4},{1,9},{9,1},{5,13},{13,5},{2,10},{10,2},... | collective-permute-start | bytes 1572872 | tf_op jit(solution)/shard_map/ppermute | solution.py:194
  78.3 3.7 %collective-permute-done.21 = f16[2,2,64,1024]{3,2,1,0:T(8,128)(2,1)S(1)} collective-permute-done((f16[2,2,64,1024]{3,2,1,0:T(8,128)(2,1)S(1)}, f16[2,2,64,1024]{3,2,1,0:T(8,128)(2,1)S(1)}, u32[]{:S(2)}, u32[]{:S(2)}) %collective-permute-start.21) | collective-permute-done | bytes 524320 | tf_op jit(solution)/shard_map/ppermute | solution.py:194
  82.3 3.3 %collective-permute-start.22 = (f16[2,64,1024]{2,1,0:T(8,128)(2,1)S(1)}, f16[2,64,1024]{2,1,0:T(8,128)(2,1)S(1)}, u32[]{:S(2)}, u32[]{:S(2)}) collective-permute-start(f16[2,64,1024]{2,1,0:T(8,128)(2,1)S(1)} %fusion.31), channel_id=1, source_target_pairs={{0,4},{4,0},{8,12},{12,8},{1,5},{5,1},{9,13},{13,9},{2,6},{6,2},{1... | collective-permute-start | bytes 786440 | tf_op jit(solution)/shard_map/ppermute | solution.py:206
  85.9 7.4 %collective-permute-done.20 = f16[2,2,64,1024]{3,2,1,0:T(8,128)(2,1)S(1)} collective-permute-done((f16[2,2,64,1024]{3,2,1,0:T(8,128)(2,1)S(1)}, f16[2,2,64,1024]{3,2,1,0:T(8,128)(2,1)S(1)}, u32[]{:S(2)}, u32[]{:S(2)}) %collective-permute-start.20) | collective-permute-done | bytes 524320 | tf_op jit(solution)/shard_map/ppermute | solution.py:194
  93.5 3.3 %collective-permute-start.25 = (f16[2,64,1024]{2,1,0:T(8,128)(2,1)S(1)}, f16[2,64,1024]{2,1,0:T(8,128)(2,1)S(1)}, u32[]{:S(2)}, u32[]{:S(2)}) collective-permute-start(f16[2,64,1024]{2,1,0:T(8,128)(2,1)S(1)} %fusion.30), channel_id=1, source_target_pairs={{0,4},{4,0},{8,12},{12,8},{1,5},{5,1},{9,13},{13,9},{2,6},{6,2},{1... | collective-permute-start | bytes 786440 | tf_op jit(solution)/shard_map/ppermute | solution.py:206
  97.2 3.4 %collective-permute-done.22 = f16[2,64,1024]{2,1,0:T(8,128)(2,1)S(1)} collective-permute-done((f16[2,64,1024]{2,1,0:T(8,128)(2,1)S(1)}, f16[2,64,1024]{2,1,0:T(8,128)(2,1)S(1)}, u32[]{:S(2)}, u32[]{:S(2)}) %collective-permute-start.22) | collective-permute-done | bytes 262176 | tf_op jit(solution)/shard_map/ppermute | solution.py:206
  100.9 5.1 %collective-permute-done.25 = f16[2,64,1024]{2,1,0:T(8,128)(2,1)S(1)} collective-permute-done((f16[2,64,1024]{2,1,0:T(8,128)(2,1)S(1)}, f16[2,64,1024]{2,1,0:T(8,128)(2,1)S(1)}, u32[]{:S(2)}, u32[]{:S(2)}) %collective-permute-start.25) | collective-permute-done | bytes 262176 | tf_op jit(solution)/shard_map/ppermute | solution.py:206
  106.5 1.4 %collective-permute-done.26 = f16[64,2048]{1,0:T(8,128)(2,1)S(1)} collective-permute-done((f16[64,2048]{1,0:T(8,128)(2,1)S(1)}, f16[64,2048]{1,0:T(8,128)(2,1)S(1)}, u32[]{:S(2)}, u32[]{:S(2)}) %collective-permute-start.26) | collective-permute-done | bytes 262176 | tf_op jit(solution)/shard_map/ppermute | solution.py:75
  109.2 1.4 %collective-permute-start.27 = (f32[4,64]{1,0:T(4,128)S(1)}, f32[4,64]{1,0:T(4,128)S(1)}, u32[]{:S(2)}, u32[]{:S(2)}) collective-permute-start(f32[4,64]{1,0:T(4,128)S(1)} %get-tuple-element.68), channel_id=1, source_target_pairs={{0,1},{1,2},{2,3},{3,0},{4,5},{5,6},{6,7},{7,4},{8,9},{9,10},{10,1... | collective-permute-start | bytes 3080 | tf_op jit(solution)/shard_map/ppermute | solution.py:44
  111.8 1.8 %collective-permute-start.29 = (f32[4,64]{1,0:T(4,128)S(1)}, f32[4,64]{1,0:T(4,128)S(1)}, u32[]{:S(2)}, u32[]{:S(2)}) collective-permute-start(f32[4,64]{1,0:T(4,128)S(1)} %get-tuple-element.68), channel_id=1, source_target_pairs={{0,3},{1,0},{2,1},{3,2},{4,7},{5,4},{6,5},{7,6},{8,11},{9,8},{10,9... | collective-permute-start | bytes 3080 | tf_op jit(solution)/shard_map/ppermute | solution.py:44
  115.4 1.6 %fusion.18 = (f32[64,4096]{1,0:T(8,128)}, f32[64,4096]{1,0:T(8,128)}) fusion(f32[64]{0:T(128)S(1)} %get-tuple-element.69, f32[64]{0:T(128)S(1)} %get-tuple-element.71, f16[64,2048]{1,0:T(8,128)(2,1)S(1)} %get-tuple-element.62, f16[64,2048]{1,0:T(8,128)(2,1)S(1)} %get-tuple-element.60, f32[64,4096]{1,0:T(8,128)S(1)} %get-tuple-element.45, ...), kind=kLoop, calls=%fused_computation.28 | loop fusion | flops 1310720 | bytes 3670784 | tf_op jit(solution)/shard_map/sub | solution.py:244
  (85 shorter events, 21.8 us)
Async XLA Ops:
  0.6 35.4 %collective-permute-start.10 = (bf16[1024,4096]{1,0:T(8,128)(2,1)}, bf16[1024,4096]{1,0:T(8,128)(2,1)}, u32[]{:S(2)}, u32[]{:S(2)}) collective-permute-start(bf16[1024,4096]{1,0:T(8,128)(2,1)} %param.5), channel_id=1, source_target_pairs={{0,16},{16,0},{1,17},{17,1},{2,18},{18,2},{3,19},{19,3},{4,20},{20... | collective-permute-start | bytes 25165832 | tf_op jit(solution)/shard_map/ppermute | solution.py:41
  3.0 11.7 %collective-permute-start = (bf16[2,64,1024]{2,1,0:T(8,128)(2,1)S(1)}, bf16[2,64,1024]{2,1,0:T(8,128)(2,1)S(1)}, u32[]{:S(2)}, u32[]{:S(2)}) collective-permute-start(bf16[2,64,1024]{2,1,0:T(8,128)(2,1)S(1)} %constant_dynamic-slice_fusion.6), channel_id=1, source_target_pairs={{0,4},{4,0},{8,12},{12,8},{1,5},{5,1},{9,13},{13,9},{2,6},{6,2},{1... | collective-permute-start | bytes 786440 | tf_op jit(solution)/shard_map/ppermute | solution.py:85
  6.8 5.6 %collective-permute-start.1 = (f32[128]{0:T(128)S(1)}, f32[128]{0:T(128)S(1)}, u32[]{:S(2)}, u32[]{:S(2)}) collective-permute-start(f32[128]{0:T(128)S(1)} %multiply_reduce_fusion), channel_id=1, source_target_pairs={{0,1},{1,2},{2,3},{3,0},{4,5},{5,6},{6,7},{7,4},{8,9},{9,10},{10,1... | collective-permute-start | bytes 1544 | tf_op jit(solution)/shard_map/ppermute | solution.py:44
  8.5 4.4 %collective-permute-start.2 = (f32[128]{0:T(128)S(1)}, f32[128]{0:T(128)S(1)}, u32[]{:S(2)}, u32[]{:S(2)}) collective-permute-start(f32[128]{0:T(128)S(1)} %multiply_reduce_fusion), channel_id=1, source_target_pairs={{0,2},{1,3},{2,0},{3,1},{4,6},{5,7},{6,4},{7,5},{8,10},{9,11},{10,... | collective-permute-start | bytes 1544 | tf_op jit(solution)/shard_map/ppermute | solution.py:44
  11.0 3.5 %collective-permute-start.3 = (f32[128]{0:T(128)S(1)}, f32[128]{0:T(128)S(1)}, u32[]{:S(2)}, u32[]{:S(2)}) collective-permute-start(f32[128]{0:T(128)S(1)} %multiply_reduce_fusion), channel_id=1, source_target_pairs={{0,3},{1,0},{2,1},{3,2},{4,7},{5,4},{6,5},{7,6},{8,11},{9,8},{10,9... | collective-permute-start | bytes 1544 | tf_op jit(solution)/shard_map/ppermute | solution.py:44
  14.9 12.6 %collective-permute-start.7 = (bf16[2,2,64,1024]{3,2,1,0:T(8,128)(2,1)S(1)}, bf16[2,2,64,1024]{3,2,1,0:T(8,128)(2,1)S(1)}, u32[]{:S(2)}, u32[]{:S(2)}) collective-permute-start(bf16[2,2,64,1024]{3,2,1,0:T(8,128)(2,1)S(1)} %pad_maximum_fusion.2), channel_id=1, source_target_pairs={{0,1},{1,2},{2,3},{4,5},{5,6},{6,7},{8,9},{9,10},{10,11},{12,13},{... | collective-permute-start | bytes 1572872 | tf_op jit(solution)/shard_map/ppermute | solution.py:92
  17.0 14.6 %collective-permute-start.4 = (bf16[2,2,64,1024]{3,2,1,0:T(8,128)(2,1)S(1)}, bf16[2,2,64,1024]{3,2,1,0:T(8,128)(2,1)S(1)}, u32[]{:S(2)}, u32[]{:S(2)}) collective-permute-start(bf16[2,2,64,1024]{3,2,1,0:T(8,128)(2,1)S(1)} %pad_maximum_fusion.2), channel_id=1, source_target_pairs={{1,0},{2,1},{3,2},{5,4},{6,5},{7,6},{9,8},{10,9},{11,10},{13,12},{... | collective-permute-start | bytes 1572872 | tf_op jit(solution)/shard_map/ppermute | solution.py:95
  18.5 5.0 %collective-permute-start.5 = (f32[64]{0:T(128)S(1)}, f32[64]{0:T(128)S(1)}, u32[]{:S(2)}, u32[]{:S(2)}) collective-permute-start(f32[64]{0:T(128)S(1)} %get-tuple-element.75), channel_id=1, source_target_pairs={{0,0},{4,8},{8,16},{12,24},{16,4},{20,12},{24,20},{28,28},{1,1},{5... | collective-permute-start | bytes 776 | tf_op jit(solution)/shard_map/ppermute | solution.py:61
  19.1 5.6 %collective-permute-start.6 = (f32[64]{0:T(128)S(1)}, f32[64]{0:T(128)S(1)}, u32[]{:S(2)}, u32[]{:S(2)}) collective-permute-start(f32[64]{0:T(128)S(1)} %get-tuple-element.76), channel_id=1, source_target_pairs={{0,4},{4,12},{8,20},{12,28},{16,0},{20,8},{24,16},{28,24},{1,5},{5... | collective-permute-start | bytes 776 | tf_op jit(solution)/shard_map/ppermute | solution.py:61
  31.6 14.9 %collective-permute-start.11 = (bf16[2,2,64,1024]{3,2,1,0:T(8,128)(2,1)S(1)}, bf16[2,2,64,1024]{3,2,1,0:T(8,128)(2,1)S(1)}, u32[]{:S(2)}, u32[]{:S(2)}) collective-permute-start(bf16[2,2,64,1024]{3,2,1,0:T(8,128)(2,1)S(1)} %collective-permute-done.4), channel_id=1, source_target_pairs={{1,0},{2,1},{5,4},{6,5},{9,8},{10,9},{13,12},{14,13},{17,16},{18,1... | collective-permute-start | bytes 1572872 | tf_op jit(solution)/shard_map/ppermute | solution.py:95
  32.9 13.6 %collective-permute-start.9 = (bf16[2,2,64,1024]{3,2,1,0:T(8,128)(2,1)S(1)}, bf16[2,2,64,1024]{3,2,1,0:T(8,128)(2,1)S(1)}, u32[]{:S(2)}, u32[]{:S(2)}) collective-permute-start(bf16[2,2,64,1024]{3,2,1,0:T(8,128)(2,1)S(1)} %collective-permute-done.7), channel_id=1, source_target_pairs={{1,2},{2,3},{5,6},{6,7},{9,10},{10,11},{13,14},{14,15},{17,18},{18... | collective-permute-start | bytes 1572872 | tf_op jit(solution)/shard_map/ppermute | solution.py:92
  34.5 12.0 %collective-permute-start.8 = (bf16[2,2,64,1024]{3,2,1,0:T(8,128)(2,1)}, bf16[2,2,64,1024]{3,2,1,0:T(8,128)(2,1)S(1)}, u32[]{:S(2)}, u32[]{:S(2)}) collective-permute-start(bf16[2,2,64,1024]{3,2,1,0:T(8,128)(2,1)} %select_select_fusion.2), channel_id=1, source_target_pairs={{0,8},{8,0},{4,12},{12,4},{1,9},{9,1},{5,13},{13,5},{2,10},{10,2},... | collective-permute-start | bytes 1572872 | tf_op jit(solution)/shard_map/ppermute | solution.py:112
  46.5 12.7 %collective-permute-start.12 = (bf16[2,2,64,1024]{3,2,1,0:T(8,128)(2,1)S(1)}, bf16[2,2,64,1024]{3,2,1,0:T(8,128)(2,1)S(1)}, u32[]{:S(2)}, u32[]{:S(2)}) collective-permute-start(bf16[2,2,64,1024]{3,2,1,0:T(8,128)(2,1)S(1)} %pad_maximum_fusion.2), channel_id=1, source_target_pairs={{0,3},{4,7},{11,8},{15,12},{16,19},{20,23},{27,24},{31,28}} | collective-permute-start | bytes 1572872 | tf_op jit(solution)/shard_map/ppermute | solution.py:140
  51.3 7.9 %collective-permute-start.13 = (bf16[2,2,64,1024]{3,2,1,0:T(8,128)(2,1)S(1)}, bf16[2,2,64,1024]{3,2,1,0:T(8,128)(2,1)S(1)}, u32[]{:S(2)}, u32[]{:S(2)}) collective-permute-start(bf16[2,2,64,1024]{3,2,1,0:T(8,128)(2,1)S(1)} %pad_maximum_fusion.2), channel_id=1, source_target_pairs={{3,8},{7,12},{8,3},{12,7},{19,24},{23,28},{24,19},{28,23}} | collective-permute-start | bytes 1572872 | tf_op jit(solution)/shard_map/ppermute | solution.py:140
  52.3 12.1 %collective-permute-start.14 = (bf16[2,2,64,1024]{3,2,1,0:T(8,128)(2,1)S(1)}, bf16[2,2,64,1024]{3,2,1,0:T(8,128)(2,1)S(1)}, u32[]{:S(2)}, u32[]{:S(2)}) collective-permute-start(bf16[2,2,64,1024]{3,2,1,0:T(8,128)(2,1)S(1)} %get-tuple-element.57), channel_id=1, source_target_pairs={{1,9},{2,10},{3,11},{5,13},{6,14},{7,15},{8,0},{9,1},{10,2},{12,4}... | collective-permute-start | bytes 1572872 | tf_op jit(solution)/shard_map/ppermute | solution.py:129
  53.9 17.1 %collective-permute-start.16 = (bf16[2,2,2,64,1024]{4,3,2,1,0:T(8,128)(2,1)S(1)}, bf16[2,2,2,64,1024]{4,3,2,1,0:T(8,128)(2,1)S(1)}, u32[]{:S(2)}, u32[]{:S(2)}) collective-permute-start(bf16[2,2,2,64,1024]{4,3,2,1,0:T(8,128)(2,1)S(1)} %pad_maximum_fusion), channel_id=1, source_target_pairs={{0,16},{16,0},{1,17},{17,1},{2,18},{18,2},{3,19},{19,3},{4,20},{20... | collective-permute-start | bytes 3145736 | tf_op jit(solution)/shard_map/ppermute | solution.py:75
  64.6 8.7 %collective-permute-start.17 = (bf16[2,2,2,64,1024]{4,3,2,1,0:T(8,128)(2,1)S(1)}, bf16[2,2,2,64,1024]{4,3,2,1,0:T(8,128)(2,1)S(1)}, u32[]{:S(2)}, u32[]{:S(2)}) collective-permute-start(bf16[2,2,2,64,1024]{4,3,2,1,0:T(8,128)(2,1)S(1)} %pad_maximum_fusion.1), channel_id=1, source_target_pairs={{0,16},{16,0},{1,17},{17,1},{2,18},{18,2},{3,19},{19,3},{4,20},{20... | collective-permute-start | bytes 3145736 | tf_op jit(solution)/shard_map/ppermute | solution.py:75
  67.3 14.8 %collective-permute-start.21 = (f16[2,2,64,1024]{3,2,1,0:T(8,128)(2,1)S(1)}, f16[2,2,64,1024]{3,2,1,0:T(8,128)(2,1)S(1)}, u32[]{:S(2)}, u32[]{:S(2)}) collective-permute-start(f16[2,2,64,1024]{3,2,1,0:T(8,128)(2,1)S(1)} %fusion.20), channel_id=1, source_target_pairs={{0,8},{8,0},{4,12},{12,4},{1,9},{9,1},{5,13},{13,5},{2,10},{10,2},... | collective-permute-start | bytes 1572872 | tf_op jit(solution)/shard_map/ppermute | solution.py:194
  68.0 17.5 %collective-permute-start.15 = (f16[2,2,64,1024]{3,2,0,1:T(8,128)(2,1)S(1)}, f16[2,2,64,1024]{3,2,0,1:T(8,128)(2,1)S(1)}, u32[]{:S(2)}, u32[]{:S(2)}) collective-permute-start(f16[2,2,64,1024]{3,2,0,1:T(8,128)(2,1)S(1)} %fusion.22), channel_id=1, source_target_pairs={{0,4},{4,0},{8,12},{12,8},{1,5},{5,1},{9,13},{13,9},{2,6},{6,2},{1... | collective-permute-start | bytes 1572872 | tf_op jit(solution)/shard_map/ppermute | solution.py:193
  74.6 18.7 %collective-permute-start.20 = (f16[2,2,64,1024]{3,2,1,0:T(8,128)(2,1)S(1)}, f16[2,2,64,1024]{3,2,1,0:T(8,128)(2,1)S(1)}, u32[]{:S(2)}, u32[]{:S(2)}) collective-permute-start(f16[2,2,64,1024]{3,2,1,0:T(8,128)(2,1)S(1)} %fusion.21), channel_id=1, source_target_pairs={{0,8},{8,0},{4,12},{12,4},{1,9},{9,1},{5,13},{13,5},{2,10},{10,2},... | collective-permute-start | bytes 1572872 | tf_op jit(solution)/shard_map/ppermute | solution.py:194
  78.3 18.5 %collective-permute-start.19 = (f16[2,2,64,1024]{3,2,0,1:T(8,128)(2,1)S(1)}, f16[2,2,64,1024]{3,2,0,1:T(8,128)(2,1)S(1)}, u32[]{:S(2)}, u32[]{:S(2)}) collective-permute-start(f16[2,2,64,1024]{3,2,0,1:T(8,128)(2,1)S(1)} %fusion.23), channel_id=1, source_target_pairs={{0,4},{4,0},{8,12},{12,8},{1,5},{5,1},{9,13},{13,9},{2,6},{6,2},{1... | collective-permute-start | bytes 1572872 | tf_op jit(solution)/shard_map/ppermute | solution.py:193
  82.3 18.3 %collective-permute-start.22 = (f16[2,64,1024]{2,1,0:T(8,128)(2,1)S(1)}, f16[2,64,1024]{2,1,0:T(8,128)(2,1)S(1)}, u32[]{:S(2)}, u32[]{:S(2)}) collective-permute-start(f16[2,64,1024]{2,1,0:T(8,128)(2,1)S(1)} %fusion.31), channel_id=1, source_target_pairs={{0,4},{4,0},{8,12},{12,8},{1,5},{5,1},{9,13},{13,9},{2,6},{6,2},{1... | collective-permute-start | bytes 786440 | tf_op jit(solution)/shard_map/ppermute | solution.py:206
  85.8 14.9 %collective-permute-start.18 = (f16[2,64,1024]{2,1,0:T(8,128)(2,1)S(1)}, f16[2,64,1024]{2,1,0:T(8,128)(2,1)S(1)}, u32[]{:S(2)}, u32[]{:S(2)}) collective-permute-start(f16[2,64,1024]{2,1,0:T(8,128)(2,1)S(1)} %fusion.28), channel_id=1, source_target_pairs={{0,8},{8,0},{4,12},{12,4},{1,9},{9,1},{5,13},{13,5},{2,10},{10,2},... | collective-permute-start | bytes 786440 | tf_op jit(solution)/shard_map/ppermute | solution.py:205
  93.5 12.5 %collective-permute-start.25 = (f16[2,64,1024]{2,1,0:T(8,128)(2,1)S(1)}, f16[2,64,1024]{2,1,0:T(8,128)(2,1)S(1)}, u32[]{:S(2)}, u32[]{:S(2)}) collective-permute-start(f16[2,64,1024]{2,1,0:T(8,128)(2,1)S(1)} %fusion.30), channel_id=1, source_target_pairs={{0,4},{4,0},{8,12},{12,8},{1,5},{5,1},{9,13},{13,9},{2,6},{6,2},{1... | collective-permute-start | bytes 786440 | tf_op jit(solution)/shard_map/ppermute | solution.py:206
  97.0 9.0 %collective-permute-start.24 = (f16[2,64,1024]{2,1,0:T(8,128)(2,1)S(1)}, f16[2,64,1024]{2,1,0:T(8,128)(2,1)S(1)}, u32[]{:S(2)}, u32[]{:S(2)}) collective-permute-start(f16[2,64,1024]{2,1,0:T(8,128)(2,1)S(1)} %fusion.29), channel_id=1, source_target_pairs={{0,8},{8,0},{4,12},{12,4},{1,9},{9,1},{5,13},{13,5},{2,10},{10,2},... | collective-permute-start | bytes 786440 | tf_op jit(solution)/shard_map/ppermute | solution.py:205
  100.8 5.5 %collective-permute-start.23 = (f16[64,2048]{1,0:T(8,128)(2,1)S(1)}, f16[64,2048]{1,0:T(8,128)(2,1)S(1)}, u32[]{:S(2)}, u32[]{:S(2)}) collective-permute-start(f16[64,2048]{1,0:T(8,128)(2,1)S(1)} %fusion.37), channel_id=1, source_target_pairs={{0,16},{16,0},{1,17},{17,1},{2,18},{18,2},{3,19},{19,3},{4,20},{20... | collective-permute-start | bytes 786440 | tf_op jit(solution)/shard_map/ppermute | solution.py:75
  106.2 1.6 %collective-permute-start.26 = (f16[64,2048]{1,0:T(8,128)(2,1)S(1)}, f16[64,2048]{1,0:T(8,128)(2,1)S(1)}, u32[]{:S(2)}, u32[]{:S(2)}) collective-permute-start(f16[64,2048]{1,0:T(8,128)(2,1)S(1)} %fusion.35), channel_id=1, source_target_pairs={{0,16},{16,0},{1,17},{17,1},{2,18},{18,2},{3,19},{19,3},{4,20},{20... | collective-permute-start | bytes 786440 | tf_op jit(solution)/shard_map/ppermute | solution.py:75
  109.2 5.4 %collective-permute-start.27 = (f32[4,64]{1,0:T(4,128)S(1)}, f32[4,64]{1,0:T(4,128)S(1)}, u32[]{:S(2)}, u32[]{:S(2)}) collective-permute-start(f32[4,64]{1,0:T(4,128)S(1)} %get-tuple-element.68), channel_id=1, source_target_pairs={{0,1},{1,2},{2,3},{3,0},{4,5},{5,6},{6,7},{7,4},{8,9},{9,10},{10,1... | collective-permute-start | bytes 3080 | tf_op jit(solution)/shard_map/ppermute | solution.py:44
  110.7 4.5 %collective-permute-start.28 = (f32[4,64]{1,0:T(4,128)S(1)}, f32[4,64]{1,0:T(4,128)S(1)}, u32[]{:S(2)}, u32[]{:S(2)}) collective-permute-start(f32[4,64]{1,0:T(4,128)S(1)} %get-tuple-element.68), channel_id=1, source_target_pairs={{0,2},{1,3},{2,0},{3,1},{4,6},{5,7},{6,4},{7,5},{8,10},{9,11},{10,... | collective-permute-start | bytes 3080 | tf_op jit(solution)/shard_map/ppermute | solution.py:44
  111.8 3.6 %collective-permute-start.29 = (f32[4,64]{1,0:T(4,128)S(1)}, f32[4,64]{1,0:T(4,128)S(1)}, u32[]{:S(2)}, u32[]{:S(2)}) collective-permute-start(f32[4,64]{1,0:T(4,128)S(1)} %get-tuple-element.68), channel_id=1, source_target_pairs={{0,3},{1,0},{2,1},{3,2},{4,7},{5,4},{6,5},{7,6},{8,11},{9,8},{10,9... | collective-permute-start | bytes 3080 | tf_op jit(solution)/shard_map/ppermute | solution.py:44
